TPU v7x, 32 devices: a whole 2x2x4 slice. The times are simulated.
32 devices in a mesh: dp: 2 (over core), ctx: 8 (over z, x), tp: 2 (over y).
Axes of the slice: x: 2, y: 2, z: 4, core: 2. Of those that a mesh axis runs over, the one named last changes fastest.
Arguments:
- queries: bfloat16 [2, 2048, 512], P('dp', 'ctx', 'tp'), may hold values from -32 to 32
- key_heads: bfloat16 [2, 2048, 512], P('dp', 'ctx', 'tp'), may hold values from -32 to 32
- value_heads: bfloat16 [2, 2048, 512], P('dp', 'ctx', 'tp'), may hold values from -6 to 6
- grad_output: bfloat16 [2, 2048, 4096], P('dp', 'ctx', 'tp'), may hold values from -6 to 6
- out_weight: bfloat16 [512, 4096], P('tp'), may hold values from -0.375 to 0.375
- block_pattern: int32 [8, 3], replicated, may hold values from 0 to 7, all different within a row; in each aligned block of 8 rows (0 to 7, 8 to 15, ...) at most 6 rows name the same one
- global_offsets: int32 [8, 8], replicated, may hold values from 0 to 255, as said below
Outputs:
- grad_queries: bfloat16 [2, 2048, 512], P('dp', 'ctx', 'tp')
- grad_keys: bfloat16 [2, 2048, 512], P('dp', 'ctx', 'tp')
- grad_values: bfloat16 [2, 2048, 512], P('dp', 'ctx', 'tp')
- grad_weight: bfloat16 [512, 4096], P('tp', ('dp', 'ctx'))
Inputs may be any that keep to these rules, and one draw needn't show every extreme that they name: `block_pattern`: each row names 3 different blocks; no block is named by more than 6 rows in all, and one block is named by exactly 6 rows. A row may name its own block or a neighbour. `global_offsets`: row b holds the positions within block b of its 8 global tokens, all different.
All inputs are finite; a program needn't handle non-finite values.
Results may differ from a plain program's by a relative error of at most 0.017.
Values may be sent and summed in bfloat16 or wider, within the bound.
No kernel may reach another device: no remote copies, remote signals or barrier semaphores. Data moves between devices by JAX's collectives and lax.ppermute only.
A program may use at most 64 MiB of HBM per device.

v0:
```python
import jax
import jax.numpy as jnp
from jax import lax
from jax.sharding import PartitionSpec as P

HD = 128


def product(left_op, right_op):
    return jnp.dot(left_op, right_op, preferred_element_type=jnp.float32)


def against(left_op, right_op):
    return lax.dot_general(
        left_op, right_op, (((1,), (1,)), ((), ())), preferred_element_type=jnp.float32
    )


def across(left_op, right_op):
    return lax.dot_general(
        left_op, right_op, (((0,), (0,)), ((), ())), preferred_element_type=jnp.float32
    )


def rounded(values):
    return lax.optimization_barrier(values.astype(jnp.bfloat16)).astype(jnp.float32)


def softmax_rows(scores):
    row_max = jnp.max(scores, axis=1)
    weights_f = jnp.exp(scores - row_max[:, None])
    row_total = jnp.sum(weights_f, axis=1)
    return (row_max, row_total, weights_f / row_total[:, None])


def moved_globals(
    query_rows,
    grad_heads,
    key_own,
    value_own,
    block_pattern,
    global_offsets,
    own_block,
    block_count,
    slot_clip,
    key_valid,
    row_keep,
    own_offsets,
    score_scale,
):
    block_size, feat_count = query_rows.shape
    head_count = feat_count // HD
    glob_count = global_offsets.shape[1]
    slot_count = slot_clip.shape[0]
    kv_own = jnp.concatenate([key_own, value_own], axis=1)
    targets = jnp.arange(block_count, dtype=jnp.int32)
    wanted = jnp.any(block_pattern == own_block, axis=1) | (jnp.abs(targets - own_block) <= 1)
    send_kv = jnp.where(wanted[:, None, None], kv_own[None], jnp.zeros_like(kv_own)[None])
    fetched = lax.all_to_all(send_kv, "ctx", split_axis=0, concat_axis=0, tiled=True)
    slot_kv = jnp.take(fetched, slot_clip, axis=0).reshape(slot_count * block_size, 2 * feat_count)
    glob_q_own = jnp.take(query_rows, own_offsets, axis=0)
    glob_g_own = jnp.take(grad_heads, own_offsets, axis=0)
    glob_k_own = jnp.take(key_own, own_offsets, axis=0)
    glob_v_own = jnp.take(value_own, own_offsets, axis=0)
    all_gq, all_gg, all_gk, all_gv = (
        lax.all_gather(glob_q_own, "ctx", axis=0, tiled=True),
        lax.all_gather(glob_g_own, "ctx", axis=0, tiled=True),
        lax.all_gather(glob_k_own, "ctx", axis=0, tiled=True),
        lax.all_gather(glob_v_own, "ctx", axis=0, tiled=True),
    )
    key_pick = jnp.concatenate([slot_kv[:, :feat_count], all_gk], axis=0)
    value_pick = jnp.concatenate([slot_kv[:, feat_count:], all_gv], axis=0)
    score_list = []
    for head_index in range(head_count):
        head_cols = slice(head_index * HD, (head_index + 1) * HD)
        score_list.append(score_scale * against(all_gq[:, head_cols], key_own[:, head_cols]))
    glob_scores = jnp.stack(score_list)
    glob_max = lax.pmax(jnp.max(glob_scores, axis=2), "ctx")
    glob_exp = jnp.exp(glob_scores - glob_max[:, :, None])
    glob_total = lax.psum(jnp.sum(glob_exp, axis=2), "ctx")
    glob_probs = glob_exp / glob_total[:, :, None]
    glob_low = glob_probs.astype(jnp.bfloat16)
    attn_parts = []
    for head_index in range(head_count):
        head_cols = slice(head_index * HD, (head_index + 1) * HD)
        attn_parts.append(product(glob_low[head_index], value_own[:, head_cols]))
    glob_attn = lax.psum(jnp.concatenate(attn_parts, axis=1).astype(jnp.bfloat16), "ctx")
    dscore_list = []
    dquery_parts = []
    for head_index in range(head_count):
        head_cols = slice(head_index * HD, (head_index + 1) * HD)
        glob_dot = jnp.sum(
            all_gg[:, head_cols].astype(jnp.float32) * glob_attn[:, head_cols].astype(jnp.float32),
            axis=1,
        )
        head_dscore = (
            glob_probs[head_index]
            * (against(all_gg[:, head_cols], value_own[:, head_cols]) - glob_dot[:, None])
        ).astype(jnp.bfloat16)
        dscore_list.append(head_dscore)
        dquery_parts.append(product(head_dscore, key_own[:, head_cols]))
    glob_dscore = jnp.stack(dscore_list)
    glob_dquery = lax.psum(
        jnp.concatenate(dquery_parts, axis=1).astype(jnp.bfloat16), "ctx"
    ).astype(jnp.float32)
    own_start = own_block * glob_count
    own_glob_attn = lax.dynamic_slice_in_dim(glob_attn, own_start, glob_count, 0)
    own_glob_dq = lax.dynamic_slice_in_dim(glob_dquery, own_start, glob_count, 0)
    grad_query_list = []
    attn_list = []
    term_list = []
    for head_index in range(head_count):
        head_cols = slice(head_index * HD, (head_index + 1) * HD)
        query_head = query_rows[:, head_cols]
        grad_head = grad_heads[:, head_cols]
        key_head = key_pick[:, head_cols]
        value_head = value_pick[:, head_cols]
        scores = jnp.where(
            key_valid[None, :], score_scale * against(query_head, key_head), -jnp.inf
        )
        local_max, local_total, attn_probs = softmax_rows(scores)
        attn_probs = jnp.where(row_keep[:, None], attn_probs, 0.0)
        probs_low = attn_probs.astype(jnp.bfloat16)
        attn_head = (
            product(probs_low, value_head)
            .at[own_offsets]
            .set(own_glob_attn[:, head_cols].astype(jnp.float32))
        )
        attn_head = attn_head.astype(jnp.bfloat16)
        row_dot = jnp.sum(grad_head.astype(jnp.float32) * attn_head.astype(jnp.float32), axis=1)
        dscore_low = (attn_probs * (against(grad_head, value_head) - row_dot[:, None])).astype(
            jnp.bfloat16
        )
        grad_query = product(dscore_low, key_head).at[own_offsets].set(own_glob_dq[:, head_cols])
        grad_query_list.append((score_scale * grad_query).astype(jnp.bfloat16))
        attn_list.append(attn_head)
        term_list.append(
            jnp.stack(
                [score_scale * across(dscore_low, query_head), across(probs_low, grad_head)], axis=1
            )
        )
    pick_term = jnp.concatenate(term_list, axis=2)
    slot_terms = pick_term[: slot_count * block_size].reshape(slot_count, block_size, 2, feat_count)
    glob_terms = pick_term[slot_count * block_size :].reshape(
        block_count, glob_count, 2, feat_count
    )
    send_terms = (
        jnp.zeros((block_count, block_size, 2, feat_count), jnp.float32)
        .at[slot_clip]
        .add(slot_terms)
    )
    send_terms = send_terms.at[targets[:, None], global_offsets].add(glob_terms)
    returned = lax.all_to_all(
        send_terms.astype(jnp.bfloat16), "ctx", split_axis=0, concat_axis=0, tiled=True
    ).astype(send_terms.dtype)

    def source_add(source, running):
        glob_start = source * glob_count
        source_dscore = lax.dynamic_slice_in_dim(glob_dscore, glob_start, glob_count, 1)
        source_low = lax.dynamic_slice_in_dim(glob_low, glob_start, glob_count, 1)
        source_query = lax.dynamic_slice_in_dim(all_gq, glob_start, glob_count, 0)
        source_grad = lax.dynamic_slice_in_dim(all_gg, glob_start, glob_count, 0)
        head_parts = []
        for head_index in range(head_count):
            head_cols = slice(head_index * HD, (head_index + 1) * HD)
            head_parts.append(
                jnp.stack(
                    [
                        score_scale * across(source_dscore[head_index], source_query[:, head_cols]),
                        across(source_low[head_index], source_grad[:, head_cols]),
                    ],
                    axis=1,
                )
            )
        block_term = jnp.concatenate(head_parts, axis=2)
        from_source = lax.dynamic_index_in_dim(returned, source, 0, keepdims=False)
        return running + rounded(block_term + from_source)

    summed = lax.fori_loop(
        0, block_count, source_add, jnp.zeros((block_size, 2, feat_count), jnp.float32)
    )
    attention = jnp.concatenate(attn_list, axis=1)
    grad_queries = jnp.concatenate(grad_query_list, axis=1)
    return (grad_queries, attention, summed)


def per_device(
    queries, key_heads, value_heads, grad_output, out_weight, block_pattern, global_offsets
):
    block_size = queries.shape[1]
    block_count = lax.axis_size("ctx")
    own_block = lax.axis_index("ctx")
    score_scale = HD ** (-0.5)
    full_grad = lax.all_gather(grad_output, "tp", axis=2, tiled=True)[0]
    grad_heads = against(full_grad, out_weight).astype(jnp.bfloat16)
    query_rows = queries[0]
    positions = jnp.arange(block_size, dtype=jnp.int32)
    glob_flags = jnp.any(global_offsets[:, :, None] == positions[None, None, :], axis=1)
    glob_positions = (
        jnp.arange(block_count, dtype=jnp.int32)[:, None] * block_size + global_offsets
    ).reshape(-1)
    own_offsets = global_offsets[own_block]
    row_keep = jnp.logical_not(glob_flags[own_block])
    neighbours = own_block + jnp.arange(-1, 2, dtype=jnp.int32)
    chosen = block_pattern[own_block]
    slot_ok = jnp.concatenate(
        [(neighbours >= 0) & (neighbours < block_count), jnp.abs(chosen - own_block) > 1]
    )
    slot_clip = jnp.clip(jnp.concatenate([neighbours, chosen]), 0, block_count - 1)
    slot_valid = (slot_ok[:, None] & jnp.logical_not(glob_flags[slot_clip])).reshape(-1)
    key_valid = jnp.concatenate([slot_valid, glob_positions >= 0])
    grad_flat, attention, summed = moved_globals(
        query_rows,
        grad_heads,
        key_heads[0],
        value_heads[0],
        block_pattern,
        global_offsets,
        own_block,
        block_count,
        slot_clip,
        key_valid,
        row_keep,
        own_offsets,
        score_scale,
    )
    grad_queries = grad_flat[None]
    grad_keys = summed[:, 0].astype(jnp.bfloat16)[None]
    grad_values = summed[:, 1].astype(jnp.bfloat16)[None]
    weight_terms = across(attention, full_grad)
    grad_weight = lax.psum_scatter(
        weight_terms.astype(jnp.bfloat16), ("dp", "ctx"), scatter_dimension=1, tiled=True
    )
    return (grad_queries, grad_keys, grad_values, grad_weight)


def solution(mesh):
    in_specs = (
        P("dp", "ctx", "tp"),
        P("dp", "ctx", "tp"),
        P("dp", "ctx", "tp"),
        P("dp", "ctx", "tp"),
        P("tp", None),
        P(),
        P(),
    )
    out_specs = (
        P("dp", "ctx", "tp"),
        P("dp", "ctx", "tp"),
        P("dp", "ctx", "tp"),
        P("tp", ("dp", "ctx")),
    )
    return jax.shard_map(
        per_device, mesh=mesh, in_specs=in_specs, out_specs=out_specs, check_vma=False
    )
```

profile of v0, /device:TPU:0, one launch (start us, length us, event | category | flops | bytes accessed | tf_op | source)
XLA Modules:
  0.0 460.2 jit_solution(1040759737267597880)
XLA Ops:
  8.6 1.0 pad_maximum_fusion.2
  9.6 1.5 broadcast_select_fusion
  11.2 7.4 %all-to-all-start = ((bf16[8,256,512]{2,1,0:T(8,128)(2,1)}), bf16[8,256,512]{2,1,0:T(8,128)(2,1)}, u32[]{:S(2)}, u32[]{:S(2)}) async-start(bf16[8,256,512]{2,1,0:T(8,128)(2,1)} %broadcast_select_fusion), calls=%async_computation | async-start | bytes 4194304 | tf_op jit(solution)/shard_map/all_to_all | solution.py:59
  23.6 21.9 %all-gather.2.cloned.1.call-done = bf16[1,256,4096]{2,1,0:T(8,128)(2,1)} async-done(((bf16[1,256,2048]{2,1,0:T(8,128)(2,1)}), bf16[1,256,4096]{2,1,0:T(8,128)(2,1)}) %all-gather.2.cloned.1.call-update) | async-done | bytes 2097168 | tf_op jit(solution)/shard_map/all_gather | solution.py:194
  45.4 2.3 fusion.24
  48.5 39.7 %all_gather.18 = bf16[64,256]{1,0:T(8,128)(2,1)} all-gather(bf16[8,256]{1,0:T(8,128)(2,1)S(1)} %get-tuple-element.203), channel_id=1, replica_groups=mesh['dp'=2,'ctx'=8,'tp'=2] {'ctx'}, dimensions={0}, use_global_device_ids=true | all-gather | bytes 36864 | tf_op jit(solution)/shard_map/all_gather | solution.py:66
  90.1 19.8 %pmax.7 = f32[2,64]{1,0:T(2,128)S(1)} all-reduce(f32[2,64]{1,0:T(2,128)S(1)} %fusion.42), channel_id=1, replica_groups=mesh['dp'=2,'ctx'=8,'tp'=2] {'ctx'}, use_global_device_ids=true, to_apply=%region_5.7 | all-reduce | flops 128 | bytes 1024 | tf_op jit(solution)/shard_map/pmax | solution.py:78
  110.1 17.1 %psum.21 = f32[2,64]{1,0:T(2,128)S(1)} all-reduce(f32[2,64]{1,0:T(2,128)S(1)} %fusion.41), channel_id=1, replica_groups=mesh['dp'=2,'ctx'=8,'tp'=2] {'ctx'}, use_global_device_ids=true, to_apply=%region_7.9 | all-reduce | flops 128 | bytes 1024 | tf_op jit(solution)/shard_map/psum | solution.py:80
  127.2 31.4 %all_gather.17 = bf16[64,256]{1,0:T(8,128)(2,1)} all-gather(bf16[8,256]{1,0:T(8,128)(2,1)S(1)} %get-tuple-element.202), channel_id=1, replica_groups=mesh['dp'=2,'ctx'=8,'tp'=2] {'ctx'}, dimensions={0}, use_global_device_ids=true | all-gather | bytes 36864 | tf_op jit(solution)/shard_map/all_gather | solution.py:69
  158.6 32.1 %all_gather.15 = bf16[64,256]{1,0:T(8,128)(2,1)} all-gather(bf16[8,256]{1,0:T(8,128)(2,1)S(1)} %get-tuple-element.204), channel_id=1, replica_groups=mesh['dp'=2,'ctx'=8,'tp'=2] {'ctx'}, dimensions={0}, use_global_device_ids=true | all-gather | bytes 36864 | tf_op jit(solution)/shard_map/all_gather | solution.py:68
  193.2 35.3 %psum.22 = bf16[64,256]{1,0:T(8,128)(2,1)} all-reduce(bf16[64,256]{1,0:T(8,128)(2,1)S(1)} %pad_maximum_fusion.9), channel_id=1, replica_groups=mesh['dp'=2,'ctx'=8,'tp'=2] {'ctx'}, use_global_device_ids=true, to_apply=%region_8.10 | all-reduce | flops 16384 | bytes 65536 | tf_op jit(solution)/shard_map/psum | solution.py:87
  228.5 3.4 gather_fusion.1
  232.0 1.7 bitcast_select_fusion
  235.7 1.3 convolution_bitcast_fusion.2
  237.0 1.2 fusion.36
  238.5 1.2 fusion.35
  239.7 1.3 convolution_bitcast_fusion.3
  241.0 2.3 scatter_custom_fusion.2
  243.2 1.0 copy.31
  244.2 2.3 scatter_custom_fusion
  246.5 1.0 copy.29
  247.7 2.2 fusion.16
  253.1 1.9 copy.32
  255.1 2.4 broadcast_in_dim.138
  257.5 8.5 %scatter_fusion = f32[8,256,2,256]{3,1,2,0:T(8,128)} fusion(f32[8,256,2,256]{3,1,2,0:T(8,128)} %broadcast_in_dim.138, s32[6]{0:T(128)S(1)} %copy-done.28, f32[6,256,2,256]{3,1,2,0:T(8,128)} %copy.32), kind=kCustom, calls=%fused_computation.10 | custom fusion | flops 786432 | bytes 9437208 | tf_op jit(solution)/shard_map/scatter-add | solution.py:150
  266.1 7.4 %copy.33 = f32[8,256,2,256]{3,2,1,0:T(2,128)} copy(f32[8,256,2,256]{3,1,2,0:T(8,128)} %scatter_fusion) | data formatting | bytes 8388608 | tf_op jit(solution)/shard_map/scatter-add | solution.py:150
  273.5 7.1 %scatter_fusion.1 = f32[8,256,2,256]{3,2,1,0:T(2,128)} fusion(f32[8,256,2,256]{3,2,1,0:T(2,128)} %copy.33, s32[64]{0:T(128)S(1)} %reshape.253, f32[64,2,256]{2,1,0:T(2,128)S(1)} %copy.34), kind=kCustom, calls=%fused_computation.11 | custom fusion | flops 32768 | bytes 393728 | tf_op jit(solution)/shard_map/scatter-add | solution.py:152
  280.6 5.0 %convert_element_type.139 = bf16[8,256,2,256]{3,2,1,0:T(2,128)(2,1)} convert(f32[8,256,2,256]{3,2,1,0:T(2,128)} %scatter_fusion.1) | non-fusion elementwise | flops 1048576 | bytes 6291456 | tf_op jit(solution)/shard_map/convert_element_type | solution.py:154
  285.6 4.5 all-to-all-start.1
  290.1 47.1 %all_gather.19 = bf16[64,256]{1,0:T(8,128)(2,1)S(1)} all-gather(bf16[8,256]{1,0:T(8,128)(2,1)S(1)} %get-tuple-element.201), channel_id=1, replica_groups=mesh['dp'=2,'ctx'=8,'tp'=2] {'ctx'}, dimensions={0}, use_global_device_ids=true | all-gather | bytes 36864 | tf_op jit(solution)/shard_map/all_gather | solution.py:67
  338.0 35.7 %psum.23 = bf16[64,256]{1,0:T(8,128)(2,1)S(1)} all-reduce(bf16[64,256]{1,0:T(8,128)(2,1)S(1)} %pad_maximum_fusion.10), channel_id=1, replica_groups=mesh['dp'=2,'ctx'=8,'tp'=2] {'ctx'}, use_global_device_ids=true, to_apply=%region_13.15 | all-reduce | flops 16384 | bytes 65536 | tf_op jit(solution)/shard_map/psum | solution.py:103
  373.7 3.6 convolution_convert_fusion
  378.1 1.6 fusion.44
  380.5 1.6 fusion.88
  382.1 1.0 scatter_custom_fusion.1
  383.9 5.0 %convert_element_type.140 = f32[8,256,2,256]{3,2,1,0:T(2,128)} convert(bf16[8,256,2,256]{3,2,1,0:T(2,128)(2,1)} %all-to-all-done.1) | non-fusion elementwise | flops 1048576 | bytes 6291456 | tf_op jit(solution)/shard_map/convert_element_type | solution.py:155
  388.9 62.6 %while.14 = (s32[]{:T(128)}, f32[256,2,256]{0,2,1:T(8,128)}, bf16[2,64,256]{2,1,0:T(8,128)(2,1)S(1)}, bf16[64,256]{1,0:T(8,128)(2,1)}, bf16[2,64,256]{2,1,0:T(8,...) while((s32[]{:T(128)}, f32[256,2,256]{0,2,1:T(8,128)}, ...), condition=%wide.region_23.25_spmd.clone, body=%wide.region_22.24_spmd.clone.sunk | while | flops 3211273 | bytes 10254721 | solution.py:179
  391.7 1.5 fusion.117
  393.2 1.2 constant_dynamic-slice_fusion.3
  394.7 1.0 fusion.118
  399.5 1.5 fusion.117
  401.0 1.2 constant_dynamic-slice_fusion.3
  402.5 1.0 fusion.118
  407.3 1.6 fusion.117
  408.8 1.2 constant_dynamic-slice_fusion.3
  410.3 1.0 fusion.118
  412.4 0.9 convolution_bitcast_fusion.6
  415.1 1.6 fusion.117
  416.6 1.2 constant_dynamic-slice_fusion.3
  418.1 1.0 fusion.118
  423.0 1.5 fusion.117
  424.5 1.2 constant_dynamic-slice_fusion.3
  426.0 1.0 fusion.118
  428.0 0.9 convolution_bitcast_fusion.6
  430.8 1.5 fusion.117
  432.3 1.2 constant_dynamic-slice_fusion.3
  433.8 1.0 fusion.118
  438.6 1.5 fusion.117
  440.1 1.2 constant_dynamic-slice_fusion.3
  441.6 1.0 fusion.118
  446.4 1.6 fusion.117
  448.0 1.2 constant_dynamic-slice_fusion.3
  449.4 1.0 fusion.118
  451.5 1.2 copy.36
  (268 shorter events, 50.9 us)
Async XLA Ops:
  7.2 38.2 %copy-start = (bf16[256,4096]{1,0:T(8,128)(2,1)S(1)}, bf16[256,4096]{1,0:T(8,128)(2,1)}, u32[]{:S(2)}) copy-start(bf16[256,4096]{1,0:T(8,128)(2,1)} %param.15) | copy-start | bytes 6291460
  7.2 38.2 %all-gather.2.cloned.1.call-start = ((), (), s32[]{:S(2)}) async-start(), calls=%async_computation.3 | async-start | bytes 3145728 | tf_op jit(solution)/shard_map/all_gather | solution.py:194
  11.1 7.4 %copy-start.26 = (s32[8,3]{0,1:T(4,128)S(1)}, s32[8,3]{0,1:T(4,128)}, u32[]{:S(2)}) copy-start(s32[8,3]{0,1:T(4,128)} %param.16) | copy-start | bytes 292
  11.1 7.6 %copy-start.23 = (s32[8,8]{1,0:T(8,128)S(1)}, s32[8,8]{1,0:T(8,128)}, u32[]{:S(2)}) copy-start(s32[8,8]{1,0:T(8,128)} %param.17) | copy-start | bytes 772
  11.1 7.6 %copy-start.10 = (bf16[1,256,256]{2,1,0:T(8,128)(2,1)S(1)}, bf16[1,256,256]{2,1,0:T(8,128)(2,1)}, u32[]{:S(2)}) copy-start(bf16[1,256,256]{2,1,0:T(8,128)(2,1)} %param.13) | copy-start | bytes 393220
  11.1 8.2 %copy-start.9 = (bf16[1,256,256]{2,1,0:T(8,128)(2,1)S(1)}, bf16[1,256,256]{2,1,0:T(8,128)(2,1)}, u32[]{:S(2)}) copy-start(bf16[1,256,256]{2,1,0:T(8,128)(2,1)} %param.12) | copy-start | bytes 393220
  11.1 10.6 %copy-start.16 = (bf16[1,256,256]{2,1,0:T(8,128)(2,1)S(1)}, bf16[1,256,256]{2,1,0:T(8,128)(2,1)}, u32[]{:S(2)}) copy-start(bf16[1,256,256]{2,1,0:T(8,128)(2,1)} %param.11) | copy-start | bytes 393220
  11.2 217.4 %all-to-all-start = ((bf16[8,256,512]{2,1,0:T(8,128)(2,1)}), bf16[8,256,512]{2,1,0:T(8,128)(2,1)}, u32[]{:S(2)}, u32[]{:S(2)}) async-start(bf16[8,256,512]{2,1,0:T(8,128)(2,1)} %broadcast_select_fusion), calls=%async_computation | async-start | bytes 4194304 | tf_op jit(solution)/shard_map/all_to_all | solution.py:59
  233.8 4.7 %copy-start.12 = (bf16[1536,256]{1,0:T(8,128)(2,1)}, bf16[1536,256]{1,0:T(8,128)(2,1)S(1)}, u32[]{:S(2)}) copy-start(bf16[1536,256]{1,0:T(8,128)(2,1)S(1)} %get-tuple-element.198) | copy-start | bytes 2359300
  234.9 2.1 copy-start.3
  235.4 4.3 copy-start.7
  235.4 4.3 copy-start.29
  235.7 1.3 copy-start.33
  235.7 1.3 copy-start.24
  238.5 1.2 copy-start.31
  247.6 2.3 copy-start.8
  247.6 2.3 copy-start.13
  247.6 2.3 copy-start.25
  247.6 2.3 copy-start.30
  247.6 2.3 copy-start.32
  247.6 2.3 copy-start.35
  251.0 1.4 copy-start.5
  251.0 1.7 copy-start.6
  255.1 2.4 copy-start.28
  285.6 51.7 %copy-start.22 = (bf16[64,256]{1,0:T(8,128)(2,1)S(1)}, bf16[64,256]{1,0:T(8,128)(2,1)}, u32[]{:S(2)}) copy-start(bf16[64,256]{1,0:T(8,128)(2,1)} %psum.22) | copy-start | bytes 98308
  285.6 98.3 %all-to-all-start.1 = ((bf16[8,256,2,256]{3,2,1,0:T(2,128)(2,1)}), bf16[8,256,2,256]{3,2,1,0:T(2,128)(2,1)}, u32[]{:S(2)}, u32[]{:S(2)}) async-start(bf16[8,256,2,256]{3,2,1,0:T(2,128)(2,1)} %convert_element_type.139), calls=%async_computation.1 | async-start | bytes 4194304 | tf_op jit(solution)/shard_map/all_to_all | solution.py:153
  290.1 163.3 %reduce-scatter.2.cloned.1.call-start = ((), (), s32[]{:S(2)}) async-start(), calls=%async_computation.4 | async-start | bytes 2228224 | tf_op jit(solution)/shard_map/reduce_scatter | solution.py:231
  388.9 2.7 copy-start.14
  388.9 2.7 copy-start.20
  394.6 1.1 copy-start.1
  394.6 2.0 copy-start.15
  394.6 2.0 copy-start.21
  396.7 2.8 copy-start.14
  396.7 2.8 copy-start.20
  402.5 1.1 copy-start.1
  402.5 2.0 copy-start.15
  402.5 2.0 copy-start.21
  404.5 2.7 copy-start.14
  404.5 2.7 copy-start.20
  410.3 1.1 copy-start.1
  410.3 2.0 copy-start.15
  410.3 2.0 copy-start.21
  412.3 2.7 copy-start.14
  412.3 2.7 copy-start.20
  418.1 1.1 copy-start.1
  418.1 2.0 copy-start.15
  418.1 2.0 copy-start.21
  420.2 2.8 copy-start.14
  420.2 2.8 copy-start.20
  425.9 1.1 copy-start.1
  425.9 2.0 copy-start.15
  426.0 2.0 copy-start.21
  428.0 2.8 copy-start.14
  428.0 2.8 copy-start.20
  433.8 2.0 copy-start.15
  433.8 2.0 copy-start.21
  435.8 2.8 copy-start.14
  435.8 2.8 copy-start.20
  441.6 2.0 copy-start.15
  441.6 2.0 copy-start.21
  443.6 2.8 copy-start.14
  443.6 2.8 copy-start.20
  449.4 2.0 copy-start.15
  449.4 2.0 copy-start.21
  (18 other events, 15.3 us)
Sparse Core Ops, SparseCore 0:
  9.6 35.8 all-gather.1
  377.5 58.9 reduce-scatter.1
where the time goes:
time: 463 us; the launch traced here: 460 us
  blocking collectives  258 us (56%)
  matrix products  56.7 us (12%)
  other arithmetic  48.9 us (11%)
  local copies, waits for them, and re-layouts  46.5 us (10%)
  waiting for transfers between devices  22.6 us (5%)
  between operations  14.6 us (3%)
  starting transfers between devices  12 us (3%)
    all_gather x1, blocking collectives, moved_globals(): lax.all_gather(glob_g_own, 'ctx', axis=0, tiled=True)  47.1 us
    dot_general x37, matrix products, across(): lax.dot_general(left_op, right_op, (((0,), (0,)), ((), ())), preferred_el...  41.2 us
    all_gather x1, blocking collectives, moved_globals(): lax.all_gather(glob_q_own, 'ctx', axis=0, tiled=True)  39.7 us
    psum x1, blocking collectives, moved_globals(): lax.psum(jnp.concatenate(dquery_parts, axis=1).astype(jnp.bfloat16), 'ctx')  35.7 us
    psum x1, blocking collectives, moved_globals(): lax.psum(jnp.concatenate(attn_parts, axis=1).astype(jnp.bfloat16), 'ctx')  35.3 us
    all_gather x1, blocking collectives, moved_globals(): lax.all_gather(glob_k_own, 'ctx', axis=0, tiled=True)  32.1 us
    all_gather x1, blocking collectives, moved_globals(): lax.all_gather(glob_v_own, 'ctx', axis=0, tiled=True)  31.4 us
    all_gather x1, waiting for transfers between devices, per_device(): full_grad = lax.all_gather(grad_output, 'tp', axis=2, tiled=True)[0]  21.9 us
  transfers between devices with their start and end apart: 4, of which 1 were waited for; matrix products, arithmetic and copies ran while one was open for 19% of the time, Pallas kernels for 0%

commit v1 on v0

v1 whole, which is shorter than its diff:
```python
import functools

import jax
import jax.numpy as jnp
from jax import lax
from jax.experimental import pallas as pl
from jax.experimental.pallas import tpu as pltpu
from jax.sharding import PartitionSpec as P

HD = 128
MASKED = -1e30


def against(left_op, right_op):
    return lax.dot_general(
        left_op, right_op, (((1,), (1,)), ((), ())), preferred_element_type=jnp.float32
    )


def across(left_op, right_op):
    return lax.dot_general(
        left_op, right_op, (((0,), (0,)), ((), ())), preferred_element_type=jnp.float32
    )


def product(left_op, right_op):
    return jnp.dot(left_op, right_op, preferred_element_type=jnp.float32)


def attention_kernel(block_count, *refs):
    query_ref, grad_ref, key_bias_ref, row_bias_ref = refs[:4]
    kv_refs = refs[4 : 4 + block_count]
    attn_ref, dquery_ref = refs[4 + block_count : 6 + block_count]
    part_refs = refs[6 + block_count : 6 + 2 * block_count]
    probs_ref, low_ref = refs[6 + 2 * block_count :]
    block_size, feat_count = query_ref.shape
    score_scale = HD ** (-0.5)
    row_bias = row_bias_ref[...]
    for head in range(feat_count // HD):
        cols = slice(head * HD, (head + 1) * HD)
        vcols = slice(feat_count + head * HD, feat_count + (head + 1) * HD)
        query = query_ref[:, cols]
        grad = grad_ref[:, cols]
        row_max = jnp.full((block_size, 1), MASKED, jnp.float32)
        for block in range(block_count):
            keys = slice(block * block_size, (block + 1) * block_size)
            scores = score_scale * against(query, kv_refs[block][:, cols])
            scores = scores + jnp.maximum(row_bias, key_bias_ref[:, keys])
            probs_ref[:, keys] = scores
            row_max = jnp.maximum(row_max, jnp.max(scores, axis=1, keepdims=True))
        row_total = jnp.zeros((block_size, 1), jnp.float32)
        for block in range(block_count):
            keys = slice(block * block_size, (block + 1) * block_size)
            weights = jnp.exp(probs_ref[:, keys] - row_max)
            probs_ref[:, keys] = weights
            row_total = row_total + jnp.sum(weights, axis=1, keepdims=True)
        inverse = 1.0 / row_total
        attn = jnp.zeros((block_size, HD), jnp.float32)
        for block in range(block_count):
            keys = slice(block * block_size, (block + 1) * block_size)
            probs = probs_ref[:, keys] * inverse
            probs_ref[:, keys] = probs
            low = probs.astype(jnp.bfloat16)
            low_ref[:, keys] = low
            attn = attn + product(low, kv_refs[block][:, vcols])
        attn_low = attn.astype(jnp.bfloat16)
        attn_ref[:, cols] = attn_low
        row_dot = jnp.sum(
            grad.astype(jnp.float32) * attn_low.astype(jnp.float32), axis=1, keepdims=True
        )
        dquery = jnp.zeros((block_size, HD), jnp.float32)
        for block in range(block_count):
            keys = slice(block * block_size, (block + 1) * block_size)
            dprobs = against(grad, kv_refs[block][:, vcols])
            dscore = (probs_ref[:, keys] * (dprobs - row_dot)).astype(jnp.bfloat16)
            dquery = dquery + product(dscore, kv_refs[block][:, cols])
            part_refs[block][:, cols] = (score_scale * across(dscore, query)).astype(jnp.bfloat16)
            part_refs[block][:, vcols] = across(low_ref[:, keys], grad).astype(jnp.bfloat16)
        dquery_ref[:, cols] = (score_scale * dquery).astype(jnp.bfloat16)


def attention_block(query, grad, key_bias, row_bias, kv_blocks):
    block_count = len(kv_blocks)
    block_size, feat_count = query.shape
    key_count = block_count * block_size
    small = jax.ShapeDtypeStruct(query.shape, jnp.bfloat16)
    part = jax.ShapeDtypeStruct((block_size, 2 * feat_count), jnp.bfloat16)
    vmem = pl.BlockSpec(memory_space=pltpu.VMEM)
    flops = 10 * block_size * key_count * feat_count
    out = pl.pallas_call(
        functools.partial(attention_kernel, block_count),
        out_shape=[small, small] + [part] * block_count,
        in_specs=[vmem] * (4 + block_count),
        out_specs=[vmem] * (2 + block_count),
        scratch_shapes=[
            pltpu.VMEM((block_size, key_count), jnp.float32),
            pltpu.VMEM((block_size, key_count), jnp.bfloat16),
        ],
        compiler_params=pltpu.CompilerParams(vmem_limit_bytes=48 * 1024 * 1024),
        cost_estimate=pl.CostEstimate(
            flops=flops,
            bytes_accessed=8 * key_count * feat_count,
            transcendentals=block_size * key_count * feat_count // HD,
        ),
        name="attention",
    )(query, grad, key_bias, row_bias, *kv_blocks)
    return out[0], out[1], out[2:]


def per_device(
    queries, key_heads, value_heads, grad_output, out_weight, block_pattern, global_offsets
):
    block_size = queries.shape[1]
    dp_count, ctx_count, tp_count = (lax.axis_size(name) for name in ("dp", "ctx", "tp"))
    dp_at, ctx_at, tp_at = (lax.axis_index(name) for name in ("dp", "ctx", "tp"))
    inner = 2 if ctx_count % 2 == 0 else 1
    outer = ctx_count // inner
    outer_at, inner_at = ctx_at // inner, ctx_at % inner

    def outer_pairs(step):
        return [
            (o * inner + i, ((o + step) % outer) * inner + i)
            for o in range(outer)
            for i in range(inner)
        ]

    def inner_pairs(step):
        return [
            (o * inner + i, o * inner + (i + step) % inner)
            for o in range(outer)
            for i in range(inner)
        ]

    def shift_pairs(count, step):
        return [(i, (i + step) % count) for i in range(count)]

    kv_own = jnp.concatenate([key_heads[0], value_heads[0]], axis=1)
    grad_own = grad_output[0]
    grad_parts = [grad_own] + [
        lax.ppermute(grad_own, "tp", shift_pairs(tp_count, -step)) for step in range(1, tp_count)
    ]
    kv_columns = [kv_own] + [
        lax.ppermute(kv_own, "ctx", outer_pairs(step)) for step in range(1, outer)
    ]
    kv_blocks, sources = [], []
    for o_step in range(outer):
        for i_step in range(inner):
            block = kv_columns[o_step]
            if i_step:
                block = lax.ppermute(block, "ctx", inner_pairs(i_step))
            kv_blocks.append(block)
            sources.append(
                ((outer_at - o_step) % outer) * inner + (inner_at - i_step) % inner
            )
    sources = jnp.stack(sources)

    positions = jnp.arange(block_size, dtype=jnp.int32)
    glob_flags = jnp.any(global_offsets[:, :, None] == positions[None, None, :], axis=1)
    chosen = block_pattern[ctx_at]
    seen = (jnp.abs(sources - ctx_at) <= 1) | jnp.any(sources[:, None] == chosen[None, :], axis=1)
    key_seen = seen[:, None] | glob_flags[sources]
    key_bias = jnp.where(key_seen, 0.0, MASKED).astype(jnp.float32).reshape(1, -1)
    row_bias = jnp.where(glob_flags[ctx_at], 0.0, MASKED).astype(jnp.float32)[:, None]

    col_count = grad_own.shape[1]
    grad_sum = 0.0
    for step in range(tp_count):
        start = ((tp_at + step) % tp_count) * col_count
        columns = lax.dynamic_slice_in_dim(out_weight, start, col_count, 1)
        grad_sum = grad_sum + against(grad_parts[step], columns)
    grad_heads = grad_sum.astype(jnp.bfloat16)

    attention, dquery, parts = attention_block(
        queries[0], grad_heads, key_bias, row_bias, kv_blocks
    )

    per_dp = tp_count // dp_count

    def dp_columns(which):
        picked = []
        for i in range(per_dp):
            step = (which * per_dp + i - tp_at) % tp_count
            piece = grad_parts[0]
            for k in range(1, tp_count):
                piece = jnp.where(step == k, grad_parts[k], piece)
            picked.append(piece)
        return picked[0] if per_dp == 1 else jnp.concatenate(picked, axis=1)

    weight_sum = across(attention, dp_columns(dp_at))
    for step in range(1, dp_count):
        send = across(attention, dp_columns((dp_at + step) % dp_count)).astype(jnp.bfloat16)
        weight_sum = weight_sum + lax.ppermute(send, "dp", shift_pairs(dp_count, step)).astype(
            jnp.float32
        )
    feat_count = weight_sum.shape[0]
    pieces = weight_sum.reshape(feat_count, outer, inner, -1).transpose(2, 1, 0, 3)
    inner_sum = lax.dynamic_index_in_dim(pieces, inner_at, 0, keepdims=False)
    for step in range(1, inner):
        send = lax.dynamic_index_in_dim(pieces, (inner_at + step) % inner, 0, keepdims=False)
        inner_sum = inner_sum + lax.ppermute(
            send.astype(jnp.bfloat16), "ctx", inner_pairs(step)
        ).astype(jnp.float32)
    grad_weight = lax.dynamic_index_in_dim(inner_sum, outer_at, 0, keepdims=False)
    for step in range(1, outer):
        send = lax.dynamic_index_in_dim(inner_sum, (outer_at + step) % outer, 0, keepdims=False)
        grad_weight = grad_weight + lax.ppermute(
            send.astype(jnp.bfloat16), "ctx", outer_pairs(step)
        ).astype(jnp.float32)

    summed = 0.0
    for o_step in range(outer):
        column = parts[o_step * inner].astype(jnp.float32)
        for i_step in range(1, inner):
            column = column + lax.ppermute(
                parts[o_step * inner + i_step], "ctx", inner_pairs(-i_step)
            ).astype(jnp.float32)
        if o_step:
            column = lax.ppermute(
                column.astype(jnp.bfloat16), "ctx", outer_pairs(-o_step)
            ).astype(jnp.float32)
        summed = summed + column
    grad_keys = summed[:, :feat_count].astype(jnp.bfloat16)
    grad_values = summed[:, feat_count:].astype(jnp.bfloat16)
    return dquery[None], grad_keys[None], grad_values[None], grad_weight.astype(jnp.bfloat16)


def solution(mesh):
    in_specs = (
        P("dp", "ctx", "tp"),
        P("dp", "ctx", "tp"),
        P("dp", "ctx", "tp"),
        P("dp", "ctx", "tp"),
        P("tp", None),
        P(),
        P(),
    )
    out_specs = (
        P("dp", "ctx", "tp"),
        P("dp", "ctx", "tp"),
        P("dp", "ctx", "tp"),
        P("tp", ("dp", "ctx")),
    )
    return jax.shard_map(
        per_device, mesh=mesh, in_specs=in_specs, out_specs=out_specs, check_vma=False
    )
```

time: 463 us -> 122 us (0.26)
  blocking collectives: 258 us -> 0 us
  matrix products: 56.7 us -> 9.88 us
  other arithmetic: 48.9 us -> 9.68 us
  local copies, waits for them, and re-layouts: 46.5 us -> 19.3 us
  starting transfers between devices: 12 us -> 32.2 us
  waiting for transfers between devices: 22.6 us -> 40.5 us
  between operations: 14.6 us -> 0.78 us
  Pallas kernels: 0 us -> 9.04 us
    all_gather x4 -> x0, blocking collectives: 150 us -> none  [the longest x1 47.1 us: moved_globals(): lax.all_gather(glob_g_own, 'ctx', axis=0, tiled=True)]
    psum x3 -> x0, blocking collectives: 88.1 us -> none  [the longest x1 35.7 us: moved_globals(): lax.psum(jnp.concatenate(dquery_parts, axis=1).astype(jnp.bfloat16), 'ctx')]
    ppermute x0 -> x20, waiting for transfers between devices: none -> 40.5 us  [the longest x1 8.9 us: per_device(): lax.ppermute(send.astype(jnp.bfloat16), 'ctx', inner_pairs(step))]
    dot_general x37 -> x2, matrix products: 41.2 us -> 5.73 us  [across(): lax.dot_general(left_op, right_op, (((0,), (0,)), ((), ())), preferred_el...]
    ppermute x0 -> x20, starting transfers between devices: none -> 32.2 us  [the longest x3 12.8 us: per_device(): lax.ppermute(column.astype(jnp.bfloat16), 'ctx', outer_pairs(-o_step))]
    all_gather x1 -> x0, waiting for transfers between devices: 21.9 us -> none  [per_device(): full_grad = lax.all_gather(grad_output, 'tp', axis=2, tiled=True)[0]]
    pmax x1 -> x0, blocking collectives: 19.8 us -> none  [moved_globals(): glob_max = lax.pmax(jnp.max(glob_scores, axis=2), 'ctx')]
    scatter-add x2 -> x0, other arithmetic: 15.7 us -> none  [the longest x1 8.55 us: moved_globals(): send_terms = jnp.zeros((block_count, block_size, 2, feat_count), jnp.floa...]
  transfers between devices with their start and end apart: 4 -> 20, of which waited for: 1 -> 8; matrix products, arithmetic and copies ran while one was open for 19% -> 21% of each run, Pallas kernels for 0% -> 0%
where the time goes in v1:
time: 122 us; the launch traced here: 121 us
  waiting for transfers between devices  40.5 us (33%)
  starting transfers between devices  32.2 us (26%)
  local copies, waits for them, and re-layouts  19.3 us (16%)
  matrix products  9.88 us (8%)
  other arithmetic  9.68 us (8%)
  Pallas kernels  9.04 us (7%)
    ppermute x3, starting transfers between devices, per_device(): lax.ppermute(column.astype(jnp.bfloat16), 'ctx', outer_pairs(-o_step))  12.8 us
    pallas_call x1, Pallas kernels, attention_block(): pl.pallas_call(functools.partial(attention_kernel, block_count), out_shap...  9.04 us
    ppermute x1, waiting for transfers between devices, per_device(): lax.ppermute(send.astype(jnp.bfloat16), 'ctx', inner_pairs(step))  8.9 us
    ppermute x3, waiting for transfers between devices, per_device(): lax.ppermute(send.astype(jnp.bfloat16), 'ctx', outer_pairs(step))  8.58 us
    ppermute x3, waiting for transfers between devices, per_device(): lax.ppermute(kv_own, 'ctx', outer_pairs(step))  8.39 us
    unnamed x34, local copies, waits for them, and re-layouts  7.05 us
    ppermute x4, waiting for transfers between devices, per_device(): lax.ppermute(parts[o_step * inner + i_step], 'ctx', inner_pairs(-i_step))  6.05 us
    ppermute x1, waiting for transfers between devices, per_device(): lax.ppermute(grad_own, 'tp', shift_pairs(tp_count, -step))  5.76 us
  transfers between devices with their start and end apart: 20, of which 8 were waited for; matrix products, arithmetic and copies ran while one was open for 21% of the time, Pallas kernels for 0%

profile of v1, /device:TPU:0, one launch (start us, length us, event | category | flops | bytes accessed | tf_op | source)
XLA Modules:
  0.0 121.3 jit_solution(3621793187128990973)
XLA Ops:
  0.6 0.0 copy-start
  0.6 1.1 pad_maximum_fusion.refs_4_
  1.8 3.0 %collective-permute-start.1 = (bf16[256,512]{1,0:T(8,128)(2,1)S(1)}, bf16[256,512]{1,0:T(8,128)(2,1)S(1)}, u32[]{:S(2)}, u32[]{:S(2)}) collective-permute-start(bf16[256,512]{1,0:T(8,128)(2,1)S(1)} %pad_maximum_fusion.refs_4_), channel_id=1, source_target_pairs={{0,2},{2,0},{4,6},{6,4},{8,10},{10,8},{12,14},{14,12},{1,3},{3,1},... | collective-permute-start | bytes 786440 | tf_op jit(solution)/shard_map/ppermute | solution.py:150
  4.8 1.6 %collective-permute-start.2 = (bf16[256,512]{1,0:T(8,128)(2,1)S(1)}, bf16[256,512]{1,0:T(8,128)(2,1)S(1)}, u32[]{:S(2)}, u32[]{:S(2)}) collective-permute-start(bf16[256,512]{1,0:T(8,128)(2,1)S(1)} %pad_maximum_fusion.refs_4_), channel_id=1, source_target_pairs={{0,4},{2,6},{4,8},{6,10},{8,12},{10,14},{12,0},{14,2},{1,5},{3,7},... | collective-permute-start | bytes 786440 | tf_op jit(solution)/shard_map/ppermute | solution.py:143
  6.4 2.6 %collective-permute-start.4 = (bf16[256,512]{1,0:T(8,128)(2,1)S(1)}, bf16[256,512]{1,0:T(8,128)(2,1)S(1)}, u32[]{:S(2)}, u32[]{:S(2)}) collective-permute-start(bf16[256,512]{1,0:T(8,128)(2,1)S(1)} %pad_maximum_fusion.refs_4_), channel_id=1, source_target_pairs={{0,8},{2,10},{4,12},{6,14},{8,0},{10,2},{12,4},{14,6},{1,9},{3,11}... | collective-permute-start | bytes 786440 | tf_op jit(solution)/shard_map/ppermute | solution.py:143
  9.0 1.3 %collective-permute-start.6 = (bf16[256,512]{1,0:T(8,128)(2,1)S(1)}, bf16[256,512]{1,0:T(8,128)(2,1)S(1)}, u32[]{:S(2)}, u32[]{:S(2)}) collective-permute-start(bf16[256,512]{1,0:T(8,128)(2,1)S(1)} %pad_maximum_fusion.refs_4_), channel_id=1, source_target_pairs={{0,12},{2,14},{4,0},{6,2},{8,4},{10,6},{12,8},{14,10},{1,13},{3,15... | collective-permute-start | bytes 786440 | tf_op jit(solution)/shard_map/ppermute | solution.py:143
  10.3 1.5 %collective-permute-start = (bf16[256,2048]{1,0:T(8,128)(2,1)}, bf16[256,2048]{1,0:T(8,128)(2,1)}, u32[]{:S(2)}, u32[]{:S(2)}) collective-permute-start(bf16[256,2048]{1,0:T(8,128)(2,1)} %bitcast.75), channel_id=1, source_target_pairs={{0,1},{1,0},{2,3},{3,2},{4,5},{5,4},{6,7},{7,6},{8,9},{9,8},{10,11... | collective-permute-start | bytes 3145736 | tf_op jit(solution)/shard_map/ppermute | solution.py:140
  11.8 0.1 stack.62
  11.9 0.8 fusion.17
  12.7 0.6 gather_fusion
  13.3 0.9 fusion.20
  14.2 0.1 stack.53
  14.3 0.1 compare_reduce_fusion
  14.4 0.1 select_bitcast_fusion
  14.5 2.4 %fusion.6 = f32[256,256]{0,1:T(8,128)} fusion(bf16[256,4096]{1,0:T(8,128)(2,1)S(1)} %copy-done, s32[]{:T(128)S(6)} %select_n.174, bf16[1,256,2048]{2,1,0:T(8,128)(2,1)} %param.10), kind=kOutput, calls=%fused_computation.12 | convolution fusion | flops 268435456 | bytes 2359300 | tf_op jit(solution)/shard_map/dot_general | solution.py:15
  16.9 0.5 collective-permute-start.3
  17.4 8.4 %collective-permute-done.4.refs_8_ = bf16[256,512]{1,0:T(8,128)(2,1)S(1)} collective-permute-done((bf16[256,512]{1,0:T(8,128)(2,1)S(1)}, bf16[256,512]{1,0:T(8,128)(2,1)S(1)}, u32[]{:S(2)}, u32[]{:S(2)}) %collective-permute-start.4) | collective-permute-done | bytes 262176 | tf_op jit(solution)/shard_map/ppermute | solution.py:143
  25.8 0.5 collective-permute-start.5
  26.3 0.0 collective-permute-done.6.refs_10_
  26.3 1.5 %collective-permute-start.7 = (bf16[256,512]{1,0:T(8,128)(2,1)S(1)}, bf16[256,512]{1,0:T(8,128)(2,1)}, u32[]{:S(2)}, u32[]{:S(2)}) collective-permute-start(bf16[256,512]{1,0:T(8,128)(2,1)S(1)} %collective-permute-done.6.refs_10_), channel_id=1, source_target_pairs={{0,2},{2,0},{4,6},{6,4},{8,10},{10,8},{12,14},{14,12},{1,3},{3,1},... | collective-permute-start | bytes 786440 | tf_op jit(solution)/shard_map/ppermute | solution.py:150
  27.8 0.8 copy.22.refs_3_
  28.6 5.8 %collective-permute-done = bf16[256,2048]{1,0:T(8,128)(2,1)} collective-permute-done((bf16[256,2048]{1,0:T(8,128)(2,1)}, bf16[256,2048]{1,0:T(8,128)(2,1)}, u32[]{:S(2)}, u32[]{:S(2)}) %collective-permute-start) | collective-permute-done | bytes 1048608 | tf_op jit(solution)/shard_map/ppermute | solution.py:140
  34.4 1.7 %fusion.1.refs_1_ = bf16[256,256]{1,0:T(8,128)(2,1)S(1)} fusion(f32[256,256]{0,1:T(8,128)} %fusion.6, bf16[256,2048]{1,0:T(8,128)(2,1)} %collective-permute-done, bf16[256,4096]{1,0:T(8,128)(2,1)S(1)} %copy-done, s32[]{:T(128)S(6)} %select_n.176), kind=kOutput, calls=%fused_computation.5 | convolution fusion | flops 268566528 | bytes 2490372 | tf_op jit(solution)/shard_map/dot_general | solution.py:15
  36.1 0.0 collective-permute-done.1.refs_5_
  36.2 0.7 copy-done.2
  36.9 2.8 %collective-permute-done.7.refs_11_ = bf16[256,512]{1,0:T(8,128)(2,1)} collective-permute-done((bf16[256,512]{1,0:T(8,128)(2,1)S(1)}, bf16[256,512]{1,0:T(8,128)(2,1)}, u32[]{:S(2)}, u32[]{:S(2)}) %collective-permute-start.7) | collective-permute-done | bytes 262176 | tf_op jit(solution)/shard_map/ppermute | solution.py:150
  39.7 0.9 copy-done.3
  40.6 0.9 copy-done.5
  41.6 0.9 copy-done.7
  42.5 0.9 copy-done.9
  43.5 0.9 copy-done.13
  44.4 9.0 %attention.1 = (bf16[256,256]{1,0:T(8,128)(2,1)S(1)}, bf16[256,256]{1,0:T(8,128)(2,1)}, bf16[256,512]{1,0:T(8,128)(2,1)S(1)}, bf16[256,512]{1,0:T(8,128)(2,1)S(1...) custom-call(bf16[256,256]{1,0:T(8,128)(2,1)S(1)} %bitcast.74, ...), custom_call_target="tpu_custom_call" | custom-call | flops 1342177280 | bytes 4194304 | tf_op jit(solution)/shard_map/attention/pallas_call | solution.py:90
  53.4 0.7 copy-done.10
  54.1 0.7 copy-done.12
  54.9 2.7 %convolution_convert_fusion = bf16[256,2048]{1,0:T(8,128)(2,1)} fusion(bf16[256,256]{1,0:T(8,128)(2,1)S(1)} %get-tuple-element.23, bf16[256,2048]{1,0:T(8,128)(2,1)} %collective-permute-done, pred[]{:T(512)S(6)} %eq.69, bf16[1,256,2048]{2,1,0:T(8,128)(2,1)S(1)} %copy-done.14), kind=kOutput, calls=%fused_computation.2 | convolution fusion | flops 269484032 | bytes 3276801 | tf_op jit(solution)/shard_map/dot_general | solution.py:21
  57.6 0.0 collective-permute-start.15
  57.6 0.5 collective-permute-start.13
  58.1 1.5 %collective-permute-start.11 = (bf16[256,512]{1,0:T(8,128)(2,1)}, bf16[256,512]{1,0:T(8,128)(2,1)}, u32[]{:S(2)}, u32[]{:S(2)}) collective-permute-start(bf16[256,512]{1,0:T(8,128)(2,1)} %get-tuple-element.20), channel_id=1, source_target_pairs={{0,2},{2,0},{4,6},{6,4},{8,10},{10,8},{12,14},{14,12},{1,3},{3,1},... | collective-permute-start | bytes 786440 | tf_op jit(solution)/shard_map/ppermute | solution.py:214
  59.6 0.5 collective-permute-start.9
  60.2 1.5 %collective-permute-start.8 = (bf16[256,512]{1,0:T(8,128)(2,1)S(1)}, bf16[256,512]{1,0:T(8,128)(2,1)}, u32[]{:S(2)}, u32[]{:S(2)}) collective-permute-start(bf16[256,512]{1,0:T(8,128)(2,1)S(1)} %copy-done.11), channel_id=1, source_target_pairs={{0,2},{2,0},{4,6},{6,4},{8,10},{10,8},{12,14},{14,12},{1,3},{3,1},... | collective-permute-start | bytes 786440 | tf_op jit(solution)/shard_map/ppermute | solution.py:214
  61.6 5.4 %collective-permute-done.13 = bf16[256,512]{1,0:T(8,128)(2,1)} collective-permute-done((bf16[256,512]{1,0:T(8,128)(2,1)}, bf16[256,512]{1,0:T(8,128)(2,1)}, u32[]{:S(2)}, u32[]{:S(2)}) %collective-permute-start.13) | collective-permute-done | bytes 262176 | tf_op jit(solution)/shard_map/ppermute | solution.py:214
  67.0 1.7 %add_convert_fusion.1 = bf16[256,512]{1,0:T(8,128)(2,1)} fusion(bf16[256,512]{1,0:T(8,128)(2,1)} %collective-permute-done.13, bf16[256,512]{1,0:T(8,128)(2,1)S(1)} %get-tuple-element.21), kind=kLoop, calls=%fused_computation.18 | loop fusion | flops 524288 | bytes 786432 | tf_op jit(solution)/shard_map/convert_element_type | solution.py:219
  68.7 4.0 %collective-permute-start.14 = (bf16[256,512]{1,0:T(8,128)(2,1)}, bf16[256,512]{1,0:T(8,128)(2,1)}, u32[]{:S(2)}, u32[]{:S(2)}) collective-permute-start(bf16[256,512]{1,0:T(8,128)(2,1)} %add_convert_fusion.1), channel_id=1, source_target_pairs={{0,4},{2,6},{4,8},{6,10},{8,12},{10,14},{12,0},{14,2},{1,5},{3,7},... | collective-permute-start | bytes 786440 | tf_op jit(solution)/shard_map/ppermute | solution.py:218
  72.7 1.7 %add_convert_fusion.2 = bf16[256,512]{1,0:T(8,128)(2,1)} fusion(bf16[256,512]{1,0:T(8,128)(2,1)} %collective-permute-done.11, bf16[256,512]{1,0:T(8,128)(2,1)S(1)} %get-tuple-element.19), kind=kLoop, calls=%fused_computation.19 | loop fusion | flops 524288 | bytes 786432 | tf_op jit(solution)/shard_map/convert_element_type | solution.py:219
  74.5 3.0 %collective-permute-start.12 = (bf16[256,512]{1,0:T(8,128)(2,1)}, bf16[256,512]{1,0:T(8,128)(2,1)}, u32[]{:S(2)}, u32[]{:S(2)}) collective-permute-start(bf16[256,512]{1,0:T(8,128)(2,1)} %add_convert_fusion.2), channel_id=1, source_target_pairs={{0,8},{2,10},{4,12},{6,14},{8,0},{10,2},{12,4},{14,6},{1,9},{3,11}... | collective-permute-start | bytes 786440 | tf_op jit(solution)/shard_map/ppermute | solution.py:218
  77.5 0.7 collective-permute-done.9
  78.1 0.8 add_convert_fusion.3
  78.9 5.8 %collective-permute-start.10 = (bf16[256,512]{1,0:T(8,128)(2,1)}, bf16[256,512]{1,0:T(8,128)(2,1)}, u32[]{:S(2)}, u32[]{:S(2)}) collective-permute-start(bf16[256,512]{1,0:T(8,128)(2,1)} %add_convert_fusion.3), channel_id=1, source_target_pairs={{0,12},{2,14},{4,0},{6,2},{8,4},{10,6},{12,8},{14,10},{1,13},{3,15... | collective-permute-start | bytes 786440 | tf_op jit(solution)/shard_map/ppermute | solution.py:218
  84.8 3.0 %convolution_add_fusion = f32[256,2048]{1,0:T(8,128)} fusion(bf16[256,256]{1,0:T(8,128)(2,1)S(1)} %get-tuple-element.23, bf16[256,2048]{1,0:T(8,128)(2,1)} %collective-permute-done.15, bf16[256,2048]{1,0:T(8,128)(2,1)} %collective-permute-done, pred[]{:T(512)S(6)} %eq.68, bf16[1,256,2048]{2,1,0:T(8,128)(2,1)S(1)} %copy-done.15), kind=kOutput, calls=%fused_computation.1 | convolution fusion | flops 270008320 | bytes 5373953 | tf_op jit(solution)/shard_map/dot_general | solution.py:21
  87.8 4.0 %reshape.440 = f32[256,4,2,256]{3,2,1,0:T(2,128)} reshape(f32[256,2048]{1,0:T(8,128)} %convolution_add_fusion) | data formatting | bytes 4194304 | tf_op jit(solution)/shard_map/reshape | solution.py:196
  91.7 2.5 %constant_dynamic-slice_fusion = bf16[256,4,1,256]{3,2,1,0:T(2,128)(2,1)S(1)} fusion(f32[256,4,2,256]{3,2,1,0:T(2,128)} %reshape.440, s32[]{:T(128)S(6)} %select_n.200), kind=kLoop, calls=%fused_computation.40 | loop fusion | bytes 1048580 | tf_op jit(solution)/shard_map/jit(dynamic_index_in_dim)/dynamic_slice | solution.py:199
  94.3 0.2 copy.36
  94.5 0.6 collective-permute-start.16
  95.1 1.4 %add_convert_fusion = bf16[256,512]{1,0:T(8,128)(2,1)S(1)} fusion(bf16[256,512]{1,0:T(8,128)(2,1)} %collective-permute-done.14, bf16[256,512]{1,0:T(8,128)(2,1)} %collective-permute-done.12, bf16[256,512]{1,0:T(8,128)(2,1)} %collective-permute-done.10, bf16[256,512]{1,0:T(8,128)(2,1)} %collective-permute-done.8, bf16[256,512]{1,0:T(8,128)(2,1)S(1)} %get-tuple-element.15), kind=kLoop, calls=%fused_computation.17 | loop fusion | flops 1310720 | bytes 1572864 | tf_op jit(solution)/shard_map/convert.1
  96.4 2.5 %constant_dynamic-slice_fusion.1 = f32[256,4,1,256]{3,2,1,0:T(1,128)S(1)} fusion(f32[256,4,2,256]{3,2,1,0:T(2,128)} %reshape.440, s32[]{:T(128)S(6)} %select_n.198), kind=kLoop, calls=%fused_computation.41 | loop fusion | bytes 2097156 | tf_op jit(solution)/shard_map/dynamic-slice
  98.9 8.9 %collective-permute-done.16 = bf16[4,256,256]{2,1,0:T(8,128)(2,1)} collective-permute-done((bf16[4,256,256]{2,1,0:T(8,128)(2,1)S(1)}, bf16[4,256,256]{2,1,0:T(8,128)(2,1)}, u32[]{:S(2)}, u32[]{:S(2)}) %collective-permute-start.16) | collective-permute-done | bytes 524320 | tf_op jit(solution)/shard_map/ppermute | solution.py:200
  107.8 1.2 %fusion.2 = f32[4,256,256]{2,1,0:T(8,128)S(1)} fusion(f32[256,4,1,256]{3,2,1,0:T(1,128)S(1)} %constant_dynamic-slice_fusion.1, bf16[4,256,256]{2,1,0:T(8,128)(2,1)} %collective-permute-done.16), kind=kLoop, calls=%fused_computation.8 | loop fusion | flops 524288 | bytes 2621440 | tf_op jit(solution)/shard_map/add | solution.py:200
  109.1 0.1 fusion.14
  109.2 0.3 collective-permute-start.19
  109.5 1.7 %collective-permute-start.17 = (bf16[256,256]{1,0:T(8,128)(2,1)S(1)}, bf16[256,256]{1,0:T(8,128)(2,1)S(1)}, u32[]{:S(2)}, u32[]{:S(2)}) collective-permute-start(bf16[256,256]{1,0:T(8,128)(2,1)S(1)} %get-tuple-element.24), channel_id=1, source_target_pairs={{0,4},{2,6},{4,8},{6,10},{8,12},{10,14},{12,0},{14,2},{1,5},{3,7},... | collective-permute-start | bytes 393224 | tf_op jit(solution)/shard_map/ppermute | solution.py:206
  111.2 0.7 slice_bitcast_fusion
  111.9 3.5 %collective-permute-done.19 = bf16[256,256]{1,0:T(8,128)(2,1)S(1)} collective-permute-done((bf16[256,256]{1,0:T(8,128)(2,1)S(1)}, bf16[256,256]{1,0:T(8,128)(2,1)S(1)}, u32[]{:S(2)}, u32[]{:S(2)}) %collective-permute-start.19) | collective-permute-done | bytes 131104 | tf_op jit(solution)/shard_map/ppermute | solution.py:206
  115.4 5.1 %collective-permute-done.18 = bf16[256,256]{1,0:T(8,128)(2,1)S(1)} collective-permute-done((bf16[256,256]{1,0:T(8,128)(2,1)S(1)}, bf16[256,256]{1,0:T(8,128)(2,1)S(1)}, u32[]{:S(2)}, u32[]{:S(2)}) %collective-permute-start.18) | collective-permute-done | bytes 131104 | tf_op jit(solution)/shard_map/ppermute | solution.py:206
  120.5 0.7 fusion.13
  (39 shorter events, 0.1 us)
Async XLA Ops:
  0.6 13.8 %copy-start = (bf16[256,4096]{1,0:T(8,128)(2,1)S(1)}, bf16[256,4096]{1,0:T(8,128)(2,1)}, u32[]{:S(2)}) copy-start(bf16[256,4096]{1,0:T(8,128)(2,1)} %param.11) | copy-start | bytes 6291460
  1.8 34.4 %collective-permute-start.1 = (bf16[256,512]{1,0:T(8,128)(2,1)S(1)}, bf16[256,512]{1,0:T(8,128)(2,1)S(1)}, u32[]{:S(2)}, u32[]{:S(2)}) collective-permute-start(bf16[256,512]{1,0:T(8,128)(2,1)S(1)} %pad_maximum_fusion.refs_4_), channel_id=1, source_target_pairs={{0,2},{2,0},{4,6},{6,4},{8,10},{10,8},{12,14},{14,12},{1,3},{3,1},... | collective-permute-start | bytes 786440 | tf_op jit(solution)/shard_map/ppermute | solution.py:150
  4.8 12.1 %collective-permute-start.2 = (bf16[256,512]{1,0:T(8,128)(2,1)S(1)}, bf16[256,512]{1,0:T(8,128)(2,1)S(1)}, u32[]{:S(2)}, u32[]{:S(2)}) collective-permute-start(bf16[256,512]{1,0:T(8,128)(2,1)S(1)} %pad_maximum_fusion.refs_4_), channel_id=1, source_target_pairs={{0,4},{2,6},{4,8},{6,10},{8,12},{10,14},{12,0},{14,2},{1,5},{3,7},... | collective-permute-start | bytes 786440 | tf_op jit(solution)/shard_map/ppermute | solution.py:143
  6.4 19.4 %collective-permute-start.4 = (bf16[256,512]{1,0:T(8,128)(2,1)S(1)}, bf16[256,512]{1,0:T(8,128)(2,1)S(1)}, u32[]{:S(2)}, u32[]{:S(2)}) collective-permute-start(bf16[256,512]{1,0:T(8,128)(2,1)S(1)} %pad_maximum_fusion.refs_4_), channel_id=1, source_target_pairs={{0,8},{2,10},{4,12},{6,14},{8,0},{10,2},{12,4},{14,6},{1,9},{3,11}... | collective-permute-start | bytes 786440 | tf_op jit(solution)/shard_map/ppermute | solution.py:143
  9.0 17.4 %collective-permute-start.6 = (bf16[256,512]{1,0:T(8,128)(2,1)S(1)}, bf16[256,512]{1,0:T(8,128)(2,1)S(1)}, u32[]{:S(2)}, u32[]{:S(2)}) collective-permute-start(bf16[256,512]{1,0:T(8,128)(2,1)S(1)} %pad_maximum_fusion.refs_4_), channel_id=1, source_target_pairs={{0,12},{2,14},{4,0},{6,2},{8,4},{10,6},{12,8},{14,10},{1,13},{3,15... | collective-permute-start | bytes 786440 | tf_op jit(solution)/shard_map/ppermute | solution.py:143
  10.3 24.1 %collective-permute-start = (bf16[256,2048]{1,0:T(8,128)(2,1)}, bf16[256,2048]{1,0:T(8,128)(2,1)}, u32[]{:S(2)}, u32[]{:S(2)}) collective-permute-start(bf16[256,2048]{1,0:T(8,128)(2,1)} %bitcast.75), channel_id=1, source_target_pairs={{0,1},{1,0},{2,3},{3,2},{4,5},{5,4},{6,7},{7,6},{8,9},{9,8},{10,11... | collective-permute-start | bytes 3145736 | tf_op jit(solution)/shard_map/ppermute | solution.py:140
  16.9 22.8 %copy-start.4 = (bf16[256,512]{1,0:T(8,128)(2,1)}, bf16[256,512]{1,0:T(8,128)(2,1)S(1)}, u32[]{:S(2)}) copy-start(bf16[256,512]{1,0:T(8,128)(2,1)S(1)} %collective-permute-done.2.refs_6_) | copy-start | bytes 786436
  16.9 20.0 %collective-permute-start.3 = (bf16[256,512]{1,0:T(8,128)(2,1)S(1)}, bf16[256,512]{1,0:T(8,128)(2,1)}, u32[]{:S(2)}, u32[]{:S(2)}) collective-permute-start(bf16[256,512]{1,0:T(8,128)(2,1)S(1)} %collective-permute-done.2.refs_6_), channel_id=1, source_target_pairs={{0,2},{2,0},{4,6},{6,4},{8,10},{10,8},{12,14},{14,12},{1,3},{3,1},... | collective-permute-start | bytes 786440 | tf_op jit(solution)/shard_map/ppermute | solution.py:150
  25.8 13.9 %copy-start.6 = (bf16[256,512]{1,0:T(8,128)(2,1)}, bf16[256,512]{1,0:T(8,128)(2,1)S(1)}, u32[]{:S(2)}) copy-start(bf16[256,512]{1,0:T(8,128)(2,1)S(1)} %collective-permute-done.4.refs_8_) | copy-start | bytes 786436
  25.8 11.1 %collective-permute-start.5 = (bf16[256,512]{1,0:T(8,128)(2,1)S(1)}, bf16[256,512]{1,0:T(8,128)(2,1)}, u32[]{:S(2)}, u32[]{:S(2)}) collective-permute-start(bf16[256,512]{1,0:T(8,128)(2,1)S(1)} %collective-permute-done.4.refs_8_), channel_id=1, source_target_pairs={{0,2},{2,0},{4,6},{6,4},{8,10},{10,8},{12,14},{14,12},{1,3},{3,1},... | collective-permute-start | bytes 786440 | tf_op jit(solution)/shard_map/ppermute | solution.py:150
  26.3 13.3 %copy-start.8 = (bf16[256,512]{1,0:T(8,128)(2,1)}, bf16[256,512]{1,0:T(8,128)(2,1)S(1)}, u32[]{:S(2)}) copy-start(bf16[256,512]{1,0:T(8,128)(2,1)S(1)} %collective-permute-done.6.refs_10_) | copy-start | bytes 786436
  26.3 13.3 %collective-permute-start.7 = (bf16[256,512]{1,0:T(8,128)(2,1)S(1)}, bf16[256,512]{1,0:T(8,128)(2,1)}, u32[]{:S(2)}, u32[]{:S(2)}) collective-permute-start(bf16[256,512]{1,0:T(8,128)(2,1)S(1)} %collective-permute-done.6.refs_10_), channel_id=1, source_target_pairs={{0,2},{2,0},{4,6},{6,4},{8,10},{10,8},{12,14},{14,12},{1,3},{3,1},... | collective-permute-start | bytes 786440 | tf_op jit(solution)/shard_map/ppermute | solution.py:150
  28.6 11.0 %copy-start.1 = (f32[256,1]{1,0:T(8,128)S(1)}, f32[256,1]{1,0:T(8,128)}, u32[]{:S(2)}) copy-start(f32[256,1]{1,0:T(8,128)} %copy.22.refs_3_) | copy-start | bytes 3076
  36.2 0.7 copy-start.2
  39.7 1.0 copy-start.3
  40.6 0.9 copy-start.5
  41.6 0.9 copy-start.7
  42.5 0.9 copy-start.9
  43.5 0.9 copy-start.13
  44.4 10.5 %copy-start.14 = (bf16[1,256,2048]{2,1,0:T(8,128)(2,1)S(1)}, bf16[1,256,2048]{2,1,0:T(8,128)(2,1)}, u32[]{:S(2)}) copy-start(bf16[1,256,2048]{2,1,0:T(8,128)(2,1)} %param.10) | copy-start | bytes 3145732
  53.4 0.7 copy-start.10
  54.1 0.7 copy-start.12
  54.9 5.3 %copy-start.11 = (bf16[256,512]{1,0:T(8,128)(2,1)S(1)}, bf16[256,512]{1,0:T(8,128)(2,1)}, u32[]{:S(2)}) copy-start(bf16[256,512]{1,0:T(8,128)(2,1)} %copy-done.10) | copy-start | bytes 786436
  57.6 27.2 %collective-permute-start.15 = (bf16[256,2048]{1,0:T(8,128)(2,1)}, bf16[256,2048]{1,0:T(8,128)(2,1)}, u32[]{:S(2)}, u32[]{:S(2)}) collective-permute-start(bf16[256,2048]{1,0:T(8,128)(2,1)} %convolution_convert_fusion), channel_id=1, source_target_pairs={{0,16},{16,0},{1,17},{17,1},{2,18},{18,2},{3,19},{19,3},{4,20},{20... | collective-permute-start | bytes 3145736 | tf_op jit(solution)/shard_map/ppermute | solution.py:192
  57.6 9.4 %collective-permute-start.13 = (bf16[256,512]{1,0:T(8,128)(2,1)}, bf16[256,512]{1,0:T(8,128)(2,1)}, u32[]{:S(2)}, u32[]{:S(2)}) collective-permute-start(bf16[256,512]{1,0:T(8,128)(2,1)} %get-tuple-element.22), channel_id=1, source_target_pairs={{0,2},{2,0},{4,6},{6,4},{8,10},{10,8},{12,14},{14,12},{1,3},{3,1},... | collective-permute-start | bytes 786440 | tf_op jit(solution)/shard_map/ppermute | solution.py:214
  58.1 14.6 %collective-permute-start.11 = (bf16[256,512]{1,0:T(8,128)(2,1)}, bf16[256,512]{1,0:T(8,128)(2,1)}, u32[]{:S(2)}, u32[]{:S(2)}) collective-permute-start(bf16[256,512]{1,0:T(8,128)(2,1)} %get-tuple-element.20), channel_id=1, source_target_pairs={{0,2},{2,0},{4,6},{6,4},{8,10},{10,8},{12,14},{14,12},{1,3},{3,1},... | collective-permute-start | bytes 786440 | tf_op jit(solution)/shard_map/ppermute | solution.py:214
  59.6 25.1 %copy-start.15 = (bf16[1,256,2048]{2,1,0:T(8,128)(2,1)S(1)}, bf16[1,256,2048]{2,1,0:T(8,128)(2,1)}, u32[]{:S(2)}) copy-start(bf16[1,256,2048]{2,1,0:T(8,128)(2,1)} %param.10) | copy-start | bytes 3145732
  59.6 18.5 %collective-permute-start.9 = (bf16[256,512]{1,0:T(8,128)(2,1)}, bf16[256,512]{1,0:T(8,128)(2,1)S(1)}, u32[]{:S(2)}, u32[]{:S(2)}) collective-permute-start(bf16[256,512]{1,0:T(8,128)(2,1)} %copy-done.12), channel_id=1, source_target_pairs={{0,2},{2,0},{4,6},{6,4},{8,10},{10,8},{12,14},{14,12},{1,3},{3,1},... | collective-permute-start | bytes 786440 | tf_op jit(solution)/shard_map/ppermute | solution.py:214
  60.2 34.9 %collective-permute-start.8 = (bf16[256,512]{1,0:T(8,128)(2,1)S(1)}, bf16[256,512]{1,0:T(8,128)(2,1)}, u32[]{:S(2)}, u32[]{:S(2)}) collective-permute-start(bf16[256,512]{1,0:T(8,128)(2,1)S(1)} %copy-done.11), channel_id=1, source_target_pairs={{0,2},{2,0},{4,6},{6,4},{8,10},{10,8},{12,14},{14,12},{1,3},{3,1},... | collective-permute-start | bytes 786440 | tf_op jit(solution)/shard_map/ppermute | solution.py:214
  68.7 26.3 %collective-permute-start.14 = (bf16[256,512]{1,0:T(8,128)(2,1)}, bf16[256,512]{1,0:T(8,128)(2,1)}, u32[]{:S(2)}, u32[]{:S(2)}) collective-permute-start(bf16[256,512]{1,0:T(8,128)(2,1)} %add_convert_fusion.1), channel_id=1, source_target_pairs={{0,4},{2,6},{4,8},{6,10},{8,12},{10,14},{12,0},{14,2},{1,5},{3,7},... | collective-permute-start | bytes 786440 | tf_op jit(solution)/shard_map/ppermute | solution.py:218
  74.5 20.6 %collective-permute-start.12 = (bf16[256,512]{1,0:T(8,128)(2,1)}, bf16[256,512]{1,0:T(8,128)(2,1)}, u32[]{:S(2)}, u32[]{:S(2)}) collective-permute-start(bf16[256,512]{1,0:T(8,128)(2,1)} %add_convert_fusion.2), channel_id=1, source_target_pairs={{0,8},{2,10},{4,12},{6,14},{8,0},{10,2},{12,4},{14,6},{1,9},{3,11}... | collective-permute-start | bytes 786440 | tf_op jit(solution)/shard_map/ppermute | solution.py:218
  78.9 16.2 %collective-permute-start.10 = (bf16[256,512]{1,0:T(8,128)(2,1)}, bf16[256,512]{1,0:T(8,128)(2,1)}, u32[]{:S(2)}, u32[]{:S(2)}) collective-permute-start(bf16[256,512]{1,0:T(8,128)(2,1)} %add_convert_fusion.3), channel_id=1, source_target_pairs={{0,12},{2,14},{4,0},{6,2},{8,4},{10,6},{12,8},{14,10},{1,13},{3,15... | collective-permute-start | bytes 786440 | tf_op jit(solution)/shard_map/ppermute | solution.py:218
  94.5 13.4 %collective-permute-start.16 = (bf16[4,256,256]{2,1,0:T(8,128)(2,1)S(1)}, bf16[4,256,256]{2,1,0:T(8,128)(2,1)}, u32[]{:S(2)}, u32[]{:S(2)}) collective-permute-start(bf16[4,256,256]{2,1,0:T(8,128)(2,1)S(1)} %bitcast.76), channel_id=1, source_target_pairs={{0,2},{2,0},{4,6},{6,4},{8,10},{10,8},{12,14},{14,12},{1,3},{3,1},... | collective-permute-start | bytes 1572872 | tf_op jit(solution)/shard_map/ppermute | solution.py:200
  109.2 6.3 %collective-permute-start.19 = (bf16[256,256]{1,0:T(8,128)(2,1)S(1)}, bf16[256,256]{1,0:T(8,128)(2,1)S(1)}, u32[]{:S(2)}, u32[]{:S(2)}) collective-permute-start(bf16[256,256]{1,0:T(8,128)(2,1)S(1)} %get-tuple-element.25), channel_id=1, source_target_pairs={{0,12},{2,14},{4,0},{6,2},{8,4},{10,6},{12,8},{14,10},{1,13},{3,15... | collective-permute-start | bytes 393224 | tf_op jit(solution)/shard_map/ppermute | solution.py:206
  109.5 11.0 %collective-permute-start.18 = (bf16[256,256]{1,0:T(8,128)(2,1)S(1)}, bf16[256,256]{1,0:T(8,128)(2,1)S(1)}, u32[]{:S(2)}, u32[]{:S(2)}) collective-permute-start(bf16[256,256]{1,0:T(8,128)(2,1)S(1)} %get-tuple-element.26), channel_id=1, source_target_pairs={{0,8},{2,10},{4,12},{6,14},{8,0},{10,2},{12,4},{14,6},{1,9},{3,11}... | collective-permute-start | bytes 393224 | tf_op jit(solution)/shard_map/ppermute | solution.py:206
  109.5 11.0 %collective-permute-start.17 = (bf16[256,256]{1,0:T(8,128)(2,1)S(1)}, bf16[256,256]{1,0:T(8,128)(2,1)S(1)}, u32[]{:S(2)}, u32[]{:S(2)}) collective-permute-start(bf16[256,256]{1,0:T(8,128)(2,1)S(1)} %get-tuple-element.24), channel_id=1, source_target_pairs={{0,4},{2,6},{4,8},{6,10},{8,12},{10,14},{12,0},{14,2},{1,5},{3,7},... | collective-permute-start | bytes 393224 | tf_op jit(solution)/shard_map/ppermute | solution.py:206

commit v2 on v1

v2 whole, which is shorter than its diff:
```python
import functools

import jax
import jax.numpy as jnp
from jax import lax
from jax.experimental import pallas as pl
from jax.experimental.pallas import tpu as pltpu
from jax.sharding import PartitionSpec as P

HD = 128
MASKED = -1e30
INNER = 2
ANY = pl.BlockSpec(memory_space=pl.ANY)
VMEM = pl.BlockSpec(memory_space=pltpu.VMEM)
SMEM = pl.BlockSpec(memory_space=pltpu.SMEM)


def against(left_op, right_op):
    return lax.dot_general(
        left_op, right_op, (((1,), (1,)), ((), ())), preferred_element_type=jnp.float32
    )


def product(left_op, right_op):
    return jnp.dot(left_op, right_op, preferred_element_type=jnp.float32)


def begin(source, target, semaphore):
    copy = pltpu.make_async_copy(source, target, semaphore)
    copy.start()
    return copy


def call(kernel, out_shape, in_specs, out_specs, scratch, flops, moved, name):
    return pl.pallas_call(
        kernel,
        out_shape=out_shape,
        in_specs=in_specs,
        out_specs=out_specs,
        scratch_shapes=scratch,
        compiler_params=pltpu.CompilerParams(vmem_limit_bytes=40 * 1024 * 1024),
        cost_estimate=pl.CostEstimate(flops=flops, bytes_accessed=moved, transcendentals=0),
        name=name,
    )


def bf16(*shape):
    return jax.ShapeDtypeStruct(shape, jnp.bfloat16)


def part_kernel(at_ref, q_ref, k_ref, v_ref, kv_mine, kv_theirs, q_mine, q_theirs):
    width = q_mine.shape[1]
    mine = pl.ds(pl.multiple_of(at_ref[0] * width, width), width)
    theirs = pl.ds(pl.multiple_of((1 - at_ref[0]) * width, width), width)
    for cols, kv_out, q_out in ((mine, kv_mine, q_mine), (theirs, kv_theirs, q_theirs)):
        kv_out[:, :width] = k_ref[:, cols]
        kv_out[:, width:] = v_ref[:, cols]
        q_out[...] = q_ref[:, cols]


def part_heads(at, queries, keys, values):
    rows, feats = queries.shape
    half = feats // INNER
    return call(
        part_kernel,
        [bf16(rows, 2 * half), bf16(rows, 2 * half), bf16(rows, half), bf16(rows, half)],
        [SMEM] + [VMEM] * 3,
        [VMEM] * 4,
        [],
        0,
        12 * rows * feats,
        "part_heads",
    )(at, queries, keys, values)


def forward_kernel(block_count, head_count, *refs):
    q_mine, q_recv, key_bias, row_bias = refs[:4]
    kv_refs = refs[4 : 4 + block_count]
    e_out, inv_out, attn_mine, attn_theirs = refs[4 + block_count : 8 + block_count]
    kv_s, e_s, s_ref, kv_sem, e_sem = refs[8 + block_count :]
    rows = q_mine.shape[0]
    feats = head_count * HD
    score_scale = HD ** (-0.5)
    loads = [begin(kv_refs[j], kv_s.at[j], kv_sem.at[j]) for j in range(block_count)]
    stores = []
    for head in range(head_count):
        cols = slice(head * HD, (head + 1) * HD)
        vcols = slice(feats + head * HD, feats + (head + 1) * HD)
        q_t = jnp.concatenate(
            [jnp.transpose(q_mine[:, cols]), jnp.transpose(q_recv[:, cols])], axis=1
        )
        tops = [jnp.full((1, rows), MASKED, jnp.float32) for _ in range(2)]
        for j in range(block_count):
            if head == 0:
                loads[j].wait()
            scores = product(kv_s[j][:, cols], q_t)
            keys = slice(j * rows, (j + 1) * rows)
            for group in range(2):
                half = slice(group * rows, (group + 1) * rows)
                biased = scores[:, half] + jnp.maximum(
                    key_bias[keys, group : group + 1], row_bias[:, half]
                )
                s_ref[keys, half] = biased
                tops[group] = jnp.maximum(tops[group], jnp.max(biased, axis=0, keepdims=True))
        top = jnp.concatenate(tops, axis=1)
        total = jnp.zeros((1, 2 * rows), jnp.float32)
        attn_t = jnp.zeros((HD, 2 * rows), jnp.float32)
        for j in range(block_count):
            keys = slice(j * rows, (j + 1) * rows)
            weights = jnp.exp((s_ref[keys, :] - top) * score_scale)
            total = total + jnp.sum(weights, axis=0, keepdims=True)
            low = weights.astype(jnp.bfloat16)
            e_s[head, keys, :] = low
            stores.append(
                begin(e_s.at[head, keys], e_out.at[head, keys], e_sem.at[head * block_count + j])
            )
            attn_t = attn_t + product(jnp.transpose(kv_s[j][:, vcols]), low)
        inverse = 1.0 / total
        inv_out[head : head + 1, :] = inverse
        attn_low = (attn_t * inverse).astype(jnp.bfloat16)
        attn_mine[cols, :] = attn_low[:, :rows]
        attn_theirs[cols, :] = attn_low[:, rows:]
    for store in stores:
        store.wait()


def forward(q_mine, q_recv, key_bias, row_bias, kv_blocks):
    block_count = len(kv_blocks)
    rows, feats = q_mine.shape
    heads = feats // HD
    keys = block_count * rows
    return call(
        functools.partial(forward_kernel, block_count, heads),
        [
            bf16(heads, keys, 2 * rows),
            jax.ShapeDtypeStruct((heads, 2 * rows), jnp.float32),
            bf16(feats, rows),
            bf16(feats, rows),
        ],
        [VMEM] * 4 + [ANY] * block_count,
        [ANY] + [VMEM] * 3,
        [
            pltpu.VMEM((block_count, rows, 2 * feats), jnp.bfloat16),
            pltpu.VMEM((heads, keys, 2 * rows), jnp.bfloat16),
            pltpu.VMEM((keys, 2 * rows), jnp.float32),
            pltpu.SemaphoreType.DMA((block_count,)),
            pltpu.SemaphoreType.DMA((heads * block_count,)),
        ],
        8 * rows * keys * feats,
        8 * keys * feats + 4 * heads * keys * rows,
        "forward",
    )(q_mine, q_recv, key_bias, row_bias, *kv_blocks)


def backward_kernel(block_count, head_count, *refs):
    q_mine, q_recv, g_mine, g_recv, attn_mine, attn_theirs, inv_ref = refs[:7]
    e_ref = refs[7]
    kv_refs = refs[8 : 8 + block_count]
    outer = block_count // INNER
    dq_mine, dq_theirs = refs[8 + block_count : 10 + block_count]
    part_outs = refs[10 + block_count : 10 + block_count + outer]
    kv_s, e_s, part_s, kv_sem, e_sem, part_sem = refs[10 + block_count + outer :]
    rows = q_mine.shape[0]
    feats = head_count * HD
    score_scale = HD ** (-0.5)
    kv_loads, e_loads = [], {}
    for j in range(block_count):
        keys = slice(j * rows, (j + 1) * rows)
        kv_loads.append(begin(kv_refs[j], kv_s.at[j], kv_sem.at[j]))
        for head in range(head_count):
            e_loads[head, j] = begin(
                e_ref.at[head, keys], e_s.at[head, keys], e_sem.at[head * block_count + j]
            )
    for head in range(head_count):
        cols = slice(head * HD, (head + 1) * HD)
        vcols = slice(feats + head * HD, feats + (head + 1) * HD)
        inverse = inv_ref[head : head + 1, :]
        g_t = jnp.concatenate([g_mine[cols, :], g_recv[cols, :]], axis=1).astype(jnp.float32)
        attn_t = jnp.concatenate([attn_mine[cols, :], attn_theirs[cols, :]], axis=1)
        row_dot = jnp.sum(g_t * attn_t.astype(jnp.float32), axis=0, keepdims=True) * inverse
        g_t = (g_t * inverse).astype(jnp.bfloat16)
        grad = jnp.transpose(g_t)
        query = jnp.concatenate([q_mine[:, cols], q_recv[:, cols]], axis=0)
        dq_t = jnp.zeros((HD, 2 * rows), jnp.float32)
        for j in range(block_count):
            keys = slice(j * rows, (j + 1) * rows)
            if head == 0:
                kv_loads[j].wait()
            e_loads[head, j].wait()
            low = e_s[head, keys, :]
            dprobs = product(kv_s[j][:, vcols], g_t)
            dscore = (low.astype(jnp.float32) * (dprobs - row_dot)).astype(jnp.bfloat16)
            dq_t = dq_t + product(jnp.transpose(kv_s[j][:, cols]), dscore)
            part_s[j, :, cols] = (score_scale * product(dscore, query)).astype(jnp.bfloat16)
            part_s[j, :, vcols] = product(low, grad).astype(jnp.bfloat16)
        dquery = (score_scale * jnp.transpose(dq_t)).astype(jnp.bfloat16)
        dq_mine[:, cols] = dquery[:rows]
        dq_theirs[:, cols] = dquery[rows:]
    stores = []
    for j in range(block_count):
        target = part_outs[j // INNER].at[j % INNER]
        stores.append(begin(part_s.at[j], target, part_sem.at[j]))
    for store in stores:
        store.wait()


def backward(q_mine, q_recv, g_mine, g_recv, attn_mine, attn_theirs, inverse, weights, kv_blocks):
    block_count = len(kv_blocks)
    rows, feats = q_mine.shape
    heads = feats // HD
    keys = block_count * rows
    outer = block_count // INNER
    out = call(
        functools.partial(backward_kernel, block_count, heads),
        [bf16(rows, feats)] * 2 + [bf16(INNER, rows, 2 * feats)] * outer,
        [VMEM] * 7 + [ANY] * (1 + block_count),
        [VMEM] * 2 + [ANY] * outer,
        [
            pltpu.VMEM((block_count, rows, 2 * feats), jnp.bfloat16),
            pltpu.VMEM((heads, keys, 2 * rows), jnp.bfloat16),
            pltpu.VMEM((block_count, rows, 2 * feats), jnp.bfloat16),
            pltpu.SemaphoreType.DMA((block_count,)),
            pltpu.SemaphoreType.DMA((heads * block_count,)),
            pltpu.SemaphoreType.DMA((block_count,)),
        ],
        16 * rows * keys * feats,
        16 * keys * feats + 4 * heads * keys * rows,
        "backward",
    )(q_mine, q_recv, g_mine, g_recv, attn_mine, attn_theirs, inverse, weights, *kv_blocks)
    return out[0], out[1], out[2:]


def grad_heads_kernel(part_count, *refs):
    at_ref, first_ref = refs[:2]
    grads = refs[2 : 2 + part_count]
    columns = refs[2 + part_count : 2 + 2 * part_count]
    mine, theirs, total = refs[2 + 2 * part_count :]
    half = mine.shape[0]
    summed = first_ref[...]
    for k in range(part_count):
        summed = summed + against(columns[k][...], grads[k][...])
    total[...] = summed
    mine[...] = total[pl.ds(pl.multiple_of(at_ref[0] * half, half), half), :].astype(jnp.bfloat16)
    theirs[...] = total[pl.ds(pl.multiple_of((1 - at_ref[0]) * half, half), half), :].astype(
        jnp.bfloat16
    )


def grad_heads(at, first, grads, columns):
    feats, rows = first.shape
    half = feats // INNER
    count = len(grads)
    width = sum(grad.shape[1] for grad in grads)
    return call(
        functools.partial(grad_heads_kernel, count),
        [bf16(half, rows), bf16(half, rows)],
        [SMEM] + [VMEM] * (1 + 2 * count),
        [VMEM] * 2,
        [pltpu.VMEM((feats, rows), jnp.float32)],
        2 * feats * rows * width,
        2 * (feats + rows) * width,
        "grad_heads",
    )(at, first, *grads, *columns)


def weight_kernel(part_count, picked, doc_count, *refs):
    at_ref = refs[0]
    attn = refs[1 : 1 + INNER * doc_count]
    refs = refs[1 + INNER * doc_count :]
    grads, refs = refs[:part_count], refs[part_count:]
    swapped, refs = refs[: doc_count - 1], refs[doc_count - 1 :]
    keep_out, send_out, attn_s, grad_s, send_s, attn_sem, grad_sem, send_sem = refs
    inner_at, outer_at = at_ref[0], at_ref[1]
    outer, feats, width = send_out.shape
    half = feats // INNER
    rows = grads[0].shape[0]
    loads = []
    for doc in range(doc_count):
        for side in range(INNER):
            at = (1 - inner_at) if side else inner_at
            index = doc * INNER + side
            target = attn_s.at[doc, pl.ds(pl.multiple_of(at * half, half), half)]
            loads.append(begin(attn[index], target, attn_sem.at[index]))
    piece = grads[0].shape[1]
    for i in range(picked):
        cols = slice(i * piece, (i + 1) * piece)
        for k in range(part_count):

            @pl.when(at_ref[2 + i] == k)
            def _():
                begin(grads[k], grad_s.at[0, :, cols], grad_sem.at[i])

        loads.append(pltpu.make_async_copy(grads[0], grad_s.at[0, :, cols], grad_sem.at[i]))
    for doc in range(1, doc_count):
        loads.append(begin(swapped[doc - 1], grad_s.at[doc], grad_sem.at[picked + doc - 1]))
    for load in loads:
        load.wait()
    stores = []
    for side in (1, 0):
        at = (1 - inner_at) if side else inner_at
        for k in range(outer):
            place = lax.rem(outer_at + k, outer) * INNER + at
            cols = pl.ds(pl.multiple_of(place * width, width), width)
            term = product(attn_s[0], grad_s[0, :, cols])
            for doc in range(1, doc_count):
                term = term + product(attn_s[doc], grad_s[doc, :, cols])
            if side:
                send_s[k] = term.astype(jnp.bfloat16)
                stores.append(begin(send_s.at[k], send_out.at[k], send_sem.at[k]))
            else:
                keep_out[k] = term
    for store in stores:
        store.wait()


def weight_terms(at, attn, grads, swapped, outer, picked):
    half, rows = attn[0].shape
    feats = half * INNER
    doc_count = len(attn) // INNER
    columns = picked * grads[0].shape[1]
    width = columns // (outer * INNER)
    return call(
        functools.partial(weight_kernel, len(grads), picked, doc_count),
        [jax.ShapeDtypeStruct((outer, feats, width), jnp.float32), bf16(outer, feats, width)],
        [SMEM] + [ANY] * (len(attn) + len(grads) + len(swapped)),
        [VMEM, ANY],
        [
            pltpu.VMEM((doc_count, feats, rows), jnp.bfloat16),
            pltpu.VMEM((doc_count, rows, columns), jnp.bfloat16),
            pltpu.VMEM((outer, feats, width), jnp.bfloat16),
            pltpu.SemaphoreType.DMA((len(attn),)),
            pltpu.SemaphoreType.DMA((picked + doc_count - 1,)),
            pltpu.SemaphoreType.DMA((outer,)),
        ],
        2 * doc_count * feats * rows * columns,
        2 * doc_count * rows * columns + 6 * feats * columns // INNER,
        "weight_terms",
    )(at, *attn, *grads, *swapped)


def join_kernel(at_ref, mine, recv, dq_mine, dq_recv, grad_q, grad_k, grad_v):
    width = dq_mine.shape[1]
    here = pl.ds(pl.multiple_of(at_ref[0] * width, width), width)
    there = pl.ds(pl.multiple_of((1 - at_ref[0]) * width, width), width)
    for cols, terms, dquery in ((here, mine, dq_mine), (there, recv, dq_recv)):
        grad_k[:, cols] = terms[:, :width]
        grad_v[:, cols] = terms[:, width:]
        grad_q[:, cols] = dquery[...]


def join_heads(at, mine, recv, dq_mine, dq_recv):
    rows, half = dq_mine.shape
    return call(
        join_kernel,
        [bf16(rows, INNER * half)] * 3,
        [SMEM] + [VMEM] * 4,
        [VMEM] * 3,
        [],
        0,
        12 * rows * half * INNER,
        "join_heads",
    )(at, mine, recv, dq_mine, dq_recv)


def per_device(
    queries, key_heads, value_heads, grad_output, out_weight, block_pattern, global_offsets
):
    rows = queries.shape[1]
    dp_count, ctx_count, tp_count = (lax.axis_size(name) for name in ("dp", "ctx", "tp"))
    dp_at, ctx_at, tp_at = (lax.axis_index(name) for name in ("dp", "ctx", "tp"))
    outer = ctx_count // INNER
    outer_at, inner_at = ctx_at // INNER, ctx_at % INNER
    at = jnp.stack([inner_at, outer_at])

    swap = [(i, i ^ 1) for i in range(ctx_count)]

    def outer_pairs(step):
        return [(i, (i + step * INNER) % ctx_count) for i in range(ctx_count)]

    def shift_pairs(count, step):
        return [(i, (i + step) % count) for i in range(count)]

    grad_own = grad_output[0]
    grads = [grad_own] + [
        lax.ppermute(grad_own, "tp", shift_pairs(tp_count, -step)) for step in range(1, tp_count)
    ]

    kv_mine, kv_theirs, q_mine, q_theirs = part_heads(at, queries[0], key_heads[0], value_heads[0])
    kv_recv = lax.ppermute(kv_theirs, "ctx", swap)
    q_recv = lax.ppermute(q_theirs, "ctx", swap)
    kv_blocks, sources = [], []
    for step in range(outer):
        for side, held in enumerate((kv_mine, kv_recv)):
            kv_blocks.append(lax.ppermute(held, "ctx", outer_pairs(step)) if step else held)
            sources.append(((outer_at - step) % outer) * INNER + (inner_at + side) % INNER)
    sources = jnp.stack(sources)

    positions = jnp.arange(rows, dtype=jnp.int32)
    glob_flags = jnp.any(global_offsets[:, :, None] == positions[None, None, :], axis=1)
    both = jnp.stack([ctx_at, ctx_at ^ 1])
    chosen = block_pattern[both]
    seen = (jnp.abs(sources[:, None] - both[None, :]) <= 1) | jnp.any(
        sources[:, None, None] == chosen[None], axis=2
    )
    key_seen = seen[:, None, :] | glob_flags[sources][:, :, None]
    key_bias = jnp.where(key_seen, 0.0, MASKED).astype(jnp.float32).reshape(-1, 2)
    row_bias = jnp.where(glob_flags[both], 0.0, MASKED).astype(jnp.float32).reshape(1, -1)

    width = grad_own.shape[1]
    columns = [
        lax.dynamic_slice_in_dim(out_weight, ((tp_at + step) % tp_count) * width, width, 1)
        for step in range(tp_count)
    ]
    first = against(columns[0], grad_own)
    g_mine, g_theirs = grad_heads(at, first, grads[1:], columns[1:])
    g_recv = lax.ppermute(g_theirs, "ctx", swap)

    picked = tp_count // dp_count

    def dp_steps(which):
        return [(which * picked + i - tp_at) % tp_count for i in range(picked)]

    def dp_columns(which):
        pieces = []
        for step in dp_steps(which):
            piece = grads[0]
            for k in range(1, tp_count):
                piece = jnp.where(step == k, grads[k], piece)
            pieces.append(piece)
        return pieces[0] if picked == 1 else jnp.concatenate(pieces, axis=1)

    swapped = [
        lax.ppermute(dp_columns((dp_at + step) % dp_count), "dp", shift_pairs(dp_count, step))
        for step in range(1, dp_count)
    ]

    weights, inverse, attn_mine, attn_theirs = forward(
        q_mine, q_recv, key_bias, row_bias, kv_blocks
    )

    attn = []
    for step in range(dp_count):
        for held, side in ((attn_mine, 0), (attn_theirs, 1)):
            pairs = [
                (d * ctx_count + c, ((d + step) % dp_count) * ctx_count + (c ^ side))
                for d in range(dp_count)
                for c in range(ctx_count)
            ]
            attn.append(lax.ppermute(held, ("dp", "ctx"), pairs) if step or side else held)
    weight_at = jnp.stack([inner_at, outer_at] + dp_steps(dp_at))
    keep, send = weight_terms(weight_at, attn, grads, swapped, outer, picked)
    weight_sum = keep + lax.ppermute(send, "ctx", swap).astype(jnp.float32)
    grad_weight = weight_sum[0]
    for step in range(1, outer):
        grad_weight = grad_weight + lax.ppermute(
            weight_sum[step].astype(jnp.bfloat16), "ctx", outer_pairs(step)
        ).astype(jnp.float32)

    dq_mine, dq_theirs, parts = backward(
        q_mine, q_recv, g_mine, g_recv, attn_mine, attn_theirs, inverse, weights, kv_blocks
    )
    dq_recv = lax.ppermute(dq_theirs, "ctx", swap)
    summed = parts[0].astype(jnp.float32)
    for step in range(1, outer):
        summed = summed + lax.ppermute(parts[step], "ctx", outer_pairs(-step)).astype(jnp.float32)
    summed = summed.astype(jnp.bfloat16)
    terms_recv = lax.ppermute(summed[1], "ctx", swap)
    grad_q, grad_k, grad_v = join_heads(at, summed[0], terms_recv, dq_mine, dq_recv)
    return grad_q[None], grad_k[None], grad_v[None], grad_weight.astype(jnp.bfloat16)


def solution(mesh):
    in_specs = (
        P("dp", "ctx", "tp"),
        P("dp", "ctx", "tp"),
        P("dp", "ctx", "tp"),
        P("dp", "ctx", "tp"),
        P("tp", None),
        P(),
        P(),
    )
    out_specs = (
        P("dp", "ctx", "tp"),
        P("dp", "ctx", "tp"),
        P("dp", "ctx", "tp"),
        P("tp", ("dp", "ctx")),
    )
    return jax.shard_map(
        per_device, mesh=mesh, in_specs=in_specs, out_specs=out_specs, check_vma=False
    )
```

time: 122 us -> 129 us (1.057)
  Pallas kernels: 9.04 us -> 22.9 us
  waiting for transfers between devices: 40.5 us -> 50.6 us
  matrix products: 9.88 us -> 0.47 us
  local copies, waits for them, and re-layouts: 19.3 us -> 15.7 us
  starting transfers between devices: 32.2 us -> 29.4 us
  other arithmetic: 9.68 us -> 8.27 us
    pallas_call x1 -> x6, Pallas kernels: 9.04 us -> 22.9 us  [the longest x1 7.32 us: backward(): call(functools.partial(backward_kernel, block_count, heads), [bf16(rows,...]
    ppermute x1, waiting for transfers between devices: 5.76 us -> 19.5 us  [per_device(): lax.ppermute(grad_own, 'tp', shift_pairs(tp_count, -step))]
    dot_general x2 -> x0, matrix products: 5.73 us -> none  [across(): lax.dot_general(left_op, right_op, (((0,), (0,)), ((), ())), preferred_el...]
    unnamed x34 -> x46, local copies, waits for them, and re-layouts: 7.05 us -> 11.8 us
    reshape x1 -> x0, local copies, waits for them, and re-layouts: 3.98 us -> none  [per_device(): weight_sum.reshape(feat_count, outer, inner, -1).transpose(2, 1, 0, 3)]
    dot_general x2 -> x1, matrix products: 4.15 us -> 0.47 us  [against(): lax.dot_general(left_op, right_op, (((1,), (1,)), ((), ())), preferred_el...]
    ppermute x19 -> x22, waiting for transfers between devices: 34.7 us -> 31.1 us  [the longest x1 8.58 us: per_device(): weight_sum = keep + lax.ppermute(send, 'ctx', swap).astype(jnp.float32)]
    convert_element_type x3 -> x1, other arithmetic: 4.23 us -> 1.24 us  [per_device(): summed = summed.astype(jnp.bfloat16)]
  transfers between devices with their start and end apart: 20 -> 23, of which waited for: 8 -> 9; matrix products, arithmetic and copies ran while one was open for 21% -> 10% of each run, Pallas kernels for 0% -> 17%
where the time goes in v2:
time: 129 us; the launch traced here: 128 us
  waiting for transfers between devices  50.6 us (39%)
  starting transfers between devices  29.4 us (23%)
  Pallas kernels  22.9 us (18%)
  local copies, waits for them, and re-layouts  15.7 us (12%)
  other arithmetic  8.27 us (6%)
    ppermute x1, waiting for transfers between devices, per_device(): lax.ppermute(grad_own, 'tp', shift_pairs(tp_count, -step))  19.5 us
    unnamed x46, local copies, waits for them, and re-layouts  11.8 us
    ppermute x6, starting transfers between devices, per_device(): lax.ppermute(held, 'ctx', outer_pairs(step))  10.8 us
    ppermute x1, waiting for transfers between devices, per_device(): weight_sum = keep + lax.ppermute(send, 'ctx', swap).astype(jnp.float32)  8.58 us
    pallas_call x1, Pallas kernels, backward(): call(functools.partial(backward_kernel, block_count, heads), [bf16(rows,...  7.32 us
    pallas_call x1, Pallas kernels, forward(): call(functools.partial(forward_kernel, block_count, heads), [bf16(heads,...  6.1 us
    ppermute x1, waiting for transfers between devices, per_device(): kv_recv = lax.ppermute(kv_theirs, 'ctx', swap)  5.69 us
    ppermute x3, starting transfers between devices, per_device(): lax.ppermute(parts[step], 'ctx', outer_pairs(-step)).astype(jnp.float32)  5.07 us
  transfers between devices with their start and end apart: 23, of which 9 were waited for; matrix products, arithmetic and copies ran while one was open for 10% of the time, Pallas kernels for 17%

profile of v2, /device:TPU:0, one launch (start us, length us, event | category | flops | bytes accessed | tf_op | source)
XLA Modules:
  0.0 128.1 jit_solution(8791912047205281868)
XLA Ops:
  0.8 1.1 copy-done.3
  1.8 0.9 copy-done.4
  2.7 0.9 copy-done.5
  3.6 1.2 part_heads.1
  4.9 0.6 copy-done.6
  5.5 0.7 copy-done.12
  6.1 3.0 %collective-permute-start.4 = (bf16[256,256]{1,0:T(8,128)(2,1)S(1)}, bf16[256,256]{1,0:T(8,128)(2,1)}, u32[]{:S(2)}, u32[]{:S(2)}) collective-permute-start(bf16[256,256]{1,0:T(8,128)(2,1)S(1)} %get-tuple-element.29.refs_4_.refs_8_), channel_id=1, source_target_pairs={{0,4},{2,6},{4,8},{6,10},{8,12},{10,14},{12,0},{14,2},{1,5},{3,7},... | collective-permute-start | bytes 393224 | tf_op jit(solution)/shard_map/ppermute | solution.py:394
  9.2 2.6 %collective-permute-start.6 = (bf16[256,256]{1,0:T(8,128)(2,1)S(1)}, bf16[256,256]{1,0:T(8,128)(2,1)}, u32[]{:S(2)}, u32[]{:S(2)}) collective-permute-start(bf16[256,256]{1,0:T(8,128)(2,1)S(1)} %get-tuple-element.29.refs_4_.refs_8_), channel_id=1, source_target_pairs={{0,8},{2,10},{4,12},{6,14},{8,0},{10,2},{12,4},{14,6},{1,9},{3,11}... | collective-permute-start | bytes 393224 | tf_op jit(solution)/shard_map/ppermute | solution.py:394
  11.8 1.3 %collective-permute-start.8 = (bf16[256,256]{1,0:T(8,128)(2,1)S(1)}, bf16[256,256]{1,0:T(8,128)(2,1)}, u32[]{:S(2)}, u32[]{:S(2)}) collective-permute-start(bf16[256,256]{1,0:T(8,128)(2,1)S(1)} %get-tuple-element.29.refs_4_.refs_8_), channel_id=1, source_target_pairs={{0,12},{2,14},{4,0},{6,2},{8,4},{10,6},{12,8},{14,10},{1,13},{3,15... | collective-permute-start | bytes 393224 | tf_op jit(solution)/shard_map/ppermute | solution.py:394
  13.1 1.5 %collective-permute-start = (bf16[256,128]{1,0:T(8,128)(2,1)}, bf16[256,128]{1,0:T(8,128)(2,1)}, u32[]{:S(2)}, u32[]{:S(2)}) collective-permute-start(bf16[256,128]{1,0:T(8,128)(2,1)} %get-tuple-element.26), channel_id=1, source_target_pairs={{0,2},{2,0},{4,6},{6,4},{8,10},{10,8},{12,14},{14,12},{1,3},{3,1},... | collective-permute-start | bytes 196616 | tf_op jit(solution)/shard_map/ppermute | solution.py:390
  14.6 1.5 %collective-permute-start.1 = (bf16[256,2048]{1,0:T(8,128)(2,1)}, bf16[256,2048]{1,0:T(8,128)(2,1)}, u32[]{:S(2)}, u32[]{:S(2)}) collective-permute-start(bf16[256,2048]{1,0:T(8,128)(2,1)} %bitcast.65), channel_id=1, source_target_pairs={{0,1},{1,0},{2,3},{3,2},{4,5},{5,4},{6,7},{7,6},{8,9},{9,8},{10,11... | collective-permute-start | bytes 3145736 | tf_op jit(solution)/shard_map/ppermute | solution.py:385
  16.2 0.8 fusion.7
  17.0 0.6 gather_fusion.2
  17.6 1.1 constant_dynamic-slice_fusion.refs_3_
  18.7 0.5 fusion.refs_1_
  19.2 19.5 %collective-permute-done.1.refs_2_.refs_6_ = bf16[256,2048]{1,0:T(8,128)(2,1)} collective-permute-done((bf16[256,2048]{1,0:T(8,128)(2,1)}, bf16[256,2048]{1,0:T(8,128)(2,1)}, u32[]{:S(2)}, u32[]{:S(2)}) %collective-permute-start.1) | collective-permute-done | bytes 1048608 | tf_op jit(solution)/shard_map/ppermute | solution.py:385
  38.7 2.3 %broadcast_select_fusion = bf16[256,2048]{1,0:T(8,128)(2,1)} fusion(bf16[256,2048]{1,0:T(8,128)(2,1)} %collective-permute-done.1.refs_2_.refs_6_, pred[]{:T(512)S(6)} %eq.58, bf16[1,256,2048]{2,1,0:T(8,128)(2,1)S(1)} %copy-done.1), kind=kLoop, calls=%fused_computation.8 | loop fusion | flops 524288 | bytes 3145729 | tf_op jit(solution)/shard_map/jit(_where)/select_n | solution.py:428
  41.0 0.6 pad_add_fusion.1
  41.5 0.8 copy.12
  42.3 1.3 gather_fusion
  43.6 0.8 compare_reduce_fusion
  44.4 1.2 compare_or_fusion
  45.7 0.6 collective-permute-start.3
  46.3 5.7 %collective-permute-done.3.refs_5_.refs_9_ = bf16[256,256]{1,0:T(8,128)(2,1)} collective-permute-done((bf16[256,256]{1,0:T(8,128)(2,1)}, bf16[256,256]{1,0:T(8,128)(2,1)}, u32[]{:S(2)}, u32[]{:S(2)}) %collective-permute-start.3) | collective-permute-done | bytes 131104 | tf_op jit(solution)/shard_map/ppermute | solution.py:389
  52.0 0.7 collective-permute-start.5
  52.6 0.3 collective-permute-start.7
  53.0 2.9 %collective-permute-start.9 = (bf16[256,256]{1,0:T(8,128)(2,1)}, bf16[256,256]{1,0:T(8,128)(2,1)}, u32[]{:S(2)}, u32[]{:S(2)}) collective-permute-start(bf16[256,256]{1,0:T(8,128)(2,1)} %collective-permute-done.3.refs_5_.refs_9_), channel_id=1, source_target_pairs={{0,12},{2,14},{4,0},{6,2},{8,4},{10,6},{12,8},{14,10},{1,13},{3,15... | collective-permute-start | bytes 393224 | tf_op jit(solution)/shard_map/ppermute | solution.py:394
  55.9 1.2 copy-done.2
  57.1 2.4 %grad_heads.1 = (bf16[128,256]{1,0:T(8,128)(2,1)S(1)}, bf16[128,256]{1,0:T(8,128)(2,1)}) custom-call(s32[2]{0:T(128)S(1)} %pad_add_fusion.at_ref.refs_0_, f32[256,256]{1,0:T(8,128)S(1)} %fusion.refs_1_, bf16[256,2048]{1,0:T(8,128)(2,1)} %collective-permute-done.1.refs_2_.refs_6_, bf16[256,2048]{1,0:T(8,128)(2,1)S(1)} %copy-done.2), custom_call_target="tpu_custom_call" | custom-call | flops 268435456 | bytes 2097152 | tf_op jit(solution)/shard_map/grad_heads/pallas_call | solution.py:254
  59.4 0.6 copy-done.16
  60.1 0.5 collective-permute-start.2
  60.6 0.6 gather_fusion.1
  61.3 0.3 fusion.2.refs_2_
  61.7 3.3 %collective-permute-done.7.refs_9_.refs_13_ = bf16[256,256]{1,0:T(8,128)(2,1)} collective-permute-done((bf16[256,256]{1,0:T(8,128)(2,1)}, bf16[256,256]{1,0:T(8,128)(2,1)}, u32[]{:S(2)}, u32[]{:S(2)}) %collective-permute-start.7) | collective-permute-done | bytes 131104 | tf_op jit(solution)/shard_map/ppermute | solution.py:394
  65.0 0.8 copy-done.7
  65.8 6.1 %forward.1 = (bf16[1,2048,512]{2,1,0:T(8,128)(2,1)S(1)}, f32[1,512]{1,0:T(1,128)S(1)}, bf16[128,256]{1,0:T(8,128)(2,1)}, bf16[128,256]{1,0:T(8,128)(2,1)S(1)}) custom-call(bf16[256,128]{1,0:T(8,128)(2,1)S(1)} %copy-done.7, bf16[256,128]{1,0:T(8,128)(2,1)} %collective-permute-done.refs_1_, f32[2048,2]{1,0:T(8,128)S(1)} %fusion.2.refs_2_, ...), custom_call_target="tpu_custom_call" | custom-call | flops 536870912 | bytes 4194304 | tf_op jit(solution)/shard_map/forward/pallas_call | solution.py:132
  71.9 0.6 collective-permute-start.15
  72.6 0.6 copy-done.18
  73.2 0.8 copy-done.19
  74.0 7.3 %backward.1 = (bf16[256,128]{1,0:T(8,128)(2,1)S(1)}, bf16[256,128]{1,0:T(8,128)(2,1)S(1)}, bf16[2,256,256]{2,1,0:T(8,128)(2,1)S(1)}, bf16[2,256,256]{2,1,0:T(8,1...) custom-call(bf16[256,128]{1,0:T(8,128)(2,1)S(1)} %copy-done.7, ...), custom_call_target="tpu_custom_call" | custom-call | flops 1073741824 | bytes 6291456 | tf_op jit(solution)/shard_map/backward/pallas_call | solution.py:213
  81.4 0.6 copy-done.10
  82.0 0.6 copy-done.13
  82.6 2.7 %collective-permute-start.12 = (bf16[2,256,256]{2,1,0:T(8,128)(2,1)}, bf16[2,256,256]{2,1,0:T(8,128)(2,1)}, u32[]{:S(2)}, u32[]{:S(2)}) collective-permute-start(bf16[2,256,256]{2,1,0:T(8,128)(2,1)} %get-tuple-element.38), channel_id=1, source_target_pairs={{0,4},{2,6},{4,8},{6,10},{8,12},{10,14},{12,0},{14,2},{1,5},{3,7},... | collective-permute-start | bytes 786440 | tf_op jit(solution)/shard_map/ppermute | solution.py:465
  85.3 0.1 collective-permute-start.11
  85.4 2.2 %collective-permute-start.10 = (bf16[2,256,256]{2,1,0:T(8,128)(2,1)}, bf16[2,256,256]{2,1,0:T(8,128)(2,1)}, u32[]{:S(2)}, u32[]{:S(2)}) collective-permute-start(bf16[2,256,256]{2,1,0:T(8,128)(2,1)} %get-tuple-element.36), channel_id=1, source_target_pairs={{0,12},{2,14},{4,0},{6,2},{8,4},{10,6},{12,8},{14,10},{1,13},{3,15... | collective-permute-start | bytes 786440 | tf_op jit(solution)/shard_map/ppermute | solution.py:465
  87.7 0.6 copy-done.8
  88.3 1.5 %collective-permute-done.16.refs_3_ = bf16[128,256]{1,0:T(8,128)(2,1)S(1)} collective-permute-done((bf16[128,256]{1,0:T(8,128)(2,1)}, bf16[128,256]{1,0:T(8,128)(2,1)S(1)}, u32[]{:S(2)}, u32[]{:S(2)}) %collective-permute-start.16) | collective-permute-done | bytes 65568 | tf_op jit(solution)/shard_map/ppermute | solution.py:449
  89.8 1.3 collective-permute-start.17
  91.1 2.9 %collective-permute-done.17.refs_4_ = bf16[128,256]{1,0:T(8,128)(2,1)S(1)} collective-permute-done((bf16[128,256]{1,0:T(8,128)(2,1)}, bf16[128,256]{1,0:T(8,128)(2,1)S(1)}, u32[]{:S(2)}, u32[]{:S(2)}) %collective-permute-start.17) | collective-permute-done | bytes 65568 | tf_op jit(solution)/shard_map/ppermute | solution.py:449
  94.1 0.8 copy-done.9
  94.9 4.5 %weight_terms.1 = (f32[4,256,256]{2,1,0:T(8,128)S(1)}, bf16[4,256,256]{2,1,0:T(8,128)(2,1)S(1)}) custom-call(s32[3]{0:T(128)S(1)} %pad_add_fusion.2.refs_0_, bf16[128,256]{1,0:T(8,128)(2,1)} %get-tuple-element.31.refs_4_.refs_1_, bf16[128,256]{1,0:T(8,128)(2,1)S(1)} %copy-done.9, bf16[128,256]{1,0:T(8,128)(2,1)S(1)} %collective-permute-done.16.refs_3_, ...), custom_call_target="tpu_custom_call" | custom-call | flops 536870912 | bytes 3670016 | tf_op jit(solution)/shard_map/weight_terms/pallas_call | solution.py:322
  99.4 1.6 %collective-permute-start.19 = (bf16[4,256,256]{2,1,0:T(8,128)(2,1)S(1)}, bf16[4,256,256]{2,1,0:T(8,128)(2,1)S(1)}, u32[]{:S(2)}, u32[]{:S(2)}) collective-permute-start(bf16[4,256,256]{2,1,0:T(8,128)(2,1)S(1)} %get-tuple-element.45), channel_id=1, source_target_pairs={{0,2},{2,0},{4,6},{6,4},{8,10},{10,8},{12,14},{14,12},{1,3},{3,1},... | collective-permute-start | bytes 1572872 | tf_op jit(solution)/shard_map/ppermute | solution.py:452
  101.0 1.9 %collective-permute-done.11 = bf16[2,256,256]{2,1,0:T(8,128)(2,1)} collective-permute-done((bf16[2,256,256]{2,1,0:T(8,128)(2,1)}, bf16[2,256,256]{2,1,0:T(8,128)(2,1)}, u32[]{:S(2)}, u32[]{:S(2)}) %collective-permute-start.11) | collective-permute-done | bytes 262176 | tf_op jit(solution)/shard_map/ppermute | solution.py:465
  102.8 1.2 add_convert_fusion
  104.1 1.6 %collective-permute-start.13 = (bf16[256,256]{1,0:T(8,128)(2,1)S(1)}, bf16[256,256]{1,0:T(8,128)(2,1)S(1)}, u32[]{:S(2)}, u32[]{:S(2)}) collective-permute-start(bf16[256,256]{1,0:T(8,128)(2,1)S(1)} %get-tuple-element.51), channel_id=1, source_target_pairs={{0,2},{2,0},{4,6},{6,4},{8,10},{10,8},{12,14},{14,12},{1,3},{3,1},... | collective-permute-start | bytes 393224 | tf_op jit(solution)/shard_map/ppermute | solution.py:467
  105.7 8.6 %collective-permute-done.19 = bf16[4,256,256]{2,1,0:T(8,128)(2,1)S(1)} collective-permute-done((bf16[4,256,256]{2,1,0:T(8,128)(2,1)S(1)}, bf16[4,256,256]{2,1,0:T(8,128)(2,1)S(1)}, u32[]{:S(2)}, u32[]{:S(2)}) %collective-permute-start.19) | collective-permute-done | bytes 524320 | tf_op jit(solution)/shard_map/ppermute | solution.py:452
  114.3 0.2 fusion.12
  114.5 2.0 %collective-permute-start.22 = (bf16[256,256]{1,0:T(8,128)(2,1)S(1)}, bf16[256,256]{1,0:T(8,128)(2,1)S(1)}, u32[]{:S(2)}, u32[]{:S(2)}) collective-permute-start(bf16[256,256]{1,0:T(8,128)(2,1)S(1)} %get-tuple-element.49), channel_id=1, source_target_pairs={{0,12},{2,14},{4,0},{6,2},{8,4},{10,6},{12,8},{14,10},{1,13},{3,15... | collective-permute-start | bytes 393224 | tf_op jit(solution)/shard_map/ppermute | solution.py:455
  116.5 0.8 collective-permute-start.20
  117.3 1.5 %collective-permute-start.14 = (bf16[256,128]{1,0:T(8,128)(2,1)S(1)}, bf16[256,128]{1,0:T(8,128)(2,1)S(1)}, u32[]{:S(2)}, u32[]{:S(2)}) collective-permute-start(bf16[256,128]{1,0:T(8,128)(2,1)S(1)} %copy-done.14), channel_id=1, source_target_pairs={{0,2},{2,0},{4,6},{6,4},{8,10},{10,8},{12,14},{14,12},{1,3},{3,1},... | collective-permute-start | bytes 196616 | tf_op jit(solution)/shard_map/ppermute | solution.py:462
  118.8 2.8 %collective-permute-done.14.dq_recv = bf16[256,128]{1,0:T(8,128)(2,1)S(1)} collective-permute-done((bf16[256,128]{1,0:T(8,128)(2,1)S(1)}, bf16[256,128]{1,0:T(8,128)(2,1)S(1)}, u32[]{:S(2)}, u32[]{:S(2)}) %collective-permute-start.14) | collective-permute-done | bytes 65568 | tf_op jit(solution)/shard_map/ppermute | solution.py:462
  121.6 1.4 %join_heads.1 = (bf16[256,256]{1,0:T(8,128)(2,1)}, bf16[256,256]{1,0:T(8,128)(2,1)}, bf16[256,256]{1,0:T(8,128)(2,1)}) custom-call(s32[2]{0:T(128)S(1)} %pad_add_fusion.at_ref.refs_0_, bf16[256,256]{1,0:T(8,128)(2,1)S(1)} %get-tuple-element.52.mine, bf16[256,256]{1,0:T(8,128)(2,1)S(1)} %collective-permute-done.13.recv, bf16[256,128]{1,0:T(8,128)(2,1)S(1)} %copy-done.11, ...), custom_call_target="tpu_custom_call" | custom-call | bytes 786432 | tf_op jit(solution)/shard_map/join_heads/pallas_call | solution.py:353
  122.9 4.4 %collective-permute-done.21 = bf16[256,256]{1,0:T(8,128)(2,1)S(1)} collective-permute-done((bf16[256,256]{1,0:T(8,128)(2,1)S(1)}, bf16[256,256]{1,0:T(8,128)(2,1)S(1)}, u32[]{:S(2)}, u32[]{:S(2)}) %collective-permute-start.21) | collective-permute-done | bytes 131104 | tf_op jit(solution)/shard_map/ppermute | solution.py:455
  127.4 0.7 fusion.6
  (61 shorter events, 0.7 us)
Async XLA Ops:
  0.6 17.0 %copy-start = (bf16[256,4096]{1,0:T(8,128)(2,1)S(1)}, bf16[256,4096]{1,0:T(8,128)(2,1)}, u32[]{:S(2)}) copy-start(bf16[256,4096]{1,0:T(8,128)(2,1)} %param.11) | copy-start | bytes 6291460
  0.6 18.0 %copy-start.1 = (bf16[1,256,2048]{2,1,0:T(8,128)(2,1)S(1)}, bf16[1,256,2048]{2,1,0:T(8,128)(2,1)}, u32[]{:S(2)}) copy-start(bf16[1,256,2048]{2,1,0:T(8,128)(2,1)} %param.10) | copy-start | bytes 3145732
  0.8 1.1 copy-start.3
  1.8 0.9 copy-start.4
  2.7 0.9 copy-start.5
  4.9 0.6 copy-start.6
  5.5 0.7 copy-start.12
  6.1 46.5 %collective-permute-start.4 = (bf16[256,256]{1,0:T(8,128)(2,1)S(1)}, bf16[256,256]{1,0:T(8,128)(2,1)}, u32[]{:S(2)}, u32[]{:S(2)}) collective-permute-start(bf16[256,256]{1,0:T(8,128)(2,1)S(1)} %get-tuple-element.29.refs_4_.refs_8_), channel_id=1, source_target_pairs={{0,4},{2,6},{4,8},{6,10},{8,12},{10,14},{12,0},{14,2},{1,5},{3,7},... | collective-permute-start | bytes 393224 | tf_op jit(solution)/shard_map/ppermute | solution.py:394
  9.2 43.8 %collective-permute-start.6 = (bf16[256,256]{1,0:T(8,128)(2,1)S(1)}, bf16[256,256]{1,0:T(8,128)(2,1)}, u32[]{:S(2)}, u32[]{:S(2)}) collective-permute-start(bf16[256,256]{1,0:T(8,128)(2,1)S(1)} %get-tuple-element.29.refs_4_.refs_8_), channel_id=1, source_target_pairs={{0,8},{2,10},{4,12},{6,14},{8,0},{10,2},{12,4},{14,6},{1,9},{3,11}... | collective-permute-start | bytes 393224 | tf_op jit(solution)/shard_map/ppermute | solution.py:394
  11.8 48.3 %collective-permute-start.8 = (bf16[256,256]{1,0:T(8,128)(2,1)S(1)}, bf16[256,256]{1,0:T(8,128)(2,1)}, u32[]{:S(2)}, u32[]{:S(2)}) collective-permute-start(bf16[256,256]{1,0:T(8,128)(2,1)S(1)} %get-tuple-element.29.refs_4_.refs_8_), channel_id=1, source_target_pairs={{0,12},{2,14},{4,0},{6,2},{8,4},{10,6},{12,8},{14,10},{1,13},{3,15... | collective-permute-start | bytes 393224 | tf_op jit(solution)/shard_map/ppermute | solution.py:394
  13.1 32.6 %collective-permute-start = (bf16[256,128]{1,0:T(8,128)(2,1)}, bf16[256,128]{1,0:T(8,128)(2,1)}, u32[]{:S(2)}, u32[]{:S(2)}) collective-permute-start(bf16[256,128]{1,0:T(8,128)(2,1)} %get-tuple-element.26), channel_id=1, source_target_pairs={{0,2},{2,0},{4,6},{6,4},{8,10},{10,8},{12,14},{14,12},{1,3},{3,1},... | collective-permute-start | bytes 196616 | tf_op jit(solution)/shard_map/ppermute | solution.py:390
  14.6 24.1 %collective-permute-start.1 = (bf16[256,2048]{1,0:T(8,128)(2,1)}, bf16[256,2048]{1,0:T(8,128)(2,1)}, u32[]{:S(2)}, u32[]{:S(2)}) collective-permute-start(bf16[256,2048]{1,0:T(8,128)(2,1)} %bitcast.65), channel_id=1, source_target_pairs={{0,1},{1,0},{2,3},{3,2},{4,5},{5,4},{6,7},{7,6},{8,9},{9,8},{10,11... | collective-permute-start | bytes 3145736 | tf_op jit(solution)/shard_map/ppermute | solution.py:385
  16.2 0.8 copy-start.20
  41.0 53.1 %collective-permute-start.18 = (bf16[256,2048]{1,0:T(8,128)(2,1)}, bf16[256,2048]{1,0:T(8,128)(2,1)}, u32[]{:S(2)}, u32[]{:S(2)}) collective-permute-start(bf16[256,2048]{1,0:T(8,128)(2,1)} %broadcast_select_fusion), channel_id=1, source_target_pairs={{0,16},{16,0},{1,17},{17,1},{2,18},{18,2},{3,19},{19,3},{4,20},{20... | collective-permute-start | bytes 3145736 | tf_op jit(solution)/shard_map/ppermute | solution.py:433
  45.7 6.3 %collective-permute-start.3 = (bf16[256,256]{1,0:T(8,128)(2,1)}, bf16[256,256]{1,0:T(8,128)(2,1)}, u32[]{:S(2)}, u32[]{:S(2)}) collective-permute-start(bf16[256,256]{1,0:T(8,128)(2,1)} %copy-done.12), channel_id=1, source_target_pairs={{0,2},{2,0},{4,6},{6,4},{8,10},{10,8},{12,14},{14,12},{1,3},{3,1},... | collective-permute-start | bytes 393224 | tf_op jit(solution)/shard_map/ppermute | solution.py:389
  52.0 9.7 %collective-permute-start.5 = (bf16[256,256]{1,0:T(8,128)(2,1)}, bf16[256,256]{1,0:T(8,128)(2,1)}, u32[]{:S(2)}, u32[]{:S(2)}) collective-permute-start(bf16[256,256]{1,0:T(8,128)(2,1)} %collective-permute-done.3.refs_5_.refs_9_), channel_id=1, source_target_pairs={{0,4},{2,6},{4,8},{6,10},{8,12},{10,14},{12,0},{14,2},{1,5},{3,7},... | collective-permute-start | bytes 393224 | tf_op jit(solution)/shard_map/ppermute | solution.py:394
  52.6 12.3 %collective-permute-start.7 = (bf16[256,256]{1,0:T(8,128)(2,1)}, bf16[256,256]{1,0:T(8,128)(2,1)}, u32[]{:S(2)}, u32[]{:S(2)}) collective-permute-start(bf16[256,256]{1,0:T(8,128)(2,1)} %collective-permute-done.3.refs_5_.refs_9_), channel_id=1, source_target_pairs={{0,8},{2,10},{4,12},{6,14},{8,0},{10,2},{12,4},{14,6},{1,9},{3,11}... | collective-permute-start | bytes 393224 | tf_op jit(solution)/shard_map/ppermute | solution.py:394
  53.0 12.0 %collective-permute-start.9 = (bf16[256,256]{1,0:T(8,128)(2,1)}, bf16[256,256]{1,0:T(8,128)(2,1)}, u32[]{:S(2)}, u32[]{:S(2)}) collective-permute-start(bf16[256,256]{1,0:T(8,128)(2,1)} %collective-permute-done.3.refs_5_.refs_9_), channel_id=1, source_target_pairs={{0,12},{2,14},{4,0},{6,2},{8,4},{10,6},{12,8},{14,10},{1,13},{3,15... | collective-permute-start | bytes 393224 | tf_op jit(solution)/shard_map/ppermute | solution.py:394
  55.8 1.2 copy-start.2
  57.1 4.1 %copy-start.21 = (pred[8,2]{0,1:T(4,128)(4,1)S(1)}, pred[8,2]{0,1:T(4,128)(4,1)}, u32[]{:S(2)}) copy-start(pred[8,2]{0,1:T(4,128)(4,1)} %compare_or_fusion) | copy-start | bytes 52
  59.4 0.6 copy-start.16
  60.1 12.5 %collective-permute-start.2 = (bf16[128,256]{1,0:T(8,128)(2,1)}, bf16[128,256]{1,0:T(8,128)(2,1)S(1)}, u32[]{:S(2)}, u32[]{:S(2)}) collective-permute-start(bf16[128,256]{1,0:T(8,128)(2,1)} %get-tuple-element.28), channel_id=1, source_target_pairs={{0,2},{2,0},{4,6},{6,4},{8,10},{10,8},{12,14},{14,12},{1,3},{3,1},... | collective-permute-start | bytes 196616 | tf_op jit(solution)/shard_map/ppermute | solution.py:416
  61.3 11.9 %copy-start.17 = (bf16[128,256]{1,0:T(8,128)(2,1)S(1)}, bf16[128,256]{1,0:T(8,128)(2,1)}, u32[]{:S(2)}) copy-start(bf16[128,256]{1,0:T(8,128)(2,1)} %copy-done.16) | copy-start | bytes 196612
  65.0 0.8 copy-start.7
  71.9 15.8 %copy-start.15 = (bf16[128,256]{1,0:T(8,128)(2,1)}, bf16[128,256]{1,0:T(8,128)(2,1)S(1)}, u32[]{:S(2)}) copy-start(bf16[128,256]{1,0:T(8,128)(2,1)S(1)} %get-tuple-element.32.refs_5_) | copy-start | bytes 196612
  71.9 15.7 %collective-permute-start.15 = (bf16[128,256]{1,0:T(8,128)(2,1)S(1)}, bf16[128,256]{1,0:T(8,128)(2,1)S(1)}, u32[]{:S(2)}, u32[]{:S(2)}) collective-permute-start(bf16[128,256]{1,0:T(8,128)(2,1)S(1)} %get-tuple-element.32.refs_5_), channel_id=1, source_target_pairs={{0,2},{2,0},{4,6},{6,4},{8,10},{10,8},{12,14},{14,12},{16,18},{18,... | collective-permute-start | bytes 196616 | tf_op jit(solution)/shard_map/ppermute | solution.py:449
  72.5 0.6 copy-start.18
  73.2 0.8 copy-start.19
  81.3 0.6 copy-start.10
  82.0 0.6 copy-start.13
  82.6 18.3 %collective-permute-start.12 = (bf16[2,256,256]{2,1,0:T(8,128)(2,1)}, bf16[2,256,256]{2,1,0:T(8,128)(2,1)}, u32[]{:S(2)}, u32[]{:S(2)}) collective-permute-start(bf16[2,256,256]{2,1,0:T(8,128)(2,1)} %get-tuple-element.38), channel_id=1, source_target_pairs={{0,4},{2,6},{4,8},{6,10},{8,12},{10,14},{12,0},{14,2},{1,5},{3,7},... | collective-permute-start | bytes 786440 | tf_op jit(solution)/shard_map/ppermute | solution.py:465
  85.3 17.5 %collective-permute-start.11 = (bf16[2,256,256]{2,1,0:T(8,128)(2,1)}, bf16[2,256,256]{2,1,0:T(8,128)(2,1)}, u32[]{:S(2)}, u32[]{:S(2)}) collective-permute-start(bf16[2,256,256]{2,1,0:T(8,128)(2,1)} %get-tuple-element.37), channel_id=1, source_target_pairs={{0,8},{2,10},{4,12},{6,14},{8,0},{10,2},{12,4},{14,6},{1,9},{3,11}... | collective-permute-start | bytes 786440 | tf_op jit(solution)/shard_map/ppermute | solution.py:465
  85.4 17.4 %collective-permute-start.10 = (bf16[2,256,256]{2,1,0:T(8,128)(2,1)}, bf16[2,256,256]{2,1,0:T(8,128)(2,1)}, u32[]{:S(2)}, u32[]{:S(2)}) collective-permute-start(bf16[2,256,256]{2,1,0:T(8,128)(2,1)} %get-tuple-element.36), channel_id=1, source_target_pairs={{0,12},{2,14},{4,0},{6,2},{8,4},{10,6},{12,8},{14,10},{1,13},{3,15... | collective-permute-start | bytes 786440 | tf_op jit(solution)/shard_map/ppermute | solution.py:465
  87.7 0.6 copy-start.8
  88.3 1.5 %collective-permute-start.16 = (bf16[128,256]{1,0:T(8,128)(2,1)}, bf16[128,256]{1,0:T(8,128)(2,1)S(1)}, u32[]{:S(2)}, u32[]{:S(2)}) collective-permute-start(bf16[128,256]{1,0:T(8,128)(2,1)} %get-tuple-element.31.refs_4_.refs_1_), channel_id=1, source_target_pairs={{0,16},{2,18},{4,20},{6,22},{8,24},{10,26},{12,28},{14,30},{16,0},... | collective-permute-start | bytes 196616 | tf_op jit(solution)/shard_map/ppermute | solution.py:449
  89.8 4.3 %collective-permute-start.17 = (bf16[128,256]{1,0:T(8,128)(2,1)}, bf16[128,256]{1,0:T(8,128)(2,1)S(1)}, u32[]{:S(2)}, u32[]{:S(2)}) collective-permute-start(bf16[128,256]{1,0:T(8,128)(2,1)} %copy-done.15), channel_id=1, source_target_pairs={{0,18},{2,16},{4,22},{6,20},{8,26},{10,24},{12,30},{14,28},{16,2},... | collective-permute-start | bytes 196616 | tf_op jit(solution)/shard_map/ppermute | solution.py:449
  94.1 0.8 copy-start.9
  99.4 14.9 %collective-permute-start.19 = (bf16[4,256,256]{2,1,0:T(8,128)(2,1)S(1)}, bf16[4,256,256]{2,1,0:T(8,128)(2,1)S(1)}, u32[]{:S(2)}, u32[]{:S(2)}) collective-permute-start(bf16[4,256,256]{2,1,0:T(8,128)(2,1)S(1)} %get-tuple-element.45), channel_id=1, source_target_pairs={{0,2},{2,0},{4,6},{6,4},{8,10},{10,8},{12,14},{14,12},{1,3},{3,1},... | collective-permute-start | bytes 1572872 | tf_op jit(solution)/shard_map/ppermute | solution.py:452
  104.1 13.2 %copy-start.14 = (bf16[256,128]{1,0:T(8,128)(2,1)S(1)}, bf16[256,128]{1,0:T(8,128)(2,1)}, u32[]{:S(2)}) copy-start(bf16[256,128]{1,0:T(8,128)(2,1)} %copy-done.13) | copy-start | bytes 196612
  104.1 17.5 %copy-start.11 = (bf16[256,128]{1,0:T(8,128)(2,1)S(1)}, bf16[256,128]{1,0:T(8,128)(2,1)}, u32[]{:S(2)}) copy-start(bf16[256,128]{1,0:T(8,128)(2,1)} %copy-done.10) | copy-start | bytes 196612
  104.1 17.5 %collective-permute-start.13 = (bf16[256,256]{1,0:T(8,128)(2,1)S(1)}, bf16[256,256]{1,0:T(8,128)(2,1)S(1)}, u32[]{:S(2)}, u32[]{:S(2)}) collective-permute-start(bf16[256,256]{1,0:T(8,128)(2,1)S(1)} %get-tuple-element.51), channel_id=1, source_target_pairs={{0,2},{2,0},{4,6},{6,4},{8,10},{10,8},{12,14},{14,12},{1,3},{3,1},... | collective-permute-start | bytes 393224 | tf_op jit(solution)/shard_map/ppermute | solution.py:467
  114.5 8.5 %collective-permute-start.22 = (bf16[256,256]{1,0:T(8,128)(2,1)S(1)}, bf16[256,256]{1,0:T(8,128)(2,1)S(1)}, u32[]{:S(2)}, u32[]{:S(2)}) collective-permute-start(bf16[256,256]{1,0:T(8,128)(2,1)S(1)} %get-tuple-element.49), channel_id=1, source_target_pairs={{0,12},{2,14},{4,0},{6,2},{8,4},{10,6},{12,8},{14,10},{1,13},{3,15... | collective-permute-start | bytes 393224 | tf_op jit(solution)/shard_map/ppermute | solution.py:455
  116.5 10.9 %collective-permute-start.21 = (bf16[256,256]{1,0:T(8,128)(2,1)S(1)}, bf16[256,256]{1,0:T(8,128)(2,1)S(1)}, u32[]{:S(2)}, u32[]{:S(2)}) collective-permute-start(bf16[256,256]{1,0:T(8,128)(2,1)S(1)} %get-tuple-element.50), channel_id=1, source_target_pairs={{0,8},{2,10},{4,12},{6,14},{8,0},{10,2},{12,4},{14,6},{1,9},{3,11}... | collective-permute-start | bytes 393224 | tf_op jit(solution)/shard_map/ppermute | solution.py:455
  116.5 10.9 %collective-permute-start.20 = (bf16[256,256]{1,0:T(8,128)(2,1)S(1)}, bf16[256,256]{1,0:T(8,128)(2,1)S(1)}, u32[]{:S(2)}, u32[]{:S(2)}) collective-permute-start(bf16[256,256]{1,0:T(8,128)(2,1)S(1)} %get-tuple-element.48), channel_id=1, source_target_pairs={{0,4},{2,6},{4,8},{6,10},{8,12},{10,14},{12,0},{14,2},{1,5},{3,7},... | collective-permute-start | bytes 393224 | tf_op jit(solution)/shard_map/ppermute | solution.py:455
  117.3 4.3 %collective-permute-start.14 = (bf16[256,128]{1,0:T(8,128)(2,1)S(1)}, bf16[256,128]{1,0:T(8,128)(2,1)S(1)}, u32[]{:S(2)}, u32[]{:S(2)}) collective-permute-start(bf16[256,128]{1,0:T(8,128)(2,1)S(1)} %copy-done.14), channel_id=1, source_target_pairs={{0,2},{2,0},{4,6},{6,4},{8,10},{10,8},{12,14},{14,12},{1,3},{3,1},... | collective-permute-start | bytes 196616 | tf_op jit(solution)/shard_map/ppermute | solution.py:462

commit v3 on v2

v3 whole, which is shorter than its diff:
```python
import functools

import jax
import jax.numpy as jnp
from jax import lax
from jax.experimental import pallas as pl
from jax.experimental.pallas import tpu as pltpu
from jax.sharding import PartitionSpec as P

HD = 128
MASKED = -1e30
INNER = 2
ANY = pl.BlockSpec(memory_space=pl.ANY)
VMEM = pl.BlockSpec(memory_space=pltpu.VMEM)
SMEM = pl.BlockSpec(memory_space=pltpu.SMEM)


def against(left_op, right_op):
    return lax.dot_general(
        left_op, right_op, (((1,), (1,)), ((), ())), preferred_element_type=jnp.float32
    )


def product(left_op, right_op):
    return jnp.dot(left_op, right_op, preferred_element_type=jnp.float32)


def begin(source, target, semaphore):
    copy = pltpu.make_async_copy(source, target, semaphore)
    copy.start()
    return copy


def call(kernel, out_shape, in_specs, out_specs, scratch, flops, moved, name):
    return pl.pallas_call(
        kernel,
        out_shape=out_shape,
        in_specs=in_specs,
        out_specs=out_specs,
        scratch_shapes=scratch,
        compiler_params=pltpu.CompilerParams(vmem_limit_bytes=56 * 1024 * 1024),
        cost_estimate=pl.CostEstimate(flops=flops, bytes_accessed=moved, transcendentals=0),
        name=name,
    )


def bf16(*shape):
    return jax.ShapeDtypeStruct(shape, jnp.bfloat16)


def part_kernel(at_ref, q_ref, k_ref, v_ref, send_out, q_theirs, sem):
    half = q_theirs.shape[1]
    copies = []
    for place in range(send_out.shape[0]):
        side = place % INNER
        cols = slice(side * half, (side + 1) * half)
        for index, held in enumerate((k_ref, v_ref)):
            target = send_out.at[place, :, index * half : (index + 1) * half]
            copies.append(begin(held.at[:, cols], target, sem.at[2 * place + index]))
    theirs = pl.ds(pl.multiple_of((1 - at_ref[0]) * half, half), half)
    copies.append(begin(q_ref.at[:, theirs], q_theirs, sem.at[2 * send_out.shape[0]]))
    for copy in copies:
        copy.wait()


def part_heads(at, queries, keys, values, count):
    rows, feats = queries.shape
    half = feats // INNER
    return call(
        part_kernel,
        [bf16(count, rows, 2 * half), bf16(rows, half)],
        [SMEM] + [ANY] * 3,
        [ANY] * 2,
        [pltpu.SemaphoreType.DMA((2 * count + 1,))],
        0,
        8 * count * rows * half,
        "part_heads",
    )(at, queries, keys, values)


def prelude_kernel(at_ref, pattern, offsets, grad_ref, weight_ref, first, key_mask, row_mask, *rest):
    grad_s, weight_s, sem = rest
    rows, width = grad_s.shape
    block_count, glob_count = offsets.shape
    start = pl.multiple_of(at_ref[2] * width, width)
    loads = [
        begin(grad_ref, grad_s, sem.at[0]),
        begin(weight_ref.at[:, pl.ds(start, width)], weight_s, sem.at[1]),
    ]
    own = at_ref[1] * INNER + at_ref[0]
    partner = at_ref[1] * INNER + 1 - at_ref[0]
    lane = lax.broadcasted_iota(jnp.int32, (1, HD), 1)
    row_at = lax.broadcasted_iota(jnp.int32, (rows, HD), 0)
    col_at = lax.broadcasted_iota(jnp.int32, (8, rows), 1)
    group_at = lax.broadcasted_iota(jnp.int32, (8, rows), 0)
    for block in range(block_count):
        hidden = []
        for target in (own, partner):
            seen = jnp.abs(block - target) <= 1
            for r in range(pattern.shape[1]):
                seen = seen | (pattern[target, r] == block)
            hidden.append(jnp.where(seen, 0, 1))
        lane_hidden = jnp.where(lane == 0, hidden[0], jnp.where(lane == 1, hidden[1], 0))
        hidden_rows = jnp.broadcast_to(lane_hidden, (rows, HD))
        for r in range(glob_count):
            hidden_rows = jnp.where(row_at == offsets[block, r], 0, hidden_rows)
        key_mask[block * rows : (block + 1) * rows, :] = hidden_rows.astype(jnp.float32).astype(
            jnp.bfloat16
        )
    for group, target in enumerate((own, partner)):
        local = jnp.where(group_at == group, MASKED, 0.0)
        for r in range(glob_count):
            local = jnp.where(col_at == offsets[target, r], 0.0, local)
        row_mask[:, group * rows : (group + 1) * rows] = local
    for load in loads:
        load.wait()
    first[...] = against(weight_s[...], grad_s[...])


def prelude(at, pattern, offsets, grad_own, out_weight):
    rows, width = grad_own.shape
    feats = out_weight.shape[0]
    keys = offsets.shape[0] * rows
    return call(
        prelude_kernel,
        [
            jax.ShapeDtypeStruct((feats, rows), jnp.float32),
            bf16(keys, HD),
            jax.ShapeDtypeStruct((8, 2 * rows), jnp.float32),
        ],
        [SMEM] * 3 + [ANY] * 2,
        [VMEM] * 3,
        [
            pltpu.VMEM((rows, width), jnp.bfloat16),
            pltpu.VMEM((feats, width), jnp.bfloat16),
            pltpu.SemaphoreType.DMA((2,)),
        ],
        2 * feats * rows * width,
        2 * (feats + rows) * width,
        "prelude",
    )(at, pattern, offsets, grad_own, out_weight)


def forward_kernel(block_count, head_count, at_ref, q_ref, q_recv, key_mask, row_mask, kv_ref, *refs):
    e_out, inv_out, attn_mine, attn_theirs = refs[:4]
    q_s, mask_s, kv_s, e_s, s_ref, attn_s, inv_s, row_s, sem, kv_sem, e_sem, out_sem = refs[4:]
    rows = q_recv.shape[0]
    feats = head_count * HD
    score_scale = HD ** (-0.5)
    mine = pl.ds(pl.multiple_of(at_ref[0] * feats, feats), feats)
    loads = [
        begin(q_ref.at[:, mine], q_s.at[0], sem.at[0]),
        begin(q_recv, q_s.at[1], sem.at[1]),
        begin(key_mask, mask_s, sem.at[2]),
        begin(row_mask, row_s, sem.at[3]),
    ]
    kv_loads = [begin(kv_ref.at[j], kv_s.at[j], kv_sem.at[j]) for j in range(block_count)]
    for load in loads:
        load.wait()
    rows_low = row_s[...].astype(jnp.bfloat16)
    hidden = jnp.concatenate([rows_low, jnp.zeros((HD - 8, 2 * rows), jnp.bfloat16)], axis=0)
    stores = []
    for head in range(head_count):
        cols = slice(head * HD, (head + 1) * HD)
        vcols = slice(feats + head * HD, feats + (head + 1) * HD)
        q_t = jnp.concatenate(
            [jnp.transpose(q_s[0, :, cols]), jnp.transpose(q_s[1, :, cols])], axis=1
        )
        q_t = jnp.concatenate([q_t, hidden], axis=0)
        top = jnp.full((1, 2 * rows), MASKED, jnp.float32)
        for j in range(block_count):
            if head == 0:
                kv_loads[j].wait()
            keys = slice(j * rows, (j + 1) * rows)
            scores = product(jnp.concatenate([kv_s[j, :, cols], mask_s[keys, :]], axis=1), q_t)
            s_ref[keys, :] = scores
            top = jnp.maximum(top, jnp.max(scores, axis=0, keepdims=True))
        total = jnp.zeros((1, 2 * rows), jnp.float32)
        attn_t = jnp.zeros((HD, 2 * rows), jnp.float32)
        for j in range(block_count):
            keys = slice(j * rows, (j + 1) * rows)
            weights = jnp.exp((s_ref[keys, :] - top) * score_scale)
            total = total + jnp.sum(weights, axis=0, keepdims=True)
            low = weights.astype(jnp.bfloat16)
            e_s[head, keys, :] = low
            stores.append(
                begin(e_s.at[head, keys], e_out.at[head, keys], e_sem.at[head * block_count + j])
            )
            attn_t = attn_t + product(jnp.transpose(kv_s[j, :, vcols]), low)
        inverse = 1.0 / total
        inv_s[head : head + 1, :] = inverse
        attn_low = (attn_t * inverse).astype(jnp.bfloat16)
        attn_s[0, cols, :] = attn_low[:, :rows]
        attn_s[1, cols, :] = attn_low[:, rows:]
    stores.append(begin(attn_s.at[0], attn_mine, out_sem.at[0]))
    stores.append(begin(attn_s.at[1], attn_theirs, out_sem.at[1]))
    stores.append(begin(inv_s, inv_out, out_sem.at[2]))
    for store in stores:
        store.wait()


def forward(at, queries, q_recv, key_mask, row_mask, kv_all):
    block_count = kv_all.shape[0]
    rows, feats = q_recv.shape
    heads = feats // HD
    keys = block_count * rows
    return call(
        functools.partial(forward_kernel, block_count, heads),
        [
            bf16(heads, keys, 2 * rows),
            jax.ShapeDtypeStruct((max(heads, 8), 2 * rows), jnp.float32),
            bf16(feats, rows),
            bf16(feats, rows),
        ],
        [SMEM] + [ANY] * 5,
        [ANY] * 4,
        [
            pltpu.VMEM((2, rows, feats), jnp.bfloat16),
            pltpu.VMEM((keys, HD), jnp.bfloat16),
            pltpu.VMEM((block_count, rows, 2 * feats), jnp.bfloat16),
            pltpu.VMEM((heads, keys, 2 * rows), jnp.bfloat16),
            pltpu.VMEM((keys, 2 * rows), jnp.float32),
            pltpu.VMEM((2, feats, rows), jnp.bfloat16),
            pltpu.VMEM((max(heads, 8), 2 * rows), jnp.float32),
            pltpu.VMEM((8, 2 * rows), jnp.float32),
            pltpu.SemaphoreType.DMA((4,)),
            pltpu.SemaphoreType.DMA((block_count,)),
            pltpu.SemaphoreType.DMA((heads * block_count,)),
            pltpu.SemaphoreType.DMA((3,)),
        ],
        8 * rows * keys * feats,
        8 * keys * feats + 4 * heads * keys * rows,
        "forward",
    )(at, queries, q_recv, key_mask, row_mask, kv_all)


def backward_kernel(block_count, head_count, at_ref, *refs):
    q_ref, q_recv, g_mine, g_recv, attn_mine, attn_theirs, inv_ref, e_ref, kv_ref = refs[:9]
    dq_mine, dq_theirs, part_out = refs[9:12]
    q_s, t_s, inv_s, kv_s, e_s, part_s, dq_s, sem, kv_sem, e_sem, part_sem, dq_sem = refs[12:]
    rows = q_recv.shape[0]
    feats = head_count * HD
    score_scale = HD ** (-0.5)
    mine = pl.ds(pl.multiple_of(at_ref[0] * feats, feats), feats)
    loads = [begin(q_ref.at[:, mine], q_s.at[0], sem.at[0]), begin(q_recv, q_s.at[1], sem.at[1])]
    for index, held in enumerate((g_mine, g_recv, attn_mine, attn_theirs)):
        loads.append(begin(held, t_s.at[index], sem.at[2 + index]))
    loads.append(begin(inv_ref, inv_s, sem.at[6]))
    kv_loads, e_loads, stores = [], {}, []
    for j in range(block_count):
        keys = slice(j * rows, (j + 1) * rows)
        kv_loads.append(begin(kv_ref.at[j], kv_s.at[j], kv_sem.at[j]))
        for head in range(head_count):
            e_loads[head, j] = begin(
                e_ref.at[head, keys], e_s.at[head, keys], e_sem.at[head * block_count + j]
            )
    for load in loads:
        load.wait()
    for head in range(head_count):
        cols = slice(head * HD, (head + 1) * HD)
        vcols = slice(feats + head * HD, feats + (head + 1) * HD)
        inverse = inv_s[head : head + 1, :]
        g_t = jnp.concatenate([t_s[0, cols, :], t_s[1, cols, :]], axis=1).astype(jnp.float32)
        attn_t = jnp.concatenate([t_s[2, cols, :], t_s[3, cols, :]], axis=1)
        row_dot = jnp.sum(g_t * attn_t.astype(jnp.float32), axis=0, keepdims=True) * inverse
        g_t = (g_t * inverse).astype(jnp.bfloat16)
        grad = jnp.transpose(g_t)
        query = jnp.concatenate([q_s[0, :, cols], q_s[1, :, cols]], axis=0)
        dq_t = jnp.zeros((HD, 2 * rows), jnp.float32)
        for j in range(block_count):
            keys = slice(j * rows, (j + 1) * rows)
            if head == 0:
                kv_loads[j].wait()
            e_loads[head, j].wait()
            low = e_s[head, keys, :]
            dprobs = product(kv_s[j, :, vcols], g_t)
            dscore = (low.astype(jnp.float32) * (dprobs - row_dot)).astype(jnp.bfloat16)
            dq_t = dq_t + product(jnp.transpose(kv_s[j, :, cols]), dscore)
            part_s[j, :, cols] = (score_scale * product(dscore, query)).astype(jnp.bfloat16)
            part_s[j, :, vcols] = product(low, grad).astype(jnp.bfloat16)
            if head == head_count - 1:
                stores.append(begin(part_s.at[j], part_out.at[j], part_sem.at[j]))
        dquery = (score_scale * jnp.transpose(dq_t)).astype(jnp.bfloat16)
        dq_s[0, :, cols] = dquery[:rows]
        dq_s[1, :, cols] = dquery[rows:]
    stores.append(begin(dq_s.at[0], dq_mine, dq_sem.at[0]))
    stores.append(begin(dq_s.at[1], dq_theirs, dq_sem.at[1]))
    for store in stores:
        store.wait()


def backward(at, queries, q_recv, g_mine, g_recv, attn_mine, attn_theirs, inverse, weights, kv_all):
    block_count = kv_all.shape[0]
    rows, feats = q_recv.shape
    heads = feats // HD
    keys = block_count * rows
    return call(
        functools.partial(backward_kernel, block_count, heads),
        [bf16(rows, feats)] * 2 + [bf16(block_count, rows, 2 * feats)],
        [SMEM] + [ANY] * 9,
        [ANY] * 3,
        [
            pltpu.VMEM((2, rows, feats), jnp.bfloat16),
            pltpu.VMEM((4, feats, rows), jnp.bfloat16),
            pltpu.VMEM(inverse.shape, jnp.float32),
            pltpu.VMEM((block_count, rows, 2 * feats), jnp.bfloat16),
            pltpu.VMEM((heads, keys, 2 * rows), jnp.bfloat16),
            pltpu.VMEM((block_count, rows, 2 * feats), jnp.bfloat16),
            pltpu.VMEM((2, rows, feats), jnp.bfloat16),
            pltpu.SemaphoreType.DMA((7,)),
            pltpu.SemaphoreType.DMA((block_count,)),
            pltpu.SemaphoreType.DMA((heads * block_count,)),
            pltpu.SemaphoreType.DMA((block_count,)),
            pltpu.SemaphoreType.DMA((2,)),
        ],
        16 * rows * keys * feats,
        16 * keys * feats + 4 * heads * keys * rows,
        "backward",
    )(at, queries, q_recv, g_mine, g_recv, attn_mine, attn_theirs, inverse, weights, kv_all)


def grad_heads_kernel(part_count, sends, picked, at_ref, first_ref, weight_ref, *refs):
    grads, refs = refs[:part_count], refs[part_count:]
    outs, refs = refs[: 2 + sends], refs[2 + sends :]
    first_s, grad_s, weight_s, out_s, sem, send_sem, out_sem = refs
    half = out_s.shape[1]
    width = grads[0].shape[1]
    first_load = begin(first_ref, first_s, sem.at[0])
    loads = []
    for k in range(1, part_count):
        start = pl.multiple_of(at_ref[2 + k] * width, width)
        loads.append(
            (
                begin(grads[k], grad_s.at[k - 1], sem.at[2 * k - 1]),
                begin(weight_ref.at[:, pl.ds(start, width)], weight_s.at[k - 1], sem.at[2 * k]),
            )
        )
    copies = []
    for send in range(sends):
        for i in range(picked):
            place = send * picked + i
            target = outs[2 + send].at[:, i * width : (i + 1) * width]
            for k in range(part_count):

                @pl.when(at_ref[2 + part_count + place] == k)
                def _():
                    begin(grads[k], target, send_sem.at[place])

            copies.append(pltpu.make_async_copy(grads[0], target, send_sem.at[place]))
    first_load.wait()
    for k, pair in enumerate(loads):
        for load in pair:
            load.wait()
        first_s[...] = first_s[...] + against(weight_s[k], grad_s[k])
    for side, at in enumerate((at_ref[0], 1 - at_ref[0])):
        kept = first_s[pl.ds(pl.multiple_of(at * half, half), half), :]
        out_s[side] = kept.astype(jnp.bfloat16)
        copies.append(begin(out_s.at[side], outs[side], out_sem.at[side]))
    for copy in copies:
        copy.wait()


def grad_heads(at, first, out_weight, grads, sends, picked):
    feats, rows = first.shape
    half = feats // INNER
    count = len(grads)
    width = grads[0].shape[1]
    out = call(
        functools.partial(grad_heads_kernel, count, sends, picked),
        [bf16(half, rows), bf16(half, rows)] + [bf16(rows, picked * width)] * sends,
        [SMEM] + [ANY] * (2 + count),
        [ANY] * (2 + sends),
        [
            pltpu.VMEM((feats, rows), jnp.float32),
            pltpu.VMEM((count - 1, rows, width), jnp.bfloat16),
            pltpu.VMEM((count - 1, feats, width), jnp.bfloat16),
            pltpu.VMEM((INNER, half, rows), jnp.bfloat16),
            pltpu.SemaphoreType.DMA((2 * count - 1,)),
            pltpu.SemaphoreType.DMA((sends * picked,)),
            pltpu.SemaphoreType.DMA((INNER,)),
        ],
        2 * feats * rows * width * (count - 1),
        2 * (feats + rows) * width * (count - 1) + 4 * sends * rows * picked * width,
        "grad_heads",
    )(at, first, out_weight, *grads)
    return out[0], out[1], out[2:]


def weight_kernel(part_count, picked, doc_count, sent, at_ref, *refs):
    attn, refs = refs[: INNER * doc_count], refs[INNER * doc_count :]
    grads, refs = refs[:part_count], refs[part_count:]
    swapped, refs = refs[: doc_count - 1], refs[doc_count - 1 :]
    out, attn_s, grad_s, out_s, attn_sem, grad_sem, out_sem = refs
    outer, feats, width = out.shape
    half = feats // INNER
    loads = []
    for doc in range(doc_count):
        for side in range(INNER):
            at = (1 - at_ref[0]) if side else at_ref[0]
            index = doc * INNER + side
            target = attn_s.at[doc, pl.ds(pl.multiple_of(at * half, half), half)]
            loads.append(begin(attn[index], target, attn_sem.at[index]))
    piece = grads[0].shape[1]
    for i in range(picked):
        cols = slice(i * piece, (i + 1) * piece)
        for k in range(part_count):

            @pl.when(at_ref[1 + i] == k)
            def _():
                begin(grads[k], grad_s.at[0, :, cols], grad_sem.at[i])

        loads.append(pltpu.make_async_copy(grads[0], grad_s.at[0, :, cols], grad_sem.at[i]))
    for doc in range(1, doc_count):
        loads.append(begin(swapped[doc - 1], grad_s.at[doc], grad_sem.at[picked + doc - 1]))
    for load in loads:
        load.wait()
    stores = []
    at = (1 - at_ref[0]) if sent else at_ref[0]
    for k in range(outer):
        cols = pl.ds(pl.multiple_of((k * INNER + at) * width, width), width)
        term = product(attn_s[0], grad_s[0, :, cols])
        for doc in range(1, doc_count):
            term = term + product(attn_s[doc], grad_s[doc, :, cols])
        out_s[k] = term.astype(out_s.dtype)
        stores.append(begin(out_s.at[k], out.at[k], out_sem.at[k]))
    for store in stores:
        store.wait()


def weight_terms(at, attn, grads, swapped, outer, picked, sent):
    half, rows = attn[0].shape
    feats = half * INNER
    doc_count = len(attn) // INNER
    columns = picked * grads[0].shape[1]
    width = columns // (outer * INNER)
    dtype = jnp.bfloat16 if sent else jnp.float32
    return call(
        functools.partial(weight_kernel, len(grads), picked, doc_count, sent),
        jax.ShapeDtypeStruct((outer, feats, width), dtype),
        [SMEM] + [ANY] * (len(attn) + len(grads) + len(swapped)),
        ANY,
        [
            pltpu.VMEM((doc_count, feats, rows), jnp.bfloat16),
            pltpu.VMEM((doc_count, rows, columns), jnp.bfloat16),
            pltpu.VMEM((outer, feats, width), dtype),
            pltpu.SemaphoreType.DMA((len(attn),)),
            pltpu.SemaphoreType.DMA((picked + doc_count - 1,)),
            pltpu.SemaphoreType.DMA((outer,)),
        ],
        doc_count * feats * rows * columns,
        2 * doc_count * rows * columns + 4 * feats * columns // INNER,
        "weight_sent" if sent else "weight_kept",
    )(at, *attn, *grads, *swapped)


def collect_kernel(at_ref, terms, dq_mine, dq_recv, grad_q, grad_k, grad_v, terms_s, out_s, *sems):
    term_sem, q_sem, out_sem = sems
    count, rows, both = terms.shape
    half = both // 2
    loads = [begin(terms.at[c], terms_s.at[c], term_sem.at[c]) for c in range(count)]
    for side, held in enumerate((dq_mine, dq_recv)):
        at = (1 - at_ref[0]) if side else at_ref[0]
        cols = pl.ds(pl.multiple_of(at * half, half), half)
        loads.append(begin(held, grad_q.at[:, cols], q_sem.at[side]))
    for load in loads[:count]:
        load.wait()
    for side in range(INNER):
        summed = terms_s[side].astype(jnp.float32)
        for c in range(side + INNER, count, INNER):
            summed = summed + terms_s[c].astype(jnp.float32)
        summed = summed.astype(jnp.bfloat16)
        cols = slice(side * half, (side + 1) * half)
        out_s[0, :, cols] = summed[:, :half]
        out_s[1, :, cols] = summed[:, half:]
    stores = [begin(out_s.at[0], grad_k, out_sem.at[0]), begin(out_s.at[1], grad_v, out_sem.at[1])]
    for copy in loads[count:] + stores:
        copy.wait()


def collect(at, terms, dq_mine, dq_recv):
    count, rows, both = terms.shape
    feats = both // 2 * INNER
    return call(
        collect_kernel,
        [bf16(rows, feats)] * 3,
        [SMEM] + [ANY] * 3,
        [ANY] * 3,
        [
            pltpu.VMEM((count, rows, both), jnp.bfloat16),
            pltpu.VMEM((2, rows, feats), jnp.bfloat16),
            pltpu.SemaphoreType.DMA((count,)),
            pltpu.SemaphoreType.DMA((2,)),
            pltpu.SemaphoreType.DMA((2,)),
        ],
        count * rows * both,
        2 * count * rows * both + 6 * rows * feats,
        "collect",
    )(at, terms, dq_mine, dq_recv)


def per_device(
    queries, key_heads, value_heads, grad_output, out_weight, block_pattern, global_offsets
):
    dp_count, ctx_count, tp_count = (lax.axis_size(name) for name in ("dp", "ctx", "tp"))
    dp_at, ctx_at, tp_at = (lax.axis_index(name) for name in ("dp", "ctx", "tp"))
    outer = ctx_count // INNER
    outer_at, inner_at = ctx_at // INNER, ctx_at % INNER
    picked = tp_count // dp_count
    place = [inner_at, outer_at]

    swap = [(i, i ^ 1) for i in range(ctx_count)]
    columns = [[o * INNER + i for o in range(outer)] for i in range(INNER)]

    def shift_pairs(count, step):
        return [(i, (i + step) % count) for i in range(count)]

    def dp_steps(which):
        return [(which * picked + i - tp_at) % tp_count for i in range(picked)]

    kv_send, q_theirs = part_heads(
        jnp.stack(place), queries[0], key_heads[0], value_heads[0], ctx_count
    )
    kv_all = lax.all_to_all(kv_send, "ctx", split_axis=0, concat_axis=0, tiled=True)
    grad_own = grad_output[0]
    grads = [grad_own] + [
        lax.ppermute(grad_own, "tp", shift_pairs(tp_count, -step)) for step in range(1, tp_count)
    ]
    q_recv = lax.ppermute(q_theirs, "ctx", swap)

    first, key_mask, row_mask = prelude(
        jnp.stack(place + [tp_at]), block_pattern, global_offsets, grad_own, out_weight
    )
    g_at = place + [(tp_at + step) % tp_count for step in range(1, tp_count)]
    g_at = g_at[:2] + [tp_at] + g_at[2:]
    for step in range(1, dp_count):
        g_at = g_at + dp_steps((dp_at + step) % dp_count)
    g_mine, g_theirs, grad_sends = grad_heads(
        jnp.stack(g_at), first, out_weight, grads, dp_count - 1, picked
    )
    g_recv = lax.ppermute(g_theirs, "ctx", swap)
    swapped = [
        lax.ppermute(send, "dp", shift_pairs(dp_count, step + 1))
        for step, send in enumerate(grad_sends)
    ]

    at = jnp.stack(place)
    weights, inverse, attn_mine, attn_theirs = forward(
        at, queries[0], q_recv, key_mask, row_mask, kv_all
    )

    attn = []
    for step in range(dp_count):
        for held, side in ((attn_mine, 0), (attn_theirs, 1)):
            pairs = [
                (d * ctx_count + c, ((d + step) % dp_count) * ctx_count + (c ^ side))
                for d in range(dp_count)
                for c in range(ctx_count)
            ]
            attn.append(lax.ppermute(held, ("dp", "ctx"), pairs) if step or side else held)

    dq_mine, dq_theirs, parts = backward(
        at, queries[0], q_recv, g_mine, g_recv, attn_mine, attn_theirs, inverse, weights, kv_all
    )
    terms = lax.all_to_all(parts, "ctx", split_axis=0, concat_axis=0, tiled=True)
    dq_recv = lax.ppermute(dq_theirs, "ctx", swap)

    weight_at = jnp.stack([inner_at] + dp_steps(dp_at))
    send = weight_terms(weight_at, attn, grads, swapped, outer, picked, True)
    weight_recv = lax.ppermute(send, "ctx", swap)
    keep = weight_terms(weight_at, attn, grads, swapped, outer, picked, False)
    weight_sum = (keep + weight_recv.astype(jnp.float32)).astype(jnp.bfloat16)
    weight_all = lax.all_to_all(
        weight_sum, "ctx", split_axis=0, concat_axis=0, axis_index_groups=columns, tiled=True
    )
    grad_weight = jnp.sum(weight_all.astype(jnp.float32), axis=0).astype(jnp.bfloat16)

    grad_q, grad_k, grad_v = collect(at, terms, dq_mine, dq_recv)
    return grad_q[None], grad_k[None], grad_v[None], grad_weight


def solution(mesh):
    in_specs = (
        P("dp", "ctx", "tp"),
        P("dp", "ctx", "tp"),
        P("dp", "ctx", "tp"),
        P("dp", "ctx", "tp"),
        P("tp", None),
        P(),
        P(),
    )
    out_specs = (
        P("dp", "ctx", "tp"),
        P("dp", "ctx", "tp"),
        P("dp", "ctx", "tp"),
        P("tp", ("dp", "ctx")),
    )
    return jax.shard_map(
        per_device, mesh=mesh, in_specs=in_specs, out_specs=out_specs, check_vma=False
    )
```

time: 129 us -> 181 us (1.40)
  Pallas kernels: 22.9 us -> 100 us
  waiting for transfers between devices: 50.6 us -> 41.2 us
  local copies, waits for them, and re-layouts: 15.7 us -> 6.54 us
  other arithmetic: 8.27 us -> 4.75 us
  starting transfers between devices: 29.4 us -> 26.9 us
    pallas_call x4 -> x6, Pallas kernels: 9.44 us -> 86.1 us  [the longest x1 35.7 us: part_heads(): call(part_kernel, [bf16(count, rows, 2 * half), bf16(rows, half)], [SMEM]...]
    ppermute x16 -> x2, starting transfers between devices: 22.5 us -> 1.47 us  [the longest x1 1.4 us: per_device(): weight_recv = lax.ppermute(send, 'ctx', swap)]
    ppermute x1, waiting for transfers between devices: 19.5 us -> 0.01 us  [per_device(): lax.ppermute(grad_own, 'tp', shift_pairs(tp_count, -step))]
    all_to_all x0 -> x3, waiting for transfers between devices: none -> 17.1 us  [the longest x1 15.9 us: per_device(): lax.all_to_all(parts, 'ctx', split_axis=0, concat_axis=0, tiled=True)]
    all_to_all x0 -> x3, starting transfers between devices: none -> 15.2 us  [the longest x1 5.82 us: per_device(): lax.all_to_all(kv_send, 'ctx', split_axis=0, concat_axis=0, tiled=True)]
    ppermute x16 -> x2, waiting for transfers between devices: 23.9 us -> 8.96 us  [the longest x1 8.96 us: per_device(): weight_recv = lax.ppermute(send, 'ctx', swap)]
    unnamed x46 -> x29, local copies, waits for them, and re-layouts: 11.8 us -> 5.89 us
    ppermute x1, waiting for transfers between devices: 0.01 us -> 3.11 us  [per_device(): g_recv = lax.ppermute(g_theirs, 'ctx', swap)]
  transfers between devices with their start and end apart: 23 -> 12, of which waited for: 9 -> 8; matrix products, arithmetic and copies ran while one was open for 10% -> 2% of each run, Pallas kernels for 17% -> 50%
where the time goes in v3:
time: 181 us; the launch traced here: 180 us
  Pallas kernels  100 us (55%)
  waiting for transfers between devices  41.2 us (23%)
  starting transfers between devices  26.9 us (15%)
  local copies, waits for them, and re-layouts  6.54 us (4%)
  other arithmetic  4.75 us (3%)
    pallas_call x1, Pallas kernels, part_heads(): call(part_kernel, [bf16(count, rows, 2 * half), bf16(rows, half)], [SMEM]...  35.7 us
    pallas_call x1, Pallas kernels, grad_heads(): call(functools.partial(grad_heads_kernel, count, sends, picked), [bf16(ha...  33.7 us
    all_to_all x1, waiting for transfers between devices, per_device(): lax.all_to_all(parts, 'ctx', split_axis=0, concat_axis=0, tiled=True)  15.9 us
    ppermute x1, waiting for transfers between devices, per_device(): weight_recv = lax.ppermute(send, 'ctx', swap)  8.96 us
    pallas_call x1, Pallas kernels, backward(): call(functools.partial(backward_kernel, block_count, heads), [bf16(rows,...  7.83 us
    pallas_call x2, Pallas kernels, weight_terms(): call(functools.partial(weight_kernel, len(grads), picked, doc_count, sent...  7.33 us
    pallas_call x1, Pallas kernels, forward(): call(functools.partial(forward_kernel, block_count, heads), [bf16(heads,...  6.17 us
    unnamed x29, local copies, waits for them, and re-layouts  5.89 us
  transfers between devices with their start and end apart: 12, of which 8 were waited for; matrix products, arithmetic and copies ran while one was open for 2% of the time, Pallas kernels for 50%

profile of v3, /device:TPU:0, one launch (start us, length us, event | category | flops | bytes accessed | tf_op | source)
XLA Modules:
  0.0 180.2 jit_solution(15114377722142975117)
XLA Ops:
  0.6 0.0 copy-start.8
  0.6 3.0 %collective-permute-start.1 = (bf16[256,2048]{1,0:T(8,128)(2,1)}, bf16[256,2048]{1,0:T(8,128)(2,1)S(1)}, u32[]{:S(2)}, u32[]{:S(2)}) collective-permute-start(bf16[256,2048]{1,0:T(8,128)(2,1)} %bitcast.13), channel_id=1, source_target_pairs={{0,1},{1,0},{2,3},{3,2},{4,5},{5,4},{6,7},{7,6},{8,9},{9,8},{10,11... | collective-permute-start | bytes 3145736 | tf_op jit(solution)/shard_map/ppermute | solution.py:526
  3.7 0.6 pad_add_fusion.at_ref
  4.3 35.7 %part_heads.1 = (bf16[8,256,256]{2,1,0:T(8,128)(2,1)}, bf16[256,128]{1,0:T(8,128)(2,1)}) custom-call(s32[2]{0:T(128)} %pad_add_fusion.at_ref, bf16[256,256]{1,0:T(8,128)(2,1)} %bitcast.20, bf16[256,256]{1,0:T(8,128)(2,1)} %bitcast.18, bf16[256,256]{1,0:T(8,128)(2,1)} %bitcast.19), custom_call_target="tpu_custom_call" | custom-call | bytes 2097152 | tf_op jit(solution)/shard_map/part_heads/pallas_call | solution.py:69
  40.0 5.8 %all-to-all-start = ((bf16[8,256,256]{2,1,0:T(8,128)(2,1)}), bf16[8,256,256]{2,1,0:T(8,128)(2,1)S(1)}, u32[]{:S(2)}, u32[]{:S(2)}) async-start(bf16[8,256,256]{2,1,0:T(8,128)(2,1)} %get-tuple-element.28), calls=%async_computation | async-start | bytes 2097152 | tf_op jit(solution)/shard_map/all_to_all | solution.py:523
  45.8 0.0 copy-done.8
  45.8 0.7 copy.11.pattern
  46.5 0.7 stack.45.at_ref
  47.1 0.7 pad_add_fusion.1.at_ref
  47.8 3.5 %prelude.1 = (f32[256,256]{1,0:T(8,128)}, bf16[2048,128]{1,0:T(8,128)(2,1)}, f32[8,512]{1,0:T(8,128)}) custom-call(s32[3]{0:T(128)} %pad_add_fusion.1.at_ref, s32[8,3]{1,0:T(8,128)} %copy.11.pattern, s32[8,8]{1,0:T(8,128)} %offsets.1, bf16[256,2048]{1,0:T(8,128)(2,1)} %bitcast.14, bf16[256,4096]{1,0:T(8,128)(2,1)} %weight_ref.3), custom_call_target="tpu_custom_call" | custom-call | flops 268435456 | bytes 2097152 | tf_op jit(solution)/shard_map/prelude/pallas_call | solution.py:124
  51.3 0.0 collective-permute-done.1.refs_1_.refs_5_
  51.3 0.0 copy-start
  51.3 1.0 copy-done
  52.3 0.0 copy-start.9
  52.3 33.7 %grad_heads.1 = (bf16[128,256]{1,0:T(8,128)(2,1)}, bf16[128,256]{1,0:T(8,128)(2,1)}, bf16[256,2048]{1,0:T(8,128)(2,1)}) custom-call(s32[5]{0:T(128)} %stack.45.at_ref, f32[256,256]{1,0:T(8,128)} %get-tuple-element.23.first_ref, bf16[256,4096]{1,0:T(8,128)(2,1)} %weight_ref.3, bf16[256,2048]{1,0:T(8,128)(2,1)} %bitcast.15, bf16[256,2048]{1,0:T(8,128)(2,1)} %copy-done), custom_call_target="tpu_custom_call" | custom-call | flops 268435456 | bytes 4194304 | tf_op jit(solution)/shard_map/grad_heads/pallas_call | solution.py:368
  86.0 0.1 collective-permute-start.7
  86.1 0.0 copy-done.9
  86.1 2.1 %collective-permute-start = (bf16[256,128]{1,0:T(8,128)(2,1)S(1)}, bf16[256,128]{1,0:T(8,128)(2,1)S(1)}, u32[]{:S(2)}, u32[]{:S(2)}) collective-permute-start(bf16[256,128]{1,0:T(8,128)(2,1)S(1)} %copy-done.9), channel_id=1, source_target_pairs={{0,2},{2,0},{4,6},{6,4},{8,10},{10,8},{12,14},{14,12},{1,3},{3,1},... | collective-permute-start | bytes 196616 | tf_op jit(solution)/shard_map/ppermute | solution.py:528
  88.2 2.7 %collective-permute-done.q_recv.refs_1_ = bf16[256,128]{1,0:T(8,128)(2,1)S(1)} collective-permute-done((bf16[256,128]{1,0:T(8,128)(2,1)S(1)}, bf16[256,128]{1,0:T(8,128)(2,1)S(1)}, u32[]{:S(2)}, u32[]{:S(2)}) %collective-permute-start) | collective-permute-done | bytes 65568 | tf_op jit(solution)/shard_map/ppermute | solution.py:528
  90.9 0.0 copy-start.11
  90.9 0.0 all-to-all-done.kv_ref.refs_8_
  90.9 0.0 copy-start.3
  90.9 0.6 copy-done.11
  91.5 0.4 copy-done.3
  91.9 6.2 %forward.1 = (bf16[1,2048,512]{2,1,0:T(8,128)(2,1)}, f32[8,512]{1,0:T(8,128)}, bf16[128,256]{1,0:T(8,128)(2,1)}, bf16[128,256]{1,0:T(8,128)(2,1)}) custom-call(s32[2]{0:T(128)} %pad_add_fusion.at_ref, bf16[256,256]{1,0:T(8,128)(2,1)} %bitcast.21, bf16[256,128]{1,0:T(8,128)(2,1)} %copy-done.11, bf16[2048,128]{1,0:T(8,128)(2,1)} %get-tuple-element.26.key_mask, ...), custom_call_target="tpu_custom_call" | custom-call | flops 536870912 | bytes 4194304 | tf_op jit(solution)/shard_map/forward/pallas_call | solution.py:207
  98.1 1.1 collective-permute-start.6
  99.2 0.8 collective-permute-start.4
  100.0 0.1 collective-permute-start.5
  100.0 0.6 pad_add_fusion.2.at_ref
  100.6 1.8 %collective-permute-done.6.refs_3_ = bf16[128,256]{1,0:T(8,128)(2,1)S(1)} collective-permute-done((bf16[128,256]{1,0:T(8,128)(2,1)}, bf16[128,256]{1,0:T(8,128)(2,1)S(1)}, u32[]{:S(2)}, u32[]{:S(2)}) %collective-permute-start.6) | collective-permute-done | bytes 65568 | tf_op jit(solution)/shard_map/ppermute | solution.py:559
  102.4 0.0 copy-start.4
  102.4 1.8 %collective-permute-done.4.refs_1_ = bf16[128,256]{1,0:T(8,128)(2,1)S(1)} collective-permute-done((bf16[128,256]{1,0:T(8,128)(2,1)}, bf16[128,256]{1,0:T(8,128)(2,1)S(1)}, u32[]{:S(2)}, u32[]{:S(2)}) %collective-permute-start.4) | collective-permute-done | bytes 65568 | tf_op jit(solution)/shard_map/ppermute | solution.py:559
  104.2 0.0 copy-start.5
  104.2 0.0 collective-permute-done.5.refs_2_
  104.2 0.0 copy-start.6
  104.2 0.0 collective-permute-done.7.refs_6_
  104.2 0.0 copy-done.4
  104.3 0.6 copy-done.5
  104.9 0.0 copy-done.6
  104.9 0.0 copy-start.1
  104.9 1.0 copy-done.1
  105.9 3.6 %weight_sent.1 = bf16[4,256,256]{2,1,0:T(8,128)(2,1)} custom-call(s32[2]{0:T(128)} %pad_add_fusion.2.at_ref, bf16[128,256]{1,0:T(8,128)(2,1)} %get-tuple-element.29.refs_4_.refs_0_, bf16[128,256]{1,0:T(8,128)(2,1)} %copy-done.5, bf16[128,256]{1,0:T(8,128)(2,1)} %copy-done.6, bf16[128,256]{1,0:T(8,128)(2,1)} %copy-done.4, bf16[256,2048]{1,0:T(8,128)(2,1)} %bitcast.16, ...), custom_call_target="tpu_custom_call" | custom-call | flops 268435456 | bytes 3145728 | tf_op jit(solution)/shard_map/weight_sent/pallas_call | solution.py:437
  109.5 1.4 collective-permute-start.8
  110.9 3.7 %weight_kept.1 = f32[4,256,256]{2,1,0:T(8,128)} custom-call(s32[2]{0:T(128)} %pad_add_fusion.2.at_ref, bf16[128,256]{1,0:T(8,128)(2,1)} %get-tuple-element.29.refs_4_.refs_0_, bf16[128,256]{1,0:T(8,128)(2,1)} %copy-done.5, bf16[128,256]{1,0:T(8,128)(2,1)} %copy-done.6, bf16[128,256]{1,0:T(8,128)(2,1)} %copy-done.4, bf16[256,2048]{1,0:T(8,128)(2,1)} %bitcast.17, ...), custom_call_target="tpu_custom_call" | custom-call | flops 268435456 | bytes 3145728 | tf_op jit(solution)/shard_map/weight_kept/pallas_call | solution.py:437
  114.6 0.0 copy-start.10
  114.6 9.0 %collective-permute-done.8 = bf16[4,256,256]{2,1,0:T(8,128)(2,1)S(1)} collective-permute-done((bf16[4,256,256]{2,1,0:T(8,128)(2,1)}, bf16[4,256,256]{2,1,0:T(8,128)(2,1)S(1)}, u32[]{:S(2)}, u32[]{:S(2)}) %collective-permute-start.8) | collective-permute-done | bytes 524320 | tf_op jit(solution)/shard_map/ppermute | solution.py:569
  123.6 2.1 %add_convert_fusion = bf16[4,256,256]{2,1,0:T(8,128)(2,1)} fusion(f32[4,256,256]{2,1,0:T(8,128)} %weight_kept.1, bf16[4,256,256]{2,1,0:T(8,128)(2,1)S(1)} %collective-permute-done.8), kind=kLoop, calls=%fused_computation | loop fusion | flops 786432 | bytes 2097152 | tf_op jit(solution)/shard_map/convert_element_type | solution.py:571
  125.7 4.8 %all-to-all-start.2 = ((bf16[4,256,256]{2,1,0:T(8,128)(2,1)}), bf16[4,256,256]{2,1,0:T(8,128)(2,1)S(1)}, u32[]{:S(2)}, u32[]{:S(2)}) async-start(bf16[4,256,256]{2,1,0:T(8,128)(2,1)} %add_convert_fusion), calls=%async_computation.2 | async-start | bytes 1048576 | tf_op jit(solution)/shard_map/all_to_all | solution.py:572
  130.5 0.0 copy-done.10
  130.6 1.2 collective-permute-start.2
  131.7 3.1 %collective-permute-done.2.refs_3_ = bf16[128,256]{1,0:T(8,128)(2,1)S(1)} collective-permute-done((bf16[128,256]{1,0:T(8,128)(2,1)S(1)}, bf16[128,256]{1,0:T(8,128)(2,1)S(1)}, u32[]{:S(2)}, u32[]{:S(2)}) %collective-permute-start.2) | collective-permute-done | bytes 65568 | tf_op jit(solution)/shard_map/ppermute | solution.py:540
  134.8 0.6 copy-done.13
  135.4 7.8 %backward.1 = (bf16[256,128]{1,0:T(8,128)(2,1)}, bf16[256,128]{1,0:T(8,128)(2,1)}, bf16[8,256,256]{2,1,0:T(8,128)(2,1)}) custom-call(s32[2]{0:T(128)} %pad_add_fusion.at_ref, bf16[256,256]{1,0:T(8,128)(2,1)} %bitcast.22, bf16[256,128]{1,0:T(8,128)(2,1)} %copy-done.11, bf16[128,256]{1,0:T(8,128)(2,1)} %get-tuple-element.24.refs_2_, ...), custom_call_target="tpu_custom_call" | custom-call | flops 1073741824 | bytes 6291456 | tf_op jit(solution)/shard_map/backward/pallas_call | solution.py:297
  143.3 0.0 copy-start.12
  143.3 1.2 all-to-all-done.2
  144.5 4.5 %all-to-all-start.1 = ((bf16[8,256,256]{2,1,0:T(8,128)(2,1)}), bf16[8,256,256]{2,1,0:T(8,128)(2,1)S(1)}, u32[]{:S(2)}, u32[]{:S(2)}) async-start(bf16[8,256,256]{2,1,0:T(8,128)(2,1)} %get-tuple-element.33), calls=%async_computation.1 | async-start | bytes 2097152 | tf_op jit(solution)/shard_map/all_to_all | solution.py:564
  149.0 0.0 copy-done.12
  149.0 2.0 %collective-permute-start.3 = (bf16[256,128]{1,0:T(8,128)(2,1)S(1)}, bf16[256,128]{1,0:T(8,128)(2,1)S(1)}, u32[]{:S(2)}, u32[]{:S(2)}) collective-permute-start(bf16[256,128]{1,0:T(8,128)(2,1)S(1)} %copy-done.12), channel_id=1, source_target_pairs={{0,2},{2,0},{4,6},{6,4},{8,10},{10,8},{12,14},{14,12},{1,3},{3,1},... | collective-permute-start | bytes 196616 | tf_op jit(solution)/shard_map/ppermute | solution.py:565
  151.0 0.7 reduce_sum.12
  151.8 5.7 %collective-permute-done.3.dq_recv = bf16[256,128]{1,0:T(8,128)(2,1)S(1)} collective-permute-done((bf16[256,128]{1,0:T(8,128)(2,1)S(1)}, bf16[256,128]{1,0:T(8,128)(2,1)S(1)}, u32[]{:S(2)}, u32[]{:S(2)}) %collective-permute-start.3) | collective-permute-done | bytes 65568 | tf_op jit(solution)/shard_map/ppermute | solution.py:565
  157.5 15.9 %all-to-all-done.1.terms = bf16[8,256,256]{2,1,0:T(8,128)(2,1)S(1)} async-done(((bf16[8,256,256]{2,1,0:T(8,128)(2,1)}), bf16[8,256,256]{2,1,0:T(8,128)(2,1)S(1)}, u32[]{:S(2)}, u32[]{:S(2)}) %all-to-all-start.1) | async-done | bytes 1048608 | tf_op jit(solution)/shard_map/all_to_all | solution.py:564
  173.4 0.0 copy-done.7
  173.4 1.0 copy-done.2
  174.4 5.9 %collect.1 = (bf16[256,256]{1,0:T(8,128)(2,1)}, bf16[256,256]{1,0:T(8,128)(2,1)}, bf16[256,256]{1,0:T(8,128)(2,1)}) custom-call(s32[2]{0:T(128)} %pad_add_fusion.at_ref, bf16[8,256,256]{2,1,0:T(8,128)(2,1)} %copy-done.2, bf16[256,128]{1,0:T(8,128)(2,1)} %get-tuple-element.34.dq_mine, bf16[256,128]{1,0:T(8,128)(2,1)} %copy-done.7), custom_call_target="tpu_custom_call" | custom-call | flops 524288 | bytes 1441792 | tf_op jit(solution)/shard_map/collect/pallas_call | solution.py:483
  (3 shorter events, 0.0 us)
Async XLA Ops:
  0.6 45.1 %copy-start.8 = (s32[8,3]{0,1:T(4,128)S(1)}, s32[8,3]{0,1:T(4,128)}, u32[]{:S(2)}) copy-start(s32[8,3]{0,1:T(4,128)} %param.12) | copy-start | bytes 292
  0.6 50.7 %collective-permute-start.1 = (bf16[256,2048]{1,0:T(8,128)(2,1)}, bf16[256,2048]{1,0:T(8,128)(2,1)S(1)}, u32[]{:S(2)}, u32[]{:S(2)}) collective-permute-start(bf16[256,2048]{1,0:T(8,128)(2,1)} %bitcast.13), channel_id=1, source_target_pairs={{0,1},{1,0},{2,3},{3,2},{4,5},{5,4},{6,7},{7,6},{8,9},{9,8},{10,11... | collective-permute-start | bytes 3145736 | tf_op jit(solution)/shard_map/ppermute | solution.py:526
  40.0 50.9 %all-to-all-start = ((bf16[8,256,256]{2,1,0:T(8,128)(2,1)}), bf16[8,256,256]{2,1,0:T(8,128)(2,1)S(1)}, u32[]{:S(2)}, u32[]{:S(2)}) async-start(bf16[8,256,256]{2,1,0:T(8,128)(2,1)} %get-tuple-element.28), calls=%async_computation | async-start | bytes 2097152 | tf_op jit(solution)/shard_map/all_to_all | solution.py:523
  51.3 1.0 copy-start
  52.3 33.8 %copy-start.9 = (bf16[256,128]{1,0:T(8,128)(2,1)S(1)}, bf16[256,128]{1,0:T(8,128)(2,1)}, u32[]{:S(2)}) copy-start(bf16[256,128]{1,0:T(8,128)(2,1)} %get-tuple-element.22) | copy-start | bytes 196612
  86.0 18.2 %collective-permute-start.7 = (bf16[256,2048]{1,0:T(8,128)(2,1)}, bf16[256,2048]{1,0:T(8,128)(2,1)S(1)}, u32[]{:S(2)}, u32[]{:S(2)}) collective-permute-start(bf16[256,2048]{1,0:T(8,128)(2,1)} %get-tuple-element.39), channel_id=1, source_target_pairs={{0,16},{16,0},{1,17},{17,1},{2,18},{18,2},{3,19},{19,3},{4,20},{20... | collective-permute-start | bytes 3145736 | tf_op jit(solution)/shard_map/ppermute | solution.py:542
  86.1 4.8 %collective-permute-start = (bf16[256,128]{1,0:T(8,128)(2,1)S(1)}, bf16[256,128]{1,0:T(8,128)(2,1)S(1)}, u32[]{:S(2)}, u32[]{:S(2)}) collective-permute-start(bf16[256,128]{1,0:T(8,128)(2,1)S(1)} %copy-done.9), channel_id=1, source_target_pairs={{0,2},{2,0},{4,6},{6,4},{8,10},{10,8},{12,14},{14,12},{1,3},{3,1},... | collective-permute-start | bytes 196616 | tf_op jit(solution)/shard_map/ppermute | solution.py:528
  90.9 0.6 copy-start.11
  90.9 1.0 copy-start.3
  98.1 4.4 %collective-permute-start.6 = (bf16[128,256]{1,0:T(8,128)(2,1)}, bf16[128,256]{1,0:T(8,128)(2,1)S(1)}, u32[]{:S(2)}, u32[]{:S(2)}) collective-permute-start(bf16[128,256]{1,0:T(8,128)(2,1)} %get-tuple-element.30.refs_5_), channel_id=1, source_target_pairs={{0,18},{2,16},{4,22},{6,20},{8,26},{10,24},{12,30},{14,28},{16,2},... | collective-permute-start | bytes 196616 | tf_op jit(solution)/shard_map/ppermute | solution.py:559
  99.2 5.1 %collective-permute-start.4 = (bf16[128,256]{1,0:T(8,128)(2,1)}, bf16[128,256]{1,0:T(8,128)(2,1)S(1)}, u32[]{:S(2)}, u32[]{:S(2)}) collective-permute-start(bf16[128,256]{1,0:T(8,128)(2,1)} %get-tuple-element.30.refs_5_), channel_id=1, source_target_pairs={{0,2},{2,0},{4,6},{6,4},{8,10},{10,8},{12,14},{14,12},{16,18},{18,... | collective-permute-start | bytes 196616 | tf_op jit(solution)/shard_map/ppermute | solution.py:559
  100.0 4.3 %collective-permute-start.5 = (bf16[128,256]{1,0:T(8,128)(2,1)}, bf16[128,256]{1,0:T(8,128)(2,1)S(1)}, u32[]{:S(2)}, u32[]{:S(2)}) collective-permute-start(bf16[128,256]{1,0:T(8,128)(2,1)} %get-tuple-element.29.refs_4_.refs_0_), channel_id=1, source_target_pairs={{0,16},{2,18},{4,20},{6,22},{8,24},{10,26},{12,28},{14,30},{16,0},... | collective-permute-start | bytes 196616 | tf_op jit(solution)/shard_map/ppermute | solution.py:559
  102.4 1.8 %copy-start.4 = (bf16[128,256]{1,0:T(8,128)(2,1)}, bf16[128,256]{1,0:T(8,128)(2,1)S(1)}, u32[]{:S(2)}) copy-start(bf16[128,256]{1,0:T(8,128)(2,1)S(1)} %collective-permute-done.6.refs_3_) | copy-start | bytes 196612
  104.2 0.6 copy-start.5
  104.2 0.6 copy-start.6
  104.9 1.0 copy-start.1
  109.5 14.1 %collective-permute-start.8 = (bf16[4,256,256]{2,1,0:T(8,128)(2,1)}, bf16[4,256,256]{2,1,0:T(8,128)(2,1)S(1)}, u32[]{:S(2)}, u32[]{:S(2)}) collective-permute-start(bf16[4,256,256]{2,1,0:T(8,128)(2,1)} %weight_sent.1), channel_id=1, source_target_pairs={{0,2},{2,0},{4,6},{6,4},{8,10},{10,8},{12,14},{14,12},{1,3},{3,1},... | collective-permute-start | bytes 1572872 | tf_op jit(solution)/shard_map/ppermute | solution.py:569
  114.6 15.9 %copy-start.10 = (bf16[128,256]{1,0:T(8,128)(2,1)S(1)}, bf16[128,256]{1,0:T(8,128)(2,1)}, u32[]{:S(2)}) copy-start(bf16[128,256]{1,0:T(8,128)(2,1)} %get-tuple-element.25) | copy-start | bytes 196612
  125.7 18.7 %all-to-all-start.2 = ((bf16[4,256,256]{2,1,0:T(8,128)(2,1)}), bf16[4,256,256]{2,1,0:T(8,128)(2,1)S(1)}, u32[]{:S(2)}, u32[]{:S(2)}) async-start(bf16[4,256,256]{2,1,0:T(8,128)(2,1)} %add_convert_fusion), calls=%async_computation.2 | async-start | bytes 1048576 | tf_op jit(solution)/shard_map/all_to_all | solution.py:572
  130.6 4.3 %collective-permute-start.2 = (bf16[128,256]{1,0:T(8,128)(2,1)S(1)}, bf16[128,256]{1,0:T(8,128)(2,1)S(1)}, u32[]{:S(2)}, u32[]{:S(2)}) collective-permute-start(bf16[128,256]{1,0:T(8,128)(2,1)S(1)} %copy-done.10), channel_id=1, source_target_pairs={{0,2},{2,0},{4,6},{6,4},{8,10},{10,8},{12,14},{14,12},{1,3},{3,1},... | collective-permute-start | bytes 196616 | tf_op jit(solution)/shard_map/ppermute | solution.py:540
  134.8 0.6 copy-start.13
  143.3 5.7 %copy-start.12 = (bf16[256,128]{1,0:T(8,128)(2,1)S(1)}, bf16[256,128]{1,0:T(8,128)(2,1)}, u32[]{:S(2)}) copy-start(bf16[256,128]{1,0:T(8,128)(2,1)} %get-tuple-element.35) | copy-start | bytes 196612
  144.5 28.9 %all-to-all-start.1 = ((bf16[8,256,256]{2,1,0:T(8,128)(2,1)}), bf16[8,256,256]{2,1,0:T(8,128)(2,1)S(1)}, u32[]{:S(2)}, u32[]{:S(2)}) async-start(bf16[8,256,256]{2,1,0:T(8,128)(2,1)} %get-tuple-element.33), calls=%async_computation.1 | async-start | bytes 2097152 | tf_op jit(solution)/shard_map/all_to_all | solution.py:564
  149.0 8.4 %collective-permute-start.3 = (bf16[256,128]{1,0:T(8,128)(2,1)S(1)}, bf16[256,128]{1,0:T(8,128)(2,1)S(1)}, u32[]{:S(2)}, u32[]{:S(2)}) collective-permute-start(bf16[256,128]{1,0:T(8,128)(2,1)S(1)} %copy-done.12), channel_id=1, source_target_pairs={{0,2},{2,0},{4,6},{6,4},{8,10},{10,8},{12,14},{14,12},{1,3},{3,1},... | collective-permute-start | bytes 196616 | tf_op jit(solution)/shard_map/ppermute | solution.py:565
  157.5 16.0 %copy-start.7 = (bf16[256,128]{1,0:T(8,128)(2,1)}, bf16[256,128]{1,0:T(8,128)(2,1)S(1)}, u32[]{:S(2)}) copy-start(bf16[256,128]{1,0:T(8,128)(2,1)S(1)} %collective-permute-done.3.dq_recv) | copy-start | bytes 196612
  173.4 1.0 copy-start.2

commit v4 on v3

v4 whole, which is shorter than its diff:
```python
import functools

import jax
import jax.numpy as jnp
from jax import lax
from jax.experimental import pallas as pl
from jax.experimental.pallas import tpu as pltpu
from jax.sharding import PartitionSpec as P

HD = 128
MASKED = -1e30
INNER = 2
HBM = pl.BlockSpec(memory_space=pltpu.HBM)
VMEM = pl.BlockSpec(memory_space=pltpu.VMEM)
SMEM = pl.BlockSpec(memory_space=pltpu.SMEM)


def against(left_op, right_op):
    return lax.dot_general(
        left_op, right_op, (((1,), (1,)), ((), ())), preferred_element_type=jnp.float32
    )


def product(left_op, right_op):
    return jnp.dot(left_op, right_op, preferred_element_type=jnp.float32)


def begin(source, target, semaphore):
    copy = pltpu.make_async_copy(source, target, semaphore)
    copy.start()
    return copy


def call(kernel, out_shape, in_specs, out_specs, scratch, name, after=()):
    skipped = len(after)
    run = pl.pallas_call(
        lambda *refs: kernel(*refs[skipped:]),
        out_shape=out_shape,
        in_specs=[HBM] * skipped + in_specs,
        out_specs=out_specs,
        scratch_shapes=scratch,
        compiler_params=pltpu.CompilerParams(vmem_limit_bytes=32 * 1024 * 1024),
        cost_estimate=pl.CostEstimate(flops=1, bytes_accessed=1, transcendentals=0),
        name=name,
    )
    return functools.partial(run, *after)


def bf16(*shape):
    return jax.ShapeDtypeStruct(shape, jnp.bfloat16)


def part_kernel(at_ref, q_ref, k_ref, v_ref, k_send, v_send, q_theirs, held_s, in_sem, out_sem):
    half = q_theirs.shape[1]
    count = k_send.shape[0]
    loads = [begin(held, held_s.at[i], in_sem.at[i]) for i, held in enumerate((k_ref, v_ref, q_ref))]
    copies = []
    for index, send in enumerate((k_send, v_send)):
        loads[index].wait()
        for place in range(count):
            side = place % INNER
            source = held_s.at[index, :, side * half : (side + 1) * half]
            copies.append(begin(source, send.at[place], out_sem.at[index * count + place]))
    loads[2].wait()
    theirs = pl.ds(pl.multiple_of((1 - at_ref[0]) * half, half), half)
    copies.append(begin(held_s.at[2, :, theirs], q_theirs, out_sem.at[2 * count]))
    for copy in copies:
        copy.wait()


def part_heads(at, queries, keys, values, count):
    rows, feats = queries.shape
    half = feats // INNER
    return call(
        part_kernel,
        [bf16(count, rows, half), bf16(count, rows, half), bf16(rows, half)],
        [SMEM] + [HBM] * 3,
        [HBM] * 3,
        [
            pltpu.VMEM((3, rows, feats), jnp.bfloat16),
            pltpu.SemaphoreType.DMA((3,)),
            pltpu.SemaphoreType.DMA((2 * count + 1,)),
        ],
        "part_heads",
    )(at, queries, keys, values)


def prelude_kernel(at_ref, pattern, offsets, grad_ref, weight_ref, first, key_mask, row_mask, *rest):
    grad_s, weight_s, sem = rest
    rows, width = grad_s.shape
    block_count, glob_count = offsets.shape
    start = pl.multiple_of(at_ref[2] * width, width)
    loads = [
        begin(grad_ref, grad_s, sem.at[0]),
        begin(weight_ref.at[:, pl.ds(start, width)], weight_s, sem.at[1]),
    ]
    own = at_ref[1] * INNER + at_ref[0]
    partner = at_ref[1] * INNER + 1 - at_ref[0]
    lane = lax.broadcasted_iota(jnp.int32, (1, HD), 1)
    row_at = lax.broadcasted_iota(jnp.int32, (rows, HD), 0)
    col_at = lax.broadcasted_iota(jnp.int32, (8, rows), 1)
    group_at = lax.broadcasted_iota(jnp.int32, (8, rows), 0)
    for block in range(block_count):
        hidden = []
        for target in (own, partner):
            seen = jnp.abs(block - target) <= 1
            for r in range(pattern.shape[1]):
                seen = seen | (pattern[target, r] == block)
            hidden.append(jnp.where(seen, 0, 1))
        lane_hidden = jnp.where(lane == 0, hidden[0], jnp.where(lane == 1, hidden[1], 0))
        hidden_rows = jnp.broadcast_to(lane_hidden, (rows, HD))
        for r in range(glob_count):
            hidden_rows = jnp.where(row_at == offsets[block, r], 0, hidden_rows)
        key_mask[block * rows : (block + 1) * rows, :] = hidden_rows.astype(jnp.float32).astype(
            jnp.bfloat16
        )
    for group, target in enumerate((own, partner)):
        local = jnp.where(group_at == group, MASKED, 0.0)
        for r in range(glob_count):
            local = jnp.where(col_at == offsets[target, r], 0.0, local)
        row_mask[:, group * rows : (group + 1) * rows] = local
    for load in loads:
        load.wait()
    first[...] = against(weight_s[...], grad_s[...])


def prelude(at, pattern, offsets, grad_own, out_weight):
    rows, width = grad_own.shape
    feats = out_weight.shape[0]
    keys = offsets.shape[0] * rows
    return call(
        prelude_kernel,
        [
            jax.ShapeDtypeStruct((feats, rows), jnp.float32),
            bf16(keys, HD),
            jax.ShapeDtypeStruct((8, 2 * rows), jnp.float32),
        ],
        [SMEM] * 3 + [HBM] * 2,
        [VMEM] * 3,
        [
            pltpu.VMEM((rows, width), jnp.bfloat16),
            pltpu.VMEM((feats, width), jnp.bfloat16),
            pltpu.SemaphoreType.DMA((2,)),
        ],
        "prelude",
    )(at, pattern, offsets, grad_own, out_weight)


def softmax_kernel(at_ref, q_ref, q_recv, key_mask, row_mask, k_ref, e_out, inv_out, *scratch):
    q_s, k_s, s_ref, sem, k_sem = scratch
    rows, feats = q_recv.shape
    block_count = k_ref.shape[0]
    score_scale = HD ** (-0.5)
    mine = pl.ds(pl.multiple_of(at_ref[0] * feats, feats), feats)
    loads = [begin(q_ref.at[:, mine], q_s.at[0], sem.at[0]), begin(q_recv, q_s.at[1], sem.at[1])]
    k_loads = [begin(k_ref.at[j], k_s.at[j], k_sem.at[j]) for j in range(block_count)]
    for load in loads:
        load.wait()
    rows_low = row_mask[...].astype(jnp.bfloat16)
    hidden = jnp.concatenate([rows_low, jnp.zeros((HD - 8, 2 * rows), jnp.bfloat16)], axis=0)
    for head in range(feats // HD):
        cols = slice(head * HD, (head + 1) * HD)
        q_t = jnp.concatenate(
            [jnp.transpose(q_s[0, :, cols]), jnp.transpose(q_s[1, :, cols])], axis=1
        )
        q_t = jnp.concatenate([q_t, hidden], axis=0)
        top = jnp.full((1, 2 * rows), MASKED, jnp.float32)
        for j in range(block_count):
            if head == 0:
                k_loads[j].wait()
            keys = slice(j * rows, (j + 1) * rows)
            scores = product(jnp.concatenate([k_s[j, :, cols], key_mask[keys, :]], axis=1), q_t)
            s_ref[keys, :] = scores
            top = jnp.maximum(top, jnp.max(scores, axis=0, keepdims=True))
        total = jnp.zeros((1, 2 * rows), jnp.float32)
        for j in range(block_count):
            keys = slice(j * rows, (j + 1) * rows)
            weights = jnp.exp((s_ref[keys, :] - top) * score_scale)
            total = total + jnp.sum(weights, axis=0, keepdims=True)
            e_out[head, keys, :] = weights.astype(jnp.bfloat16)
        inv_out[head : head + 1, :] = 1.0 / total


def softmax(at, queries, q_recv, key_mask, row_mask, k_all):
    block_count, rows, feats = k_all.shape
    heads = feats // HD
    keys = block_count * rows
    return call(
        softmax_kernel,
        [
            bf16(heads, keys, 2 * rows),
            jax.ShapeDtypeStruct((max(heads, 8), 2 * rows), jnp.float32),
        ],
        [SMEM, HBM, HBM, VMEM, VMEM, HBM],
        [VMEM] * 2,
        [
            pltpu.VMEM((2, rows, feats), jnp.bfloat16),
            pltpu.VMEM((block_count, rows, feats), jnp.bfloat16),
            pltpu.VMEM((keys, 2 * rows), jnp.float32),
            pltpu.SemaphoreType.DMA((2,)),
            pltpu.SemaphoreType.DMA((block_count,)),
        ],
        "softmax",
    )(at, queries, q_recv, key_mask, row_mask, k_all)


def attend_kernel(e_ref, inv_ref, v_ref, attn_mine, attn_theirs, v_s, attn_s, v_sem, out_sem):
    block_count, rows, feats = v_ref.shape
    loads = [begin(v_ref.at[j], v_s.at[j], v_sem.at[j]) for j in range(block_count)]
    for head in range(feats // HD):
        cols = slice(head * HD, (head + 1) * HD)
        attn_t = jnp.zeros((HD, 2 * rows), jnp.float32)
        for j in range(block_count):
            keys = slice(j * rows, (j + 1) * rows)
            if head == 0:
                loads[j].wait()
            attn_t = attn_t + product(jnp.transpose(v_s[j, :, cols]), e_ref[head, keys, :])
        attn_low = (attn_t * inv_ref[head : head + 1, :]).astype(jnp.bfloat16)
        attn_s[0, cols, :] = attn_low[:, :rows]
        attn_s[1, cols, :] = attn_low[:, rows:]
    stores = [
        begin(attn_s.at[0], attn_mine, out_sem.at[0]),
        begin(attn_s.at[1], attn_theirs, out_sem.at[1]),
    ]
    for store in stores:
        store.wait()


def attend(e_all, inverse, v_all, after):
    block_count, rows, feats = v_all.shape
    return call(
        attend_kernel,
        [bf16(feats, rows)] * 2,
        [VMEM, VMEM, HBM],
        [HBM] * 2,
        [
            pltpu.VMEM((block_count, rows, feats), jnp.bfloat16),
            pltpu.VMEM((2, feats, rows), jnp.bfloat16),
            pltpu.SemaphoreType.DMA((block_count,)),
            pltpu.SemaphoreType.DMA((2,)),
        ],
        "attend",
        after,
    )(e_all, inverse, v_all)


def value_terms_kernel(g_mine, g_recv, inv_ref, e_ref, part_out, g_s, part_s, sem, part_sem):
    block_count, rows, feats = part_out.shape
    loads = [begin(g_mine, g_s.at[0], sem.at[0]), begin(g_recv, g_s.at[1], sem.at[1])]
    for load in loads:
        load.wait()
    stores = []
    for head in range(feats // HD):
        cols = slice(head * HD, (head + 1) * HD)
        g_t = jnp.concatenate([g_s[0, cols, :], g_s[1, cols, :]], axis=1).astype(jnp.float32)
        grad = jnp.transpose((g_t * inv_ref[head : head + 1, :]).astype(jnp.bfloat16))
        for j in range(block_count):
            keys = slice(j * rows, (j + 1) * rows)
            part_s[j, :, cols] = product(e_ref[head, keys, :], grad).astype(jnp.bfloat16)
            if (head + 1) * HD == feats:
                stores.append(begin(part_s.at[j], part_out.at[j], part_sem.at[j]))
    for store in stores:
        store.wait()


def value_terms(g_mine, g_recv, inverse, e_all, block_count, after):
    feats, rows = g_mine.shape
    return call(
        value_terms_kernel,
        bf16(block_count, rows, feats),
        [HBM, HBM, VMEM, VMEM],
        HBM,
        [
            pltpu.VMEM((2, feats, rows), jnp.bfloat16),
            pltpu.VMEM((block_count, rows, feats), jnp.bfloat16),
            pltpu.SemaphoreType.DMA((2,)),
            pltpu.SemaphoreType.DMA((block_count,)),
        ],
        "value_terms",
        after,
    )(g_mine, g_recv, inverse, e_all)


def key_terms_kernel(at_ref, q_ref, q_recv, g_mine, g_recv, attn_mine, attn_theirs, *refs):
    inv_ref, e_ref, k_ref, v_ref, dq_mine, dq_theirs, part_out = refs[:7]
    q_s, t_s, kv_s, part_s, dq_s, sem, kv_sem, part_sem, dq_sem = refs[7:]
    block_count, rows, feats = part_out.shape
    score_scale = HD ** (-0.5)
    mine = pl.ds(pl.multiple_of(at_ref[0] * feats, feats), feats)
    loads = [begin(q_ref.at[:, mine], q_s.at[0], sem.at[0]), begin(q_recv, q_s.at[1], sem.at[1])]
    for index, held in enumerate((g_mine, g_recv, attn_mine, attn_theirs)):
        loads.append(begin(held, t_s.at[index], sem.at[2 + index]))
    kv_loads, stores = [], []
    for j in range(block_count):
        for index, held in enumerate((v_ref, k_ref)):
            kv_loads.append(begin(held.at[j], kv_s.at[index, j], kv_sem.at[2 * j + index]))
    for load in loads:
        load.wait()
    for head in range(feats // HD):
        cols = slice(head * HD, (head + 1) * HD)
        inverse = inv_ref[head : head + 1, :]
        g_t = jnp.concatenate([t_s[0, cols, :], t_s[1, cols, :]], axis=1).astype(jnp.float32)
        attn_t = jnp.concatenate([t_s[2, cols, :], t_s[3, cols, :]], axis=1)
        row_dot = jnp.sum(g_t * attn_t.astype(jnp.float32), axis=0, keepdims=True) * inverse
        g_t = (g_t * inverse).astype(jnp.bfloat16)
        query = jnp.concatenate([q_s[0, :, cols], q_s[1, :, cols]], axis=0)
        dq_t = jnp.zeros((HD, 2 * rows), jnp.float32)
        for j in range(block_count):
            keys = slice(j * rows, (j + 1) * rows)
            if head == 0:
                kv_loads[2 * j].wait()
                kv_loads[2 * j + 1].wait()
            low = e_ref[head, keys, :].astype(jnp.float32)
            dprobs = product(kv_s[0, j, :, cols], g_t)
            dscore = (low * (dprobs - row_dot)).astype(jnp.bfloat16)
            dq_t = dq_t + product(jnp.transpose(kv_s[1, j, :, cols]), dscore)
            part_s[j, :, cols] = (score_scale * product(dscore, query)).astype(jnp.bfloat16)
            if (head + 1) * HD == feats:
                stores.append(begin(part_s.at[j], part_out.at[j], part_sem.at[j]))
        dquery = (score_scale * jnp.transpose(dq_t)).astype(jnp.bfloat16)
        dq_s[0, :, cols] = dquery[:rows]
        dq_s[1, :, cols] = dquery[rows:]
    stores.append(begin(dq_s.at[0], dq_mine, dq_sem.at[0]))
    stores.append(begin(dq_s.at[1], dq_theirs, dq_sem.at[1]))
    for store in stores:
        store.wait()


def key_terms(at, queries, q_recv, g_mine, g_recv, attn_mine, attn_theirs, inverse, e_all, k_all, v_all, after):
    block_count, rows, feats = v_all.shape
    return call(
        key_terms_kernel,
        [bf16(rows, feats)] * 2 + [bf16(block_count, rows, feats)],
        [SMEM] + [HBM] * 6 + [VMEM] * 2 + [HBM] * 2,
        [HBM] * 3,
        [
            pltpu.VMEM((2, rows, feats), jnp.bfloat16),
            pltpu.VMEM((4, feats, rows), jnp.bfloat16),
            pltpu.VMEM((2, block_count, rows, feats), jnp.bfloat16),
            pltpu.VMEM((block_count, rows, feats), jnp.bfloat16),
            pltpu.VMEM((2, rows, feats), jnp.bfloat16),
            pltpu.SemaphoreType.DMA((6,)),
            pltpu.SemaphoreType.DMA((2 * block_count,)),
            pltpu.SemaphoreType.DMA((block_count,)),
            pltpu.SemaphoreType.DMA((2,)),
        ],
        "key_terms",
        after,
    )(at, queries, q_recv, g_mine, g_recv, attn_mine, attn_theirs, inverse, e_all, k_all, v_all)


def grad_heads_kernel(part_count, sends, picked, at_ref, first_ref, weight_ref, *refs):
    grads, refs = refs[:part_count], refs[part_count:]
    outs, refs = refs[: 2 + sends], refs[2 + sends :]
    first_s, grad_s, weight_s, out_s, sem, send_sem, out_sem = refs
    half = out_s.shape[1]
    width = grads[0].shape[1]
    loads = []
    for k in range(1, part_count):
        start = pl.multiple_of(at_ref[2 + k] * width, width)
        columns = weight_ref.at[:, pl.ds(start, width)]
        loads.append(begin(columns, weight_s.at[k - 1], sem.at[2 * k]))
    grad_loads = [begin(grads[k], grad_s.at[k], sem.at[2 * k - 1 if k else 0]) for k in range(part_count)]
    for load in grad_loads:
        load.wait()
    copies = []
    for send in range(sends):
        for i in range(picked):
            place = send * picked + i
            target = outs[2 + send].at[:, i * width : (i + 1) * width]
            for k in range(part_count):

                @pl.when(at_ref[2 + part_count + place] == k)
                def _():
                    begin(grad_s.at[k], target, send_sem.at[place])

            copies.append(pltpu.make_async_copy(grad_s.at[0], target, send_sem.at[place]))
    summed = first_ref[...]
    for k in range(1, part_count):
        loads[k - 1].wait()
        summed = summed + against(weight_s[k - 1], grad_s[k])
    first_s[...] = summed
    for side, at in enumerate((at_ref[0], 1 - at_ref[0])):
        kept = first_s[pl.ds(pl.multiple_of(at * half, half), half), :]
        out_s[side] = kept.astype(jnp.bfloat16)
        copies.append(begin(out_s.at[side], outs[side], out_sem.at[side]))
    for copy in copies:
        copy.wait()


def grad_heads(at, first, out_weight, grads, sends, picked, after):
    feats, rows = first.shape
    half = feats // INNER
    count = len(grads)
    width = grads[0].shape[1]
    out = call(
        functools.partial(grad_heads_kernel, count, sends, picked),
        [bf16(half, rows), bf16(half, rows)] + [bf16(rows, picked * width)] * sends,
        [SMEM, VMEM] + [HBM] * (1 + count),
        [HBM] * (2 + sends),
        [
            pltpu.VMEM((feats, rows), jnp.float32),
            pltpu.VMEM((count, rows, width), jnp.bfloat16),
            pltpu.VMEM((count - 1, feats, width), jnp.bfloat16),
            pltpu.VMEM((INNER, half, rows), jnp.bfloat16),
            pltpu.SemaphoreType.DMA((2 * count - 1,)),
            pltpu.SemaphoreType.DMA((sends * picked,)),
            pltpu.SemaphoreType.DMA((INNER,)),
        ],
        "grad_heads",
        after,
    )(at, first, out_weight, *grads)
    return out[0], out[1], out[2:]


def weight_kernel(part_count, picked, doc_count, sent, at_ref, *refs):
    attn, refs = refs[: INNER * doc_count], refs[INNER * doc_count :]
    grads, refs = refs[:part_count], refs[part_count:]
    swapped, refs = refs[: doc_count - 1], refs[doc_count - 1 :]
    out, attn_s, grad_s, out_s, attn_sem, grad_sem, out_sem = refs
    outer, feats, width = out.shape
    half = feats // INNER
    loads = []
    for doc in range(doc_count):
        for side in range(INNER):
            at = (1 - at_ref[0]) if side else at_ref[0]
            index = doc * INNER + side
            target = attn_s.at[doc, pl.ds(pl.multiple_of(at * half, half), half)]
            loads.append(begin(attn[index], target, attn_sem.at[index]))
    piece = grads[0].shape[1]
    for i in range(picked):
        cols = slice(i * piece, (i + 1) * piece)
        for k in range(part_count):

            @pl.when(at_ref[1 + i] == k)
            def _():
                begin(grads[k], grad_s.at[0, :, cols], grad_sem.at[i])

        loads.append(pltpu.make_async_copy(grads[0], grad_s.at[0, :, cols], grad_sem.at[i]))
    for doc in range(1, doc_count):
        loads.append(begin(swapped[doc - 1], grad_s.at[doc], grad_sem.at[picked + doc - 1]))
    for load in loads:
        load.wait()
    stores = []
    at = (1 - at_ref[0]) if sent else at_ref[0]
    for k in range(outer):
        cols = pl.ds(pl.multiple_of((k * INNER + at) * width, width), width)
        term = product(attn_s[0], grad_s[0, :, cols])
        for doc in range(1, doc_count):
            term = term + product(attn_s[doc], grad_s[doc, :, cols])
        out_s[k] = term.astype(out_s.dtype)
        stores.append(begin(out_s.at[k], out.at[k], out_sem.at[k]))
    for store in stores:
        store.wait()


def weight_terms(at, attn, grads, swapped, outer, picked, sent, after=()):
    half, rows = attn[0].shape
    feats = half * INNER
    doc_count = len(attn) // INNER
    columns = picked * grads[0].shape[1]
    width = columns // (outer * INNER)
    dtype = jnp.bfloat16
    return call(
        functools.partial(weight_kernel, len(grads), picked, doc_count, sent),
        jax.ShapeDtypeStruct((outer, feats, width), dtype),
        [SMEM] + [HBM] * (len(attn) + len(grads) + len(swapped)),
        HBM,
        [
            pltpu.VMEM((doc_count, feats, rows), jnp.bfloat16),
            pltpu.VMEM((doc_count, rows, columns), jnp.bfloat16),
            pltpu.VMEM((outer, feats, width), dtype),
            pltpu.SemaphoreType.DMA((len(attn),)),
            pltpu.SemaphoreType.DMA((picked + doc_count - 1,)),
            pltpu.SemaphoreType.DMA((outer,)),
        ],
        "weight_sent" if sent else "weight_kept",
        after,
    )(at, *attn, *grads, *swapped)


def collect_kernel(terms, out, terms_s, out_s, sem, out_sem):
    count, rows, half = terms.shape
    loads = [begin(terms.at[c], terms_s.at[c], sem.at[c]) for c in range(count)]
    for load in loads:
        load.wait()
    for side in range(INNER):
        summed = terms_s[side].astype(jnp.float32)
        for c in range(side + INNER, count, INNER):
            summed = summed + terms_s[c].astype(jnp.float32)
        out_s[:, side * half : (side + 1) * half] = summed.astype(jnp.bfloat16)
    begin(out_s, out, out_sem).wait()


def collect(terms, name, after=()):
    count, rows, half = terms.shape
    return call(
        collect_kernel,
        bf16(rows, INNER * half),
        [HBM],
        HBM,
        [
            pltpu.VMEM((count, rows, half), jnp.bfloat16),
            pltpu.VMEM((rows, INNER * half), jnp.bfloat16),
            pltpu.SemaphoreType.DMA((count,)),
            pltpu.SemaphoreType.DMA,
        ],
        name,
        after,
    )(terms)


def join_kernel(at_ref, mine, recv, out, held_s, out_s, sem, out_sem):
    half = mine.shape[1]
    loads = [begin(held, held_s.at[i], sem.at[i]) for i, held in enumerate((mine, recv))]
    for side, at in enumerate((at_ref[0], 1 - at_ref[0])):
        loads[side].wait()
        out_s[:, pl.ds(pl.multiple_of(at * half, half), half)] = held_s[side]
    begin(out_s, out, out_sem).wait()


def join_heads(at, mine, recv):
    rows, half = mine.shape
    return call(
        join_kernel,
        bf16(rows, INNER * half),
        [SMEM, HBM, HBM],
        HBM,
        [
            pltpu.VMEM((2, rows, half), jnp.bfloat16),
            pltpu.VMEM((rows, INNER * half), jnp.bfloat16),
            pltpu.SemaphoreType.DMA((2,)),
            pltpu.SemaphoreType.DMA,
        ],
        "join_heads",
    )(at, mine, recv)


def per_device(
    queries, key_heads, value_heads, grad_output, out_weight, block_pattern, global_offsets
):
    dp_count, ctx_count, tp_count = (lax.axis_size(name) for name in ("dp", "ctx", "tp"))
    dp_at, ctx_at, tp_at = (lax.axis_index(name) for name in ("dp", "ctx", "tp"))
    outer = ctx_count // INNER
    outer_at, inner_at = ctx_at // INNER, ctx_at % INNER
    picked = tp_count // dp_count
    place = [inner_at, outer_at]

    swap = [(i, i ^ 1) for i in range(ctx_count)]
    columns = [[o * INNER + i for o in range(outer)] for i in range(INNER)]

    def shift_pairs(count, step):
        return [(i, (i + step) % count) for i in range(count)]

    def dp_steps(which):
        return [(which * picked + i - tp_at) % tp_count for i in range(picked)]

    def exchange(values, groups=None):
        return lax.all_to_all(
            values, "ctx", split_axis=0, concat_axis=0, axis_index_groups=groups, tiled=True
        )

    at = jnp.stack(place)
    grad_own = grad_output[0]
    grads = [grad_own] + [
        lax.ppermute(grad_own, "tp", shift_pairs(tp_count, -step)) for step in range(1, tp_count)
    ]
    k_send, v_send, q_theirs = part_heads(at, queries[0], key_heads[0], value_heads[0], ctx_count)
    k_all = exchange(k_send)
    q_recv = lax.ppermute(q_theirs, "ctx", swap)
    first, key_mask, row_mask = prelude(
        jnp.stack(place + [tp_at]), block_pattern, global_offsets, grad_own, out_weight
    )
    v_send, first = lax.optimization_barrier((v_send, first))
    v_all = exchange(v_send)

    e_all, inverse = softmax(at, queries[0], q_recv, key_mask, row_mask, k_all)

    g_at = place + [(tp_at + step) % tp_count for step in range(tp_count)]
    for step in range(1, dp_count):
        g_at = g_at + dp_steps((dp_at + step) % dp_count)
    g_mine, g_theirs, grad_sends = grad_heads(
        jnp.stack(g_at), first, out_weight, grads, dp_count - 1, picked, (inverse,)
    )
    g_recv = lax.ppermute(g_theirs, "ctx", swap)
    swapped = [
        lax.ppermute(send, "dp", shift_pairs(dp_count, step + 1))
        for step, send in enumerate(grad_sends)
    ]

    attn_mine, attn_theirs = attend(e_all, inverse, v_all, (g_theirs,))
    attn = []
    for step in range(dp_count):
        for held, side in ((attn_mine, 0), (attn_theirs, 1)):
            pairs = [
                (d * ctx_count + c, ((d + step) % dp_count) * ctx_count + (c ^ side))
                for d in range(dp_count)
                for c in range(ctx_count)
            ]
            attn.append(lax.ppermute(held, ("dp", "ctx"), pairs) if step or side else held)

    value_parts = value_terms(g_mine, g_recv, inverse, e_all, ctx_count, (attn_mine,))
    weight_at = jnp.stack([inner_at] + dp_steps(dp_at))
    send = weight_terms(weight_at, attn, grads, swapped, outer, picked, True, (value_parts,))
    weight_recv = lax.ppermute(send, "ctx", swap)
    terms_v = exchange(value_parts)

    dq_mine, dq_theirs, key_parts = key_terms(
        at, queries[0], q_recv, g_mine, g_recv, attn_mine, attn_theirs, inverse, e_all, k_all, v_all, (send,)
    )
    terms_k = exchange(key_parts)
    dq_recv = lax.ppermute(dq_theirs, "ctx", swap)

    keep = weight_terms(weight_at, attn, grads, swapped, outer, picked, False, (key_parts,))
    weight_sum = keep + weight_recv
    weight_all = exchange(weight_sum, columns)
    grad_weight = jnp.sum(weight_all.astype(jnp.float32), axis=0).astype(jnp.bfloat16)

    grad_q = join_heads(at, dq_mine, dq_recv)
    grad_v = collect(terms_v, "collect_values")
    grad_k = collect(terms_k, "collect_keys")
    return grad_q[None], grad_k[None], grad_v[None], grad_weight


def solution(mesh):
    in_specs = (
        P("dp", "ctx", "tp"),
        P("dp", "ctx", "tp"),
        P("dp", "ctx", "tp"),
        P("dp", "ctx", "tp"),
        P("tp", None),
        P(),
        P(),
    )
    out_specs = (
        P("dp", "ctx", "tp"),
        P("dp", "ctx", "tp"),
        P("dp", "ctx", "tp"),
        P("tp", ("dp", "ctx")),
    )
    return jax.shard_map(
        per_device, mesh=mesh, in_specs=in_specs, out_specs=out_specs, check_vma=False
    )
```

time: 181 us -> 136 us (0.75)
  Pallas kernels: 100 us -> 36.7 us
  local copies, waits for them, and re-layouts: 6.54 us -> 18.5 us
  starting transfers between devices: 26.9 us -> 35.9 us
  other arithmetic: 4.75 us -> 1.9 us
    pallas_call x4 -> x8, Pallas kernels: 55.5 us -> 23.4 us  [the longest x1 6.61 us: key_terms(): call(key_terms_kernel, [bf16(rows, feats)] * 2 + [bf16(block_count, rows,...]
    pallas_call x1, Pallas kernels: 33.7 us -> 2.99 us  [grad_heads(): call(functools.partial(grad_heads_kernel, count, sends, picked), [bf16(ha...]
    unnamed x29 -> x71, local copies, waits for them, and re-layouts: 5.89 us -> 18.4 us
    all_to_all x3 -> x5, starting transfers between devices: 15.2 us -> 26.8 us  [exchange(): lax.all_to_all(values, 'ctx', split_axis=0, concat_axis=0, axis_index_gro...]
    all_to_all x3 -> x5, waiting for transfers between devices: 17.1 us -> 13.4 us  [exchange(): lax.all_to_all(values, 'ctx', split_axis=0, concat_axis=0, axis_index_gro...]
    ppermute x1, waiting for transfers between devices: 5.68 us -> 2.14 us  [per_device(): dq_recv = lax.ppermute(dq_theirs, 'ctx', swap)]
    ppermute x3, waiting for transfers between devices: 3.61 us -> 6.96 us  [per_device(): lax.ppermute(held, ('dp', 'ctx'), pairs)]
    ppermute x1, waiting for transfers between devices: 8.96 us -> 12.2 us  [per_device(): weight_recv = lax.ppermute(send, 'ctx', swap)]
  transfers between devices with their start and end apart: 12 -> 14, of which waited for: 8 -> 7; matrix products, arithmetic and copies ran while one was open for 2% -> 1% of each run, Pallas kernels for 50% -> 26%
where the time goes in v4:
time: 136 us; the launch traced here: 135 us
  waiting for transfers between devices  40.8 us (30%)
  Pallas kernels  36.7 us (27%)
  starting transfers between devices  35.9 us (26%)
  local copies, waits for them, and re-layouts  18.5 us (14%)
  other arithmetic  1.9 us (1%)
    all_to_all x5, starting transfers between devices, exchange(): lax.all_to_all(values, 'ctx', split_axis=0, concat_axis=0, axis_index_gro...  26.8 us
    unnamed x71, local copies, waits for them, and re-layouts  18.4 us
    all_to_all x5, waiting for transfers between devices, exchange(): lax.all_to_all(values, 'ctx', split_axis=0, concat_axis=0, axis_index_gro...  13.4 us
    ppermute x1, waiting for transfers between devices, per_device(): weight_recv = lax.ppermute(send, 'ctx', swap)  12.2 us
    pallas_call x2, Pallas kernels, weight_terms(): call(functools.partial(weight_kernel, len(grads), picked, doc_count, sent...  8.19 us
    ppermute x3, waiting for transfers between devices, per_device(): lax.ppermute(held, ('dp', 'ctx'), pairs)  6.96 us
    pallas_call x1, Pallas kernels, key_terms(): call(key_terms_kernel, [bf16(rows, feats)] * 2 + [bf16(block_count, rows,...  6.61 us
    ppermute x1, waiting for transfers between devices, per_device(): q_recv = lax.ppermute(q_theirs, 'ctx', swap)  5.34 us
  transfers between devices with their start and end apart: 14, of which 7 were waited for; matrix products, arithmetic and copies ran while one was open for 1% of the time, Pallas kernels for 26%

profile of v4, /device:TPU:0, one launch (start us, length us, event | category | flops | bytes accessed | tf_op | source)
XLA Modules:
  0.0 134.7 jit_solution(2767764497585031036)
XLA Ops:
  0.6 0.0 copy-start
  0.7 0.1 pad_add_fusion.refs_0_.refs_1_
  0.7 1.0 copy-done.11
  1.7 0.9 copy-done.23
  2.6 0.9 copy-done.24
  3.5 2.2 %part_heads.1 = (bf16[8,256,128]{2,1,0:T(8,128)(2,1)}, bf16[8,256,128]{2,1,0:T(8,128)(2,1)}, bf16[256,128]{1,0:T(8,128)(2,1)S(1)}) custom-call(s32[2]{0:T(128)S(1)} %pad_add_fusion.refs_0_.refs_1_, bf16[256,256]{1,0:T(8,128)(2,1)S(1)} %bitcast.19, bf16[256,256]{1,0:T(8,128)(2,1)S(1)} %bitcast.22, bf16[256,256]{1,0:T(8,128)(2,1)S(1)} %bitcast.23), custom_call_target="tpu_custom_call" | custom-call | flops 1 | bytes 1 | tf_op jit(solution)/shard_map/part_heads/pallas_call | solution.py:74
  5.7 7.3 %all-to-all-start = ((bf16[8,256,128]{2,1,0:T(8,128)(2,1)}), bf16[8,256,128]{2,1,0:T(8,128)(2,1)S(1)}, u32[]{:S(2)}, u32[]{:S(2)}) async-start(bf16[8,256,128]{2,1,0:T(8,128)(2,1)} %get-tuple-element.25), calls=%async_computation | async-start | bytes 1048576 | tf_op jit(solution)/shard_map/all_to_all | solution.py:559
  13.0 1.5 %collective-permute-start.1 = (bf16[256,2048]{1,0:T(8,128)(2,1)}, bf16[256,2048]{1,0:T(8,128)(2,1)}, u32[]{:S(2)}, u32[]{:S(2)}) collective-permute-start(bf16[256,2048]{1,0:T(8,128)(2,1)} %bitcast.14), channel_id=1, source_target_pairs={{0,1},{1,0},{2,3},{3,2},{4,5},{5,4},{6,7},{7,6},{8,9},{9,8},{10,11... | collective-permute-start | bytes 3145736 | tf_op jit(solution)/shard_map/ppermute | solution.py:566
  14.5 0.8 copy.11.refs_1_
  15.3 0.1 pad_add_fusion.1.refs_0_
  15.3 1.6 %copy-done.1 = bf16[256,4096]{1,0:T(8,128)(2,1)S(1)} copy-done((bf16[256,4096]{1,0:T(8,128)(2,1)S(1)}, bf16[256,4096]{1,0:T(8,128)(2,1)}, u32[]{:S(2)}) %copy-start.1) | copy-done | bytes 2097176
  16.9 0.7 copy-done.30
  17.6 2.1 %prelude.1 = (f32[256,256]{1,0:T(8,128)S(1)}, bf16[2048,128]{1,0:T(8,128)(2,1)S(1)}, f32[8,512]{1,0:T(8,128)S(1)}) custom-call(s32[3]{0:T(128)S(1)} %pad_add_fusion.1.refs_0_, s32[8,3]{1,0:T(8,128)S(1)} %copy.11.refs_1_, s32[8,8]{1,0:T(8,128)S(1)} %copy-done.30, bf16[256,2048]{1,0:T(8,128)(2,1)S(1)} %bitcast.15, bf16[256,4096]{1,0:T(8,128)(2,1)S(1)} %copy-done.1), custom_call_target="tpu_custom_call" | custom-call | flops 1 | bytes 1 | tf_op jit(solution)/shard_map/prelude/pallas_call | solution.py:131
  19.7 0.8 copy-done.13
  20.5 0.7 copy-done.21
  21.2 6.2 %all-to-all-done.refs_5_.refs_10_ = bf16[8,256,128]{2,1,0:T(8,128)(2,1)S(1)} async-done(((bf16[8,256,128]{2,1,0:T(8,128)(2,1)}), bf16[8,256,128]{2,1,0:T(8,128)(2,1)S(1)}, u32[]{:S(2)}, u32[]{:S(2)}) %all-to-all-start) | async-done | bytes 524320 | tf_op jit(solution)/shard_map/all_to_all | solution.py:559
  27.5 4.1 %all-to-all-start.1 = ((bf16[8,256,128]{2,1,0:T(8,128)(2,1)}), bf16[8,256,128]{2,1,0:T(8,128)(2,1)}, u32[]{:S(2)}, u32[]{:S(2)}) async-start(bf16[8,256,128]{2,1,0:T(8,128)(2,1)} %get-tuple-element.32), calls=%async_computation.1 | async-start | bytes 1048576 | tf_op jit(solution)/shard_map/all_to_all | solution.py:559
  31.6 1.9 %collective-permute-start = (bf16[256,128]{1,0:T(8,128)(2,1)S(1)}, bf16[256,128]{1,0:T(8,128)(2,1)S(1)}, u32[]{:S(2)}, u32[]{:S(2)}) collective-permute-start(bf16[256,128]{1,0:T(8,128)(2,1)S(1)} %get-tuple-element.22), channel_id=1, source_target_pairs={{0,2},{2,0},{4,6},{6,4},{8,10},{10,8},{12,14},{14,12},{1,3},{3,1},... | collective-permute-start | bytes 196616 | tf_op jit(solution)/shard_map/ppermute | solution.py:570
  33.5 0.1 stack.46.refs_1_
  33.6 5.3 %collective-permute-done.refs_2_.refs_3_ = bf16[256,128]{1,0:T(8,128)(2,1)S(1)} collective-permute-done((bf16[256,128]{1,0:T(8,128)(2,1)S(1)}, bf16[256,128]{1,0:T(8,128)(2,1)S(1)}, u32[]{:S(2)}, u32[]{:S(2)}) %collective-permute-start) | collective-permute-done | bytes 65568 | tf_op jit(solution)/shard_map/ppermute | solution.py:570
  39.0 1.1 copy-done.4
  40.0 1.0 copy-done.14
  41.1 4.2 %softmax.1 = (bf16[1,2048,512]{2,1,0:T(8,128)(2,1)S(1)}, f32[8,512]{1,0:T(8,128)S(1)}) custom-call(s32[2]{0:T(128)S(1)} %pad_add_fusion.refs_0_.refs_1_, bf16[256,256]{1,0:T(8,128)(2,1)S(1)} %bitcast.20, bf16[256,128]{1,0:T(8,128)(2,1)S(1)} %collective-permute-done.refs_2_.refs_3_, bf16[2048,128]{1,0:T(8,128)(2,1)S(1)} %copy-done.14, ...), custom_call_target="tpu_custom_call" | custom-call | flops 1 | bytes 1 | tf_op jit(solution)/shard_map/softmax/pallas_call | solution.py:188
  45.3 0.0 collective-permute-done.1.refs_5_.refs_7_
  45.3 0.0 copy-start.2
  45.3 1.6 %copy-done.2 = bf16[256,4096]{1,0:T(8,128)(2,1)S(1)} copy-done((bf16[256,4096]{1,0:T(8,128)(2,1)S(1)}, bf16[256,4096]{1,0:T(8,128)(2,1)}, u32[]{:S(2)}) %copy-start.2) | copy-done | bytes 2097176
  46.9 0.9 copy-done.22
  47.8 3.0 %grad_heads.1 = (bf16[128,256]{1,0:T(8,128)(2,1)S(1)}, bf16[128,256]{1,0:T(8,128)(2,1)S(1)}, bf16[256,2048]{1,0:T(8,128)(2,1)}) custom-call(f32[8,512]{1,0:T(8,128)S(1)} %get-tuple-element.26.refs_0_.refs_2_.refs_3_.refs_8_, s32[5]{0:T(128)S(1)} %stack.46.refs_1_, f32[256,256]{1,0:T(8,128)S(1)} %copy-done.22, bf16[256,4096]{1,0:T(8,128)(2,1)S(1)} %copy-done.2, ...), custom_call_target="tpu_custom_call" | custom-call | flops 1 | bytes 1 | tf_op jit(solution)/shard_map/grad_heads/pallas_call | solution.py:396
  50.8 0.0 copy-start.17
  50.8 0.1 collective-permute-start.6
  50.9 1.1 collective-permute-start.2
  52.1 2.6 %attend.1 = (bf16[128,256]{1,0:T(8,128)(2,1)S(1)}, bf16[128,256]{1,0:T(8,128)(2,1)}) custom-call(bf16[128,256]{1,0:T(8,128)(2,1)S(1)} %get-tuple-element.30.refs_0_, bf16[1,2048,512]{2,1,0:T(8,128)(2,1)S(1)} %get-tuple-element.31.refs_1_.refs_4_.refs_9_, f32[8,512]{1,0:T(8,128)S(1)} %get-tuple-element.26.refs_0_.refs_2_.refs_3_.refs_8_, ...), custom_call_target="tpu_custom_call" | custom-call | flops 1 | bytes 1 | tf_op jit(solution)/shard_map/attend/pallas_call | solution.py:231
  54.7 0.8 collective-permute-done.2.refs_2_.refs_5_
  55.4 3.1 %value_terms.1.refs_0_ = bf16[8,256,128]{2,1,0:T(8,128)(2,1)S(1)} custom-call(bf16[128,256]{1,0:T(8,128)(2,1)S(1)} %get-tuple-element.33.refs_0_.refs_2_.refs_6_, bf16[128,256]{1,0:T(8,128)(2,1)S(1)} %get-tuple-element.34.refs_1_.refs_4_, bf16[128,256]{1,0:T(8,128)(2,1)S(1)} %collective-permute-done.2.refs_2_.refs_5_, ...), custom_call_target="tpu_custom_call" | custom-call | flops 1 | bytes 1 | tf_op jit(solution)/shard_map/value_terms/pallas_call | solution.py:268
  58.5 0.8 copy-done.6
  59.3 4.9 %all-to-all-start.3 = ((bf16[8,256,128]{2,1,0:T(8,128)(2,1)}), bf16[8,256,128]{2,1,0:T(8,128)(2,1)}, u32[]{:S(2)}, u32[]{:S(2)}) async-start(bf16[8,256,128]{2,1,0:T(8,128)(2,1)} %copy-done.6), calls=%async_computation.3 | async-start | bytes 1048576 | tf_op jit(solution)/shard_map/all_to_all | solution.py:559
  64.2 2.1 %collective-permute-start.3 = (bf16[128,256]{1,0:T(8,128)(2,1)}, bf16[128,256]{1,0:T(8,128)(2,1)S(1)}, u32[]{:S(2)}, u32[]{:S(2)}) collective-permute-start(bf16[128,256]{1,0:T(8,128)(2,1)} %get-tuple-element.35.refs_7_), channel_id=1, source_target_pairs={{0,2},{2,0},{4,6},{6,4},{8,10},{10,8},{12,14},{14,12},{16,18},{18,... | collective-permute-start | bytes 196616 | tf_op jit(solution)/shard_map/ppermute | solution.py:600
  66.3 0.1 collective-permute-start.5
  66.4 0.1 pad_add_fusion.2.refs_1_
  66.4 7.0 %collective-permute-done.3.refs_3_ = bf16[128,256]{1,0:T(8,128)(2,1)S(1)} collective-permute-done((bf16[128,256]{1,0:T(8,128)(2,1)}, bf16[128,256]{1,0:T(8,128)(2,1)S(1)}, u32[]{:S(2)}, u32[]{:S(2)}) %collective-permute-start.3) | collective-permute-done | bytes 65568 | tf_op jit(solution)/shard_map/ppermute | solution.py:600
  73.4 1.0 copy-done.7
  74.5 4.1 %weight_sent.1.refs_0_ = bf16[4,256,256]{2,1,0:T(8,128)(2,1)S(1)} custom-call(bf16[8,256,128]{2,1,0:T(8,128)(2,1)S(1)} %copy-done.7, s32[2]{0:T(128)S(1)} %pad_add_fusion.2.refs_1_, bf16[128,256]{1,0:T(8,128)(2,1)S(1)} %get-tuple-element.33.refs_0_.refs_2_.refs_6_, bf16[128,256]{1,0:T(8,128)(2,1)S(1)} %collective-permute-done.3.refs_3_, ...), custom_call_target="tpu_custom_call" | custom-call | flops 1 | bytes 1 | tf_op jit(solution)/shard_map/weight_sent/pallas_call | solution.py:464
  78.6 6.6 %key_terms.1 = (bf16[256,128]{1,0:T(8,128)(2,1)S(1)}, bf16[256,128]{1,0:T(8,128)(2,1)S(1)}, bf16[8,256,128]{2,1,0:T(8,128)(2,1)S(1)}) custom-call(bf16[4,256,256]{2,1,0:T(8,128)(2,1)S(1)} %weight_sent.1.refs_0_, s32[2]{0:T(128)S(1)} %copy-done.28, bf16[256,256]{1,0:T(8,128)(2,1)S(1)} %bitcast.21, bf16[256,128]{1,0:T(8,128)(2,1)S(1)} %copy-done.16, ...), custom_call_target="tpu_custom_call" | custom-call | flops 1 | bytes 1 | tf_op jit(solution)/shard_map/key_terms/pallas_call | solution.py:331
  85.3 0.8 copy-done.8
  86.0 0.8 copy-done.9
  86.8 0.6 copy-done.25
  87.5 0.6 copy-done.33
  88.1 6.0 %all-to-all-start.2 = ((bf16[8,256,128]{2,1,0:T(8,128)(2,1)}), bf16[8,256,128]{2,1,0:T(8,128)(2,1)S(1)}, u32[]{:S(2)}, u32[]{:S(2)}) async-start(bf16[8,256,128]{2,1,0:T(8,128)(2,1)} %copy-done.9), calls=%async_computation.2 | async-start | bytes 1048576 | tf_op jit(solution)/shard_map/all_to_all | solution.py:559
  94.1 2.0 %collective-permute-start.8 = (bf16[4,256,256]{2,1,0:T(8,128)(2,1)}, bf16[4,256,256]{2,1,0:T(8,128)(2,1)S(1)}, u32[]{:S(2)}, u32[]{:S(2)}) collective-permute-start(bf16[4,256,256]{2,1,0:T(8,128)(2,1)} %copy-done.8), channel_id=1, source_target_pairs={{0,2},{2,0},{4,6},{6,4},{8,10},{10,8},{12,14},{14,12},{1,3},{3,1},... | collective-permute-start | bytes 1572872 | tf_op jit(solution)/shard_map/ppermute | solution.py:605
  96.1 1.0 copy-done.10
  97.2 0.7 copy-done.32
  97.8 4.1 %weight_kept.1 = bf16[4,256,256]{2,1,0:T(8,128)(2,1)S(1)} custom-call(bf16[8,256,128]{2,1,0:T(8,128)(2,1)S(1)} %copy-done.10, s32[2]{0:T(128)S(1)} %copy-done.32, bf16[128,256]{1,0:T(8,128)(2,1)S(1)} %get-tuple-element.33.refs_0_.refs_2_.refs_6_, bf16[128,256]{1,0:T(8,128)(2,1)S(1)} %collective-permute-done.3.refs_3_, ...), custom_call_target="tpu_custom_call" | custom-call | flops 1 | bytes 1 | tf_op jit(solution)/shard_map/weight_kept/pallas_call | solution.py:464
  101.9 0.0 copy-start.34
  101.9 0.0 copy-start.26
  102.0 12.2 %collective-permute-done.8 = bf16[4,256,256]{2,1,0:T(8,128)(2,1)S(1)} collective-permute-done((bf16[4,256,256]{2,1,0:T(8,128)(2,1)}, bf16[4,256,256]{2,1,0:T(8,128)(2,1)S(1)}, u32[]{:S(2)}, u32[]{:S(2)}) %collective-permute-start.8) | collective-permute-done | bytes 524320 | tf_op jit(solution)/shard_map/ppermute | solution.py:605
  114.2 0.9 add.37
  115.1 4.5 %all-to-all-start.4 = ((bf16[4,256,256]{2,1,0:T(8,128)(2,1)}), bf16[4,256,256]{2,1,0:T(8,128)(2,1)S(1)}, u32[]{:S(2)}, u32[]{:S(2)}) async-start(bf16[4,256,256]{2,1,0:T(8,128)(2,1)} %add.37), calls=%async_computation.4 | async-start | bytes 1048576 | tf_op jit(solution)/shard_map/all_to_all | solution.py:559
  119.6 0.3 collective-permute-start.7
  119.9 1.9 %collect_values.1 = bf16[256,256]{1,0:T(8,128)(2,1)} custom-call(bf16[8,256,128]{2,1,0:T(8,128)(2,1)} %all-to-all-done.3.refs_0_), custom_call_target="tpu_custom_call" | custom-call | flops 1 | bytes 1 | tf_op jit(solution)/shard_map/collect_values/pallas_call | solution.py:497
  121.8 2.1 %collective-permute-done.7.refs_2_ = bf16[256,128]{1,0:T(8,128)(2,1)S(1)} collective-permute-done((bf16[256,128]{1,0:T(8,128)(2,1)S(1)}, bf16[256,128]{1,0:T(8,128)(2,1)S(1)}, u32[]{:S(2)}, u32[]{:S(2)}) %collective-permute-start.7) | collective-permute-done | bytes 65568 | tf_op jit(solution)/shard_map/ppermute | solution.py:612
  123.9 1.4 %join_heads.1 = bf16[256,256]{1,0:T(8,128)(2,1)} custom-call(s32[2]{0:T(128)S(1)} %copy-done.29, bf16[256,128]{1,0:T(8,128)(2,1)S(1)} %copy-done.26, bf16[256,128]{1,0:T(8,128)(2,1)S(1)} %collective-permute-done.7.refs_2_), custom_call_target="tpu_custom_call" | custom-call | flops 1 | bytes 1 | tf_op jit(solution)/shard_map/join_heads/pallas_call | solution.py:524
  125.3 1.5 %collect_keys.1 = bf16[256,256]{1,0:T(8,128)(2,1)} custom-call(bf16[8,256,128]{2,1,0:T(8,128)(2,1)S(1)} %all-to-all-done.2.refs_0_), custom_call_target="tpu_custom_call" | custom-call | flops 1 | bytes 1 | tf_op jit(solution)/shard_map/collect_keys/pallas_call | solution.py:497
  126.8 7.1 %all-to-all-done.4 = bf16[4,256,256]{2,1,0:T(8,128)(2,1)S(1)} async-done(((bf16[4,256,256]{2,1,0:T(8,128)(2,1)}), bf16[4,256,256]{2,1,0:T(8,128)(2,1)S(1)}, u32[]{:S(2)}, u32[]{:S(2)}) %all-to-all-start.4) | async-done | bytes 524320 | tf_op jit(solution)/shard_map/all_to_all | solution.py:559
  134.0 0.7 reduce_sum.12
  (53 shorter events, 0.1 us)
Async XLA Ops:
  0.6 14.7 %copy-start = (bf16[1,256,2048]{2,1,0:T(8,128)(2,1)S(1)}, bf16[1,256,2048]{2,1,0:T(8,128)(2,1)}, u32[]{:S(2)}) copy-start(bf16[1,256,2048]{2,1,0:T(8,128)(2,1)} %param.10) | copy-start | bytes 3145732
  0.7 38.2 %copy-start.27 = (s32[2]{0:T(128)}, s32[2]{0:T(128)S(1)}, u32[]{:S(2)}) copy-start(s32[2]{0:T(128)S(1)} %pad_add_fusion.refs_0_.refs_1_) | copy-start | bytes 28
  0.7 1.0 copy-start.11
  1.7 0.9 copy-start.23
  2.6 0.9 copy-start.24
  5.7 21.8 %all-to-all-start = ((bf16[8,256,128]{2,1,0:T(8,128)(2,1)}), bf16[8,256,128]{2,1,0:T(8,128)(2,1)S(1)}, u32[]{:S(2)}, u32[]{:S(2)}) async-start(bf16[8,256,128]{2,1,0:T(8,128)(2,1)} %get-tuple-element.25), calls=%async_computation | async-start | bytes 1048576 | tf_op jit(solution)/shard_map/all_to_all | solution.py:559
  13.0 32.3 %collective-permute-start.1 = (bf16[256,2048]{1,0:T(8,128)(2,1)}, bf16[256,2048]{1,0:T(8,128)(2,1)}, u32[]{:S(2)}, u32[]{:S(2)}) collective-permute-start(bf16[256,2048]{1,0:T(8,128)(2,1)} %bitcast.14), channel_id=1, source_target_pairs={{0,1},{1,0},{2,3},{3,2},{4,5},{5,4},{6,7},{7,6},{8,9},{9,8},{10,11... | collective-permute-start | bytes 3145736 | tf_op jit(solution)/shard_map/ppermute | solution.py:566
  15.3 1.6 %copy-start.1 = (bf16[256,4096]{1,0:T(8,128)(2,1)S(1)}, bf16[256,4096]{1,0:T(8,128)(2,1)}, u32[]{:S(2)}) copy-start(bf16[256,4096]{1,0:T(8,128)(2,1)} %refs_3_.1) | copy-start | bytes 6291460
  16.9 0.7 copy-start.30
  17.6 21.3 %copy-start.12 = (bf16[1,256,256]{2,1,0:T(8,128)(2,1)S(1)}, bf16[1,256,256]{2,1,0:T(8,128)(2,1)}, u32[]{:S(2)}) copy-start(bf16[1,256,256]{2,1,0:T(8,128)(2,1)} %param.7) | copy-start | bytes 393220
  19.7 0.8 copy-start.13
  20.5 0.7 copy-start.21
  27.5 11.5 %copy-start.3 = (bf16[8,256,128]{2,1,0:T(8,128)(2,1)}, bf16[8,256,128]{2,1,0:T(8,128)(2,1)S(1)}, u32[]{:S(2)}) copy-start(bf16[8,256,128]{2,1,0:T(8,128)(2,1)S(1)} %all-to-all-done.refs_5_.refs_10_) | copy-start | bytes 1572868
  27.5 24.6 %all-to-all-start.1 = ((bf16[8,256,128]{2,1,0:T(8,128)(2,1)}), bf16[8,256,128]{2,1,0:T(8,128)(2,1)}, u32[]{:S(2)}, u32[]{:S(2)}) async-start(bf16[8,256,128]{2,1,0:T(8,128)(2,1)} %get-tuple-element.32), calls=%async_computation.1 | async-start | bytes 1048576 | tf_op jit(solution)/shard_map/all_to_all | solution.py:559
  31.6 7.3 %collective-permute-start = (bf16[256,128]{1,0:T(8,128)(2,1)S(1)}, bf16[256,128]{1,0:T(8,128)(2,1)S(1)}, u32[]{:S(2)}, u32[]{:S(2)}) collective-permute-start(bf16[256,128]{1,0:T(8,128)(2,1)S(1)} %get-tuple-element.22), channel_id=1, source_target_pairs={{0,2},{2,0},{4,6},{6,4},{8,10},{10,8},{12,14},{14,12},{1,3},{3,1},... | collective-permute-start | bytes 196616 | tf_op jit(solution)/shard_map/ppermute | solution.py:570
  38.9 11.9 %copy-start.15 = (bf16[256,128]{1,0:T(8,128)(2,1)}, bf16[256,128]{1,0:T(8,128)(2,1)S(1)}, u32[]{:S(2)}) copy-start(bf16[256,128]{1,0:T(8,128)(2,1)S(1)} %collective-permute-done.refs_2_.refs_3_) | copy-start | bytes 196612
  38.9 1.1 copy-start.4
  40.0 1.0 copy-start.14
  45.3 1.6 %copy-start.2 = (bf16[256,4096]{1,0:T(8,128)(2,1)S(1)}, bf16[256,4096]{1,0:T(8,128)(2,1)}, u32[]{:S(2)}) copy-start(bf16[256,4096]{1,0:T(8,128)(2,1)} %refs_3_.1) | copy-start | bytes 6291460
  46.9 0.9 copy-start.22
  50.8 7.7 %copy-start.17 = (bf16[128,256]{1,0:T(8,128)(2,1)}, bf16[128,256]{1,0:T(8,128)(2,1)S(1)}, u32[]{:S(2)}) copy-start(bf16[128,256]{1,0:T(8,128)(2,1)S(1)} %get-tuple-element.34.refs_1_.refs_4_) | copy-start | bytes 196612
  50.8 22.6 %collective-permute-start.6 = (bf16[256,2048]{1,0:T(8,128)(2,1)}, bf16[256,2048]{1,0:T(8,128)(2,1)}, u32[]{:S(2)}, u32[]{:S(2)}) collective-permute-start(bf16[256,2048]{1,0:T(8,128)(2,1)} %get-tuple-element.36), channel_id=1, source_target_pairs={{0,16},{16,0},{1,17},{17,1},{2,18},{18,2},{3,19},{19,3},{4,20},{20... | collective-permute-start | bytes 3145736 | tf_op jit(solution)/shard_map/ppermute | solution.py:587
  50.9 4.5 %collective-permute-start.2 = (bf16[128,256]{1,0:T(8,128)(2,1)S(1)}, bf16[128,256]{1,0:T(8,128)(2,1)S(1)}, u32[]{:S(2)}, u32[]{:S(2)}) collective-permute-start(bf16[128,256]{1,0:T(8,128)(2,1)S(1)} %get-tuple-element.30.refs_0_), channel_id=1, source_target_pairs={{0,2},{2,0},{4,6},{6,4},{8,10},{10,8},{12,14},{14,12},{1,3},{3,1},... | collective-permute-start | bytes 196616 | tf_op jit(solution)/shard_map/ppermute | solution.py:585
  55.4 8.8 %copy-start.19 = (bf16[128,256]{1,0:T(8,128)(2,1)}, bf16[128,256]{1,0:T(8,128)(2,1)S(1)}, u32[]{:S(2)}) copy-start(bf16[128,256]{1,0:T(8,128)(2,1)S(1)} %collective-permute-done.2.refs_2_.refs_5_) | copy-start | bytes 196612
  58.5 0.8 copy-start.6
  59.3 28.8 %all-to-all-start.3 = ((bf16[8,256,128]{2,1,0:T(8,128)(2,1)}), bf16[8,256,128]{2,1,0:T(8,128)(2,1)}, u32[]{:S(2)}, u32[]{:S(2)}) async-start(bf16[8,256,128]{2,1,0:T(8,128)(2,1)} %copy-done.6), calls=%async_computation.3 | async-start | bytes 1048576 | tf_op jit(solution)/shard_map/all_to_all | solution.py:559
  64.2 9.2 %collective-permute-start.4 = (bf16[128,256]{1,0:T(8,128)(2,1)S(1)}, bf16[128,256]{1,0:T(8,128)(2,1)S(1)}, u32[]{:S(2)}, u32[]{:S(2)}) collective-permute-start(bf16[128,256]{1,0:T(8,128)(2,1)S(1)} %get-tuple-element.33.refs_0_.refs_2_.refs_6_), channel_id=1, source_target_pairs={{0,16},{2,18},{4,20},{6,22},{8,24},{10,26},{12,28},{14,30},{16,0},... | collective-permute-start | bytes 196616 | tf_op jit(solution)/shard_map/ppermute | solution.py:600
  64.2 9.2 %collective-permute-start.3 = (bf16[128,256]{1,0:T(8,128)(2,1)}, bf16[128,256]{1,0:T(8,128)(2,1)S(1)}, u32[]{:S(2)}, u32[]{:S(2)}) collective-permute-start(bf16[128,256]{1,0:T(8,128)(2,1)} %get-tuple-element.35.refs_7_), channel_id=1, source_target_pairs={{0,2},{2,0},{4,6},{6,4},{8,10},{10,8},{12,14},{14,12},{16,18},{18,... | collective-permute-start | bytes 196616 | tf_op jit(solution)/shard_map/ppermute | solution.py:600
  66.3 7.1 %collective-permute-start.5 = (bf16[128,256]{1,0:T(8,128)(2,1)}, bf16[128,256]{1,0:T(8,128)(2,1)S(1)}, u32[]{:S(2)}, u32[]{:S(2)}) collective-permute-start(bf16[128,256]{1,0:T(8,128)(2,1)} %get-tuple-element.35.refs_7_), channel_id=1, source_target_pairs={{0,18},{2,16},{4,22},{6,20},{8,26},{10,24},{12,30},{14,28},{16,2},... | collective-permute-start | bytes 196616 | tf_op jit(solution)/shard_map/ppermute | solution.py:600
  66.4 12.2 %copy-start.28 = (s32[2]{0:T(128)S(1)}, s32[2]{0:T(128)}, u32[]{:S(2)}) copy-start(s32[2]{0:T(128)} %copy-done.27) | copy-start | bytes 28
  66.4 12.1 %copy-start.31 = (s32[2]{0:T(128)}, s32[2]{0:T(128)S(1)}, u32[]{:S(2)}) copy-start(s32[2]{0:T(128)S(1)} %pad_add_fusion.2.refs_1_) | copy-start | bytes 28
  66.4 12.2 %copy-start.5 = (bf16[8,256,128]{2,1,0:T(8,128)(2,1)S(1)}, bf16[8,256,128]{2,1,0:T(8,128)(2,1)}, u32[]{:S(2)}) copy-start(bf16[8,256,128]{2,1,0:T(8,128)(2,1)} %copy-done.3) | copy-start | bytes 1572868
  73.4 1.0 copy-start.7
  74.5 4.1 %copy-start.16 = (bf16[256,128]{1,0:T(8,128)(2,1)S(1)}, bf16[256,128]{1,0:T(8,128)(2,1)}, u32[]{:S(2)}) copy-start(bf16[256,128]{1,0:T(8,128)(2,1)} %copy-done.15) | copy-start | bytes 196612
  74.5 4.2 %copy-start.18 = (bf16[128,256]{1,0:T(8,128)(2,1)S(1)}, bf16[128,256]{1,0:T(8,128)(2,1)}, u32[]{:S(2)}) copy-start(bf16[128,256]{1,0:T(8,128)(2,1)} %copy-done.17) | copy-start | bytes 196612
  74.5 4.2 %copy-start.20 = (bf16[128,256]{1,0:T(8,128)(2,1)S(1)}, bf16[128,256]{1,0:T(8,128)(2,1)}, u32[]{:S(2)}) copy-start(bf16[128,256]{1,0:T(8,128)(2,1)} %copy-done.19) | copy-start | bytes 196612
  85.2 0.8 copy-start.8
  86.0 0.8 copy-start.9
  86.8 0.6 copy-start.25
  87.5 0.6 copy-start.33
  88.1 27.0 %all-to-all-start.2 = ((bf16[8,256,128]{2,1,0:T(8,128)(2,1)}), bf16[8,256,128]{2,1,0:T(8,128)(2,1)S(1)}, u32[]{:S(2)}, u32[]{:S(2)}) async-start(bf16[8,256,128]{2,1,0:T(8,128)(2,1)} %copy-done.9), calls=%async_computation.2 | async-start | bytes 1048576 | tf_op jit(solution)/shard_map/all_to_all | solution.py:559
  94.1 20.1 %collective-permute-start.8 = (bf16[4,256,256]{2,1,0:T(8,128)(2,1)}, bf16[4,256,256]{2,1,0:T(8,128)(2,1)S(1)}, u32[]{:S(2)}, u32[]{:S(2)}) collective-permute-start(bf16[4,256,256]{2,1,0:T(8,128)(2,1)} %copy-done.8), channel_id=1, source_target_pairs={{0,2},{2,0},{4,6},{6,4},{8,10},{10,8},{12,14},{14,12},{1,3},{3,1},... | collective-permute-start | bytes 1572872 | tf_op jit(solution)/shard_map/ppermute | solution.py:605
  96.1 1.0 copy-start.10
  97.2 0.7 copy-start.32
  101.9 17.7 %copy-start.34 = (bf16[256,128]{1,0:T(8,128)(2,1)S(1)}, bf16[256,128]{1,0:T(8,128)(2,1)}, u32[]{:S(2)}) copy-start(bf16[256,128]{1,0:T(8,128)(2,1)} %copy-done.33) | copy-start | bytes 196612
  101.9 22.0 %copy-start.26 = (bf16[256,128]{1,0:T(8,128)(2,1)S(1)}, bf16[256,128]{1,0:T(8,128)(2,1)}, u32[]{:S(2)}) copy-start(bf16[256,128]{1,0:T(8,128)(2,1)} %copy-done.25) | copy-start | bytes 196612
  102.0 22.0 %copy-start.29 = (s32[2]{0:T(128)S(1)}, s32[2]{0:T(128)}, u32[]{:S(2)}) copy-start(s32[2]{0:T(128)} %copy-done.27) | copy-start | bytes 28
  115.1 18.9 %all-to-all-start.4 = ((bf16[4,256,256]{2,1,0:T(8,128)(2,1)}), bf16[4,256,256]{2,1,0:T(8,128)(2,1)S(1)}, u32[]{:S(2)}, u32[]{:S(2)}) async-start(bf16[4,256,256]{2,1,0:T(8,128)(2,1)} %add.37), calls=%async_computation.4 | async-start | bytes 1048576 | tf_op jit(solution)/shard_map/all_to_all | solution.py:559
  119.6 4.3 %collective-permute-start.7 = (bf16[256,128]{1,0:T(8,128)(2,1)S(1)}, bf16[256,128]{1,0:T(8,128)(2,1)S(1)}, u32[]{:S(2)}, u32[]{:S(2)}) collective-permute-start(bf16[256,128]{1,0:T(8,128)(2,1)S(1)} %copy-done.34), channel_id=1, source_target_pairs={{0,2},{2,0},{4,6},{6,4},{8,10},{10,8},{12,14},{14,12},{1,3},{3,1},... | collective-permute-start | bytes 196616 | tf_op jit(solution)/shard_map/ppermute | solution.py:612

commit v5 on v3

v5 whole, which is shorter than its diff:
```python
import functools

import jax
import jax.numpy as jnp
from jax import lax
from jax.experimental import pallas as pl
from jax.experimental.pallas import tpu as pltpu
from jax.sharding import PartitionSpec as P

HD = 128
MASKED = -1e30
INNER = 2
SOURCES = 3
ANY = pl.BlockSpec(memory_space=pl.ANY)
VMEM = pl.BlockSpec(memory_space=pltpu.VMEM)
SMEM = pl.BlockSpec(memory_space=pltpu.SMEM)


def against(left_op, right_op):
    return lax.dot_general(
        left_op, right_op, (((1,), (1,)), ((), ())), preferred_element_type=jnp.float32
    )


def product(left_op, right_op):
    return jnp.dot(left_op, right_op, preferred_element_type=jnp.float32)


def begin(source, target, semaphore):
    copy = pltpu.make_async_copy(source, target, semaphore)
    copy.start()
    return copy


def call(kernel, out_shape, in_specs, out_specs, scratch, micros, name, after=()):
    skipped = len(after)
    in_specs = [ANY] * skipped + in_specs
    run = pl.pallas_call(
        lambda *refs: kernel(*refs[skipped:]),
        out_shape=out_shape,
        in_specs=in_specs,
        out_specs=out_specs,
        scratch_shapes=scratch,
        compiler_params=pltpu.CompilerParams(vmem_limit_bytes=60 * 1024 * 1024),
        cost_estimate=pl.CostEstimate(
            flops=int(micros * 1e9), bytes_accessed=int(micros * 3e6), transcendentals=0
        ),
        name=name,
    )

    def placed(*args):
        args = [
            pltpu.with_memory_space_constraint(arg, pltpu.HBM) if spec is ANY else arg
            for spec, arg in zip(in_specs, (*after, *args))
        ]
        return run(*args)

    return placed


def bf16(*shape):
    return pltpu.HBM(shape, jnp.bfloat16)


def f32(*shape):
    return pltpu.HBM(shape, jnp.float32)


def part_kernel(at_ref, q_ref, k_ref, v_ref, kv_mine, kv_theirs, q_theirs, held_s, in_sem, out_sem):
    half = q_theirs.shape[1]
    loads = [begin(held, held_s.at[i], in_sem.at[i]) for i, held in enumerate((k_ref, v_ref, q_ref))]
    mine = pl.ds(pl.multiple_of(at_ref[0] * half, half), half)
    theirs = pl.ds(pl.multiple_of((1 - at_ref[0]) * half, half), half)
    copies = []
    for index in range(2):
        loads[index].wait()
        place = slice(index * half, (index + 1) * half)
        for side, (cols, out) in enumerate(((mine, kv_mine), (theirs, kv_theirs))):
            sem = out_sem.at[2 * index + side]
            copies.append(begin(held_s.at[index, :, cols], out.at[:, place], sem))
    loads[2].wait()
    copies.append(begin(held_s.at[2, :, theirs], q_theirs, out_sem.at[4]))
    for copy in copies:
        copy.wait()


def part_heads(at, queries, keys, values):
    rows, feats = queries.shape
    half = feats // INNER
    return call(
        part_kernel,
        [bf16(rows, 2 * half), bf16(rows, 2 * half), bf16(rows, half)],
        [SMEM] + [ANY] * 3,
        [ANY] * 3,
        [
            pltpu.VMEM((3, rows, feats), jnp.bfloat16),
            pltpu.SemaphoreType.DMA((3,)),
            pltpu.SemaphoreType.DMA((5,)),
        ],
        2,
        "part_heads",
    )(at, queries, keys, values)


def prelude_kernel(at_ref, pattern, offsets, grad_ref, weight_ref, first, key_mask, row_mask, *rest):
    grad_s, weight_s, first_s, mask_s, row_s, sem, out_sem = rest
    rows, width = grad_s.shape
    block_count, glob_count = offsets.shape
    start = pl.multiple_of(at_ref[2] * width, width)
    loads = [
        begin(grad_ref, grad_s, sem.at[0]),
        begin(weight_ref.at[:, pl.ds(start, width)], weight_s, sem.at[1]),
    ]
    own = at_ref[1] * INNER + at_ref[0]
    partner = at_ref[1] * INNER + 1 - at_ref[0]
    lane = lax.broadcasted_iota(jnp.int32, (1, HD), 1)
    row_at = lax.broadcasted_iota(jnp.int32, (rows, HD), 0)
    col_at = lax.broadcasted_iota(jnp.int32, (8, rows), 1)
    group_at = lax.broadcasted_iota(jnp.int32, (8, rows), 0)
    for index in range(block_count):
        block = at_ref[SOURCES + index]
        hidden = []
        for target in (own, partner):
            seen = jnp.abs(block - target) <= 1
            for r in range(pattern.shape[1]):
                seen = seen | (pattern[target, r] == block)
            hidden.append(jnp.where(seen, 0, 1))
        lane_hidden = jnp.where(lane == 0, hidden[0], jnp.where(lane == 1, hidden[1], 0))
        hidden_rows = jnp.broadcast_to(lane_hidden, (rows, HD))
        for r in range(glob_count):
            hidden_rows = jnp.where(row_at == offsets[block, r], 0, hidden_rows)
        mask_s[index * rows : (index + 1) * rows, :] = hidden_rows.astype(jnp.float32).astype(
            jnp.bfloat16
        )
    for group, target in enumerate((own, partner)):
        local = jnp.where(group_at == group, MASKED, 0.0)
        for r in range(glob_count):
            local = jnp.where(col_at == offsets[target, r], 0.0, local)
        row_s[:, group * rows : (group + 1) * rows] = local
    stores = [begin(mask_s, key_mask, out_sem.at[0]), begin(row_s, row_mask, out_sem.at[1])]
    for load in loads:
        load.wait()
    first_s[...] = against(weight_s[...], grad_s[...])
    stores.append(begin(first_s, first, out_sem.at[2]))
    for store in stores:
        store.wait()


def prelude(at, pattern, offsets, grad_own, out_weight):
    rows, width = grad_own.shape
    feats = out_weight.shape[0]
    keys = offsets.shape[0] * rows
    return call(
        prelude_kernel,
        [
            f32(*(feats, rows)),
            bf16(keys, HD),
            f32(*(8, 2 * rows)),
        ],
        [SMEM] * 3 + [ANY] * 2,
        [ANY] * 3,
        [
            pltpu.VMEM((rows, width), jnp.bfloat16),
            pltpu.VMEM((feats, width), jnp.bfloat16),
            pltpu.VMEM((feats, rows), jnp.float32),
            pltpu.VMEM((keys, HD), jnp.bfloat16),
            pltpu.VMEM((8, 2 * rows), jnp.float32),
            pltpu.SemaphoreType.DMA((2,)),
            pltpu.SemaphoreType.DMA((3,)),
        ],
        3,
        "prelude",
    )(at, pattern, offsets, grad_own, out_weight)


def forward_kernel(block_count, head_count, at_ref, q_ref, q_recv, key_mask, row_mask, *refs):
    kv_refs, refs = refs[:block_count], refs[block_count:]
    e_out, inv_out, attn_mine, attn_theirs = refs[:4]
    q_s, mask_s, kv_s, e_s, s_ref, attn_s, inv_s, row_s, sem, kv_sem, e_sem, out_sem = refs[4:]
    rows = q_recv.shape[0]
    feats = head_count * HD
    score_scale = HD ** (-0.5)
    mine = pl.ds(pl.multiple_of(at_ref[0] * feats, feats), feats)
    loads = [
        begin(q_ref.at[:, mine], q_s.at[0], sem.at[0]),
        begin(q_recv, q_s.at[1], sem.at[1]),
        begin(key_mask, mask_s, sem.at[2]),
        begin(row_mask, row_s, sem.at[3]),
    ]
    kv_loads = [begin(kv_refs[j], kv_s.at[j], kv_sem.at[j]) for j in range(block_count)]
    for load in loads:
        load.wait()
    rows_low = row_s[...].astype(jnp.bfloat16)
    hidden = jnp.concatenate([rows_low, jnp.zeros((HD - 8, 2 * rows), jnp.bfloat16)], axis=0)
    stores = []
    for head in range(head_count):
        cols = slice(head * HD, (head + 1) * HD)
        vcols = slice(feats + head * HD, feats + (head + 1) * HD)
        q_t = jnp.concatenate(
            [jnp.transpose(q_s[0, :, cols]), jnp.transpose(q_s[1, :, cols])], axis=1
        )
        q_t = jnp.concatenate([q_t, hidden], axis=0)
        top = jnp.full((1, 2 * rows), MASKED, jnp.float32)
        for j in range(block_count):
            if head == 0:
                kv_loads[j].wait()
            keys = slice(j * rows, (j + 1) * rows)
            scores = product(jnp.concatenate([kv_s[j, :, cols], mask_s[keys, :]], axis=1), q_t)
            s_ref[keys, :] = scores
            top = jnp.maximum(top, jnp.max(scores, axis=0, keepdims=True))
        total = jnp.zeros((1, 2 * rows), jnp.float32)
        attn_t = jnp.zeros((HD, 2 * rows), jnp.float32)
        for j in range(block_count):
            keys = slice(j * rows, (j + 1) * rows)
            weights = jnp.exp((s_ref[keys, :] - top) * score_scale)
            total = total + jnp.sum(weights, axis=0, keepdims=True)
            low = weights.astype(jnp.bfloat16)
            e_s[head, keys, :] = low
            stores.append(
                begin(e_s.at[head, keys], e_out.at[head, keys], e_sem.at[head * block_count + j])
            )
            attn_t = attn_t + product(jnp.transpose(kv_s[j, :, vcols]), low)
        inverse = 1.0 / total
        inv_s[head : head + 1, :] = inverse
        attn_low = (attn_t * inverse).astype(jnp.bfloat16)
        attn_s[0, cols, :] = attn_low[:, :rows]
        attn_s[1, cols, :] = attn_low[:, rows:]
    stores.append(begin(attn_s.at[0], attn_mine, out_sem.at[0]))
    stores.append(begin(attn_s.at[1], attn_theirs, out_sem.at[1]))
    stores.append(begin(inv_s, inv_out, out_sem.at[2]))
    for store in stores:
        store.wait()


def forward(at, queries, q_recv, key_mask, row_mask, kv_blocks, after):
    block_count = len(kv_blocks)
    rows, feats = q_recv.shape
    heads = feats // HD
    keys = block_count * rows
    return call(
        functools.partial(forward_kernel, block_count, heads),
        [
            bf16(heads, keys, 2 * rows),
            f32(*(max(heads, 8), 2 * rows)),
            bf16(feats, rows),
            bf16(feats, rows),
        ],
        [SMEM] + [ANY] * (4 + block_count),
        [ANY] * 4,
        [
            pltpu.VMEM((2, rows, feats), jnp.bfloat16),
            pltpu.VMEM((keys, HD), jnp.bfloat16),
            pltpu.VMEM((block_count, rows, 2 * feats), jnp.bfloat16),
            pltpu.VMEM((heads, keys, 2 * rows), jnp.bfloat16),
            pltpu.VMEM((keys, 2 * rows), jnp.float32),
            pltpu.VMEM((2, feats, rows), jnp.bfloat16),
            pltpu.VMEM((max(heads, 8), 2 * rows), jnp.float32),
            pltpu.VMEM((8, 2 * rows), jnp.float32),
            pltpu.SemaphoreType.DMA((4,)),
            pltpu.SemaphoreType.DMA((block_count,)),
            pltpu.SemaphoreType.DMA((heads * block_count,)),
            pltpu.SemaphoreType.DMA((3,)),
        ],
        6,
        "forward",
        after,
    )(at, queries, q_recv, key_mask, row_mask, *kv_blocks)


def backward_kernel(block_count, head_count, at_ref, *refs):
    q_ref, q_recv, g_mine, g_recv, attn_mine, attn_theirs, inv_ref, e_ref = refs[:8]
    kv_refs, refs = refs[8 : 8 + block_count], refs[8 + block_count :]
    dq_mine, dq_theirs = refs[:2]
    part_outs, refs = refs[2 : 2 + block_count], refs[2 + block_count :]
    q_s, t_s, inv_s, kv_s, e_s, part_s, dq_s, sem, kv_sem, e_sem, part_sem, dq_sem = refs
    rows = q_recv.shape[0]
    feats = head_count * HD
    score_scale = HD ** (-0.5)
    mine = pl.ds(pl.multiple_of(at_ref[0] * feats, feats), feats)
    loads = [begin(q_ref.at[:, mine], q_s.at[0], sem.at[0]), begin(q_recv, q_s.at[1], sem.at[1])]
    for index, held in enumerate((g_mine, g_recv, attn_mine, attn_theirs)):
        loads.append(begin(held, t_s.at[index], sem.at[2 + index]))
    loads.append(begin(inv_ref, inv_s, sem.at[6]))
    kv_loads, e_loads, stores = [], {}, []
    for j in range(block_count):
        keys = slice(j * rows, (j + 1) * rows)
        kv_loads.append(begin(kv_refs[j], kv_s.at[j], kv_sem.at[j]))
        for head in range(head_count):
            e_loads[head, j] = begin(
                e_ref.at[head, keys], e_s.at[head, keys], e_sem.at[head * block_count + j]
            )
    for load in loads:
        load.wait()
    for head in range(head_count):
        cols = slice(head * HD, (head + 1) * HD)
        vcols = slice(feats + head * HD, feats + (head + 1) * HD)
        inverse = inv_s[head : head + 1, :]
        g_t = jnp.concatenate([t_s[0, cols, :], t_s[1, cols, :]], axis=1).astype(jnp.float32)
        attn_t = jnp.concatenate([t_s[2, cols, :], t_s[3, cols, :]], axis=1)
        row_dot = jnp.sum(g_t * attn_t.astype(jnp.float32), axis=0, keepdims=True) * inverse
        g_t = (g_t * inverse).astype(jnp.bfloat16)
        grad = jnp.transpose(g_t)
        query = jnp.concatenate([q_s[0, :, cols], q_s[1, :, cols]], axis=0)
        dq_t = jnp.zeros((HD, 2 * rows), jnp.float32)
        for j in range(block_count):
            keys = slice(j * rows, (j + 1) * rows)
            if head == 0:
                kv_loads[j].wait()
            e_loads[head, j].wait()
            low = e_s[head, keys, :]
            dprobs = product(kv_s[j, :, vcols], g_t)
            dscore = (low.astype(jnp.float32) * (dprobs - row_dot)).astype(jnp.bfloat16)
            dq_t = dq_t + product(jnp.transpose(kv_s[j, :, cols]), dscore)
            part_s[j, :, cols] = (score_scale * product(dscore, query)).astype(jnp.bfloat16)
            part_s[j, :, vcols] = product(low, grad).astype(jnp.bfloat16)
            if head == head_count - 1:
                stores.append(begin(part_s.at[j], part_outs[j], part_sem.at[j]))
        dquery = (score_scale * jnp.transpose(dq_t)).astype(jnp.bfloat16)
        dq_s[0, :, cols] = dquery[:rows]
        dq_s[1, :, cols] = dquery[rows:]
    stores.append(begin(dq_s.at[0], dq_mine, dq_sem.at[0]))
    stores.append(begin(dq_s.at[1], dq_theirs, dq_sem.at[1]))
    for store in stores:
        store.wait()


def backward(at, queries, q_recv, g_mine, g_recv, attn_mine, attn_theirs, inverse, weights, kv_blocks):
    block_count = len(kv_blocks)
    rows, feats = q_recv.shape
    heads = feats // HD
    keys = block_count * rows
    out = call(
        functools.partial(backward_kernel, block_count, heads),
        [bf16(rows, feats)] * 2 + [bf16(rows, 2 * feats)] * block_count,
        [SMEM] + [ANY] * (8 + block_count),
        [ANY] * (2 + block_count),
        [
            pltpu.VMEM((2, rows, feats), jnp.bfloat16),
            pltpu.VMEM((4, feats, rows), jnp.bfloat16),
            pltpu.VMEM(inverse.shape, jnp.float32),
            pltpu.VMEM((block_count, rows, 2 * feats), jnp.bfloat16),
            pltpu.VMEM((heads, keys, 2 * rows), jnp.bfloat16),
            pltpu.VMEM((block_count, rows, 2 * feats), jnp.bfloat16),
            pltpu.VMEM((2, rows, feats), jnp.bfloat16),
            pltpu.SemaphoreType.DMA((7,)),
            pltpu.SemaphoreType.DMA((block_count,)),
            pltpu.SemaphoreType.DMA((heads * block_count,)),
            pltpu.SemaphoreType.DMA((block_count,)),
            pltpu.SemaphoreType.DMA((2,)),
        ],
        8,
        "backward",
    )(at, queries, q_recv, g_mine, g_recv, attn_mine, attn_theirs, inverse, weights, *kv_blocks)
    return out[0], out[1], out[2:]


def grad_heads_kernel(part_count, sends, picked, at_ref, first_ref, weight_ref, *refs):
    grads, refs = refs[:part_count], refs[part_count:]
    outs, refs = refs[: 2 + sends], refs[2 + sends :]
    first_s, grad_s, weight_s, out_s, first_sem, weight_sem, grad_sem, send_sem, out_sem = refs
    half = out_s.shape[1]
    width = grads[0].shape[1]
    first_load = begin(first_ref, first_s, first_sem)
    weight_loads, grad_loads = [], []
    for k in range(part_count):
        grad_loads.append(begin(grads[k], grad_s.at[k], grad_sem.at[k]))
        if k:
            start = pl.multiple_of(at_ref[k] * width, width)
            columns = weight_ref.at[:, pl.ds(start, width)]
            weight_loads.append(begin(columns, weight_s.at[k - 1], weight_sem.at[k - 1]))
    for load in grad_loads:
        load.wait()
    copies = []
    for send in range(sends):
        for i in range(picked):
            place = send * picked + i
            target = outs[2 + send].at[:, i * width : (i + 1) * width]
            for k in range(part_count):

                @pl.when(at_ref[part_count + place] == k)
                def _():
                    begin(grad_s.at[k], target, send_sem.at[place])

            copies.append(pltpu.make_async_copy(grad_s.at[0], target, send_sem.at[place]))
    first_load.wait()
    summed = first_s[...]
    for k in range(1, part_count):
        weight_loads[k - 1].wait()
        summed = summed + against(weight_s[k - 1], grad_s[k])
    first_s[...] = summed
    for side, at in enumerate((at_ref[0], 1 - at_ref[0])):
        kept = first_s[pl.ds(pl.multiple_of(at * half, half), half), :]
        out_s[side] = kept.astype(jnp.bfloat16)
        copies.append(begin(out_s.at[side], outs[side], out_sem.at[side]))
    for copy in copies:
        copy.wait()


def grad_heads(at, first, out_weight, grads, sends, picked):
    feats, rows = first.shape
    half = feats // INNER
    count = len(grads)
    width = grads[0].shape[1]
    out = call(
        functools.partial(grad_heads_kernel, count, sends, picked),
        [bf16(half, rows), bf16(half, rows)] + [bf16(rows, picked * width)] * sends,
        [SMEM] + [ANY] * (2 + count),
        [ANY] * (2 + sends),
        [
            pltpu.VMEM((feats, rows), jnp.float32),
            pltpu.VMEM((count, rows, width), jnp.bfloat16),
            pltpu.VMEM((count - 1, feats, width), jnp.bfloat16),
            pltpu.VMEM((INNER, half, rows), jnp.bfloat16),
            pltpu.SemaphoreType.DMA,
            pltpu.SemaphoreType.DMA((count - 1,)),
            pltpu.SemaphoreType.DMA((count,)),
            pltpu.SemaphoreType.DMA((sends * picked,)),
            pltpu.SemaphoreType.DMA((INNER,)),
        ],
        3,
        "grad_heads",
    )(at, first, out_weight, *grads)
    return out[0], out[1], out[2:]


def weight_kernel(part_count, picked, doc_count, sent, at_ref, *refs):
    attn, refs = refs[: INNER * doc_count], refs[INNER * doc_count :]
    grads, refs = refs[:part_count], refs[part_count:]
    swapped, refs = refs[: doc_count - 1], refs[doc_count - 1 :]
    out, attn_s, grad_s, out_s, attn_sem, grad_sem, out_sem = refs
    outer, feats, width = out.shape
    half = feats // INNER
    piece = grads[0].shape[1]
    pieces = piece // width
    here = (1 - at_ref[0]) if sent else at_ref[0]
    attn_loads, grad_loads = [], []
    for doc in range(doc_count):
        for side in range(INNER):
            at = (1 - at_ref[0]) if side else at_ref[0]
            index = doc * INNER + side
            target = attn_s.at[doc, pl.ds(pl.multiple_of(at * half, half), half)]
            attn_loads.append(begin(attn[index], target, attn_sem.at[index]))
    for k in range(outer):
        place = lax.rem(at_ref[1] + k, outer) * INNER + here
        which = at_ref[2 + place // pieces]
        cols = pl.ds(pl.multiple_of(lax.rem(place, pieces) * width, width), width)
        for i in range(part_count):

            @pl.when(which == i)
            def _():
                begin(grads[i].at[:, cols], grad_s.at[0, k], grad_sem.at[k])

        loads = [pltpu.make_async_copy(grads[0].at[:, cols], grad_s.at[0, k], grad_sem.at[k])]
        cols = pl.ds(pl.multiple_of(place * width, width), width)
        for doc in range(1, doc_count):
            source = swapped[doc - 1].at[:, cols]
            loads.append(begin(source, grad_s.at[doc, k], grad_sem.at[doc * outer + k]))
        grad_loads.append(loads)
    for load in attn_loads:
        load.wait()
    stores = []
    for k in range(outer):
        term = 0.0
        for doc in range(doc_count):
            grad_loads[k][doc].wait()
            term = term + product(attn_s[doc], grad_s[doc, k])
        out_s[k] = term.astype(out_s.dtype)
        stores.append(begin(out_s.at[k], out.at[k], out_sem.at[k]))
    for store in stores:
        store.wait()


def weight_terms(at, attn, grads, swapped, outer, picked, sent, after=()):
    half, rows = attn[0].shape
    feats = half * INNER
    doc_count = len(attn) // INNER
    width = picked * grads[0].shape[1] // (outer * INNER)
    return call(
        functools.partial(weight_kernel, len(grads), picked, doc_count, sent),
        bf16(outer, feats, width),
        [SMEM] + [ANY] * (len(attn) + len(grads) + len(swapped)),
        ANY,
        [
            pltpu.VMEM((doc_count, feats, rows), jnp.bfloat16),
            pltpu.VMEM((doc_count, outer, rows, width), jnp.bfloat16),
            pltpu.VMEM((outer, feats, width), jnp.bfloat16),
            pltpu.SemaphoreType.DMA((len(attn),)),
            pltpu.SemaphoreType.DMA((doc_count * outer,)),
            pltpu.SemaphoreType.DMA((outer,)),
        ],
        3,
        "weight_sent" if sent else "weight_kept",
        after,
    )(at, *attn, *grads, *swapped)


def weight_add_kernel(keep, recv, *refs):
    outer = keep.shape[0]
    outs, (held_s, out_s, sem, out_sem) = refs[:outer], refs[outer:]
    loads = []
    for k in range(outer):
        for index, held in enumerate((keep, recv)):
            loads.append(begin(held.at[k], held_s.at[index, k], sem.at[2 * k + index]))
    stores = []
    for k in range(outer):
        loads[2 * k].wait()
        loads[2 * k + 1].wait()
        summed = held_s[0, k].astype(jnp.float32) + held_s[1, k].astype(jnp.float32)
        out_s[k] = summed.astype(jnp.bfloat16)
        stores.append(begin(out_s.at[k], outs[k], out_sem.at[k]))
    for store in stores:
        store.wait()


def weight_add(keep, recv):
    outer, feats, width = keep.shape
    return call(
        weight_add_kernel,
        [bf16(feats, width)] * outer,
        [ANY] * 2,
        [ANY] * outer,
        [
            pltpu.VMEM((2, outer, feats, width), jnp.bfloat16),
            pltpu.VMEM((outer, feats, width), jnp.bfloat16),
            pltpu.SemaphoreType.DMA((2 * outer,)),
            pltpu.SemaphoreType.DMA((outer,)),
        ],
        1.5,
        "weight_add",
    )(keep, recv)


def collect_kernel(count, at_ref, dq_mine, dq_recv, *refs):
    terms, (grad_q, grad_k, grad_v) = refs[:count], refs[count : count + 3]
    terms_s, dq_s, out_s, term_sem, dq_sem, out_sem = refs[count + 3 :]
    half = dq_mine.shape[1]
    dq_loads = [begin(held, dq_s.at[i], dq_sem.at[i]) for i, held in enumerate((dq_mine, dq_recv))]
    loads = [begin(terms[c], terms_s.at[c], term_sem.at[c]) for c in range(count)]
    for load in dq_loads + loads:
        load.wait()
    for side, at in enumerate((at_ref[0], 1 - at_ref[0])):
        cols = pl.ds(pl.multiple_of(at * half, half), half)
        summed = terms_s[side].astype(jnp.float32)
        for c in range(side + INNER, count, INNER):
            summed = summed + terms_s[c].astype(jnp.float32)
        summed = summed.astype(jnp.bfloat16)
        out_s[0, :, cols] = dq_s[side]
        out_s[1, :, cols] = summed[:, :half]
        out_s[2, :, cols] = summed[:, half:]
    stores = [
        begin(out_s.at[i], out, out_sem.at[i]) for i, out in enumerate((grad_q, grad_k, grad_v))
    ]
    for store in stores:
        store.wait()


def collect(at, dq_mine, dq_recv, terms):
    rows, half = dq_mine.shape
    count = len(terms)
    return call(
        functools.partial(collect_kernel, count),
        [bf16(rows, INNER * half)] * 3,
        [SMEM] + [ANY] * (2 + count),
        [ANY] * 3,
        [
            pltpu.VMEM((count, rows, 2 * half), jnp.bfloat16),
            pltpu.VMEM((2, rows, half), jnp.bfloat16),
            pltpu.VMEM((3, rows, INNER * half), jnp.bfloat16),
            pltpu.SemaphoreType.DMA((count,)),
            pltpu.SemaphoreType.DMA((2,)),
            pltpu.SemaphoreType.DMA((3,)),
        ],
        2,
        "collect",
    )(at, dq_mine, dq_recv, *terms)


def per_device(
    queries, key_heads, value_heads, grad_output, out_weight, block_pattern, global_offsets
):
    dp_count, ctx_count, tp_count = (lax.axis_size(name) for name in ("dp", "ctx", "tp"))
    dp_at, ctx_at, tp_at = (lax.axis_index(name) for name in ("dp", "ctx", "tp"))
    outer = ctx_count // INNER
    outer_at, inner_at = ctx_at // INNER, ctx_at % INNER
    picked = tp_count // dp_count

    def ctx_pairs(step, side, dp_step=0):
        moved = [(c + step * INNER) % ctx_count ^ side for c in range(ctx_count)]
        if not dp_step:
            return list(enumerate(moved))
        return [
            (d * ctx_count + c, (d + dp_step) % dp_count * ctx_count + moved[c])
            for d in range(dp_count)
            for c in range(ctx_count)
        ]

    def shift_pairs(count, step):
        return [(i, (i + step) % count) for i in range(count)]

    def dp_steps(which):
        return [(which * picked + i - tp_at) % tp_count for i in range(picked)]

    routes = [(step, side) for step in range(outer) for side in range(INNER)]
    sources = [
        ((outer_at - step) % outer) * INNER + (inner_at + side) % INNER for step, side in routes
    ]
    at = jnp.stack([inner_at, outer_at, tp_at] + sources)
    columns_at = [(tp_at + step) % tp_count for step in range(1, tp_count)]
    for step in range(1, dp_count):
        columns_at = columns_at + dp_steps((dp_at + step) % dp_count)
    columns_at = jnp.stack([inner_at] + columns_at)
    weight_at = jnp.stack([inner_at, outer_at] + dp_steps(dp_at))

    grad_own = grad_output[0]
    grads = [grad_own] + [
        lax.ppermute(grad_own, "tp", shift_pairs(tp_count, -step)) for step in range(1, tp_count)
    ]
    kv_mine, kv_theirs, q_theirs = part_heads(at, queries[0], key_heads[0], value_heads[0])
    kv_blocks = [
        lax.ppermute(kv_theirs if side else kv_mine, "ctx", ctx_pairs(step, side))
        if step or side
        else kv_mine
        for step, side in routes
    ]
    q_recv = lax.ppermute(q_theirs, "ctx", ctx_pairs(0, 1))

    first, key_mask, row_mask = prelude(at, block_pattern, global_offsets, grad_own, out_weight)
    g_mine, g_theirs, grad_sends = grad_heads(
        columns_at, first, out_weight, grads, dp_count - 1, picked
    )
    g_recv = lax.ppermute(g_theirs, "ctx", ctx_pairs(0, 1))
    swapped = [
        lax.ppermute(send, "dp", shift_pairs(dp_count, step + 1))
        for step, send in enumerate(grad_sends)
    ]

    weights, inverse, attn_mine, attn_theirs = forward(
        at, queries[0], q_recv, key_mask, row_mask, kv_blocks, (g_theirs,)
    )

    attn = []
    for step in range(dp_count):
        for held, side in ((attn_mine, 0), (attn_theirs, 1)):
            pairs = ctx_pairs(0, side, step)
            axes = ("dp", "ctx") if step else "ctx"
            attn.append(lax.ppermute(held, axes, pairs) if step or side else held)

    dq_mine, dq_theirs, parts = backward(
        at, queries[0], q_recv, g_mine, g_recv, attn_mine, attn_theirs, inverse, weights, kv_blocks
    )
    send = weight_terms(weight_at, attn, grads, swapped, outer, picked, True, (dq_mine,))
    weight_recv = lax.ppermute(send, "ctx", ctx_pairs(0, 1))
    terms = [
        lax.ppermute(part, "ctx", ctx_pairs(-step, side)) if step or side else part
        for (step, side), part in zip(routes, parts)
    ]
    dq_recv = lax.ppermute(dq_theirs, "ctx", ctx_pairs(0, 1))
    keep = weight_terms(weight_at, attn, grads, swapped, outer, picked, False, (send,))
    weight_sums = weight_add(keep, weight_recv)
    grad_weight = weight_sums[0].astype(jnp.float32)
    for step in range(1, outer):
        grad_weight = grad_weight + lax.ppermute(
            weight_sums[step], "ctx", ctx_pairs(step, 0)
        ).astype(jnp.float32)

    grad_q, grad_k, grad_v = collect(at, dq_mine, dq_recv, terms)
    return grad_q[None], grad_k[None], grad_v[None], grad_weight.astype(jnp.bfloat16)


def solution(mesh):
    in_specs = (
        P("dp", "ctx", "tp"),
        P("dp", "ctx", "tp"),
        P("dp", "ctx", "tp"),
        P("dp", "ctx", "tp"),
        P("tp", None),
        P(),
        P(),
    )
    out_specs = (
        P("dp", "ctx", "tp"),
        P("dp", "ctx", "tp"),
        P("dp", "ctx", "tp"),
        P("tp", ("dp", "ctx")),
    )
    return jax.shard_map(
        per_device, mesh=mesh, in_specs=in_specs, out_specs=out_specs, check_vma=False
    )
```

time: 181 us -> 112 us (0.62)
  Pallas kernels: 100 us -> 37.9 us
  waiting for transfers between devices: 41.2 us -> 29.5 us
  starting transfers between devices: 26.9 us -> 36.4 us
  other arithmetic: 4.75 us -> 2.01 us
  local copies, waits for them, and re-layouts: 6.54 us -> 4.35 us
    pallas_call x8 -> x9, Pallas kernels: 100 us -> 37.9 us  [placed(): return run(*args)]
    ppermute x7 -> x24, starting transfers between devices: 8.62 us -> 33.4 us  [the longest x7 14.2 us: per_device(): lax.ppermute(kv_theirs if side else kv_mine, 'ctx', ctx_pairs(step, side))]
    all_to_all x3 -> x0, waiting for transfers between devices: 17.1 us -> none  [the longest x1 15.9 us: per_device(): lax.all_to_all(parts, 'ctx', split_axis=0, concat_axis=0, tiled=True)]
    all_to_all x3 -> x0, starting transfers between devices: 15.2 us -> none  [the longest x1 5.82 us: per_device(): lax.all_to_all(kv_send, 'ctx', split_axis=0, concat_axis=0, tiled=True)]
    ppermute x7 -> x24, waiting for transfers between devices: 24 us -> 28.6 us  [the longest x7 16.5 us: per_device(): lax.ppermute(part, 'ctx', ctx_pairs(-step, side))]
    unnamed x29 -> x71, local copies, waits for them, and re-layouts: 5.89 us -> 3.73 us
  transfers between devices with their start and end apart: 12 -> 26, of which waited for: 8 -> 6; matrix products, arithmetic and copies ran while one was open for 2% -> 2% of each run, Pallas kernels for 50% -> 30%
where the time goes in v5:
time: 112 us; the launch traced here: 111 us
  Pallas kernels  37.9 us (34%)
  starting transfers between devices  36.4 us (32%)
  waiting for transfers between devices  29.5 us (26%)
  local copies, waits for them, and re-layouts  4.35 us (4%)
  other arithmetic  2.01 us (2%)
    pallas_call x9, Pallas kernels, placed(): return run(*args)  37.9 us
    ppermute x7, waiting for transfers between devices, per_device(): lax.ppermute(part, 'ctx', ctx_pairs(-step, side))  16.5 us
    ppermute x7, starting transfers between devices, per_device(): lax.ppermute(kv_theirs if side else kv_mine, 'ctx', ctx_pairs(step, side))  14.2 us
    ppermute x7, starting transfers between devices, per_device(): lax.ppermute(part, 'ctx', ctx_pairs(-step, side))  12.5 us
    ppermute x1, waiting for transfers between devices, per_device(): dq_recv = lax.ppermute(dq_theirs, 'ctx', ctx_pairs(0, 1))  7.77 us
    unnamed x71, local copies, waits for them, and re-layouts  3.73 us
    ppermute x7, waiting for transfers between devices, per_device(): lax.ppermute(kv_theirs if side else kv_mine, 'ctx', ctx_pairs(step, side))  3.06 us
    ppermute x1, starting transfers between devices, per_device(): lax.ppermute(grad_own, 'tp', shift_pairs(tp_count, -step))  3.03 us
  transfers between devices with their start and end apart: 26, of which 6 were waited for; matrix products, arithmetic and copies ran while one was open for 2% of the time, Pallas kernels for 30%

profile of v5, /device:TPU:0, one launch (start us, length us, event | category | flops | bytes accessed | tf_op | source)
XLA Modules:
  0.0 111.2 jit_solution(4285523772522573731)
XLA Ops:
  0.6 3.0 %collective-permute-start.1 = (bf16[256,2048]{1,0:T(8,128)(2,1)}, bf16[256,2048]{1,0:T(8,128)(2,1)S(1)}, u32[]{:S(2)}, u32[]{:S(2)}) collective-permute-start(bf16[256,2048]{1,0:T(8,128)(2,1)} %bitcast.21), channel_id=1, source_target_pairs={{0,1},{1,0},{2,3},{3,2},{4,5},{5,4},{6,7},{7,6},{8,9},{9,8},{10,11... | collective-permute-start | bytes 3145736 | tf_op jit(solution)/shard_map/ppermute | solution.py:616
  3.7 0.6 stack.65.refs_0_.refs_1_
  4.3 2.5 %part_heads.1 = (bf16[256,256]{1,0:T(8,128)(2,1)}, bf16[256,256]{1,0:T(8,128)(2,1)}, bf16[256,128]{1,0:T(8,128)(2,1)}) custom-call(s32[11]{0:T(128)} %stack.65.refs_0_.refs_1_, bf16[256,256]{1,0:T(8,128)(2,1)} %bitcast.28, bf16[256,256]{1,0:T(8,128)(2,1)} %bitcast.26, bf16[256,256]{1,0:T(8,128)(2,1)} %bitcast.27), custom_call_target="tpu_custom_call" | custom-call | flops 2000000000 | bytes 6000000 | tf_op jit(solution)/shard_map/part_heads/pallas_call | solution.py:56
  6.8 4.6 %collective-permute-start.9 = (bf16[256,256]{1,0:T(8,128)(2,1)}, bf16[256,256]{1,0:T(8,128)(2,1)S(1)}, u32[]{:S(2)}, u32[]{:S(2)}) collective-permute-start(bf16[256,256]{1,0:T(8,128)(2,1)} %get-tuple-element.41), channel_id=1, source_target_pairs={{0,14},{2,12},{4,2},{6,0},{8,6},{10,4},{12,10},{14,8},{1,15},{3,13... | collective-permute-start | bytes 393224 | tf_op jit(solution)/shard_map/ppermute | solution.py:620
  11.4 1.9 %collective-permute-start.5 = (bf16[256,256]{1,0:T(8,128)(2,1)}, bf16[256,256]{1,0:T(8,128)(2,1)S(1)}, u32[]{:S(2)}, u32[]{:S(2)}) collective-permute-start(bf16[256,256]{1,0:T(8,128)(2,1)} %get-tuple-element.41), channel_id=1, source_target_pairs={{0,6},{2,4},{4,10},{6,8},{8,14},{10,12},{12,2},{14,0},{1,7},{3,5},... | collective-permute-start | bytes 393224 | tf_op jit(solution)/shard_map/ppermute | solution.py:620
  13.3 0.5 collective-permute-start
  13.8 0.7 copy.11.refs_1_
  14.5 4.4 %prelude.1 = (f32[256,256]{1,0:T(8,128)}, bf16[2048,128]{1,0:T(8,128)(2,1)}, f32[8,512]{1,0:T(8,128)}) custom-call(s32[11]{0:T(128)} %stack.65.refs_0_.refs_1_, s32[8,3]{1,0:T(8,128)} %copy.11.refs_1_, s32[8,8]{1,0:T(8,128)} %refs_2_.2, bf16[256,2048]{1,0:T(8,128)(2,1)} %bitcast.22, bf16[256,4096]{1,0:T(8,128)(2,1)} %refs_2_.3), custom_call_target="tpu_custom_call" | custom-call | flops 3000000000 | bytes 9000000 | tf_op jit(solution)/shard_map/prelude/pallas_call | solution.py:56
  19.0 0.6 pad_add_fusion.1.refs_1_
  19.6 0.7 pad_add_fusion.refs_0_
  20.3 0.0 collective-permute-done.refs_3_.refs_2_
  20.3 1.6 %collective-permute-start.3 = (bf16[256,256]{1,0:T(8,128)(2,1)S(1)}, bf16[256,256]{1,0:T(8,128)(2,1)S(1)}, u32[]{:S(2)}, u32[]{:S(2)}) collective-permute-start(bf16[256,256]{1,0:T(8,128)(2,1)S(1)} %copy-done.9), channel_id=1, source_target_pairs={{0,2},{2,0},{4,6},{6,4},{8,10},{10,8},{12,14},{14,12},{1,3},{3,1},... | collective-permute-start | bytes 393224 | tf_op jit(solution)/shard_map/ppermute | solution.py:620
  21.8 4.3 %collective-permute-start.8 = (bf16[256,256]{1,0:T(8,128)(2,1)S(1)}, bf16[256,256]{1,0:T(8,128)(2,1)S(1)}, u32[]{:S(2)}, u32[]{:S(2)}) collective-permute-start(bf16[256,256]{1,0:T(8,128)(2,1)S(1)} %copy-done.5), channel_id=1, source_target_pairs={{0,12},{2,14},{4,0},{6,2},{8,4},{10,6},{12,8},{14,10},{1,13},{3,15... | collective-permute-start | bytes 393224 | tf_op jit(solution)/shard_map/ppermute | solution.py:620
  26.1 0.0 collective-permute-done.7.refs_11_.refs_14_
  26.2 0.9 collective-permute-done.1.refs_4_.refs_7_
  27.0 1.8 %collective-permute-start.4 = (bf16[256,256]{1,0:T(8,128)(2,1)S(1)}, bf16[256,256]{1,0:T(8,128)(2,1)S(1)}, u32[]{:S(2)}, u32[]{:S(2)}) collective-permute-start(bf16[256,256]{1,0:T(8,128)(2,1)S(1)} %copy-done.5), channel_id=1, source_target_pairs={{0,4},{2,6},{4,8},{6,10},{8,12},{10,14},{12,0},{14,2},{1,5},{3,7},... | collective-permute-start | bytes 393224 | tf_op jit(solution)/shard_map/ppermute | solution.py:620
  28.8 3.8 %grad_heads.1 = (bf16[128,256]{1,0:T(8,128)(2,1)}, bf16[128,256]{1,0:T(8,128)(2,1)}, bf16[256,2048]{1,0:T(8,128)(2,1)}) custom-call(s32[3]{0:T(128)} %pad_add_fusion.refs_0_, f32[256,256]{1,0:T(8,128)} %get-tuple-element.35.refs_1_, bf16[256,4096]{1,0:T(8,128)(2,1)} %refs_2_.3, bf16[256,2048]{1,0:T(8,128)(2,1)} %bitcast.23, bf16[256,2048]{1,0:T(8,128)(2,1)} %copy-done.2), custom_call_target="tpu_custom_call" | custom-call | flops 3000000000 | bytes 9000000 | tf_op jit(solution)/shard_map/grad_heads/pallas_call | solution.py:56
  32.6 0.0 copy-start.8
  32.6 1.6 %collective-permute-start.2 = (bf16[128,256]{1,0:T(8,128)(2,1)}, bf16[128,256]{1,0:T(8,128)(2,1)S(1)}, u32[]{:S(2)}, u32[]{:S(2)}) collective-permute-start(bf16[128,256]{1,0:T(8,128)(2,1)} %get-tuple-element.37.refs_0_), channel_id=1, source_target_pairs={{0,2},{2,0},{4,6},{6,4},{8,10},{10,8},{12,14},{14,12},{1,3},{3,1},... | collective-permute-start | bytes 196616 | tf_op jit(solution)/shard_map/ppermute | solution.py:631
  34.2 0.0 collective-permute-done.8.refs_12_.refs_15_
  34.2 3.0 %collective-permute-done.6.refs_10_.refs_13_ = bf16[256,256]{1,0:T(8,128)(2,1)S(1)} collective-permute-done((bf16[256,256]{1,0:T(8,128)(2,1)S(1)}, bf16[256,256]{1,0:T(8,128)(2,1)S(1)}, u32[]{:S(2)}, u32[]{:S(2)}) %collective-permute-start.6) | collective-permute-done | bytes 131104 | tf_op jit(solution)/shard_map/ppermute | solution.py:620
  37.3 0.0 collective-permute-done.4.refs_8_.refs_11_
  37.3 0.6 copy-done.20
  37.9 0.0 copy-done.22
  38.0 6.2 %forward.1 = (bf16[1,2048,512]{2,1,0:T(8,128)(2,1)}, f32[8,512]{1,0:T(8,128)}, bf16[128,256]{1,0:T(8,128)(2,1)}, bf16[128,256]{1,0:T(8,128)(2,1)}) custom-call(bf16[128,256]{1,0:T(8,128)(2,1)} %get-tuple-element.37.refs_0_, s32[11]{0:T(128)} %stack.65.refs_0_.refs_1_, bf16[256,256]{1,0:T(8,128)(2,1)} %bitcast.29, bf16[256,128]{1,0:T(8,128)(2,1)} %copy-done.28, ...), custom_call_target="tpu_custom_call" | custom-call | flops 6000000000 | bytes 18000000 | tf_op jit(solution)/shard_map/forward/pallas_call | solution.py:56
  44.2 0.2 collective-permute-start.20
  44.4 1.2 %collective-permute-start.18 = (bf16[128,256]{1,0:T(8,128)(2,1)}, bf16[128,256]{1,0:T(8,128)(2,1)S(1)}, u32[]{:S(2)}, u32[]{:S(2)}) collective-permute-start(bf16[128,256]{1,0:T(8,128)(2,1)} %get-tuple-element.43.refs_6_), channel_id=1, source_target_pairs={{0,2},{2,0},{4,6},{6,4},{8,10},{10,8},{12,14},{14,12},{1,3},{3,1},... | collective-permute-start | bytes 196616 | tf_op jit(solution)/shard_map/ppermute | solution.py:646
  45.6 0.5 collective-permute-start.19
  46.1 0.0 collective-permute-done.2.refs_4_
  46.1 0.6 copy-done.34
  46.7 7.8 %backward.1 = (bf16[256,128]{1,0:T(8,128)(2,1)}, bf16[256,128]{1,0:T(8,128)(2,1)}, bf16[256,256]{1,0:T(8,128)(2,1)}, bf16[256,256]{1,0:T(8,128)(2,1)}, bf16[256,...) custom-call(s32[11]{0:T(128)} %stack.65.refs_0_.refs_1_, ...), custom_call_target="tpu_custom_call" | custom-call | flops 8000000000 | bytes 24000000 | tf_op jit(solution)/shard_map/backward/pallas_call | solution.py:56
  54.6 0.0 collective-permute-done.20.refs_5_
  54.6 0.0 copy-start.30
  54.6 0.0 copy-start.31
  54.6 0.0 collective-permute-done.19.refs_4_
  54.6 0.0 copy-start.32
  54.7 0.6 copy-done.30
  55.2 0.0 copy-done.31
  55.3 0.0 copy-done.32
  55.3 0.4 copy-done.3
  55.7 4.1 %weight_sent.1.refs_0_ = bf16[4,256,256]{2,1,0:T(8,128)(2,1)} custom-call(bf16[256,128]{1,0:T(8,128)(2,1)} %get-tuple-element.46.refs_1_.refs_0_, s32[3]{0:T(128)} %pad_add_fusion.1.refs_1_, bf16[128,256]{1,0:T(8,128)(2,1)} %get-tuple-element.42.refs_5_.refs_2_, bf16[128,256]{1,0:T(8,128)(2,1)} %copy-done.31, bf16[128,256]{1,0:T(8,128)(2,1)} %copy-done.32, ...), custom_call_target="tpu_custom_call" | custom-call | flops 3000000000 | bytes 9000000 | tf_op jit(solution)/shard_map/weight_sent/pallas_call | solution.py:56
  59.8 1.3 %collective-permute-start.22 = (bf16[4,256,256]{2,1,0:T(8,128)(2,1)}, bf16[4,256,256]{2,1,0:T(8,128)(2,1)S(1)}, u32[]{:S(2)}, u32[]{:S(2)}) collective-permute-start(bf16[4,256,256]{2,1,0:T(8,128)(2,1)} %weight_sent.1.refs_0_), channel_id=1, source_target_pairs={{0,2},{2,0},{4,6},{6,4},{8,10},{10,8},{12,14},{14,12},{1,3},{3,1},... | collective-permute-start | bytes 1572872 | tf_op jit(solution)/shard_map/ppermute | solution.py:652
  61.1 0.8 collective-permute-start.10
  61.9 1.3 %collective-permute-start.11 = (bf16[256,256]{1,0:T(8,128)(2,1)S(1)}, bf16[256,256]{1,0:T(8,128)(2,1)S(1)}, u32[]{:S(2)}, u32[]{:S(2)}) collective-permute-start(bf16[256,256]{1,0:T(8,128)(2,1)S(1)} %copy-done.24), channel_id=1, source_target_pairs={{0,2},{2,0},{4,6},{6,4},{8,10},{10,8},{12,14},{14,12},{1,3},{3,1},... | collective-permute-start | bytes 393224 | tf_op jit(solution)/shard_map/ppermute | solution.py:654
  63.1 1.5 %collective-permute-start.12 = (bf16[256,256]{1,0:T(8,128)(2,1)S(1)}, bf16[256,256]{1,0:T(8,128)(2,1)S(1)}, u32[]{:S(2)}, u32[]{:S(2)}) collective-permute-start(bf16[256,256]{1,0:T(8,128)(2,1)S(1)} %copy-done.21), channel_id=1, source_target_pairs={{0,12},{2,14},{4,0},{6,2},{8,4},{10,6},{12,8},{14,10},{1,13},{3,15... | collective-permute-start | bytes 393224 | tf_op jit(solution)/shard_map/ppermute | solution.py:654
  64.7 2.7 %collective-permute-start.13 = (bf16[256,256]{1,0:T(8,128)(2,1)S(1)}, bf16[256,256]{1,0:T(8,128)(2,1)S(1)}, u32[]{:S(2)}, u32[]{:S(2)}) collective-permute-start(bf16[256,256]{1,0:T(8,128)(2,1)S(1)} %copy-done.14), channel_id=1, source_target_pairs={{0,14},{2,12},{4,2},{6,0},{8,6},{10,4},{12,10},{14,8},{1,15},{3,13... | collective-permute-start | bytes 393224 | tf_op jit(solution)/shard_map/ppermute | solution.py:654
  67.4 3.9 %weight_kept.1.refs_0_ = bf16[4,256,256]{2,1,0:T(8,128)(2,1)} custom-call(bf16[4,256,256]{2,1,0:T(8,128)(2,1)} %weight_sent.1.refs_0_, s32[3]{0:T(128)} %pad_add_fusion.1.refs_1_, bf16[128,256]{1,0:T(8,128)(2,1)} %get-tuple-element.42.refs_5_.refs_2_, bf16[128,256]{1,0:T(8,128)(2,1)} %copy-done.31, bf16[128,256]{1,0:T(8,128)(2,1)} %copy-done.32, ...), custom_call_target="tpu_custom_call" | custom-call | flops 3000000000 | bytes 9000000 | tf_op jit(solution)/shard_map/weight_kept/pallas_call | solution.py:56
  71.3 7.8 %collective-permute-done.10.refs_2_ = bf16[256,128]{1,0:T(8,128)(2,1)S(1)} collective-permute-done((bf16[256,128]{1,0:T(8,128)(2,1)S(1)}, bf16[256,128]{1,0:T(8,128)(2,1)S(1)}, u32[]{:S(2)}, u32[]{:S(2)}) %collective-permute-start.10) | collective-permute-done | bytes 65568 | tf_op jit(solution)/shard_map/ppermute | solution.py:657
  79.0 2.5 %collective-permute-start.14 = (bf16[256,256]{1,0:T(8,128)(2,1)S(1)}, bf16[256,256]{1,0:T(8,128)(2,1)S(1)}, u32[]{:S(2)}, u32[]{:S(2)}) collective-permute-start(bf16[256,256]{1,0:T(8,128)(2,1)S(1)} %copy-done.13), channel_id=1, source_target_pairs={{0,8},{2,10},{4,12},{6,14},{8,0},{10,2},{12,4},{14,6},{1,9},{3,11}... | collective-permute-start | bytes 393224 | tf_op jit(solution)/shard_map/ppermute | solution.py:654
  81.6 2.6 %collective-permute-start.15 = (bf16[256,256]{1,0:T(8,128)(2,1)S(1)}, bf16[256,256]{1,0:T(8,128)(2,1)S(1)}, u32[]{:S(2)}, u32[]{:S(2)}) collective-permute-start(bf16[256,256]{1,0:T(8,128)(2,1)S(1)} %copy-done.12), channel_id=1, source_target_pairs={{0,10},{2,8},{4,14},{6,12},{8,2},{10,0},{12,6},{14,4},{1,11},{3,9}... | collective-permute-start | bytes 393224 | tf_op jit(solution)/shard_map/ppermute | solution.py:654
  84.1 0.1 collective-permute-start.16
  84.2 0.0 collective-permute-done.22.refs_1_
  84.2 1.9 %collective-permute-start.17 = (bf16[256,256]{1,0:T(8,128)(2,1)S(1)}, bf16[256,256]{1,0:T(8,128)(2,1)S(1)}, u32[]{:S(2)}, u32[]{:S(2)}) collective-permute-start(bf16[256,256]{1,0:T(8,128)(2,1)S(1)} %copy-done.10), channel_id=1, source_target_pairs={{0,6},{2,4},{4,10},{6,8},{8,14},{10,12},{12,2},{14,0},{1,7},{3,5},... | collective-permute-start | bytes 393224 | tf_op jit(solution)/shard_map/ppermute | solution.py:654
  86.1 2.1 %weight_add.1 = (bf16[256,256]{1,0:T(8,128)(2,1)}, bf16[256,256]{1,0:T(8,128)(2,1)}, bf16[256,256]{1,0:T(8,128)(2,1)}, bf16[256,256]{1,0:T(8,128)(2,1)}) custom-call(bf16[4,256,256]{2,1,0:T(8,128)(2,1)} %weight_kept.1.refs_0_, bf16[4,256,256]{2,1,0:T(8,128)(2,1)} %copy-done.4), custom_call_target="tpu_custom_call" | custom-call | flops 1500000000 | bytes 4500000 | tf_op jit(solution)/shard_map/weight_add/pallas_call | solution.py:56
  88.2 0.0 collective-permute-done.13.refs_6_
  88.2 0.6 collective-permute-start.23
  88.8 12.9 %collective-permute-done.14.refs_7_ = bf16[256,256]{1,0:T(8,128)(2,1)S(1)} collective-permute-done((bf16[256,256]{1,0:T(8,128)(2,1)S(1)}, bf16[256,256]{1,0:T(8,128)(2,1)S(1)}, u32[]{:S(2)}, u32[]{:S(2)}) %collective-permute-start.14) | collective-permute-done | bytes 131104 | tf_op jit(solution)/shard_map/ppermute | solution.py:654
  101.8 3.5 %collective-permute-done.15.refs_8_ = bf16[256,256]{1,0:T(8,128)(2,1)S(1)} collective-permute-done((bf16[256,256]{1,0:T(8,128)(2,1)S(1)}, bf16[256,256]{1,0:T(8,128)(2,1)S(1)}, u32[]{:S(2)}, u32[]{:S(2)}) %collective-permute-start.15) | collective-permute-done | bytes 131104 | tf_op jit(solution)/shard_map/ppermute | solution.py:654
  105.4 0.6 copy-done.25
  106.0 0.1 copy-done.26
  106.0 0.1 copy-done.27
  106.1 3.1 %collect.1 = (bf16[256,256]{1,0:T(8,128)(2,1)}, bf16[256,256]{1,0:T(8,128)(2,1)}, bf16[256,256]{1,0:T(8,128)(2,1)}) custom-call(s32[11]{0:T(128)} %stack.65.refs_0_.refs_1_, bf16[256,128]{1,0:T(8,128)(2,1)} %get-tuple-element.46.refs_1_.refs_0_, bf16[256,128]{1,0:T(8,128)(2,1)} %copy-done.29, bf16[256,256]{1,0:T(8,128)(2,1)} %get-tuple-element.48.refs_3_, ...), custom_call_target="tpu_custom_call" | custom-call | flops 2000000000 | bytes 6000000 | tf_op jit(solution)/shard_map/collect/pallas_call | solution.py:56
  109.2 1.3 %collective-permute-done.25 = bf16[256,256]{1,0:T(8,128)(2,1)S(1)} collective-permute-done((bf16[256,256]{1,0:T(8,128)(2,1)}, bf16[256,256]{1,0:T(8,128)(2,1)S(1)}, u32[]{:S(2)}, u32[]{:S(2)}) %collective-permute-start.25) | collective-permute-done | bytes 131104 | tf_op jit(solution)/shard_map/ppermute | solution.py:662
  110.5 0.7 add_convert_fusion
  (72 shorter events, 0.1 us)
Async XLA Ops:
  0.6 26.4 %collective-permute-start.1 = (bf16[256,2048]{1,0:T(8,128)(2,1)}, bf16[256,2048]{1,0:T(8,128)(2,1)S(1)}, u32[]{:S(2)}, u32[]{:S(2)}) collective-permute-start(bf16[256,2048]{1,0:T(8,128)(2,1)} %bitcast.21), channel_id=1, source_target_pairs={{0,1},{1,0},{2,3},{3,2},{4,5},{5,4},{6,7},{7,6},{8,9},{9,8},{10,11... | collective-permute-start | bytes 3145736 | tf_op jit(solution)/shard_map/ppermute | solution.py:616
  4.3 9.6 %copy-start.1 = (s32[8,3]{0,1:T(4,128)S(1)}, s32[8,3]{0,1:T(4,128)}, u32[]{:S(2)}) copy-start(s32[8,3]{0,1:T(4,128)} %param.12) | copy-start | bytes 292
  6.8 15.0 %collective-permute-start.9 = (bf16[256,256]{1,0:T(8,128)(2,1)}, bf16[256,256]{1,0:T(8,128)(2,1)S(1)}, u32[]{:S(2)}, u32[]{:S(2)}) collective-permute-start(bf16[256,256]{1,0:T(8,128)(2,1)} %get-tuple-element.41), channel_id=1, source_target_pairs={{0,14},{2,12},{4,2},{6,0},{8,6},{10,4},{12,10},{14,8},{1,15},{3,13... | collective-permute-start | bytes 393224 | tf_op jit(solution)/shard_map/ppermute | solution.py:620
  11.4 14.8 %collective-permute-start.7 = (bf16[256,256]{1,0:T(8,128)(2,1)}, bf16[256,256]{1,0:T(8,128)(2,1)S(1)}, u32[]{:S(2)}, u32[]{:S(2)}) collective-permute-start(bf16[256,256]{1,0:T(8,128)(2,1)} %get-tuple-element.41), channel_id=1, source_target_pairs={{0,10},{2,8},{4,14},{6,12},{8,2},{10,0},{12,6},{14,4},{1,11},{3,9}... | collective-permute-start | bytes 393224 | tf_op jit(solution)/shard_map/ppermute | solution.py:620
  11.4 21.2 %collective-permute-start.5 = (bf16[256,256]{1,0:T(8,128)(2,1)}, bf16[256,256]{1,0:T(8,128)(2,1)S(1)}, u32[]{:S(2)}, u32[]{:S(2)}) collective-permute-start(bf16[256,256]{1,0:T(8,128)(2,1)} %get-tuple-element.41), channel_id=1, source_target_pairs={{0,6},{2,4},{4,10},{6,8},{8,14},{10,12},{12,2},{14,0},{1,7},{3,5},... | collective-permute-start | bytes 393224 | tf_op jit(solution)/shard_map/ppermute | solution.py:620
  13.3 7.0 %collective-permute-start = (bf16[256,128]{1,0:T(8,128)(2,1)}, bf16[256,128]{1,0:T(8,128)(2,1)S(1)}, u32[]{:S(2)}, u32[]{:S(2)}) collective-permute-start(bf16[256,128]{1,0:T(8,128)(2,1)} %get-tuple-element.34), channel_id=1, source_target_pairs={{0,2},{2,0},{4,6},{6,4},{8,10},{10,8},{12,14},{14,12},{1,3},{3,1},... | collective-permute-start | bytes 196616 | tf_op jit(solution)/shard_map/ppermute | solution.py:625
  14.5 5.7 %copy-start.9 = (bf16[256,256]{1,0:T(8,128)(2,1)S(1)}, bf16[256,256]{1,0:T(8,128)(2,1)}, u32[]{:S(2)}) copy-start(bf16[256,256]{1,0:T(8,128)(2,1)} %get-tuple-element.41) | copy-start | bytes 393220
  14.5 7.3 %copy-start.5 = (bf16[256,256]{1,0:T(8,128)(2,1)S(1)}, bf16[256,256]{1,0:T(8,128)(2,1)}, u32[]{:S(2)}) copy-start(bf16[256,256]{1,0:T(8,128)(2,1)} %get-tuple-element.40.refs_6_.refs_9_) | copy-start | bytes 393220
  20.3 17.0 %copy-start.28 = (bf16[256,128]{1,0:T(8,128)(2,1)}, bf16[256,128]{1,0:T(8,128)(2,1)S(1)}, u32[]{:S(2)}) copy-start(bf16[256,128]{1,0:T(8,128)(2,1)S(1)} %collective-permute-done.refs_3_.refs_2_) | copy-start | bytes 196612
  20.3 13.9 %collective-permute-start.3 = (bf16[256,256]{1,0:T(8,128)(2,1)S(1)}, bf16[256,256]{1,0:T(8,128)(2,1)S(1)}, u32[]{:S(2)}, u32[]{:S(2)}) collective-permute-start(bf16[256,256]{1,0:T(8,128)(2,1)S(1)} %copy-done.9), channel_id=1, source_target_pairs={{0,2},{2,0},{4,6},{6,4},{8,10},{10,8},{12,14},{14,12},{1,3},{3,1},... | collective-permute-start | bytes 393224 | tf_op jit(solution)/shard_map/ppermute | solution.py:620
  21.8 15.5 %copy-start.6 = (bf16[256,256]{1,0:T(8,128)(2,1)}, bf16[256,256]{1,0:T(8,128)(2,1)S(1)}, u32[]{:S(2)}) copy-start(bf16[256,256]{1,0:T(8,128)(2,1)S(1)} %collective-permute-done.9.refs_13_.refs_16_) | copy-start | bytes 393220
  21.8 12.4 %collective-permute-start.8 = (bf16[256,256]{1,0:T(8,128)(2,1)S(1)}, bf16[256,256]{1,0:T(8,128)(2,1)S(1)}, u32[]{:S(2)}, u32[]{:S(2)}) collective-permute-start(bf16[256,256]{1,0:T(8,128)(2,1)S(1)} %copy-done.5), channel_id=1, source_target_pairs={{0,12},{2,14},{4,0},{6,2},{8,4},{10,6},{12,8},{14,10},{1,13},{3,15... | collective-permute-start | bytes 393224 | tf_op jit(solution)/shard_map/ppermute | solution.py:620
  26.1 11.2 %copy-start.7 = (bf16[256,256]{1,0:T(8,128)(2,1)}, bf16[256,256]{1,0:T(8,128)(2,1)S(1)}, u32[]{:S(2)}) copy-start(bf16[256,256]{1,0:T(8,128)(2,1)S(1)} %collective-permute-done.7.refs_11_.refs_14_) | copy-start | bytes 393220
  26.1 11.1 %collective-permute-start.6 = (bf16[256,256]{1,0:T(8,128)(2,1)S(1)}, bf16[256,256]{1,0:T(8,128)(2,1)S(1)}, u32[]{:S(2)}, u32[]{:S(2)}) collective-permute-start(bf16[256,256]{1,0:T(8,128)(2,1)S(1)} %copy-done.5), channel_id=1, source_target_pairs={{0,8},{2,10},{4,12},{6,14},{8,0},{10,2},{12,4},{14,6},{1,9},{3,11}... | collective-permute-start | bytes 393224 | tf_op jit(solution)/shard_map/ppermute | solution.py:620
  27.0 1.8 %copy-start.2 = (bf16[256,2048]{1,0:T(8,128)(2,1)}, bf16[256,2048]{1,0:T(8,128)(2,1)S(1)}, u32[]{:S(2)}) copy-start(bf16[256,2048]{1,0:T(8,128)(2,1)S(1)} %collective-permute-done.1.refs_4_.refs_7_) | copy-start | bytes 3145732
  27.0 10.2 %collective-permute-start.4 = (bf16[256,256]{1,0:T(8,128)(2,1)S(1)}, bf16[256,256]{1,0:T(8,128)(2,1)S(1)}, u32[]{:S(2)}, u32[]{:S(2)}) collective-permute-start(bf16[256,256]{1,0:T(8,128)(2,1)S(1)} %copy-done.5), channel_id=1, source_target_pairs={{0,4},{2,6},{4,8},{6,10},{8,12},{10,14},{12,0},{14,2},{1,5},{3,7},... | collective-permute-start | bytes 393224 | tf_op jit(solution)/shard_map/ppermute | solution.py:620
  32.6 4.7 %copy-start.8 = (bf16[256,256]{1,0:T(8,128)(2,1)}, bf16[256,256]{1,0:T(8,128)(2,1)S(1)}, u32[]{:S(2)}) copy-start(bf16[256,256]{1,0:T(8,128)(2,1)S(1)} %collective-permute-done.5.refs_9_.refs_12_) | copy-start | bytes 393220
  32.6 13.5 %collective-permute-start.2 = (bf16[128,256]{1,0:T(8,128)(2,1)}, bf16[128,256]{1,0:T(8,128)(2,1)S(1)}, u32[]{:S(2)}, u32[]{:S(2)}) collective-permute-start(bf16[128,256]{1,0:T(8,128)(2,1)} %get-tuple-element.37.refs_0_), channel_id=1, source_target_pairs={{0,2},{2,0},{4,6},{6,4},{8,10},{10,8},{12,14},{14,12},{1,3},{3,1},... | collective-permute-start | bytes 196616 | tf_op jit(solution)/shard_map/ppermute | solution.py:631
  34.2 3.1 %copy-start.16 = (bf16[256,256]{1,0:T(8,128)(2,1)}, bf16[256,256]{1,0:T(8,128)(2,1)S(1)}, u32[]{:S(2)}) copy-start(bf16[256,256]{1,0:T(8,128)(2,1)S(1)} %collective-permute-done.3.refs_7_.refs_10_) | copy-start | bytes 393220
  34.2 20.5 %collective-permute-start.21 = (bf16[256,2048]{1,0:T(8,128)(2,1)}, bf16[256,2048]{1,0:T(8,128)(2,1)S(1)}, u32[]{:S(2)}, u32[]{:S(2)}) collective-permute-start(bf16[256,2048]{1,0:T(8,128)(2,1)} %get-tuple-element.59), channel_id=1, source_target_pairs={{0,16},{16,0},{1,17},{17,1},{2,18},{18,2},{3,19},{19,3},{4,20},{20... | collective-permute-start | bytes 3145736 | tf_op jit(solution)/shard_map/ppermute | solution.py:633
  34.2 3.1 %copy-start.19 = (bf16[256,256]{1,0:T(8,128)(2,1)}, bf16[256,256]{1,0:T(8,128)(2,1)S(1)}, u32[]{:S(2)}) copy-start(bf16[256,256]{1,0:T(8,128)(2,1)S(1)} %collective-permute-done.8.refs_12_.refs_15_) | copy-start | bytes 393220
  37.3 0.7 copy-start.20
  37.3 0.7 copy-start.22
  44.2 10.4 %collective-permute-start.20 = (bf16[128,256]{1,0:T(8,128)(2,1)}, bf16[128,256]{1,0:T(8,128)(2,1)S(1)}, u32[]{:S(2)}, u32[]{:S(2)}) collective-permute-start(bf16[128,256]{1,0:T(8,128)(2,1)} %get-tuple-element.43.refs_6_), channel_id=1, source_target_pairs={{0,18},{2,16},{4,22},{6,20},{8,26},{10,24},{12,30},{14,28},{16,2},... | collective-permute-start | bytes 196616 | tf_op jit(solution)/shard_map/ppermute | solution.py:646
  44.4 10.2 %collective-permute-start.18 = (bf16[128,256]{1,0:T(8,128)(2,1)}, bf16[128,256]{1,0:T(8,128)(2,1)S(1)}, u32[]{:S(2)}, u32[]{:S(2)}) collective-permute-start(bf16[128,256]{1,0:T(8,128)(2,1)} %get-tuple-element.43.refs_6_), channel_id=1, source_target_pairs={{0,2},{2,0},{4,6},{6,4},{8,10},{10,8},{12,14},{14,12},{1,3},{3,1},... | collective-permute-start | bytes 196616 | tf_op jit(solution)/shard_map/ppermute | solution.py:646
  45.6 9.0 %collective-permute-start.19 = (bf16[128,256]{1,0:T(8,128)(2,1)}, bf16[128,256]{1,0:T(8,128)(2,1)S(1)}, u32[]{:S(2)}, u32[]{:S(2)}) collective-permute-start(bf16[128,256]{1,0:T(8,128)(2,1)} %get-tuple-element.42.refs_5_.refs_2_), channel_id=1, source_target_pairs={{0,16},{2,18},{4,20},{6,22},{8,24},{10,26},{12,28},{14,30},{16,0},... | collective-permute-start | bytes 196616 | tf_op jit(solution)/shard_map/ppermute | solution.py:646
  46.1 0.6 copy-start.34
  54.6 0.6 copy-start.30
  54.6 0.6 copy-start.31
  54.6 0.6 copy-start.32
  54.7 1.0 copy-start.3
  55.7 5.4 %copy-start.33 = (bf16[256,128]{1,0:T(8,128)(2,1)S(1)}, bf16[256,128]{1,0:T(8,128)(2,1)}, u32[]{:S(2)}) copy-start(bf16[256,128]{1,0:T(8,128)(2,1)} %get-tuple-element.47) | copy-start | bytes 196612
  55.7 6.2 %copy-start.24 = (bf16[256,256]{1,0:T(8,128)(2,1)S(1)}, bf16[256,256]{1,0:T(8,128)(2,1)}, u32[]{:S(2)}) copy-start(bf16[256,256]{1,0:T(8,128)(2,1)} %get-tuple-element.49) | copy-start | bytes 393220
  55.7 7.4 %copy-start.21 = (bf16[256,256]{1,0:T(8,128)(2,1)S(1)}, bf16[256,256]{1,0:T(8,128)(2,1)}, u32[]{:S(2)}) copy-start(bf16[256,256]{1,0:T(8,128)(2,1)} %get-tuple-element.50) | copy-start | bytes 393220
  55.7 9.0 %copy-start.14 = (bf16[256,256]{1,0:T(8,128)(2,1)S(1)}, bf16[256,256]{1,0:T(8,128)(2,1)}, u32[]{:S(2)}) copy-start(bf16[256,256]{1,0:T(8,128)(2,1)} %get-tuple-element.51) | copy-start | bytes 393220
  59.8 24.4 %collective-permute-start.22 = (bf16[4,256,256]{2,1,0:T(8,128)(2,1)}, bf16[4,256,256]{2,1,0:T(8,128)(2,1)S(1)}, u32[]{:S(2)}, u32[]{:S(2)}) collective-permute-start(bf16[4,256,256]{2,1,0:T(8,128)(2,1)} %weight_sent.1.refs_0_), channel_id=1, source_target_pairs={{0,2},{2,0},{4,6},{6,4},{8,10},{10,8},{12,14},{14,12},{1,3},{3,1},... | collective-permute-start | bytes 1572872 | tf_op jit(solution)/shard_map/ppermute | solution.py:652
  61.1 17.9 %collective-permute-start.10 = (bf16[256,128]{1,0:T(8,128)(2,1)S(1)}, bf16[256,128]{1,0:T(8,128)(2,1)S(1)}, u32[]{:S(2)}, u32[]{:S(2)}) collective-permute-start(bf16[256,128]{1,0:T(8,128)(2,1)S(1)} %copy-done.33), channel_id=1, source_target_pairs={{0,2},{2,0},{4,6},{6,4},{8,10},{10,8},{12,14},{14,12},{1,3},{3,1},... | collective-permute-start | bytes 196616 | tf_op jit(solution)/shard_map/ppermute | solution.py:657
  61.9 19.7 %collective-permute-start.11 = (bf16[256,256]{1,0:T(8,128)(2,1)S(1)}, bf16[256,256]{1,0:T(8,128)(2,1)S(1)}, u32[]{:S(2)}, u32[]{:S(2)}) collective-permute-start(bf16[256,256]{1,0:T(8,128)(2,1)S(1)} %copy-done.24), channel_id=1, source_target_pairs={{0,2},{2,0},{4,6},{6,4},{8,10},{10,8},{12,14},{14,12},{1,3},{3,1},... | collective-permute-start | bytes 393224 | tf_op jit(solution)/shard_map/ppermute | solution.py:654
  63.1 21.0 %collective-permute-start.12 = (bf16[256,256]{1,0:T(8,128)(2,1)S(1)}, bf16[256,256]{1,0:T(8,128)(2,1)S(1)}, u32[]{:S(2)}, u32[]{:S(2)}) collective-permute-start(bf16[256,256]{1,0:T(8,128)(2,1)S(1)} %copy-done.21), channel_id=1, source_target_pairs={{0,12},{2,14},{4,0},{6,2},{8,4},{10,6},{12,8},{14,10},{1,13},{3,15... | collective-permute-start | bytes 393224 | tf_op jit(solution)/shard_map/ppermute | solution.py:654
  64.7 14.4 %copy-start.13 = (bf16[256,256]{1,0:T(8,128)(2,1)S(1)}, bf16[256,256]{1,0:T(8,128)(2,1)}, u32[]{:S(2)}) copy-start(bf16[256,256]{1,0:T(8,128)(2,1)} %get-tuple-element.52) | copy-start | bytes 393220
  64.7 16.9 %copy-start.12 = (bf16[256,256]{1,0:T(8,128)(2,1)S(1)}, bf16[256,256]{1,0:T(8,128)(2,1)}, u32[]{:S(2)}) copy-start(bf16[256,256]{1,0:T(8,128)(2,1)} %get-tuple-element.53) | copy-start | bytes 393220
  64.7 19.4 %copy-start.11 = (bf16[256,256]{1,0:T(8,128)(2,1)S(1)}, bf16[256,256]{1,0:T(8,128)(2,1)}, u32[]{:S(2)}) copy-start(bf16[256,256]{1,0:T(8,128)(2,1)} %get-tuple-element.54) | copy-start | bytes 393220
  64.7 19.5 %copy-start.10 = (bf16[256,256]{1,0:T(8,128)(2,1)S(1)}, bf16[256,256]{1,0:T(8,128)(2,1)}, u32[]{:S(2)}) copy-start(bf16[256,256]{1,0:T(8,128)(2,1)} %get-tuple-element.55) | copy-start | bytes 393220
  64.7 23.5 %collective-permute-start.13 = (bf16[256,256]{1,0:T(8,128)(2,1)S(1)}, bf16[256,256]{1,0:T(8,128)(2,1)S(1)}, u32[]{:S(2)}, u32[]{:S(2)}) collective-permute-start(bf16[256,256]{1,0:T(8,128)(2,1)S(1)} %copy-done.14), channel_id=1, source_target_pairs={{0,14},{2,12},{4,2},{6,0},{8,6},{10,4},{12,10},{14,8},{1,15},{3,13... | collective-permute-start | bytes 393224 | tf_op jit(solution)/shard_map/ppermute | solution.py:654
  79.0 26.3 %copy-start.29 = (bf16[256,128]{1,0:T(8,128)(2,1)}, bf16[256,128]{1,0:T(8,128)(2,1)S(1)}, u32[]{:S(2)}) copy-start(bf16[256,128]{1,0:T(8,128)(2,1)S(1)} %collective-permute-done.10.refs_2_) | copy-start | bytes 196612
  79.0 22.7 %collective-permute-start.14 = (bf16[256,256]{1,0:T(8,128)(2,1)S(1)}, bf16[256,256]{1,0:T(8,128)(2,1)S(1)}, u32[]{:S(2)}, u32[]{:S(2)}) collective-permute-start(bf16[256,256]{1,0:T(8,128)(2,1)S(1)} %copy-done.13), channel_id=1, source_target_pairs={{0,8},{2,10},{4,12},{6,14},{8,0},{10,2},{12,4},{14,6},{1,9},{3,11}... | collective-permute-start | bytes 393224 | tf_op jit(solution)/shard_map/ppermute | solution.py:654
  81.5 23.8 %copy-start.15 = (bf16[256,256]{1,0:T(8,128)(2,1)}, bf16[256,256]{1,0:T(8,128)(2,1)S(1)}, u32[]{:S(2)}) copy-start(bf16[256,256]{1,0:T(8,128)(2,1)S(1)} %collective-permute-done.11.refs_4_) | copy-start | bytes 393220
  81.6 23.7 %collective-permute-start.15 = (bf16[256,256]{1,0:T(8,128)(2,1)S(1)}, bf16[256,256]{1,0:T(8,128)(2,1)S(1)}, u32[]{:S(2)}, u32[]{:S(2)}) collective-permute-start(bf16[256,256]{1,0:T(8,128)(2,1)S(1)} %copy-done.12), channel_id=1, source_target_pairs={{0,10},{2,8},{4,14},{6,12},{8,2},{10,0},{12,6},{14,4},{1,11},{3,9}... | collective-permute-start | bytes 393224 | tf_op jit(solution)/shard_map/ppermute | solution.py:654
  84.1 21.3 %copy-start.17 = (bf16[256,256]{1,0:T(8,128)(2,1)}, bf16[256,256]{1,0:T(8,128)(2,1)S(1)}, u32[]{:S(2)}) copy-start(bf16[256,256]{1,0:T(8,128)(2,1)S(1)} %collective-permute-done.12.refs_5_) | copy-start | bytes 393220
  84.1 21.2 %collective-permute-start.16 = (bf16[256,256]{1,0:T(8,128)(2,1)S(1)}, bf16[256,256]{1,0:T(8,128)(2,1)S(1)}, u32[]{:S(2)}, u32[]{:S(2)}) collective-permute-start(bf16[256,256]{1,0:T(8,128)(2,1)S(1)} %copy-done.11), channel_id=1, source_target_pairs={{0,4},{2,6},{4,8},{6,10},{8,12},{10,14},{12,0},{14,2},{1,5},{3,7},... | collective-permute-start | bytes 393224 | tf_op jit(solution)/shard_map/ppermute | solution.py:654
  84.2 1.9 %copy-start.4 = (bf16[4,256,256]{2,1,0:T(8,128)(2,1)}, bf16[4,256,256]{2,1,0:T(8,128)(2,1)S(1)}, u32[]{:S(2)}) copy-start(bf16[4,256,256]{2,1,0:T(8,128)(2,1)S(1)} %collective-permute-done.22.refs_1_) | copy-start | bytes 1572868
  84.2 21.1 %collective-permute-start.17 = (bf16[256,256]{1,0:T(8,128)(2,1)S(1)}, bf16[256,256]{1,0:T(8,128)(2,1)S(1)}, u32[]{:S(2)}, u32[]{:S(2)}) collective-permute-start(bf16[256,256]{1,0:T(8,128)(2,1)S(1)} %copy-done.10), channel_id=1, source_target_pairs={{0,6},{2,4},{4,10},{6,8},{8,14},{10,12},{12,2},{14,0},{1,7},{3,5},... | collective-permute-start | bytes 393224 | tf_op jit(solution)/shard_map/ppermute | solution.py:654
  88.2 17.2 %copy-start.18 = (bf16[256,256]{1,0:T(8,128)(2,1)}, bf16[256,256]{1,0:T(8,128)(2,1)S(1)}, u32[]{:S(2)}) copy-start(bf16[256,256]{1,0:T(8,128)(2,1)S(1)} %collective-permute-done.13.refs_6_) | copy-start | bytes 393220
  88.2 21.0 %collective-permute-start.23 = (bf16[256,256]{1,0:T(8,128)(2,1)}, bf16[256,256]{1,0:T(8,128)(2,1)S(1)}, u32[]{:S(2)}, u32[]{:S(2)}) collective-permute-start(bf16[256,256]{1,0:T(8,128)(2,1)} %get-tuple-element.61), channel_id=1, source_target_pairs={{0,4},{2,6},{4,8},{6,10},{8,12},{10,14},{12,0},{14,2},{1,5},{3,7},... | collective-permute-start | bytes 393224 | tf_op jit(solution)/shard_map/ppermute | solution.py:662
  101.8 3.6 %copy-start.23 = (bf16[256,256]{1,0:T(8,128)(2,1)}, bf16[256,256]{1,0:T(8,128)(2,1)S(1)}, u32[]{:S(2)}) copy-start(bf16[256,256]{1,0:T(8,128)(2,1)S(1)} %collective-permute-done.14.refs_7_) | copy-start | bytes 393220
  101.8 7.4 %collective-permute-start.24 = (bf16[256,256]{1,0:T(8,128)(2,1)}, bf16[256,256]{1,0:T(8,128)(2,1)S(1)}, u32[]{:S(2)}, u32[]{:S(2)}) collective-permute-start(bf16[256,256]{1,0:T(8,128)(2,1)} %get-tuple-element.62), channel_id=1, source_target_pairs={{0,8},{2,10},{4,12},{6,14},{8,0},{10,2},{12,4},{14,6},{1,9},{3,11}... | collective-permute-start | bytes 393224 | tf_op jit(solution)/shard_map/ppermute | solution.py:662
  105.3 0.7 copy-start.25
  105.3 5.2 %collective-permute-start.25 = (bf16[256,256]{1,0:T(8,128)(2,1)}, bf16[256,256]{1,0:T(8,128)(2,1)S(1)}, u32[]{:S(2)}, u32[]{:S(2)}) collective-permute-start(bf16[256,256]{1,0:T(8,128)(2,1)} %get-tuple-element.63), channel_id=1, source_target_pairs={{0,12},{2,14},{4,0},{6,2},{8,4},{10,6},{12,8},{14,10},{1,13},{3,15... | collective-permute-start | bytes 393224 | tf_op jit(solution)/shard_map/ppermute | solution.py:662
  105.3 0.7 copy-start.26
  105.3 0.7 copy-start.27
  106.1 4.4 %copy-start = (bf16[256,256]{1,0:T(8,128)(2,1)S(1)}, bf16[256,256]{1,0:T(8,128)(2,1)}, u32[]{:S(2)}) copy-start(bf16[256,256]{1,0:T(8,128)(2,1)} %get-tuple-element.60) | copy-start | bytes 393220

commit v6 on v5

--- a/solution.py
+++ b/solution.py
@@ -66,9 +66,9 @@
     return pltpu.HBM(shape, jnp.float32)
 
 
-def part_kernel(at_ref, q_ref, k_ref, v_ref, kv_mine, kv_theirs, q_theirs, held_s, in_sem, out_sem):
-    half = q_theirs.shape[1]
-    loads = [begin(held, held_s.at[i], in_sem.at[i]) for i, held in enumerate((k_ref, v_ref, q_ref))]
+def part_kernel(at_ref, k_ref, v_ref, kv_mine, kv_theirs, held_s, in_sem, out_sem):
+    half = kv_mine.shape[1] // 2
+    loads = [begin(held, held_s.at[i], in_sem.at[i]) for i, held in enumerate((k_ref, v_ref))]
     mine = pl.ds(pl.multiple_of(at_ref[0] * half, half), half)
     theirs = pl.ds(pl.multiple_of((1 - at_ref[0]) * half, half), half)
     copies = []
@@ -78,32 +78,33 @@
         for side, (cols, out) in enumerate(((mine, kv_mine), (theirs, kv_theirs))):
             sem = out_sem.at[2 * index + side]
             copies.append(begin(held_s.at[index, :, cols], out.at[:, place], sem))
-    loads[2].wait()
-    copies.append(begin(held_s.at[2, :, theirs], q_theirs, out_sem.at[4]))
     for copy in copies:
         copy.wait()
 
 
-def part_heads(at, queries, keys, values):
-    rows, feats = queries.shape
-    half = feats // INNER
+def part_heads(at, keys, values):
+    rows, feats = keys.shape
     return call(
         part_kernel,
-        [bf16(rows, 2 * half), bf16(rows, 2 * half), bf16(rows, half)],
-        [SMEM] + [ANY] * 3,
-        [ANY] * 3,
-        [
-            pltpu.VMEM((3, rows, feats), jnp.bfloat16),
-            pltpu.SemaphoreType.DMA((3,)),
-            pltpu.SemaphoreType.DMA((5,)),
+        [bf16(rows, feats), bf16(rows, feats)],
+        [SMEM] + [ANY] * 2,
+        [ANY] * 2,
+        [
+            pltpu.VMEM((2, rows, feats), jnp.bfloat16),
+            pltpu.SemaphoreType.DMA((2,)),
+            pltpu.SemaphoreType.DMA((4,)),
         ],
         2,
         "part_heads",
-    )(at, queries, keys, values)
-
-
-def prelude_kernel(at_ref, pattern, offsets, grad_ref, weight_ref, first, key_mask, row_mask, *rest):
-    grad_s, weight_s, first_s, mask_s, row_s, sem, out_sem = rest
+    )(at, keys, values)
+
+
+def prelude_kernel(at_ref, pattern, offsets, q_ref, grad_ref, weight_ref, *refs):
+    first, key_mask, row_mask, q_theirs = refs[:4]
+    grad_s, weight_s, first_s, mask_s, row_s, q_s, sem, out_sem = refs[4:]
+    half = q_theirs.shape[1]
+    theirs = pl.ds(pl.multiple_of((1 - at_ref[0]) * half, half), half)
+    q_load = begin(q_ref.at[:, theirs], q_s, sem.at[2])
     rows, width = grad_s.shape
     block_count, glob_count = offsets.shape
     start = pl.multiple_of(at_ref[2] * width, width)
@@ -111,6 +112,8 @@
         begin(grad_ref, grad_s, sem.at[0]),
         begin(weight_ref.at[:, pl.ds(start, width)], weight_s, sem.at[1]),
     ]
+    q_load.wait()
+    stores = [begin(q_s, q_theirs, out_sem.at[3])]
     own = at_ref[1] * INNER + at_ref[0]
     partner = at_ref[1] * INNER + 1 - at_ref[0]
     lane = lax.broadcasted_iota(jnp.int32, (1, HD), 1)
@@ -137,7 +140,8 @@
         for r in range(glob_count):
             local = jnp.where(col_at == offsets[target, r], 0.0, local)
         row_s[:, group * rows : (group + 1) * rows] = local
-    stores = [begin(mask_s, key_mask, out_sem.at[0]), begin(row_s, row_mask, out_sem.at[1])]
+    stores.append(begin(mask_s, key_mask, out_sem.at[0]))
+    stores.append(begin(row_s, row_mask, out_sem.at[1]))
     for load in loads:
         load.wait()
     first_s[...] = against(weight_s[...], grad_s[...])
@@ -146,31 +150,35 @@
         store.wait()
 
 
-def prelude(at, pattern, offsets, grad_own, out_weight):
+def prelude(at, pattern, offsets, queries, grad_own, out_weight, after):
     rows, width = grad_own.shape
     feats = out_weight.shape[0]
     keys = offsets.shape[0] * rows
+    half = queries.shape[1] // INNER
     return call(
         prelude_kernel,
         [
-            f32(*(feats, rows)),
+            f32(feats, rows),
             bf16(keys, HD),
-            f32(*(8, 2 * rows)),
-        ],
-        [SMEM] * 3 + [ANY] * 2,
-        [ANY] * 3,
+            f32(8, 2 * rows),
+            bf16(rows, half),
+        ],
+        [SMEM] * 3 + [ANY] * 3,
+        [ANY] * 4,
         [
             pltpu.VMEM((rows, width), jnp.bfloat16),
             pltpu.VMEM((feats, width), jnp.bfloat16),
             pltpu.VMEM((feats, rows), jnp.float32),
             pltpu.VMEM((keys, HD), jnp.bfloat16),
             pltpu.VMEM((8, 2 * rows), jnp.float32),
-            pltpu.SemaphoreType.DMA((2,)),
+            pltpu.VMEM((rows, half), jnp.bfloat16),
             pltpu.SemaphoreType.DMA((3,)),
-        ],
-        3,
+            pltpu.SemaphoreType.DMA((4,)),
+        ],
+        4,
         "prelude",
-    )(at, pattern, offsets, grad_own, out_weight)
+        after,
+    )(at, pattern, offsets, queries, grad_own, out_weight)
 
 
 def forward_kernel(block_count, head_count, at_ref, q_ref, q_recv, key_mask, row_mask, *refs):
@@ -241,7 +249,7 @@
         functools.partial(forward_kernel, block_count, heads),
         [
             bf16(heads, keys, 2 * rows),
-            f32(*(max(heads, 8), 2 * rows)),
+            f32(max(heads, 8), 2 * rows),
             bf16(feats, rows),
             bf16(feats, rows),
         ],
@@ -271,7 +279,8 @@
     q_ref, q_recv, g_mine, g_recv, attn_mine, attn_theirs, inv_ref, e_ref = refs[:8]
     kv_refs, refs = refs[8 : 8 + block_count], refs[8 + block_count :]
     dq_mine, dq_theirs = refs[:2]
-    part_outs, refs = refs[2 : 2 + block_count], refs[2 + block_count :]
+    outer = block_count // INNER
+    part_outs, refs = refs[2 : 2 + outer], refs[2 + outer :]
     q_s, t_s, inv_s, kv_s, e_s, part_s, dq_s, sem, kv_sem, e_sem, part_sem, dq_sem = refs
     rows = q_recv.shape[0]
     feats = head_count * HD
@@ -314,7 +323,7 @@
             part_s[j, :, cols] = (score_scale * product(dscore, query)).astype(jnp.bfloat16)
             part_s[j, :, vcols] = product(low, grad).astype(jnp.bfloat16)
             if head == head_count - 1:
-                stores.append(begin(part_s.at[j], part_outs[j], part_sem.at[j]))
+                stores.append(begin(part_s.at[j], part_outs[j // INNER].at[j % INNER], part_sem.at[j]))
         dquery = (score_scale * jnp.transpose(dq_t)).astype(jnp.bfloat16)
         dq_s[0, :, cols] = dquery[:rows]
         dq_s[1, :, cols] = dquery[rows:]
@@ -331,9 +340,9 @@
     keys = block_count * rows
     out = call(
         functools.partial(backward_kernel, block_count, heads),
-        [bf16(rows, feats)] * 2 + [bf16(rows, 2 * feats)] * block_count,
+        [bf16(rows, feats)] * 2 + [bf16(INNER, rows, 2 * feats)] * (block_count // INNER),
         [SMEM] + [ANY] * (8 + block_count),
-        [ANY] * (2 + block_count),
+        [ANY] * (2 + block_count // INNER),
         [
             pltpu.VMEM((2, rows, feats), jnp.bfloat16),
             pltpu.VMEM((4, feats, rows), jnp.bfloat16),
@@ -530,49 +539,86 @@
     )(keep, recv)
 
 
-def collect_kernel(count, at_ref, dq_mine, dq_recv, *refs):
-    terms, (grad_q, grad_k, grad_v) = refs[:count], refs[count : count + 3]
-    terms_s, dq_s, out_s, term_sem, dq_sem, out_sem = refs[count + 3 :]
-    half = dq_mine.shape[1]
-    dq_loads = [begin(held, dq_s.at[i], dq_sem.at[i]) for i, held in enumerate((dq_mine, dq_recv))]
-    loads = [begin(terms[c], terms_s.at[c], term_sem.at[c]) for c in range(count)]
-    for load in dq_loads + loads:
-        load.wait()
-    for side, at in enumerate((at_ref[0], 1 - at_ref[0])):
-        cols = pl.ds(pl.multiple_of(at * half, half), half)
-        summed = terms_s[side].astype(jnp.float32)
-        for c in range(side + INNER, count, INNER):
-            summed = summed + terms_s[c].astype(jnp.float32)
-        summed = summed.astype(jnp.bfloat16)
-        out_s[0, :, cols] = dq_s[side]
-        out_s[1, :, cols] = summed[:, :half]
-        out_s[2, :, cols] = summed[:, half:]
-    stores = [
-        begin(out_s.at[i], out, out_sem.at[i]) for i, out in enumerate((grad_q, grad_k, grad_v))
-    ]
+def add_kernel(count, *refs):
+    terms, (mine, theirs) = refs[:count], refs[count : count + 2]
+    terms_s, out_s, term_sem, out_sem = refs[count + 2 :]
+    loads = [
+        begin(terms[c].at[side], terms_s.at[c, side], term_sem.at[c * INNER + side])
+        for side in (1, 0)
+        for c in range(count)
+    ]
+    stores = []
+    for index, (side, out) in enumerate(((1, theirs), (0, mine))):
+        for load in loads[index * count : (index + 1) * count]:
+            load.wait()
+        summed = terms_s[0, side].astype(jnp.float32)
+        for c in range(1, count):
+            summed = summed + terms_s[c, side].astype(jnp.float32)
+        out_s[side] = summed.astype(jnp.bfloat16)
+        stores.append(begin(out_s.at[side], out, out_sem.at[side]))
     for store in stores:
         store.wait()
 
 
-def collect(at, dq_mine, dq_recv, terms):
-    rows, half = dq_mine.shape
+def add_terms(terms, after):
+    _, rows, width = terms[0].shape
     count = len(terms)
     return call(
-        functools.partial(collect_kernel, count),
+        functools.partial(add_kernel, count),
+        [bf16(rows, width)] * 2,
+        [ANY] * count,
+        [ANY] * 2,
+        [
+            pltpu.VMEM((count, INNER, rows, width), jnp.bfloat16),
+            pltpu.VMEM((INNER, rows, width), jnp.bfloat16),
+            pltpu.SemaphoreType.DMA((count * INNER,)),
+            pltpu.SemaphoreType.DMA((INNER,)),
+        ],
+        2,
+        "add_terms",
+        after,
+    )(*terms)
+
+
+def join_kernel(at_ref, dq_mine, dq_recv, mine, recv, *refs):
+    outs, (held_s, out_s, sem, out_sem) = refs[:3], refs[3:]
+    half = dq_mine.shape[1]
+    loads = [
+        begin(dq_mine, held_s.at[0, 0], sem.at[0]),
+        begin(dq_recv, held_s.at[1, 0], sem.at[1]),
+    ]
+    for side, held in enumerate((mine, recv)):
+        for index in range(2):
+            source = held.at[:, index * half : (index + 1) * half]
+            loads.append(begin(source, held_s.at[side, 1 + index], sem.at[2 + 2 * side + index]))
+    for load in loads:
+        load.wait()
+    stores = []
+    for index, out in enumerate(outs):
+        for side, at in enumerate((at_ref[0], 1 - at_ref[0])):
+            cols = pl.ds(pl.multiple_of(at * half, half), half)
+            out_s[index, :, cols] = held_s[side, index]
+        stores.append(begin(out_s.at[index], out, out_sem.at[index]))
+    for store in stores:
+        store.wait()
+
+
+def join_heads(at, dq_mine, dq_recv, mine, recv):
+    rows, half = dq_mine.shape
+    return call(
+        join_kernel,
         [bf16(rows, INNER * half)] * 3,
-        [SMEM] + [ANY] * (2 + count),
+        [SMEM] + [ANY] * 4,
         [ANY] * 3,
         [
-            pltpu.VMEM((count, rows, 2 * half), jnp.bfloat16),
-            pltpu.VMEM((2, rows, half), jnp.bfloat16),
+            pltpu.VMEM((INNER, 3, rows, half), jnp.bfloat16),
             pltpu.VMEM((3, rows, INNER * half), jnp.bfloat16),
-            pltpu.SemaphoreType.DMA((count,)),
-            pltpu.SemaphoreType.DMA((2,)),
+            pltpu.SemaphoreType.DMA((6,)),
             pltpu.SemaphoreType.DMA((3,)),
         ],
         2,
-        "collect",
-    )(at, dq_mine, dq_recv, *terms)
+        "join_heads",
+    )(at, dq_mine, dq_recv, mine, recv)
 
 
 def per_device(
@@ -615,16 +661,18 @@
     grads = [grad_own] + [
         lax.ppermute(grad_own, "tp", shift_pairs(tp_count, -step)) for step in range(1, tp_count)
     ]
-    kv_mine, kv_theirs, q_theirs = part_heads(at, queries[0], key_heads[0], value_heads[0])
+    kv_mine, kv_theirs = part_heads(at, key_heads[0], value_heads[0])
+    kv_recv = lax.ppermute(kv_theirs, "ctx", ctx_pairs(0, 1))
     kv_blocks = [
-        lax.ppermute(kv_theirs if side else kv_mine, "ctx", ctx_pairs(step, side))
-        if step or side
-        else kv_mine
+        lax.ppermute(kv_recv if side else kv_mine, "ctx", ctx_pairs(step, 0))
+        if step
+        else (kv_recv if side else kv_mine)
         for step, side in routes
     ]
+    first, key_mask, row_mask, q_theirs = prelude(
+        at, block_pattern, global_offsets, queries[0], grad_own, out_weight, (kv_recv,)
+    )
     q_recv = lax.ppermute(q_theirs, "ctx", ctx_pairs(0, 1))
-
-    first, key_mask, row_mask = prelude(at, block_pattern, global_offsets, grad_own, out_weight)
     g_mine, g_theirs, grad_sends = grad_heads(
         columns_at, first, out_weight, grads, dp_count - 1, picked
     )
@@ -651,8 +699,8 @@
     send = weight_terms(weight_at, attn, grads, swapped, outer, picked, True, (dq_mine,))
     weight_recv = lax.ppermute(send, "ctx", ctx_pairs(0, 1))
     terms = [
-        lax.ppermute(part, "ctx", ctx_pairs(-step, side)) if step or side else part
-        for (step, side), part in zip(routes, parts)
+        lax.ppermute(part, "ctx", ctx_pairs(-step, 0)) if step else part
+        for step, part in enumerate(parts)
     ]
     dq_recv = lax.ppermute(dq_theirs, "ctx", ctx_pairs(0, 1))
     keep = weight_terms(weight_at, attn, grads, swapped, outer, picked, False, (send,))
@@ -663,7 +711,9 @@
             weight_sums[step], "ctx", ctx_pairs(step, 0)
         ).astype(jnp.float32)
 
-    grad_q, grad_k, grad_v = collect(at, dq_mine, dq_recv, terms)
+    terms_mine, terms_theirs = add_terms(terms, (weight_sums[0],))
+    terms_recv = lax.ppermute(terms_theirs, "ctx", ctx_pairs(0, 1))
+    grad_q, grad_k, grad_v = join_heads(at, dq_mine, dq_recv, terms_mine, terms_recv)
     return grad_q[None], grad_k[None], grad_v[None], grad_weight.astype(jnp.bfloat16)
 
 

time: 112 us -> 104 us (0.929)
  starting transfers between devices: 36.4 us -> 28.5 us
  waiting for transfers between devices: 29.5 us -> 26.6 us
  local copies, waits for them, and re-layouts: 4.35 us -> 6.54 us
    ppermute x14 -> x11, starting transfers between devices: 26.6 us -> 16 us  [the longest x6 10.4 us: per_device(): lax.ppermute(kv_recv if side else kv_mine, 'ctx', ctx_pairs(step, 0))]
    ppermute x1, waiting for transfers between devices: 7.77 us -> 0.01 us  [per_device(): dq_recv = lax.ppermute(dq_theirs, 'ctx', ctx_pairs(0, 1))]
    ppermute x1, waiting for transfers between devices: 0.01 us -> 5.35 us  [per_device(): weight_recv = lax.ppermute(send, 'ctx', ctx_pairs(0, 1))]
    unnamed x71 -> x53, local copies, waits for them, and re-layouts: 3.73 us -> 5.9 us
    ppermute x3, starting transfers between devices: 0.62 us -> 2.38 us  [per_device(): lax.ppermute(weight_sums[step], 'ctx', ctx_pairs(step, 0))]
    pallas_call x9 -> x10, Pallas kernels: 37.9 us -> 38.6 us  [placed(): return run(*args)]
    ppermute x14 -> x11, waiting for transfers between devices: 19.5 us -> 19 us  [the longest x3 13.2 us: per_device(): lax.ppermute(part, 'ctx', ctx_pairs(-step, 0))]
  transfers between devices with their start and end apart: 26 -> 23, of which waited for: 6 -> 7; matrix products, arithmetic and copies ran while one was open for 2% -> 3% of each run, Pallas kernels for 30% -> 31%
where the time goes in v6:
time: 104 us; the launch traced here: 103 us
  Pallas kernels  38.6 us (37%)
  starting transfers between devices  28.5 us (27%)
  waiting for transfers between devices  26.6 us (26%)
  local copies, waits for them, and re-layouts  6.54 us (6%)
  other arithmetic  2.03 us (2%)
    pallas_call x10, Pallas kernels, placed(): return run(*args)  38.6 us
    ppermute x3, waiting for transfers between devices, per_device(): lax.ppermute(part, 'ctx', ctx_pairs(-step, 0))  13.2 us
    ppermute x6, starting transfers between devices, per_device(): lax.ppermute(kv_recv if side else kv_mine, 'ctx', ctx_pairs(step, 0))  10.4 us
    unnamed x53, local copies, waits for them, and re-layouts  5.9 us
    ppermute x1, waiting for transfers between devices, per_device(): weight_recv = lax.ppermute(send, 'ctx', ctx_pairs(0, 1))  5.35 us
    ppermute x3, starting transfers between devices, per_device(): lax.ppermute(part, 'ctx', ctx_pairs(-step, 0))  3.44 us
    ppermute x1, starting transfers between devices, per_device(): lax.ppermute(grad_own, 'tp', shift_pairs(tp_count, -step))  3.03 us
    ppermute x3, starting transfers between devices, per_device(): lax.ppermute(weight_sums[step], 'ctx', ctx_pairs(step, 0))  2.38 us
  transfers between devices with their start and end apart: 23, of which 7 were waited for; matrix products, arithmetic and copies ran while one was open for 3% of the time, Pallas kernels for 31%

profile of v6, /device:TPU:0, one launch (start us, length us, event | category | flops | bytes accessed | tf_op | source)
XLA Modules:
  0.0 103.2 jit_solution(17000837282258786189)
XLA Ops:
  0.6 3.0 %collective-permute-start.2 = (bf16[256,2048]{1,0:T(8,128)(2,1)}, bf16[256,2048]{1,0:T(8,128)(2,1)S(1)}, u32[]{:S(2)}, u32[]{:S(2)}) collective-permute-start(bf16[256,2048]{1,0:T(8,128)(2,1)} %bitcast.21), channel_id=1, source_target_pairs={{0,1},{1,0},{2,3},{3,2},{4,5},{5,4},{6,7},{7,6},{8,9},{9,8},{10,11... | collective-permute-start | bytes 3145736 | tf_op jit(solution)/shard_map/ppermute | solution.py:662
  3.7 0.6 stack.65.refs_0_.refs_1_
  4.3 2.5 %part_heads.1 = (bf16[256,256]{1,0:T(8,128)(2,1)}, bf16[256,256]{1,0:T(8,128)(2,1)}) custom-call(s32[11]{0:T(128)} %stack.65.refs_0_.refs_1_, bf16[256,256]{1,0:T(8,128)(2,1)} %bitcast.26, bf16[256,256]{1,0:T(8,128)(2,1)} %bitcast.27), custom_call_target="tpu_custom_call" | custom-call | flops 2000000000 | bytes 6000000 | tf_op jit(solution)/shard_map/part_heads/pallas_call | solution.py:56
  6.8 3.7 %collective-permute-start.8 = (bf16[256,256]{1,0:T(8,128)(2,1)}, bf16[256,256]{1,0:T(8,128)(2,1)S(1)}, u32[]{:S(2)}, u32[]{:S(2)}) collective-permute-start(bf16[256,256]{1,0:T(8,128)(2,1)} %get-tuple-element.39.refs_6_.refs_9_), channel_id=1, source_target_pairs={{0,12},{2,14},{4,0},{6,2},{8,4},{10,6},{12,8},{14,10},{1,13},{3,15... | collective-permute-start | bytes 393224 | tf_op jit(solution)/shard_map/ppermute | solution.py:667
  10.4 1.0 collective-permute-start.4
  11.4 1.5 %collective-permute-start = (bf16[256,256]{1,0:T(8,128)(2,1)}, bf16[256,256]{1,0:T(8,128)(2,1)S(1)}, u32[]{:S(2)}, u32[]{:S(2)}) collective-permute-start(bf16[256,256]{1,0:T(8,128)(2,1)} %get-tuple-element.32), channel_id=1, source_target_pairs={{0,2},{2,0},{4,6},{6,4},{8,10},{10,8},{12,14},{14,12},{1,3},{3,1},... | collective-permute-start | bytes 393224 | tf_op jit(solution)/shard_map/ppermute | solution.py:665
  12.9 0.7 pad_add_fusion.1.refs_1_
  13.6 0.7 copy.11.refs_2_
  14.3 0.7 pad_add_fusion.refs_0_
  14.9 1.7 %collective-permute-done.refs_0_.refs_7_.refs_10_ = bf16[256,256]{1,0:T(8,128)(2,1)S(1)} collective-permute-done((bf16[256,256]{1,0:T(8,128)(2,1)}, bf16[256,256]{1,0:T(8,128)(2,1)S(1)}, u32[]{:S(2)}, u32[]{:S(2)}) %collective-permute-start) | collective-permute-done | bytes 131104 | tf_op jit(solution)/shard_map/ppermute | solution.py:665
  16.6 0.7 copy-done.14
  17.3 3.6 %prelude.1 = (f32[256,256]{1,0:T(8,128)}, bf16[2048,128]{1,0:T(8,128)(2,1)}, f32[8,512]{1,0:T(8,128)}, bf16[256,128]{1,0:T(8,128)(2,1)}) custom-call(bf16[256,256]{1,0:T(8,128)(2,1)} %copy-done.14, s32[11]{0:T(128)} %stack.65.refs_0_.refs_1_, s32[8,3]{1,0:T(8,128)} %copy.11.refs_2_, s32[8,8]{1,0:T(8,128)} %refs_3_.1, bf16[256,256]{1,0:T(8,128)(2,1)} %bitcast.28, ...), custom_call_target="tpu_custom_call" | custom-call | flops 4000000000 | bytes 12000000 | tf_op jit(solution)/shard_map/prelude/pallas_call | solution.py:56
  20.9 1.6 %collective-permute-start.1 = (bf16[256,128]{1,0:T(8,128)(2,1)}, bf16[256,128]{1,0:T(8,128)(2,1)S(1)}, u32[]{:S(2)}, u32[]{:S(2)}) collective-permute-start(bf16[256,128]{1,0:T(8,128)(2,1)} %get-tuple-element.33), channel_id=1, source_target_pairs={{0,2},{2,0},{4,6},{6,4},{8,10},{10,8},{12,14},{14,12},{1,3},{3,1},... | collective-permute-start | bytes 196616 | tf_op jit(solution)/shard_map/ppermute | solution.py:675
  22.5 0.0 collective-permute-done.8.refs_12_.refs_15_
  22.5 2.8 %collective-permute-start.9 = (bf16[256,256]{1,0:T(8,128)(2,1)}, bf16[256,256]{1,0:T(8,128)(2,1)S(1)}, u32[]{:S(2)}, u32[]{:S(2)}) collective-permute-start(bf16[256,256]{1,0:T(8,128)(2,1)} %copy-done.14), channel_id=1, source_target_pairs={{0,12},{2,14},{4,0},{6,2},{8,4},{10,6},{12,8},{14,10},{1,13},{3,15... | collective-permute-start | bytes 393224 | tf_op jit(solution)/shard_map/ppermute | solution.py:667
  25.3 0.0 collective-permute-done.6.refs_10_.refs_13_
  25.3 1.1 %collective-permute-start.7 = (bf16[256,256]{1,0:T(8,128)(2,1)}, bf16[256,256]{1,0:T(8,128)(2,1)S(1)}, u32[]{:S(2)}, u32[]{:S(2)}) collective-permute-start(bf16[256,256]{1,0:T(8,128)(2,1)} %copy-done.14), channel_id=1, source_target_pairs={{0,8},{2,10},{4,12},{6,14},{8,0},{10,2},{12,4},{14,6},{1,9},{3,11}... | collective-permute-start | bytes 393224 | tf_op jit(solution)/shard_map/ppermute | solution.py:667
  26.4 0.6 collective-permute-done.2.refs_4_.refs_7_
  27.0 1.8 %collective-permute-start.5 = (bf16[256,256]{1,0:T(8,128)(2,1)}, bf16[256,256]{1,0:T(8,128)(2,1)S(1)}, u32[]{:S(2)}, u32[]{:S(2)}) collective-permute-start(bf16[256,256]{1,0:T(8,128)(2,1)} %copy-done.14), channel_id=1, source_target_pairs={{0,4},{2,6},{4,8},{6,10},{8,12},{10,14},{12,0},{14,2},{1,5},{3,7},... | collective-permute-start | bytes 393224 | tf_op jit(solution)/shard_map/ppermute | solution.py:667
  28.8 3.8 %grad_heads.1 = (bf16[128,256]{1,0:T(8,128)(2,1)}, bf16[128,256]{1,0:T(8,128)(2,1)}, bf16[256,2048]{1,0:T(8,128)(2,1)}) custom-call(s32[3]{0:T(128)} %pad_add_fusion.refs_0_, f32[256,256]{1,0:T(8,128)} %get-tuple-element.34.refs_1_, bf16[256,4096]{1,0:T(8,128)(2,1)} %refs_2_.2, bf16[256,2048]{1,0:T(8,128)(2,1)} %bitcast.23, bf16[256,2048]{1,0:T(8,128)(2,1)} %copy-done.2), custom_call_target="tpu_custom_call" | custom-call | flops 3000000000 | bytes 9000000 | tf_op jit(solution)/shard_map/grad_heads/pallas_call | solution.py:56
  32.6 0.0 copy-start.13
  32.7 1.6 %collective-permute-start.3 = (bf16[128,256]{1,0:T(8,128)(2,1)}, bf16[128,256]{1,0:T(8,128)(2,1)S(1)}, u32[]{:S(2)}, u32[]{:S(2)}) collective-permute-start(bf16[128,256]{1,0:T(8,128)(2,1)} %get-tuple-element.36.refs_0_), channel_id=1, source_target_pairs={{0,2},{2,0},{4,6},{6,4},{8,10},{10,8},{12,14},{14,12},{1,3},{3,1},... | collective-permute-start | bytes 196616 | tf_op jit(solution)/shard_map/ppermute | solution.py:679
  34.2 0.0 collective-permute-done.9.refs_13_.refs_16_
  34.2 1.7 %collective-permute-done.7.refs_11_.refs_14_ = bf16[256,256]{1,0:T(8,128)(2,1)S(1)} collective-permute-done((bf16[256,256]{1,0:T(8,128)(2,1)}, bf16[256,256]{1,0:T(8,128)(2,1)S(1)}, u32[]{:S(2)}, u32[]{:S(2)}) %collective-permute-start.7) | collective-permute-done | bytes 131104 | tf_op jit(solution)/shard_map/ppermute | solution.py:667
  36.0 0.0 collective-permute-done.5.refs_9_.refs_12_
  36.0 0.6 copy-done.16
  36.7 0.0 copy-done.17
  36.7 6.2 %forward.1 = (bf16[1,2048,512]{2,1,0:T(8,128)(2,1)}, f32[8,512]{1,0:T(8,128)}, bf16[128,256]{1,0:T(8,128)(2,1)}, bf16[128,256]{1,0:T(8,128)(2,1)}) custom-call(bf16[128,256]{1,0:T(8,128)(2,1)} %get-tuple-element.36.refs_0_, s32[11]{0:T(128)} %stack.65.refs_0_.refs_1_, bf16[256,256]{1,0:T(8,128)(2,1)} %bitcast.29, bf16[256,128]{1,0:T(8,128)(2,1)} %copy-done.21, ...), custom_call_target="tpu_custom_call" | custom-call | flops 6000000000 | bytes 18000000 | tf_op jit(solution)/shard_map/forward/pallas_call | solution.py:56
  42.9 0.1 collective-permute-start.13
  43.0 0.6 collective-permute-start.11
  43.6 1.2 %collective-permute-start.12 = (bf16[128,256]{1,0:T(8,128)(2,1)}, bf16[128,256]{1,0:T(8,128)(2,1)S(1)}, u32[]{:S(2)}, u32[]{:S(2)}) collective-permute-start(bf16[128,256]{1,0:T(8,128)(2,1)} %get-tuple-element.40.refs_5_.refs_2_), channel_id=1, source_target_pairs={{0,16},{2,18},{4,20},{6,22},{8,24},{10,26},{12,28},{14,30},{16,0},... | collective-permute-start | bytes 196616 | tf_op jit(solution)/shard_map/ppermute | solution.py:694
  44.8 0.6 copy-done.25
  45.4 7.9 %backward.1 = (bf16[256,128]{1,0:T(8,128)(2,1)}, bf16[256,128]{1,0:T(8,128)(2,1)}, bf16[2,256,256]{2,1,0:T(8,128)(2,1)}, bf16[2,256,256]{2,1,0:T(8,128)(2,1)}, b...) custom-call(s32[11]{0:T(128)} %stack.65.refs_0_.refs_1_, bf16[256,256]{1,0:T(8,128)(2,1)} %bitcast.30, ...), custom_call_target="tpu_custom_call" | custom-call | flops 8000000000 | bytes 24000000 | tf_op jit(solution)/shard_map/backward/pallas_call | solution.py:56
  53.4 0.0 copy-start.22
  53.4 0.0 collective-permute-done.11.refs_3_
  53.4 0.0 copy-start.23
  53.4 0.0 copy-start.24
  53.4 0.0 collective-permute-done.14.refs_8_
  53.5 0.6 copy-done.22
  54.0 0.0 copy-done.23
  54.0 0.0 copy-done.24
  54.1 0.4 copy-done.3
  54.5 4.1 %weight_sent.1.refs_0_ = bf16[4,256,256]{2,1,0:T(8,128)(2,1)} custom-call(bf16[256,128]{1,0:T(8,128)(2,1)} %get-tuple-element.44.refs_0_.refs_1_, s32[3]{0:T(128)} %pad_add_fusion.1.refs_1_, bf16[128,256]{1,0:T(8,128)(2,1)} %get-tuple-element.40.refs_5_.refs_2_, bf16[128,256]{1,0:T(8,128)(2,1)} %copy-done.23, bf16[128,256]{1,0:T(8,128)(2,1)} %copy-done.24, ...), custom_call_target="tpu_custom_call" | custom-call | flops 3000000000 | bytes 9000000 | tf_op jit(solution)/shard_map/weight_sent/pallas_call | solution.py:56
  58.5 0.6 collective-permute-start.15
  59.1 1.5 %collective-permute-start.10 = (bf16[256,128]{1,0:T(8,128)(2,1)S(1)}, bf16[256,128]{1,0:T(8,128)(2,1)S(1)}, u32[]{:S(2)}, u32[]{:S(2)}) collective-permute-start(bf16[256,128]{1,0:T(8,128)(2,1)S(1)} %copy-done.19), channel_id=1, source_target_pairs={{0,2},{2,0},{4,6},{6,4},{8,10},{10,8},{12,14},{14,12},{1,3},{3,1},... | collective-permute-start | bytes 196616 | tf_op jit(solution)/shard_map/ppermute | solution.py:705
  60.6 1.6 %collective-permute-start.16 = (bf16[2,256,256]{2,1,0:T(8,128)(2,1)S(1)}, bf16[2,256,256]{2,1,0:T(8,128)(2,1)S(1)}, u32[]{:S(2)}, u32[]{:S(2)}) collective-permute-start(bf16[2,256,256]{2,1,0:T(8,128)(2,1)S(1)} %copy-done.7), channel_id=1, source_target_pairs={{0,12},{2,14},{4,0},{6,2},{8,4},{10,6},{12,8},{14,10},{1,13},{3,15... | collective-permute-start | bytes 786440 | tf_op jit(solution)/shard_map/ppermute | solution.py:702
  62.2 0.0 collective-permute-start.17
  62.2 1.9 %collective-permute-start.18 = (bf16[2,256,256]{2,1,0:T(8,128)(2,1)S(1)}, bf16[2,256,256]{2,1,0:T(8,128)(2,1)S(1)}, u32[]{:S(2)}, u32[]{:S(2)}) collective-permute-start(bf16[2,256,256]{2,1,0:T(8,128)(2,1)S(1)} %copy-done.5), channel_id=1, source_target_pairs={{0,4},{2,6},{4,8},{6,10},{8,12},{10,14},{12,0},{14,2},{1,5},{3,7},... | collective-permute-start | bytes 786440 | tf_op jit(solution)/shard_map/ppermute | solution.py:702
  64.1 3.9 %weight_kept.1.refs_0_ = bf16[4,256,256]{2,1,0:T(8,128)(2,1)} custom-call(bf16[4,256,256]{2,1,0:T(8,128)(2,1)} %weight_sent.1.refs_0_, s32[3]{0:T(128)} %pad_add_fusion.1.refs_1_, bf16[128,256]{1,0:T(8,128)(2,1)} %get-tuple-element.40.refs_5_.refs_2_, bf16[128,256]{1,0:T(8,128)(2,1)} %copy-done.23, bf16[128,256]{1,0:T(8,128)(2,1)} %copy-done.24, ...), custom_call_target="tpu_custom_call" | custom-call | flops 3000000000 | bytes 9000000 | tf_op jit(solution)/shard_map/weight_kept/pallas_call | solution.py:56
  68.0 5.3 %collective-permute-done.15.refs_1_ = bf16[4,256,256]{2,1,0:T(8,128)(2,1)S(1)} collective-permute-done((bf16[4,256,256]{2,1,0:T(8,128)(2,1)}, bf16[4,256,256]{2,1,0:T(8,128)(2,1)S(1)}, u32[]{:S(2)}, u32[]{:S(2)}) %collective-permute-start.15) | collective-permute-done | bytes 524320 | tf_op jit(solution)/shard_map/ppermute | solution.py:700
  73.3 0.8 copy-done.4
  74.2 2.1 %weight_add.1 = (bf16[256,256]{1,0:T(8,128)(2,1)}, bf16[256,256]{1,0:T(8,128)(2,1)}, bf16[256,256]{1,0:T(8,128)(2,1)}, bf16[256,256]{1,0:T(8,128)(2,1)}) custom-call(bf16[4,256,256]{2,1,0:T(8,128)(2,1)} %weight_kept.1.refs_0_, bf16[4,256,256]{2,1,0:T(8,128)(2,1)} %copy-done.4), custom_call_target="tpu_custom_call" | custom-call | flops 1500000000 | bytes 4500000 | tf_op jit(solution)/shard_map/weight_add/pallas_call | solution.py:56
  76.2 0.4 collective-permute-start.20
  76.6 2.0 %collective-permute-start.21 = (bf16[256,256]{1,0:T(8,128)(2,1)}, bf16[256,256]{1,0:T(8,128)(2,1)S(1)}, u32[]{:S(2)}, u32[]{:S(2)}) collective-permute-start(bf16[256,256]{1,0:T(8,128)(2,1)} %get-tuple-element.58), channel_id=1, source_target_pairs={{0,8},{2,10},{4,12},{6,14},{8,0},{10,2},{12,4},{14,6},{1,9},{3,11}... | collective-permute-start | bytes 393224 | tf_op jit(solution)/shard_map/ppermute | solution.py:710
  78.6 13.2 %collective-permute-done.17.refs_3_ = bf16[2,256,256]{2,1,0:T(8,128)(2,1)S(1)} collective-permute-done((bf16[2,256,256]{2,1,0:T(8,128)(2,1)S(1)}, bf16[2,256,256]{2,1,0:T(8,128)(2,1)S(1)}, u32[]{:S(2)}, u32[]{:S(2)}) %collective-permute-start.17) | collective-permute-done | bytes 262176 | tf_op jit(solution)/shard_map/ppermute | solution.py:702
  91.9 0.7 copy-done.9
  92.6 0.1 copy-done.10
  92.7 2.1 %add_terms.1 = (bf16[256,256]{1,0:T(8,128)(2,1)}, bf16[256,256]{1,0:T(8,128)(2,1)}) custom-call(bf16[256,256]{1,0:T(8,128)(2,1)} %get-tuple-element.47.refs_0_, bf16[2,256,256]{2,1,0:T(8,128)(2,1)} %get-tuple-element.48.refs_1_, bf16[2,256,256]{2,1,0:T(8,128)(2,1)} %copy-done.8, bf16[2,256,256]{2,1,0:T(8,128)(2,1)} %copy-done.9, bf16[2,256,256]{2,1,0:T(8,128)(2,1)} %copy-done.10), custom_call_target="tpu_custom_call" | custom-call | flops 2000000000 | bytes 6000000 | tf_op jit(solution)/shard_map/add_terms/pallas_call | solution.py:56
  94.8 0.6 collective-permute-start.19
  95.4 1.6 %collective-permute-done.22 = bf16[256,256]{1,0:T(8,128)(2,1)S(1)} collective-permute-done((bf16[256,256]{1,0:T(8,128)(2,1)}, bf16[256,256]{1,0:T(8,128)(2,1)S(1)}, u32[]{:S(2)}, u32[]{:S(2)}) %collective-permute-start.22) | collective-permute-done | bytes 131104 | tf_op jit(solution)/shard_map/ppermute | solution.py:710
  97.0 0.7 add_convert_fusion
  97.8 2.3 %collective-permute-done.19.refs_4_ = bf16[256,256]{1,0:T(8,128)(2,1)S(1)} collective-permute-done((bf16[256,256]{1,0:T(8,128)(2,1)}, bf16[256,256]{1,0:T(8,128)(2,1)S(1)}, u32[]{:S(2)}, u32[]{:S(2)}) %collective-permute-start.19) | collective-permute-done | bytes 131104 | tf_op jit(solution)/shard_map/ppermute | solution.py:715
  100.0 0.7 copy-done.18
  100.7 2.5 %join_heads.1 = (bf16[256,256]{1,0:T(8,128)(2,1)}, bf16[256,256]{1,0:T(8,128)(2,1)}, bf16[256,256]{1,0:T(8,128)(2,1)}) custom-call(s32[11]{0:T(128)} %stack.65.refs_0_.refs_1_, bf16[256,128]{1,0:T(8,128)(2,1)} %get-tuple-element.44.refs_0_.refs_1_, bf16[256,128]{1,0:T(8,128)(2,1)} %copy-done.20, bf16[256,256]{1,0:T(8,128)(2,1)} %get-tuple-element.52.refs_3_, ...), custom_call_target="tpu_custom_call" | custom-call | flops 2000000000 | bytes 6000000 | tf_op jit(solution)/shard_map/join_heads/pallas_call | solution.py:56
  (49 shorter events, 0.1 us)
Async XLA Ops:
  0.6 26.4 %collective-permute-start.2 = (bf16[256,2048]{1,0:T(8,128)(2,1)}, bf16[256,2048]{1,0:T(8,128)(2,1)S(1)}, u32[]{:S(2)}, u32[]{:S(2)}) collective-permute-start(bf16[256,2048]{1,0:T(8,128)(2,1)} %bitcast.21), channel_id=1, source_target_pairs={{0,1},{1,0},{2,3},{3,2},{4,5},{5,4},{6,7},{7,6},{8,9},{9,8},{10,11... | collective-permute-start | bytes 3145736 | tf_op jit(solution)/shard_map/ppermute | solution.py:662
  4.3 9.3 %copy-start.1 = (s32[8,3]{0,1:T(4,128)S(1)}, s32[8,3]{0,1:T(4,128)}, u32[]{:S(2)}) copy-start(s32[8,3]{0,1:T(4,128)} %param.12) | copy-start | bytes 292
  6.8 15.7 %collective-permute-start.8 = (bf16[256,256]{1,0:T(8,128)(2,1)}, bf16[256,256]{1,0:T(8,128)(2,1)S(1)}, u32[]{:S(2)}, u32[]{:S(2)}) collective-permute-start(bf16[256,256]{1,0:T(8,128)(2,1)} %get-tuple-element.39.refs_6_.refs_9_), channel_id=1, source_target_pairs={{0,12},{2,14},{4,0},{6,2},{8,4},{10,6},{12,8},{14,10},{1,13},{3,15... | collective-permute-start | bytes 393224 | tf_op jit(solution)/shard_map/ppermute | solution.py:667
  10.4 14.8 %collective-permute-start.6 = (bf16[256,256]{1,0:T(8,128)(2,1)}, bf16[256,256]{1,0:T(8,128)(2,1)S(1)}, u32[]{:S(2)}, u32[]{:S(2)}) collective-permute-start(bf16[256,256]{1,0:T(8,128)(2,1)} %get-tuple-element.39.refs_6_.refs_9_), channel_id=1, source_target_pairs={{0,8},{2,10},{4,12},{6,14},{8,0},{10,2},{12,4},{14,6},{1,9},{3,11}... | collective-permute-start | bytes 393224 | tf_op jit(solution)/shard_map/ppermute | solution.py:667
  10.4 22.2 %collective-permute-start.4 = (bf16[256,256]{1,0:T(8,128)(2,1)}, bf16[256,256]{1,0:T(8,128)(2,1)S(1)}, u32[]{:S(2)}, u32[]{:S(2)}) collective-permute-start(bf16[256,256]{1,0:T(8,128)(2,1)} %get-tuple-element.39.refs_6_.refs_9_), channel_id=1, source_target_pairs={{0,4},{2,6},{4,8},{6,10},{8,12},{10,14},{12,0},{14,2},{1,5},{3,7},... | collective-permute-start | bytes 393224 | tf_op jit(solution)/shard_map/ppermute | solution.py:667
  11.4 5.2 %collective-permute-start = (bf16[256,256]{1,0:T(8,128)(2,1)}, bf16[256,256]{1,0:T(8,128)(2,1)S(1)}, u32[]{:S(2)}, u32[]{:S(2)}) collective-permute-start(bf16[256,256]{1,0:T(8,128)(2,1)} %get-tuple-element.32), channel_id=1, source_target_pairs={{0,2},{2,0},{4,6},{6,4},{8,10},{10,8},{12,14},{14,12},{1,3},{3,1},... | collective-permute-start | bytes 393224 | tf_op jit(solution)/shard_map/ppermute | solution.py:665
  16.6 0.7 copy-start.14
  20.9 13.3 %collective-permute-start.1 = (bf16[256,128]{1,0:T(8,128)(2,1)}, bf16[256,128]{1,0:T(8,128)(2,1)S(1)}, u32[]{:S(2)}, u32[]{:S(2)}) collective-permute-start(bf16[256,128]{1,0:T(8,128)(2,1)} %get-tuple-element.33), channel_id=1, source_target_pairs={{0,2},{2,0},{4,6},{6,4},{8,10},{10,8},{12,14},{14,12},{1,3},{3,1},... | collective-permute-start | bytes 196616 | tf_op jit(solution)/shard_map/ppermute | solution.py:675
  22.5 13.5 %copy-start.11 = (bf16[256,256]{1,0:T(8,128)(2,1)}, bf16[256,256]{1,0:T(8,128)(2,1)S(1)}, u32[]{:S(2)}) copy-start(bf16[256,256]{1,0:T(8,128)(2,1)S(1)} %collective-permute-done.8.refs_12_.refs_15_) | copy-start | bytes 393220
  22.5 11.8 %collective-permute-start.9 = (bf16[256,256]{1,0:T(8,128)(2,1)}, bf16[256,256]{1,0:T(8,128)(2,1)S(1)}, u32[]{:S(2)}, u32[]{:S(2)}) collective-permute-start(bf16[256,256]{1,0:T(8,128)(2,1)} %copy-done.14), channel_id=1, source_target_pairs={{0,12},{2,14},{4,0},{6,2},{8,4},{10,6},{12,8},{14,10},{1,13},{3,15... | collective-permute-start | bytes 393224 | tf_op jit(solution)/shard_map/ppermute | solution.py:667
  25.3 10.7 %copy-start.12 = (bf16[256,256]{1,0:T(8,128)(2,1)}, bf16[256,256]{1,0:T(8,128)(2,1)S(1)}, u32[]{:S(2)}) copy-start(bf16[256,256]{1,0:T(8,128)(2,1)S(1)} %collective-permute-done.6.refs_10_.refs_13_) | copy-start | bytes 393220
  25.3 10.7 %collective-permute-start.7 = (bf16[256,256]{1,0:T(8,128)(2,1)}, bf16[256,256]{1,0:T(8,128)(2,1)S(1)}, u32[]{:S(2)}, u32[]{:S(2)}) collective-permute-start(bf16[256,256]{1,0:T(8,128)(2,1)} %copy-done.14), channel_id=1, source_target_pairs={{0,8},{2,10},{4,12},{6,14},{8,0},{10,2},{12,4},{14,6},{1,9},{3,11}... | collective-permute-start | bytes 393224 | tf_op jit(solution)/shard_map/ppermute | solution.py:667
  27.0 1.8 %copy-start.2 = (bf16[256,2048]{1,0:T(8,128)(2,1)}, bf16[256,2048]{1,0:T(8,128)(2,1)S(1)}, u32[]{:S(2)}) copy-start(bf16[256,2048]{1,0:T(8,128)(2,1)S(1)} %collective-permute-done.2.refs_4_.refs_7_) | copy-start | bytes 3145732
  27.0 9.0 %collective-permute-start.5 = (bf16[256,256]{1,0:T(8,128)(2,1)}, bf16[256,256]{1,0:T(8,128)(2,1)S(1)}, u32[]{:S(2)}, u32[]{:S(2)}) collective-permute-start(bf16[256,256]{1,0:T(8,128)(2,1)} %copy-done.14), channel_id=1, source_target_pairs={{0,4},{2,6},{4,8},{6,10},{8,12},{10,14},{12,0},{14,2},{1,5},{3,7},... | collective-permute-start | bytes 393224 | tf_op jit(solution)/shard_map/ppermute | solution.py:667
  32.6 3.4 %copy-start.13 = (bf16[256,256]{1,0:T(8,128)(2,1)}, bf16[256,256]{1,0:T(8,128)(2,1)S(1)}, u32[]{:S(2)}) copy-start(bf16[256,256]{1,0:T(8,128)(2,1)S(1)} %collective-permute-done.4.refs_8_.refs_11_) | copy-start | bytes 393220
  32.7 12.2 %collective-permute-start.3 = (bf16[128,256]{1,0:T(8,128)(2,1)}, bf16[128,256]{1,0:T(8,128)(2,1)S(1)}, u32[]{:S(2)}, u32[]{:S(2)}) collective-permute-start(bf16[128,256]{1,0:T(8,128)(2,1)} %get-tuple-element.36.refs_0_), channel_id=1, source_target_pairs={{0,2},{2,0},{4,6},{6,4},{8,10},{10,8},{12,14},{14,12},{1,3},{3,1},... | collective-permute-start | bytes 196616 | tf_op jit(solution)/shard_map/ppermute | solution.py:679
  34.2 1.8 %copy-start.21 = (bf16[256,128]{1,0:T(8,128)(2,1)}, bf16[256,128]{1,0:T(8,128)(2,1)S(1)}, u32[]{:S(2)}) copy-start(bf16[256,128]{1,0:T(8,128)(2,1)S(1)} %collective-permute-done.1.refs_3_.refs_2_) | copy-start | bytes 196612
  34.2 19.2 %collective-permute-start.14 = (bf16[256,2048]{1,0:T(8,128)(2,1)}, bf16[256,2048]{1,0:T(8,128)(2,1)S(1)}, u32[]{:S(2)}, u32[]{:S(2)}) collective-permute-start(bf16[256,2048]{1,0:T(8,128)(2,1)} %get-tuple-element.46), channel_id=1, source_target_pairs={{0,16},{16,0},{1,17},{17,1},{2,18},{18,2},{3,19},{19,3},{4,20},{20... | collective-permute-start | bytes 3145736 | tf_op jit(solution)/shard_map/ppermute | solution.py:681
  34.2 1.8 %copy-start.15 = (bf16[256,256]{1,0:T(8,128)(2,1)}, bf16[256,256]{1,0:T(8,128)(2,1)S(1)}, u32[]{:S(2)}) copy-start(bf16[256,256]{1,0:T(8,128)(2,1)S(1)} %collective-permute-done.9.refs_13_.refs_16_) | copy-start | bytes 393220
  36.0 0.7 copy-start.16
  36.0 0.7 copy-start.17
  42.9 10.5 %collective-permute-start.13 = (bf16[128,256]{1,0:T(8,128)(2,1)}, bf16[128,256]{1,0:T(8,128)(2,1)S(1)}, u32[]{:S(2)}, u32[]{:S(2)}) collective-permute-start(bf16[128,256]{1,0:T(8,128)(2,1)} %get-tuple-element.41.refs_6_), channel_id=1, source_target_pairs={{0,18},{2,16},{4,22},{6,20},{8,26},{10,24},{12,30},{14,28},{16,2},... | collective-permute-start | bytes 196616 | tf_op jit(solution)/shard_map/ppermute | solution.py:694
  43.0 10.4 %collective-permute-start.11 = (bf16[128,256]{1,0:T(8,128)(2,1)}, bf16[128,256]{1,0:T(8,128)(2,1)S(1)}, u32[]{:S(2)}, u32[]{:S(2)}) collective-permute-start(bf16[128,256]{1,0:T(8,128)(2,1)} %get-tuple-element.41.refs_6_), channel_id=1, source_target_pairs={{0,2},{2,0},{4,6},{6,4},{8,10},{10,8},{12,14},{14,12},{1,3},{3,1},... | collective-permute-start | bytes 196616 | tf_op jit(solution)/shard_map/ppermute | solution.py:694
  43.6 9.9 %collective-permute-start.12 = (bf16[128,256]{1,0:T(8,128)(2,1)}, bf16[128,256]{1,0:T(8,128)(2,1)S(1)}, u32[]{:S(2)}, u32[]{:S(2)}) collective-permute-start(bf16[128,256]{1,0:T(8,128)(2,1)} %get-tuple-element.40.refs_5_.refs_2_), channel_id=1, source_target_pairs={{0,16},{2,18},{4,20},{6,22},{8,24},{10,26},{12,28},{14,30},{16,0},... | collective-permute-start | bytes 196616 | tf_op jit(solution)/shard_map/ppermute | solution.py:694
  44.8 0.6 copy-start.25
  53.4 0.6 copy-start.22
  53.4 0.6 copy-start.23
  53.4 0.6 copy-start.24
  53.5 1.0 copy-start.3
  54.5 4.7 %copy-start.19 = (bf16[256,128]{1,0:T(8,128)(2,1)S(1)}, bf16[256,128]{1,0:T(8,128)(2,1)}, u32[]{:S(2)}) copy-start(bf16[256,128]{1,0:T(8,128)(2,1)} %get-tuple-element.45) | copy-start | bytes 196612
  54.5 6.2 %copy-start.7 = (bf16[2,256,256]{2,1,0:T(8,128)(2,1)S(1)}, bf16[2,256,256]{2,1,0:T(8,128)(2,1)}, u32[]{:S(2)}) copy-start(bf16[2,256,256]{2,1,0:T(8,128)(2,1)} %get-tuple-element.49) | copy-start | bytes 786436
  54.5 7.7 %copy-start.6 = (bf16[2,256,256]{2,1,0:T(8,128)(2,1)S(1)}, bf16[2,256,256]{2,1,0:T(8,128)(2,1)}, u32[]{:S(2)}) copy-start(bf16[2,256,256]{2,1,0:T(8,128)(2,1)} %get-tuple-element.50) | copy-start | bytes 786436
  54.5 7.8 %copy-start.5 = (bf16[2,256,256]{2,1,0:T(8,128)(2,1)S(1)}, bf16[2,256,256]{2,1,0:T(8,128)(2,1)}, u32[]{:S(2)}) copy-start(bf16[2,256,256]{2,1,0:T(8,128)(2,1)} %get-tuple-element.51) | copy-start | bytes 786436
  58.5 14.8 %collective-permute-start.15 = (bf16[4,256,256]{2,1,0:T(8,128)(2,1)}, bf16[4,256,256]{2,1,0:T(8,128)(2,1)S(1)}, u32[]{:S(2)}, u32[]{:S(2)}) collective-permute-start(bf16[4,256,256]{2,1,0:T(8,128)(2,1)} %weight_sent.1.refs_0_), channel_id=1, source_target_pairs={{0,2},{2,0},{4,6},{6,4},{8,10},{10,8},{12,14},{14,12},{1,3},{3,1},... | collective-permute-start | bytes 1572872 | tf_op jit(solution)/shard_map/ppermute | solution.py:700
  59.1 38.6 %collective-permute-start.10 = (bf16[256,128]{1,0:T(8,128)(2,1)S(1)}, bf16[256,128]{1,0:T(8,128)(2,1)S(1)}, u32[]{:S(2)}, u32[]{:S(2)}) collective-permute-start(bf16[256,128]{1,0:T(8,128)(2,1)S(1)} %copy-done.19), channel_id=1, source_target_pairs={{0,2},{2,0},{4,6},{6,4},{8,10},{10,8},{12,14},{14,12},{1,3},{3,1},... | collective-permute-start | bytes 196616 | tf_op jit(solution)/shard_map/ppermute | solution.py:705
  60.6 16.0 %collective-permute-start.16 = (bf16[2,256,256]{2,1,0:T(8,128)(2,1)S(1)}, bf16[2,256,256]{2,1,0:T(8,128)(2,1)S(1)}, u32[]{:S(2)}, u32[]{:S(2)}) collective-permute-start(bf16[2,256,256]{2,1,0:T(8,128)(2,1)S(1)} %copy-done.7), channel_id=1, source_target_pairs={{0,12},{2,14},{4,0},{6,2},{8,4},{10,6},{12,8},{14,10},{1,13},{3,15... | collective-permute-start | bytes 786440 | tf_op jit(solution)/shard_map/ppermute | solution.py:702
  62.2 29.6 %collective-permute-start.17 = (bf16[2,256,256]{2,1,0:T(8,128)(2,1)S(1)}, bf16[2,256,256]{2,1,0:T(8,128)(2,1)S(1)}, u32[]{:S(2)}, u32[]{:S(2)}) collective-permute-start(bf16[2,256,256]{2,1,0:T(8,128)(2,1)S(1)} %copy-done.6), channel_id=1, source_target_pairs={{0,8},{2,10},{4,12},{6,14},{8,0},{10,2},{12,4},{14,6},{1,9},{3,11}... | collective-permute-start | bytes 786440 | tf_op jit(solution)/shard_map/ppermute | solution.py:702
  62.2 29.6 %collective-permute-start.18 = (bf16[2,256,256]{2,1,0:T(8,128)(2,1)S(1)}, bf16[2,256,256]{2,1,0:T(8,128)(2,1)S(1)}, u32[]{:S(2)}, u32[]{:S(2)}) collective-permute-start(bf16[2,256,256]{2,1,0:T(8,128)(2,1)S(1)} %copy-done.5), channel_id=1, source_target_pairs={{0,4},{2,6},{4,8},{6,10},{8,12},{10,14},{12,0},{14,2},{1,5},{3,7},... | collective-permute-start | bytes 786440 | tf_op jit(solution)/shard_map/ppermute | solution.py:702
  73.3 0.8 copy-start.4
  76.2 19.2 %collective-permute-start.20 = (bf16[256,256]{1,0:T(8,128)(2,1)}, bf16[256,256]{1,0:T(8,128)(2,1)S(1)}, u32[]{:S(2)}, u32[]{:S(2)}) collective-permute-start(bf16[256,256]{1,0:T(8,128)(2,1)} %get-tuple-element.57), channel_id=1, source_target_pairs={{0,4},{2,6},{4,8},{6,10},{8,12},{10,14},{12,0},{14,2},{1,5},{3,7},... | collective-permute-start | bytes 393224 | tf_op jit(solution)/shard_map/ppermute | solution.py:710
  76.6 15.3 %copy-start.8 = (bf16[2,256,256]{2,1,0:T(8,128)(2,1)}, bf16[2,256,256]{2,1,0:T(8,128)(2,1)S(1)}, u32[]{:S(2)}) copy-start(bf16[2,256,256]{2,1,0:T(8,128)(2,1)S(1)} %collective-permute-done.16.refs_2_) | copy-start | bytes 786436
  76.6 18.8 %collective-permute-start.21 = (bf16[256,256]{1,0:T(8,128)(2,1)}, bf16[256,256]{1,0:T(8,128)(2,1)S(1)}, u32[]{:S(2)}, u32[]{:S(2)}) collective-permute-start(bf16[256,256]{1,0:T(8,128)(2,1)} %get-tuple-element.58), channel_id=1, source_target_pairs={{0,8},{2,10},{4,12},{6,14},{8,0},{10,2},{12,4},{14,6},{1,9},{3,11}... | collective-permute-start | bytes 393224 | tf_op jit(solution)/shard_map/ppermute | solution.py:710
  91.8 0.7 copy-start.9
  91.8 5.2 %collective-permute-start.22 = (bf16[256,256]{1,0:T(8,128)(2,1)}, bf16[256,256]{1,0:T(8,128)(2,1)S(1)}, u32[]{:S(2)}, u32[]{:S(2)}) collective-permute-start(bf16[256,256]{1,0:T(8,128)(2,1)} %get-tuple-element.59), channel_id=1, source_target_pairs={{0,12},{2,14},{4,0},{6,2},{8,4},{10,6},{12,8},{14,10},{1,13},{3,15... | collective-permute-start | bytes 393224 | tf_op jit(solution)/shard_map/ppermute | solution.py:710
  91.9 0.8 copy-start.10
  92.7 4.4 %copy-start = (bf16[256,256]{1,0:T(8,128)(2,1)S(1)}, bf16[256,256]{1,0:T(8,128)(2,1)}, u32[]{:S(2)}) copy-start(bf16[256,256]{1,0:T(8,128)(2,1)} %get-tuple-element.47.refs_0_) | copy-start | bytes 393220
  94.8 5.2 %collective-permute-start.19 = (bf16[256,256]{1,0:T(8,128)(2,1)}, bf16[256,256]{1,0:T(8,128)(2,1)S(1)}, u32[]{:S(2)}, u32[]{:S(2)}) collective-permute-start(bf16[256,256]{1,0:T(8,128)(2,1)} %get-tuple-element.53), channel_id=1, source_target_pairs={{0,2},{2,0},{4,6},{6,4},{8,10},{10,8},{12,14},{14,12},{1,3},{3,1},... | collective-permute-start | bytes 393224 | tf_op jit(solution)/shard_map/ppermute | solution.py:715
  97.8 2.3 %copy-start.20 = (bf16[256,128]{1,0:T(8,128)(2,1)}, bf16[256,128]{1,0:T(8,128)(2,1)S(1)}, u32[]{:S(2)}) copy-start(bf16[256,128]{1,0:T(8,128)(2,1)S(1)} %collective-permute-done.10.refs_2_) | copy-start | bytes 196612
  100.0 0.7 copy-start.18

commit v7 on v6

--- a/solution.py
+++ b/solution.py
@@ -66,45 +66,46 @@
     return pltpu.HBM(shape, jnp.float32)
 
 
-def part_kernel(at_ref, k_ref, v_ref, kv_mine, kv_theirs, held_s, in_sem, out_sem):
-    half = kv_mine.shape[1] // 2
-    loads = [begin(held, held_s.at[i], in_sem.at[i]) for i, held in enumerate((k_ref, v_ref))]
-    mine = pl.ds(pl.multiple_of(at_ref[0] * half, half), half)
-    theirs = pl.ds(pl.multiple_of((1 - at_ref[0]) * half, half), half)
+def part_kernel(at_ref, q_ref, k_ref, v_ref, send, q_theirs, held_s, in_sem, out_sem):
+    count, rows, both = send.shape
+    half = both // 2
+    loads = [begin(held, held_s.at[i], in_sem.at[i]) for i, held in enumerate((k_ref, v_ref, q_ref))]
     copies = []
     for index in range(2):
         loads[index].wait()
-        place = slice(index * half, (index + 1) * half)
-        for side, (cols, out) in enumerate(((mine, kv_mine), (theirs, kv_theirs))):
-            sem = out_sem.at[2 * index + side]
-            copies.append(begin(held_s.at[index, :, cols], out.at[:, place], sem))
+        for place in range(count):
+            side = place % INNER
+            source = held_s.at[index, :, side * half : (side + 1) * half]
+            target = send.at[place, :, index * half : (index + 1) * half]
+            copies.append(begin(source, target, out_sem.at[index * count + place]))
+    loads[2].wait()
+    theirs = pl.ds(pl.multiple_of((1 - at_ref[0]) * half, half), half)
+    copies.append(begin(held_s.at[2, :, theirs], q_theirs, out_sem.at[2 * count]))
     for copy in copies:
         copy.wait()
 
 
-def part_heads(at, keys, values):
-    rows, feats = keys.shape
+def part_heads(at, queries, keys, values, count):
+    rows, feats = queries.shape
+    half = feats // INNER
     return call(
         part_kernel,
-        [bf16(rows, feats), bf16(rows, feats)],
-        [SMEM] + [ANY] * 2,
+        [bf16(count, rows, 2 * half), bf16(rows, half)],
+        [SMEM] + [ANY] * 3,
         [ANY] * 2,
         [
-            pltpu.VMEM((2, rows, feats), jnp.bfloat16),
-            pltpu.SemaphoreType.DMA((2,)),
-            pltpu.SemaphoreType.DMA((4,)),
+            pltpu.VMEM((3, rows, feats), jnp.bfloat16),
+            pltpu.SemaphoreType.DMA((3,)),
+            pltpu.SemaphoreType.DMA((2 * count + 1,)),
         ],
         2,
         "part_heads",
-    )(at, keys, values)
-
-
-def prelude_kernel(at_ref, pattern, offsets, q_ref, grad_ref, weight_ref, *refs):
-    first, key_mask, row_mask, q_theirs = refs[:4]
-    grad_s, weight_s, first_s, mask_s, row_s, q_s, sem, out_sem = refs[4:]
-    half = q_theirs.shape[1]
-    theirs = pl.ds(pl.multiple_of((1 - at_ref[0]) * half, half), half)
-    q_load = begin(q_ref.at[:, theirs], q_s, sem.at[2])
+    )(at, queries, keys, values)
+
+
+def prelude_kernel(at_ref, pattern, offsets, grad_ref, weight_ref, *refs):
+    first, key_mask, row_mask = refs[:3]
+    grad_s, weight_s, first_s, mask_s, row_s, sem, out_sem = refs[3:]
     rows, width = grad_s.shape
     block_count, glob_count = offsets.shape
     start = pl.multiple_of(at_ref[2] * width, width)
@@ -112,8 +113,7 @@
         begin(grad_ref, grad_s, sem.at[0]),
         begin(weight_ref.at[:, pl.ds(start, width)], weight_s, sem.at[1]),
     ]
-    q_load.wait()
-    stores = [begin(q_s, q_theirs, out_sem.at[3])]
+    stores = []
     own = at_ref[1] * INNER + at_ref[0]
     partner = at_ref[1] * INNER + 1 - at_ref[0]
     lane = lax.broadcasted_iota(jnp.int32, (1, HD), 1)
@@ -150,41 +150,42 @@
         store.wait()
 
 
-def prelude(at, pattern, offsets, queries, grad_own, out_weight, after):
+def prelude(at, pattern, offsets, grad_own, out_weight, after):
     rows, width = grad_own.shape
     feats = out_weight.shape[0]
     keys = offsets.shape[0] * rows
-    half = queries.shape[1] // INNER
     return call(
         prelude_kernel,
         [
             f32(feats, rows),
             bf16(keys, HD),
             f32(8, 2 * rows),
-            bf16(rows, half),
-        ],
-        [SMEM] * 3 + [ANY] * 3,
-        [ANY] * 4,
+        ],
+        [SMEM] * 3 + [ANY] * 2,
+        [ANY] * 3,
         [
             pltpu.VMEM((rows, width), jnp.bfloat16),
             pltpu.VMEM((feats, width), jnp.bfloat16),
             pltpu.VMEM((feats, rows), jnp.float32),
             pltpu.VMEM((keys, HD), jnp.bfloat16),
             pltpu.VMEM((8, 2 * rows), jnp.float32),
-            pltpu.VMEM((rows, half), jnp.bfloat16),
+            pltpu.SemaphoreType.DMA((2,)),
             pltpu.SemaphoreType.DMA((3,)),
-            pltpu.SemaphoreType.DMA((4,)),
         ],
         4,
         "prelude",
         after,
-    )(at, pattern, offsets, queries, grad_own, out_weight)
+    )(at, pattern, offsets, grad_own, out_weight)
 
 
 def forward_kernel(block_count, head_count, at_ref, q_ref, q_recv, key_mask, row_mask, *refs):
-    kv_refs, refs = refs[:block_count], refs[block_count:]
+    g_mine, g_recv = refs[:2]
+    kv_ref, refs = refs[2], refs[3:]
+    outer = block_count // INNER
     e_out, inv_out, attn_mine, attn_theirs = refs[:4]
-    q_s, mask_s, kv_s, e_s, s_ref, attn_s, inv_s, row_s, sem, kv_sem, e_sem, out_sem = refs[4:]
+    part_outs, refs = refs[4 : 4 + outer], refs[4 + outer :]
+    q_s, g_s, mask_s, kv_s, e_s, s_ref, attn_s, inv_s, row_s, part_s = refs[:10]
+    sem, kv_sem, e_sem, out_sem, part_sem = refs[10:]
     rows = q_recv.shape[0]
     feats = head_count * HD
     score_scale = HD ** (-0.5)
@@ -195,7 +196,8 @@
         begin(key_mask, mask_s, sem.at[2]),
         begin(row_mask, row_s, sem.at[3]),
     ]
-    kv_loads = [begin(kv_refs[j], kv_s.at[j], kv_sem.at[j]) for j in range(block_count)]
+    kv_loads = [begin(kv_ref.at[at_ref[SOURCES + j]], kv_s.at[j], kv_sem.at[j]) for j in range(block_count)]
+    g_loads = [begin(g_mine, g_s.at[0], sem.at[4]), begin(g_recv, g_s.at[1], sem.at[5])]
     for load in loads:
         load.wait()
     rows_low = row_s[...].astype(jnp.bfloat16)
@@ -233,30 +235,45 @@
         attn_low = (attn_t * inverse).astype(jnp.bfloat16)
         attn_s[0, cols, :] = attn_low[:, :rows]
         attn_s[1, cols, :] = attn_low[:, rows:]
-    stores.append(begin(attn_s.at[0], attn_mine, out_sem.at[0]))
-    stores.append(begin(attn_s.at[1], attn_theirs, out_sem.at[1]))
-    stores.append(begin(inv_s, inv_out, out_sem.at[2]))
+        if head == 0:
+            for load in g_loads:
+                load.wait()
+        if head == head_count - 1:
+            stores.append(begin(attn_s.at[0], attn_mine, out_sem.at[0]))
+            stores.append(begin(attn_s.at[1], attn_theirs, out_sem.at[1]))
+            stores.append(begin(inv_s, inv_out, out_sem.at[2]))
+        g_t = jnp.concatenate([g_s[0, cols, :], g_s[1, cols, :]], axis=1).astype(jnp.float32)
+        grad = jnp.transpose((g_t * inverse).astype(jnp.bfloat16))
+        for j in range(block_count):
+            keys = slice(j * rows, (j + 1) * rows)
+            part_s[j, :, cols] = product(e_s[head, keys, :], grad).astype(jnp.bfloat16)
+            if head == head_count - 1:
+                target = part_outs[j // INNER].at[j % INNER]
+                stores.append(begin(part_s.at[j], target, part_sem.at[j]))
     for store in stores:
         store.wait()
 
 
-def forward(at, queries, q_recv, key_mask, row_mask, kv_blocks, after):
-    block_count = len(kv_blocks)
+def forward(at, queries, q_recv, key_mask, row_mask, g_mine, g_recv, kv_all, after=()):
+    block_count = kv_all.shape[0]
     rows, feats = q_recv.shape
     heads = feats // HD
     keys = block_count * rows
-    return call(
+    outer = block_count // INNER
+    out = call(
         functools.partial(forward_kernel, block_count, heads),
         [
             bf16(heads, keys, 2 * rows),
             f32(max(heads, 8), 2 * rows),
             bf16(feats, rows),
             bf16(feats, rows),
-        ],
-        [SMEM] + [ANY] * (4 + block_count),
-        [ANY] * 4,
+        ]
+        + [bf16(INNER, rows, feats)] * outer,
+        [SMEM] + [ANY] * 7,
+        [ANY] * (4 + outer),
         [
             pltpu.VMEM((2, rows, feats), jnp.bfloat16),
+            pltpu.VMEM((2, feats, rows), jnp.bfloat16),
             pltpu.VMEM((keys, HD), jnp.bfloat16),
             pltpu.VMEM((block_count, rows, 2 * feats), jnp.bfloat16),
             pltpu.VMEM((heads, keys, 2 * rows), jnp.bfloat16),
@@ -264,26 +281,29 @@
             pltpu.VMEM((2, feats, rows), jnp.bfloat16),
             pltpu.VMEM((max(heads, 8), 2 * rows), jnp.float32),
             pltpu.VMEM((8, 2 * rows), jnp.float32),
-            pltpu.SemaphoreType.DMA((4,)),
+            pltpu.VMEM((block_count, rows, feats), jnp.bfloat16),
+            pltpu.SemaphoreType.DMA((6,)),
             pltpu.SemaphoreType.DMA((block_count,)),
             pltpu.SemaphoreType.DMA((heads * block_count,)),
             pltpu.SemaphoreType.DMA((3,)),
-        ],
-        6,
+            pltpu.SemaphoreType.DMA((block_count,)),
+        ],
+        8,
         "forward",
         after,
-    )(at, queries, q_recv, key_mask, row_mask, *kv_blocks)
-
-
-def backward_kernel(block_count, head_count, at_ref, *refs):
-    q_ref, q_recv, g_mine, g_recv, attn_mine, attn_theirs, inv_ref, e_ref = refs[:8]
-    kv_refs, refs = refs[8 : 8 + block_count], refs[8 + block_count :]
+    )(at, queries, q_recv, key_mask, row_mask, g_mine, g_recv, kv_all)
+    return out[0], out[1], out[2], out[3], out[4:]
+
+
+def key_terms_kernel(block_count, at_ref, q_ref, q_recv, g_mine, g_recv, attn_mine, attn_theirs, *refs):
+    inv_ref, e_ref = refs[:2]
+    kv_ref, refs = refs[2], refs[3:]
+    outer = block_count // INNER
     dq_mine, dq_theirs = refs[:2]
-    outer = block_count // INNER
     part_outs, refs = refs[2 : 2 + outer], refs[2 + outer :]
     q_s, t_s, inv_s, kv_s, e_s, part_s, dq_s, sem, kv_sem, e_sem, part_sem, dq_sem = refs
-    rows = q_recv.shape[0]
-    feats = head_count * HD
+    rows, feats = q_recv.shape
+    head_count = feats // HD
     score_scale = HD ** (-0.5)
     mine = pl.ds(pl.multiple_of(at_ref[0] * feats, feats), feats)
     loads = [begin(q_ref.at[:, mine], q_s.at[0], sem.at[0]), begin(q_recv, q_s.at[1], sem.at[1])]
@@ -293,7 +313,7 @@
     kv_loads, e_loads, stores = [], {}, []
     for j in range(block_count):
         keys = slice(j * rows, (j + 1) * rows)
-        kv_loads.append(begin(kv_refs[j], kv_s.at[j], kv_sem.at[j]))
+        kv_loads.append(begin(kv_ref.at[at_ref[SOURCES + j]], kv_s.at[j], kv_sem.at[j]))
         for head in range(head_count):
             e_loads[head, j] = begin(
                 e_ref.at[head, keys], e_s.at[head, keys], e_sem.at[head * block_count + j]
@@ -308,7 +328,6 @@
         attn_t = jnp.concatenate([t_s[2, cols, :], t_s[3, cols, :]], axis=1)
         row_dot = jnp.sum(g_t * attn_t.astype(jnp.float32), axis=0, keepdims=True) * inverse
         g_t = (g_t * inverse).astype(jnp.bfloat16)
-        grad = jnp.transpose(g_t)
         query = jnp.concatenate([q_s[0, :, cols], q_s[1, :, cols]], axis=0)
         dq_t = jnp.zeros((HD, 2 * rows), jnp.float32)
         for j in range(block_count):
@@ -316,14 +335,15 @@
             if head == 0:
                 kv_loads[j].wait()
             e_loads[head, j].wait()
-            low = e_s[head, keys, :]
             dprobs = product(kv_s[j, :, vcols], g_t)
-            dscore = (low.astype(jnp.float32) * (dprobs - row_dot)).astype(jnp.bfloat16)
+            dscore = (e_s[head, keys, :].astype(jnp.float32) * (dprobs - row_dot)).astype(
+                jnp.bfloat16
+            )
             dq_t = dq_t + product(jnp.transpose(kv_s[j, :, cols]), dscore)
             part_s[j, :, cols] = (score_scale * product(dscore, query)).astype(jnp.bfloat16)
-            part_s[j, :, vcols] = product(low, grad).astype(jnp.bfloat16)
             if head == head_count - 1:
-                stores.append(begin(part_s.at[j], part_outs[j // INNER].at[j % INNER], part_sem.at[j]))
+                target = part_outs[j // INNER].at[j % INNER]
+                stores.append(begin(part_s.at[j], target, part_sem.at[j]))
         dquery = (score_scale * jnp.transpose(dq_t)).astype(jnp.bfloat16)
         dq_s[0, :, cols] = dquery[:rows]
         dq_s[1, :, cols] = dquery[rows:]
@@ -333,23 +353,24 @@
         store.wait()
 
 
-def backward(at, queries, q_recv, g_mine, g_recv, attn_mine, attn_theirs, inverse, weights, kv_blocks):
-    block_count = len(kv_blocks)
+def key_terms(at, queries, q_recv, g_mine, g_recv, attn_mine, attn_theirs, inverse, weights, kv_all, after):
+    block_count = kv_all.shape[0]
     rows, feats = q_recv.shape
     heads = feats // HD
     keys = block_count * rows
+    outer = block_count // INNER
     out = call(
-        functools.partial(backward_kernel, block_count, heads),
-        [bf16(rows, feats)] * 2 + [bf16(INNER, rows, 2 * feats)] * (block_count // INNER),
-        [SMEM] + [ANY] * (8 + block_count),
-        [ANY] * (2 + block_count // INNER),
+        functools.partial(key_terms_kernel, block_count),
+        [bf16(rows, feats)] * 2 + [bf16(INNER, rows, feats)] * outer,
+        [SMEM] + [ANY] * 9,
+        [ANY] * (2 + outer),
         [
             pltpu.VMEM((2, rows, feats), jnp.bfloat16),
             pltpu.VMEM((4, feats, rows), jnp.bfloat16),
             pltpu.VMEM(inverse.shape, jnp.float32),
             pltpu.VMEM((block_count, rows, 2 * feats), jnp.bfloat16),
             pltpu.VMEM((heads, keys, 2 * rows), jnp.bfloat16),
-            pltpu.VMEM((block_count, rows, 2 * feats), jnp.bfloat16),
+            pltpu.VMEM((block_count, rows, feats), jnp.bfloat16),
             pltpu.VMEM((2, rows, feats), jnp.bfloat16),
             pltpu.SemaphoreType.DMA((7,)),
             pltpu.SemaphoreType.DMA((block_count,)),
@@ -357,13 +378,14 @@
             pltpu.SemaphoreType.DMA((block_count,)),
             pltpu.SemaphoreType.DMA((2,)),
         ],
-        8,
-        "backward",
-    )(at, queries, q_recv, g_mine, g_recv, attn_mine, attn_theirs, inverse, weights, *kv_blocks)
+        7,
+        "key_terms",
+        after,
+    )(at, queries, q_recv, g_mine, g_recv, attn_mine, attn_theirs, inverse, weights, kv_all)
     return out[0], out[1], out[2:]
 
 
-def grad_heads_kernel(part_count, sends, picked, at_ref, first_ref, weight_ref, *refs):
+def grad_heads_kernel(part_count, sends, picked, columns_at, send_at, at_ref, first_ref, weight_ref, *refs):
     grads, refs = refs[:part_count], refs[part_count:]
     outs, refs = refs[: 2 + sends], refs[2 + sends :]
     first_s, grad_s, weight_s, out_s, first_sem, weight_sem, grad_sem, send_sem, out_sem = refs
@@ -374,7 +396,7 @@
     for k in range(part_count):
         grad_loads.append(begin(grads[k], grad_s.at[k], grad_sem.at[k]))
         if k:
-            start = pl.multiple_of(at_ref[k] * width, width)
+            start = pl.multiple_of(at_ref[columns_at + k - 1] * width, width)
             columns = weight_ref.at[:, pl.ds(start, width)]
             weight_loads.append(begin(columns, weight_s.at[k - 1], weight_sem.at[k - 1]))
     for load in grad_loads:
@@ -386,7 +408,7 @@
             target = outs[2 + send].at[:, i * width : (i + 1) * width]
             for k in range(part_count):
 
-                @pl.when(at_ref[part_count + place] == k)
+                @pl.when(at_ref[send_at + place] == k)
                 def _():
                     begin(grad_s.at[k], target, send_sem.at[place])
 
@@ -405,13 +427,13 @@
         copy.wait()
 
 
-def grad_heads(at, first, out_weight, grads, sends, picked):
+def grad_heads(at, columns_at, send_at, first, out_weight, grads, sends, picked):
     feats, rows = first.shape
     half = feats // INNER
     count = len(grads)
     width = grads[0].shape[1]
     out = call(
-        functools.partial(grad_heads_kernel, count, sends, picked),
+        functools.partial(grad_heads_kernel, count, sends, picked, columns_at, send_at),
         [bf16(half, rows), bf16(half, rows)] + [bf16(rows, picked * width)] * sends,
         [SMEM] + [ANY] * (2 + count),
         [ANY] * (2 + sends),
@@ -432,7 +454,7 @@
     return out[0], out[1], out[2:]
 
 
-def weight_kernel(part_count, picked, doc_count, sent, at_ref, *refs):
+def weight_kernel(part_count, doc_count, sent, step_at, at_ref, *refs):
     attn, refs = refs[: INNER * doc_count], refs[INNER * doc_count :]
     grads, refs = refs[:part_count], refs[part_count:]
     swapped, refs = refs[: doc_count - 1], refs[doc_count - 1 :]
@@ -451,7 +473,7 @@
             attn_loads.append(begin(attn[index], target, attn_sem.at[index]))
     for k in range(outer):
         place = lax.rem(at_ref[1] + k, outer) * INNER + here
-        which = at_ref[2 + place // pieces]
+        which = at_ref[step_at + place // pieces]
         cols = pl.ds(pl.multiple_of(lax.rem(place, pieces) * width, width), width)
         for i in range(part_count):
 
@@ -479,13 +501,13 @@
         store.wait()
 
 
-def weight_terms(at, attn, grads, swapped, outer, picked, sent, after=()):
+def weight_terms(at, step_at, attn, grads, swapped, outer, picked, sent, after=()):
     half, rows = attn[0].shape
     feats = half * INNER
     doc_count = len(attn) // INNER
     width = picked * grads[0].shape[1] // (outer * INNER)
     return call(
-        functools.partial(weight_kernel, len(grads), picked, doc_count, sent),
+        functools.partial(weight_kernel, len(grads), doc_count, sent, step_at),
         bf16(outer, feats, width),
         [SMEM] + [ANY] * (len(attn) + len(grads) + len(swapped)),
         ANY,
@@ -540,44 +562,45 @@
 
 
 def add_kernel(count, *refs):
-    terms, (mine, theirs) = refs[:count], refs[count : count + 2]
-    terms_s, out_s, term_sem, out_sem = refs[count + 2 :]
-    loads = [
-        begin(terms[c].at[side], terms_s.at[c, side], term_sem.at[c * INNER + side])
-        for side in (1, 0)
-        for c in range(count)
-    ]
+    terms, (mine, theirs) = refs[: 2 * count], refs[2 * count : 2 * count + 2]
+    terms_s, out_s, term_sem, out_sem = refs[2 * count + 2 :]
+    half = terms[0].shape[2]
+    loads = {}
+    for side in (1, 0):
+        for c, held in enumerate(terms):
+            sem = term_sem.at[c * INNER + side]
+            loads[side, c] = begin(held.at[side], terms_s.at[c, side], sem)
     stores = []
-    for index, (side, out) in enumerate(((1, theirs), (0, mine))):
-        for load in loads[index * count : (index + 1) * count]:
-            load.wait()
-        summed = terms_s[0, side].astype(jnp.float32)
-        for c in range(1, count):
-            summed = summed + terms_s[c, side].astype(jnp.float32)
-        out_s[side] = summed.astype(jnp.bfloat16)
+    for side, out in ((1, theirs), (0, mine)):
+        for kind in range(2):
+            summed = 0.0
+            for c in range(kind * count, (kind + 1) * count):
+                loads[side, c].wait()
+                summed = summed + terms_s[c, side].astype(jnp.float32)
+            out_s[side, :, kind * half : (kind + 1) * half] = summed.astype(jnp.bfloat16)
         stores.append(begin(out_s.at[side], out, out_sem.at[side]))
     for store in stores:
         store.wait()
 
 
-def add_terms(terms, after):
-    _, rows, width = terms[0].shape
-    count = len(terms)
+def add_terms(key_parts, value_parts, after):
+    _, rows, half = key_parts[0].shape
+    count = len(key_parts)
     return call(
         functools.partial(add_kernel, count),
-        [bf16(rows, width)] * 2,
-        [ANY] * count,
+        [bf16(rows, 2 * half)] * 2,
+        [ANY] * (2 * count),
         [ANY] * 2,
         [
-            pltpu.VMEM((count, INNER, rows, width), jnp.bfloat16),
-            pltpu.VMEM((INNER, rows, width), jnp.bfloat16),
-            pltpu.SemaphoreType.DMA((count * INNER,)),
+            pltpu.VMEM((2 * count, INNER, rows, half), jnp.bfloat16),
+            pltpu.VMEM((INNER, rows, 2 * half), jnp.bfloat16),
+            pltpu.SemaphoreType.DMA((2 * count * INNER,)),
             pltpu.SemaphoreType.DMA((INNER,)),
         ],
         2,
         "add_terms",
         after,
-    )(*terms)
+    )(*key_parts, *value_parts)
 
 
 def join_kernel(at_ref, dq_mine, dq_recv, mine, recv, *refs):
@@ -650,31 +673,27 @@
     sources = [
         ((outer_at - step) % outer) * INNER + (inner_at + side) % INNER for step, side in routes
     ]
-    at = jnp.stack([inner_at, outer_at, tp_at] + sources)
-    columns_at = [(tp_at + step) % tp_count for step in range(1, tp_count)]
+    scalars = [inner_at, outer_at, tp_at] + sources
+    columns_at = len(scalars)
+    scalars = scalars + [(tp_at + step) % tp_count for step in range(1, tp_count)]
+    send_at = len(scalars)
     for step in range(1, dp_count):
-        columns_at = columns_at + dp_steps((dp_at + step) % dp_count)
-    columns_at = jnp.stack([inner_at] + columns_at)
-    weight_at = jnp.stack([inner_at, outer_at] + dp_steps(dp_at))
+        scalars = scalars + dp_steps((dp_at + step) % dp_count)
+    keep_at = len(scalars)
+    at = jnp.stack(scalars + dp_steps(dp_at))
 
     grad_own = grad_output[0]
     grads = [grad_own] + [
         lax.ppermute(grad_own, "tp", shift_pairs(tp_count, -step)) for step in range(1, tp_count)
     ]
-    kv_mine, kv_theirs = part_heads(at, key_heads[0], value_heads[0])
-    kv_recv = lax.ppermute(kv_theirs, "ctx", ctx_pairs(0, 1))
-    kv_blocks = [
-        lax.ppermute(kv_recv if side else kv_mine, "ctx", ctx_pairs(step, 0))
-        if step
-        else (kv_recv if side else kv_mine)
-        for step, side in routes
-    ]
-    first, key_mask, row_mask, q_theirs = prelude(
-        at, block_pattern, global_offsets, queries[0], grad_own, out_weight, (kv_recv,)
-    )
+    kv_send, q_theirs = part_heads(at, queries[0], key_heads[0], value_heads[0], ctx_count)
+    kv_all = lax.all_to_all(kv_send, "ctx", split_axis=0, concat_axis=0, tiled=True)
     q_recv = lax.ppermute(q_theirs, "ctx", ctx_pairs(0, 1))
+    first, key_mask, row_mask = prelude(
+        at, block_pattern, global_offsets, grad_own, out_weight, (q_theirs,)
+    )
     g_mine, g_theirs, grad_sends = grad_heads(
-        columns_at, first, out_weight, grads, dp_count - 1, picked
+        at, columns_at, send_at, first, out_weight, grads, dp_count - 1, picked
     )
     g_recv = lax.ppermute(g_theirs, "ctx", ctx_pairs(0, 1))
     swapped = [
@@ -682,8 +701,8 @@
         for step, send in enumerate(grad_sends)
     ]
 
-    weights, inverse, attn_mine, attn_theirs = forward(
-        at, queries[0], q_recv, key_mask, row_mask, kv_blocks, (g_theirs,)
+    weights, inverse, attn_mine, attn_theirs, value_parts = forward(
+        at, queries[0], q_recv, key_mask, row_mask, g_mine, g_recv, kv_all
     )
 
     attn = []
@@ -693,17 +712,21 @@
             axes = ("dp", "ctx") if step else "ctx"
             attn.append(lax.ppermute(held, axes, pairs) if step or side else held)
 
-    dq_mine, dq_theirs, parts = backward(
-        at, queries[0], q_recv, g_mine, g_recv, attn_mine, attn_theirs, inverse, weights, kv_blocks
-    )
-    send = weight_terms(weight_at, attn, grads, swapped, outer, picked, True, (dq_mine,))
+    def returned(parts):
+        return [
+            lax.ppermute(part, "ctx", ctx_pairs(-step, 0)) if step else part
+            for step, part in enumerate(parts)
+        ]
+
+    value_parts = returned(value_parts)
+    send = weight_terms(at, keep_at, attn, grads, swapped, outer, picked, True)
     weight_recv = lax.ppermute(send, "ctx", ctx_pairs(0, 1))
-    terms = [
-        lax.ppermute(part, "ctx", ctx_pairs(-step, 0)) if step else part
-        for step, part in enumerate(parts)
-    ]
+    dq_mine, dq_theirs, key_parts = key_terms(
+        at, queries[0], q_recv, g_mine, g_recv, attn_mine, attn_theirs, inverse, weights, kv_all, (send,)
+    )
+    key_parts = returned(key_parts)
     dq_recv = lax.ppermute(dq_theirs, "ctx", ctx_pairs(0, 1))
-    keep = weight_terms(weight_at, attn, grads, swapped, outer, picked, False, (send,))
+    keep = weight_terms(at, keep_at, attn, grads, swapped, outer, picked, False, (dq_mine, *value_parts[1:]))
     weight_sums = weight_add(keep, weight_recv)
     grad_weight = weight_sums[0].astype(jnp.float32)
     for step in range(1, outer):
@@ -711,7 +734,7 @@
             weight_sums[step], "ctx", ctx_pairs(step, 0)
         ).astype(jnp.float32)
 
-    terms_mine, terms_theirs = add_terms(terms, (weight_sums[0],))
+    terms_mine, terms_theirs = add_terms(key_parts, value_parts, (weight_sums[0],))
     terms_recv = lax.ppermute(terms_theirs, "ctx", ctx_pairs(0, 1))
     grad_q, grad_k, grad_v = join_heads(at, dq_mine, dq_recv, terms_mine, terms_recv)
     return grad_q[None], grad_k[None], grad_v[None], grad_weight.astype(jnp.bfloat16)

time: 104 us -> 107 us (1.029)
  waiting for transfers between devices: 26.6 us -> 28.3 us
  starting transfers between devices: 28.5 us -> 30.1 us
  other arithmetic: 2.03 us -> 0.72 us
    ppermute x1, waiting for transfers between devices: 0.63 us -> 18.1 us  [per_device(): lax.ppermute(grad_own, 'tp', shift_pairs(tp_count, -step))]
    ppermute x10 -> x6, waiting for transfers between devices: 16.7 us -> 3.01 us  [returned(): lax.ppermute(part, 'ctx', ctx_pairs(-step, 0))]
    all_to_all x0 -> x1, starting transfers between devices: none -> 7.4 us  [per_device(): lax.all_to_all(kv_send, 'ctx', split_axis=0, concat_axis=0, tiled=True)]
    ppermute x10 -> x6, starting transfers between devices: 15.3 us -> 9.77 us  [returned(): lax.ppermute(part, 'ctx', ctx_pairs(-step, 0))]
    ppermute x1, waiting for transfers between devices: 5.35 us -> 0.01 us  [per_device(): weight_recv = lax.ppermute(send, 'ctx', ctx_pairs(0, 1))]
    ppermute x1, waiting for transfers between devices: 0.01 us -> 2.41 us  [per_device(): q_recv = lax.ppermute(q_theirs, 'ctx', ctx_pairs(0, 1))]
    ppermute x1, waiting for transfers between devices: 0.01 us -> 1.71 us  [per_device(): g_recv = lax.ppermute(g_theirs, 'ctx', ctx_pairs(0, 1))]
    ppermute x1, waiting for transfers between devices: 2.27 us -> 0.8 us  [per_device(): terms_recv = lax.ppermute(terms_theirs, 'ctx', ctx_pairs(0, 1))]
  transfers between devices with their start and end apart: 23 -> 20, of which waited for: 7 -> 7; matrix products, arithmetic and copies ran while one was open for 3% -> 1% of each run, Pallas kernels for 31% -> 32%
where the time goes in v7:
time: 107 us
  Pallas kernels  39.5 us (37%)
  starting transfers between devices  30.1 us (28%)
  waiting for transfers between devices  28.3 us (26%)
  local copies, waits for them, and re-layouts  7.08 us (7%)
    pallas_call x10, Pallas kernels, placed(): return run(*args)  39.5 us
    ppermute x1, waiting for transfers between devices, per_device(): lax.ppermute(grad_own, 'tp', shift_pairs(tp_count, -step))  18.1 us
    ppermute x6, starting transfers between devices, returned(): lax.ppermute(part, 'ctx', ctx_pairs(-step, 0))  9.77 us
    all_to_all x1, starting transfers between devices, per_device(): lax.all_to_all(kv_send, 'ctx', split_axis=0, concat_axis=0, tiled=True)  7.4 us
    unnamed x43, local copies, waits for them, and re-layouts  6.4 us
    ppermute x3, starting transfers between devices, per_device(): lax.ppermute(weight_sums[step], 'ctx', ctx_pairs(step, 0))  3.63 us
    ppermute x6, waiting for transfers between devices, returned(): lax.ppermute(part, 'ctx', ctx_pairs(-step, 0))  3.01 us
    ppermute x1, waiting for transfers between devices, per_device(): q_recv = lax.ppermute(q_theirs, 'ctx', ctx_pairs(0, 1))  2.41 us
  transfers between devices with their start and end apart: 20, of which 7 were waited for; matrix products, arithmetic and copies ran while one was open for 1% of the time, Pallas kernels for 32%

profile of v7, /device:TPU:0, one launch (start us, length us, event | category | flops | bytes accessed | tf_op | source)
XLA Modules:
  0.0 106.7 jit_solution(6510816053634690885)
XLA Ops:
  0.8 0.7 stack.59.refs_0_.refs_1_.refs_4_
  1.5 2.8 %part_heads.1 = (bf16[8,256,256]{2,1,0:T(8,128)(2,1)}, bf16[256,128]{1,0:T(8,128)(2,1)}) custom-call(s32[14]{0:T(128)} %stack.59.refs_0_.refs_1_.refs_4_, bf16[256,256]{1,0:T(8,128)(2,1)} %bitcast.28, bf16[256,256]{1,0:T(8,128)(2,1)} %bitcast.26, bf16[256,256]{1,0:T(8,128)(2,1)} %bitcast.27), custom_call_target="tpu_custom_call" | custom-call | flops 2000000000 | bytes 6000000 | tf_op jit(solution)/shard_map/part_heads/pallas_call | solution.py:56
  4.2 0.0 copy-start.3
  4.3 0.0 copy-start.2
  4.3 7.4 %all-to-all-start = ((bf16[8,256,256]{2,1,0:T(8,128)(2,1)}), bf16[8,256,256]{2,1,0:T(8,128)(2,1)S(1)}, u32[]{:S(2)}, u32[]{:S(2)}) async-start(bf16[8,256,256]{2,1,0:T(8,128)(2,1)} %get-tuple-element.41), calls=%async_computation | async-start | bytes 2097152 | tf_op jit(solution)/shard_map/all_to_all | solution.py:690
  11.7 1.6 %collective-permute-start.1 = (bf16[256,2048]{1,0:T(8,128)(2,1)S(1)}, bf16[256,2048]{1,0:T(8,128)(2,1)S(1)}, u32[]{:S(2)}, u32[]{:S(2)}) collective-permute-start(bf16[256,2048]{1,0:T(8,128)(2,1)S(1)} %bitcast.25), channel_id=1, source_target_pairs={{0,1},{1,0},{2,3},{3,2},{4,5},{5,4},{6,7},{7,6},{8,9},{9,8},{10,11... | collective-permute-start | bytes 3145736 | tf_op jit(solution)/shard_map/ppermute | solution.py:687
  13.3 0.7 copy.11.refs_2_
  13.9 4.3 %prelude.1 = (f32[256,256]{1,0:T(8,128)}, bf16[2048,128]{1,0:T(8,128)(2,1)}, f32[8,512]{1,0:T(8,128)}) custom-call(bf16[256,128]{1,0:T(8,128)(2,1)} %get-tuple-element.35.refs_0_, s32[14]{0:T(128)} %stack.59.refs_0_.refs_1_.refs_4_, s32[8,3]{1,0:T(8,128)} %copy.11.refs_2_, s32[8,8]{1,0:T(8,128)} %refs_3_.1, bf16[256,2048]{1,0:T(8,128)(2,1)} %bitcast.21, ...), custom_call_target="tpu_custom_call" | custom-call | flops 4000000000 | bytes 12000000 | tf_op jit(solution)/shard_map/prelude/pallas_call | solution.py:56
  18.2 18.1 %collective-permute-done.1.refs_4_.refs_6_.refs_10_ = bf16[256,2048]{1,0:T(8,128)(2,1)S(1)} collective-permute-done((bf16[256,2048]{1,0:T(8,128)(2,1)S(1)}, bf16[256,2048]{1,0:T(8,128)(2,1)S(1)}, u32[]{:S(2)}, u32[]{:S(2)}) %collective-permute-start.1) | collective-permute-done | bytes 1048608 | tf_op jit(solution)/shard_map/ppermute | solution.py:687
  36.4 1.0 copy-done.4
  37.3 3.9 %grad_heads.1 = (bf16[128,256]{1,0:T(8,128)(2,1)}, bf16[128,256]{1,0:T(8,128)(2,1)}, bf16[256,2048]{1,0:T(8,128)(2,1)}) custom-call(s32[14]{0:T(128)} %stack.59.refs_0_.refs_1_.refs_4_, f32[256,256]{1,0:T(8,128)} %get-tuple-element.38.refs_1_, bf16[256,4096]{1,0:T(8,128)(2,1)} %refs_2_.2, bf16[256,2048]{1,0:T(8,128)(2,1)} %bitcast.22, ...), custom_call_target="tpu_custom_call" | custom-call | flops 3000000000 | bytes 9000000 | tf_op jit(solution)/shard_map/grad_heads/pallas_call | solution.py:56
  41.2 0.1 collective-permute-start.6
  41.3 1.7 %collective-permute-start = (bf16[256,128]{1,0:T(8,128)(2,1)S(1)}, bf16[256,128]{1,0:T(8,128)(2,1)S(1)}, u32[]{:S(2)}, u32[]{:S(2)}) collective-permute-start(bf16[256,128]{1,0:T(8,128)(2,1)S(1)} %copy-done.20), channel_id=1, source_target_pairs={{0,2},{2,0},{4,6},{6,4},{8,10},{10,8},{12,14},{14,12},{1,3},{3,1},... | collective-permute-start | bytes 196616 | tf_op jit(solution)/shard_map/ppermute | solution.py:691
  43.1 0.4 collective-permute-start.2
  43.4 2.4 %collective-permute-done.refs_2_.refs_3_ = bf16[256,128]{1,0:T(8,128)(2,1)S(1)} collective-permute-done((bf16[256,128]{1,0:T(8,128)(2,1)S(1)}, bf16[256,128]{1,0:T(8,128)(2,1)S(1)}, u32[]{:S(2)}, u32[]{:S(2)}) %collective-permute-start) | collective-permute-done | bytes 65568 | tf_op jit(solution)/shard_map/ppermute | solution.py:691
  45.8 1.7 %collective-permute-done.2.refs_6_.refs_5_ = bf16[128,256]{1,0:T(8,128)(2,1)S(1)} collective-permute-done((bf16[128,256]{1,0:T(8,128)(2,1)}, bf16[128,256]{1,0:T(8,128)(2,1)S(1)}, u32[]{:S(2)}, u32[]{:S(2)}) %collective-permute-start.2) | collective-permute-done | bytes 65568 | tf_op jit(solution)/shard_map/ppermute | solution.py:698
  47.6 0.0 all-to-all-done.refs_7_.refs_10_
  47.6 0.6 copy-done.18
  48.2 0.4 copy-done
  48.5 7.0 %forward.1 = (bf16[1,2048,512]{2,1,0:T(8,128)(2,1)}, f32[8,512]{1,0:T(8,128)}, bf16[128,256]{1,0:T(8,128)(2,1)}, bf16[128,256]{1,0:T(8,128)(2,1)}, bf16[2,256,12...) custom-call(s32[14]{0:T(128)} %stack.59.refs_0_.refs_1_.refs_4_, ...), custom_call_target="tpu_custom_call" | custom-call | flops 8000000000 | bytes 24000000 | tf_op jit(solution)/shard_map/forward/pallas_call | solution.py:56
  55.6 0.7 collective-permute-start.5
  56.2 0.8 collective-permute-start.3
  57.0 0.4 collective-permute-start.4
  57.5 3.3 %collective-permute-start.8 = (bf16[2,256,128]{2,1,0:T(8,128)(2,1)}, bf16[2,256,128]{2,1,0:T(8,128)(2,1)S(1)}, u32[]{:S(2)}, u32[]{:S(2)}) collective-permute-start(bf16[2,256,128]{2,1,0:T(8,128)(2,1)} %get-tuple-element.49), channel_id=1, source_target_pairs={{0,12},{2,14},{4,0},{6,2},{8,4},{10,6},{12,8},{14,10},{1,13},{3,15... | collective-permute-start | bytes 393224 | tf_op jit(solution)/shard_map/ppermute | solution.py:717
  60.7 0.0 collective-permute-done.5.refs_4_.refs_8_
  60.7 1.8 %collective-permute-start.9 = (bf16[2,256,128]{2,1,0:T(8,128)(2,1)}, bf16[2,256,128]{2,1,0:T(8,128)(2,1)S(1)}, u32[]{:S(2)}, u32[]{:S(2)}) collective-permute-start(bf16[2,256,128]{2,1,0:T(8,128)(2,1)} %get-tuple-element.50), channel_id=1, source_target_pairs={{0,8},{2,10},{4,12},{6,14},{8,0},{10,2},{12,4},{14,6},{1,9},{3,11}... | collective-permute-start | bytes 393224 | tf_op jit(solution)/shard_map/ppermute | solution.py:717
  62.6 0.0 collective-permute-done.3.refs_2_.refs_6_
  62.6 1.4 %collective-permute-start.10 = (bf16[2,256,128]{2,1,0:T(8,128)(2,1)}, bf16[2,256,128]{2,1,0:T(8,128)(2,1)S(1)}, u32[]{:S(2)}, u32[]{:S(2)}) collective-permute-start(bf16[2,256,128]{2,1,0:T(8,128)(2,1)} %get-tuple-element.51), channel_id=1, source_target_pairs={{0,4},{2,6},{4,8},{6,10},{8,12},{10,14},{12,0},{14,2},{1,5},{3,7},... | collective-permute-start | bytes 393224 | tf_op jit(solution)/shard_map/ppermute | solution.py:717
  64.0 0.0 collective-permute-done.4.refs_3_.refs_7_
  64.0 0.0 collective-permute-done.6.refs_7_.refs_11_
  64.1 0.6 copy-done.19
  64.7 1.0 copy-done.5
  65.7 3.9 %weight_sent.1.refs_0_ = bf16[4,256,256]{2,1,0:T(8,128)(2,1)} custom-call(s32[14]{0:T(128)} %stack.59.refs_0_.refs_1_.refs_4_, bf16[128,256]{1,0:T(8,128)(2,1)} %get-tuple-element.42.refs_1_.refs_6_.refs_5_, bf16[128,256]{1,0:T(8,128)(2,1)} %copy-done.17, bf16[128,256]{1,0:T(8,128)(2,1)} %copy-done.19, bf16[128,256]{1,0:T(8,128)(2,1)} %copy-done.15, ...), custom_call_target="tpu_custom_call" | custom-call | flops 3000000000 | bytes 9000000 | tf_op jit(solution)/shard_map/weight_sent/pallas_call | solution.py:56
  69.6 1.4 %collective-permute-start.11 = (bf16[4,256,256]{2,1,0:T(8,128)(2,1)}, bf16[4,256,256]{2,1,0:T(8,128)(2,1)S(1)}, u32[]{:S(2)}, u32[]{:S(2)}) collective-permute-start(bf16[4,256,256]{2,1,0:T(8,128)(2,1)} %weight_sent.1.refs_0_), channel_id=1, source_target_pairs={{0,2},{2,0},{4,6},{6,4},{8,10},{10,8},{12,14},{14,12},{1,3},{3,1},... | collective-permute-start | bytes 1572872 | tf_op jit(solution)/shard_map/ppermute | solution.py:723
  71.0 7.1 %key_terms.1 = (bf16[256,128]{1,0:T(8,128)(2,1)}, bf16[256,128]{1,0:T(8,128)(2,1)}, bf16[2,256,128]{2,1,0:T(8,128)(2,1)}, bf16[2,256,128]{2,1,0:T(8,128)(2,1)}, ...) custom-call(bf16[4,256,256]{2,1,0:T(8,128)(2,1)} %weight_sent.1.refs_0_, s32[14]{0:T(128)} %stack.59.refs_0_.refs_1_.refs_4_, ...), custom_call_target="tpu_custom_call" | custom-call | flops 7000000000 | bytes 21000000 | tf_op jit(solution)/shard_map/key_terms/pallas_call | solution.py:56
  78.1 0.7 collective-permute-start.7
  78.8 0.0 collective-permute-done.8.refs_1_.refs_6_
  78.8 2.4 %collective-permute-start.12 = (bf16[2,256,128]{2,1,0:T(8,128)(2,1)}, bf16[2,256,128]{2,1,0:T(8,128)(2,1)S(1)}, u32[]{:S(2)}, u32[]{:S(2)}) collective-permute-start(bf16[2,256,128]{2,1,0:T(8,128)(2,1)} %get-tuple-element.54), channel_id=1, source_target_pairs={{0,12},{2,14},{4,0},{6,2},{8,4},{10,6},{12,8},{14,10},{1,13},{3,15... | collective-permute-start | bytes 393224 | tf_op jit(solution)/shard_map/ppermute | solution.py:717
  81.2 0.0 collective-permute-done.9.refs_2_.refs_7_
  81.2 0.0 collective-permute-start.13
  81.2 0.0 collective-permute-done.10.refs_3_.refs_8_
  81.2 0.0 copy-start.9
  81.2 0.9 collective-permute-start.14
  82.1 3.9 %weight_kept.1.refs_0_ = bf16[4,256,256]{2,1,0:T(8,128)(2,1)} custom-call(bf16[256,128]{1,0:T(8,128)(2,1)} %get-tuple-element.47.refs_0_.refs_1_, bf16[2,256,128]{2,1,0:T(8,128)(2,1)} %copy-done.7, bf16[2,256,128]{2,1,0:T(8,128)(2,1)} %copy-done.8, bf16[2,256,128]{2,1,0:T(8,128)(2,1)} %copy-done.9, s32[14]{0:T(128)} %stack.59.refs_0_.refs_1_.refs_4_, ...), custom_call_target="tpu_custom_call" | custom-call | flops 3000000000 | bytes 9000000 | tf_op jit(solution)/shard_map/weight_kept/pallas_call | solution.py:56
  86.0 0.8 copy-done.6
  86.8 2.1 %weight_add.1 = (bf16[256,256]{1,0:T(8,128)(2,1)}, bf16[256,256]{1,0:T(8,128)(2,1)}, bf16[256,256]{1,0:T(8,128)(2,1)}, bf16[256,256]{1,0:T(8,128)(2,1)}) custom-call(bf16[4,256,256]{2,1,0:T(8,128)(2,1)} %weight_kept.1.refs_0_, bf16[4,256,256]{2,1,0:T(8,128)(2,1)} %copy-done.6), custom_call_target="tpu_custom_call" | custom-call | flops 1500000000 | bytes 4500000 | tf_op jit(solution)/shard_map/weight_add/pallas_call | solution.py:56
  88.9 2.7 %collective-permute-start.16 = (bf16[256,256]{1,0:T(8,128)(2,1)}, bf16[256,256]{1,0:T(8,128)(2,1)S(1)}, u32[]{:S(2)}, u32[]{:S(2)}) collective-permute-start(bf16[256,256]{1,0:T(8,128)(2,1)} %get-tuple-element.63), channel_id=1, source_target_pairs={{0,4},{2,6},{4,8},{6,10},{8,12},{10,14},{12,0},{14,2},{1,5},{3,7},... | collective-permute-start | bytes 393224 | tf_op jit(solution)/shard_map/ppermute | solution.py:733
  91.5 0.0 collective-permute-done.12.refs_2_
  91.5 1.0 collective-permute-start.17
  92.5 3.0 %collective-permute-done.13.refs_3_ = bf16[2,256,128]{2,1,0:T(8,128)(2,1)S(1)} collective-permute-done((bf16[2,256,128]{2,1,0:T(8,128)(2,1)}, bf16[2,256,128]{2,1,0:T(8,128)(2,1)S(1)}, u32[]{:S(2)}, u32[]{:S(2)}) %collective-permute-start.13) | collective-permute-done | bytes 131104 | tf_op jit(solution)/shard_map/ppermute | solution.py:717
  95.5 0.0 collective-permute-start.18
  95.5 0.0 collective-permute-done.14.refs_4_
  95.5 0.6 copy-done.11
  96.2 0.1 copy-done.12
  96.2 2.1 %add_terms.1 = (bf16[256,256]{1,0:T(8,128)(2,1)}, bf16[256,256]{1,0:T(8,128)(2,1)}) custom-call(bf16[256,256]{1,0:T(8,128)(2,1)} %get-tuple-element.52.refs_0_, bf16[2,256,128]{2,1,0:T(8,128)(2,1)} %get-tuple-element.53.refs_1_, bf16[2,256,128]{2,1,0:T(8,128)(2,1)} %copy-done.10, bf16[2,256,128]{2,1,0:T(8,128)(2,1)} %copy-done.11, ...), custom_call_target="tpu_custom_call" | custom-call | flops 2000000000 | bytes 6000000 | tf_op jit(solution)/shard_map/add_terms/pallas_call | solution.py:56
  98.3 1.5 %collective-permute-start.15 = (bf16[256,256]{1,0:T(8,128)(2,1)}, bf16[256,256]{1,0:T(8,128)(2,1)S(1)}, u32[]{:S(2)}, u32[]{:S(2)}) collective-permute-start(bf16[256,256]{1,0:T(8,128)(2,1)} %get-tuple-element.59), channel_id=1, source_target_pairs={{0,2},{2,0},{4,6},{6,4},{8,10},{10,8},{12,14},{14,12},{1,3},{3,1},... | collective-permute-start | bytes 393224 | tf_op jit(solution)/shard_map/ppermute | solution.py:738
  99.8 0.0 collective-permute-done.16
  99.8 1.3 %collective-permute-done.17 = bf16[256,256]{1,0:T(8,128)(2,1)S(1)} collective-permute-done((bf16[256,256]{1,0:T(8,128)(2,1)}, bf16[256,256]{1,0:T(8,128)(2,1)S(1)}, u32[]{:S(2)}, u32[]{:S(2)}) %collective-permute-start.17) | collective-permute-done | bytes 131104 | tf_op jit(solution)/shard_map/ppermute | solution.py:733
  101.1 1.0 collective-permute-done.18
  102.0 0.7 add_convert_fusion
  102.8 0.0 collective-permute-done.7.refs_2_
  102.8 0.8 collective-permute-done.15.refs_4_
  103.6 0.6 copy-done.13
  104.2 2.5 %join_heads.1 = (bf16[256,256]{1,0:T(8,128)(2,1)}, bf16[256,256]{1,0:T(8,128)(2,1)}, bf16[256,256]{1,0:T(8,128)(2,1)}) custom-call(s32[14]{0:T(128)} %stack.59.refs_0_.refs_1_.refs_4_, bf16[256,128]{1,0:T(8,128)(2,1)} %get-tuple-element.47.refs_0_.refs_1_, bf16[256,128]{1,0:T(8,128)(2,1)} %copy-done.14, bf16[256,256]{1,0:T(8,128)(2,1)} %get-tuple-element.58.refs_3_, ...), custom_call_target="tpu_custom_call" | custom-call | flops 2000000000 | bytes 6000000 | tf_op jit(solution)/shard_map/join_heads/pallas_call | solution.py:56
  (31 shorter events, 0.1 us)
Async XLA Ops:
  4.2 7.4 %copy-start.3 = (bf16[1,256,2048]{2,1,0:T(8,128)(2,1)S(1)}, bf16[1,256,2048]{2,1,0:T(8,128)(2,1)}, u32[]{:S(2)}) copy-start(bf16[1,256,2048]{2,1,0:T(8,128)(2,1)} %param.10) | copy-start | bytes 3145732
  4.3 9.0 %copy-start.2 = (s32[8,3]{0,1:T(4,128)S(1)}, s32[8,3]{0,1:T(4,128)}, u32[]{:S(2)}) copy-start(s32[8,3]{0,1:T(4,128)} %param.12) | copy-start | bytes 292
  4.3 43.3 %all-to-all-start = ((bf16[8,256,256]{2,1,0:T(8,128)(2,1)}), bf16[8,256,256]{2,1,0:T(8,128)(2,1)S(1)}, u32[]{:S(2)}, u32[]{:S(2)}) async-start(bf16[8,256,256]{2,1,0:T(8,128)(2,1)} %get-tuple-element.41), calls=%async_computation | async-start | bytes 2097152 | tf_op jit(solution)/shard_map/all_to_all | solution.py:690
  11.7 24.7 %collective-permute-start.1 = (bf16[256,2048]{1,0:T(8,128)(2,1)S(1)}, bf16[256,2048]{1,0:T(8,128)(2,1)S(1)}, u32[]{:S(2)}, u32[]{:S(2)}) collective-permute-start(bf16[256,2048]{1,0:T(8,128)(2,1)S(1)} %bitcast.25), channel_id=1, source_target_pairs={{0,1},{1,0},{2,3},{3,2},{4,5},{5,4},{6,7},{7,6},{8,9},{9,8},{10,11... | collective-permute-start | bytes 3145736 | tf_op jit(solution)/shard_map/ppermute | solution.py:687
  36.3 1.0 copy-start.4
  37.3 4.0 %copy-start.20 = (bf16[256,128]{1,0:T(8,128)(2,1)S(1)}, bf16[256,128]{1,0:T(8,128)(2,1)}, u32[]{:S(2)}) copy-start(bf16[256,128]{1,0:T(8,128)(2,1)} %get-tuple-element.35.refs_0_) | copy-start | bytes 196612
  41.2 22.8 %collective-permute-start.6 = (bf16[256,2048]{1,0:T(8,128)(2,1)}, bf16[256,2048]{1,0:T(8,128)(2,1)S(1)}, u32[]{:S(2)}, u32[]{:S(2)}) collective-permute-start(bf16[256,2048]{1,0:T(8,128)(2,1)} %get-tuple-element.44), channel_id=1, source_target_pairs={{0,16},{16,0},{1,17},{17,1},{2,18},{18,2},{3,19},{19,3},{4,20},{20... | collective-permute-start | bytes 3145736 | tf_op jit(solution)/shard_map/ppermute | solution.py:700
  41.3 4.5 %collective-permute-start = (bf16[256,128]{1,0:T(8,128)(2,1)S(1)}, bf16[256,128]{1,0:T(8,128)(2,1)S(1)}, u32[]{:S(2)}, u32[]{:S(2)}) collective-permute-start(bf16[256,128]{1,0:T(8,128)(2,1)S(1)} %copy-done.20), channel_id=1, source_target_pairs={{0,2},{2,0},{4,6},{6,4},{8,10},{10,8},{12,14},{14,12},{1,3},{3,1},... | collective-permute-start | bytes 196616 | tf_op jit(solution)/shard_map/ppermute | solution.py:691
  43.1 4.5 %collective-permute-start.2 = (bf16[128,256]{1,0:T(8,128)(2,1)}, bf16[128,256]{1,0:T(8,128)(2,1)S(1)}, u32[]{:S(2)}, u32[]{:S(2)}) collective-permute-start(bf16[128,256]{1,0:T(8,128)(2,1)} %get-tuple-element.40), channel_id=1, source_target_pairs={{0,2},{2,0},{4,6},{6,4},{8,10},{10,8},{12,14},{14,12},{1,3},{3,1},... | collective-permute-start | bytes 196616 | tf_op jit(solution)/shard_map/ppermute | solution.py:698
  45.8 1.7 %copy-start.16 = (bf16[256,128]{1,0:T(8,128)(2,1)}, bf16[256,128]{1,0:T(8,128)(2,1)S(1)}, u32[]{:S(2)}) copy-start(bf16[256,128]{1,0:T(8,128)(2,1)S(1)} %collective-permute-done.refs_2_.refs_3_) | copy-start | bytes 196612
  47.5 0.6 copy-start.18
  47.6 1.0 copy-start
  55.6 5.2 %collective-permute-start.5 = (bf16[128,256]{1,0:T(8,128)(2,1)}, bf16[128,256]{1,0:T(8,128)(2,1)S(1)}, u32[]{:S(2)}, u32[]{:S(2)}) collective-permute-start(bf16[128,256]{1,0:T(8,128)(2,1)} %get-tuple-element.43.refs_7_), channel_id=1, source_target_pairs={{0,18},{2,16},{4,22},{6,20},{8,26},{10,24},{12,30},{14,28},{16,2},... | collective-permute-start | bytes 196616 | tf_op jit(solution)/shard_map/ppermute | solution.py:713
  56.2 6.4 %collective-permute-start.3 = (bf16[128,256]{1,0:T(8,128)(2,1)}, bf16[128,256]{1,0:T(8,128)(2,1)S(1)}, u32[]{:S(2)}, u32[]{:S(2)}) collective-permute-start(bf16[128,256]{1,0:T(8,128)(2,1)} %get-tuple-element.43.refs_7_), channel_id=1, source_target_pairs={{0,2},{2,0},{4,6},{6,4},{8,10},{10,8},{12,14},{14,12},{1,3},{3,1},... | collective-permute-start | bytes 196616 | tf_op jit(solution)/shard_map/ppermute | solution.py:713
  57.0 7.0 %collective-permute-start.4 = (bf16[128,256]{1,0:T(8,128)(2,1)}, bf16[128,256]{1,0:T(8,128)(2,1)S(1)}, u32[]{:S(2)}, u32[]{:S(2)}) collective-permute-start(bf16[128,256]{1,0:T(8,128)(2,1)} %get-tuple-element.42.refs_1_.refs_6_.refs_5_), channel_id=1, source_target_pairs={{0,16},{2,18},{4,20},{6,22},{8,24},{10,26},{12,28},{14,30},{16,0},... | collective-permute-start | bytes 196616 | tf_op jit(solution)/shard_map/ppermute | solution.py:713
  57.5 21.3 %collective-permute-start.8 = (bf16[2,256,128]{2,1,0:T(8,128)(2,1)}, bf16[2,256,128]{2,1,0:T(8,128)(2,1)S(1)}, u32[]{:S(2)}, u32[]{:S(2)}) collective-permute-start(bf16[2,256,128]{2,1,0:T(8,128)(2,1)} %get-tuple-element.49), channel_id=1, source_target_pairs={{0,12},{2,14},{4,0},{6,2},{8,4},{10,6},{12,8},{14,10},{1,13},{3,15... | collective-permute-start | bytes 393224 | tf_op jit(solution)/shard_map/ppermute | solution.py:717
  60.7 3.3 %copy-start.15 = (bf16[128,256]{1,0:T(8,128)(2,1)}, bf16[128,256]{1,0:T(8,128)(2,1)S(1)}, u32[]{:S(2)}) copy-start(bf16[128,256]{1,0:T(8,128)(2,1)S(1)} %collective-permute-done.5.refs_4_.refs_8_) | copy-start | bytes 196612
  60.7 20.4 %collective-permute-start.9 = (bf16[2,256,128]{2,1,0:T(8,128)(2,1)}, bf16[2,256,128]{2,1,0:T(8,128)(2,1)S(1)}, u32[]{:S(2)}, u32[]{:S(2)}) collective-permute-start(bf16[2,256,128]{2,1,0:T(8,128)(2,1)} %get-tuple-element.50), channel_id=1, source_target_pairs={{0,8},{2,10},{4,12},{6,14},{8,0},{10,2},{12,4},{14,6},{1,9},{3,11}... | collective-permute-start | bytes 393224 | tf_op jit(solution)/shard_map/ppermute | solution.py:717
  62.6 1.5 %copy-start.17 = (bf16[128,256]{1,0:T(8,128)(2,1)}, bf16[128,256]{1,0:T(8,128)(2,1)S(1)}, u32[]{:S(2)}) copy-start(bf16[128,256]{1,0:T(8,128)(2,1)S(1)} %collective-permute-done.3.refs_2_.refs_6_) | copy-start | bytes 196612
  62.6 18.6 %collective-permute-start.10 = (bf16[2,256,128]{2,1,0:T(8,128)(2,1)}, bf16[2,256,128]{2,1,0:T(8,128)(2,1)S(1)}, u32[]{:S(2)}, u32[]{:S(2)}) collective-permute-start(bf16[2,256,128]{2,1,0:T(8,128)(2,1)} %get-tuple-element.51), channel_id=1, source_target_pairs={{0,4},{2,6},{4,8},{6,10},{8,12},{10,14},{12,0},{14,2},{1,5},{3,7},... | collective-permute-start | bytes 393224 | tf_op jit(solution)/shard_map/ppermute | solution.py:717
  64.0 0.6 copy-start.19
  64.7 1.0 copy-start.5
  69.6 16.4 %collective-permute-start.11 = (bf16[4,256,256]{2,1,0:T(8,128)(2,1)}, bf16[4,256,256]{2,1,0:T(8,128)(2,1)S(1)}, u32[]{:S(2)}, u32[]{:S(2)}) collective-permute-start(bf16[4,256,256]{2,1,0:T(8,128)(2,1)} %weight_sent.1.refs_0_), channel_id=1, source_target_pairs={{0,2},{2,0},{4,6},{6,4},{8,10},{10,8},{12,14},{14,12},{1,3},{3,1},... | collective-permute-start | bytes 1572872 | tf_op jit(solution)/shard_map/ppermute | solution.py:723
  78.1 24.7 %collective-permute-start.7 = (bf16[256,128]{1,0:T(8,128)(2,1)}, bf16[256,128]{1,0:T(8,128)(2,1)S(1)}, u32[]{:S(2)}, u32[]{:S(2)}) collective-permute-start(bf16[256,128]{1,0:T(8,128)(2,1)} %get-tuple-element.48), channel_id=1, source_target_pairs={{0,2},{2,0},{4,6},{6,4},{8,10},{10,8},{12,14},{14,12},{1,3},{3,1},... | collective-permute-start | bytes 196616 | tf_op jit(solution)/shard_map/ppermute | solution.py:728
  78.8 3.3 %copy-start.7 = (bf16[2,256,128]{2,1,0:T(8,128)(2,1)}, bf16[2,256,128]{2,1,0:T(8,128)(2,1)S(1)}, u32[]{:S(2)}) copy-start(bf16[2,256,128]{2,1,0:T(8,128)(2,1)S(1)} %collective-permute-done.8.refs_1_.refs_6_) | copy-start | bytes 393220
  78.8 12.7 %collective-permute-start.12 = (bf16[2,256,128]{2,1,0:T(8,128)(2,1)}, bf16[2,256,128]{2,1,0:T(8,128)(2,1)S(1)}, u32[]{:S(2)}, u32[]{:S(2)}) collective-permute-start(bf16[2,256,128]{2,1,0:T(8,128)(2,1)} %get-tuple-element.54), channel_id=1, source_target_pairs={{0,12},{2,14},{4,0},{6,2},{8,4},{10,6},{12,8},{14,10},{1,13},{3,15... | collective-permute-start | bytes 393224 | tf_op jit(solution)/shard_map/ppermute | solution.py:717
  81.2 0.9 copy-start.8
  81.2 14.3 %collective-permute-start.13 = (bf16[2,256,128]{2,1,0:T(8,128)(2,1)}, bf16[2,256,128]{2,1,0:T(8,128)(2,1)S(1)}, u32[]{:S(2)}, u32[]{:S(2)}) collective-permute-start(bf16[2,256,128]{2,1,0:T(8,128)(2,1)} %get-tuple-element.55), channel_id=1, source_target_pairs={{0,8},{2,10},{4,12},{6,14},{8,0},{10,2},{12,4},{14,6},{1,9},{3,11}... | collective-permute-start | bytes 393224 | tf_op jit(solution)/shard_map/ppermute | solution.py:717
  81.2 0.9 copy-start.9
  81.2 14.3 %collective-permute-start.14 = (bf16[2,256,128]{2,1,0:T(8,128)(2,1)}, bf16[2,256,128]{2,1,0:T(8,128)(2,1)S(1)}, u32[]{:S(2)}, u32[]{:S(2)}) collective-permute-start(bf16[2,256,128]{2,1,0:T(8,128)(2,1)} %get-tuple-element.56), channel_id=1, source_target_pairs={{0,4},{2,6},{4,8},{6,10},{8,12},{10,14},{12,0},{14,2},{1,5},{3,7},... | collective-permute-start | bytes 393224 | tf_op jit(solution)/shard_map/ppermute | solution.py:717
  86.0 0.8 copy-start.6
  88.9 10.9 %collective-permute-start.16 = (bf16[256,256]{1,0:T(8,128)(2,1)}, bf16[256,256]{1,0:T(8,128)(2,1)S(1)}, u32[]{:S(2)}, u32[]{:S(2)}) collective-permute-start(bf16[256,256]{1,0:T(8,128)(2,1)} %get-tuple-element.63), channel_id=1, source_target_pairs={{0,4},{2,6},{4,8},{6,10},{8,12},{10,14},{12,0},{14,2},{1,5},{3,7},... | collective-permute-start | bytes 393224 | tf_op jit(solution)/shard_map/ppermute | solution.py:733
  91.5 4.0 %copy-start.10 = (bf16[2,256,128]{2,1,0:T(8,128)(2,1)}, bf16[2,256,128]{2,1,0:T(8,128)(2,1)S(1)}, u32[]{:S(2)}) copy-start(bf16[2,256,128]{2,1,0:T(8,128)(2,1)S(1)} %collective-permute-done.12.refs_2_) | copy-start | bytes 393220
  91.5 9.5 %collective-permute-start.17 = (bf16[256,256]{1,0:T(8,128)(2,1)}, bf16[256,256]{1,0:T(8,128)(2,1)S(1)}, u32[]{:S(2)}, u32[]{:S(2)}) collective-permute-start(bf16[256,256]{1,0:T(8,128)(2,1)} %get-tuple-element.64), channel_id=1, source_target_pairs={{0,8},{2,10},{4,12},{6,14},{8,0},{10,2},{12,4},{14,6},{1,9},{3,11}... | collective-permute-start | bytes 393224 | tf_op jit(solution)/shard_map/ppermute | solution.py:733
  95.5 0.7 copy-start.11
  95.5 6.5 %collective-permute-start.18 = (bf16[256,256]{1,0:T(8,128)(2,1)}, bf16[256,256]{1,0:T(8,128)(2,1)S(1)}, u32[]{:S(2)}, u32[]{:S(2)}) collective-permute-start(bf16[256,256]{1,0:T(8,128)(2,1)} %get-tuple-element.65), channel_id=1, source_target_pairs={{0,12},{2,14},{4,0},{6,2},{8,4},{10,6},{12,8},{14,10},{1,13},{3,15... | collective-permute-start | bytes 393224 | tf_op jit(solution)/shard_map/ppermute | solution.py:733
  95.5 0.7 copy-start.12
  96.2 5.8 %copy-start.1 = (bf16[256,256]{1,0:T(8,128)(2,1)S(1)}, bf16[256,256]{1,0:T(8,128)(2,1)}, u32[]{:S(2)}) copy-start(bf16[256,256]{1,0:T(8,128)(2,1)} %get-tuple-element.52.refs_0_) | copy-start | bytes 393220
  98.3 5.2 %collective-permute-start.15 = (bf16[256,256]{1,0:T(8,128)(2,1)}, bf16[256,256]{1,0:T(8,128)(2,1)S(1)}, u32[]{:S(2)}, u32[]{:S(2)}) collective-permute-start(bf16[256,256]{1,0:T(8,128)(2,1)} %get-tuple-element.59), channel_id=1, source_target_pairs={{0,2},{2,0},{4,6},{6,4},{8,10},{10,8},{12,14},{14,12},{1,3},{3,1},... | collective-permute-start | bytes 393224 | tf_op jit(solution)/shard_map/ppermute | solution.py:738
  102.8 0.8 copy-start.14
  103.6 0.7 copy-start.13

commit v8 on v6

--- a/solution.py
+++ b/solution.py
@@ -182,9 +182,12 @@
 
 
 def forward_kernel(block_count, head_count, at_ref, q_ref, q_recv, key_mask, row_mask, *refs):
-    kv_refs, refs = refs[:block_count], refs[block_count:]
+    g_mine, g_recv = refs[:2]
+    kv_refs, refs = refs[2 : 2 + block_count], refs[2 + block_count :]
     e_out, inv_out, attn_mine, attn_theirs = refs[:4]
-    q_s, mask_s, kv_s, e_s, s_ref, attn_s, inv_s, row_s, sem, kv_sem, e_sem, out_sem = refs[4:]
+    part_out, refs = refs[4], refs[5:]
+    q_s, g_s, mask_s, kv_s, e_s, s_ref, attn_s, inv_s, row_s, part_s = refs[:10]
+    sem, kv_sem, e_sem, out_sem, part_sem = refs[10:]
     rows = q_recv.shape[0]
     feats = head_count * HD
     score_scale = HD ** (-0.5)
@@ -196,6 +199,7 @@
         begin(row_mask, row_s, sem.at[3]),
     ]
     kv_loads = [begin(kv_refs[j], kv_s.at[j], kv_sem.at[j]) for j in range(block_count)]
+    g_loads = [begin(g_mine, g_s.at[0], sem.at[4]), begin(g_recv, g_s.at[1], sem.at[5])]
     for load in loads:
         load.wait()
     rows_low = row_s[...].astype(jnp.bfloat16)
@@ -233,14 +237,26 @@
         attn_low = (attn_t * inverse).astype(jnp.bfloat16)
         attn_s[0, cols, :] = attn_low[:, :rows]
         attn_s[1, cols, :] = attn_low[:, rows:]
-    stores.append(begin(attn_s.at[0], attn_mine, out_sem.at[0]))
-    stores.append(begin(attn_s.at[1], attn_theirs, out_sem.at[1]))
-    stores.append(begin(inv_s, inv_out, out_sem.at[2]))
+        if head == 0:
+            for load in g_loads:
+                load.wait()
+        if head == head_count - 1:
+            stores.append(begin(attn_s.at[0], attn_mine, out_sem.at[0]))
+            stores.append(begin(attn_s.at[1], attn_theirs, out_sem.at[1]))
+            stores.append(begin(inv_s, inv_out, out_sem.at[2]))
+        g_t = jnp.concatenate([g_s[0, cols, :], g_s[1, cols, :]], axis=1).astype(jnp.float32)
+        grad = jnp.transpose((g_t * inverse).astype(jnp.bfloat16))
+        for j in range(block_count):
+            keys = slice(j * rows, (j + 1) * rows)
+            part_s[j, :, cols] = product(e_s[head, keys, :], grad).astype(jnp.bfloat16)
+            if head == head_count - 1:
+                target = part_out.at[at_ref[SOURCES + j]]
+                stores.append(begin(part_s.at[j], target, part_sem.at[j]))
     for store in stores:
         store.wait()
 
 
-def forward(at, queries, q_recv, key_mask, row_mask, kv_blocks, after):
+def forward(at, queries, q_recv, key_mask, row_mask, g_mine, g_recv, kv_blocks, after):
     block_count = len(kv_blocks)
     rows, feats = q_recv.shape
     heads = feats // HD
@@ -252,11 +268,13 @@
             f32(max(heads, 8), 2 * rows),
             bf16(feats, rows),
             bf16(feats, rows),
+            bf16(block_count, rows, feats),
         ],
-        [SMEM] + [ANY] * (4 + block_count),
-        [ANY] * 4,
+        [SMEM] + [ANY] * (6 + block_count),
+        [ANY] * 5,
         [
             pltpu.VMEM((2, rows, feats), jnp.bfloat16),
+            pltpu.VMEM((2, feats, rows), jnp.bfloat16),
             pltpu.VMEM((keys, HD), jnp.bfloat16),
             pltpu.VMEM((block_count, rows, 2 * feats), jnp.bfloat16),
             pltpu.VMEM((heads, keys, 2 * rows), jnp.bfloat16),
@@ -264,26 +282,27 @@
             pltpu.VMEM((2, feats, rows), jnp.bfloat16),
             pltpu.VMEM((max(heads, 8), 2 * rows), jnp.float32),
             pltpu.VMEM((8, 2 * rows), jnp.float32),
-            pltpu.SemaphoreType.DMA((4,)),
+            pltpu.VMEM((block_count, rows, feats), jnp.bfloat16),
+            pltpu.SemaphoreType.DMA((6,)),
             pltpu.SemaphoreType.DMA((block_count,)),
             pltpu.SemaphoreType.DMA((heads * block_count,)),
             pltpu.SemaphoreType.DMA((3,)),
+            pltpu.SemaphoreType.DMA((block_count,)),
         ],
-        6,
+        20,
         "forward",
         after,
-    )(at, queries, q_recv, key_mask, row_mask, *kv_blocks)
-
-
-def backward_kernel(block_count, head_count, at_ref, *refs):
-    q_ref, q_recv, g_mine, g_recv, attn_mine, attn_theirs, inv_ref, e_ref = refs[:8]
-    kv_refs, refs = refs[8 : 8 + block_count], refs[8 + block_count :]
-    dq_mine, dq_theirs = refs[:2]
-    outer = block_count // INNER
-    part_outs, refs = refs[2 : 2 + outer], refs[2 + outer :]
+    )(at, queries, q_recv, key_mask, row_mask, g_mine, g_recv, *kv_blocks)
+
+
+def key_terms_kernel(block_count, at_ref, q_ref, q_recv, g_mine, g_recv, attn_mine, attn_theirs, *refs):
+    inv_ref, e_ref = refs[:2]
+    kv_refs, refs = refs[2 : 2 + block_count], refs[2 + block_count :]
+    dq_mine, dq_theirs, part_out = refs[:3]
+    refs = refs[3:]
     q_s, t_s, inv_s, kv_s, e_s, part_s, dq_s, sem, kv_sem, e_sem, part_sem, dq_sem = refs
-    rows = q_recv.shape[0]
-    feats = head_count * HD
+    rows, feats = q_recv.shape
+    head_count = feats // HD
     score_scale = HD ** (-0.5)
     mine = pl.ds(pl.multiple_of(at_ref[0] * feats, feats), feats)
     loads = [begin(q_ref.at[:, mine], q_s.at[0], sem.at[0]), begin(q_recv, q_s.at[1], sem.at[1])]
@@ -308,7 +327,6 @@
         attn_t = jnp.concatenate([t_s[2, cols, :], t_s[3, cols, :]], axis=1)
         row_dot = jnp.sum(g_t * attn_t.astype(jnp.float32), axis=0, keepdims=True) * inverse
         g_t = (g_t * inverse).astype(jnp.bfloat16)
-        grad = jnp.transpose(g_t)
         query = jnp.concatenate([q_s[0, :, cols], q_s[1, :, cols]], axis=0)
         dq_t = jnp.zeros((HD, 2 * rows), jnp.float32)
         for j in range(block_count):
@@ -316,14 +334,15 @@
             if head == 0:
                 kv_loads[j].wait()
             e_loads[head, j].wait()
-            low = e_s[head, keys, :]
             dprobs = product(kv_s[j, :, vcols], g_t)
-            dscore = (low.astype(jnp.float32) * (dprobs - row_dot)).astype(jnp.bfloat16)
+            dscore = (e_s[head, keys, :].astype(jnp.float32) * (dprobs - row_dot)).astype(
+                jnp.bfloat16
+            )
             dq_t = dq_t + product(jnp.transpose(kv_s[j, :, cols]), dscore)
             part_s[j, :, cols] = (score_scale * product(dscore, query)).astype(jnp.bfloat16)
-            part_s[j, :, vcols] = product(low, grad).astype(jnp.bfloat16)
             if head == head_count - 1:
-                stores.append(begin(part_s.at[j], part_outs[j // INNER].at[j % INNER], part_sem.at[j]))
+                target = part_out.at[at_ref[SOURCES + j]]
+                stores.append(begin(part_s.at[j], target, part_sem.at[j]))
         dquery = (score_scale * jnp.transpose(dq_t)).astype(jnp.bfloat16)
         dq_s[0, :, cols] = dquery[:rows]
         dq_s[1, :, cols] = dquery[rows:]
@@ -333,23 +352,23 @@
         store.wait()
 
 
-def backward(at, queries, q_recv, g_mine, g_recv, attn_mine, attn_theirs, inverse, weights, kv_blocks):
+def key_terms(at, queries, q_recv, g_mine, g_recv, attn_mine, attn_theirs, inverse, weights, kv_blocks, after):
     block_count = len(kv_blocks)
     rows, feats = q_recv.shape
     heads = feats // HD
     keys = block_count * rows
-    out = call(
-        functools.partial(backward_kernel, block_count, heads),
-        [bf16(rows, feats)] * 2 + [bf16(INNER, rows, 2 * feats)] * (block_count // INNER),
+    return call(
+        functools.partial(key_terms_kernel, block_count),
+        [bf16(rows, feats)] * 2 + [bf16(block_count, rows, feats)],
         [SMEM] + [ANY] * (8 + block_count),
-        [ANY] * (2 + block_count // INNER),
+        [ANY] * 3,
         [
             pltpu.VMEM((2, rows, feats), jnp.bfloat16),
             pltpu.VMEM((4, feats, rows), jnp.bfloat16),
             pltpu.VMEM(inverse.shape, jnp.float32),
             pltpu.VMEM((block_count, rows, 2 * feats), jnp.bfloat16),
             pltpu.VMEM((heads, keys, 2 * rows), jnp.bfloat16),
-            pltpu.VMEM((block_count, rows, 2 * feats), jnp.bfloat16),
+            pltpu.VMEM((block_count, rows, feats), jnp.bfloat16),
             pltpu.VMEM((2, rows, feats), jnp.bfloat16),
             pltpu.SemaphoreType.DMA((7,)),
             pltpu.SemaphoreType.DMA((block_count,)),
@@ -357,13 +376,13 @@
             pltpu.SemaphoreType.DMA((block_count,)),
             pltpu.SemaphoreType.DMA((2,)),
         ],
-        8,
-        "backward",
+        7,
+        "key_terms",
+        after,
     )(at, queries, q_recv, g_mine, g_recv, attn_mine, attn_theirs, inverse, weights, *kv_blocks)
-    return out[0], out[1], out[2:]
-
-
-def grad_heads_kernel(part_count, sends, picked, at_ref, first_ref, weight_ref, *refs):
+
+
+def grad_heads_kernel(part_count, sends, picked, columns_at, send_at, at_ref, first_ref, weight_ref, *refs):
     grads, refs = refs[:part_count], refs[part_count:]
     outs, refs = refs[: 2 + sends], refs[2 + sends :]
     first_s, grad_s, weight_s, out_s, first_sem, weight_sem, grad_sem, send_sem, out_sem = refs
@@ -374,7 +393,7 @@
     for k in range(part_count):
         grad_loads.append(begin(grads[k], grad_s.at[k], grad_sem.at[k]))
         if k:
-            start = pl.multiple_of(at_ref[k] * width, width)
+            start = pl.multiple_of(at_ref[columns_at + k - 1] * width, width)
             columns = weight_ref.at[:, pl.ds(start, width)]
             weight_loads.append(begin(columns, weight_s.at[k - 1], weight_sem.at[k - 1]))
     for load in grad_loads:
@@ -386,7 +405,7 @@
             target = outs[2 + send].at[:, i * width : (i + 1) * width]
             for k in range(part_count):
 
-                @pl.when(at_ref[part_count + place] == k)
+                @pl.when(at_ref[send_at + place] == k)
                 def _():
                     begin(grad_s.at[k], target, send_sem.at[place])
 
@@ -405,13 +424,13 @@
         copy.wait()
 
 
-def grad_heads(at, first, out_weight, grads, sends, picked):
+def grad_heads(at, columns_at, send_at, first, out_weight, grads, sends, picked):
     feats, rows = first.shape
     half = feats // INNER
     count = len(grads)
     width = grads[0].shape[1]
     out = call(
-        functools.partial(grad_heads_kernel, count, sends, picked),
+        functools.partial(grad_heads_kernel, count, sends, picked, columns_at, send_at),
         [bf16(half, rows), bf16(half, rows)] + [bf16(rows, picked * width)] * sends,
         [SMEM] + [ANY] * (2 + count),
         [ANY] * (2 + sends),
@@ -432,12 +451,19 @@
     return out[0], out[1], out[2:]
 
 
-def weight_kernel(part_count, picked, doc_count, sent, at_ref, *refs):
+def weight_kernel(part_count, doc_count, sent, step_at, at_ref, *refs):
     attn, refs = refs[: INNER * doc_count], refs[INNER * doc_count :]
     grads, refs = refs[:part_count], refs[part_count:]
     swapped, refs = refs[: doc_count - 1], refs[doc_count - 1 :]
-    out, attn_s, grad_s, out_s, attn_sem, grad_sem, out_sem = refs
-    outer, feats, width = out.shape
+    if sent:
+        out, refs = refs[0], refs[1:]
+        outs = [out.at[k] for k in range(out.shape[0])]
+    else:
+        recv, refs = refs[0], refs[1:]
+        outs, refs = refs[: recv.shape[0]], refs[recv.shape[0] :]
+        recv_s, recv_sem, refs = refs[0], refs[1], refs[2:]
+    attn_s, grad_s, out_s, attn_sem, grad_sem, out_sem = refs
+    outer, feats, width = out_s.shape
     half = feats // INNER
     piece = grads[0].shape[1]
     pieces = piece // width
@@ -451,7 +477,7 @@
             attn_loads.append(begin(attn[index], target, attn_sem.at[index]))
     for k in range(outer):
         place = lax.rem(at_ref[1] + k, outer) * INNER + here
-        which = at_ref[2 + place // pieces]
+        which = at_ref[step_at + place // pieces]
         cols = pl.ds(pl.multiple_of(lax.rem(place, pieces) * width, width), width)
         for i in range(part_count):
 
@@ -464,6 +490,8 @@
         for doc in range(1, doc_count):
             source = swapped[doc - 1].at[:, cols]
             loads.append(begin(source, grad_s.at[doc, k], grad_sem.at[doc * outer + k]))
+        if not sent:
+            loads.append(begin(recv.at[k], recv_s.at[k], recv_sem.at[k]))
         grad_loads.append(loads)
     for load in attn_loads:
         load.wait()
@@ -473,152 +501,99 @@
         for doc in range(doc_count):
             grad_loads[k][doc].wait()
             term = term + product(attn_s[doc], grad_s[doc, k])
+        if not sent:
+            grad_loads[k][doc_count].wait()
+            term = term + recv_s[k].astype(jnp.float32)
         out_s[k] = term.astype(out_s.dtype)
-        stores.append(begin(out_s.at[k], out.at[k], out_sem.at[k]))
+        stores.append(begin(out_s.at[k], outs[k], out_sem.at[k]))
     for store in stores:
         store.wait()
 
 
-def weight_terms(at, attn, grads, swapped, outer, picked, sent, after=()):
+def weight_terms(at, step_at, attn, grads, swapped, outer, picked, recv=None, after=()):
     half, rows = attn[0].shape
     feats = half * INNER
     doc_count = len(attn) // INNER
     width = picked * grads[0].shape[1] // (outer * INNER)
+    sent = recv is None
+    operands = [*attn, *grads, *swapped] + ([] if sent else [recv])
+    scratch = [
+        pltpu.VMEM((doc_count, feats, rows), jnp.bfloat16),
+        pltpu.VMEM((doc_count, outer, rows, width), jnp.bfloat16),
+        pltpu.VMEM((outer, feats, width), jnp.bfloat16),
+        pltpu.SemaphoreType.DMA((len(attn),)),
+        pltpu.SemaphoreType.DMA((doc_count * outer,)),
+        pltpu.SemaphoreType.DMA((outer,)),
+    ]
+    if not sent:
+        added = [pltpu.VMEM((outer, feats, width), jnp.bfloat16), pltpu.SemaphoreType.DMA((outer,))]
+        scratch = added + scratch
     return call(
-        functools.partial(weight_kernel, len(grads), picked, doc_count, sent),
-        bf16(outer, feats, width),
-        [SMEM] + [ANY] * (len(attn) + len(grads) + len(swapped)),
-        ANY,
-        [
-            pltpu.VMEM((doc_count, feats, rows), jnp.bfloat16),
-            pltpu.VMEM((doc_count, outer, rows, width), jnp.bfloat16),
-            pltpu.VMEM((outer, feats, width), jnp.bfloat16),
-            pltpu.SemaphoreType.DMA((len(attn),)),
-            pltpu.SemaphoreType.DMA((doc_count * outer,)),
-            pltpu.SemaphoreType.DMA((outer,)),
-        ],
-        3,
+        functools.partial(weight_kernel, len(grads), doc_count, sent, step_at),
+        bf16(outer, feats, width) if sent else [bf16(feats, width)] * outer,
+        [SMEM] + [ANY] * len(operands),
+        ANY if sent else [ANY] * outer,
+        scratch,
+        4,
         "weight_sent" if sent else "weight_kept",
         after,
-    )(at, *attn, *grads, *swapped)
-
-
-def weight_add_kernel(keep, recv, *refs):
-    outer = keep.shape[0]
-    outs, (held_s, out_s, sem, out_sem) = refs[:outer], refs[outer:]
-    loads = []
-    for k in range(outer):
-        for index, held in enumerate((keep, recv)):
-            loads.append(begin(held.at[k], held_s.at[index, k], sem.at[2 * k + index]))
+    )(at, *operands)
+
+
+def collect_kernel(joined, *refs):
+    if joined:
+        at_ref, dq_mine, dq_recv, terms, grad_q, out = refs[:6]
+        dq_s, q_s, dq_sem, q_sem = refs[6:10]
+        terms_s, out_s, sem, out_sem = refs[10:]
+    else:
+        terms, out, terms_s, out_s, sem, out_sem = refs
+    count, rows, half = terms.shape
+    loads = [begin(terms.at[c], terms_s.at[c], sem.at[c]) for c in range(count)]
     stores = []
-    for k in range(outer):
-        loads[2 * k].wait()
-        loads[2 * k + 1].wait()
-        summed = held_s[0, k].astype(jnp.float32) + held_s[1, k].astype(jnp.float32)
-        out_s[k] = summed.astype(jnp.bfloat16)
-        stores.append(begin(out_s.at[k], outs[k], out_sem.at[k]))
+    if joined:
+        held = [begin(dq, dq_s.at[i], dq_sem.at[i]) for i, dq in enumerate((dq_mine, dq_recv))]
+        for side, at in enumerate((at_ref[0], 1 - at_ref[0])):
+            held[side].wait()
+            q_s[:, pl.ds(pl.multiple_of(at * half, half), half)] = dq_s[side]
+        stores.append(begin(q_s, grad_q, q_sem))
+    for load in loads:
+        load.wait()
+    for side in range(INNER):
+        summed = terms_s[side].astype(jnp.float32)
+        for c in range(side + INNER, count, INNER):
+            summed = summed + terms_s[c].astype(jnp.float32)
+        out_s[:, side * half : (side + 1) * half] = summed.astype(jnp.bfloat16)
+    stores.append(begin(out_s, out, out_sem))
     for store in stores:
         store.wait()
 
 
-def weight_add(keep, recv):
-    outer, feats, width = keep.shape
+def collect(terms, name, joined=(), after=()):
+    count, rows, half = terms.shape
+    whole = bf16(rows, INNER * half)
+    scratch = [
+        pltpu.VMEM((count, rows, half), jnp.bfloat16),
+        pltpu.VMEM((rows, INNER * half), jnp.bfloat16),
+        pltpu.SemaphoreType.DMA((count,)),
+        pltpu.SemaphoreType.DMA,
+    ]
+    if joined:
+        scratch = [
+            pltpu.VMEM((INNER, rows, half), jnp.bfloat16),
+            pltpu.VMEM((rows, INNER * half), jnp.bfloat16),
+            pltpu.SemaphoreType.DMA((INNER,)),
+            pltpu.SemaphoreType.DMA,
+        ] + scratch
     return call(
-        weight_add_kernel,
-        [bf16(feats, width)] * outer,
-        [ANY] * 2,
-        [ANY] * outer,
-        [
-            pltpu.VMEM((2, outer, feats, width), jnp.bfloat16),
-            pltpu.VMEM((outer, feats, width), jnp.bfloat16),
-            pltpu.SemaphoreType.DMA((2 * outer,)),
-            pltpu.SemaphoreType.DMA((outer,)),
-        ],
-        1.5,
-        "weight_add",
-    )(keep, recv)
-
-
-def add_kernel(count, *refs):
-    terms, (mine, theirs) = refs[:count], refs[count : count + 2]
-    terms_s, out_s, term_sem, out_sem = refs[count + 2 :]
-    loads = [
-        begin(terms[c].at[side], terms_s.at[c, side], term_sem.at[c * INNER + side])
-        for side in (1, 0)
-        for c in range(count)
-    ]
-    stores = []
-    for index, (side, out) in enumerate(((1, theirs), (0, mine))):
-        for load in loads[index * count : (index + 1) * count]:
-            load.wait()
-        summed = terms_s[0, side].astype(jnp.float32)
-        for c in range(1, count):
-            summed = summed + terms_s[c, side].astype(jnp.float32)
-        out_s[side] = summed.astype(jnp.bfloat16)
-        stores.append(begin(out_s.at[side], out, out_sem.at[side]))
-    for store in stores:
-        store.wait()
-
-
-def add_terms(terms, after):
-    _, rows, width = terms[0].shape
-    count = len(terms)
-    return call(
-        functools.partial(add_kernel, count),
-        [bf16(rows, width)] * 2,
-        [ANY] * count,
-        [ANY] * 2,
-        [
-            pltpu.VMEM((count, INNER, rows, width), jnp.bfloat16),
-            pltpu.VMEM((INNER, rows, width), jnp.bfloat16),
-            pltpu.SemaphoreType.DMA((count * INNER,)),
-            pltpu.SemaphoreType.DMA((INNER,)),
-        ],
+        functools.partial(collect_kernel, bool(joined)),
+        [whole, whole] if joined else whole,
+        [SMEM, ANY, ANY, ANY] if joined else [ANY],
+        [ANY, ANY] if joined else ANY,
+        scratch,
         2,
-        "add_terms",
+        name,
         after,
-    )(*terms)
-
-
-def join_kernel(at_ref, dq_mine, dq_recv, mine, recv, *refs):
-    outs, (held_s, out_s, sem, out_sem) = refs[:3], refs[3:]
-    half = dq_mine.shape[1]
-    loads = [
-        begin(dq_mine, held_s.at[0, 0], sem.at[0]),
-        begin(dq_recv, held_s.at[1, 0], sem.at[1]),
-    ]
-    for side, held in enumerate((mine, recv)):
-        for index in range(2):
-            source = held.at[:, index * half : (index + 1) * half]
-            loads.append(begin(source, held_s.at[side, 1 + index], sem.at[2 + 2 * side + index]))
-    for load in loads:
-        load.wait()
-    stores = []
-    for index, out in enumerate(outs):
-        for side, at in enumerate((at_ref[0], 1 - at_ref[0])):
-            cols = pl.ds(pl.multiple_of(at * half, half), half)
-            out_s[index, :, cols] = held_s[side, index]
-        stores.append(begin(out_s.at[index], out, out_sem.at[index]))
-    for store in stores:
-        store.wait()
-
-
-def join_heads(at, dq_mine, dq_recv, mine, recv):
-    rows, half = dq_mine.shape
-    return call(
-        join_kernel,
-        [bf16(rows, INNER * half)] * 3,
-        [SMEM] + [ANY] * 4,
-        [ANY] * 3,
-        [
-            pltpu.VMEM((INNER, 3, rows, half), jnp.bfloat16),
-            pltpu.VMEM((3, rows, INNER * half), jnp.bfloat16),
-            pltpu.SemaphoreType.DMA((6,)),
-            pltpu.SemaphoreType.DMA((3,)),
-        ],
-        2,
-        "join_heads",
-    )(at, dq_mine, dq_recv, mine, recv)
+    )(*joined, terms)
 
 
 def per_device(
@@ -650,12 +625,14 @@
     sources = [
         ((outer_at - step) % outer) * INNER + (inner_at + side) % INNER for step, side in routes
     ]
-    at = jnp.stack([inner_at, outer_at, tp_at] + sources)
-    columns_at = [(tp_at + step) % tp_count for step in range(1, tp_count)]
+    scalars = [inner_at, outer_at, tp_at] + sources
+    columns_at = len(scalars)
+    scalars = scalars + [(tp_at + step) % tp_count for step in range(1, tp_count)]
+    send_at = len(scalars)
     for step in range(1, dp_count):
-        columns_at = columns_at + dp_steps((dp_at + step) % dp_count)
-    columns_at = jnp.stack([inner_at] + columns_at)
-    weight_at = jnp.stack([inner_at, outer_at] + dp_steps(dp_at))
+        scalars = scalars + dp_steps((dp_at + step) % dp_count)
+    keep_at = len(scalars)
+    at = jnp.stack(scalars + dp_steps(dp_at))
 
     grad_own = grad_output[0]
     grads = [grad_own] + [
@@ -674,7 +651,7 @@
     )
     q_recv = lax.ppermute(q_theirs, "ctx", ctx_pairs(0, 1))
     g_mine, g_theirs, grad_sends = grad_heads(
-        columns_at, first, out_weight, grads, dp_count - 1, picked
+        at, columns_at, send_at, first, out_weight, grads, dp_count - 1, picked
     )
     g_recv = lax.ppermute(g_theirs, "ctx", ctx_pairs(0, 1))
     swapped = [
@@ -682,8 +659,8 @@
         for step, send in enumerate(grad_sends)
     ]
 
-    weights, inverse, attn_mine, attn_theirs = forward(
-        at, queries[0], q_recv, key_mask, row_mask, kv_blocks, (g_theirs,)
+    weights, inverse, attn_mine, attn_theirs, value_parts = forward(
+        at, queries[0], q_recv, key_mask, row_mask, g_mine, g_recv, kv_blocks, ()
     )
 
     attn = []
@@ -693,27 +670,28 @@
             axes = ("dp", "ctx") if step else "ctx"
             attn.append(lax.ppermute(held, axes, pairs) if step or side else held)
 
-    dq_mine, dq_theirs, parts = backward(
-        at, queries[0], q_recv, g_mine, g_recv, attn_mine, attn_theirs, inverse, weights, kv_blocks
-    )
-    send = weight_terms(weight_at, attn, grads, swapped, outer, picked, True, (dq_mine,))
+    def returned(parts):
+        return lax.all_to_all(parts, "ctx", split_axis=0, concat_axis=0, tiled=True)
+
+    value_parts = returned(value_parts)
+    send = weight_terms(at, keep_at, attn, grads, swapped, outer, picked)
     weight_recv = lax.ppermute(send, "ctx", ctx_pairs(0, 1))
-    terms = [
-        lax.ppermute(part, "ctx", ctx_pairs(-step, 0)) if step else part
-        for step, part in enumerate(parts)
-    ]
+    dq_mine, dq_theirs, key_parts = key_terms(
+        at, queries[0], q_recv, g_mine, g_recv, attn_mine, attn_theirs, inverse, weights, kv_blocks, (send,)
+    )
+    key_parts = returned(key_parts)
     dq_recv = lax.ppermute(dq_theirs, "ctx", ctx_pairs(0, 1))
-    keep = weight_terms(weight_at, attn, grads, swapped, outer, picked, False, (send,))
-    weight_sums = weight_add(keep, weight_recv)
+    weight_sums = weight_terms(
+        at, keep_at, attn, grads, swapped, outer, picked, weight_recv, (dq_mine,)
+    )
     grad_weight = weight_sums[0].astype(jnp.float32)
     for step in range(1, outer):
         grad_weight = grad_weight + lax.ppermute(
             weight_sums[step], "ctx", ctx_pairs(step, 0)
         ).astype(jnp.float32)
 
-    terms_mine, terms_theirs = add_terms(terms, (weight_sums[0],))
-    terms_recv = lax.ppermute(terms_theirs, "ctx", ctx_pairs(0, 1))
-    grad_q, grad_k, grad_v = join_heads(at, dq_mine, dq_recv, terms_mine, terms_recv)
+    grad_v = collect(value_parts, "collect_values", (), (weight_sums[0],))
+    grad_q, grad_k = collect(key_parts, "collect_keys", (at, dq_mine, dq_recv), (grad_v,))
     return grad_q[None], grad_k[None], grad_v[None], grad_weight.astype(jnp.bfloat16)
 
 

time: 104 us -> 100 us (0.962)
  waiting for transfers between devices: 26.6 us -> 15.8 us
  starting transfers between devices: 28.5 us -> 39.3 us
  Pallas kernels: 38.6 us -> 36.6 us
  other arithmetic: 2.03 us -> 0.72 us
    ppermute x4 -> x0, waiting for transfers between devices: 15.5 us -> none  [the longest x3 13.2 us: per_device(): lax.ppermute(part, 'ctx', ctx_pairs(-step, 0))]
    all_to_all x0 -> x2, starting transfers between devices: none -> 9.76 us  [returned(): return lax.all_to_all(parts, 'ctx', split_axis=0, concat_axis=0, tiled=True)]
    ppermute x3, waiting for transfers between devices: 1.62 us -> 7.31 us  [per_device(): lax.ppermute(weight_sums[step], 'ctx', ctx_pairs(step, 0))]
    ppermute x1, waiting for transfers between devices: 5.35 us -> 0.01 us  [per_device(): weight_recv = lax.ppermute(send, 'ctx', ctx_pairs(0, 1))]
    ppermute x3, starting transfers between devices: 2.38 us -> 7.42 us  [per_device(): lax.ppermute(weight_sums[step], 'ctx', ctx_pairs(step, 0))]
    ppermute x4 -> x0, starting transfers between devices: 4.06 us -> none  [the longest x3 3.44 us: per_device(): lax.ppermute(part, 'ctx', ctx_pairs(-step, 0))]
    ppermute x1, waiting for transfers between devices: 0.01 us -> 2.91 us  [per_device(): g_recv = lax.ppermute(g_theirs, 'ctx', ctx_pairs(0, 1))]
    ppermute x1, waiting for transfers between devices: 0.63 us -> 2.7 us  [per_device(): lax.ppermute(grad_own, 'tp', shift_pairs(tp_count, -step))]
  transfers between devices with their start and end apart: 23 -> 21, of which waited for: 7 -> 5; matrix products, arithmetic and copies ran while one was open for 3% -> 2% of each run, Pallas kernels for 31% -> 34%
where the time goes in v8:
time: 100 us; the launch traced here: 99.8 us
  starting transfers between devices  39.3 us (39%)
  Pallas kernels  36.6 us (37%)
  waiting for transfers between devices  15.8 us (16%)
  local copies, waits for them, and re-layouts  6.45 us (6%)
    pallas_call x9, Pallas kernels, placed(): return run(*args)  36.6 us
    all_to_all x2, starting transfers between devices, returned(): return lax.all_to_all(parts, 'ctx', split_axis=0, concat_axis=0, tiled=True)  9.76 us
    ppermute x6, starting transfers between devices, per_device(): lax.ppermute(kv_recv if side else kv_mine, 'ctx', ctx_pairs(step, 0))  9.36 us
    ppermute x3, starting transfers between devices, per_device(): lax.ppermute(weight_sums[step], 'ctx', ctx_pairs(step, 0))  7.42 us
    ppermute x3, waiting for transfers between devices, per_device(): lax.ppermute(weight_sums[step], 'ctx', ctx_pairs(step, 0))  7.31 us
    unnamed x41, local copies, waits for them, and re-layouts  5.78 us
    ppermute x1, starting transfers between devices, per_device(): lax.ppermute(grad_own, 'tp', shift_pairs(tp_count, -step))  3.03 us
    ppermute x1, waiting for transfers between devices, per_device(): g_recv = lax.ppermute(g_theirs, 'ctx', ctx_pairs(0, 1))  2.91 us
  transfers between devices with their start and end apart: 21, of which 5 were waited for; matrix products, arithmetic and copies ran while one was open for 2% of the time, Pallas kernels for 34%

profile of v8, /device:TPU:0, one launch (start us, length us, event | category | flops | bytes accessed | tf_op | source)
XLA Modules:
  0.0 99.8 jit_solution(16913555699983785893)
XLA Ops:
  0.6 3.0 %collective-permute-start.2 = (bf16[256,2048]{1,0:T(8,128)(2,1)}, bf16[256,2048]{1,0:T(8,128)(2,1)S(1)}, u32[]{:S(2)}, u32[]{:S(2)}) collective-permute-start(bf16[256,2048]{1,0:T(8,128)(2,1)} %bitcast.21), channel_id=1, source_target_pairs={{0,1},{1,0},{2,3},{3,2},{4,5},{5,4},{6,7},{7,6},{8,9},{9,8},{10,11... | collective-permute-start | bytes 3145736 | tf_op jit(solution)/shard_map/ppermute | solution.py:639
  3.7 0.7 stack.59.refs_0_.refs_1_
  4.3 2.5 %part_heads.1 = (bf16[256,256]{1,0:T(8,128)(2,1)}, bf16[256,256]{1,0:T(8,128)(2,1)}) custom-call(s32[14]{0:T(128)} %stack.59.refs_0_.refs_1_, bf16[256,256]{1,0:T(8,128)(2,1)} %bitcast.26, bf16[256,256]{1,0:T(8,128)(2,1)} %bitcast.27), custom_call_target="tpu_custom_call" | custom-call | flops 2000000000 | bytes 6000000 | tf_op jit(solution)/shard_map/part_heads/pallas_call | solution.py:56
  6.8 1.6 %collective-permute-start = (bf16[256,256]{1,0:T(8,128)(2,1)}, bf16[256,256]{1,0:T(8,128)(2,1)S(1)}, u32[]{:S(2)}, u32[]{:S(2)}) collective-permute-start(bf16[256,256]{1,0:T(8,128)(2,1)} %get-tuple-element.27), channel_id=1, source_target_pairs={{0,2},{2,0},{4,6},{6,4},{8,10},{10,8},{12,14},{14,12},{1,3},{3,1},... | collective-permute-start | bytes 393224 | tf_op jit(solution)/shard_map/ppermute | solution.py:642
  8.4 3.6 %collective-permute-start.8 = (bf16[256,256]{1,0:T(8,128)(2,1)}, bf16[256,256]{1,0:T(8,128)(2,1)S(1)}, u32[]{:S(2)}, u32[]{:S(2)}) collective-permute-start(bf16[256,256]{1,0:T(8,128)(2,1)} %get-tuple-element.34.refs_7_.refs_10_), channel_id=1, source_target_pairs={{0,12},{2,14},{4,0},{6,2},{8,4},{10,6},{12,8},{14,10},{1,13},{3,15... | collective-permute-start | bytes 393224 | tf_op jit(solution)/shard_map/ppermute | solution.py:644
  12.0 0.0 collective-permute-start.6
  12.0 1.0 %collective-permute-start.4 = (bf16[256,256]{1,0:T(8,128)(2,1)}, bf16[256,256]{1,0:T(8,128)(2,1)S(1)}, u32[]{:S(2)}, u32[]{:S(2)}) collective-permute-start(bf16[256,256]{1,0:T(8,128)(2,1)} %get-tuple-element.34.refs_7_.refs_10_), channel_id=1, source_target_pairs={{0,4},{2,6},{4,8},{6,10},{8,12},{10,14},{12,0},{14,2},{1,5},{3,7},... | collective-permute-start | bytes 393224 | tf_op jit(solution)/shard_map/ppermute | solution.py:644
  13.0 0.7 copy.11.refs_2_
  13.7 0.0 collective-permute-done.refs_0_.refs_8_.refs_11_
  13.7 0.7 copy-done.7
  14.3 3.6 %prelude.1 = (f32[256,256]{1,0:T(8,128)}, bf16[2048,128]{1,0:T(8,128)(2,1)}, f32[8,512]{1,0:T(8,128)}, bf16[256,128]{1,0:T(8,128)(2,1)}) custom-call(bf16[256,256]{1,0:T(8,128)(2,1)} %copy-done.7, s32[14]{0:T(128)} %stack.59.refs_0_.refs_1_, s32[8,3]{1,0:T(8,128)} %copy.11.refs_2_, s32[8,8]{1,0:T(8,128)} %refs_3_.1, bf16[256,256]{1,0:T(8,128)(2,1)} %bitcast.28, ...), custom_call_target="tpu_custom_call" | custom-call | flops 4000000000 | bytes 12000000 | tf_op jit(solution)/shard_map/prelude/pallas_call | solution.py:56
  17.9 0.6 collective-permute-start.1
  18.5 0.0 collective-permute-done.8.refs_13_.refs_16_
  18.5 2.9 %collective-permute-start.9 = (bf16[256,256]{1,0:T(8,128)(2,1)}, bf16[256,256]{1,0:T(8,128)(2,1)S(1)}, u32[]{:S(2)}, u32[]{:S(2)}) collective-permute-start(bf16[256,256]{1,0:T(8,128)(2,1)} %copy-done.7), channel_id=1, source_target_pairs={{0,12},{2,14},{4,0},{6,2},{8,4},{10,6},{12,8},{14,10},{1,13},{3,15... | collective-permute-start | bytes 393224 | tf_op jit(solution)/shard_map/ppermute | solution.py:644
  21.5 2.8 %collective-permute-done.6.refs_11_.refs_14_ = bf16[256,256]{1,0:T(8,128)(2,1)S(1)} collective-permute-done((bf16[256,256]{1,0:T(8,128)(2,1)}, bf16[256,256]{1,0:T(8,128)(2,1)S(1)}, u32[]{:S(2)}, u32[]{:S(2)}) %collective-permute-start.6) | collective-permute-done | bytes 131104 | tf_op jit(solution)/shard_map/ppermute | solution.py:644
  24.3 0.0 collective-permute-start.7
  24.3 2.7 %collective-permute-done.2.refs_4_.refs_6_.refs_7_ = bf16[256,2048]{1,0:T(8,128)(2,1)S(1)} collective-permute-done((bf16[256,2048]{1,0:T(8,128)(2,1)}, bf16[256,2048]{1,0:T(8,128)(2,1)S(1)}, u32[]{:S(2)}, u32[]{:S(2)}) %collective-permute-start.2) | collective-permute-done | bytes 1048608 | tf_op jit(solution)/shard_map/ppermute | solution.py:639
  27.0 1.8 %collective-permute-start.5 = (bf16[256,256]{1,0:T(8,128)(2,1)}, bf16[256,256]{1,0:T(8,128)(2,1)S(1)}, u32[]{:S(2)}, u32[]{:S(2)}) collective-permute-start(bf16[256,256]{1,0:T(8,128)(2,1)} %copy-done.7), channel_id=1, source_target_pairs={{0,4},{2,6},{4,8},{6,10},{8,12},{10,14},{12,0},{14,2},{1,5},{3,7},... | collective-permute-start | bytes 393224 | tf_op jit(solution)/shard_map/ppermute | solution.py:644
  28.8 3.8 %grad_heads.1 = (bf16[128,256]{1,0:T(8,128)(2,1)}, bf16[128,256]{1,0:T(8,128)(2,1)}, bf16[256,2048]{1,0:T(8,128)(2,1)}) custom-call(s32[14]{0:T(128)} %stack.59.refs_0_.refs_1_, f32[256,256]{1,0:T(8,128)} %get-tuple-element.31.refs_1_, bf16[256,4096]{1,0:T(8,128)(2,1)} %refs_2_.2, bf16[256,2048]{1,0:T(8,128)(2,1)} %bitcast.23, bf16[256,2048]{1,0:T(8,128)(2,1)} %copy-done.4), custom_call_target="tpu_custom_call" | custom-call | flops 3000000000 | bytes 9000000 | tf_op jit(solution)/shard_map/grad_heads/pallas_call | solution.py:56
  32.6 0.0 collective-permute-done.4.refs_9_.refs_12_
  32.6 0.0 copy-start.10
  32.7 1.6 %collective-permute-start.3 = (bf16[128,256]{1,0:T(8,128)(2,1)}, bf16[128,256]{1,0:T(8,128)(2,1)S(1)}, u32[]{:S(2)}, u32[]{:S(2)}) collective-permute-start(bf16[128,256]{1,0:T(8,128)(2,1)} %get-tuple-element.33), channel_id=1, source_target_pairs={{0,2},{2,0},{4,6},{6,4},{8,10},{10,8},{12,14},{14,12},{1,3},{3,1},... | collective-permute-start | bytes 196616 | tf_op jit(solution)/shard_map/ppermute | solution.py:656
  34.2 0.0 collective-permute-done.1.refs_2_.refs_3_
  34.2 0.0 collective-permute-start.13
  34.2 0.0 collective-permute-done.9.refs_14_.refs_17_
  34.2 0.0 collective-permute-done.7.refs_12_.refs_15_
  34.3 0.0 collective-permute-done.5.refs_10_.refs_13_
  34.3 0.0 copy-start.13
  34.3 2.9 %collective-permute-done.3.refs_6_.refs_5_ = bf16[128,256]{1,0:T(8,128)(2,1)S(1)} collective-permute-done((bf16[128,256]{1,0:T(8,128)(2,1)}, bf16[128,256]{1,0:T(8,128)(2,1)S(1)}, u32[]{:S(2)}, u32[]{:S(2)}) %collective-permute-start.3) | collective-permute-done | bytes 65568 | tf_op jit(solution)/shard_map/ppermute | solution.py:656
  37.2 0.6 copy-done.15
  37.8 7.1 %forward.1 = (bf16[1,2048,512]{2,1,0:T(8,128)(2,1)}, f32[8,512]{1,0:T(8,128)}, bf16[128,256]{1,0:T(8,128)(2,1)}, bf16[128,256]{1,0:T(8,128)(2,1)}, bf16[8,256,128]{2,1,0:T(8,128)(2,1)}) custom-call(s32[14]{0:T(128)} %stack.59.refs_0_.refs_1_, bf16[256,256]{1,0:T(8,128)(2,1)} %bitcast.29, bf16[256,128]{1,0:T(8,128)(2,1)} %copy-done.14, ...), custom_call_target="tpu_custom_call" | custom-call | flops 20000000000 | bytes 60000000 | tf_op jit(solution)/shard_map/forward/pallas_call | solution.py:56
  44.9 0.1 collective-permute-start.12
  45.0 1.5 %collective-permute-start.10 = (bf16[128,256]{1,0:T(8,128)(2,1)}, bf16[128,256]{1,0:T(8,128)(2,1)S(1)}, u32[]{:S(2)}, u32[]{:S(2)}) collective-permute-start(bf16[128,256]{1,0:T(8,128)(2,1)} %get-tuple-element.36.refs_7_), channel_id=1, source_target_pairs={{0,2},{2,0},{4,6},{6,4},{8,10},{10,8},{12,14},{14,12},{1,3},{3,1},... | collective-permute-start | bytes 196616 | tf_op jit(solution)/shard_map/ppermute | solution.py:671
  46.5 0.3 collective-permute-start.11
  46.8 5.2 %all-to-all-start = ((bf16[8,256,128]{2,1,0:T(8,128)(2,1)}), bf16[8,256,128]{2,1,0:T(8,128)(2,1)S(1)}, u32[]{:S(2)}, u32[]{:S(2)}) async-start(bf16[8,256,128]{2,1,0:T(8,128)(2,1)} %get-tuple-element.42), calls=%async_computation | async-start | bytes 1048576 | tf_op jit(solution)/shard_map/all_to_all | solution.py:674
  52.0 0.0 collective-permute-done.12.refs_4_.refs_5_
  52.1 0.0 collective-permute-done.10.refs_2_.refs_3_
  52.1 0.0 collective-permute-done.11.refs_3_.refs_4_
  52.1 0.0 collective-permute-done.13.refs_7_.refs_8_
  52.1 0.6 copy-done.16
  52.7 0.0 copy-done.17
  52.7 0.0 copy-done.18
  52.7 1.0 copy-done.5
  53.7 3.9 %weight_sent.1.refs_0_ = bf16[4,256,256]{2,1,0:T(8,128)(2,1)} custom-call(s32[14]{0:T(128)} %stack.59.refs_0_.refs_1_, bf16[128,256]{1,0:T(8,128)(2,1)} %get-tuple-element.35.refs_1_.refs_6_.refs_2_, bf16[128,256]{1,0:T(8,128)(2,1)} %copy-done.17, bf16[128,256]{1,0:T(8,128)(2,1)} %copy-done.18, bf16[128,256]{1,0:T(8,128)(2,1)} %copy-done.16, ...), custom_call_target="tpu_custom_call" | custom-call | flops 4000000000 | bytes 12000000 | tf_op jit(solution)/shard_map/weight_sent/pallas_call | solution.py:56
  57.6 2.1 %collective-permute-start.14 = (bf16[4,256,256]{2,1,0:T(8,128)(2,1)}, bf16[4,256,256]{2,1,0:T(8,128)(2,1)S(1)}, u32[]{:S(2)}, u32[]{:S(2)}) collective-permute-start(bf16[4,256,256]{2,1,0:T(8,128)(2,1)} %weight_sent.1.refs_0_), channel_id=1, source_target_pairs={{0,2},{2,0},{4,6},{6,4},{8,10},{10,8},{12,14},{14,12},{1,3},{3,1},... | collective-permute-start | bytes 1572872 | tf_op jit(solution)/shard_map/ppermute | solution.py:678
  59.7 7.0 %key_terms.1 = (bf16[256,128]{1,0:T(8,128)(2,1)}, bf16[256,128]{1,0:T(8,128)(2,1)}, bf16[8,256,128]{2,1,0:T(8,128)(2,1)}) custom-call(bf16[4,256,256]{2,1,0:T(8,128)(2,1)} %weight_sent.1.refs_0_, s32[14]{0:T(128)} %stack.59.refs_0_.refs_1_, bf16[256,256]{1,0:T(8,128)(2,1)} %bitcast.30, bf16[256,128]{1,0:T(8,128)(2,1)} %copy-done.14, ...), custom_call_target="tpu_custom_call" | custom-call | flops 7000000000 | bytes 21000000 | tf_op jit(solution)/shard_map/key_terms/pallas_call | solution.py:56
  66.7 0.0 all-to-all-done.refs_1_
  66.7 4.6 %all-to-all-start.1 = ((bf16[8,256,128]{2,1,0:T(8,128)(2,1)}), bf16[8,256,128]{2,1,0:T(8,128)(2,1)S(1)}, u32[]{:S(2)}, u32[]{:S(2)}) async-start(bf16[8,256,128]{2,1,0:T(8,128)(2,1)} %get-tuple-element.44), calls=%async_computation.1 | async-start | bytes 1048576 | tf_op jit(solution)/shard_map/all_to_all | solution.py:674
  71.3 2.0 %collective-permute-start.15 = (bf16[256,128]{1,0:T(8,128)(2,1)}, bf16[256,128]{1,0:T(8,128)(2,1)S(1)}, u32[]{:S(2)}, u32[]{:S(2)}) collective-permute-start(bf16[256,128]{1,0:T(8,128)(2,1)} %get-tuple-element.43), channel_id=1, source_target_pairs={{0,2},{2,0},{4,6},{6,4},{8,10},{10,8},{12,14},{14,12},{1,3},{3,1},... | collective-permute-start | bytes 196616 | tf_op jit(solution)/shard_map/ppermute | solution.py:683
  73.3 0.0 collective-permute-done.14.refs_9_
  73.3 0.8 copy-done.6
  74.1 4.2 %weight_kept.1 = (bf16[256,256]{1,0:T(8,128)(2,1)}, bf16[256,256]{1,0:T(8,128)(2,1)}, bf16[256,256]{1,0:T(8,128)(2,1)}, bf16[256,256]{1,0:T(8,128)(2,1)}) custom-call(bf16[256,128]{1,0:T(8,128)(2,1)} %get-tuple-element.40.refs_0_.refs_2_, s32[14]{0:T(128)} %stack.59.refs_0_.refs_1_, bf16[128,256]{1,0:T(8,128)(2,1)} %get-tuple-element.35.refs_1_.refs_6_.refs_2_, ...), custom_call_target="tpu_custom_call" | custom-call | flops 4000000000 | bytes 12000000 | tf_op jit(solution)/shard_map/weight_kept/pallas_call | solution.py:56
  78.4 2.1 %collective-permute-start.16 = (bf16[256,256]{1,0:T(8,128)(2,1)}, bf16[256,256]{1,0:T(8,128)(2,1)S(1)}, u32[]{:S(2)}, u32[]{:S(2)}) collective-permute-start(bf16[256,256]{1,0:T(8,128)(2,1)} %get-tuple-element.47), channel_id=1, source_target_pairs={{0,4},{2,6},{4,8},{6,10},{8,12},{10,14},{12,0},{14,2},{1,5},{3,7},... | collective-permute-start | bytes 393224 | tf_op jit(solution)/shard_map/ppermute | solution.py:689
  80.5 3.9 %collective-permute-start.17 = (bf16[256,256]{1,0:T(8,128)(2,1)}, bf16[256,256]{1,0:T(8,128)(2,1)S(1)}, u32[]{:S(2)}, u32[]{:S(2)}) collective-permute-start(bf16[256,256]{1,0:T(8,128)(2,1)} %get-tuple-element.48), channel_id=1, source_target_pairs={{0,8},{2,10},{4,12},{6,14},{8,0},{10,2},{12,4},{14,6},{1,9},{3,11}... | collective-permute-start | bytes 393224 | tf_op jit(solution)/shard_map/ppermute | solution.py:689
  84.4 1.4 %collective-permute-start.18 = (bf16[256,256]{1,0:T(8,128)(2,1)}, bf16[256,256]{1,0:T(8,128)(2,1)S(1)}, u32[]{:S(2)}, u32[]{:S(2)}) collective-permute-start(bf16[256,256]{1,0:T(8,128)(2,1)} %get-tuple-element.49), channel_id=1, source_target_pairs={{0,12},{2,14},{4,0},{6,2},{8,4},{10,6},{12,8},{14,10},{1,13},{3,15... | collective-permute-start | bytes 393224 | tf_op jit(solution)/shard_map/ppermute | solution.py:689
  85.8 1.9 %collect_values.1.refs_0_ = bf16[256,256]{1,0:T(8,128)(2,1)} custom-call(bf16[256,256]{1,0:T(8,128)(2,1)} %get-tuple-element.41.refs_0_, bf16[8,256,128]{2,1,0:T(8,128)(2,1)} %copy-done), custom_call_target="tpu_custom_call" | custom-call | flops 2000000000 | bytes 6000000 | tf_op jit(solution)/shard_map/collect_values/pallas_call | solution.py:56
  87.7 0.9 collective-permute-done.16
  88.6 6.4 %collective-permute-done.17 = bf16[256,256]{1,0:T(8,128)(2,1)S(1)} collective-permute-done((bf16[256,256]{1,0:T(8,128)(2,1)}, bf16[256,256]{1,0:T(8,128)(2,1)S(1)}, u32[]{:S(2)}, u32[]{:S(2)}) %collective-permute-start.17) | collective-permute-done | bytes 131104 | tf_op jit(solution)/shard_map/ppermute | solution.py:689
  95.0 0.7 add_convert_fusion
  95.7 0.0 collective-permute-done.15.refs_3_
  95.7 0.0 all-to-all-done.1.refs_4_
  95.7 0.6 copy-done.19
  96.4 0.8 copy-done.1
  97.2 2.6 %collect_keys.1 = (bf16[256,256]{1,0:T(8,128)(2,1)}, bf16[256,256]{1,0:T(8,128)(2,1)}) custom-call(bf16[256,256]{1,0:T(8,128)(2,1)} %collect_values.1.refs_0_, s32[14]{0:T(128)} %stack.59.refs_0_.refs_1_, bf16[256,128]{1,0:T(8,128)(2,1)} %get-tuple-element.40.refs_0_.refs_2_, bf16[256,128]{1,0:T(8,128)(2,1)} %copy-done.19, bf16[8,256,128]{2,1,0:T(8,128)(2,1)} %copy-done.1), custom_call_target="tpu_custom_call" | custom-call | flops 2000000000 | bytes 6000000 | tf_op jit(solution)/shard_map/collect_keys/pallas_call | solution.py:56
  (30 shorter events, 0.1 us)
Async XLA Ops:
  0.6 26.4 %collective-permute-start.2 = (bf16[256,2048]{1,0:T(8,128)(2,1)}, bf16[256,2048]{1,0:T(8,128)(2,1)S(1)}, u32[]{:S(2)}, u32[]{:S(2)}) collective-permute-start(bf16[256,2048]{1,0:T(8,128)(2,1)} %bitcast.21), channel_id=1, source_target_pairs={{0,1},{1,0},{2,3},{3,2},{4,5},{5,4},{6,7},{7,6},{8,9},{9,8},{10,11... | collective-permute-start | bytes 3145736 | tf_op jit(solution)/shard_map/ppermute | solution.py:639
  4.3 8.6 %copy-start.3 = (s32[8,3]{0,1:T(4,128)S(1)}, s32[8,3]{0,1:T(4,128)}, u32[]{:S(2)}) copy-start(s32[8,3]{0,1:T(4,128)} %param.12) | copy-start | bytes 292
  6.8 6.9 %collective-permute-start = (bf16[256,256]{1,0:T(8,128)(2,1)}, bf16[256,256]{1,0:T(8,128)(2,1)S(1)}, u32[]{:S(2)}, u32[]{:S(2)}) collective-permute-start(bf16[256,256]{1,0:T(8,128)(2,1)} %get-tuple-element.27), channel_id=1, source_target_pairs={{0,2},{2,0},{4,6},{6,4},{8,10},{10,8},{12,14},{14,12},{1,3},{3,1},... | collective-permute-start | bytes 393224 | tf_op jit(solution)/shard_map/ppermute | solution.py:642
  8.4 10.2 %collective-permute-start.8 = (bf16[256,256]{1,0:T(8,128)(2,1)}, bf16[256,256]{1,0:T(8,128)(2,1)S(1)}, u32[]{:S(2)}, u32[]{:S(2)}) collective-permute-start(bf16[256,256]{1,0:T(8,128)(2,1)} %get-tuple-element.34.refs_7_.refs_10_), channel_id=1, source_target_pairs={{0,12},{2,14},{4,0},{6,2},{8,4},{10,6},{12,8},{14,10},{1,13},{3,15... | collective-permute-start | bytes 393224 | tf_op jit(solution)/shard_map/ppermute | solution.py:644
  12.0 12.4 %collective-permute-start.6 = (bf16[256,256]{1,0:T(8,128)(2,1)}, bf16[256,256]{1,0:T(8,128)(2,1)S(1)}, u32[]{:S(2)}, u32[]{:S(2)}) collective-permute-start(bf16[256,256]{1,0:T(8,128)(2,1)} %get-tuple-element.34.refs_7_.refs_10_), channel_id=1, source_target_pairs={{0,8},{2,10},{4,12},{6,14},{8,0},{10,2},{12,4},{14,6},{1,9},{3,11}... | collective-permute-start | bytes 393224 | tf_op jit(solution)/shard_map/ppermute | solution.py:644
  12.0 20.7 %collective-permute-start.4 = (bf16[256,256]{1,0:T(8,128)(2,1)}, bf16[256,256]{1,0:T(8,128)(2,1)S(1)}, u32[]{:S(2)}, u32[]{:S(2)}) collective-permute-start(bf16[256,256]{1,0:T(8,128)(2,1)} %get-tuple-element.34.refs_7_.refs_10_), channel_id=1, source_target_pairs={{0,4},{2,6},{4,8},{6,10},{8,12},{10,14},{12,0},{14,2},{1,5},{3,7},... | collective-permute-start | bytes 393224 | tf_op jit(solution)/shard_map/ppermute | solution.py:644
  13.7 0.7 copy-start.7
  17.9 16.3 %collective-permute-start.1 = (bf16[256,128]{1,0:T(8,128)(2,1)}, bf16[256,128]{1,0:T(8,128)(2,1)S(1)}, u32[]{:S(2)}, u32[]{:S(2)}) collective-permute-start(bf16[256,128]{1,0:T(8,128)(2,1)} %get-tuple-element.28), channel_id=1, source_target_pairs={{0,2},{2,0},{4,6},{6,4},{8,10},{10,8},{12,14},{14,12},{1,3},{3,1},... | collective-permute-start | bytes 196616 | tf_op jit(solution)/shard_map/ppermute | solution.py:652
  18.5 18.7 %copy-start.8 = (bf16[256,256]{1,0:T(8,128)(2,1)}, bf16[256,256]{1,0:T(8,128)(2,1)S(1)}, u32[]{:S(2)}) copy-start(bf16[256,256]{1,0:T(8,128)(2,1)S(1)} %collective-permute-done.8.refs_13_.refs_16_) | copy-start | bytes 393220
  18.5 15.7 %collective-permute-start.9 = (bf16[256,256]{1,0:T(8,128)(2,1)}, bf16[256,256]{1,0:T(8,128)(2,1)S(1)}, u32[]{:S(2)}, u32[]{:S(2)}) collective-permute-start(bf16[256,256]{1,0:T(8,128)(2,1)} %copy-done.7), channel_id=1, source_target_pairs={{0,12},{2,14},{4,0},{6,2},{8,4},{10,6},{12,8},{14,10},{1,13},{3,15... | collective-permute-start | bytes 393224 | tf_op jit(solution)/shard_map/ppermute | solution.py:644
  24.3 12.9 %copy-start.9 = (bf16[256,256]{1,0:T(8,128)(2,1)}, bf16[256,256]{1,0:T(8,128)(2,1)S(1)}, u32[]{:S(2)}) copy-start(bf16[256,256]{1,0:T(8,128)(2,1)S(1)} %collective-permute-done.6.refs_11_.refs_14_) | copy-start | bytes 393220
  24.3 9.9 %collective-permute-start.7 = (bf16[256,256]{1,0:T(8,128)(2,1)}, bf16[256,256]{1,0:T(8,128)(2,1)S(1)}, u32[]{:S(2)}, u32[]{:S(2)}) collective-permute-start(bf16[256,256]{1,0:T(8,128)(2,1)} %copy-done.7), channel_id=1, source_target_pairs={{0,8},{2,10},{4,12},{6,14},{8,0},{10,2},{12,4},{14,6},{1,9},{3,11}... | collective-permute-start | bytes 393224 | tf_op jit(solution)/shard_map/ppermute | solution.py:644
  27.0 1.8 %copy-start.4 = (bf16[256,2048]{1,0:T(8,128)(2,1)}, bf16[256,2048]{1,0:T(8,128)(2,1)S(1)}, u32[]{:S(2)}) copy-start(bf16[256,2048]{1,0:T(8,128)(2,1)S(1)} %collective-permute-done.2.refs_4_.refs_6_.refs_7_) | copy-start | bytes 3145732
  27.0 7.2 %collective-permute-start.5 = (bf16[256,256]{1,0:T(8,128)(2,1)}, bf16[256,256]{1,0:T(8,128)(2,1)S(1)}, u32[]{:S(2)}, u32[]{:S(2)}) collective-permute-start(bf16[256,256]{1,0:T(8,128)(2,1)} %copy-done.7), channel_id=1, source_target_pairs={{0,4},{2,6},{4,8},{6,10},{8,12},{10,14},{12,0},{14,2},{1,5},{3,7},... | collective-permute-start | bytes 393224 | tf_op jit(solution)/shard_map/ppermute | solution.py:644
  32.6 4.6 %copy-start.10 = (bf16[256,256]{1,0:T(8,128)(2,1)}, bf16[256,256]{1,0:T(8,128)(2,1)S(1)}, u32[]{:S(2)}) copy-start(bf16[256,256]{1,0:T(8,128)(2,1)S(1)} %collective-permute-done.4.refs_9_.refs_12_) | copy-start | bytes 393220
  32.7 4.5 %collective-permute-start.3 = (bf16[128,256]{1,0:T(8,128)(2,1)}, bf16[128,256]{1,0:T(8,128)(2,1)S(1)}, u32[]{:S(2)}, u32[]{:S(2)}) collective-permute-start(bf16[128,256]{1,0:T(8,128)(2,1)} %get-tuple-element.33), channel_id=1, source_target_pairs={{0,2},{2,0},{4,6},{6,4},{8,10},{10,8},{12,14},{14,12},{1,3},{3,1},... | collective-permute-start | bytes 196616 | tf_op jit(solution)/shard_map/ppermute | solution.py:656
  34.2 3.0 %copy-start.14 = (bf16[256,128]{1,0:T(8,128)(2,1)}, bf16[256,128]{1,0:T(8,128)(2,1)S(1)}, u32[]{:S(2)}) copy-start(bf16[256,128]{1,0:T(8,128)(2,1)S(1)} %collective-permute-done.1.refs_2_.refs_3_) | copy-start | bytes 196612
  34.2 17.9 %collective-permute-start.13 = (bf16[256,2048]{1,0:T(8,128)(2,1)}, bf16[256,2048]{1,0:T(8,128)(2,1)S(1)}, u32[]{:S(2)}, u32[]{:S(2)}) collective-permute-start(bf16[256,2048]{1,0:T(8,128)(2,1)} %get-tuple-element.37), channel_id=1, source_target_pairs={{0,16},{16,0},{1,17},{17,1},{2,18},{18,2},{3,19},{19,3},{4,20},{20... | collective-permute-start | bytes 3145736 | tf_op jit(solution)/shard_map/ppermute | solution.py:658
  34.2 3.0 %copy-start.11 = (bf16[256,256]{1,0:T(8,128)(2,1)}, bf16[256,256]{1,0:T(8,128)(2,1)S(1)}, u32[]{:S(2)}) copy-start(bf16[256,256]{1,0:T(8,128)(2,1)S(1)} %collective-permute-done.9.refs_14_.refs_17_) | copy-start | bytes 393220
  34.3 3.0 %copy-start.12 = (bf16[256,256]{1,0:T(8,128)(2,1)}, bf16[256,256]{1,0:T(8,128)(2,1)S(1)}, u32[]{:S(2)}) copy-start(bf16[256,256]{1,0:T(8,128)(2,1)S(1)} %collective-permute-done.7.refs_12_.refs_15_) | copy-start | bytes 393220
  34.3 3.0 %copy-start.13 = (bf16[256,256]{1,0:T(8,128)(2,1)}, bf16[256,256]{1,0:T(8,128)(2,1)S(1)}, u32[]{:S(2)}) copy-start(bf16[256,256]{1,0:T(8,128)(2,1)S(1)} %collective-permute-done.5.refs_10_.refs_13_) | copy-start | bytes 393220
  37.2 0.6 copy-start.15
  44.9 7.1 %collective-permute-start.12 = (bf16[128,256]{1,0:T(8,128)(2,1)}, bf16[128,256]{1,0:T(8,128)(2,1)S(1)}, u32[]{:S(2)}, u32[]{:S(2)}) collective-permute-start(bf16[128,256]{1,0:T(8,128)(2,1)} %get-tuple-element.36.refs_7_), channel_id=1, source_target_pairs={{0,18},{2,16},{4,22},{6,20},{8,26},{10,24},{12,30},{14,28},{16,2},... | collective-permute-start | bytes 196616 | tf_op jit(solution)/shard_map/ppermute | solution.py:671
  45.0 7.1 %collective-permute-start.10 = (bf16[128,256]{1,0:T(8,128)(2,1)}, bf16[128,256]{1,0:T(8,128)(2,1)S(1)}, u32[]{:S(2)}, u32[]{:S(2)}) collective-permute-start(bf16[128,256]{1,0:T(8,128)(2,1)} %get-tuple-element.36.refs_7_), channel_id=1, source_target_pairs={{0,2},{2,0},{4,6},{6,4},{8,10},{10,8},{12,14},{14,12},{1,3},{3,1},... | collective-permute-start | bytes 196616 | tf_op jit(solution)/shard_map/ppermute | solution.py:671
  46.5 5.6 %collective-permute-start.11 = (bf16[128,256]{1,0:T(8,128)(2,1)}, bf16[128,256]{1,0:T(8,128)(2,1)S(1)}, u32[]{:S(2)}, u32[]{:S(2)}) collective-permute-start(bf16[128,256]{1,0:T(8,128)(2,1)} %get-tuple-element.35.refs_1_.refs_6_.refs_2_), channel_id=1, source_target_pairs={{0,16},{2,18},{4,20},{6,22},{8,24},{10,26},{12,28},{14,30},{16,0},... | collective-permute-start | bytes 196616 | tf_op jit(solution)/shard_map/ppermute | solution.py:671
  46.8 19.9 %all-to-all-start = ((bf16[8,256,128]{2,1,0:T(8,128)(2,1)}), bf16[8,256,128]{2,1,0:T(8,128)(2,1)S(1)}, u32[]{:S(2)}, u32[]{:S(2)}) async-start(bf16[8,256,128]{2,1,0:T(8,128)(2,1)} %get-tuple-element.42), calls=%async_computation | async-start | bytes 1048576 | tf_op jit(solution)/shard_map/all_to_all | solution.py:674
  52.0 0.6 copy-start.16
  52.1 0.6 copy-start.17
  52.1 0.6 copy-start.18
  52.7 1.0 copy-start.5
  57.6 15.7 %collective-permute-start.14 = (bf16[4,256,256]{2,1,0:T(8,128)(2,1)}, bf16[4,256,256]{2,1,0:T(8,128)(2,1)S(1)}, u32[]{:S(2)}, u32[]{:S(2)}) collective-permute-start(bf16[4,256,256]{2,1,0:T(8,128)(2,1)} %weight_sent.1.refs_0_), channel_id=1, source_target_pairs={{0,2},{2,0},{4,6},{6,4},{8,10},{10,8},{12,14},{14,12},{1,3},{3,1},... | collective-permute-start | bytes 1572872 | tf_op jit(solution)/shard_map/ppermute | solution.py:678
  66.7 11.6 %copy-start = (bf16[8,256,128]{2,1,0:T(8,128)(2,1)}, bf16[8,256,128]{2,1,0:T(8,128)(2,1)S(1)}, u32[]{:S(2)}) copy-start(bf16[8,256,128]{2,1,0:T(8,128)(2,1)S(1)} %all-to-all-done.refs_1_) | copy-start | bytes 1572868
  66.7 29.0 %all-to-all-start.1 = ((bf16[8,256,128]{2,1,0:T(8,128)(2,1)}), bf16[8,256,128]{2,1,0:T(8,128)(2,1)S(1)}, u32[]{:S(2)}, u32[]{:S(2)}) async-start(bf16[8,256,128]{2,1,0:T(8,128)(2,1)} %get-tuple-element.44), calls=%async_computation.1 | async-start | bytes 1048576 | tf_op jit(solution)/shard_map/all_to_all | solution.py:674
  71.3 24.4 %collective-permute-start.15 = (bf16[256,128]{1,0:T(8,128)(2,1)}, bf16[256,128]{1,0:T(8,128)(2,1)S(1)}, u32[]{:S(2)}, u32[]{:S(2)}) collective-permute-start(bf16[256,128]{1,0:T(8,128)(2,1)} %get-tuple-element.43), channel_id=1, source_target_pairs={{0,2},{2,0},{4,6},{6,4},{8,10},{10,8},{12,14},{14,12},{1,3},{3,1},... | collective-permute-start | bytes 196616 | tf_op jit(solution)/shard_map/ppermute | solution.py:683
  73.3 0.8 copy-start.6
  78.4 10.2 %collective-permute-start.16 = (bf16[256,256]{1,0:T(8,128)(2,1)}, bf16[256,256]{1,0:T(8,128)(2,1)S(1)}, u32[]{:S(2)}, u32[]{:S(2)}) collective-permute-start(bf16[256,256]{1,0:T(8,128)(2,1)} %get-tuple-element.47), channel_id=1, source_target_pairs={{0,4},{2,6},{4,8},{6,10},{8,12},{10,14},{12,0},{14,2},{1,5},{3,7},... | collective-permute-start | bytes 393224 | tf_op jit(solution)/shard_map/ppermute | solution.py:689
  80.5 14.5 %collective-permute-start.17 = (bf16[256,256]{1,0:T(8,128)(2,1)}, bf16[256,256]{1,0:T(8,128)(2,1)S(1)}, u32[]{:S(2)}, u32[]{:S(2)}) collective-permute-start(bf16[256,256]{1,0:T(8,128)(2,1)} %get-tuple-element.48), channel_id=1, source_target_pairs={{0,8},{2,10},{4,12},{6,14},{8,0},{10,2},{12,4},{14,6},{1,9},{3,11}... | collective-permute-start | bytes 393224 | tf_op jit(solution)/shard_map/ppermute | solution.py:689
  84.4 10.6 %collective-permute-start.18 = (bf16[256,256]{1,0:T(8,128)(2,1)}, bf16[256,256]{1,0:T(8,128)(2,1)S(1)}, u32[]{:S(2)}, u32[]{:S(2)}) collective-permute-start(bf16[256,256]{1,0:T(8,128)(2,1)} %get-tuple-element.49), channel_id=1, source_target_pairs={{0,12},{2,14},{4,0},{6,2},{8,4},{10,6},{12,8},{14,10},{1,13},{3,15... | collective-permute-start | bytes 393224 | tf_op jit(solution)/shard_map/ppermute | solution.py:689
  85.8 9.2 %copy-start.2 = (bf16[256,256]{1,0:T(8,128)(2,1)S(1)}, bf16[256,256]{1,0:T(8,128)(2,1)}, u32[]{:S(2)}) copy-start(bf16[256,256]{1,0:T(8,128)(2,1)} %get-tuple-element.41.refs_0_) | copy-start | bytes 393220
  95.7 0.6 copy-start.19
  96.4 0.8 copy-start.1

commit v9 on v8

--- a/solution.py
+++ b/solution.py
@@ -41,7 +41,7 @@
         in_specs=in_specs,
         out_specs=out_specs,
         scratch_shapes=scratch,
-        compiler_params=pltpu.CompilerParams(vmem_limit_bytes=60 * 1024 * 1024),
+        compiler_params=pltpu.CompilerParams(vmem_limit_bytes=64 * 1024 * 1024),
         cost_estimate=pl.CostEstimate(
             flops=int(micros * 1e9), bytes_accessed=int(micros * 3e6), transcendentals=0
         ),
@@ -390,15 +390,25 @@
     width = grads[0].shape[1]
     first_load = begin(first_ref, first_s, first_sem)
     weight_loads, grad_loads = [], []
-    for k in range(part_count):
+    for k in range(1, part_count):
+        start = pl.multiple_of(at_ref[columns_at + k - 1] * width, width)
+        columns = weight_ref.at[:, pl.ds(start, width)]
+        weight_loads.append(begin(columns, weight_s.at[k - 1], weight_sem.at[k - 1]))
         grad_loads.append(begin(grads[k], grad_s.at[k], grad_sem.at[k]))
-        if k:
-            start = pl.multiple_of(at_ref[columns_at + k - 1] * width, width)
-            columns = weight_ref.at[:, pl.ds(start, width)]
-            weight_loads.append(begin(columns, weight_s.at[k - 1], weight_sem.at[k - 1]))
-    for load in grad_loads:
-        load.wait()
+    own_load = begin(grads[0], grad_s.at[0], grad_sem.at[0])
+    first_load.wait()
+    summed = first_s[...]
+    for k in range(1, part_count):
+        weight_loads[k - 1].wait()
+        grad_loads[k - 1].wait()
+        summed = summed + against(weight_s[k - 1], grad_s[k])
+    first_s[...] = summed
     copies = []
+    for side, at in enumerate((at_ref[0], 1 - at_ref[0])):
+        kept = first_s[pl.ds(pl.multiple_of(at * half, half), half), :]
+        out_s[side] = kept.astype(jnp.bfloat16)
+        copies.append(begin(out_s.at[side], outs[side], out_sem.at[side]))
+    own_load.wait()
     for send in range(sends):
         for i in range(picked):
             place = send * picked + i
@@ -410,16 +420,6 @@
                     begin(grad_s.at[k], target, send_sem.at[place])
 
             copies.append(pltpu.make_async_copy(grad_s.at[0], target, send_sem.at[place]))
-    first_load.wait()
-    summed = first_s[...]
-    for k in range(1, part_count):
-        weight_loads[k - 1].wait()
-        summed = summed + against(weight_s[k - 1], grad_s[k])
-    first_s[...] = summed
-    for side, at in enumerate((at_ref[0], 1 - at_ref[0])):
-        kept = first_s[pl.ds(pl.multiple_of(at * half, half), half), :]
-        out_s[side] = kept.astype(jnp.bfloat16)
-        copies.append(begin(out_s.at[side], outs[side], out_sem.at[side]))
     for copy in copies:
         copy.wait()
 
@@ -459,9 +459,11 @@
         out, refs = refs[0], refs[1:]
         outs = [out.at[k] for k in range(out.shape[0])]
     else:
-        recv, refs = refs[0], refs[1:]
+        recv, passed, refs = refs[0], refs[1], refs[2:]
         outs, refs = refs[: recv.shape[0]], refs[recv.shape[0] :]
-        recv_s, recv_sem, refs = refs[0], refs[1], refs[2:]
+        passed_out, recv_s, passed_s, recv_sem, passed_sem = refs[:5]
+        refs = refs[5:]
+        passed_load = begin(passed, passed_s, passed_sem)
     attn_s, grad_s, out_s, attn_sem, grad_sem, out_sem = refs
     outer, feats, width = out_s.shape
     half = feats // INNER
@@ -496,6 +498,9 @@
     for load in attn_loads:
         load.wait()
     stores = []
+    if not sent:
+        passed_load.wait()
+        stores.append(begin(passed_s, passed_out, passed_sem))
     for k in range(outer):
         term = 0.0
         for doc in range(doc_count):
@@ -510,13 +515,13 @@
         store.wait()
 
 
-def weight_terms(at, step_at, attn, grads, swapped, outer, picked, recv=None, after=()):
+def weight_terms(at, step_at, attn, grads, swapped, outer, picked, recv=None, passed=None, after=()):
     half, rows = attn[0].shape
     feats = half * INNER
     doc_count = len(attn) // INNER
     width = picked * grads[0].shape[1] // (outer * INNER)
     sent = recv is None
-    operands = [*attn, *grads, *swapped] + ([] if sent else [recv])
+    operands = [*attn, *grads, *swapped] + ([] if sent else [recv, passed])
     scratch = [
         pltpu.VMEM((doc_count, feats, rows), jnp.bfloat16),
         pltpu.VMEM((doc_count, outer, rows, width), jnp.bfloat16),
@@ -526,13 +531,17 @@
         pltpu.SemaphoreType.DMA((outer,)),
     ]
     if not sent:
-        added = [pltpu.VMEM((outer, feats, width), jnp.bfloat16), pltpu.SemaphoreType.DMA((outer,))]
-        scratch = added + scratch
+        scratch = [
+            pltpu.VMEM((outer, feats, width), jnp.bfloat16),
+            pltpu.VMEM(passed.shape, jnp.bfloat16),
+            pltpu.SemaphoreType.DMA((outer,)),
+            pltpu.SemaphoreType.DMA,
+        ] + scratch
     return call(
         functools.partial(weight_kernel, len(grads), doc_count, sent, step_at),
-        bf16(outer, feats, width) if sent else [bf16(feats, width)] * outer,
+        bf16(outer, feats, width) if sent else [bf16(feats, width)] * outer + [bf16(*passed.shape)],
         [SMEM] + [ANY] * len(operands),
-        ANY if sent else [ANY] * outer,
+        ANY if sent else [ANY] * (outer + 1),
         scratch,
         4,
         "weight_sent" if sent else "weight_kept",
@@ -680,18 +689,20 @@
         at, queries[0], q_recv, g_mine, g_recv, attn_mine, attn_theirs, inverse, weights, kv_blocks, (send,)
     )
     key_parts = returned(key_parts)
+    *weight_sums, dq_theirs = weight_terms(
+        at, keep_at, attn, grads, swapped, outer, picked, weight_recv, dq_theirs
+    )
+    weight_parts = [
+        lax.ppermute(weight_sums[step], "ctx", ctx_pairs(step, 0)) for step in range(1, outer)
+    ]
     dq_recv = lax.ppermute(dq_theirs, "ctx", ctx_pairs(0, 1))
-    weight_sums = weight_terms(
-        at, keep_at, attn, grads, swapped, outer, picked, weight_recv, (dq_mine,)
-    )
-    grad_weight = weight_sums[0].astype(jnp.float32)
-    for step in range(1, outer):
-        grad_weight = grad_weight + lax.ppermute(
-            weight_sums[step], "ctx", ctx_pairs(step, 0)
-        ).astype(jnp.float32)
-
     grad_v = collect(value_parts, "collect_values", (), (weight_sums[0],))
     grad_q, grad_k = collect(key_parts, "collect_keys", (at, dq_mine, dq_recv), (grad_v,))
+    weight_parts, grad_k = lax.optimization_barrier((weight_parts, grad_k))
+    grad_weight = weight_sums[0].astype(jnp.float32)
+    for part in weight_parts:
+        grad_weight = grad_weight + part.astype(jnp.float32)
+
     return grad_q[None], grad_k[None], grad_v[None], grad_weight.astype(jnp.bfloat16)
 
 

time: 100 us -> 97.3 us (0.973)
  waiting for transfers between devices: 15.8 us -> 20.5 us
  starting transfers between devices: 39.3 us -> 34.7 us
  local copies, waits for them, and re-layouts: 6.45 us -> 1.93 us
  other arithmetic: 0.72 us -> 1.82 us
    all_to_all x2, waiting for transfers between devices: 0.01 us -> 9.91 us  [returned(): return lax.all_to_all(parts, 'ctx', split_axis=0, concat_axis=0, tiled=True)]
    ppermute x3, waiting for transfers between devices: 7.31 us -> 0.01 us  [per_device(): lax.ppermute(weight_sums[step], 'ctx', ctx_pairs(step, 0))]
    unnamed x41 -> x1, local copies, waits for them, and re-layouts: 5.78 us -> 1.35 us
    ppermute x3, starting transfers between devices: 7.42 us -> 4.97 us  [per_device(): lax.ppermute(weight_sums[step], 'ctx', ctx_pairs(step, 0))]
    ppermute x1, waiting for transfers between devices: 0.01 us -> 1.52 us  [per_device(): weight_recv = lax.ppermute(send, 'ctx', ctx_pairs(0, 1))]
    ppermute x1, starting transfers between devices: 2.02 us -> 0.79 us  [per_device(): dq_recv = lax.ppermute(dq_theirs, 'ctx', ctx_pairs(0, 1))]
    convert_element_type x1, other arithmetic: 0.72 us -> 1.82 us  [per_device(): grad_weight.astype(jnp.bfloat16)]
  transfers between devices with their start and end apart: 21 -> 21, of which waited for: 5 -> 6; matrix products, arithmetic and copies ran while one was open for 2% -> 2% of each run, Pallas kernels for 34% -> 38%
where the time goes in v9:
time: 97.3 us; the launch traced here: 96.6 us
  Pallas kernels  36.8 us (38%)
  starting transfers between devices  34.7 us (36%)
  waiting for transfers between devices  20.5 us (21%)
  local copies, waits for them, and re-layouts  1.93 us (2%)
  other arithmetic  1.82 us (2%)
    pallas_call x9, Pallas kernels, placed(): return run(*args)  36.8 us
    all_to_all x2, waiting for transfers between devices, returned(): return lax.all_to_all(parts, 'ctx', split_axis=0, concat_axis=0, tiled=True)  9.91 us
    ppermute x6, starting transfers between devices, per_device(): lax.ppermute(kv_recv if side else kv_mine, 'ctx', ctx_pairs(step, 0))  9.22 us
    all_to_all x2, starting transfers between devices, returned(): return lax.all_to_all(parts, 'ctx', split_axis=0, concat_axis=0, tiled=True)  8.93 us
    ppermute x3, starting transfers between devices, per_device(): lax.ppermute(weight_sums[step], 'ctx', ctx_pairs(step, 0))  4.97 us
    ppermute x1, waiting for transfers between devices, per_device(): lax.ppermute(grad_own, 'tp', shift_pairs(tp_count, -step))  3.06 us
    ppermute x1, waiting for transfers between devices, per_device(): g_recv = lax.ppermute(g_theirs, 'ctx', ctx_pairs(0, 1))  3.06 us
    ppermute x1, starting transfers between devices, per_device(): lax.ppermute(grad_own, 'tp', shift_pairs(tp_count, -step))  3.03 us
  transfers between devices with their start and end apart: 21, of which 6 were waited for; matrix products, arithmetic and copies ran while one was open for 2% of the time, Pallas kernels for 38%

profile of v9, /device:TPU:0, one launch (start us, length us, event | category | flops | bytes accessed | tf_op | source)
XLA Modules:
  0.0 96.6 jit_solution(9033536432916494950)
XLA Ops:
  0.6 3.0 %collective-permute-start.2 = (bf16[256,2048]{1,0:T(8,128)(2,1)}, bf16[256,2048]{1,0:T(8,128)(2,1)}, u32[]{:S(2)}, u32[]{:S(2)}) collective-permute-start(bf16[256,2048]{1,0:T(8,128)(2,1)} %bitcast.21), channel_id=1, source_target_pairs={{0,1},{1,0},{2,3},{3,2},{4,5},{5,4},{6,7},{7,6},{8,9},{9,8},{10,11... | collective-permute-start | bytes 3145736 | tf_op jit(solution)/shard_map/ppermute | solution.py:648
  3.7 0.6 stack.59.refs_0_.refs_1_
  4.2 2.3 %part_heads.1 = (bf16[256,256]{1,0:T(8,128)(2,1)}, bf16[256,256]{1,0:T(8,128)(2,1)}) custom-call(s32[14]{0:T(128)} %stack.59.refs_0_.refs_1_, bf16[256,256]{1,0:T(8,128)(2,1)} %bitcast.26, bf16[256,256]{1,0:T(8,128)(2,1)} %bitcast.27), custom_call_target="tpu_custom_call" | custom-call | flops 2000000000 | bytes 6000000 | tf_op jit(solution)/shard_map/part_heads/pallas_call | solution.py:56
  6.6 1.6 %collective-permute-start = (bf16[256,256]{1,0:T(8,128)(2,1)}, bf16[256,256]{1,0:T(8,128)(2,1)}, u32[]{:S(2)}, u32[]{:S(2)}) collective-permute-start(bf16[256,256]{1,0:T(8,128)(2,1)} %get-tuple-element.32), channel_id=1, source_target_pairs={{0,2},{2,0},{4,6},{6,4},{8,10},{10,8},{12,14},{14,12},{1,3},{3,1},... | collective-permute-start | bytes 393224 | tf_op jit(solution)/shard_map/ppermute | solution.py:651
  8.1 3.6 %collective-permute-start.8 = (bf16[256,256]{1,0:T(8,128)(2,1)}, bf16[256,256]{1,0:T(8,128)(2,1)}, u32[]{:S(2)}, u32[]{:S(2)}) collective-permute-start(bf16[256,256]{1,0:T(8,128)(2,1)} %get-tuple-element.39.refs_7_.refs_10_), channel_id=1, source_target_pairs={{0,12},{2,14},{4,0},{6,2},{8,4},{10,6},{12,8},{14,10},{1,13},{3,15... | collective-permute-start | bytes 393224 | tf_op jit(solution)/shard_map/ppermute | solution.py:653
  11.7 0.0 collective-permute-start.6
  11.7 1.0 %collective-permute-start.4 = (bf16[256,256]{1,0:T(8,128)(2,1)}, bf16[256,256]{1,0:T(8,128)(2,1)}, u32[]{:S(2)}, u32[]{:S(2)}) collective-permute-start(bf16[256,256]{1,0:T(8,128)(2,1)} %get-tuple-element.39.refs_7_.refs_10_), channel_id=1, source_target_pairs={{0,4},{2,6},{4,8},{6,10},{8,12},{10,14},{12,0},{14,2},{1,5},{3,7},... | collective-permute-start | bytes 393224 | tf_op jit(solution)/shard_map/ppermute | solution.py:653
  12.8 1.3 %copy.11.refs_2_ = s32[8,3]{1,0:T(8,128)} copy(s32[8,3]{0,1:T(4,128)} %param.12) | data formatting | bytes 192 | tf_op args[5]
  14.1 0.0 collective-permute-done.refs_0_.refs_8_.refs_11_
  14.1 3.6 %prelude.1 = (f32[256,256]{1,0:T(8,128)}, bf16[2048,128]{1,0:T(8,128)(2,1)}, f32[8,512]{1,0:T(8,128)}, bf16[256,128]{1,0:T(8,128)(2,1)}) custom-call(bf16[256,256]{1,0:T(8,128)(2,1)} %collective-permute-done.refs_0_.refs_8_.refs_11_, s32[14]{0:T(128)} %stack.59.refs_0_.refs_1_, s32[8,3]{1,0:T(8,128)} %copy.11.refs_2_, s32[8,8]{1,0:T(8,128)} %refs_3_.1, ...), custom_call_target="tpu_custom_call" | custom-call | flops 4000000000 | bytes 12000000 | tf_op jit(solution)/shard_map/prelude/pallas_call | solution.py:56
  17.7 0.6 collective-permute-start.1
  18.3 0.0 collective-permute-done.8.refs_13_.refs_16_
  18.3 2.8 %collective-permute-start.9 = (bf16[256,256]{1,0:T(8,128)(2,1)}, bf16[256,256]{1,0:T(8,128)(2,1)}, u32[]{:S(2)}, u32[]{:S(2)}) collective-permute-start(bf16[256,256]{1,0:T(8,128)(2,1)} %collective-permute-done.refs_0_.refs_8_.refs_11_), channel_id=1, source_target_pairs={{0,12},{2,14},{4,0},{6,2},{8,4},{10,6},{12,8},{14,10},{1,13},{3,15... | collective-permute-start | bytes 393224 | tf_op jit(solution)/shard_map/ppermute | solution.py:653
  21.1 2.9 %collective-permute-done.6.refs_11_.refs_14_ = bf16[256,256]{1,0:T(8,128)(2,1)} collective-permute-done((bf16[256,256]{1,0:T(8,128)(2,1)}, bf16[256,256]{1,0:T(8,128)(2,1)}, u32[]{:S(2)}, u32[]{:S(2)}) %collective-permute-start.6) | collective-permute-done | bytes 131104 | tf_op jit(solution)/shard_map/ppermute | solution.py:653
  24.1 0.0 collective-permute-start.7
  24.1 3.1 %collective-permute-done.2.refs_4_.refs_6_ = bf16[256,2048]{1,0:T(8,128)(2,1)} collective-permute-done((bf16[256,2048]{1,0:T(8,128)(2,1)}, bf16[256,2048]{1,0:T(8,128)(2,1)}, u32[]{:S(2)}, u32[]{:S(2)}) %collective-permute-start.2) | collective-permute-done | bytes 1048608 | tf_op jit(solution)/shard_map/ppermute | solution.py:648
  27.1 1.8 %collective-permute-start.5 = (bf16[256,256]{1,0:T(8,128)(2,1)}, bf16[256,256]{1,0:T(8,128)(2,1)}, u32[]{:S(2)}, u32[]{:S(2)}) collective-permute-start(bf16[256,256]{1,0:T(8,128)(2,1)} %collective-permute-done.refs_0_.refs_8_.refs_11_), channel_id=1, source_target_pairs={{0,4},{2,6},{4,8},{6,10},{8,12},{10,14},{12,0},{14,2},{1,5},{3,7},... | collective-permute-start | bytes 393224 | tf_op jit(solution)/shard_map/ppermute | solution.py:653
  28.9 4.2 %grad_heads.1 = (bf16[128,256]{1,0:T(8,128)(2,1)}, bf16[128,256]{1,0:T(8,128)(2,1)}, bf16[256,2048]{1,0:T(8,128)(2,1)}) custom-call(s32[14]{0:T(128)} %stack.59.refs_0_.refs_1_, f32[256,256]{1,0:T(8,128)} %get-tuple-element.36.refs_1_, bf16[256,4096]{1,0:T(8,128)(2,1)} %refs_2_.2, bf16[256,2048]{1,0:T(8,128)(2,1)} %bitcast.23, ...), custom_call_target="tpu_custom_call" | custom-call | flops 3000000000 | bytes 9000000 | tf_op jit(solution)/shard_map/grad_heads/pallas_call | solution.py:56
  33.1 0.0 collective-permute-done.4.refs_9_.refs_12_
  33.1 1.6 %collective-permute-start.3 = (bf16[128,256]{1,0:T(8,128)(2,1)}, bf16[128,256]{1,0:T(8,128)(2,1)}, u32[]{:S(2)}, u32[]{:S(2)}) collective-permute-start(bf16[128,256]{1,0:T(8,128)(2,1)} %get-tuple-element.38), channel_id=1, source_target_pairs={{0,2},{2,0},{4,6},{6,4},{8,10},{10,8},{12,14},{14,12},{1,3},{3,1},... | collective-permute-start | bytes 196616 | tf_op jit(solution)/shard_map/ppermute | solution.py:665
  34.7 0.0 collective-permute-done.1.refs_2_.refs_3_
  34.7 0.0 collective-permute-start.13
  34.7 0.0 collective-permute-done.9.refs_14_.refs_17_
  34.7 0.0 collective-permute-done.7.refs_12_.refs_15_
  34.7 0.0 collective-permute-done.5.refs_10_.refs_13_
  34.7 3.1 %collective-permute-done.3.refs_6_.refs_5_ = bf16[128,256]{1,0:T(8,128)(2,1)} collective-permute-done((bf16[128,256]{1,0:T(8,128)(2,1)}, bf16[128,256]{1,0:T(8,128)(2,1)}, u32[]{:S(2)}, u32[]{:S(2)}) %collective-permute-start.3) | collective-permute-done | bytes 65568 | tf_op jit(solution)/shard_map/ppermute | solution.py:665
  37.8 7.1 %forward.1 = (bf16[1,2048,512]{2,1,0:T(8,128)(2,1)}, f32[8,512]{1,0:T(8,128)}, bf16[128,256]{1,0:T(8,128)(2,1)}, bf16[128,256]{1,0:T(8,128)(2,1)}, bf16[8,256,128]{2,1,0:T(8,128)(2,1)}) custom-call(s32[14]{0:T(128)} %stack.59.refs_0_.refs_1_, bf16[256,256]{1,0:T(8,128)(2,1)} %bitcast.29, bf16[256,128]{1,0:T(8,128)(2,1)} %collective-permute-done.1.refs_2_.refs_3_, ...), custom_call_target="tpu_custom_call" | custom-call | flops 20000000000 | bytes 60000000 | tf_op jit(solution)/shard_map/forward/pallas_call | solution.py:56
  44.9 0.1 collective-permute-start.12
  44.9 1.6 %collective-permute-start.10 = (bf16[128,256]{1,0:T(8,128)(2,1)}, bf16[128,256]{1,0:T(8,128)(2,1)}, u32[]{:S(2)}, u32[]{:S(2)}) collective-permute-start(bf16[128,256]{1,0:T(8,128)(2,1)} %get-tuple-element.41.refs_7_), channel_id=1, source_target_pairs={{0,2},{2,0},{4,6},{6,4},{8,10},{10,8},{12,14},{14,12},{1,3},{3,1},... | collective-permute-start | bytes 196616 | tf_op jit(solution)/shard_map/ppermute | solution.py:680
  46.5 0.3 collective-permute-start.11
  46.8 4.8 %all-to-all-start = ((bf16[8,256,128]{2,1,0:T(8,128)(2,1)}), bf16[8,256,128]{2,1,0:T(8,128)(2,1)}, u32[]{:S(2)}, u32[]{:S(2)}) async-start(bf16[8,256,128]{2,1,0:T(8,128)(2,1)} %get-tuple-element.47), calls=%async_computation | async-start | bytes 1048576 | tf_op jit(solution)/shard_map/all_to_all | solution.py:683
  51.6 0.0 collective-permute-done.12.refs_4_
  51.6 0.0 collective-permute-done.10.refs_2_
  51.6 0.0 collective-permute-done.11.refs_3_
  51.6 0.0 collective-permute-done.13.refs_7_
  51.6 3.9 %weight_sent.1.refs_0_ = bf16[4,256,256]{2,1,0:T(8,128)(2,1)} custom-call(s32[14]{0:T(128)} %stack.59.refs_0_.refs_1_, bf16[128,256]{1,0:T(8,128)(2,1)} %get-tuple-element.40.refs_1_.refs_6_, bf16[128,256]{1,0:T(8,128)(2,1)} %collective-permute-done.10.refs_2_, bf16[128,256]{1,0:T(8,128)(2,1)} %collective-permute-done.11.refs_3_, ...), custom_call_target="tpu_custom_call" | custom-call | flops 4000000000 | bytes 12000000 | tf_op jit(solution)/shard_map/weight_sent/pallas_call | solution.py:56
  55.6 2.1 %collective-permute-start.14 = (bf16[4,256,256]{2,1,0:T(8,128)(2,1)}, bf16[4,256,256]{2,1,0:T(8,128)(2,1)}, u32[]{:S(2)}, u32[]{:S(2)}) collective-permute-start(bf16[4,256,256]{2,1,0:T(8,128)(2,1)} %weight_sent.1.refs_0_), channel_id=1, source_target_pairs={{0,2},{2,0},{4,6},{6,4},{8,10},{10,8},{12,14},{14,12},{1,3},{3,1},... | collective-permute-start | bytes 1572872 | tf_op jit(solution)/shard_map/ppermute | solution.py:687
  57.6 7.0 %key_terms.1 = (bf16[256,128]{1,0:T(8,128)(2,1)}, bf16[256,128]{1,0:T(8,128)(2,1)}, bf16[8,256,128]{2,1,0:T(8,128)(2,1)}) custom-call(bf16[4,256,256]{2,1,0:T(8,128)(2,1)} %weight_sent.1.refs_0_, s32[14]{0:T(128)} %stack.59.refs_0_.refs_1_, bf16[256,256]{1,0:T(8,128)(2,1)} %bitcast.30, bf16[256,128]{1,0:T(8,128)(2,1)} %collective-permute-done.1.refs_2_.refs_3_, ...), custom_call_target="tpu_custom_call" | custom-call | flops 7000000000 | bytes 21000000 | tf_op jit(solution)/shard_map/key_terms/pallas_call | solution.py:56
  64.6 1.7 %all-to-all-done.refs_1_ = bf16[8,256,128]{2,1,0:T(8,128)(2,1)} async-done(((bf16[8,256,128]{2,1,0:T(8,128)(2,1)}), bf16[8,256,128]{2,1,0:T(8,128)(2,1)}, u32[]{:S(2)}, u32[]{:S(2)}) %all-to-all-start) | async-done | bytes 524320 | tf_op jit(solution)/shard_map/all_to_all | solution.py:683
  66.3 4.1 %all-to-all-start.1 = ((bf16[8,256,128]{2,1,0:T(8,128)(2,1)}), bf16[8,256,128]{2,1,0:T(8,128)(2,1)}, u32[]{:S(2)}, u32[]{:S(2)}) async-start(bf16[8,256,128]{2,1,0:T(8,128)(2,1)} %get-tuple-element.50), calls=%async_computation.1 | async-start | bytes 1048576 | tf_op jit(solution)/shard_map/all_to_all | solution.py:683
  70.5 1.5 %collective-permute-done.14.refs_8_ = bf16[4,256,256]{2,1,0:T(8,128)(2,1)} collective-permute-done((bf16[4,256,256]{2,1,0:T(8,128)(2,1)}, bf16[4,256,256]{2,1,0:T(8,128)(2,1)}, u32[]{:S(2)}, u32[]{:S(2)}) %collective-permute-start.14) | collective-permute-done | bytes 524320 | tf_op jit(solution)/shard_map/ppermute | solution.py:687
  72.0 4.2 %weight_kept.1 = (bf16[256,256]{1,0:T(8,128)(2,1)}, bf16[256,256]{1,0:T(8,128)(2,1)}, bf16[256,256]{1,0:T(8,128)(2,1)}, bf16[256,256]{1,0:T(8,128)(2,1)}, bf16[256,128]{1,0:T(8,128)(2,1)}) custom-call(s32[14]{0:T(128)} %stack.59.refs_0_.refs_1_, bf16[128,256]{1,0:T(8,128)(2,1)} %get-tuple-element.40.refs_1_.refs_6_, ...), custom_call_target="tpu_custom_call" | custom-call | flops 4000000000 | bytes 12000000 | tf_op jit(solution)/shard_map/weight_kept/pallas_call | solution.py:56
  76.2 0.8 collective-permute-start.15
  77.0 1.5 %collective-permute-start.16 = (bf16[256,256]{1,0:T(8,128)(2,1)}, bf16[256,256]{1,0:T(8,128)(2,1)}, u32[]{:S(2)}, u32[]{:S(2)}) collective-permute-start(bf16[256,256]{1,0:T(8,128)(2,1)} %get-tuple-element.52), channel_id=1, source_target_pairs={{0,4},{2,6},{4,8},{6,10},{8,12},{10,14},{12,0},{14,2},{1,5},{3,7},... | collective-permute-start | bytes 393224 | tf_op jit(solution)/shard_map/ppermute | solution.py:696
  78.5 2.2 %collective-permute-start.17 = (bf16[256,256]{1,0:T(8,128)(2,1)}, bf16[256,256]{1,0:T(8,128)(2,1)}, u32[]{:S(2)}, u32[]{:S(2)}) collective-permute-start(bf16[256,256]{1,0:T(8,128)(2,1)} %get-tuple-element.53), channel_id=1, source_target_pairs={{0,8},{2,10},{4,12},{6,14},{8,0},{10,2},{12,4},{14,6},{1,9},{3,11}... | collective-permute-start | bytes 393224 | tf_op jit(solution)/shard_map/ppermute | solution.py:696
  80.7 1.3 %collective-permute-start.18 = (bf16[256,256]{1,0:T(8,128)(2,1)}, bf16[256,256]{1,0:T(8,128)(2,1)}, u32[]{:S(2)}, u32[]{:S(2)}) collective-permute-start(bf16[256,256]{1,0:T(8,128)(2,1)} %get-tuple-element.54), channel_id=1, source_target_pairs={{0,12},{2,14},{4,0},{6,2},{8,4},{10,6},{12,8},{14,10},{1,13},{3,15... | collective-permute-start | bytes 393224 | tf_op jit(solution)/shard_map/ppermute | solution.py:696
  82.0 1.9 %collect_values.1.refs_0_ = bf16[256,256]{1,0:T(8,128)(2,1)} custom-call(bf16[256,256]{1,0:T(8,128)(2,1)} %get-tuple-element.46.refs_0_, bf16[8,256,128]{2,1,0:T(8,128)(2,1)} %all-to-all-done.refs_1_), custom_call_target="tpu_custom_call" | custom-call | flops 2000000000 | bytes 6000000 | tf_op jit(solution)/shard_map/collect_values/pallas_call | solution.py:56
  83.9 0.0 collective-permute-done.15.refs_3_
  83.9 8.2 %all-to-all-done.1.refs_4_ = bf16[8,256,128]{2,1,0:T(8,128)(2,1)} async-done(((bf16[8,256,128]{2,1,0:T(8,128)(2,1)}), bf16[8,256,128]{2,1,0:T(8,128)(2,1)}, u32[]{:S(2)}, u32[]{:S(2)}) %all-to-all-start.1) | async-done | bytes 524320 | tf_op jit(solution)/shard_map/all_to_all | solution.py:683
  92.1 2.6 %collect_keys.1 = (bf16[256,256]{1,0:T(8,128)(2,1)}, bf16[256,256]{1,0:T(8,128)(2,1)}) custom-call(bf16[256,256]{1,0:T(8,128)(2,1)} %collect_values.1.refs_0_, s32[14]{0:T(128)} %stack.59.refs_0_.refs_1_, bf16[256,128]{1,0:T(8,128)(2,1)} %get-tuple-element.48.refs_2_, bf16[256,128]{1,0:T(8,128)(2,1)} %collective-permute-done.15.refs_3_, ...), custom_call_target="tpu_custom_call" | custom-call | flops 2000000000 | bytes 6000000 | tf_op jit(solution)/shard_map/collect_keys/pallas_call | solution.py:56
  94.7 0.0 collective-permute-done.16
  94.7 0.0 collective-permute-done.17
  94.8 0.0 collective-permute-done.18
  94.8 1.8 %add_convert_fusion = bf16[256,256]{1,0:T(8,128)(2,1)} fusion(bf16[256,256]{1,0:T(8,128)(2,1)} %collective-permute-done.18, bf16[256,256]{1,0:T(8,128)(2,1)} %collective-permute-done.17, bf16[256,256]{1,0:T(8,128)(2,1)} %collective-permute-done.16, bf16[256,256]{1,0:T(8,128)(2,1)} %get-tuple-element.46.refs_0_), kind=kLoop, calls=%fused_computation | loop fusion | flops 524288 | bytes 655360 | tf_op jit(solution)/shard_map/convert_element_type | solution.py:706
Async XLA Ops:
  0.6 26.5 %collective-permute-start.2 = (bf16[256,2048]{1,0:T(8,128)(2,1)}, bf16[256,2048]{1,0:T(8,128)(2,1)}, u32[]{:S(2)}, u32[]{:S(2)}) collective-permute-start(bf16[256,2048]{1,0:T(8,128)(2,1)} %bitcast.21), channel_id=1, source_target_pairs={{0,1},{1,0},{2,3},{3,2},{4,5},{5,4},{6,7},{7,6},{8,9},{9,8},{10,11... | collective-permute-start | bytes 3145736 | tf_op jit(solution)/shard_map/ppermute | solution.py:648
  6.6 7.5 %collective-permute-start = (bf16[256,256]{1,0:T(8,128)(2,1)}, bf16[256,256]{1,0:T(8,128)(2,1)}, u32[]{:S(2)}, u32[]{:S(2)}) collective-permute-start(bf16[256,256]{1,0:T(8,128)(2,1)} %get-tuple-element.32), channel_id=1, source_target_pairs={{0,2},{2,0},{4,6},{6,4},{8,10},{10,8},{12,14},{14,12},{1,3},{3,1},... | collective-permute-start | bytes 393224 | tf_op jit(solution)/shard_map/ppermute | solution.py:651
  8.1 10.2 %collective-permute-start.8 = (bf16[256,256]{1,0:T(8,128)(2,1)}, bf16[256,256]{1,0:T(8,128)(2,1)}, u32[]{:S(2)}, u32[]{:S(2)}) collective-permute-start(bf16[256,256]{1,0:T(8,128)(2,1)} %get-tuple-element.39.refs_7_.refs_10_), channel_id=1, source_target_pairs={{0,12},{2,14},{4,0},{6,2},{8,4},{10,6},{12,8},{14,10},{1,13},{3,15... | collective-permute-start | bytes 393224 | tf_op jit(solution)/shard_map/ppermute | solution.py:653
  11.7 12.3 %collective-permute-start.6 = (bf16[256,256]{1,0:T(8,128)(2,1)}, bf16[256,256]{1,0:T(8,128)(2,1)}, u32[]{:S(2)}, u32[]{:S(2)}) collective-permute-start(bf16[256,256]{1,0:T(8,128)(2,1)} %get-tuple-element.39.refs_7_.refs_10_), channel_id=1, source_target_pairs={{0,8},{2,10},{4,12},{6,14},{8,0},{10,2},{12,4},{14,6},{1,9},{3,11}... | collective-permute-start | bytes 393224 | tf_op jit(solution)/shard_map/ppermute | solution.py:653
  11.7 21.4 %collective-permute-start.4 = (bf16[256,256]{1,0:T(8,128)(2,1)}, bf16[256,256]{1,0:T(8,128)(2,1)}, u32[]{:S(2)}, u32[]{:S(2)}) collective-permute-start(bf16[256,256]{1,0:T(8,128)(2,1)} %get-tuple-element.39.refs_7_.refs_10_), channel_id=1, source_target_pairs={{0,4},{2,6},{4,8},{6,10},{8,12},{10,14},{12,0},{14,2},{1,5},{3,7},... | collective-permute-start | bytes 393224 | tf_op jit(solution)/shard_map/ppermute | solution.py:653
  17.7 17.0 %collective-permute-start.1 = (bf16[256,128]{1,0:T(8,128)(2,1)}, bf16[256,128]{1,0:T(8,128)(2,1)}, u32[]{:S(2)}, u32[]{:S(2)}) collective-permute-start(bf16[256,128]{1,0:T(8,128)(2,1)} %get-tuple-element.33), channel_id=1, source_target_pairs={{0,2},{2,0},{4,6},{6,4},{8,10},{10,8},{12,14},{14,12},{1,3},{3,1},... | collective-permute-start | bytes 196616 | tf_op jit(solution)/shard_map/ppermute | solution.py:661
  18.3 16.4 %collective-permute-start.9 = (bf16[256,256]{1,0:T(8,128)(2,1)}, bf16[256,256]{1,0:T(8,128)(2,1)}, u32[]{:S(2)}, u32[]{:S(2)}) collective-permute-start(bf16[256,256]{1,0:T(8,128)(2,1)} %collective-permute-done.refs_0_.refs_8_.refs_11_), channel_id=1, source_target_pairs={{0,12},{2,14},{4,0},{6,2},{8,4},{10,6},{12,8},{14,10},{1,13},{3,15... | collective-permute-start | bytes 393224 | tf_op jit(solution)/shard_map/ppermute | solution.py:653
  24.1 10.6 %collective-permute-start.7 = (bf16[256,256]{1,0:T(8,128)(2,1)}, bf16[256,256]{1,0:T(8,128)(2,1)}, u32[]{:S(2)}, u32[]{:S(2)}) collective-permute-start(bf16[256,256]{1,0:T(8,128)(2,1)} %collective-permute-done.refs_0_.refs_8_.refs_11_), channel_id=1, source_target_pairs={{0,8},{2,10},{4,12},{6,14},{8,0},{10,2},{12,4},{14,6},{1,9},{3,11}... | collective-permute-start | bytes 393224 | tf_op jit(solution)/shard_map/ppermute | solution.py:653
  27.1 7.6 %collective-permute-start.5 = (bf16[256,256]{1,0:T(8,128)(2,1)}, bf16[256,256]{1,0:T(8,128)(2,1)}, u32[]{:S(2)}, u32[]{:S(2)}) collective-permute-start(bf16[256,256]{1,0:T(8,128)(2,1)} %collective-permute-done.refs_0_.refs_8_.refs_11_), channel_id=1, source_target_pairs={{0,4},{2,6},{4,8},{6,10},{8,12},{10,14},{12,0},{14,2},{1,5},{3,7},... | collective-permute-start | bytes 393224 | tf_op jit(solution)/shard_map/ppermute | solution.py:653
  33.1 4.6 %collective-permute-start.3 = (bf16[128,256]{1,0:T(8,128)(2,1)}, bf16[128,256]{1,0:T(8,128)(2,1)}, u32[]{:S(2)}, u32[]{:S(2)}) collective-permute-start(bf16[128,256]{1,0:T(8,128)(2,1)} %get-tuple-element.38), channel_id=1, source_target_pairs={{0,2},{2,0},{4,6},{6,4},{8,10},{10,8},{12,14},{14,12},{1,3},{3,1},... | collective-permute-start | bytes 196616 | tf_op jit(solution)/shard_map/ppermute | solution.py:665
  34.7 16.9 %collective-permute-start.13 = (bf16[256,2048]{1,0:T(8,128)(2,1)}, bf16[256,2048]{1,0:T(8,128)(2,1)}, u32[]{:S(2)}, u32[]{:S(2)}) collective-permute-start(bf16[256,2048]{1,0:T(8,128)(2,1)} %get-tuple-element.42), channel_id=1, source_target_pairs={{0,16},{16,0},{1,17},{17,1},{2,18},{18,2},{3,19},{19,3},{4,20},{20... | collective-permute-start | bytes 3145736 | tf_op jit(solution)/shard_map/ppermute | solution.py:667
  44.9 6.7 %collective-permute-start.12 = (bf16[128,256]{1,0:T(8,128)(2,1)}, bf16[128,256]{1,0:T(8,128)(2,1)}, u32[]{:S(2)}, u32[]{:S(2)}) collective-permute-start(bf16[128,256]{1,0:T(8,128)(2,1)} %get-tuple-element.41.refs_7_), channel_id=1, source_target_pairs={{0,18},{2,16},{4,22},{6,20},{8,26},{10,24},{12,30},{14,28},{16,2},... | collective-permute-start | bytes 196616 | tf_op jit(solution)/shard_map/ppermute | solution.py:680
  44.9 6.7 %collective-permute-start.10 = (bf16[128,256]{1,0:T(8,128)(2,1)}, bf16[128,256]{1,0:T(8,128)(2,1)}, u32[]{:S(2)}, u32[]{:S(2)}) collective-permute-start(bf16[128,256]{1,0:T(8,128)(2,1)} %get-tuple-element.41.refs_7_), channel_id=1, source_target_pairs={{0,2},{2,0},{4,6},{6,4},{8,10},{10,8},{12,14},{14,12},{1,3},{3,1},... | collective-permute-start | bytes 196616 | tf_op jit(solution)/shard_map/ppermute | solution.py:680
  46.5 5.1 %collective-permute-start.11 = (bf16[128,256]{1,0:T(8,128)(2,1)}, bf16[128,256]{1,0:T(8,128)(2,1)}, u32[]{:S(2)}, u32[]{:S(2)}) collective-permute-start(bf16[128,256]{1,0:T(8,128)(2,1)} %get-tuple-element.40.refs_1_.refs_6_), channel_id=1, source_target_pairs={{0,16},{2,18},{4,20},{6,22},{8,24},{10,26},{12,28},{14,30},{16,0},... | collective-permute-start | bytes 196616 | tf_op jit(solution)/shard_map/ppermute | solution.py:680
  46.8 19.6 %all-to-all-start = ((bf16[8,256,128]{2,1,0:T(8,128)(2,1)}), bf16[8,256,128]{2,1,0:T(8,128)(2,1)}, u32[]{:S(2)}, u32[]{:S(2)}) async-start(bf16[8,256,128]{2,1,0:T(8,128)(2,1)} %get-tuple-element.47), calls=%async_computation | async-start | bytes 1048576 | tf_op jit(solution)/shard_map/all_to_all | solution.py:683
  55.6 16.5 %collective-permute-start.14 = (bf16[4,256,256]{2,1,0:T(8,128)(2,1)}, bf16[4,256,256]{2,1,0:T(8,128)(2,1)}, u32[]{:S(2)}, u32[]{:S(2)}) collective-permute-start(bf16[4,256,256]{2,1,0:T(8,128)(2,1)} %weight_sent.1.refs_0_), channel_id=1, source_target_pairs={{0,2},{2,0},{4,6},{6,4},{8,10},{10,8},{12,14},{14,12},{1,3},{3,1},... | collective-permute-start | bytes 1572872 | tf_op jit(solution)/shard_map/ppermute | solution.py:687
  66.3 25.7 %all-to-all-start.1 = ((bf16[8,256,128]{2,1,0:T(8,128)(2,1)}), bf16[8,256,128]{2,1,0:T(8,128)(2,1)}, u32[]{:S(2)}, u32[]{:S(2)}) async-start(bf16[8,256,128]{2,1,0:T(8,128)(2,1)} %get-tuple-element.50), calls=%async_computation.1 | async-start | bytes 1048576 | tf_op jit(solution)/shard_map/all_to_all | solution.py:683
  76.2 7.6 %collective-permute-start.15 = (bf16[256,128]{1,0:T(8,128)(2,1)}, bf16[256,128]{1,0:T(8,128)(2,1)}, u32[]{:S(2)}, u32[]{:S(2)}) collective-permute-start(bf16[256,128]{1,0:T(8,128)(2,1)} %get-tuple-element.49), channel_id=1, source_target_pairs={{0,2},{2,0},{4,6},{6,4},{8,10},{10,8},{12,14},{14,12},{1,3},{3,1},... | collective-permute-start | bytes 196616 | tf_op jit(solution)/shard_map/ppermute | solution.py:698
  77.0 17.7 %collective-permute-start.16 = (bf16[256,256]{1,0:T(8,128)(2,1)}, bf16[256,256]{1,0:T(8,128)(2,1)}, u32[]{:S(2)}, u32[]{:S(2)}) collective-permute-start(bf16[256,256]{1,0:T(8,128)(2,1)} %get-tuple-element.52), channel_id=1, source_target_pairs={{0,4},{2,6},{4,8},{6,10},{8,12},{10,14},{12,0},{14,2},{1,5},{3,7},... | collective-permute-start | bytes 393224 | tf_op jit(solution)/shard_map/ppermute | solution.py:696
  78.5 16.2 %collective-permute-start.17 = (bf16[256,256]{1,0:T(8,128)(2,1)}, bf16[256,256]{1,0:T(8,128)(2,1)}, u32[]{:S(2)}, u32[]{:S(2)}) collective-permute-start(bf16[256,256]{1,0:T(8,128)(2,1)} %get-tuple-element.53), channel_id=1, source_target_pairs={{0,8},{2,10},{4,12},{6,14},{8,0},{10,2},{12,4},{14,6},{1,9},{3,11}... | collective-permute-start | bytes 393224 | tf_op jit(solution)/shard_map/ppermute | solution.py:696
  80.7 14.0 %collective-permute-start.18 = (bf16[256,256]{1,0:T(8,128)(2,1)}, bf16[256,256]{1,0:T(8,128)(2,1)}, u32[]{:S(2)}, u32[]{:S(2)}) collective-permute-start(bf16[256,256]{1,0:T(8,128)(2,1)} %get-tuple-element.54), channel_id=1, source_target_pairs={{0,12},{2,14},{4,0},{6,2},{8,4},{10,6},{12,8},{14,10},{1,13},{3,15... | collective-permute-start | bytes 393224 | tf_op jit(solution)/shard_map/ppermute | solution.py:696

commit v10 on v9

v10 whole, which is shorter than its diff:
```python
import functools

import jax
import jax.numpy as jnp
from jax import lax
from jax.experimental import pallas as pl
from jax.experimental.pallas import tpu as pltpu
from jax.sharding import PartitionSpec as P

HD = 128
MASKED = -1e30
INNER = 2
SOURCES = 3
ANY = pl.BlockSpec(memory_space=pl.ANY)
VMEM = pl.BlockSpec(memory_space=pltpu.VMEM)
SMEM = pl.BlockSpec(memory_space=pltpu.SMEM)


def against(left_op, right_op):
    return lax.dot_general(
        left_op, right_op, (((1,), (1,)), ((), ())), preferred_element_type=jnp.float32
    )


def product(left_op, right_op):
    return jnp.dot(left_op, right_op, preferred_element_type=jnp.float32)


def begin(source, target, semaphore):
    copy = pltpu.make_async_copy(source, target, semaphore)
    copy.start()
    return copy


def call(kernel, out_shape, in_specs, out_specs, scratch, micros, name, after=()):
    skipped = len(after)
    in_specs = [ANY] * skipped + in_specs
    run = pl.pallas_call(
        lambda *refs: kernel(*refs[skipped:]),
        out_shape=out_shape,
        in_specs=in_specs,
        out_specs=out_specs,
        scratch_shapes=scratch,
        compiler_params=pltpu.CompilerParams(vmem_limit_bytes=64 * 1024 * 1024),
        cost_estimate=pl.CostEstimate(
            flops=int(micros * 1e9), bytes_accessed=int(micros * 3e6), transcendentals=0
        ),
        name=name,
    )

    def placed(*args):
        args = [
            pltpu.with_memory_space_constraint(arg, pltpu.HBM) if spec is ANY else arg
            for spec, arg in zip(in_specs, (*after, *args))
        ]
        return run(*args)

    return placed


def bf16(*shape):
    return pltpu.HBM(shape, jnp.bfloat16)


def f32(*shape):
    return pltpu.HBM(shape, jnp.float32)


def part_kernel(at_ref, k_ref, v_ref, kv_mine, kv_theirs, held_s, in_sem, out_sem):
    half = kv_mine.shape[1] // 2
    loads = [begin(held, held_s.at[i], in_sem.at[i]) for i, held in enumerate((k_ref, v_ref))]
    mine = pl.ds(pl.multiple_of(at_ref[0] * half, half), half)
    theirs = pl.ds(pl.multiple_of((1 - at_ref[0]) * half, half), half)
    copies = []
    for index in range(2):
        loads[index].wait()
        place = slice(index * half, (index + 1) * half)
        for side, (cols, out) in enumerate(((mine, kv_mine), (theirs, kv_theirs))):
            sem = out_sem.at[2 * index + side]
            copies.append(begin(held_s.at[index, :, cols], out.at[:, place], sem))
    for copy in copies:
        copy.wait()


def part_heads(at, keys, values):
    rows, feats = keys.shape
    return call(
        part_kernel,
        [bf16(rows, feats), bf16(rows, feats)],
        [SMEM] + [ANY] * 2,
        [ANY] * 2,
        [
            pltpu.VMEM((2, rows, feats), jnp.bfloat16),
            pltpu.SemaphoreType.DMA((2,)),
            pltpu.SemaphoreType.DMA((4,)),
        ],
        2,
        "part_heads",
    )(at, keys, values)


def prelude_kernel(at_ref, pattern, offsets, q_ref, grad_ref, weight_ref, *refs):
    first, key_mask, row_mask, q_theirs = refs[:4]
    grad_s, weight_s, first_s, mask_s, row_s, q_s, sem, out_sem = refs[4:]
    half = q_theirs.shape[1]
    theirs = pl.ds(pl.multiple_of((1 - at_ref[0]) * half, half), half)
    q_load = begin(q_ref.at[:, theirs], q_s, sem.at[2])
    rows, width = grad_s.shape
    block_count, glob_count = offsets.shape
    start = pl.multiple_of(at_ref[2] * width, width)
    loads = [
        begin(grad_ref, grad_s, sem.at[0]),
        begin(weight_ref.at[:, pl.ds(start, width)], weight_s, sem.at[1]),
    ]
    q_load.wait()
    stores = [begin(q_s, q_theirs, out_sem.at[3])]
    own = at_ref[1] * INNER + at_ref[0]
    partner = at_ref[1] * INNER + 1 - at_ref[0]
    lane = lax.broadcasted_iota(jnp.int32, (1, HD), 1)
    row_at = lax.broadcasted_iota(jnp.int32, (rows, HD), 0)
    col_at = lax.broadcasted_iota(jnp.int32, (8, rows), 1)
    group_at = lax.broadcasted_iota(jnp.int32, (8, rows), 0)
    for index in range(block_count):
        block = at_ref[SOURCES + index]
        hidden = []
        for target in (own, partner):
            seen = jnp.abs(block - target) <= 1
            for r in range(pattern.shape[1]):
                seen = seen | (pattern[target, r] == block)
            hidden.append(jnp.where(seen, 0, 1))
        lane_hidden = jnp.where(lane == 0, hidden[0], jnp.where(lane == 1, hidden[1], 0))
        hidden_rows = jnp.broadcast_to(lane_hidden, (rows, HD))
        for r in range(glob_count):
            hidden_rows = jnp.where(row_at == offsets[block, r], 0, hidden_rows)
        mask_s[index * rows : (index + 1) * rows, :] = hidden_rows.astype(jnp.float32).astype(
            jnp.bfloat16
        )
    for group, target in enumerate((own, partner)):
        local = jnp.where(group_at == group, MASKED, 0.0)
        for r in range(glob_count):
            local = jnp.where(col_at == offsets[target, r], 0.0, local)
        row_s[:, group * rows : (group + 1) * rows] = local
    stores.append(begin(mask_s, key_mask, out_sem.at[0]))
    stores.append(begin(row_s, row_mask, out_sem.at[1]))
    for load in loads:
        load.wait()
    first_s[...] = against(weight_s[...], grad_s[...])
    stores.append(begin(first_s, first, out_sem.at[2]))
    for store in stores:
        store.wait()


def prelude(at, pattern, offsets, queries, grad_own, out_weight, after):
    rows, width = grad_own.shape
    feats = out_weight.shape[0]
    keys = offsets.shape[0] * rows
    half = queries.shape[1] // INNER
    return call(
        prelude_kernel,
        [
            f32(feats, rows),
            bf16(keys, HD),
            f32(8, 2 * rows),
            bf16(rows, half),
        ],
        [SMEM] * 3 + [ANY] * 3,
        [ANY] * 4,
        [
            pltpu.VMEM((rows, width), jnp.bfloat16),
            pltpu.VMEM((feats, width), jnp.bfloat16),
            pltpu.VMEM((feats, rows), jnp.float32),
            pltpu.VMEM((keys, HD), jnp.bfloat16),
            pltpu.VMEM((8, 2 * rows), jnp.float32),
            pltpu.VMEM((rows, half), jnp.bfloat16),
            pltpu.SemaphoreType.DMA((3,)),
            pltpu.SemaphoreType.DMA((4,)),
        ],
        4,
        "prelude",
        after,
    )(at, pattern, offsets, queries, grad_own, out_weight)


def forward_kernel(block_count, head_count, at_ref, q_ref, q_recv, key_mask, row_mask, *refs):
    kv_refs, refs = refs[:block_count], refs[block_count:]
    e_out, inv_out, attn_out = refs[:3]
    q_s, mask_s, kv_s, e_s, s_ref, attn_s, inv_s, row_s, sem, kv_sem, e_sem, out_sem = refs[3:]
    rows = q_recv.shape[0]
    feats = head_count * HD
    score_scale = HD ** (-0.5)
    mine = pl.ds(pl.multiple_of(at_ref[0] * feats, feats), feats)
    loads = [
        begin(q_ref.at[:, mine], q_s.at[0], sem.at[0]),
        begin(q_recv, q_s.at[1], sem.at[1]),
        begin(key_mask, mask_s, sem.at[2]),
        begin(row_mask, row_s, sem.at[3]),
    ]
    kv_loads = [begin(kv_refs[j], kv_s.at[j], kv_sem.at[j]) for j in range(block_count)]
    for load in loads:
        load.wait()
    rows_low = row_s[...].astype(jnp.bfloat16)
    hidden = jnp.concatenate([rows_low, jnp.zeros((HD - 8, 2 * rows), jnp.bfloat16)], axis=0)
    stores = []
    for head in range(head_count):
        cols = slice(head * HD, (head + 1) * HD)
        vcols = slice(feats + head * HD, feats + (head + 1) * HD)
        q_t = jnp.concatenate(
            [jnp.transpose(q_s[0, :, cols]), jnp.transpose(q_s[1, :, cols])], axis=1
        )
        q_t = jnp.concatenate([q_t, hidden], axis=0)
        top = jnp.full((1, 2 * rows), MASKED, jnp.float32)
        for j in range(block_count):
            if head == 0:
                kv_loads[j].wait()
            keys = slice(j * rows, (j + 1) * rows)
            scores = product(jnp.concatenate([kv_s[j, :, cols], mask_s[keys, :]], axis=1), q_t)
            s_ref[keys, :] = scores
            top = jnp.maximum(top, jnp.max(scores, axis=0, keepdims=True))
        total = jnp.zeros((1, 2 * rows), jnp.float32)
        attn_t = jnp.zeros((HD, 2 * rows), jnp.float32)
        for j in range(block_count):
            keys = slice(j * rows, (j + 1) * rows)
            weights = jnp.exp((s_ref[keys, :] - top) * score_scale)
            total = total + jnp.sum(weights, axis=0, keepdims=True)
            low = weights.astype(jnp.bfloat16)
            e_s[head, keys, :] = low
            stores.append(
                begin(e_s.at[head, keys], e_out.at[head, keys], e_sem.at[head * block_count + j])
            )
            attn_t = attn_t + product(jnp.transpose(kv_s[j, :, vcols]), low)
        inverse = 1.0 / total
        inv_s[head : head + 1, :] = inverse
        attn_low = (attn_t * inverse).astype(jnp.bfloat16)
        attn_s[0, cols, :] = attn_low[:, :rows]
        attn_s[1, cols, :] = attn_low[:, rows:]
    stores.append(begin(attn_s, attn_out, out_sem.at[0]))
    stores.append(begin(inv_s, inv_out, out_sem.at[1]))
    for store in stores:
        store.wait()


def forward(at, queries, q_recv, key_mask, row_mask, kv_blocks, after=()):
    block_count = len(kv_blocks)
    rows, feats = q_recv.shape
    heads = feats // HD
    keys = block_count * rows
    return call(
        functools.partial(forward_kernel, block_count, heads),
        [
            bf16(heads, keys, 2 * rows),
            f32(max(heads, 8), 2 * rows),
            bf16(INNER, feats, rows),
        ],
        [SMEM] + [ANY] * (4 + block_count),
        [ANY] * 3,
        [
            pltpu.VMEM((2, rows, feats), jnp.bfloat16),
            pltpu.VMEM((keys, HD), jnp.bfloat16),
            pltpu.VMEM((block_count, rows, 2 * feats), jnp.bfloat16),
            pltpu.VMEM((heads, keys, 2 * rows), jnp.bfloat16),
            pltpu.VMEM((keys, 2 * rows), jnp.float32),
            pltpu.VMEM((2, feats, rows), jnp.bfloat16),
            pltpu.VMEM((max(heads, 8), 2 * rows), jnp.float32),
            pltpu.VMEM((8, 2 * rows), jnp.float32),
            pltpu.SemaphoreType.DMA((4,)),
            pltpu.SemaphoreType.DMA((block_count,)),
            pltpu.SemaphoreType.DMA((heads * block_count,)),
            pltpu.SemaphoreType.DMA((2,)),
        ],
        6,
        "forward",
        after,
    )(at, queries, q_recv, key_mask, row_mask, *kv_blocks)


def backward_kernel(block_count, head_count, at_ref, *refs):
    q_ref, q_recv, g_mine, g_recv, attn_ref, inv_ref, e_ref = refs[:7]
    kv_refs, refs = refs[7 : 7 + block_count], refs[7 + block_count :]
    dq_mine, dq_theirs, part_out, attn_out = refs[:4]
    q_s, t_s, attn_s, inv_s, kv_s, e_s, part_s, dq_s, sem, kv_sem, e_sem, part_sem, dq_sem = refs[4:]
    rows = q_recv.shape[0]
    feats = head_count * HD
    score_scale = HD ** (-0.5)
    mine = pl.ds(pl.multiple_of(at_ref[0] * feats, feats), feats)
    loads = [begin(q_ref.at[:, mine], q_s.at[0], sem.at[0]), begin(q_recv, q_s.at[1], sem.at[1])]
    for index, held in enumerate((g_mine, g_recv)):
        loads.append(begin(held, t_s.at[index], sem.at[2 + index]))
    loads.append(begin(attn_ref, attn_s, sem.at[4]))
    loads.append(begin(inv_ref, inv_s, sem.at[5]))
    kv_loads, e_loads, stores = [], {}, []
    for j in range(block_count):
        keys = slice(j * rows, (j + 1) * rows)
        kv_loads.append(begin(kv_refs[j], kv_s.at[j], kv_sem.at[j]))
        for head in range(head_count):
            e_loads[head, j] = begin(
                e_ref.at[head, keys], e_s.at[head, keys], e_sem.at[head * block_count + j]
            )
    for load in loads:
        load.wait()
    stores.append(begin(attn_s, attn_out, dq_sem.at[2]))
    for head in range(head_count):
        cols = slice(head * HD, (head + 1) * HD)
        vcols = slice(feats + head * HD, feats + (head + 1) * HD)
        inverse = inv_s[head : head + 1, :]
        g_t = jnp.concatenate([t_s[0, cols, :], t_s[1, cols, :]], axis=1).astype(jnp.float32)
        attn_t = jnp.concatenate([attn_s[0, cols, :], attn_s[1, cols, :]], axis=1)
        row_dot = jnp.sum(g_t * attn_t.astype(jnp.float32), axis=0, keepdims=True) * inverse
        g_t = (g_t * inverse).astype(jnp.bfloat16)
        grad = jnp.transpose(g_t)
        query = jnp.concatenate([q_s[0, :, cols], q_s[1, :, cols]], axis=0)
        dq_t = jnp.zeros((HD, 2 * rows), jnp.float32)
        for j in range(block_count):
            keys = slice(j * rows, (j + 1) * rows)
            if head == 0:
                kv_loads[j].wait()
            e_loads[head, j].wait()
            low = e_s[head, keys, :]
            dprobs = product(kv_s[j, :, vcols], g_t)
            dscore = (low.astype(jnp.float32) * (dprobs - row_dot)).astype(jnp.bfloat16)
            dq_t = dq_t + product(jnp.transpose(kv_s[j, :, cols]), dscore)
            part_s[j, :, cols] = (score_scale * product(dscore, query)).astype(jnp.bfloat16)
            part_s[j, :, vcols] = product(low, grad).astype(jnp.bfloat16)
            if head == head_count - 1:
                stores.append(begin(part_s.at[j], part_out.at[at_ref[SOURCES + j]], part_sem.at[j]))
        dquery = (score_scale * jnp.transpose(dq_t)).astype(jnp.bfloat16)
        dq_s[0, :, cols] = dquery[:rows]
        dq_s[1, :, cols] = dquery[rows:]
    stores.append(begin(dq_s.at[0], dq_mine, dq_sem.at[0]))
    stores.append(begin(dq_s.at[1], dq_theirs, dq_sem.at[1]))
    for store in stores:
        store.wait()


def backward(at, queries, q_recv, g_mine, g_recv, attn, inverse, weights, kv_blocks):
    block_count = len(kv_blocks)
    rows, feats = q_recv.shape
    heads = feats // HD
    keys = block_count * rows
    return call(
        functools.partial(backward_kernel, block_count, heads),
        [bf16(rows, feats)] * 2 + [bf16(block_count, rows, 2 * feats), bf16(*attn.shape)],
        [SMEM] + [ANY] * (7 + block_count),
        [ANY] * 4,
        [
            pltpu.VMEM((2, rows, feats), jnp.bfloat16),
            pltpu.VMEM((2, feats, rows), jnp.bfloat16),
            pltpu.VMEM(attn.shape, jnp.bfloat16),
            pltpu.VMEM(inverse.shape, jnp.float32),
            pltpu.VMEM((block_count, rows, 2 * feats), jnp.bfloat16),
            pltpu.VMEM((heads, keys, 2 * rows), jnp.bfloat16),
            pltpu.VMEM((block_count, rows, 2 * feats), jnp.bfloat16),
            pltpu.VMEM((2, rows, feats), jnp.bfloat16),
            pltpu.SemaphoreType.DMA((6,)),
            pltpu.SemaphoreType.DMA((block_count,)),
            pltpu.SemaphoreType.DMA((heads * block_count,)),
            pltpu.SemaphoreType.DMA((block_count,)),
            pltpu.SemaphoreType.DMA((3,)),
        ],
        8,
        "backward",
    )(at, queries, q_recv, g_mine, g_recv, attn, inverse, weights, *kv_blocks)


def chunk(at_ref, steps_at, parts, place, width, target, semaphore):
    pieces = parts[0].shape[1] // width
    which = at_ref[steps_at + place // pieces]
    cols = pl.ds(pl.multiple_of(lax.rem(place, pieces) * width, width), width)
    for k, part in enumerate(parts):

        @pl.when(which == k)
        def _():
            begin(part.at[:, cols], target, semaphore)

    return pltpu.make_async_copy(parts[0].at[:, cols], target, semaphore)


def grad_heads_kernel(part_count, routes, picked, columns_at, groups_at, at_ref, first_ref, weight_ref, *refs):
    grads, refs = refs[:part_count], refs[part_count:]
    outs, sends, refs = refs[:2], refs[2 : 2 + len(routes)], refs[2 + len(routes) :]
    first_s, grad_s, weight_s, out_s, first_sem, weight_sem, grad_sem, send_sem, out_sem = refs
    half = out_s.shape[1]
    width = grads[0].shape[1]
    first_load = begin(first_ref, first_s, first_sem)
    weight_loads, grad_loads = [], []
    for k in range(1, part_count):
        start = pl.multiple_of(at_ref[columns_at + k - 1] * width, width)
        columns = weight_ref.at[:, pl.ds(start, width)]
        weight_loads.append(begin(columns, weight_s.at[k - 1], weight_sem.at[k - 1]))
        grad_loads.append(begin(grads[k], grad_s.at[k], grad_sem.at[k]))
    own_load = begin(grads[0], grad_s.at[0], grad_sem.at[0])
    first_load.wait()
    summed = first_s[...]
    for k in range(1, part_count):
        weight_loads[k - 1].wait()
        grad_loads[k - 1].wait()
        summed = summed + against(weight_s[k - 1], grad_s[k])
    first_s[...] = summed
    copies = []
    for side, at in enumerate((at_ref[0], 1 - at_ref[0])):
        kept = first_s[pl.ds(pl.multiple_of(at * half, half), half), :]
        out_s[side] = kept.astype(jnp.bfloat16)
        copies.append(begin(out_s.at[side], outs[side], out_sem.at[side]))
    own_load.wait()
    parts = [grad_s.at[k] for k in range(part_count)]
    for index, (step, side) in enumerate(routes):
        outer, _, block = sends[index].shape
        here = (1 - at_ref[0]) if side else at_ref[0]
        for k in range(outer):
            place = lax.rem(at_ref[1] + k, outer) * INNER + here
            target, sem = sends[index].at[k], send_sem.at[index * outer + k]
            copies.append(chunk(at_ref, groups_at + step * picked, parts, place, block, target, sem))
    for copy in copies:
        copy.wait()


def grad_heads(at, columns_at, groups_at, first, out_weight, grads, routes, outer, picked):
    feats, rows = first.shape
    half = feats // INNER
    count = len(grads)
    width = grads[0].shape[1]
    block = picked * width // (outer * INNER)
    out = call(
        functools.partial(grad_heads_kernel, count, routes, picked, columns_at, groups_at),
        [bf16(half, rows), bf16(half, rows)] + [bf16(outer, rows, block)] * len(routes),
        [SMEM] + [ANY] * (2 + count),
        [ANY] * (2 + len(routes)),
        [
            pltpu.VMEM((feats, rows), jnp.float32),
            pltpu.VMEM((count, rows, width), jnp.bfloat16),
            pltpu.VMEM((count - 1, feats, width), jnp.bfloat16),
            pltpu.VMEM((INNER, half, rows), jnp.bfloat16),
            pltpu.SemaphoreType.DMA,
            pltpu.SemaphoreType.DMA((count - 1,)),
            pltpu.SemaphoreType.DMA((count,)),
            pltpu.SemaphoreType.DMA((len(routes) * outer,)),
            pltpu.SemaphoreType.DMA((INNER,)),
        ],
        4,
        "grad_heads",
    )(at, first, out_weight, *grads)
    return out[0], out[1], out[2:]


def weight_kernel(part_count, doc_count, groups_at, at_ref, *refs):
    route_count = INNER * doc_count
    attn, refs = refs[:route_count], refs[route_count:]
    grads, refs = refs[:part_count], refs[part_count:]
    swapped, refs = refs[: route_count - 1], refs[route_count - 1 :]
    attn_s, grad_s, out_s, attn_sem, grad_sem, out_sem = refs[-6:]
    outs = refs[:-6]
    outer, feats, width = out_s.shape
    half = feats // INNER
    attn_loads, grad_loads = [], []
    for doc in range(doc_count):
        for side in range(INNER):
            for group, at in enumerate((at_ref[0], 1 - at_ref[0])):
                source = attn[doc * INNER + group].at[side ^ group]
                target = attn_s.at[doc * INNER + side, pl.ds(pl.multiple_of(at * half, half), half)]
                sem = attn_sem.at[(doc * INNER + side) * INNER + group]
                attn_loads.append(begin(source, target, sem))
    for k in range(outer):
        place = lax.rem(at_ref[1] + k, outer) * INNER + at_ref[0]
        target, sem = grad_s.at[0, k], grad_sem.at[k]
        loads = [chunk(at_ref, groups_at, grads, place, width, target, sem)]
        for index, held in enumerate(swapped):
            sem = grad_sem.at[(index + 1) * outer + k]
            loads.append(begin(held.at[k], grad_s.at[index + 1, k], sem))
        grad_loads.append(loads)
    for load in attn_loads:
        load.wait()
    stores = []
    for k in range(outer):
        term = 0.0
        for index in range(route_count):
            grad_loads[k][index].wait()
            term = term + product(attn_s[index], grad_s[index, k])
        out_s[k] = term.astype(out_s.dtype)
        stores.append(begin(out_s.at[k], outs[k], out_sem.at[k]))
    for store in stores:
        store.wait()


def weight_terms(at, groups_at, attn, grads, swapped, after=()):
    _, half, rows = attn[0].shape
    outer, _, width = swapped[0].shape
    feats = half * INNER
    routes = len(attn)
    operands = [*attn, *grads, *swapped]
    return call(
        functools.partial(weight_kernel, len(grads), routes // INNER, groups_at),
        [bf16(feats, width)] * outer,
        [SMEM] + [ANY] * len(operands),
        [ANY] * outer,
        [
            pltpu.VMEM((routes, feats, rows), jnp.bfloat16),
            pltpu.VMEM((routes, outer, rows, width), jnp.bfloat16),
            pltpu.VMEM((outer, feats, width), jnp.bfloat16),
            pltpu.SemaphoreType.DMA((routes * INNER,)),
            pltpu.SemaphoreType.DMA((routes * outer,)),
            pltpu.SemaphoreType.DMA((outer,)),
        ],
        5,
        "weight_terms",
        after,
    )(at, *operands)


def collect_kernel(at_ref, dq_mine, dq_recv, terms, *refs):
    outs, (dq_s, terms_s, out_s, dq_sem, sem, out_sem) = refs[:3], refs[3:]
    count, rows, both = terms.shape
    half = both // 2
    loads = [begin(terms.at[c], terms_s.at[c], sem.at[c]) for c in range(count)]
    held = [begin(dq, dq_s.at[i], dq_sem.at[i]) for i, dq in enumerate((dq_mine, dq_recv))]
    for side, at in enumerate((at_ref[0], 1 - at_ref[0])):
        held[side].wait()
        out_s[0, :, pl.ds(pl.multiple_of(at * half, half), half)] = dq_s[side]
    stores = [begin(out_s.at[0], outs[0], out_sem.at[0])]
    for load in loads:
        load.wait()
    for side in range(INNER):
        summed = terms_s[side].astype(jnp.float32)
        for c in range(side + INNER, count, INNER):
            summed = summed + terms_s[c].astype(jnp.float32)
        summed = summed.astype(jnp.bfloat16)
        for kind in range(2):
            cols = slice(side * half, (side + 1) * half)
            out_s[1 + kind, :, cols] = summed[:, kind * half : (kind + 1) * half]
    for index in (1, 2):
        stores.append(begin(out_s.at[index], outs[index], out_sem.at[index]))
    for store in stores:
        store.wait()


def collect(at, dq_mine, dq_recv, terms):
    count, rows, both = terms.shape
    half = both // 2
    return call(
        collect_kernel,
        [bf16(rows, INNER * half)] * 3,
        [SMEM] + [ANY] * 3,
        [ANY] * 3,
        [
            pltpu.VMEM((INNER, rows, half), jnp.bfloat16),
            pltpu.VMEM((count, rows, both), jnp.bfloat16),
            pltpu.VMEM((3, rows, INNER * half), jnp.bfloat16),
            pltpu.SemaphoreType.DMA((INNER,)),
            pltpu.SemaphoreType.DMA((count,)),
            pltpu.SemaphoreType.DMA((3,)),
        ],
        3,
        "collect",
    )(at, dq_mine, dq_recv, terms)


def per_device(
    queries, key_heads, value_heads, grad_output, out_weight, block_pattern, global_offsets
):
    dp_count, ctx_count, tp_count = (lax.axis_size(name) for name in ("dp", "ctx", "tp"))
    dp_at, ctx_at, tp_at = (lax.axis_index(name) for name in ("dp", "ctx", "tp"))
    outer = ctx_count // INNER
    outer_at, inner_at = ctx_at // INNER, ctx_at % INNER
    picked = tp_count // dp_count

    def ctx_pairs(step, side, dp_step=0):
        moved = [(c + step * INNER) % ctx_count ^ side for c in range(ctx_count)]
        if not dp_step:
            return list(enumerate(moved))
        return [
            (d * ctx_count + c, (d + dp_step) % dp_count * ctx_count + moved[c])
            for d in range(dp_count)
            for c in range(ctx_count)
        ]

    def shift_pairs(count, step):
        return [(i, (i + step) % count) for i in range(count)]

    def dp_steps(which):
        return [(which * picked + i - tp_at) % tp_count for i in range(picked)]

    routes = [(step, side) for step in range(outer) for side in range(INNER)]
    sources = [
        ((outer_at - step) % outer) * INNER + (inner_at + side) % INNER for step, side in routes
    ]
    scalars = [inner_at, outer_at, tp_at] + sources
    columns_at = len(scalars)
    scalars = scalars + [(tp_at + step) % tp_count for step in range(1, tp_count)]
    groups_at = len(scalars)
    for step in range(dp_count):
        scalars = scalars + dp_steps((dp_at + step) % dp_count)
    at = jnp.stack(scalars)

    grad_own = grad_output[0]
    grads = [grad_own] + [
        lax.ppermute(grad_own, "tp", shift_pairs(tp_count, -step)) for step in range(1, tp_count)
    ]
    kv_mine, kv_theirs = part_heads(at, key_heads[0], value_heads[0])
    kv_recv = lax.ppermute(kv_theirs, "ctx", ctx_pairs(0, 1))
    kv_blocks = [
        lax.ppermute(kv_recv if side else kv_mine, "ctx", ctx_pairs(step, 0))
        if step
        else (kv_recv if side else kv_mine)
        for step, side in routes
    ]
    first, key_mask, row_mask, q_theirs = prelude(
        at, block_pattern, global_offsets, queries[0], grad_own, out_weight, (kv_recv,)
    )
    q_recv = lax.ppermute(q_theirs, "ctx", ctx_pairs(0, 1))
    partners = [(step, side) for step in range(dp_count) for side in range(INNER)][1:]

    def to_partners(arrays):
        return [
            lax.ppermute(held, ("dp", "ctx") if step else "ctx", ctx_pairs(0, side, step))
            for (step, side), held in zip(partners, arrays)
        ]

    g_mine, g_theirs, grad_sends = grad_heads(
        at, columns_at, groups_at, first, out_weight, grads, partners, outer, picked
    )
    g_recv = lax.ppermute(g_theirs, "ctx", ctx_pairs(0, 1))
    swapped = to_partners(grad_sends)

    weights, inverse, attn = forward(at, queries[0], q_recv, key_mask, row_mask, kv_blocks)
    dq_mine, dq_theirs, parts, attn = backward(
        at, queries[0], q_recv, g_mine, g_recv, attn, inverse, weights, kv_blocks
    )
    terms = lax.all_to_all(parts, "ctx", split_axis=0, concat_axis=0, tiled=True)
    dq_recv = lax.ppermute(dq_theirs, "ctx", ctx_pairs(0, 1))

    attn_all = [attn] + to_partners([attn] * len(partners))
    weight_sums = weight_terms(at, groups_at, attn_all, grads, swapped)
    weight_parts = [
        lax.ppermute(weight_sums[step], "ctx", ctx_pairs(step, 0)) for step in range(1, outer)
    ]
    grad_q, grad_k, grad_v = collect(at, dq_mine, dq_recv, terms)
    grad_weight = weight_sums[0].astype(jnp.float32)
    for part in weight_parts:
        grad_weight = grad_weight + part.astype(jnp.float32)

    return grad_q[None], grad_k[None], grad_v[None], grad_weight.astype(jnp.bfloat16)


def solution(mesh):
    in_specs = (
        P("dp", "ctx", "tp"),
        P("dp", "ctx", "tp"),
        P("dp", "ctx", "tp"),
        P("dp", "ctx", "tp"),
        P("tp", None),
        P(),
        P(),
    )
    out_specs = (
        P("dp", "ctx", "tp"),
        P("dp", "ctx", "tp"),
        P("dp", "ctx", "tp"),
        P("tp", ("dp", "ctx")),
    )
    return jax.shard_map(
        per_device, mesh=mesh, in_specs=in_specs, out_specs=out_specs, check_vma=False
    )
```

time: 97.3 us -> 121 us (1.24)
  waiting for transfers between devices: 20.5 us -> 48.3 us
  Pallas kernels: 36.8 us -> 32.5 us
  local copies, waits for them, and re-layouts: 1.93 us -> 3.54 us
    ppermute x5 -> x6, waiting for transfers between devices: 1.53 us -> 36 us  [to_partners(): lax.ppermute(held, ('dp', 'ctx') if step else 'ctx', ctx_pairs(0, side, s...]
    all_to_all x2 -> x1, waiting for transfers between devices: 9.91 us -> 0.01 us  [per_device(): lax.all_to_all(parts, 'ctx', split_axis=0, concat_axis=0, tiled=True)]
    ppermute x3, waiting for transfers between devices: 0.01 us -> 6.23 us  [per_device(): lax.ppermute(weight_sums[step], 'ctx', ctx_pairs(step, 0))]
    all_to_all x2 -> x1, starting transfers between devices: 8.93 us -> 4.38 us  [per_device(): lax.all_to_all(parts, 'ctx', split_axis=0, concat_axis=0, tiled=True)]
    pallas_call x9 -> x7, Pallas kernels: 36.8 us -> 32.5 us  [placed(): return run(*args)]
    ppermute x1, waiting for transfers between devices: 3.06 us -> 0.01 us  [per_device(): g_recv = lax.ppermute(g_theirs, 'ctx', ctx_pairs(0, 1))]
    ppermute x3, starting transfers between devices: 4.97 us -> 6.97 us  [per_device(): lax.ppermute(weight_sums[step], 'ctx', ctx_pairs(step, 0))]
    ppermute x5 -> x6, starting transfers between devices: 4 us -> 5.66 us  [to_partners(): lax.ppermute(held, ('dp', 'ctx') if step else 'ctx', ctx_pairs(0, side, s...]
  transfers between devices with their start and end apart: 21 -> 21, of which waited for: 6 -> 6; matrix products, arithmetic and copies ran while one was open for 2% -> 3% of each run, Pallas kernels for 38% -> 18%
where the time goes in v10:
time: 121 us; the launch traced here: 120 us
  waiting for transfers between devices  48.3 us (40%)
  starting transfers between devices  33.6 us (28%)
  Pallas kernels  32.5 us (27%)
  local copies, waits for them, and re-layouts  3.54 us (3%)
  other arithmetic  1.63 us (1%)
    ppermute x6, waiting for transfers between devices, to_partners(): lax.ppermute(held, ('dp', 'ctx') if step else 'ctx', ctx_pairs(0, side, s...  36 us
    pallas_call x7, Pallas kernels, placed(): return run(*args)  32.5 us
    ppermute x6, starting transfers between devices, per_device(): lax.ppermute(kv_recv if side else kv_mine, 'ctx', ctx_pairs(step, 0))  9.22 us
    ppermute x3, starting transfers between devices, per_device(): lax.ppermute(weight_sums[step], 'ctx', ctx_pairs(step, 0))  6.97 us
    ppermute x3, waiting for transfers between devices, per_device(): lax.ppermute(weight_sums[step], 'ctx', ctx_pairs(step, 0))  6.23 us
    ppermute x6, starting transfers between devices, to_partners(): lax.ppermute(held, ('dp', 'ctx') if step else 'ctx', ctx_pairs(0, side, s...  5.66 us
    all_to_all x1, starting transfers between devices, per_device(): lax.all_to_all(parts, 'ctx', split_axis=0, concat_axis=0, tiled=True)  4.38 us
    ppermute x1, waiting for transfers between devices, per_device(): lax.ppermute(grad_own, 'tp', shift_pairs(tp_count, -step))  3.07 us
  transfers between devices with their start and end apart: 21, of which 6 were waited for; matrix products, arithmetic and copies ran while one was open for 3% of the time, Pallas kernels for 18%

profile of v10, /device:TPU:0, one launch (start us, length us, event | category | flops | bytes accessed | tf_op | source)
XLA Modules:
  0.0 120.4 jit_solution(7565958232060656087)
XLA Ops:
  0.6 3.0 %collective-permute-start.2 = (bf16[256,2048]{1,0:T(8,128)(2,1)}, bf16[256,2048]{1,0:T(8,128)(2,1)}, u32[]{:S(2)}, u32[]{:S(2)}) collective-permute-start(bf16[256,2048]{1,0:T(8,128)(2,1)} %bitcast.21), channel_id=1, source_target_pairs={{0,1},{1,0},{2,3},{3,2},{4,5},{5,4},{6,7},{7,6},{8,9},{9,8},{10,11... | collective-permute-start | bytes 3145736 | tf_op jit(solution)/shard_map/ppermute | solution.py:594
  3.7 0.6 stack.59.refs_0_.refs_1_
  4.2 2.3 %part_heads.1 = (bf16[256,256]{1,0:T(8,128)(2,1)}, bf16[256,256]{1,0:T(8,128)(2,1)}) custom-call(s32[14]{0:T(128)} %stack.59.refs_0_.refs_1_, bf16[256,256]{1,0:T(8,128)(2,1)} %bitcast.25, bf16[256,256]{1,0:T(8,128)(2,1)} %bitcast.26), custom_call_target="tpu_custom_call" | custom-call | flops 2000000000 | bytes 6000000 | tf_op jit(solution)/shard_map/part_heads/pallas_call | solution.py:56
  6.6 1.6 %collective-permute-start = (bf16[256,256]{1,0:T(8,128)(2,1)}, bf16[256,256]{1,0:T(8,128)(2,1)}, u32[]{:S(2)}, u32[]{:S(2)}) collective-permute-start(bf16[256,256]{1,0:T(8,128)(2,1)} %get-tuple-element.29), channel_id=1, source_target_pairs={{0,2},{2,0},{4,6},{6,4},{8,10},{10,8},{12,14},{14,12},{1,3},{3,1},... | collective-permute-start | bytes 393224 | tf_op jit(solution)/shard_map/ppermute | solution.py:597
  8.1 3.6 %collective-permute-start.8 = (bf16[256,256]{1,0:T(8,128)(2,1)}, bf16[256,256]{1,0:T(8,128)(2,1)}, u32[]{:S(2)}, u32[]{:S(2)}) collective-permute-start(bf16[256,256]{1,0:T(8,128)(2,1)} %get-tuple-element.36.refs_5_.refs_8_), channel_id=1, source_target_pairs={{0,12},{2,14},{4,0},{6,2},{8,4},{10,6},{12,8},{14,10},{1,13},{3,15... | collective-permute-start | bytes 393224 | tf_op jit(solution)/shard_map/ppermute | solution.py:599
  11.7 0.0 collective-permute-start.6
  11.7 1.0 collective-permute-start.4
  12.8 1.3 %copy.11.refs_2_ = s32[8,3]{1,0:T(8,128)} copy(s32[8,3]{0,1:T(4,128)} %param.12) | data formatting | bytes 192 | tf_op args[5]
  14.1 0.0 collective-permute-done.refs_0_.refs_6_.refs_9_
  14.1 3.6 %prelude.1 = (f32[256,256]{1,0:T(8,128)}, bf16[2048,128]{1,0:T(8,128)(2,1)}, f32[8,512]{1,0:T(8,128)}, bf16[256,128]{1,0:T(8,128)(2,1)}) custom-call(bf16[256,256]{1,0:T(8,128)(2,1)} %collective-permute-done.refs_0_.refs_6_.refs_9_, s32[14]{0:T(128)} %stack.59.refs_0_.refs_1_, s32[8,3]{1,0:T(8,128)} %copy.11.refs_2_, s32[8,8]{1,0:T(8,128)} %refs_3_.1, ...), custom_call_target="tpu_custom_call" | custom-call | flops 4000000000 | bytes 12000000 | tf_op jit(solution)/shard_map/prelude/pallas_call | solution.py:56
  17.7 0.6 collective-permute-start.1
  18.3 0.0 collective-permute-done.8.refs_11_.refs_14_
  18.3 2.8 %collective-permute-start.9 = (bf16[256,256]{1,0:T(8,128)(2,1)}, bf16[256,256]{1,0:T(8,128)(2,1)}, u32[]{:S(2)}, u32[]{:S(2)}) collective-permute-start(bf16[256,256]{1,0:T(8,128)(2,1)} %collective-permute-done.refs_0_.refs_6_.refs_9_), channel_id=1, source_target_pairs={{0,12},{2,14},{4,0},{6,2},{8,4},{10,6},{12,8},{14,10},{1,13},{3,15... | collective-permute-start | bytes 393224 | tf_op jit(solution)/shard_map/ppermute | solution.py:599
  21.1 2.9 %collective-permute-done.6.refs_9_.refs_12_ = bf16[256,256]{1,0:T(8,128)(2,1)} collective-permute-done((bf16[256,256]{1,0:T(8,128)(2,1)}, bf16[256,256]{1,0:T(8,128)(2,1)}, u32[]{:S(2)}, u32[]{:S(2)}) %collective-permute-start.6) | collective-permute-done | bytes 131104 | tf_op jit(solution)/shard_map/ppermute | solution.py:599
  24.1 0.0 collective-permute-start.7
  24.1 3.1 %collective-permute-done.2.refs_4_.refs_6_ = bf16[256,2048]{1,0:T(8,128)(2,1)} collective-permute-done((bf16[256,2048]{1,0:T(8,128)(2,1)}, bf16[256,2048]{1,0:T(8,128)(2,1)}, u32[]{:S(2)}, u32[]{:S(2)}) %collective-permute-start.2) | collective-permute-done | bytes 1048608 | tf_op jit(solution)/shard_map/ppermute | solution.py:594
  27.1 1.8 %collective-permute-start.5 = (bf16[256,256]{1,0:T(8,128)(2,1)}, bf16[256,256]{1,0:T(8,128)(2,1)}, u32[]{:S(2)}, u32[]{:S(2)}) collective-permute-start(bf16[256,256]{1,0:T(8,128)(2,1)} %collective-permute-done.refs_0_.refs_6_.refs_9_), channel_id=1, source_target_pairs={{0,4},{2,6},{4,8},{6,10},{8,12},{10,14},{12,0},{14,2},{1,5},{3,7},... | collective-permute-start | bytes 393224 | tf_op jit(solution)/shard_map/ppermute | solution.py:599
  28.9 4.4 %grad_heads.1 = (bf16[128,256]{1,0:T(8,128)(2,1)}, bf16[128,256]{1,0:T(8,128)(2,1)}, bf16[4,256,256]{2,1,0:T(8,128)(2,1)}, bf16[4,256,256]{2,1,0:T(8,128)(2,1)}, bf16[4,256,256]{2,1,0:T(8,128)(2,1)}) custom-call(s32[14]{0:T(128)} %stack.59.refs_0_.refs_1_, f32[256,256]{1,0:T(8,128)} %get-tuple-element.31.refs_1_, bf16[256,4096]{1,0:T(8,128)(2,1)} %refs_2_.2, ...), custom_call_target="tpu_custom_call" | custom-call | flops 4000000000 | bytes 12000000 | tf_op jit(solution)/shard_map/grad_heads/pallas_call | solution.py:56
  33.3 0.0 collective-permute-done.4.refs_7_.refs_10_
  33.3 1.6 %collective-permute-start.3 = (bf16[128,256]{1,0:T(8,128)(2,1)}, bf16[128,256]{1,0:T(8,128)(2,1)}, u32[]{:S(2)}, u32[]{:S(2)}) collective-permute-start(bf16[128,256]{1,0:T(8,128)(2,1)} %get-tuple-element.33), channel_id=1, source_target_pairs={{0,2},{2,0},{4,6},{6,4},{8,10},{10,8},{12,14},{14,12},{1,3},{3,1},... | collective-permute-start | bytes 196616 | tf_op jit(solution)/shard_map/ppermute | solution.py:619
  34.9 0.0 collective-permute-done.1.refs_2_
  34.9 0.0 collective-permute-done.9.refs_12_.refs_15_
  34.9 0.0 collective-permute-done.7.refs_10_.refs_13_
  34.9 0.0 collective-permute-done.5.refs_8_.refs_11_
  34.9 6.2 %forward.1 = (bf16[1,2048,512]{2,1,0:T(8,128)(2,1)}, f32[8,512]{1,0:T(8,128)}, bf16[2,128,256]{2,1,0:T(8,128)(2,1)}) custom-call(s32[14]{0:T(128)} %stack.59.refs_0_.refs_1_, bf16[256,256]{1,0:T(8,128)(2,1)} %bitcast.28, bf16[256,128]{1,0:T(8,128)(2,1)} %collective-permute-done.1.refs_2_, bf16[2048,128]{1,0:T(8,128)(2,1)} %get-tuple-element.34.refs_3_, ...), custom_call_target="tpu_custom_call" | custom-call | flops 6000000000 | bytes 18000000 | tf_op jit(solution)/shard_map/forward/pallas_call | solution.py:56
  41.1 0.0 collective-permute-done.3.refs_4_
  41.1 7.9 %backward.1 = (bf16[256,128]{1,0:T(8,128)(2,1)}, bf16[256,128]{1,0:T(8,128)(2,1)}, bf16[8,256,256]{2,1,0:T(8,128)(2,1)}, bf16[2,128,256]{2,1,0:T(8,128)(2,1)}) custom-call(s32[14]{0:T(128)} %stack.59.refs_0_.refs_1_, bf16[256,256]{1,0:T(8,128)(2,1)} %bitcast.29, bf16[256,128]{1,0:T(8,128)(2,1)} %collective-permute-done.1.refs_2_, ...), custom_call_target="tpu_custom_call" | custom-call | flops 8000000000 | bytes 24000000 | tf_op jit(solution)/shard_map/backward/pallas_call | solution.py:56
  49.0 0.0 copy-start.2
  49.0 0.0 copy-start.1
  49.0 0.0 copy-start
  49.0 0.0 copy-start.5
  49.0 4.4 %all-to-all-start = ((bf16[8,256,256]{2,1,0:T(8,128)(2,1)}), bf16[8,256,256]{2,1,0:T(8,128)(2,1)}, u32[]{:S(2)}, u32[]{:S(2)}) async-start(bf16[8,256,256]{2,1,0:T(8,128)(2,1)} %get-tuple-element.42), calls=%async_computation | async-start | bytes 2097152 | tf_op jit(solution)/shard_map/all_to_all | solution.py:626
  53.4 0.0 copy-done.2
  53.4 1.9 %collective-permute-start.14 = (bf16[4,256,256]{2,1,0:T(8,128)(2,1)S(1)}, bf16[4,256,256]{2,1,0:T(8,128)(2,1)S(1)}, u32[]{:S(2)}, u32[]{:S(2)}) collective-permute-start(bf16[4,256,256]{2,1,0:T(8,128)(2,1)S(1)} %copy-done.2), channel_id=1, source_target_pairs={{0,2},{2,0},{4,6},{6,4},{8,10},{10,8},{12,14},{14,12},{1,3},{3,1},... | collective-permute-start | bytes 1572872 | tf_op jit(solution)/shard_map/ppermute | solution.py:612
  55.3 0.0 copy-done.1
  55.3 0.0 collective-permute-start.15
  55.3 0.0 copy-done
  55.3 0.3 collective-permute-start.16
  55.6 0.0 copy-done.5
  55.6 1.5 %collective-permute-start.13 = (bf16[2,128,256]{2,1,0:T(8,128)(2,1)S(1)}, bf16[2,128,256]{2,1,0:T(8,128)(2,1)S(1)}, u32[]{:S(2)}, u32[]{:S(2)}) collective-permute-start(bf16[2,128,256]{2,1,0:T(8,128)(2,1)S(1)} %copy-done.5), channel_id=1, source_target_pairs={{0,18},{2,16},{4,22},{6,20},{8,26},{10,24},{12,30},{14,28},{16,2},... | collective-permute-start | bytes 393224 | tf_op jit(solution)/shard_map/ppermute | solution.py:612
  57.1 0.4 collective-permute-start.12
  57.6 32.0 %collective-permute-done.13.refs_4_ = bf16[2,128,256]{2,1,0:T(8,128)(2,1)S(1)} collective-permute-done((bf16[2,128,256]{2,1,0:T(8,128)(2,1)S(1)}, bf16[2,128,256]{2,1,0:T(8,128)(2,1)S(1)}, u32[]{:S(2)}, u32[]{:S(2)}) %collective-permute-start.13) | collective-permute-done | bytes 131104 | tf_op jit(solution)/shard_map/ppermute | solution.py:612
  89.6 1.5 %collective-permute-start.11 = (bf16[2,128,256]{2,1,0:T(8,128)(2,1)S(1)}, bf16[2,128,256]{2,1,0:T(8,128)(2,1)S(1)}, u32[]{:S(2)}, u32[]{:S(2)}) collective-permute-start(bf16[2,128,256]{2,1,0:T(8,128)(2,1)S(1)} %copy-done.5), channel_id=1, source_target_pairs={{0,2},{2,0},{4,6},{6,4},{8,10},{10,8},{12,14},{14,12},{1,3},{3,1},... | collective-permute-start | bytes 393224 | tf_op jit(solution)/shard_map/ppermute | solution.py:612
  91.1 0.0 collective-permute-done.12.refs_3_
  91.1 4.0 %collective-permute-done.11.refs_2_ = bf16[2,128,256]{2,1,0:T(8,128)(2,1)S(1)} collective-permute-done((bf16[2,128,256]{2,1,0:T(8,128)(2,1)S(1)}, bf16[2,128,256]{2,1,0:T(8,128)(2,1)S(1)}, u32[]{:S(2)}, u32[]{:S(2)}) %collective-permute-start.11) | collective-permute-done | bytes 131104 | tf_op jit(solution)/shard_map/ppermute | solution.py:612
  95.1 0.0 collective-permute-done.14.refs_7_
  95.1 0.0 collective-permute-done.15.refs_8_
  95.1 0.0 copy-done.6
  95.2 0.6 copy-done.8
  95.8 0.2 copy-done.3
  96.0 0.8 copy-done.4
  96.8 0.0 collective-permute-done.16.refs_9_
  96.8 5.3 %weight_terms.1 = (bf16[256,256]{1,0:T(8,128)(2,1)}, bf16[256,256]{1,0:T(8,128)(2,1)}, bf16[256,256]{1,0:T(8,128)(2,1)}, bf16[256,256]{1,0:T(8,128)(2,1)}) custom-call(s32[14]{0:T(128)} %stack.59.refs_0_.refs_1_, bf16[2,128,256]{2,1,0:T(8,128)(2,1)} %get-tuple-element.46.refs_1_, bf16[2,128,256]{2,1,0:T(8,128)(2,1)} %copy-done.8, ...), custom_call_target="tpu_custom_call" | custom-call | flops 5000000000 | bytes 15000000 | tf_op jit(solution)/shard_map/weight_terms/pallas_call | solution.py:56
  102.0 1.6 %collective-permute-start.17 = (bf16[256,256]{1,0:T(8,128)(2,1)}, bf16[256,256]{1,0:T(8,128)(2,1)S(1)}, u32[]{:S(2)}, u32[]{:S(2)}) collective-permute-start(bf16[256,256]{1,0:T(8,128)(2,1)} %get-tuple-element.51), channel_id=1, source_target_pairs={{0,4},{2,6},{4,8},{6,10},{8,12},{10,14},{12,0},{14,2},{1,5},{3,7},... | collective-permute-start | bytes 393224 | tf_op jit(solution)/shard_map/ppermute | solution.py:632
  103.7 2.5 %collective-permute-start.18 = (bf16[256,256]{1,0:T(8,128)(2,1)}, bf16[256,256]{1,0:T(8,128)(2,1)S(1)}, u32[]{:S(2)}, u32[]{:S(2)}) collective-permute-start(bf16[256,256]{1,0:T(8,128)(2,1)} %get-tuple-element.52), channel_id=1, source_target_pairs={{0,8},{2,10},{4,12},{6,14},{8,0},{10,2},{12,4},{14,6},{1,9},{3,11}... | collective-permute-start | bytes 393224 | tf_op jit(solution)/shard_map/ppermute | solution.py:632
  106.2 2.8 %collective-permute-start.19 = (bf16[256,256]{1,0:T(8,128)(2,1)}, bf16[256,256]{1,0:T(8,128)(2,1)S(1)}, u32[]{:S(2)}, u32[]{:S(2)}) collective-permute-start(bf16[256,256]{1,0:T(8,128)(2,1)} %get-tuple-element.53), channel_id=1, source_target_pairs={{0,12},{2,14},{4,0},{6,2},{8,4},{10,6},{12,8},{14,10},{1,13},{3,15... | collective-permute-start | bytes 393224 | tf_op jit(solution)/shard_map/ppermute | solution.py:632
  109.0 0.6 collective-permute-start.10
  109.6 1.0 collective-permute-done.17
  110.6 5.2 %collective-permute-done.18 = bf16[256,256]{1,0:T(8,128)(2,1)S(1)} collective-permute-done((bf16[256,256]{1,0:T(8,128)(2,1)}, bf16[256,256]{1,0:T(8,128)(2,1)S(1)}, u32[]{:S(2)}, u32[]{:S(2)}) %collective-permute-start.18) | collective-permute-done | bytes 131104 | tf_op jit(solution)/shard_map/ppermute | solution.py:632
  115.8 0.0 collective-permute-done.19
  115.8 1.6 %add_convert_fusion = bf16[256,256]{1,0:T(8,128)(2,1)} fusion(bf16[256,256]{1,0:T(8,128)(2,1)S(1)} %collective-permute-done.19, bf16[256,256]{1,0:T(8,128)(2,1)S(1)} %collective-permute-done.18, bf16[256,256]{1,0:T(8,128)(2,1)S(1)} %collective-permute-done.17, bf16[256,256]{1,0:T(8,128)(2,1)} %get-tuple-element.50), kind=kLoop, calls=%fused_computation | loop fusion | flops 524288 | bytes 655360 | tf_op jit(solution)/shard_map/convert_element_type | solution.py:639
  117.4 0.0 collective-permute-done.10.refs_2_
  117.4 0.0 all-to-all-done.refs_3_
  117.4 2.9 %collect.1 = (bf16[256,256]{1,0:T(8,128)(2,1)}, bf16[256,256]{1,0:T(8,128)(2,1)}, bf16[256,256]{1,0:T(8,128)(2,1)}) custom-call(s32[14]{0:T(128)} %stack.59.refs_0_.refs_1_, bf16[256,128]{1,0:T(8,128)(2,1)} %get-tuple-element.40.refs_1_, bf16[256,128]{1,0:T(8,128)(2,1)} %collective-permute-done.10.refs_2_, bf16[8,256,256]{2,1,0:T(8,128)(2,1)} %all-to-all-done.refs_3_), custom_call_target="tpu_custom_call" | custom-call | flops 3000000000 | bytes 9000000 | tf_op jit(solution)/shard_map/collect/pallas_call | solution.py:56
  (6 shorter events, 0.0 us)
Async XLA Ops:
  0.6 26.5 %collective-permute-start.2 = (bf16[256,2048]{1,0:T(8,128)(2,1)}, bf16[256,2048]{1,0:T(8,128)(2,1)}, u32[]{:S(2)}, u32[]{:S(2)}) collective-permute-start(bf16[256,2048]{1,0:T(8,128)(2,1)} %bitcast.21), channel_id=1, source_target_pairs={{0,1},{1,0},{2,3},{3,2},{4,5},{5,4},{6,7},{7,6},{8,9},{9,8},{10,11... | collective-permute-start | bytes 3145736 | tf_op jit(solution)/shard_map/ppermute | solution.py:594
  6.6 7.5 %collective-permute-start = (bf16[256,256]{1,0:T(8,128)(2,1)}, bf16[256,256]{1,0:T(8,128)(2,1)}, u32[]{:S(2)}, u32[]{:S(2)}) collective-permute-start(bf16[256,256]{1,0:T(8,128)(2,1)} %get-tuple-element.29), channel_id=1, source_target_pairs={{0,2},{2,0},{4,6},{6,4},{8,10},{10,8},{12,14},{14,12},{1,3},{3,1},... | collective-permute-start | bytes 393224 | tf_op jit(solution)/shard_map/ppermute | solution.py:597
  8.1 10.2 %collective-permute-start.8 = (bf16[256,256]{1,0:T(8,128)(2,1)}, bf16[256,256]{1,0:T(8,128)(2,1)}, u32[]{:S(2)}, u32[]{:S(2)}) collective-permute-start(bf16[256,256]{1,0:T(8,128)(2,1)} %get-tuple-element.36.refs_5_.refs_8_), channel_id=1, source_target_pairs={{0,12},{2,14},{4,0},{6,2},{8,4},{10,6},{12,8},{14,10},{1,13},{3,15... | collective-permute-start | bytes 393224 | tf_op jit(solution)/shard_map/ppermute | solution.py:599
  11.7 12.3 %collective-permute-start.6 = (bf16[256,256]{1,0:T(8,128)(2,1)}, bf16[256,256]{1,0:T(8,128)(2,1)}, u32[]{:S(2)}, u32[]{:S(2)}) collective-permute-start(bf16[256,256]{1,0:T(8,128)(2,1)} %get-tuple-element.36.refs_5_.refs_8_), channel_id=1, source_target_pairs={{0,8},{2,10},{4,12},{6,14},{8,0},{10,2},{12,4},{14,6},{1,9},{3,11}... | collective-permute-start | bytes 393224 | tf_op jit(solution)/shard_map/ppermute | solution.py:599
  11.7 21.6 %collective-permute-start.4 = (bf16[256,256]{1,0:T(8,128)(2,1)}, bf16[256,256]{1,0:T(8,128)(2,1)}, u32[]{:S(2)}, u32[]{:S(2)}) collective-permute-start(bf16[256,256]{1,0:T(8,128)(2,1)} %get-tuple-element.36.refs_5_.refs_8_), channel_id=1, source_target_pairs={{0,4},{2,6},{4,8},{6,10},{8,12},{10,14},{12,0},{14,2},{1,5},{3,7},... | collective-permute-start | bytes 393224 | tf_op jit(solution)/shard_map/ppermute | solution.py:599
  17.7 17.2 %collective-permute-start.1 = (bf16[256,128]{1,0:T(8,128)(2,1)}, bf16[256,128]{1,0:T(8,128)(2,1)}, u32[]{:S(2)}, u32[]{:S(2)}) collective-permute-start(bf16[256,128]{1,0:T(8,128)(2,1)} %get-tuple-element.30), channel_id=1, source_target_pairs={{0,2},{2,0},{4,6},{6,4},{8,10},{10,8},{12,14},{14,12},{1,3},{3,1},... | collective-permute-start | bytes 196616 | tf_op jit(solution)/shard_map/ppermute | solution.py:607
  18.3 16.6 %collective-permute-start.9 = (bf16[256,256]{1,0:T(8,128)(2,1)}, bf16[256,256]{1,0:T(8,128)(2,1)}, u32[]{:S(2)}, u32[]{:S(2)}) collective-permute-start(bf16[256,256]{1,0:T(8,128)(2,1)} %collective-permute-done.refs_0_.refs_6_.refs_9_), channel_id=1, source_target_pairs={{0,12},{2,14},{4,0},{6,2},{8,4},{10,6},{12,8},{14,10},{1,13},{3,15... | collective-permute-start | bytes 393224 | tf_op jit(solution)/shard_map/ppermute | solution.py:599
  24.1 10.8 %collective-permute-start.7 = (bf16[256,256]{1,0:T(8,128)(2,1)}, bf16[256,256]{1,0:T(8,128)(2,1)}, u32[]{:S(2)}, u32[]{:S(2)}) collective-permute-start(bf16[256,256]{1,0:T(8,128)(2,1)} %collective-permute-done.refs_0_.refs_6_.refs_9_), channel_id=1, source_target_pairs={{0,8},{2,10},{4,12},{6,14},{8,0},{10,2},{12,4},{14,6},{1,9},{3,11}... | collective-permute-start | bytes 393224 | tf_op jit(solution)/shard_map/ppermute | solution.py:599
  27.1 7.8 %collective-permute-start.5 = (bf16[256,256]{1,0:T(8,128)(2,1)}, bf16[256,256]{1,0:T(8,128)(2,1)}, u32[]{:S(2)}, u32[]{:S(2)}) collective-permute-start(bf16[256,256]{1,0:T(8,128)(2,1)} %collective-permute-done.refs_0_.refs_6_.refs_9_), channel_id=1, source_target_pairs={{0,4},{2,6},{4,8},{6,10},{8,12},{10,14},{12,0},{14,2},{1,5},{3,7},... | collective-permute-start | bytes 393224 | tf_op jit(solution)/shard_map/ppermute | solution.py:599
  33.3 7.8 %collective-permute-start.3 = (bf16[128,256]{1,0:T(8,128)(2,1)}, bf16[128,256]{1,0:T(8,128)(2,1)}, u32[]{:S(2)}, u32[]{:S(2)}) collective-permute-start(bf16[128,256]{1,0:T(8,128)(2,1)} %get-tuple-element.33), channel_id=1, source_target_pairs={{0,2},{2,0},{4,6},{6,4},{8,10},{10,8},{12,14},{14,12},{1,3},{3,1},... | collective-permute-start | bytes 196616 | tf_op jit(solution)/shard_map/ppermute | solution.py:619
  49.0 4.4 %copy-start.2 = (bf16[4,256,256]{2,1,0:T(8,128)(2,1)S(1)}, bf16[4,256,256]{2,1,0:T(8,128)(2,1)}, u32[]{:S(2)}) copy-start(bf16[4,256,256]{2,1,0:T(8,128)(2,1)} %get-tuple-element.47) | copy-start | bytes 1572868
  49.0 6.3 %copy-start.1 = (bf16[4,256,256]{2,1,0:T(8,128)(2,1)S(1)}, bf16[4,256,256]{2,1,0:T(8,128)(2,1)}, u32[]{:S(2)}) copy-start(bf16[4,256,256]{2,1,0:T(8,128)(2,1)} %get-tuple-element.48) | copy-start | bytes 1572868
  49.0 6.3 %copy-start = (bf16[4,256,256]{2,1,0:T(8,128)(2,1)S(1)}, bf16[4,256,256]{2,1,0:T(8,128)(2,1)}, u32[]{:S(2)}) copy-start(bf16[4,256,256]{2,1,0:T(8,128)(2,1)} %get-tuple-element.49) | copy-start | bytes 1572868
  49.0 6.6 %copy-start.5 = (bf16[2,128,256]{2,1,0:T(8,128)(2,1)S(1)}, bf16[2,128,256]{2,1,0:T(8,128)(2,1)}, u32[]{:S(2)}) copy-start(bf16[2,128,256]{2,1,0:T(8,128)(2,1)} %get-tuple-element.46.refs_1_) | copy-start | bytes 393220
  49.0 68.4 %all-to-all-start = ((bf16[8,256,256]{2,1,0:T(8,128)(2,1)}), bf16[8,256,256]{2,1,0:T(8,128)(2,1)}, u32[]{:S(2)}, u32[]{:S(2)}) async-start(bf16[8,256,256]{2,1,0:T(8,128)(2,1)} %get-tuple-element.42), calls=%async_computation | async-start | bytes 2097152 | tf_op jit(solution)/shard_map/all_to_all | solution.py:626
  53.4 41.7 %collective-permute-start.14 = (bf16[4,256,256]{2,1,0:T(8,128)(2,1)S(1)}, bf16[4,256,256]{2,1,0:T(8,128)(2,1)S(1)}, u32[]{:S(2)}, u32[]{:S(2)}) collective-permute-start(bf16[4,256,256]{2,1,0:T(8,128)(2,1)S(1)} %copy-done.2), channel_id=1, source_target_pairs={{0,2},{2,0},{4,6},{6,4},{8,10},{10,8},{12,14},{14,12},{1,3},{3,1},... | collective-permute-start | bytes 1572872 | tf_op jit(solution)/shard_map/ppermute | solution.py:612
  55.3 39.8 %collective-permute-start.15 = (bf16[4,256,256]{2,1,0:T(8,128)(2,1)S(1)}, bf16[4,256,256]{2,1,0:T(8,128)(2,1)S(1)}, u32[]{:S(2)}, u32[]{:S(2)}) collective-permute-start(bf16[4,256,256]{2,1,0:T(8,128)(2,1)S(1)} %copy-done.1), channel_id=1, source_target_pairs={{0,16},{2,18},{4,20},{6,22},{8,24},{10,26},{12,28},{14,30},{16,0},... | collective-permute-start | bytes 1572872 | tf_op jit(solution)/shard_map/ppermute | solution.py:612
  55.3 41.4 %collective-permute-start.16 = (bf16[4,256,256]{2,1,0:T(8,128)(2,1)S(1)}, bf16[4,256,256]{2,1,0:T(8,128)(2,1)}, u32[]{:S(2)}, u32[]{:S(2)}) collective-permute-start(bf16[4,256,256]{2,1,0:T(8,128)(2,1)S(1)} %copy-done), channel_id=1, source_target_pairs={{0,18},{2,16},{4,22},{6,20},{8,26},{10,24},{12,30},{14,28},{16,2},... | collective-permute-start | bytes 1572872 | tf_op jit(solution)/shard_map/ppermute | solution.py:612
  55.6 33.9 %collective-permute-start.13 = (bf16[2,128,256]{2,1,0:T(8,128)(2,1)S(1)}, bf16[2,128,256]{2,1,0:T(8,128)(2,1)S(1)}, u32[]{:S(2)}, u32[]{:S(2)}) collective-permute-start(bf16[2,128,256]{2,1,0:T(8,128)(2,1)S(1)} %copy-done.5), channel_id=1, source_target_pairs={{0,18},{2,16},{4,22},{6,20},{8,26},{10,24},{12,30},{14,28},{16,2},... | collective-permute-start | bytes 393224 | tf_op jit(solution)/shard_map/ppermute | solution.py:612
  57.1 34.0 %collective-permute-start.12 = (bf16[2,128,256]{2,1,0:T(8,128)(2,1)S(1)}, bf16[2,128,256]{2,1,0:T(8,128)(2,1)S(1)}, u32[]{:S(2)}, u32[]{:S(2)}) collective-permute-start(bf16[2,128,256]{2,1,0:T(8,128)(2,1)S(1)} %copy-done.5), channel_id=1, source_target_pairs={{0,16},{2,18},{4,20},{6,22},{8,24},{10,26},{12,28},{14,30},{16,0},... | collective-permute-start | bytes 393224 | tf_op jit(solution)/shard_map/ppermute | solution.py:612
  89.6 5.6 %copy-start.6 = (bf16[2,128,256]{2,1,0:T(8,128)(2,1)}, bf16[2,128,256]{2,1,0:T(8,128)(2,1)S(1)}, u32[]{:S(2)}) copy-start(bf16[2,128,256]{2,1,0:T(8,128)(2,1)S(1)} %collective-permute-done.13.refs_4_) | copy-start | bytes 393220
  89.6 5.6 %collective-permute-start.11 = (bf16[2,128,256]{2,1,0:T(8,128)(2,1)S(1)}, bf16[2,128,256]{2,1,0:T(8,128)(2,1)S(1)}, u32[]{:S(2)}, u32[]{:S(2)}) collective-permute-start(bf16[2,128,256]{2,1,0:T(8,128)(2,1)S(1)} %copy-done.5), channel_id=1, source_target_pairs={{0,2},{2,0},{4,6},{6,4},{8,10},{10,8},{12,14},{14,12},{1,3},{3,1},... | collective-permute-start | bytes 393224 | tf_op jit(solution)/shard_map/ppermute | solution.py:612
  91.1 4.1 %copy-start.7 = (bf16[2,128,256]{2,1,0:T(8,128)(2,1)}, bf16[2,128,256]{2,1,0:T(8,128)(2,1)S(1)}, u32[]{:S(2)}) copy-start(bf16[2,128,256]{2,1,0:T(8,128)(2,1)S(1)} %collective-permute-done.12.refs_3_) | copy-start | bytes 393220
  95.1 0.7 copy-start.8
  95.1 0.8 copy-start.3
  96.0 0.8 copy-start.4
  102.0 8.5 %collective-permute-start.17 = (bf16[256,256]{1,0:T(8,128)(2,1)}, bf16[256,256]{1,0:T(8,128)(2,1)S(1)}, u32[]{:S(2)}, u32[]{:S(2)}) collective-permute-start(bf16[256,256]{1,0:T(8,128)(2,1)} %get-tuple-element.51), channel_id=1, source_target_pairs={{0,4},{2,6},{4,8},{6,10},{8,12},{10,14},{12,0},{14,2},{1,5},{3,7},... | collective-permute-start | bytes 393224 | tf_op jit(solution)/shard_map/ppermute | solution.py:632
  103.7 12.1 %collective-permute-start.18 = (bf16[256,256]{1,0:T(8,128)(2,1)}, bf16[256,256]{1,0:T(8,128)(2,1)S(1)}, u32[]{:S(2)}, u32[]{:S(2)}) collective-permute-start(bf16[256,256]{1,0:T(8,128)(2,1)} %get-tuple-element.52), channel_id=1, source_target_pairs={{0,8},{2,10},{4,12},{6,14},{8,0},{10,2},{12,4},{14,6},{1,9},{3,11}... | collective-permute-start | bytes 393224 | tf_op jit(solution)/shard_map/ppermute | solution.py:632
  106.2 9.6 %collective-permute-start.19 = (bf16[256,256]{1,0:T(8,128)(2,1)}, bf16[256,256]{1,0:T(8,128)(2,1)S(1)}, u32[]{:S(2)}, u32[]{:S(2)}) collective-permute-start(bf16[256,256]{1,0:T(8,128)(2,1)} %get-tuple-element.53), channel_id=1, source_target_pairs={{0,12},{2,14},{4,0},{6,2},{8,4},{10,6},{12,8},{14,10},{1,13},{3,15... | collective-permute-start | bytes 393224 | tf_op jit(solution)/shard_map/ppermute | solution.py:632
  109.0 8.4 %collective-permute-start.10 = (bf16[256,128]{1,0:T(8,128)(2,1)}, bf16[256,128]{1,0:T(8,128)(2,1)}, u32[]{:S(2)}, u32[]{:S(2)}) collective-permute-start(bf16[256,128]{1,0:T(8,128)(2,1)} %get-tuple-element.41), channel_id=1, source_target_pairs={{0,2},{2,0},{4,6},{6,4},{8,10},{10,8},{12,14},{14,12},{1,3},{3,1},... | collective-permute-start | bytes 196616 | tf_op jit(solution)/shard_map/ppermute | solution.py:627

commit v11 on v10

--- a/solution.py
+++ b/solution.py
@@ -276,8 +276,10 @@
 def backward_kernel(block_count, head_count, at_ref, *refs):
     q_ref, q_recv, g_mine, g_recv, attn_ref, inv_ref, e_ref = refs[:7]
     kv_refs, refs = refs[7 : 7 + block_count], refs[7 + block_count :]
-    dq_mine, dq_theirs, part_out, attn_out = refs[:4]
-    q_s, t_s, attn_s, inv_s, kv_s, e_s, part_s, dq_s, sem, kv_sem, e_sem, part_sem, dq_sem = refs[4:]
+    outer = block_count // INNER
+    dq_mine, dq_theirs, attn_out = refs[:3]
+    part_outs, refs = refs[3 : 3 + outer], refs[3 + outer :]
+    q_s, t_s, attn_s, inv_s, kv_s, e_s, part_s, dq_s, sem, kv_sem, e_sem, part_sem, dq_sem = refs
     rows = q_recv.shape[0]
     feats = head_count * HD
     score_scale = HD ** (-0.5)
@@ -321,7 +323,7 @@
             part_s[j, :, cols] = (score_scale * product(dscore, query)).astype(jnp.bfloat16)
             part_s[j, :, vcols] = product(low, grad).astype(jnp.bfloat16)
             if head == head_count - 1:
-                stores.append(begin(part_s.at[j], part_out.at[at_ref[SOURCES + j]], part_sem.at[j]))
+                stores.append(begin(part_s.at[j], part_outs[j // INNER].at[j % INNER], part_sem.at[j]))
         dquery = (score_scale * jnp.transpose(dq_t)).astype(jnp.bfloat16)
         dq_s[0, :, cols] = dquery[:rows]
         dq_s[1, :, cols] = dquery[rows:]
@@ -336,11 +338,12 @@
     rows, feats = q_recv.shape
     heads = feats // HD
     keys = block_count * rows
-    return call(
+    outer = block_count // INNER
+    out = call(
         functools.partial(backward_kernel, block_count, heads),
-        [bf16(rows, feats)] * 2 + [bf16(block_count, rows, 2 * feats), bf16(*attn.shape)],
+        [bf16(rows, feats)] * 2 + [bf16(*attn.shape)] + [bf16(INNER, rows, 2 * feats)] * outer,
         [SMEM] + [ANY] * (7 + block_count),
-        [ANY] * 4,
+        [ANY] * (3 + outer),
         [
             pltpu.VMEM((2, rows, feats), jnp.bfloat16),
             pltpu.VMEM((2, feats, rows), jnp.bfloat16),
@@ -359,6 +362,7 @@
         8,
         "backward",
     )(at, queries, q_recv, g_mine, g_recv, attn, inverse, weights, *kv_blocks)
+    return out[0], out[1], out[2], out[3:]
 
 
 def chunk(at_ref, steps_at, parts, place, width, target, semaphore):
@@ -374,9 +378,9 @@
     return pltpu.make_async_copy(parts[0].at[:, cols], target, semaphore)
 
 
-def grad_heads_kernel(part_count, routes, picked, columns_at, groups_at, at_ref, first_ref, weight_ref, *refs):
+def grad_heads_kernel(part_count, picked, columns_at, groups_at, at_ref, first_ref, weight_ref, *refs):
     grads, refs = refs[:part_count], refs[part_count:]
-    outs, sends, refs = refs[:2], refs[2 : 2 + len(routes)], refs[2 + len(routes) :]
+    outs, sends, refs = refs[:2], refs[2], refs[3:]
     first_s, grad_s, weight_s, out_s, first_sem, weight_sem, grad_sem, send_sem, out_sem = refs
     half = out_s.shape[1]
     width = grads[0].shape[1]
@@ -402,28 +406,28 @@
         copies.append(begin(out_s.at[side], outs[side], out_sem.at[side]))
     own_load.wait()
     parts = [grad_s.at[k] for k in range(part_count)]
-    for index, (step, side) in enumerate(routes):
-        outer, _, block = sends[index].shape
-        here = (1 - at_ref[0]) if side else at_ref[0]
+    route_count, outer, _, block = sends.shape
+    for index in range(route_count):
         for k in range(outer):
-            place = lax.rem(at_ref[1] + k, outer) * INNER + here
-            target, sem = sends[index].at[k], send_sem.at[index * outer + k]
-            copies.append(chunk(at_ref, groups_at + step * picked, parts, place, block, target, sem))
+            place = lax.rem(at_ref[1] + k, outer) * INNER + index % INNER
+            target, sem = sends.at[index, k], send_sem.at[index * outer + k]
+            steps_at = groups_at + index // INNER * picked
+            copies.append(chunk(at_ref, steps_at, parts, place, block, target, sem))
     for copy in copies:
         copy.wait()
 
 
-def grad_heads(at, columns_at, groups_at, first, out_weight, grads, routes, outer, picked):
+def grad_heads(at, columns_at, groups_at, first, out_weight, grads, route_count, outer, picked):
     feats, rows = first.shape
     half = feats // INNER
     count = len(grads)
     width = grads[0].shape[1]
     block = picked * width // (outer * INNER)
-    out = call(
-        functools.partial(grad_heads_kernel, count, routes, picked, columns_at, groups_at),
-        [bf16(half, rows), bf16(half, rows)] + [bf16(outer, rows, block)] * len(routes),
+    return call(
+        functools.partial(grad_heads_kernel, count, picked, columns_at, groups_at),
+        [bf16(half, rows), bf16(half, rows), bf16(route_count, outer, rows, block)],
         [SMEM] + [ANY] * (2 + count),
-        [ANY] * (2 + len(routes)),
+        [ANY] * 3,
         [
             pltpu.VMEM((feats, rows), jnp.float32),
             pltpu.VMEM((count, rows, width), jnp.bfloat16),
@@ -432,20 +436,17 @@
             pltpu.SemaphoreType.DMA,
             pltpu.SemaphoreType.DMA((count - 1,)),
             pltpu.SemaphoreType.DMA((count,)),
-            pltpu.SemaphoreType.DMA((len(routes) * outer,)),
+            pltpu.SemaphoreType.DMA((route_count * outer,)),
             pltpu.SemaphoreType.DMA((INNER,)),
         ],
         4,
         "grad_heads",
     )(at, first, out_weight, *grads)
-    return out[0], out[1], out[2:]
-
-
-def weight_kernel(part_count, doc_count, groups_at, at_ref, *refs):
+
+
+def weight_kernel(doc_count, doc_at, at_ref, *refs):
     route_count = INNER * doc_count
-    attn, refs = refs[:route_count], refs[route_count:]
-    grads, refs = refs[:part_count], refs[part_count:]
-    swapped, refs = refs[: route_count - 1], refs[route_count - 1 :]
+    attn, grads, refs = refs[:route_count], refs[route_count], refs[route_count + 1 :]
     attn_s, grad_s, out_s, attn_sem, grad_sem, out_sem = refs[-6:]
     outs = refs[:-6]
     outer, feats, width = out_s.shape
@@ -459,12 +460,12 @@
                 sem = attn_sem.at[(doc * INNER + side) * INNER + group]
                 attn_loads.append(begin(source, target, sem))
     for k in range(outer):
-        place = lax.rem(at_ref[1] + k, outer) * INNER + at_ref[0]
-        target, sem = grad_s.at[0, k], grad_sem.at[k]
-        loads = [chunk(at_ref, groups_at, grads, place, width, target, sem)]
-        for index, held in enumerate(swapped):
-            sem = grad_sem.at[(index + 1) * outer + k]
-            loads.append(begin(held.at[k], grad_s.at[index + 1, k], sem))
+        loads = []
+        for index in range(route_count):
+            doc = lax.rem(at_ref[doc_at] + doc_count - index // INNER, doc_count)
+            at = (1 - at_ref[0]) if index % INNER else at_ref[0]
+            sem = grad_sem.at[index * outer + k]
+            loads.append(begin(grads.at[doc * INNER + at, k], grad_s.at[index, k], sem))
         grad_loads.append(loads)
     for load in attn_loads:
         load.wait()
@@ -480,16 +481,15 @@
         store.wait()
 
 
-def weight_terms(at, groups_at, attn, grads, swapped, after=()):
+def weight_terms(at, doc_at, attn, grads, after=()):
     _, half, rows = attn[0].shape
-    outer, _, width = swapped[0].shape
+    _, outer, _, width = grads.shape
     feats = half * INNER
     routes = len(attn)
-    operands = [*attn, *grads, *swapped]
     return call(
-        functools.partial(weight_kernel, len(grads), routes // INNER, groups_at),
+        functools.partial(weight_kernel, routes // INNER, doc_at),
         [bf16(feats, width)] * outer,
-        [SMEM] + [ANY] * len(operands),
+        [SMEM] + [ANY] * (routes + 1),
         [ANY] * outer,
         [
             pltpu.VMEM((routes, feats, rows), jnp.bfloat16),
@@ -502,54 +502,89 @@
         5,
         "weight_terms",
         after,
-    )(at, *operands)
-
-
-def collect_kernel(at_ref, dq_mine, dq_recv, terms, *refs):
-    outs, (dq_s, terms_s, out_s, dq_sem, sem, out_sem) = refs[:3], refs[3:]
-    count, rows, both = terms.shape
-    half = both // 2
-    loads = [begin(terms.at[c], terms_s.at[c], sem.at[c]) for c in range(count)]
-    held = [begin(dq, dq_s.at[i], dq_sem.at[i]) for i, dq in enumerate((dq_mine, dq_recv))]
-    for side, at in enumerate((at_ref[0], 1 - at_ref[0])):
-        held[side].wait()
-        out_s[0, :, pl.ds(pl.multiple_of(at * half, half), half)] = dq_s[side]
-    stores = [begin(out_s.at[0], outs[0], out_sem.at[0])]
+    )(at, *attn, grads)
+
+
+def add_kernel(count, *refs):
+    terms, (mine, theirs) = refs[:count], refs[count : count + 2]
+    terms_s, out_s, term_sem, out_sem = refs[count + 2 :]
+    loads = [
+        begin(terms[c].at[side], terms_s.at[c, side], term_sem.at[c * INNER + side])
+        for side in (1, 0)
+        for c in range(count)
+    ]
+    stores = []
+    for index, (side, out) in enumerate(((1, theirs), (0, mine))):
+        for load in loads[index * count : (index + 1) * count]:
+            load.wait()
+        summed = terms_s[0, side].astype(jnp.float32)
+        for c in range(1, count):
+            summed = summed + terms_s[c, side].astype(jnp.float32)
+        out_s[side] = summed.astype(jnp.bfloat16)
+        stores.append(begin(out_s.at[side], out, out_sem.at[side]))
+    for store in stores:
+        store.wait()
+
+
+def add_terms(terms, after):
+    _, rows, width = terms[0].shape
+    count = len(terms)
+    return call(
+        functools.partial(add_kernel, count),
+        [bf16(rows, width)] * 2,
+        [ANY] * count,
+        [ANY] * 2,
+        [
+            pltpu.VMEM((count, INNER, rows, width), jnp.bfloat16),
+            pltpu.VMEM((INNER, rows, width), jnp.bfloat16),
+            pltpu.SemaphoreType.DMA((count * INNER,)),
+            pltpu.SemaphoreType.DMA((INNER,)),
+        ],
+        2,
+        "add_terms",
+        after,
+    )(*terms)
+
+
+def join_kernel(at_ref, dq_mine, dq_recv, mine, recv, *refs):
+    outs, (held_s, out_s, sem, out_sem) = refs[:3], refs[3:]
+    half = dq_mine.shape[1]
+    loads = [
+        begin(dq_mine, held_s.at[0, 0], sem.at[0]),
+        begin(dq_recv, held_s.at[1, 0], sem.at[1]),
+    ]
+    for side, held in enumerate((mine, recv)):
+        for index in range(2):
+            source = held.at[:, index * half : (index + 1) * half]
+            loads.append(begin(source, held_s.at[side, 1 + index], sem.at[2 + 2 * side + index]))
     for load in loads:
         load.wait()
-    for side in range(INNER):
-        summed = terms_s[side].astype(jnp.float32)
-        for c in range(side + INNER, count, INNER):
-            summed = summed + terms_s[c].astype(jnp.float32)
-        summed = summed.astype(jnp.bfloat16)
-        for kind in range(2):
-            cols = slice(side * half, (side + 1) * half)
-            out_s[1 + kind, :, cols] = summed[:, kind * half : (kind + 1) * half]
-    for index in (1, 2):
-        stores.append(begin(out_s.at[index], outs[index], out_sem.at[index]))
+    stores = []
+    for index, out in enumerate(outs):
+        for side, at in enumerate((at_ref[0], 1 - at_ref[0])):
+            cols = pl.ds(pl.multiple_of(at * half, half), half)
+            out_s[index, :, cols] = held_s[side, index]
+        stores.append(begin(out_s.at[index], out, out_sem.at[index]))
     for store in stores:
         store.wait()
 
 
-def collect(at, dq_mine, dq_recv, terms):
-    count, rows, both = terms.shape
-    half = both // 2
+def join_heads(at, dq_mine, dq_recv, mine, recv):
+    rows, half = dq_mine.shape
     return call(
-        collect_kernel,
+        join_kernel,
         [bf16(rows, INNER * half)] * 3,
-        [SMEM] + [ANY] * 3,
+        [SMEM] + [ANY] * 4,
         [ANY] * 3,
         [
-            pltpu.VMEM((INNER, rows, half), jnp.bfloat16),
-            pltpu.VMEM((count, rows, both), jnp.bfloat16),
+            pltpu.VMEM((INNER, 3, rows, half), jnp.bfloat16),
             pltpu.VMEM((3, rows, INNER * half), jnp.bfloat16),
-            pltpu.SemaphoreType.DMA((INNER,)),
-            pltpu.SemaphoreType.DMA((count,)),
+            pltpu.SemaphoreType.DMA((6,)),
             pltpu.SemaphoreType.DMA((3,)),
         ],
-        3,
-        "collect",
-    )(at, dq_mine, dq_recv, terms)
+        2,
+        "join_heads",
+    )(at, dq_mine, dq_recv, mine, recv)
 
 
 def per_device(
@@ -586,8 +621,9 @@
     scalars = scalars + [(tp_at + step) % tp_count for step in range(1, tp_count)]
     groups_at = len(scalars)
     for step in range(dp_count):
-        scalars = scalars + dp_steps((dp_at + step) % dp_count)
-    at = jnp.stack(scalars)
+        scalars = scalars + dp_steps(step)
+    doc_at = len(scalars)
+    at = jnp.stack(scalars + [dp_at])
 
     grad_own = grad_output[0]
     grads = [grad_own] + [
@@ -605,38 +641,45 @@
         at, block_pattern, global_offsets, queries[0], grad_own, out_weight, (kv_recv,)
     )
     q_recv = lax.ppermute(q_theirs, "ctx", ctx_pairs(0, 1))
-    partners = [(step, side) for step in range(dp_count) for side in range(INNER)][1:]
-
-    def to_partners(arrays):
-        return [
-            lax.ppermute(held, ("dp", "ctx") if step else "ctx", ctx_pairs(0, side, step))
-            for (step, side), held in zip(partners, arrays)
-        ]
-
-    g_mine, g_theirs, grad_sends = grad_heads(
-        at, columns_at, groups_at, first, out_weight, grads, partners, outer, picked
+    g_mine, g_theirs, sends = grad_heads(
+        at, columns_at, groups_at, first, out_weight, grads, dp_count * INNER, outer, picked
     )
     g_recv = lax.ppermute(g_theirs, "ctx", ctx_pairs(0, 1))
-    swapped = to_partners(grad_sends)
+    sharers = [
+        [d * ctx_count + o * INNER + i for d in range(dp_count) for i in range(INNER)]
+        for o in range(outer)
+    ]
+    columns = lax.all_to_all(
+        sends, ("dp", "ctx"), split_axis=0, concat_axis=0, axis_index_groups=sharers, tiled=True
+    )
 
     weights, inverse, attn = forward(at, queries[0], q_recv, key_mask, row_mask, kv_blocks)
-    dq_mine, dq_theirs, parts, attn = backward(
+    dq_mine, dq_theirs, attn, parts = backward(
         at, queries[0], q_recv, g_mine, g_recv, attn, inverse, weights, kv_blocks
     )
-    terms = lax.all_to_all(parts, "ctx", split_axis=0, concat_axis=0, tiled=True)
-    dq_recv = lax.ppermute(dq_theirs, "ctx", ctx_pairs(0, 1))
-
-    attn_all = [attn] + to_partners([attn] * len(partners))
-    weight_sums = weight_terms(at, groups_at, attn_all, grads, swapped)
+    terms = [
+        lax.ppermute(part, "ctx", ctx_pairs(-step, 0)) if step else part
+        for step, part in enumerate(parts)
+    ]
+
+    attn_all = [attn, lax.ppermute(attn, "ctx", ctx_pairs(0, 1))]
+    for step in range(1, dp_count):
+        pairs = shift_pairs(dp_count, step)
+        attn_all = attn_all + [lax.ppermute(held, "dp", pairs) for held in attn_all[:INNER]]
+    weight_sums = weight_terms(at, doc_at, attn_all, columns)
     weight_parts = [
         lax.ppermute(weight_sums[step], "ctx", ctx_pairs(step, 0)) for step in range(1, outer)
     ]
-    grad_q, grad_k, grad_v = collect(at, dq_mine, dq_recv, terms)
+
+    dq_recv = lax.ppermute(dq_theirs, "ctx", ctx_pairs(0, 1))
+    terms_mine, terms_theirs = add_terms(terms, (weight_sums[0],))
+    terms_recv = lax.ppermute(terms_theirs, "ctx", ctx_pairs(0, 1))
+    grad_q, grad_k, grad_v = join_heads(at, dq_mine, dq_recv, terms_mine, terms_recv)
     grad_weight = weight_sums[0].astype(jnp.float32)
     for part in weight_parts:
         grad_weight = grad_weight + part.astype(jnp.float32)
-
-    return grad_q[None], grad_k[None], grad_v[None], grad_weight.astype(jnp.bfloat16)
+    grad_weight = grad_weight.astype(jnp.bfloat16)
+    return grad_q[None], grad_k[None], grad_v[None], grad_weight
 
 
 def solution(mesh):

time: 121 us -> 123 us (1.017)
  waiting for transfers between devices: 48.3 us -> 52.1 us
  starting transfers between devices: 33.6 us -> 30.9 us
  Pallas kernels: 32.5 us -> 34.5 us
    ppermute x1, waiting for transfers between devices: 0.01 us -> 19 us  [per_device(): g_recv = lax.ppermute(g_theirs, 'ctx', ctx_pairs(0, 1))]
    ppermute x6 -> x7, waiting for transfers between devices: 36 us -> 25.4 us  [the longest x3 20.2 us: per_device(): lax.ppermute(part, 'ctx', ctx_pairs(-step, 0))]
    ppermute x3, waiting for transfers between devices: 6.23 us -> 1.73 us  [per_device(): lax.ppermute(weight_sums[step], 'ctx', ctx_pairs(step, 0))]
    ppermute x3, starting transfers between devices: 6.97 us -> 2.87 us  [per_device(): lax.ppermute(weight_sums[step], 'ctx', ctx_pairs(step, 0))]
    pallas_call x7 -> x8, Pallas kernels: 32.5 us -> 34.5 us  [placed(): return run(*args)]
    unnamed x19 -> x3, local copies, waits for them, and re-layouts: 2.96 us -> 2 us
    ppermute x6 -> x7, starting transfers between devices: 5.66 us -> 6.51 us  [the longest x3 4.62 us: per_device(): lax.ppermute(part, 'ctx', ctx_pairs(-step, 0))]
  transfers between devices with their start and end apart: 21 -> 22, of which waited for: 6 -> 7; matrix products, arithmetic and copies ran while one was open for 3% -> 3% of each run, Pallas kernels for 18% -> 26%
where the time goes in v11:
time: 123 us
  waiting for transfers between devices  52.1 us (42%)
  Pallas kernels  34.5 us (28%)
  starting transfers between devices  30.9 us (25%)
  local copies, waits for them, and re-layouts  2.6 us (2%)
  other arithmetic  1.82 us (1%)
    pallas_call x8, Pallas kernels, placed(): return run(*args)  34.5 us
    ppermute x3, waiting for transfers between devices, per_device(): lax.ppermute(part, 'ctx', ctx_pairs(-step, 0))  20.2 us
    ppermute x1, waiting for transfers between devices, per_device(): g_recv = lax.ppermute(g_theirs, 'ctx', ctx_pairs(0, 1))  19 us
    ppermute x6, starting transfers between devices, per_device(): lax.ppermute(kv_recv if side else kv_mine, 'ctx', ctx_pairs(step, 0))  9.22 us
    ppermute x1, waiting for transfers between devices, per_device(): attn_all = [attn, lax.ppermute(attn, 'ctx', ctx_pairs(0, 1))]  4.88 us
    ppermute x3, starting transfers between devices, per_device(): lax.ppermute(part, 'ctx', ctx_pairs(-step, 0))  4.62 us
    all_to_all x1, starting transfers between devices, per_device(): lax.all_to_all(sends, ('dp', 'ctx'), split_axis=0, concat_axis=0, axis_in...  4.47 us
    ppermute x1, waiting for transfers between devices, per_device(): lax.ppermute(grad_own, 'tp', shift_pairs(tp_count, -step))  3.03 us
  transfers between devices with their start and end apart: 22, of which 7 were waited for; matrix products, arithmetic and copies ran while one was open for 3% of the time, Pallas kernels for 26%

profile of v11, /device:TPU:0, one launch (start us, length us, event | category | flops | bytes accessed | tf_op | source)
XLA Modules:
  0.0 122.6 jit_solution(15731517543908324022)
XLA Ops:
  0.6 3.0 %collective-permute-start.2 = (bf16[256,2048]{1,0:T(8,128)(2,1)}, bf16[256,2048]{1,0:T(8,128)(2,1)}, u32[]{:S(2)}, u32[]{:S(2)}) collective-permute-start(bf16[256,2048]{1,0:T(8,128)(2,1)} %bitcast.22), channel_id=1, source_target_pairs={{0,1},{1,0},{2,3},{3,2},{4,5},{5,4},{6,7},{7,6},{8,9},{9,8},{10,11... | collective-permute-start | bytes 3145736 | tf_op jit(solution)/shard_map/ppermute | solution.py:630
  3.7 0.6 stack.63.refs_0_.refs_1_
  4.3 2.3 %part_heads.1 = (bf16[256,256]{1,0:T(8,128)(2,1)}, bf16[256,256]{1,0:T(8,128)(2,1)}) custom-call(s32[15]{0:T(128)} %stack.63.refs_0_.refs_1_, bf16[256,256]{1,0:T(8,128)(2,1)} %bitcast.25, bf16[256,256]{1,0:T(8,128)(2,1)} %bitcast.26), custom_call_target="tpu_custom_call" | custom-call | flops 2000000000 | bytes 6000000 | tf_op jit(solution)/shard_map/part_heads/pallas_call | solution.py:56
  6.6 1.6 %collective-permute-start = (bf16[256,256]{1,0:T(8,128)(2,1)}, bf16[256,256]{1,0:T(8,128)(2,1)}, u32[]{:S(2)}, u32[]{:S(2)}) collective-permute-start(bf16[256,256]{1,0:T(8,128)(2,1)} %get-tuple-element.32), channel_id=1, source_target_pairs={{0,2},{2,0},{4,6},{6,4},{8,10},{10,8},{12,14},{14,12},{1,3},{3,1},... | collective-permute-start | bytes 393224 | tf_op jit(solution)/shard_map/ppermute | solution.py:633
  8.2 3.6 %collective-permute-start.8 = (bf16[256,256]{1,0:T(8,128)(2,1)}, bf16[256,256]{1,0:T(8,128)(2,1)}, u32[]{:S(2)}, u32[]{:S(2)}) collective-permute-start(bf16[256,256]{1,0:T(8,128)(2,1)} %get-tuple-element.39.refs_5_.refs_8_), channel_id=1, source_target_pairs={{0,12},{2,14},{4,0},{6,2},{8,4},{10,6},{12,8},{14,10},{1,13},{3,15... | collective-permute-start | bytes 393224 | tf_op jit(solution)/shard_map/ppermute | solution.py:635
  11.8 0.0 collective-permute-start.6
  11.8 1.0 collective-permute-start.4
  12.8 1.3 %copy.11.refs_2_ = s32[8,3]{1,0:T(8,128)} copy(s32[8,3]{0,1:T(4,128)} %param.12) | data formatting | bytes 192 | tf_op args[5]
  14.1 0.0 collective-permute-done.refs_0_.refs_6_.refs_9_
  14.1 3.6 %prelude.1 = (f32[256,256]{1,0:T(8,128)}, bf16[2048,128]{1,0:T(8,128)(2,1)}, f32[8,512]{1,0:T(8,128)}, bf16[256,128]{1,0:T(8,128)(2,1)}) custom-call(bf16[256,256]{1,0:T(8,128)(2,1)} %collective-permute-done.refs_0_.refs_6_.refs_9_, s32[15]{0:T(128)} %stack.63.refs_0_.refs_1_, s32[8,3]{1,0:T(8,128)} %copy.11.refs_2_, s32[8,8]{1,0:T(8,128)} %refs_3_.1, ...), custom_call_target="tpu_custom_call" | custom-call | flops 4000000000 | bytes 12000000 | tf_op jit(solution)/shard_map/prelude/pallas_call | solution.py:56
  17.7 0.6 collective-permute-start.1
  18.3 0.0 collective-permute-done.8.refs_11_.refs_14_
  18.4 2.8 %collective-permute-start.9 = (bf16[256,256]{1,0:T(8,128)(2,1)}, bf16[256,256]{1,0:T(8,128)(2,1)}, u32[]{:S(2)}, u32[]{:S(2)}) collective-permute-start(bf16[256,256]{1,0:T(8,128)(2,1)} %collective-permute-done.refs_0_.refs_6_.refs_9_), channel_id=1, source_target_pairs={{0,12},{2,14},{4,0},{6,2},{8,4},{10,6},{12,8},{14,10},{1,13},{3,15... | collective-permute-start | bytes 393224 | tf_op jit(solution)/shard_map/ppermute | solution.py:635
  21.2 2.9 %collective-permute-done.6.refs_9_.refs_12_ = bf16[256,256]{1,0:T(8,128)(2,1)} collective-permute-done((bf16[256,256]{1,0:T(8,128)(2,1)}, bf16[256,256]{1,0:T(8,128)(2,1)}, u32[]{:S(2)}, u32[]{:S(2)}) %collective-permute-start.6) | collective-permute-done | bytes 131104 | tf_op jit(solution)/shard_map/ppermute | solution.py:635
  24.1 0.0 collective-permute-start.7
  24.1 3.0 %collective-permute-done.2.refs_4_ = bf16[256,2048]{1,0:T(8,128)(2,1)} collective-permute-done((bf16[256,2048]{1,0:T(8,128)(2,1)}, bf16[256,2048]{1,0:T(8,128)(2,1)}, u32[]{:S(2)}, u32[]{:S(2)}) %collective-permute-start.2) | collective-permute-done | bytes 1048608 | tf_op jit(solution)/shard_map/ppermute | solution.py:630
  27.1 1.8 %collective-permute-start.5 = (bf16[256,256]{1,0:T(8,128)(2,1)}, bf16[256,256]{1,0:T(8,128)(2,1)}, u32[]{:S(2)}, u32[]{:S(2)}) collective-permute-start(bf16[256,256]{1,0:T(8,128)(2,1)} %collective-permute-done.refs_0_.refs_6_.refs_9_), channel_id=1, source_target_pairs={{0,4},{2,6},{4,8},{6,10},{8,12},{10,14},{12,0},{14,2},{1,5},{3,7},... | collective-permute-start | bytes 393224 | tf_op jit(solution)/shard_map/ppermute | solution.py:635
  28.9 4.6 %grad_heads.1 = (bf16[128,256]{1,0:T(8,128)(2,1)}, bf16[128,256]{1,0:T(8,128)(2,1)}, bf16[4,4,256,256]{3,2,1,0:T(8,128)(2,1)}) custom-call(s32[15]{0:T(128)} %stack.63.refs_0_.refs_1_, f32[256,256]{1,0:T(8,128)} %get-tuple-element.34.refs_1_, bf16[256,4096]{1,0:T(8,128)(2,1)} %refs_2_.2, bf16[256,2048]{1,0:T(8,128)(2,1)} %bitcast.24, ...), custom_call_target="tpu_custom_call" | custom-call | flops 4000000000 | bytes 12000000 | tf_op jit(solution)/shard_map/grad_heads/pallas_call | solution.py:56
  33.5 4.5 %all-to-all-start = ((bf16[4,4,256,256]{3,2,1,0:T(8,128)(2,1)}), bf16[4,4,256,256]{3,2,1,0:T(8,128)(2,1)}, u32[]{:S(2)}, u32[]{:S(2)}) async-start(bf16[4,4,256,256]{3,2,1,0:T(8,128)(2,1)} %get-tuple-element.46), calls=%async_computation | async-start | bytes 4194304 | tf_op jit(solution)/shard_map/all_to_all | solution.py:652
  38.0 0.0 collective-permute-done.4.refs_7_.refs_10_
  38.0 2.0 %collective-permute-start.3 = (bf16[128,256]{1,0:T(8,128)(2,1)}, bf16[128,256]{1,0:T(8,128)(2,1)}, u32[]{:S(2)}, u32[]{:S(2)}) collective-permute-start(bf16[128,256]{1,0:T(8,128)(2,1)} %get-tuple-element.36), channel_id=1, source_target_pairs={{0,2},{2,0},{4,6},{6,4},{8,10},{10,8},{12,14},{14,12},{1,3},{3,1},... | collective-permute-start | bytes 196616 | tf_op jit(solution)/shard_map/ppermute | solution.py:647
  40.0 0.0 collective-permute-done.1.refs_2_
  40.0 0.0 collective-permute-done.9.refs_12_.refs_15_
  40.0 0.0 collective-permute-done.7.refs_10_.refs_13_
  40.0 0.0 collective-permute-done.5.refs_8_.refs_11_
  40.0 6.2 %forward.1 = (bf16[1,2048,512]{2,1,0:T(8,128)(2,1)}, f32[8,512]{1,0:T(8,128)}, bf16[2,128,256]{2,1,0:T(8,128)(2,1)}) custom-call(s32[15]{0:T(128)} %stack.63.refs_0_.refs_1_, bf16[256,256]{1,0:T(8,128)(2,1)} %bitcast.28, bf16[256,128]{1,0:T(8,128)(2,1)} %collective-permute-done.1.refs_2_, bf16[2048,128]{1,0:T(8,128)(2,1)} %get-tuple-element.37.refs_3_, ...), custom_call_target="tpu_custom_call" | custom-call | flops 6000000000 | bytes 18000000 | tf_op jit(solution)/shard_map/forward/pallas_call | solution.py:56
  46.2 19.0 %collective-permute-done.3.refs_4_ = bf16[128,256]{1,0:T(8,128)(2,1)} collective-permute-done((bf16[128,256]{1,0:T(8,128)(2,1)}, bf16[128,256]{1,0:T(8,128)(2,1)}, u32[]{:S(2)}, u32[]{:S(2)}) %collective-permute-start.3) | collective-permute-done | bytes 65568 | tf_op jit(solution)/shard_map/ppermute | solution.py:647
  65.2 7.9 %backward.1 = (bf16[256,128]{1,0:T(8,128)(2,1)}, bf16[256,128]{1,0:T(8,128)(2,1)}, bf16[2,128,256]{2,1,0:T(8,128)(2,1)}, bf16[2,256,256]{2,1,0:T(8,128)(2,1)}, b...) custom-call(s32[15]{0:T(128)} %stack.63.refs_0_.refs_1_, ...), custom_call_target="tpu_custom_call" | custom-call | flops 8000000000 | bytes 24000000 | tf_op jit(solution)/shard_map/backward/pallas_call | solution.py:56
  73.1 0.4 collective-permute-start.11
  73.6 0.0 collective-permute-start.12
  73.6 4.9 %collective-permute-done.11.refs_2_ = bf16[2,128,256]{2,1,0:T(8,128)(2,1)S(1)} collective-permute-done((bf16[2,128,256]{2,1,0:T(8,128)(2,1)}, bf16[2,128,256]{2,1,0:T(8,128)(2,1)S(1)}, u32[]{:S(2)}, u32[]{:S(2)}) %collective-permute-start.11) | collective-permute-done | bytes 131104 | tf_op jit(solution)/shard_map/ppermute | solution.py:665
  78.4 0.0 copy-start
  78.4 0.7 copy-done
  79.1 0.0 collective-permute-start.13
  79.1 0.6 collective-permute-start.10
  79.7 2.0 %collective-permute-start.14 = (bf16[2,256,256]{2,1,0:T(8,128)(2,1)}, bf16[2,256,256]{2,1,0:T(8,128)(2,1)}, u32[]{:S(2)}, u32[]{:S(2)}) collective-permute-start(bf16[2,256,256]{2,1,0:T(8,128)(2,1)} %get-tuple-element.49), channel_id=1, source_target_pairs={{0,12},{2,14},{4,0},{6,2},{8,4},{10,6},{12,8},{14,10},{1,13},{3,15... | collective-permute-start | bytes 786440 | tf_op jit(solution)/shard_map/ppermute | solution.py:661
  81.8 1.0 collective-permute-start.15
  82.8 0.0 collective-permute-done.12.refs_3_
  82.8 1.6 %collective-permute-start.16 = (bf16[2,256,256]{2,1,0:T(8,128)(2,1)}, bf16[2,256,256]{2,1,0:T(8,128)(2,1)}, u32[]{:S(2)}, u32[]{:S(2)}) collective-permute-start(bf16[2,256,256]{2,1,0:T(8,128)(2,1)} %get-tuple-element.51), channel_id=1, source_target_pairs={{0,4},{2,6},{4,8},{6,10},{8,12},{10,14},{12,0},{14,2},{1,5},{3,7},... | collective-permute-start | bytes 786440 | tf_op jit(solution)/shard_map/ppermute | solution.py:661
  84.4 0.0 collective-permute-done.13.refs_4_
  84.4 0.0 all-to-all-done.refs_5_
  84.4 5.2 %weight_terms.1 = (bf16[256,256]{1,0:T(8,128)(2,1)}, bf16[256,256]{1,0:T(8,128)(2,1)}, bf16[256,256]{1,0:T(8,128)(2,1)}, bf16[256,256]{1,0:T(8,128)(2,1)}) custom-call(s32[15]{0:T(128)} %stack.63.refs_0_.refs_1_, bf16[2,128,256]{2,1,0:T(8,128)(2,1)} %get-tuple-element.45.refs_1_, bf16[2,128,256]{2,1,0:T(8,128)(2,1)} %copy-done, ...), custom_call_target="tpu_custom_call" | custom-call | flops 5000000000 | bytes 15000000 | tf_op jit(solution)/shard_map/weight_terms/pallas_call | solution.py:56
  89.6 1.0 collective-permute-start.18
  90.6 0.0 collective-permute-done.14.refs_2_
  90.6 1.9 %collective-permute-start.19 = (bf16[256,256]{1,0:T(8,128)(2,1)}, bf16[256,256]{1,0:T(8,128)(2,1)}, u32[]{:S(2)}, u32[]{:S(2)}) collective-permute-start(bf16[256,256]{1,0:T(8,128)(2,1)} %get-tuple-element.58), channel_id=1, source_target_pairs={{0,8},{2,10},{4,12},{6,14},{8,0},{10,2},{12,4},{14,6},{1,9},{3,11}... | collective-permute-start | bytes 393224 | tf_op jit(solution)/shard_map/ppermute | solution.py:671
  92.5 20.2 %collective-permute-done.15.refs_3_ = bf16[2,256,256]{2,1,0:T(8,128)(2,1)} collective-permute-done((bf16[2,256,256]{2,1,0:T(8,128)(2,1)}, bf16[2,256,256]{2,1,0:T(8,128)(2,1)}, u32[]{:S(2)}, u32[]{:S(2)}) %collective-permute-start.15) | collective-permute-done | bytes 262176 | tf_op jit(solution)/shard_map/ppermute | solution.py:661
  112.7 0.0 collective-permute-start.20
  112.7 0.0 collective-permute-done.16.refs_4_
  112.7 2.1 %add_terms.1 = (bf16[256,256]{1,0:T(8,128)(2,1)}, bf16[256,256]{1,0:T(8,128)(2,1)}) custom-call(bf16[256,256]{1,0:T(8,128)(2,1)} %get-tuple-element.47.refs_0_, bf16[2,256,256]{2,1,0:T(8,128)(2,1)} %get-tuple-element.48.refs_1_, bf16[2,256,256]{2,1,0:T(8,128)(2,1)} %collective-permute-done.14.refs_2_, bf16[2,256,256]{2,1,0:T(8,128)(2,1)} %collective-permute-done.15.refs_3_, ...), custom_call_target="tpu_custom_call" | custom-call | flops 2000000000 | bytes 6000000 | tf_op jit(solution)/shard_map/add_terms/pallas_call | solution.py:56
  114.8 1.5 %collective-permute-start.17 = (bf16[256,256]{1,0:T(8,128)(2,1)}, bf16[256,256]{1,0:T(8,128)(2,1)}, u32[]{:S(2)}, u32[]{:S(2)}) collective-permute-start(bf16[256,256]{1,0:T(8,128)(2,1)} %get-tuple-element.53), channel_id=1, source_target_pairs={{0,2},{2,0},{4,6},{6,4},{8,10},{10,8},{12,14},{14,12},{1,3},{3,1},... | collective-permute-start | bytes 393224 | tf_op jit(solution)/shard_map/ppermute | solution.py:676
  116.2 0.0 collective-permute-done.18
  116.2 0.0 collective-permute-done.19
  116.2 1.7 %collective-permute-done.20 = bf16[256,256]{1,0:T(8,128)(2,1)} collective-permute-done((bf16[256,256]{1,0:T(8,128)(2,1)}, bf16[256,256]{1,0:T(8,128)(2,1)}, u32[]{:S(2)}, u32[]{:S(2)}) %collective-permute-start.20) | collective-permute-done | bytes 131104 | tf_op jit(solution)/shard_map/ppermute | solution.py:671
  118.0 1.8 %add_convert_fusion = bf16[256,256]{1,0:T(8,128)(2,1)} fusion(bf16[256,256]{1,0:T(8,128)(2,1)} %collective-permute-done.20, bf16[256,256]{1,0:T(8,128)(2,1)} %collective-permute-done.19, bf16[256,256]{1,0:T(8,128)(2,1)} %collective-permute-done.18, bf16[256,256]{1,0:T(8,128)(2,1)} %get-tuple-element.47.refs_0_), kind=kLoop, calls=%fused_computation | loop fusion | flops 524288 | bytes 655360 | tf_op jit(solution)/shard_map/convert_element_type | solution.py:681
  119.8 0.0 collective-permute-done.10.refs_2_
  119.8 0.3 collective-permute-done.17.refs_4_
  120.1 2.5 %join_heads.1 = (bf16[256,256]{1,0:T(8,128)(2,1)}, bf16[256,256]{1,0:T(8,128)(2,1)}, bf16[256,256]{1,0:T(8,128)(2,1)}) custom-call(s32[15]{0:T(128)} %stack.63.refs_0_.refs_1_, bf16[256,128]{1,0:T(8,128)(2,1)} %get-tuple-element.43.refs_1_, bf16[256,128]{1,0:T(8,128)(2,1)} %collective-permute-done.10.refs_2_, bf16[256,256]{1,0:T(8,128)(2,1)} %get-tuple-element.52.refs_3_, ...), custom_call_target="tpu_custom_call" | custom-call | flops 2000000000 | bytes 6000000 | tf_op jit(solution)/shard_map/join_heads/pallas_call | solution.py:56
Async XLA Ops:
  0.6 26.5 %collective-permute-start.2 = (bf16[256,2048]{1,0:T(8,128)(2,1)}, bf16[256,2048]{1,0:T(8,128)(2,1)}, u32[]{:S(2)}, u32[]{:S(2)}) collective-permute-start(bf16[256,2048]{1,0:T(8,128)(2,1)} %bitcast.22), channel_id=1, source_target_pairs={{0,1},{1,0},{2,3},{3,2},{4,5},{5,4},{6,7},{7,6},{8,9},{9,8},{10,11... | collective-permute-start | bytes 3145736 | tf_op jit(solution)/shard_map/ppermute | solution.py:630
  6.6 7.5 %collective-permute-start = (bf16[256,256]{1,0:T(8,128)(2,1)}, bf16[256,256]{1,0:T(8,128)(2,1)}, u32[]{:S(2)}, u32[]{:S(2)}) collective-permute-start(bf16[256,256]{1,0:T(8,128)(2,1)} %get-tuple-element.32), channel_id=1, source_target_pairs={{0,2},{2,0},{4,6},{6,4},{8,10},{10,8},{12,14},{14,12},{1,3},{3,1},... | collective-permute-start | bytes 393224 | tf_op jit(solution)/shard_map/ppermute | solution.py:633
  8.2 10.2 %collective-permute-start.8 = (bf16[256,256]{1,0:T(8,128)(2,1)}, bf16[256,256]{1,0:T(8,128)(2,1)}, u32[]{:S(2)}, u32[]{:S(2)}) collective-permute-start(bf16[256,256]{1,0:T(8,128)(2,1)} %get-tuple-element.39.refs_5_.refs_8_), channel_id=1, source_target_pairs={{0,12},{2,14},{4,0},{6,2},{8,4},{10,6},{12,8},{14,10},{1,13},{3,15... | collective-permute-start | bytes 393224 | tf_op jit(solution)/shard_map/ppermute | solution.py:635
  11.8 12.3 %collective-permute-start.6 = (bf16[256,256]{1,0:T(8,128)(2,1)}, bf16[256,256]{1,0:T(8,128)(2,1)}, u32[]{:S(2)}, u32[]{:S(2)}) collective-permute-start(bf16[256,256]{1,0:T(8,128)(2,1)} %get-tuple-element.39.refs_5_.refs_8_), channel_id=1, source_target_pairs={{0,8},{2,10},{4,12},{6,14},{8,0},{10,2},{12,4},{14,6},{1,9},{3,11}... | collective-permute-start | bytes 393224 | tf_op jit(solution)/shard_map/ppermute | solution.py:635
  11.8 26.3 %collective-permute-start.4 = (bf16[256,256]{1,0:T(8,128)(2,1)}, bf16[256,256]{1,0:T(8,128)(2,1)}, u32[]{:S(2)}, u32[]{:S(2)}) collective-permute-start(bf16[256,256]{1,0:T(8,128)(2,1)} %get-tuple-element.39.refs_5_.refs_8_), channel_id=1, source_target_pairs={{0,4},{2,6},{4,8},{6,10},{8,12},{10,14},{12,0},{14,2},{1,5},{3,7},... | collective-permute-start | bytes 393224 | tf_op jit(solution)/shard_map/ppermute | solution.py:635
  17.7 22.3 %collective-permute-start.1 = (bf16[256,128]{1,0:T(8,128)(2,1)}, bf16[256,128]{1,0:T(8,128)(2,1)}, u32[]{:S(2)}, u32[]{:S(2)}) collective-permute-start(bf16[256,128]{1,0:T(8,128)(2,1)} %get-tuple-element.33), channel_id=1, source_target_pairs={{0,2},{2,0},{4,6},{6,4},{8,10},{10,8},{12,14},{14,12},{1,3},{3,1},... | collective-permute-start | bytes 196616 | tf_op jit(solution)/shard_map/ppermute | solution.py:643
  18.4 21.7 %collective-permute-start.9 = (bf16[256,256]{1,0:T(8,128)(2,1)}, bf16[256,256]{1,0:T(8,128)(2,1)}, u32[]{:S(2)}, u32[]{:S(2)}) collective-permute-start(bf16[256,256]{1,0:T(8,128)(2,1)} %collective-permute-done.refs_0_.refs_6_.refs_9_), channel_id=1, source_target_pairs={{0,12},{2,14},{4,0},{6,2},{8,4},{10,6},{12,8},{14,10},{1,13},{3,15... | collective-permute-start | bytes 393224 | tf_op jit(solution)/shard_map/ppermute | solution.py:635
  24.1 15.9 %collective-permute-start.7 = (bf16[256,256]{1,0:T(8,128)(2,1)}, bf16[256,256]{1,0:T(8,128)(2,1)}, u32[]{:S(2)}, u32[]{:S(2)}) collective-permute-start(bf16[256,256]{1,0:T(8,128)(2,1)} %collective-permute-done.refs_0_.refs_6_.refs_9_), channel_id=1, source_target_pairs={{0,8},{2,10},{4,12},{6,14},{8,0},{10,2},{12,4},{14,6},{1,9},{3,11}... | collective-permute-start | bytes 393224 | tf_op jit(solution)/shard_map/ppermute | solution.py:635
  27.1 12.9 %collective-permute-start.5 = (bf16[256,256]{1,0:T(8,128)(2,1)}, bf16[256,256]{1,0:T(8,128)(2,1)}, u32[]{:S(2)}, u32[]{:S(2)}) collective-permute-start(bf16[256,256]{1,0:T(8,128)(2,1)} %collective-permute-done.refs_0_.refs_6_.refs_9_), channel_id=1, source_target_pairs={{0,4},{2,6},{4,8},{6,10},{8,12},{10,14},{12,0},{14,2},{1,5},{3,7},... | collective-permute-start | bytes 393224 | tf_op jit(solution)/shard_map/ppermute | solution.py:635
  33.5 50.8 %all-to-all-start = ((bf16[4,4,256,256]{3,2,1,0:T(8,128)(2,1)}), bf16[4,4,256,256]{3,2,1,0:T(8,128)(2,1)}, u32[]{:S(2)}, u32[]{:S(2)}) async-start(bf16[4,4,256,256]{3,2,1,0:T(8,128)(2,1)} %get-tuple-element.46), calls=%async_computation | async-start | bytes 4194304 | tf_op jit(solution)/shard_map/all_to_all | solution.py:652
  38.0 27.1 %collective-permute-start.3 = (bf16[128,256]{1,0:T(8,128)(2,1)}, bf16[128,256]{1,0:T(8,128)(2,1)}, u32[]{:S(2)}, u32[]{:S(2)}) collective-permute-start(bf16[128,256]{1,0:T(8,128)(2,1)} %get-tuple-element.36), channel_id=1, source_target_pairs={{0,2},{2,0},{4,6},{6,4},{8,10},{10,8},{12,14},{14,12},{1,3},{3,1},... | collective-permute-start | bytes 196616 | tf_op jit(solution)/shard_map/ppermute | solution.py:647
  73.1 5.3 %collective-permute-start.11 = (bf16[2,128,256]{2,1,0:T(8,128)(2,1)}, bf16[2,128,256]{2,1,0:T(8,128)(2,1)S(1)}, u32[]{:S(2)}, u32[]{:S(2)}) collective-permute-start(bf16[2,128,256]{2,1,0:T(8,128)(2,1)} %get-tuple-element.45.refs_1_), channel_id=1, source_target_pairs={{0,2},{2,0},{4,6},{6,4},{8,10},{10,8},{12,14},{14,12},{1,3},{3,1},... | collective-permute-start | bytes 393224 | tf_op jit(solution)/shard_map/ppermute | solution.py:665
  73.6 9.2 %collective-permute-start.12 = (bf16[2,128,256]{2,1,0:T(8,128)(2,1)}, bf16[2,128,256]{2,1,0:T(8,128)(2,1)}, u32[]{:S(2)}, u32[]{:S(2)}) collective-permute-start(bf16[2,128,256]{2,1,0:T(8,128)(2,1)} %get-tuple-element.45.refs_1_), channel_id=1, source_target_pairs={{0,16},{16,0},{1,17},{17,1},{2,18},{18,2},{3,19},{19,3},{4,20},{20... | collective-permute-start | bytes 393224 | tf_op jit(solution)/shard_map/ppermute | solution.py:668
  78.4 0.7 copy-start
  79.1 5.3 %collective-permute-start.13 = (bf16[2,128,256]{2,1,0:T(8,128)(2,1)S(1)}, bf16[2,128,256]{2,1,0:T(8,128)(2,1)}, u32[]{:S(2)}, u32[]{:S(2)}) collective-permute-start(bf16[2,128,256]{2,1,0:T(8,128)(2,1)S(1)} %collective-permute-done.11.refs_2_), channel_id=1, source_target_pairs={{0,16},{16,0},{1,17},{17,1},{2,18},{18,2},{3,19},{19,3},{4,20},{20... | collective-permute-start | bytes 393224 | tf_op jit(solution)/shard_map/ppermute | solution.py:668
  79.1 40.7 %collective-permute-start.10 = (bf16[256,128]{1,0:T(8,128)(2,1)}, bf16[256,128]{1,0:T(8,128)(2,1)}, u32[]{:S(2)}, u32[]{:S(2)}) collective-permute-start(bf16[256,128]{1,0:T(8,128)(2,1)} %get-tuple-element.44), channel_id=1, source_target_pairs={{0,2},{2,0},{4,6},{6,4},{8,10},{10,8},{12,14},{14,12},{1,3},{3,1},... | collective-permute-start | bytes 196616 | tf_op jit(solution)/shard_map/ppermute | solution.py:674
  79.7 10.8 %collective-permute-start.14 = (bf16[2,256,256]{2,1,0:T(8,128)(2,1)}, bf16[2,256,256]{2,1,0:T(8,128)(2,1)}, u32[]{:S(2)}, u32[]{:S(2)}) collective-permute-start(bf16[2,256,256]{2,1,0:T(8,128)(2,1)} %get-tuple-element.49), channel_id=1, source_target_pairs={{0,12},{2,14},{4,0},{6,2},{8,4},{10,6},{12,8},{14,10},{1,13},{3,15... | collective-permute-start | bytes 786440 | tf_op jit(solution)/shard_map/ppermute | solution.py:661
  81.8 30.9 %collective-permute-start.15 = (bf16[2,256,256]{2,1,0:T(8,128)(2,1)}, bf16[2,256,256]{2,1,0:T(8,128)(2,1)}, u32[]{:S(2)}, u32[]{:S(2)}) collective-permute-start(bf16[2,256,256]{2,1,0:T(8,128)(2,1)} %get-tuple-element.50), channel_id=1, source_target_pairs={{0,8},{2,10},{4,12},{6,14},{8,0},{10,2},{12,4},{14,6},{1,9},{3,11}... | collective-permute-start | bytes 786440 | tf_op jit(solution)/shard_map/ppermute | solution.py:661
  82.8 29.9 %collective-permute-start.16 = (bf16[2,256,256]{2,1,0:T(8,128)(2,1)}, bf16[2,256,256]{2,1,0:T(8,128)(2,1)}, u32[]{:S(2)}, u32[]{:S(2)}) collective-permute-start(bf16[2,256,256]{2,1,0:T(8,128)(2,1)} %get-tuple-element.51), channel_id=1, source_target_pairs={{0,4},{2,6},{4,8},{6,10},{8,12},{10,14},{12,0},{14,2},{1,5},{3,7},... | collective-permute-start | bytes 786440 | tf_op jit(solution)/shard_map/ppermute | solution.py:661
  89.6 26.6 %collective-permute-start.18 = (bf16[256,256]{1,0:T(8,128)(2,1)}, bf16[256,256]{1,0:T(8,128)(2,1)}, u32[]{:S(2)}, u32[]{:S(2)}) collective-permute-start(bf16[256,256]{1,0:T(8,128)(2,1)} %get-tuple-element.57), channel_id=1, source_target_pairs={{0,4},{2,6},{4,8},{6,10},{8,12},{10,14},{12,0},{14,2},{1,5},{3,7},... | collective-permute-start | bytes 393224 | tf_op jit(solution)/shard_map/ppermute | solution.py:671
  90.6 25.7 %collective-permute-start.19 = (bf16[256,256]{1,0:T(8,128)(2,1)}, bf16[256,256]{1,0:T(8,128)(2,1)}, u32[]{:S(2)}, u32[]{:S(2)}) collective-permute-start(bf16[256,256]{1,0:T(8,128)(2,1)} %get-tuple-element.58), channel_id=1, source_target_pairs={{0,8},{2,10},{4,12},{6,14},{8,0},{10,2},{12,4},{14,6},{1,9},{3,11}... | collective-permute-start | bytes 393224 | tf_op jit(solution)/shard_map/ppermute | solution.py:671
  112.7 5.3 %collective-permute-start.20 = (bf16[256,256]{1,0:T(8,128)(2,1)}, bf16[256,256]{1,0:T(8,128)(2,1)}, u32[]{:S(2)}, u32[]{:S(2)}) collective-permute-start(bf16[256,256]{1,0:T(8,128)(2,1)} %get-tuple-element.59), channel_id=1, source_target_pairs={{0,12},{2,14},{4,0},{6,2},{8,4},{10,6},{12,8},{14,10},{1,13},{3,15... | collective-permute-start | bytes 393224 | tf_op jit(solution)/shard_map/ppermute | solution.py:671
  114.8 5.3 %collective-permute-start.17 = (bf16[256,256]{1,0:T(8,128)(2,1)}, bf16[256,256]{1,0:T(8,128)(2,1)}, u32[]{:S(2)}, u32[]{:S(2)}) collective-permute-start(bf16[256,256]{1,0:T(8,128)(2,1)} %get-tuple-element.53), channel_id=1, source_target_pairs={{0,2},{2,0},{4,6},{6,4},{8,10},{10,8},{12,14},{14,12},{1,3},{3,1},... | collective-permute-start | bytes 393224 | tf_op jit(solution)/shard_map/ppermute | solution.py:676

commit v12 on v9

v12 whole, which is shorter than its diff:
```python
import functools

import jax
import jax.numpy as jnp
from jax import lax
from jax.experimental import pallas as pl
from jax.experimental.pallas import tpu as pltpu
from jax.sharding import PartitionSpec as P

HD = 128
MASKED = -1e30
INNER = 2
SOURCES = 3
ANY = pl.BlockSpec(memory_space=pl.ANY)
VMEM = pl.BlockSpec(memory_space=pltpu.VMEM)
SMEM = pl.BlockSpec(memory_space=pltpu.SMEM)


def against(left_op, right_op):
    return lax.dot_general(
        left_op, right_op, (((1,), (1,)), ((), ())), preferred_element_type=jnp.float32
    )


def product(left_op, right_op):
    return jnp.dot(left_op, right_op, preferred_element_type=jnp.float32)


def begin(source, target, semaphore):
    copy = pltpu.make_async_copy(source, target, semaphore)
    copy.start()
    return copy


def call(kernel, out_shape, in_specs, out_specs, scratch, micros, name, after=()):
    skipped = len(after)
    in_specs = [ANY] * skipped + in_specs
    run = pl.pallas_call(
        lambda *refs: kernel(*refs[skipped:]),
        out_shape=out_shape,
        in_specs=in_specs,
        out_specs=out_specs,
        scratch_shapes=scratch,
        compiler_params=pltpu.CompilerParams(vmem_limit_bytes=64 * 1024 * 1024),
        cost_estimate=pl.CostEstimate(
            flops=int(micros * 1e9), bytes_accessed=int(micros * 3e6), transcendentals=0
        ),
        name=name,
    )

    def placed(*args):
        args = [
            pltpu.with_memory_space_constraint(arg, pltpu.HBM) if spec is ANY else arg
            for spec, arg in zip(in_specs, (*after, *args))
        ]
        return run(*args)

    return placed


def bf16(*shape):
    return pltpu.HBM(shape, jnp.bfloat16)


def f32(*shape):
    return pltpu.HBM(shape, jnp.float32)


def part_kernel(at_ref, k_ref, v_ref, kv_mine, kv_theirs, held_s, in_sem, out_sem):
    half = kv_mine.shape[1] // 2
    loads = [begin(held, held_s.at[i], in_sem.at[i]) for i, held in enumerate((k_ref, v_ref))]
    mine = pl.ds(pl.multiple_of(at_ref[0] * half, half), half)
    theirs = pl.ds(pl.multiple_of((1 - at_ref[0]) * half, half), half)
    copies = []
    for index in range(2):
        loads[index].wait()
        place = slice(index * half, (index + 1) * half)
        for side, (cols, out) in enumerate(((mine, kv_mine), (theirs, kv_theirs))):
            sem = out_sem.at[2 * index + side]
            copies.append(begin(held_s.at[index, :, cols], out.at[:, place], sem))
    for copy in copies:
        copy.wait()


def part_heads(at, keys, values):
    rows, feats = keys.shape
    return call(
        part_kernel,
        [bf16(rows, feats), bf16(rows, feats)],
        [SMEM] + [ANY] * 2,
        [ANY] * 2,
        [
            pltpu.VMEM((2, rows, feats), jnp.bfloat16),
            pltpu.SemaphoreType.DMA((2,)),
            pltpu.SemaphoreType.DMA((4,)),
        ],
        2,
        "part_heads",
    )(at, keys, values)


def prelude_kernel(at_ref, pattern, offsets, grad_ref, weight_ref, *refs):
    first, key_mask, row_mask = refs[:3]
    grad_s, weight_s, first_s, mask_s, row_s, sem, out_sem = refs[3:]
    rows, width = grad_s.shape
    block_count, glob_count = offsets.shape
    start = pl.multiple_of(at_ref[2] * width, width)
    loads = [
        begin(grad_ref, grad_s, sem.at[0]),
        begin(weight_ref.at[:, pl.ds(start, width)], weight_s, sem.at[1]),
    ]
    stores = []
    own = at_ref[1] * INNER + at_ref[0]
    partner = at_ref[1] * INNER + 1 - at_ref[0]
    lane = lax.broadcasted_iota(jnp.int32, (1, HD), 1)
    row_at = lax.broadcasted_iota(jnp.int32, (rows, HD), 0)
    col_at = lax.broadcasted_iota(jnp.int32, (8, rows), 1)
    group_at = lax.broadcasted_iota(jnp.int32, (8, rows), 0)
    for index in range(block_count):
        block = at_ref[SOURCES + index]
        hidden = []
        for target in (own, partner):
            seen = jnp.abs(block - target) <= 1
            for r in range(pattern.shape[1]):
                seen = seen | (pattern[target, r] == block)
            hidden.append(jnp.where(seen, 0, 1))
        lane_hidden = jnp.where(lane == 0, hidden[0], jnp.where(lane == 1, hidden[1], 0))
        hidden_rows = jnp.broadcast_to(lane_hidden, (rows, HD))
        for r in range(glob_count):
            hidden_rows = jnp.where(row_at == offsets[block, r], 0, hidden_rows)
        mask_s[index * rows : (index + 1) * rows, :] = hidden_rows.astype(jnp.float32).astype(
            jnp.bfloat16
        )
    for group, target in enumerate((own, partner)):
        local = jnp.where(group_at == group, MASKED, 0.0)
        for r in range(glob_count):
            local = jnp.where(col_at == offsets[target, r], 0.0, local)
        row_s[:, group * rows : (group + 1) * rows] = local
    stores.append(begin(mask_s, key_mask, out_sem.at[0]))
    stores.append(begin(row_s, row_mask, out_sem.at[1]))
    for load in loads:
        load.wait()
    first_s[...] = against(weight_s[...], grad_s[...])
    stores.append(begin(first_s, first, out_sem.at[2]))
    for store in stores:
        store.wait()


def prelude(at, pattern, offsets, grad_own, out_weight, after):
    rows, width = grad_own.shape
    feats = out_weight.shape[0]
    keys = offsets.shape[0] * rows
    return call(
        prelude_kernel,
        [
            f32(feats, rows),
            bf16(keys, HD),
            f32(8, 2 * rows),
        ],
        [SMEM] * 3 + [ANY] * 2,
        [ANY] * 3,
        [
            pltpu.VMEM((rows, width), jnp.bfloat16),
            pltpu.VMEM((feats, width), jnp.bfloat16),
            pltpu.VMEM((feats, rows), jnp.float32),
            pltpu.VMEM((keys, HD), jnp.bfloat16),
            pltpu.VMEM((8, 2 * rows), jnp.float32),
            pltpu.SemaphoreType.DMA((2,)),
            pltpu.SemaphoreType.DMA((3,)),
        ],
        4,
        "prelude",
        after,
    )(at, pattern, offsets, grad_own, out_weight)


def attention_kernel(block_count, head_count, at_ref, q_ref, recv_ref, g_mine, key_mask, row_mask, *refs):
    kv_refs, refs = refs[:block_count], refs[block_count:]
    attn_mine, attn_theirs, dq_mine, dq_theirs, part_out = refs[:5]
    q_s, recv_s, g_s, mask_s, row_s, kv_s, e_s, s_ref, attn_s, dq_s, part_s = refs[5:16]
    sem, kv_sem, out_sem, part_sem = refs[16:]
    rows = q_ref.shape[0]
    feats = head_count * HD
    score_scale = HD ** (-0.5)
    mine = pl.ds(pl.multiple_of(at_ref[0] * feats, feats), feats)
    loads = [
        begin(q_ref.at[:, mine], q_s, sem.at[0]),
        begin(recv_ref, recv_s, sem.at[1]),
        begin(key_mask, mask_s, sem.at[2]),
        begin(row_mask, row_s, sem.at[3]),
        begin(g_mine, g_s, sem.at[4]),
    ]
    kv_loads = [begin(kv_refs[j], kv_s.at[j], kv_sem.at[j]) for j in range(block_count)]
    for load in loads:
        load.wait()
    rows_low = row_s[...].astype(jnp.bfloat16)
    hidden = jnp.concatenate([rows_low, jnp.zeros((HD - 8, 2 * rows), jnp.bfloat16)], axis=0)
    stores = []
    for head in range(head_count):
        cols = slice(head * HD, (head + 1) * HD)
        vcols = slice(feats + head * HD, feats + (head + 1) * HD)
        query_recv = recv_s[1, cols, :]
        q_t = jnp.concatenate([jnp.transpose(q_s[:, cols]), query_recv], axis=1)
        q_t = jnp.concatenate([q_t, hidden], axis=0)
        top = jnp.full((1, 2 * rows), MASKED, jnp.float32)
        for j in range(block_count):
            if head == 0:
                kv_loads[j].wait()
            keys = slice(j * rows, (j + 1) * rows)
            scores = product(jnp.concatenate([kv_s[j, :, cols], mask_s[keys, :]], axis=1), q_t)
            s_ref[keys, :] = scores
            top = jnp.maximum(top, jnp.max(scores, axis=0, keepdims=True))
        total = jnp.zeros((1, 2 * rows), jnp.float32)
        attn_t = jnp.zeros((HD, 2 * rows), jnp.float32)
        for j in range(block_count):
            keys = slice(j * rows, (j + 1) * rows)
            weights = jnp.exp((s_ref[keys, :] - top) * score_scale)
            total = total + jnp.sum(weights, axis=0, keepdims=True)
            low = weights.astype(jnp.bfloat16)
            e_s[keys, :] = low
            attn_t = attn_t + product(jnp.transpose(kv_s[j, :, vcols]), low)
        inverse = 1.0 / total
        attn_low = (attn_t * inverse).astype(jnp.bfloat16)
        attn_s[0, cols, :] = attn_low[:, :rows]
        attn_s[1, cols, :] = attn_low[:, rows:]
        if head == head_count - 1:
            stores.append(begin(attn_s.at[0], attn_mine, out_sem.at[0]))
            stores.append(begin(attn_s.at[1], attn_theirs, out_sem.at[1]))
        g_t = jnp.concatenate([g_s[cols, :], recv_s[0, cols, :]], axis=1).astype(jnp.float32)
        row_dot = jnp.sum(g_t * attn_low.astype(jnp.float32), axis=0, keepdims=True) * inverse
        g_t = (g_t * inverse).astype(jnp.bfloat16)
        grad = jnp.transpose(g_t)
        query = jnp.concatenate([q_s[:, cols], jnp.transpose(query_recv)], axis=0)
        dq_t = jnp.zeros((HD, 2 * rows), jnp.float32)
        for j in range(block_count):
            keys = slice(j * rows, (j + 1) * rows)
            low = e_s[keys, :]
            dprobs = product(kv_s[j, :, vcols], g_t)
            dscore = (low.astype(jnp.float32) * (dprobs - row_dot)).astype(jnp.bfloat16)
            dq_t = dq_t + product(jnp.transpose(kv_s[j, :, cols]), dscore)
            part_s[j, :, cols] = (score_scale * product(dscore, query)).astype(jnp.bfloat16)
            part_s[j, :, vcols] = product(low, grad).astype(jnp.bfloat16)
            if head == head_count - 1:
                target = part_out.at[at_ref[SOURCES + j]]
                stores.append(begin(part_s.at[j], target, part_sem.at[j]))
        dquery = (score_scale * jnp.transpose(dq_t)).astype(jnp.bfloat16)
        dq_s[0, :, cols] = dquery[:rows]
        dq_s[1, :, cols] = dquery[rows:]
    stores.append(begin(dq_s.at[0], dq_mine, out_sem.at[2]))
    stores.append(begin(dq_s.at[1], dq_theirs, out_sem.at[3]))
    for store in stores:
        store.wait()


def attention(at, queries, recv, g_mine, key_mask, row_mask, kv_blocks):
    block_count = len(kv_blocks)
    feats, rows = g_mine.shape
    heads = feats // HD
    keys = block_count * rows
    return call(
        functools.partial(attention_kernel, block_count, heads),
        [bf16(feats, rows)] * 2 + [bf16(rows, feats)] * 2 + [bf16(block_count, rows, 2 * feats)],
        [SMEM] + [ANY] * (5 + block_count),
        [ANY] * 5,
        [
            pltpu.VMEM((rows, feats), jnp.bfloat16),
            pltpu.VMEM((2, feats, rows), jnp.bfloat16),
            pltpu.VMEM((feats, rows), jnp.bfloat16),
            pltpu.VMEM((keys, HD), jnp.bfloat16),
            pltpu.VMEM((8, 2 * rows), jnp.float32),
            pltpu.VMEM((block_count, rows, 2 * feats), jnp.bfloat16),
            pltpu.VMEM((keys, 2 * rows), jnp.bfloat16),
            pltpu.VMEM((keys, 2 * rows), jnp.float32),
            pltpu.VMEM((2, feats, rows), jnp.bfloat16),
            pltpu.VMEM((2, rows, feats), jnp.bfloat16),
            pltpu.VMEM((block_count, rows, 2 * feats), jnp.bfloat16),
            pltpu.SemaphoreType.DMA((5,)),
            pltpu.SemaphoreType.DMA((block_count,)),
            pltpu.SemaphoreType.DMA((4,)),
            pltpu.SemaphoreType.DMA((block_count,)),
        ],
        20,
        "attention",
    )(at, queries, recv, g_mine, key_mask, row_mask, *kv_blocks)


def grad_heads_kernel(part_count, place, at_ref, first_ref, q_ref, weight_ref, *refs):
    grads, refs = refs[: part_count - 1], refs[part_count - 1 :]
    mine, theirs = refs[:2]
    first_s, q_s, grad_s, weight_s, out_s, sem, weight_sem, grad_sem, out_sem = refs[2:]
    half = out_s.shape[1]
    width = grads[0].shape[1]
    first_load = begin(first_ref, first_s, sem.at[0])
    cols = pl.ds(pl.multiple_of((1 - at_ref[0]) * half, half), half)
    q_load = begin(q_ref.at[:, cols], q_s, sem.at[1])
    loads = []
    for k in range(part_count - 1):
        start = pl.multiple_of(at_ref[place + k] * width, width)
        columns = weight_ref.at[:, pl.ds(start, width)]
        loads.append(begin(grads[k], grad_s.at[k], grad_sem.at[k]))
        loads.append(begin(columns, weight_s.at[k], weight_sem.at[k]))
    q_load.wait()
    out_s[2] = jnp.transpose(q_s[...])
    copies = [begin(out_s.at[2], theirs.at[1], out_sem.at[2])]
    first_load.wait()
    summed = first_s[...]
    for k in range(part_count - 1):
        loads[2 * k].wait()
        loads[2 * k + 1].wait()
        summed = summed + against(weight_s[k], grad_s[k])
    first_s[...] = summed
    for side, target in enumerate((mine, theirs.at[0])):
        at = (1 - at_ref[0]) if side else at_ref[0]
        kept = first_s[pl.ds(pl.multiple_of(at * half, half), half), :]
        out_s[side] = kept.astype(jnp.bfloat16)
        copies.append(begin(out_s.at[side], target, out_sem.at[side]))
    for copy in copies:
        copy.wait()


def grad_heads(at, place, first, queries, out_weight, grads):
    feats, rows = first.shape
    half = feats // INNER
    count = len(grads)
    width = grads[0].shape[1]
    return call(
        functools.partial(grad_heads_kernel, count, place),
        [bf16(half, rows), bf16(2, half, rows)],
        [SMEM] + [ANY] * (2 + count),
        [ANY] * 2,
        [
            pltpu.VMEM((feats, rows), jnp.float32),
            pltpu.VMEM((rows, half), jnp.bfloat16),
            pltpu.VMEM((count - 1, rows, width), jnp.bfloat16),
            pltpu.VMEM((count - 1, feats, width), jnp.bfloat16),
            pltpu.VMEM((3, half, rows), jnp.bfloat16),
            pltpu.SemaphoreType.DMA((2,)),
            pltpu.SemaphoreType.DMA((count - 1,)),
            pltpu.SemaphoreType.DMA((count - 1,)),
            pltpu.SemaphoreType.DMA((3,)),
        ],
        3,
        "grad_heads",
    )(at, first, queries, out_weight, *grads[1:])


def pick_kernel(part_count, place, at_ref, *refs):
    grads, (out, held_s, sem, out_sem) = refs[:part_count], refs[part_count:]
    width = grads[0].shape[1]
    picked = out.shape[1] // width
    for i in range(picked):
        for k in range(part_count):

            @pl.when(at_ref[place + i] == k)
            def _():
                begin(grads[k], held_s.at[i], sem.at[i])

    stores = []
    for i in range(picked):
        pltpu.make_async_copy(grads[0], held_s.at[i], sem.at[i]).wait()
        target = out.at[:, i * width : (i + 1) * width]
        stores.append(begin(held_s.at[i], target, out_sem.at[i]))
    for store in stores:
        store.wait()


def pick_columns(at, place, grads, picked, after):
    rows, width = grads[0].shape
    return call(
        functools.partial(pick_kernel, len(grads), place),
        bf16(rows, picked * width),
        [SMEM] + [ANY] * len(grads),
        ANY,
        [
            pltpu.VMEM((picked, rows, width), jnp.bfloat16),
            pltpu.SemaphoreType.DMA((picked,)),
            pltpu.SemaphoreType.DMA((picked,)),
        ],
        2,
        "pick_columns",
        after,
    )(at, *grads)


def weight_kernel(part_count, doc_count, sent, step_at, at_ref, *refs):
    attn, refs = refs[: INNER * doc_count], refs[INNER * doc_count :]
    grads, refs = refs[:part_count], refs[part_count:]
    swapped, refs = refs[: doc_count - 1], refs[doc_count - 1 :]
    if sent:
        out, refs = refs[0], refs[1:]
        outs = [out.at[k] for k in range(out.shape[0])]
    else:
        recv, passed, refs = refs[0], refs[1], refs[2:]
        outs, refs = refs[: recv.shape[0]], refs[recv.shape[0] :]
        passed_out, recv_s, passed_s, recv_sem, passed_sem = refs[:5]
        refs = refs[5:]
        passed_load = begin(passed, passed_s, passed_sem)
    attn_s, grad_s, out_s, attn_sem, grad_sem, out_sem = refs
    outer, feats, width = out_s.shape
    half = feats // INNER
    piece = grads[0].shape[1]
    pieces = piece // width
    here = (1 - at_ref[0]) if sent else at_ref[0]
    attn_loads, grad_loads = [], []
    for doc in range(doc_count):
        for side in range(INNER):
            at = (1 - at_ref[0]) if side else at_ref[0]
            index = doc * INNER + side
            target = attn_s.at[doc, pl.ds(pl.multiple_of(at * half, half), half)]
            attn_loads.append(begin(attn[index], target, attn_sem.at[index]))
    for k in range(outer):
        place = lax.rem(at_ref[1] + k, outer) * INNER + here
        which = at_ref[step_at + place // pieces]
        cols = pl.ds(pl.multiple_of(lax.rem(place, pieces) * width, width), width)
        for i in range(part_count):

            @pl.when(which == i)
            def _():
                begin(grads[i].at[:, cols], grad_s.at[0, k], grad_sem.at[k])

        loads = [pltpu.make_async_copy(grads[0].at[:, cols], grad_s.at[0, k], grad_sem.at[k])]
        cols = pl.ds(pl.multiple_of(place * width, width), width)
        for doc in range(1, doc_count):
            source = swapped[doc - 1].at[:, cols]
            loads.append(begin(source, grad_s.at[doc, k], grad_sem.at[doc * outer + k]))
        if not sent:
            loads.append(begin(recv.at[k], recv_s.at[k], recv_sem.at[k]))
        grad_loads.append(loads)
    for load in attn_loads:
        load.wait()
    stores = []
    if not sent:
        passed_load.wait()
        stores.append(begin(passed_s, passed_out, passed_sem))
    for k in range(outer):
        term = 0.0
        for doc in range(doc_count):
            grad_loads[k][doc].wait()
            term = term + product(attn_s[doc], grad_s[doc, k])
        if not sent:
            grad_loads[k][doc_count].wait()
            term = term + recv_s[k].astype(jnp.float32)
        out_s[k] = term.astype(out_s.dtype)
        stores.append(begin(out_s.at[k], outs[k], out_sem.at[k]))
    for store in stores:
        store.wait()


def weight_terms(at, step_at, attn, grads, swapped, outer, picked, recv=None, passed=None, after=()):
    half, rows = attn[0].shape
    feats = half * INNER
    doc_count = len(attn) // INNER
    width = picked * grads[0].shape[1] // (outer * INNER)
    sent = recv is None
    operands = [*attn, *grads, *swapped] + ([] if sent else [recv, passed])
    scratch = [
        pltpu.VMEM((doc_count, feats, rows), jnp.bfloat16),
        pltpu.VMEM((doc_count, outer, rows, width), jnp.bfloat16),
        pltpu.VMEM((outer, feats, width), jnp.bfloat16),
        pltpu.SemaphoreType.DMA((len(attn),)),
        pltpu.SemaphoreType.DMA((doc_count * outer,)),
        pltpu.SemaphoreType.DMA((outer,)),
    ]
    if not sent:
        scratch = [
            pltpu.VMEM((outer, feats, width), jnp.bfloat16),
            pltpu.VMEM(passed.shape, jnp.bfloat16),
            pltpu.SemaphoreType.DMA((outer,)),
            pltpu.SemaphoreType.DMA,
        ] + scratch
    return call(
        functools.partial(weight_kernel, len(grads), doc_count, sent, step_at),
        bf16(outer, feats, width) if sent else [bf16(feats, width)] * outer + [bf16(*passed.shape)],
        [SMEM] + [ANY] * len(operands),
        ANY if sent else [ANY] * (outer + 1),
        scratch,
        4,
        "weight_sent" if sent else "weight_kept",
        after,
    )(at, *operands)


def collect_kernel(at_ref, dq_mine, dq_recv, terms, *refs):
    outs, (dq_s, terms_s, out_s, dq_sem, sem, out_sem) = refs[:3], refs[3:]
    count, rows, both = terms.shape
    half = both // 2
    loads = [begin(terms.at[c], terms_s.at[c], sem.at[c]) for c in range(count)]
    held = [begin(dq, dq_s.at[i], dq_sem.at[i]) for i, dq in enumerate((dq_mine, dq_recv))]
    for side, at in enumerate((at_ref[0], 1 - at_ref[0])):
        held[side].wait()
        out_s[0, :, pl.ds(pl.multiple_of(at * half, half), half)] = dq_s[side]
    stores = [begin(out_s.at[0], outs[0], out_sem.at[0])]
    for load in loads:
        load.wait()
    for side in range(INNER):
        summed = terms_s[side].astype(jnp.float32)
        for c in range(side + INNER, count, INNER):
            summed = summed + terms_s[c].astype(jnp.float32)
        summed = summed.astype(jnp.bfloat16)
        for kind in range(2):
            cols = slice(side * half, (side + 1) * half)
            out_s[1 + kind, :, cols] = summed[:, kind * half : (kind + 1) * half]
    for index in (1, 2):
        stores.append(begin(out_s.at[index], outs[index], out_sem.at[index]))
    for store in stores:
        store.wait()


def collect(at, dq_mine, dq_recv, terms):
    count, rows, both = terms.shape
    half = both // 2
    return call(
        collect_kernel,
        [bf16(rows, INNER * half)] * 3,
        [SMEM] + [ANY] * 3,
        [ANY] * 3,
        [
            pltpu.VMEM((INNER, rows, half), jnp.bfloat16),
            pltpu.VMEM((count, rows, both), jnp.bfloat16),
            pltpu.VMEM((3, rows, INNER * half), jnp.bfloat16),
            pltpu.SemaphoreType.DMA((INNER,)),
            pltpu.SemaphoreType.DMA((count,)),
            pltpu.SemaphoreType.DMA((3,)),
        ],
        3,
        "collect",
    )(at, dq_mine, dq_recv, terms)


def per_device(
    queries, key_heads, value_heads, grad_output, out_weight, block_pattern, global_offsets
):
    dp_count, ctx_count, tp_count = (lax.axis_size(name) for name in ("dp", "ctx", "tp"))
    dp_at, ctx_at, tp_at = (lax.axis_index(name) for name in ("dp", "ctx", "tp"))
    outer = ctx_count // INNER
    outer_at, inner_at = ctx_at // INNER, ctx_at % INNER
    picked = tp_count // dp_count

    def ctx_pairs(step, side, dp_step=0):
        moved = [(c + step * INNER) % ctx_count ^ side for c in range(ctx_count)]
        if not dp_step:
            return list(enumerate(moved))
        return [
            (d * ctx_count + c, (d + dp_step) % dp_count * ctx_count + moved[c])
            for d in range(dp_count)
            for c in range(ctx_count)
        ]

    def shift_pairs(count, step):
        return [(i, (i + step) % count) for i in range(count)]

    def dp_steps(which):
        return [(which * picked + i - tp_at) % tp_count for i in range(picked)]

    routes = [(step, side) for step in range(outer) for side in range(INNER)]
    sources = [
        ((outer_at - step) % outer) * INNER + (inner_at + side) % INNER for step, side in routes
    ]
    scalars = [inner_at, outer_at, tp_at] + sources
    columns_at = len(scalars)
    scalars = scalars + [(tp_at + step) % tp_count for step in range(1, tp_count)]
    send_at = len(scalars)
    for step in range(1, dp_count):
        scalars = scalars + dp_steps((dp_at + step) % dp_count)
    keep_at = len(scalars)
    at = jnp.stack(scalars + dp_steps(dp_at))

    grad_own = grad_output[0]
    grads = [grad_own] + [
        lax.ppermute(grad_own, "tp", shift_pairs(tp_count, -step)) for step in range(1, tp_count)
    ]
    kv_mine, kv_theirs = part_heads(at, key_heads[0], value_heads[0])
    kv_recv = lax.ppermute(kv_theirs, "ctx", ctx_pairs(0, 1))
    kv_blocks = [
        lax.ppermute(kv_recv if side else kv_mine, "ctx", ctx_pairs(step, 0))
        if step
        else (kv_recv if side else kv_mine)
        for step, side in routes
    ]
    first, key_mask, row_mask = prelude(
        at, block_pattern, global_offsets, grad_own, out_weight, (kv_recv, *kv_blocks[INNER::INNER])
    )
    g_mine, theirs = grad_heads(at, columns_at, first, queries[0], out_weight, grads)
    recv = lax.ppermute(theirs, "ctx", ctx_pairs(0, 1))
    grad_sends = [
        pick_columns(at, send_at + step * picked, grads, picked, (g_mine,))
        for step in range(dp_count - 1)
    ]
    swapped = [
        lax.ppermute(send, "dp", shift_pairs(dp_count, step + 1))
        for step, send in enumerate(grad_sends)
    ]

    attn_mine, attn_theirs, dq_mine, dq_theirs, parts = attention(
        at, queries[0], recv, g_mine, key_mask, row_mask, kv_blocks
    )
    terms = lax.all_to_all(parts, "ctx", split_axis=0, concat_axis=0, tiled=True)

    attn = []
    for step in range(dp_count):
        for held, side in ((attn_mine, 0), (attn_theirs, 1)):
            pairs = ctx_pairs(0, side, step)
            axes = ("dp", "ctx") if step else "ctx"
            attn.append(lax.ppermute(held, axes, pairs) if step or side else held)

    send = weight_terms(at, keep_at, attn, grads, swapped, outer, picked)
    weight_recv = lax.ppermute(send, "ctx", ctx_pairs(0, 1))
    *weight_sums, dq_theirs = weight_terms(
        at, keep_at, attn, grads, swapped, outer, picked, weight_recv, dq_theirs
    )
    weight_parts = [
        lax.ppermute(weight_sums[step], "ctx", ctx_pairs(step, 0)) for step in range(1, outer)
    ]
    dq_recv = lax.ppermute(dq_theirs, "ctx", ctx_pairs(0, 1))
    grad_q, grad_k, grad_v = collect(at, dq_mine, dq_recv, terms)
    weight_parts, grad_k = lax.optimization_barrier((weight_parts, grad_k))
    grad_weight = weight_sums[0].astype(jnp.float32)
    for part in weight_parts:
        grad_weight = grad_weight + part.astype(jnp.float32)

    return grad_q[None], grad_k[None], grad_v[None], grad_weight.astype(jnp.bfloat16)


def solution(mesh):
    in_specs = (
        P("dp", "ctx", "tp"),
        P("dp", "ctx", "tp"),
        P("dp", "ctx", "tp"),
        P("dp", "ctx", "tp"),
        P("tp", None),
        P(),
        P(),
    )
    out_specs = (
        P("dp", "ctx", "tp"),
        P("dp", "ctx", "tp"),
        P("dp", "ctx", "tp"),
        P("tp", ("dp", "ctx")),
    )
    return jax.shard_map(
        per_device, mesh=mesh, in_specs=in_specs, out_specs=out_specs, check_vma=False
    )
```

time: 97.3 us -> 109 us (1.12)
  waiting for transfers between devices: 20.5 us -> 37.2 us
  Pallas kernels: 36.8 us -> 33.1 us
  starting transfers between devices: 34.7 us -> 32.6 us
  local copies, waits for them, and re-layouts: 1.93 us -> 3.19 us
    ppermute x1, waiting for transfers between devices: 1.52 us -> 12.6 us  [per_device(): weight_recv = lax.ppermute(send, 'ctx', ctx_pairs(0, 1))]
    ppermute x3, waiting for transfers between devices: 0.01 us -> 11 us  [per_device(): attn.append(lax.ppermute(held, axes, pairs) if step or side else held)]
    all_to_all x2 -> x1, waiting for transfers between devices: 9.91 us -> 0.01 us  [per_device(): lax.all_to_all(parts, 'ctx', split_axis=0, concat_axis=0, tiled=True)]
    ppermute x3, waiting for transfers between devices: 0.01 us -> 5.02 us  [per_device(): lax.ppermute(weight_sums[step], 'ctx', ctx_pairs(step, 0))]
    ppermute x6, waiting for transfers between devices: 2.95 us -> 6.81 us  [per_device(): lax.ppermute(kv_recv if side else kv_mine, 'ctx', ctx_pairs(step, 0))]
    pallas_call x9 -> x8, Pallas kernels: 36.8 us -> 33.1 us  [placed(): return run(*args)]
    ppermute x1, waiting for transfers between devices: 3.06 us -> 0.01 us  [per_device(): lax.ppermute(grad_own, 'tp', shift_pairs(tp_count, -step))]
    ppermute x1, starting transfers between devices: 0.79 us -> 2.55 us  [per_device(): dq_recv = lax.ppermute(dq_theirs, 'ctx', ctx_pairs(0, 1))]
  transfers between devices with their start and end apart: 21 -> 19, of which waited for: 6 -> 7; matrix products, arithmetic and copies ran while one was open for 2% -> 2% of each run, Pallas kernels for 38% -> 30%
where the time goes in v12:
time: 109 us
  waiting for transfers between devices  37.2 us (34%)
  Pallas kernels  33.1 us (30%)
  starting transfers between devices  32.6 us (30%)
  local copies, waits for them, and re-layouts  3.19 us (3%)
  other arithmetic  1.82 us (2%)
    pallas_call x8, Pallas kernels, placed(): return run(*args)  33.1 us
    ppermute x1, waiting for transfers between devices, per_device(): weight_recv = lax.ppermute(send, 'ctx', ctx_pairs(0, 1))  12.6 us
    ppermute x3, waiting for transfers between devices, per_device(): attn.append(lax.ppermute(held, axes, pairs) if step or side else held)  11 us
    ppermute x6, starting transfers between devices, per_device(): lax.ppermute(kv_recv if side else kv_mine, 'ctx', ctx_pairs(step, 0))  8.56 us
    all_to_all x1, starting transfers between devices, per_device(): lax.all_to_all(parts, 'ctx', split_axis=0, concat_axis=0, tiled=True)  8.39 us
    ppermute x6, waiting for transfers between devices, per_device(): lax.ppermute(kv_recv if side else kv_mine, 'ctx', ctx_pairs(step, 0))  6.81 us
    ppermute x3, waiting for transfers between devices, per_device(): lax.ppermute(weight_sums[step], 'ctx', ctx_pairs(step, 0))  5.02 us
    ppermute x3, starting transfers between devices, per_device(): lax.ppermute(weight_sums[step], 'ctx', ctx_pairs(step, 0))  4.07 us
  transfers between devices with their start and end apart: 19, of which 7 were waited for; matrix products, arithmetic and copies ran while one was open for 2% of the time, Pallas kernels for 30%

profile of v12, /device:TPU:0, one launch (start us, length us, event | category | flops | bytes accessed | tf_op | source)
XLA Modules:
  0.0 108.6 jit_solution(559884615544214962)
XLA Ops:
  0.6 3.0 %collective-permute-start.4 = (bf16[256,2048]{1,0:T(8,128)(2,1)}, bf16[256,2048]{1,0:T(8,128)(2,1)}, u32[]{:S(2)}, u32[]{:S(2)}) collective-permute-start(bf16[256,2048]{1,0:T(8,128)(2,1)} %bitcast.21), channel_id=1, source_target_pairs={{0,1},{1,0},{2,3},{3,2},{4,5},{5,4},{6,7},{7,6},{8,9},{9,8},{10,11... | collective-permute-start | bytes 3145736 | tf_op jit(solution)/shard_map/ppermute | solution.py:570
  3.7 0.6 stack.59.refs_0_.refs_4_.refs_1_
  4.2 2.3 %part_heads.1 = (bf16[256,256]{1,0:T(8,128)(2,1)}, bf16[256,256]{1,0:T(8,128)(2,1)}) custom-call(s32[14]{0:T(128)} %stack.59.refs_0_.refs_4_.refs_1_, bf16[256,256]{1,0:T(8,128)(2,1)} %bitcast.26, bf16[256,256]{1,0:T(8,128)(2,1)} %bitcast.27), custom_call_target="tpu_custom_call" | custom-call | flops 2000000000 | bytes 6000000 | tf_op jit(solution)/shard_map/part_heads/pallas_call | solution.py:56
  6.6 1.6 %collective-permute-start = (bf16[256,256]{1,0:T(8,128)(2,1)}, bf16[256,256]{1,0:T(8,128)(2,1)}, u32[]{:S(2)}, u32[]{:S(2)}) collective-permute-start(bf16[256,256]{1,0:T(8,128)(2,1)} %get-tuple-element.28), channel_id=1, source_target_pairs={{0,2},{2,0},{4,6},{6,4},{8,10},{10,8},{12,14},{14,12},{1,3},{3,1},... | collective-permute-start | bytes 393224 | tf_op jit(solution)/shard_map/ppermute | solution.py:573
  8.1 3.6 %collective-permute-start.3 = (bf16[256,256]{1,0:T(8,128)(2,1)}, bf16[256,256]{1,0:T(8,128)(2,1)}, u32[]{:S(2)}, u32[]{:S(2)}) collective-permute-start(bf16[256,256]{1,0:T(8,128)(2,1)} %get-tuple-element.29.refs_6_), channel_id=1, source_target_pairs={{0,12},{2,14},{4,0},{6,2},{8,4},{10,6},{12,8},{14,10},{1,13},{3,15... | collective-permute-start | bytes 393224 | tf_op jit(solution)/shard_map/ppermute | solution.py:575
  11.7 0.0 collective-permute-start.2
  11.7 1.0 collective-permute-start.1
  12.8 1.3 %copy.11.refs_5_ = s32[8,3]{1,0:T(8,128)} copy(s32[8,3]{0,1:T(4,128)} %param.12) | data formatting | bytes 192 | tf_op args[5]
  14.1 0.0 collective-permute-done.refs_0_.refs_7_
  14.1 2.8 %collective-permute-start.8 = (bf16[256,256]{1,0:T(8,128)(2,1)}, bf16[256,256]{1,0:T(8,128)(2,1)}, u32[]{:S(2)}, u32[]{:S(2)}) collective-permute-start(bf16[256,256]{1,0:T(8,128)(2,1)} %collective-permute-done.refs_0_.refs_7_), channel_id=1, source_target_pairs={{0,12},{2,14},{4,0},{6,2},{8,4},{10,6},{12,8},{14,10},{1,13},{3,15... | collective-permute-start | bytes 393224 | tf_op jit(solution)/shard_map/ppermute | solution.py:575
  16.9 0.0 collective-permute-done.3.refs_3_.refs_12_
  16.9 1.1 %collective-permute-start.7 = (bf16[256,256]{1,0:T(8,128)(2,1)}, bf16[256,256]{1,0:T(8,128)(2,1)}, u32[]{:S(2)}, u32[]{:S(2)}) collective-permute-start(bf16[256,256]{1,0:T(8,128)(2,1)} %collective-permute-done.refs_0_.refs_7_), channel_id=1, source_target_pairs={{0,8},{2,10},{4,12},{6,14},{8,0},{10,2},{12,4},{14,6},{1,9},{3,11}... | collective-permute-start | bytes 393224 | tf_op jit(solution)/shard_map/ppermute | solution.py:575
  18.0 6.8 %collective-permute-done.2.refs_2_.refs_10_ = bf16[256,256]{1,0:T(8,128)(2,1)} collective-permute-done((bf16[256,256]{1,0:T(8,128)(2,1)}, bf16[256,256]{1,0:T(8,128)(2,1)}, u32[]{:S(2)}, u32[]{:S(2)}) %collective-permute-start.2) | collective-permute-done | bytes 131104 | tf_op jit(solution)/shard_map/ppermute | solution.py:575
  24.8 0.0 collective-permute-start.6
  24.9 0.0 collective-permute-done.1.refs_1_.refs_8_
  24.9 4.3 %prelude.1 = (f32[256,256]{1,0:T(8,128)}, bf16[2048,128]{1,0:T(8,128)(2,1)}, f32[8,512]{1,0:T(8,128)}) custom-call(bf16[256,256]{1,0:T(8,128)(2,1)} %collective-permute-done.refs_0_.refs_7_, bf16[256,256]{1,0:T(8,128)(2,1)} %collective-permute-done.1.refs_1_.refs_8_, bf16[256,256]{1,0:T(8,128)(2,1)} %collective-permute-done.2.refs_2_.refs_10_, ...), custom_call_target="tpu_custom_call" | custom-call | flops 4000000000 | bytes 12000000 | tf_op jit(solution)/shard_map/prelude/pallas_call | solution.py:56
  29.2 0.0 collective-permute-done.4.refs_4_.refs_3_.refs_6_
  29.2 3.5 %grad_heads.1 = (bf16[128,256]{1,0:T(8,128)(2,1)}, bf16[2,128,256]{2,1,0:T(8,128)(2,1)}) custom-call(s32[14]{0:T(128)} %stack.59.refs_0_.refs_4_.refs_1_, f32[256,256]{1,0:T(8,128)} %get-tuple-element.30.refs_1_, bf16[256,256]{1,0:T(8,128)(2,1)} %bitcast.28, bf16[256,4096]{1,0:T(8,128)(2,1)} %refs_3_.1, ...), custom_call_target="tpu_custom_call" | custom-call | flops 3000000000 | bytes 9000000 | tf_op jit(solution)/shard_map/grad_heads/pallas_call | solution.py:56
  32.7 0.6 collective-permute-start.5
  33.3 2.9 %pick_columns.1 = bf16[256,2048]{1,0:T(8,128)(2,1)} custom-call(bf16[128,256]{1,0:T(8,128)(2,1)} %get-tuple-element.32.refs_3_.refs_0_, s32[14]{0:T(128)} %stack.59.refs_0_.refs_4_.refs_1_, bf16[256,2048]{1,0:T(8,128)(2,1)} %bitcast.23, bf16[256,2048]{1,0:T(8,128)(2,1)} %collective-permute-done.4.refs_4_.refs_3_.refs_6_), custom_call_target="tpu_custom_call" | custom-call | flops 2000000000 | bytes 6000000 | tf_op jit(solution)/shard_map/pick_columns/pallas_call | solution.py:56
  36.2 0.1 collective-permute-start.12
  36.3 0.0 collective-permute-done.8.refs_13_
  36.3 0.0 collective-permute-done.7.refs_11_
  36.3 0.0 collective-permute-done.6.refs_9_
  36.4 1.7 %collective-permute-done.5.refs_2_ = bf16[2,128,256]{2,1,0:T(8,128)(2,1)} collective-permute-done((bf16[2,128,256]{2,1,0:T(8,128)(2,1)}, bf16[2,128,256]{2,1,0:T(8,128)(2,1)}, u32[]{:S(2)}, u32[]{:S(2)}) %collective-permute-start.5) | collective-permute-done | bytes 131104 | tf_op jit(solution)/shard_map/ppermute | solution.py:584
  38.1 8.9 %attention.1 = (bf16[128,256]{1,0:T(8,128)(2,1)}, bf16[128,256]{1,0:T(8,128)(2,1)}, bf16[256,128]{1,0:T(8,128)(2,1)}, bf16[256,128]{1,0:T(8,128)(2,1)}, bf16[8,256,256]{2,1,0:T(8,128)(2,1)}) custom-call(s32[14]{0:T(128)} %stack.59.refs_0_.refs_4_.refs_1_, bf16[256,256]{1,0:T(8,128)(2,1)} %bitcast.29, bf16[2,128,256]{2,1,0:T(8,128)(2,1)} %collective-permute-done.5.refs_2_, ...), custom_call_target="tpu_custom_call" | custom-call | flops 20000000000 | bytes 60000000 | tf_op jit(solution)/shard_map/attention/pallas_call | solution.py:56
  46.9 0.0 copy-start.3
  47.0 0.0 copy-start
  47.0 8.4 %all-to-all-start = ((bf16[8,256,256]{2,1,0:T(8,128)(2,1)}), bf16[8,256,256]{2,1,0:T(8,128)(2,1)}, u32[]{:S(2)}, u32[]{:S(2)}) async-start(bf16[8,256,256]{2,1,0:T(8,128)(2,1)} %get-tuple-element.40), calls=%async_computation | async-start | bytes 2097152 | tf_op jit(solution)/shard_map/all_to_all | solution.py:597
  55.4 0.0 copy-done.3
  55.4 0.8 collective-permute-start.11
  56.1 1.3 %collective-permute-start.9 = (bf16[128,256]{1,0:T(8,128)(2,1)S(1)}, bf16[128,256]{1,0:T(8,128)(2,1)S(1)}, u32[]{:S(2)}, u32[]{:S(2)}) collective-permute-start(bf16[128,256]{1,0:T(8,128)(2,1)S(1)} %copy-done.3), channel_id=1, source_target_pairs={{0,2},{2,0},{4,6},{6,4},{8,10},{10,8},{12,14},{14,12},{1,3},{3,1},... | collective-permute-start | bytes 196616 | tf_op jit(solution)/shard_map/ppermute | solution.py:604
  57.5 0.0 copy-done
  57.5 0.0 collective-permute-start.10
  57.5 9.1 %collective-permute-done.11.refs_4_ = bf16[128,256]{1,0:T(8,128)(2,1)S(1)} collective-permute-done((bf16[128,256]{1,0:T(8,128)(2,1)S(1)}, bf16[128,256]{1,0:T(8,128)(2,1)S(1)}, u32[]{:S(2)}, u32[]{:S(2)}) %collective-permute-start.11) | collective-permute-done | bytes 65568 | tf_op jit(solution)/shard_map/ppermute | solution.py:604
  66.6 0.0 copy-start.1
  66.6 1.9 %collective-permute-done.9.refs_2_ = bf16[128,256]{1,0:T(8,128)(2,1)S(1)} collective-permute-done((bf16[128,256]{1,0:T(8,128)(2,1)S(1)}, bf16[128,256]{1,0:T(8,128)(2,1)S(1)}, u32[]{:S(2)}, u32[]{:S(2)}) %collective-permute-start.9) | collective-permute-done | bytes 65568 | tf_op jit(solution)/shard_map/ppermute | solution.py:604
  68.5 0.0 copy-start.2
  68.5 0.0 collective-permute-done.10.refs_3_
  68.5 0.0 copy-done.1
  68.5 0.6 copy-done.2
  69.1 0.0 copy-start.4
  69.1 0.6 copy-done.4
  69.8 0.0 collective-permute-done.12.refs_7_
  69.8 3.9 %weight_sent.1 = bf16[4,256,256]{2,1,0:T(8,128)(2,1)} custom-call(s32[14]{0:T(128)} %stack.59.refs_0_.refs_4_.refs_1_, bf16[128,256]{1,0:T(8,128)(2,1)} %get-tuple-element.36.refs_1_, bf16[128,256]{1,0:T(8,128)(2,1)} %copy-done.2, bf16[128,256]{1,0:T(8,128)(2,1)} %copy-done.4, bf16[128,256]{1,0:T(8,128)(2,1)} %copy-done.1, bf16[256,2048]{1,0:T(8,128)(2,1)} %bitcast.24, ...), custom_call_target="tpu_custom_call" | custom-call | flops 4000000000 | bytes 12000000 | tf_op jit(solution)/shard_map/weight_sent/pallas_call | solution.py:56
  73.7 1.6 %collective-permute-start.13 = (bf16[4,256,256]{2,1,0:T(8,128)(2,1)}, bf16[4,256,256]{2,1,0:T(8,128)(2,1)}, u32[]{:S(2)}, u32[]{:S(2)}) collective-permute-start(bf16[4,256,256]{2,1,0:T(8,128)(2,1)} %weight_sent.1), channel_id=1, source_target_pairs={{0,2},{2,0},{4,6},{6,4},{8,10},{10,8},{12,14},{14,12},{1,3},{3,1},... | collective-permute-start | bytes 1572872 | tf_op jit(solution)/shard_map/ppermute | solution.py:607
  75.4 12.6 %collective-permute-done.13.refs_8_ = bf16[4,256,256]{2,1,0:T(8,128)(2,1)} collective-permute-done((bf16[4,256,256]{2,1,0:T(8,128)(2,1)}, bf16[4,256,256]{2,1,0:T(8,128)(2,1)}, u32[]{:S(2)}, u32[]{:S(2)}) %collective-permute-start.13) | collective-permute-done | bytes 524320 | tf_op jit(solution)/shard_map/ppermute | solution.py:607
  87.9 4.3 %weight_kept.1 = (bf16[256,256]{1,0:T(8,128)(2,1)}, bf16[256,256]{1,0:T(8,128)(2,1)}, bf16[256,256]{1,0:T(8,128)(2,1)}, bf16[256,256]{1,0:T(8,128)(2,1)}, bf16[256,128]{1,0:T(8,128)(2,1)}) custom-call(s32[14]{0:T(128)} %stack.59.refs_0_.refs_4_.refs_1_, bf16[128,256]{1,0:T(8,128)(2,1)} %get-tuple-element.36.refs_1_, bf16[128,256]{1,0:T(8,128)(2,1)} %copy-done.2, ...), custom_call_target="tpu_custom_call" | custom-call | flops 4000000000 | bytes 12000000 | tf_op jit(solution)/shard_map/weight_kept/pallas_call | solution.py:56
  92.2 2.5 %collective-permute-start.14 = (bf16[256,128]{1,0:T(8,128)(2,1)}, bf16[256,128]{1,0:T(8,128)(2,1)}, u32[]{:S(2)}, u32[]{:S(2)}) collective-permute-start(bf16[256,128]{1,0:T(8,128)(2,1)} %get-tuple-element.39), channel_id=1, source_target_pairs={{0,2},{2,0},{4,6},{6,4},{8,10},{10,8},{12,14},{14,12},{1,3},{3,1},... | collective-permute-start | bytes 196616 | tf_op jit(solution)/shard_map/ppermute | solution.py:614
  94.8 0.0 collective-permute-start.15
  94.8 2.3 %collective-permute-start.16 = (bf16[256,256]{1,0:T(8,128)(2,1)}, bf16[256,256]{1,0:T(8,128)(2,1)}, u32[]{:S(2)}, u32[]{:S(2)}) collective-permute-start(bf16[256,256]{1,0:T(8,128)(2,1)} %get-tuple-element.43), channel_id=1, source_target_pairs={{0,8},{2,10},{4,12},{6,14},{8,0},{10,2},{12,4},{14,6},{1,9},{3,11}... | collective-permute-start | bytes 393224 | tf_op jit(solution)/shard_map/ppermute | solution.py:612
  97.0 1.8 %collective-permute-start.17 = (bf16[256,256]{1,0:T(8,128)(2,1)}, bf16[256,256]{1,0:T(8,128)(2,1)}, u32[]{:S(2)}, u32[]{:S(2)}) collective-permute-start(bf16[256,256]{1,0:T(8,128)(2,1)} %get-tuple-element.44), channel_id=1, source_target_pairs={{0,12},{2,14},{4,0},{6,2},{8,4},{10,6},{12,8},{14,10},{1,13},{3,15... | collective-permute-start | bytes 393224 | tf_op jit(solution)/shard_map/ppermute | solution.py:612
  98.8 0.0 collective-permute-done.14.refs_2_
  98.8 0.0 all-to-all-done.refs_3_
  98.8 2.9 %collect.1 = (bf16[256,256]{1,0:T(8,128)(2,1)}, bf16[256,256]{1,0:T(8,128)(2,1)}, bf16[256,256]{1,0:T(8,128)(2,1)}) custom-call(s32[14]{0:T(128)} %stack.59.refs_0_.refs_4_.refs_1_, bf16[256,128]{1,0:T(8,128)(2,1)} %get-tuple-element.35.refs_1_, bf16[256,128]{1,0:T(8,128)(2,1)} %collective-permute-done.14.refs_2_, bf16[8,256,256]{2,1,0:T(8,128)(2,1)} %all-to-all-done.refs_3_), custom_call_target="tpu_custom_call" | custom-call | flops 3000000000 | bytes 9000000 | tf_op jit(solution)/shard_map/collect/pallas_call | solution.py:56
  101.8 1.6 %collective-permute-done.15 = bf16[256,256]{1,0:T(8,128)(2,1)} collective-permute-done((bf16[256,256]{1,0:T(8,128)(2,1)}, bf16[256,256]{1,0:T(8,128)(2,1)}, u32[]{:S(2)}, u32[]{:S(2)}) %collective-permute-start.15) | collective-permute-done | bytes 131104 | tf_op jit(solution)/shard_map/ppermute | solution.py:612
  103.3 3.4 %collective-permute-done.16 = bf16[256,256]{1,0:T(8,128)(2,1)} collective-permute-done((bf16[256,256]{1,0:T(8,128)(2,1)}, bf16[256,256]{1,0:T(8,128)(2,1)}, u32[]{:S(2)}, u32[]{:S(2)}) %collective-permute-start.16) | collective-permute-done | bytes 131104 | tf_op jit(solution)/shard_map/ppermute | solution.py:612
  106.8 0.0 collective-permute-done.17
  106.8 1.8 %add_convert_fusion = bf16[256,256]{1,0:T(8,128)(2,1)} fusion(bf16[256,256]{1,0:T(8,128)(2,1)} %collective-permute-done.17, bf16[256,256]{1,0:T(8,128)(2,1)} %collective-permute-done.16, bf16[256,256]{1,0:T(8,128)(2,1)} %collective-permute-done.15, bf16[256,256]{1,0:T(8,128)(2,1)} %get-tuple-element.48), kind=kLoop, calls=%fused_computation | loop fusion | flops 524288 | bytes 655360 | tf_op jit(solution)/shard_map/convert_element_type | solution.py:621
Async XLA Ops:
  0.6 28.6 %collective-permute-start.4 = (bf16[256,2048]{1,0:T(8,128)(2,1)}, bf16[256,2048]{1,0:T(8,128)(2,1)}, u32[]{:S(2)}, u32[]{:S(2)}) collective-permute-start(bf16[256,2048]{1,0:T(8,128)(2,1)} %bitcast.21), channel_id=1, source_target_pairs={{0,1},{1,0},{2,3},{3,2},{4,5},{5,4},{6,7},{7,6},{8,9},{9,8},{10,11... | collective-permute-start | bytes 3145736 | tf_op jit(solution)/shard_map/ppermute | solution.py:570
  6.6 7.5 %collective-permute-start = (bf16[256,256]{1,0:T(8,128)(2,1)}, bf16[256,256]{1,0:T(8,128)(2,1)}, u32[]{:S(2)}, u32[]{:S(2)}) collective-permute-start(bf16[256,256]{1,0:T(8,128)(2,1)} %get-tuple-element.28), channel_id=1, source_target_pairs={{0,2},{2,0},{4,6},{6,4},{8,10},{10,8},{12,14},{14,12},{1,3},{3,1},... | collective-permute-start | bytes 393224 | tf_op jit(solution)/shard_map/ppermute | solution.py:573
  8.1 8.8 %collective-permute-start.3 = (bf16[256,256]{1,0:T(8,128)(2,1)}, bf16[256,256]{1,0:T(8,128)(2,1)}, u32[]{:S(2)}, u32[]{:S(2)}) collective-permute-start(bf16[256,256]{1,0:T(8,128)(2,1)} %get-tuple-element.29.refs_6_), channel_id=1, source_target_pairs={{0,12},{2,14},{4,0},{6,2},{8,4},{10,6},{12,8},{14,10},{1,13},{3,15... | collective-permute-start | bytes 393224 | tf_op jit(solution)/shard_map/ppermute | solution.py:575
  11.7 13.1 %collective-permute-start.2 = (bf16[256,256]{1,0:T(8,128)(2,1)}, bf16[256,256]{1,0:T(8,128)(2,1)}, u32[]{:S(2)}, u32[]{:S(2)}) collective-permute-start(bf16[256,256]{1,0:T(8,128)(2,1)} %get-tuple-element.29.refs_6_), channel_id=1, source_target_pairs={{0,8},{2,10},{4,12},{6,14},{8,0},{10,2},{12,4},{14,6},{1,9},{3,11}... | collective-permute-start | bytes 393224 | tf_op jit(solution)/shard_map/ppermute | solution.py:575
  11.7 13.1 %collective-permute-start.1 = (bf16[256,256]{1,0:T(8,128)(2,1)}, bf16[256,256]{1,0:T(8,128)(2,1)}, u32[]{:S(2)}, u32[]{:S(2)}) collective-permute-start(bf16[256,256]{1,0:T(8,128)(2,1)} %get-tuple-element.29.refs_6_), channel_id=1, source_target_pairs={{0,4},{2,6},{4,8},{6,10},{8,12},{10,14},{12,0},{14,2},{1,5},{3,7},... | collective-permute-start | bytes 393224 | tf_op jit(solution)/shard_map/ppermute | solution.py:575
  14.1 22.2 %collective-permute-start.8 = (bf16[256,256]{1,0:T(8,128)(2,1)}, bf16[256,256]{1,0:T(8,128)(2,1)}, u32[]{:S(2)}, u32[]{:S(2)}) collective-permute-start(bf16[256,256]{1,0:T(8,128)(2,1)} %collective-permute-done.refs_0_.refs_7_), channel_id=1, source_target_pairs={{0,12},{2,14},{4,0},{6,2},{8,4},{10,6},{12,8},{14,10},{1,13},{3,15... | collective-permute-start | bytes 393224 | tf_op jit(solution)/shard_map/ppermute | solution.py:575
  16.9 19.4 %collective-permute-start.7 = (bf16[256,256]{1,0:T(8,128)(2,1)}, bf16[256,256]{1,0:T(8,128)(2,1)}, u32[]{:S(2)}, u32[]{:S(2)}) collective-permute-start(bf16[256,256]{1,0:T(8,128)(2,1)} %collective-permute-done.refs_0_.refs_7_), channel_id=1, source_target_pairs={{0,8},{2,10},{4,12},{6,14},{8,0},{10,2},{12,4},{14,6},{1,9},{3,11}... | collective-permute-start | bytes 393224 | tf_op jit(solution)/shard_map/ppermute | solution.py:575
  24.8 11.5 %collective-permute-start.6 = (bf16[256,256]{1,0:T(8,128)(2,1)}, bf16[256,256]{1,0:T(8,128)(2,1)}, u32[]{:S(2)}, u32[]{:S(2)}) collective-permute-start(bf16[256,256]{1,0:T(8,128)(2,1)} %collective-permute-done.refs_0_.refs_7_), channel_id=1, source_target_pairs={{0,4},{2,6},{4,8},{6,10},{8,12},{10,14},{12,0},{14,2},{1,5},{3,7},... | collective-permute-start | bytes 393224 | tf_op jit(solution)/shard_map/ppermute | solution.py:575
  32.7 5.3 %collective-permute-start.5 = (bf16[2,128,256]{2,1,0:T(8,128)(2,1)}, bf16[2,128,256]{2,1,0:T(8,128)(2,1)}, u32[]{:S(2)}, u32[]{:S(2)}) collective-permute-start(bf16[2,128,256]{2,1,0:T(8,128)(2,1)} %get-tuple-element.31), channel_id=1, source_target_pairs={{0,2},{2,0},{4,6},{6,4},{8,10},{10,8},{12,14},{14,12},{1,3},{3,1},... | collective-permute-start | bytes 393224 | tf_op jit(solution)/shard_map/ppermute | solution.py:584
  36.2 33.5 %collective-permute-start.12 = (bf16[256,2048]{1,0:T(8,128)(2,1)}, bf16[256,2048]{1,0:T(8,128)(2,1)}, u32[]{:S(2)}, u32[]{:S(2)}) collective-permute-start(bf16[256,2048]{1,0:T(8,128)(2,1)} %pick_columns.1), channel_id=1, source_target_pairs={{0,16},{16,0},{1,17},{17,1},{2,18},{18,2},{3,19},{19,3},{4,20},{20... | collective-permute-start | bytes 3145736 | tf_op jit(solution)/shard_map/ppermute | solution.py:590
  46.9 8.4 %copy-start.3 = (bf16[128,256]{1,0:T(8,128)(2,1)S(1)}, bf16[128,256]{1,0:T(8,128)(2,1)}, u32[]{:S(2)}) copy-start(bf16[128,256]{1,0:T(8,128)(2,1)} %get-tuple-element.37) | copy-start | bytes 196612
  47.0 10.5 %copy-start = (bf16[128,256]{1,0:T(8,128)(2,1)S(1)}, bf16[128,256]{1,0:T(8,128)(2,1)}, u32[]{:S(2)}) copy-start(bf16[128,256]{1,0:T(8,128)(2,1)} %get-tuple-element.36.refs_1_) | copy-start | bytes 196612
  47.0 51.9 %all-to-all-start = ((bf16[8,256,256]{2,1,0:T(8,128)(2,1)}), bf16[8,256,256]{2,1,0:T(8,128)(2,1)}, u32[]{:S(2)}, u32[]{:S(2)}) async-start(bf16[8,256,256]{2,1,0:T(8,128)(2,1)} %get-tuple-element.40), calls=%async_computation | async-start | bytes 2097152 | tf_op jit(solution)/shard_map/all_to_all | solution.py:597
  55.4 11.3 %collective-permute-start.11 = (bf16[128,256]{1,0:T(8,128)(2,1)S(1)}, bf16[128,256]{1,0:T(8,128)(2,1)S(1)}, u32[]{:S(2)}, u32[]{:S(2)}) collective-permute-start(bf16[128,256]{1,0:T(8,128)(2,1)S(1)} %copy-done.3), channel_id=1, source_target_pairs={{0,18},{2,16},{4,22},{6,20},{8,26},{10,24},{12,30},{14,28},{16,2},... | collective-permute-start | bytes 196616 | tf_op jit(solution)/shard_map/ppermute | solution.py:604
  56.1 12.4 %collective-permute-start.9 = (bf16[128,256]{1,0:T(8,128)(2,1)S(1)}, bf16[128,256]{1,0:T(8,128)(2,1)S(1)}, u32[]{:S(2)}, u32[]{:S(2)}) collective-permute-start(bf16[128,256]{1,0:T(8,128)(2,1)S(1)} %copy-done.3), channel_id=1, source_target_pairs={{0,2},{2,0},{4,6},{6,4},{8,10},{10,8},{12,14},{14,12},{1,3},{3,1},... | collective-permute-start | bytes 196616 | tf_op jit(solution)/shard_map/ppermute | solution.py:604
  57.5 11.1 %collective-permute-start.10 = (bf16[128,256]{1,0:T(8,128)(2,1)S(1)}, bf16[128,256]{1,0:T(8,128)(2,1)S(1)}, u32[]{:S(2)}, u32[]{:S(2)}) collective-permute-start(bf16[128,256]{1,0:T(8,128)(2,1)S(1)} %copy-done), channel_id=1, source_target_pairs={{0,16},{2,18},{4,20},{6,22},{8,24},{10,26},{12,28},{14,30},{16,0},... | collective-permute-start | bytes 196616 | tf_op jit(solution)/shard_map/ppermute | solution.py:604
  66.6 1.9 %copy-start.1 = (bf16[128,256]{1,0:T(8,128)(2,1)}, bf16[128,256]{1,0:T(8,128)(2,1)S(1)}, u32[]{:S(2)}) copy-start(bf16[128,256]{1,0:T(8,128)(2,1)S(1)} %collective-permute-done.11.refs_4_) | copy-start | bytes 196612
  68.5 0.6 copy-start.2
  69.1 0.6 copy-start.4
  73.7 14.2 %collective-permute-start.13 = (bf16[4,256,256]{2,1,0:T(8,128)(2,1)}, bf16[4,256,256]{2,1,0:T(8,128)(2,1)}, u32[]{:S(2)}, u32[]{:S(2)}) collective-permute-start(bf16[4,256,256]{2,1,0:T(8,128)(2,1)} %weight_sent.1), channel_id=1, source_target_pairs={{0,2},{2,0},{4,6},{6,4},{8,10},{10,8},{12,14},{14,12},{1,3},{3,1},... | collective-permute-start | bytes 1572872 | tf_op jit(solution)/shard_map/ppermute | solution.py:607
  92.2 6.6 %collective-permute-start.14 = (bf16[256,128]{1,0:T(8,128)(2,1)}, bf16[256,128]{1,0:T(8,128)(2,1)}, u32[]{:S(2)}, u32[]{:S(2)}) collective-permute-start(bf16[256,128]{1,0:T(8,128)(2,1)} %get-tuple-element.39), channel_id=1, source_target_pairs={{0,2},{2,0},{4,6},{6,4},{8,10},{10,8},{12,14},{14,12},{1,3},{3,1},... | collective-permute-start | bytes 196616 | tf_op jit(solution)/shard_map/ppermute | solution.py:614
  94.8 8.6 %collective-permute-start.15 = (bf16[256,256]{1,0:T(8,128)(2,1)}, bf16[256,256]{1,0:T(8,128)(2,1)}, u32[]{:S(2)}, u32[]{:S(2)}) collective-permute-start(bf16[256,256]{1,0:T(8,128)(2,1)} %get-tuple-element.42), channel_id=1, source_target_pairs={{0,4},{2,6},{4,8},{6,10},{8,12},{10,14},{12,0},{14,2},{1,5},{3,7},... | collective-permute-start | bytes 393224 | tf_op jit(solution)/shard_map/ppermute | solution.py:612
  94.8 12.0 %collective-permute-start.16 = (bf16[256,256]{1,0:T(8,128)(2,1)}, bf16[256,256]{1,0:T(8,128)(2,1)}, u32[]{:S(2)}, u32[]{:S(2)}) collective-permute-start(bf16[256,256]{1,0:T(8,128)(2,1)} %get-tuple-element.43), channel_id=1, source_target_pairs={{0,8},{2,10},{4,12},{6,14},{8,0},{10,2},{12,4},{14,6},{1,9},{3,11}... | collective-permute-start | bytes 393224 | tf_op jit(solution)/shard_map/ppermute | solution.py:612
  97.0 9.8 %collective-permute-start.17 = (bf16[256,256]{1,0:T(8,128)(2,1)}, bf16[256,256]{1,0:T(8,128)(2,1)}, u32[]{:S(2)}, u32[]{:S(2)}) collective-permute-start(bf16[256,256]{1,0:T(8,128)(2,1)} %get-tuple-element.44), channel_id=1, source_target_pairs={{0,12},{2,14},{4,0},{6,2},{8,4},{10,6},{12,8},{14,10},{1,13},{3,15... | collective-permute-start | bytes 393224 | tf_op jit(solution)/shard_map/ppermute | solution.py:612

commit v13 on v12

--- a/solution.py
+++ b/solution.py
@@ -176,9 +176,11 @@
 
 def attention_kernel(block_count, head_count, at_ref, q_ref, recv_ref, g_mine, key_mask, row_mask, *refs):
     kv_refs, refs = refs[:block_count], refs[block_count:]
-    attn_mine, attn_theirs, dq_mine, dq_theirs, part_out = refs[:5]
-    q_s, recv_s, g_s, mask_s, row_s, kv_s, e_s, s_ref, attn_s, dq_s, part_s = refs[5:16]
-    sem, kv_sem, out_sem, part_sem = refs[16:]
+    outer = block_count // INNER
+    attn_mine, attn_theirs, dq_mine, dq_theirs = refs[:4]
+    part_outs, refs = refs[4 : 4 + outer], refs[4 + outer :]
+    q_s, recv_s, g_s, mask_s, row_s, kv_s, e_s, s_ref, attn_s, dq_s, part_s = refs[:11]
+    sem, kv_sem, out_sem, part_sem = refs[11:]
     rows = q_ref.shape[0]
     feats = head_count * HD
     score_scale = HD ** (-0.5)
@@ -241,7 +243,7 @@
             part_s[j, :, cols] = (score_scale * product(dscore, query)).astype(jnp.bfloat16)
             part_s[j, :, vcols] = product(low, grad).astype(jnp.bfloat16)
             if head == head_count - 1:
-                target = part_out.at[at_ref[SOURCES + j]]
+                target = part_outs[j // INNER].at[j % INNER]
                 stores.append(begin(part_s.at[j], target, part_sem.at[j]))
         dquery = (score_scale * jnp.transpose(dq_t)).astype(jnp.bfloat16)
         dq_s[0, :, cols] = dquery[:rows]
@@ -257,11 +259,12 @@
     feats, rows = g_mine.shape
     heads = feats // HD
     keys = block_count * rows
-    return call(
+    outer = block_count // INNER
+    out = call(
         functools.partial(attention_kernel, block_count, heads),
-        [bf16(feats, rows)] * 2 + [bf16(rows, feats)] * 2 + [bf16(block_count, rows, 2 * feats)],
+        [bf16(feats, rows)] * 2 + [bf16(rows, feats)] * 2 + [bf16(INNER, rows, 2 * feats)] * outer,
         [SMEM] + [ANY] * (5 + block_count),
-        [ANY] * 5,
+        [ANY] * (4 + outer),
         [
             pltpu.VMEM((rows, feats), jnp.bfloat16),
             pltpu.VMEM((2, feats, rows), jnp.bfloat16),
@@ -282,6 +285,7 @@
         20,
         "attention",
     )(at, queries, recv, g_mine, key_mask, row_mask, *kv_blocks)
+    return *out[:4], out[4:]
 
 
 def grad_heads_kernel(part_count, place, at_ref, first_ref, q_ref, weight_ref, *refs):
@@ -344,63 +348,60 @@
     )(at, first, queries, out_weight, *grads[1:])
 
 
-def pick_kernel(part_count, place, at_ref, *refs):
-    grads, (out, held_s, sem, out_sem) = refs[:part_count], refs[part_count:]
-    width = grads[0].shape[1]
-    picked = out.shape[1] // width
-    for i in range(picked):
-        for k in range(part_count):
-
-            @pl.when(at_ref[place + i] == k)
-            def _():
-                begin(grads[k], held_s.at[i], sem.at[i])
-
+def pick_kernel(part_count, picked, places, at_ref, *refs):
+    grads, refs = refs[:part_count], refs[part_count:]
+    outs, (held_s, sem, out_sem) = refs[: len(places)], refs[len(places) :]
+    _, outer, _, block = outs[0].shape
+    pieces = grads[0].shape[1] // block
+    loads = [begin(grads[k], held_s.at[k], sem.at[k]) for k in range(part_count)]
+    for load in loads:
+        load.wait()
     stores = []
-    for i in range(picked):
-        pltpu.make_async_copy(grads[0], held_s.at[i], sem.at[i]).wait()
-        target = out.at[:, i * width : (i + 1) * width]
-        stores.append(begin(held_s.at[i], target, out_sem.at[i]))
+    for index, steps_at in enumerate(places):
+        for side in range(INNER):
+            here = (1 - at_ref[0]) if side else at_ref[0]
+            for k in range(outer):
+                place = lax.rem(at_ref[1] + k, outer) * INNER + here
+                cols = pl.ds(pl.multiple_of(lax.rem(place, pieces) * block, block), block)
+                source = held_s.at[at_ref[steps_at + place // pieces], :, cols]
+                order = (index * INNER + side) * outer + k
+                stores.append(begin(source, outs[index].at[side, k], out_sem.at[order]))
     for store in stores:
         store.wait()
 
 
-def pick_columns(at, place, grads, picked, after):
+def pick_columns(at, places, grads, outer, picked, after):
     rows, width = grads[0].shape
+    block = picked * width // (outer * INNER)
     return call(
-        functools.partial(pick_kernel, len(grads), place),
-        bf16(rows, picked * width),
+        functools.partial(pick_kernel, len(grads), picked, places),
+        [bf16(INNER, outer, rows, block)] * len(places),
         [SMEM] + [ANY] * len(grads),
-        ANY,
-        [
-            pltpu.VMEM((picked, rows, width), jnp.bfloat16),
-            pltpu.SemaphoreType.DMA((picked,)),
-            pltpu.SemaphoreType.DMA((picked,)),
-        ],
-        2,
+        [ANY] * len(places),
+        [
+            pltpu.VMEM((len(grads), rows, width), jnp.bfloat16),
+            pltpu.SemaphoreType.DMA((len(grads),)),
+            pltpu.SemaphoreType.DMA((len(places) * INNER * outer,)),
+        ],
+        3,
         "pick_columns",
         after,
     )(at, *grads)
 
 
-def weight_kernel(part_count, doc_count, sent, step_at, at_ref, *refs):
+def weight_kernel(doc_count, sent, at_ref, *refs):
     attn, refs = refs[: INNER * doc_count], refs[INNER * doc_count :]
-    grads, refs = refs[:part_count], refs[part_count:]
-    swapped, refs = refs[: doc_count - 1], refs[doc_count - 1 :]
+    grads, refs = refs[:doc_count], refs[doc_count:]
     if sent:
         out, refs = refs[0], refs[1:]
         outs = [out.at[k] for k in range(out.shape[0])]
     else:
-        recv, passed, refs = refs[0], refs[1], refs[2:]
+        recv, refs = refs[0], refs[1:]
         outs, refs = refs[: recv.shape[0]], refs[recv.shape[0] :]
-        passed_out, recv_s, passed_s, recv_sem, passed_sem = refs[:5]
-        refs = refs[5:]
-        passed_load = begin(passed, passed_s, passed_sem)
+        recv_s, recv_sem, refs = refs[0], refs[1], refs[2:]
     attn_s, grad_s, out_s, attn_sem, grad_sem, out_sem = refs
-    outer, feats, width = out_s.shape
+    outer, feats, _ = out_s.shape
     half = feats // INNER
-    piece = grads[0].shape[1]
-    pieces = piece // width
-    here = (1 - at_ref[0]) if sent else at_ref[0]
     attn_loads, grad_loads = [], []
     for doc in range(doc_count):
         for side in range(INNER):
@@ -409,29 +410,16 @@
             target = attn_s.at[doc, pl.ds(pl.multiple_of(at * half, half), half)]
             attn_loads.append(begin(attn[index], target, attn_sem.at[index]))
     for k in range(outer):
-        place = lax.rem(at_ref[1] + k, outer) * INNER + here
-        which = at_ref[step_at + place // pieces]
-        cols = pl.ds(pl.multiple_of(lax.rem(place, pieces) * width, width), width)
-        for i in range(part_count):
-
-            @pl.when(which == i)
-            def _():
-                begin(grads[i].at[:, cols], grad_s.at[0, k], grad_sem.at[k])
-
-        loads = [pltpu.make_async_copy(grads[0].at[:, cols], grad_s.at[0, k], grad_sem.at[k])]
-        cols = pl.ds(pl.multiple_of(place * width, width), width)
-        for doc in range(1, doc_count):
-            source = swapped[doc - 1].at[:, cols]
-            loads.append(begin(source, grad_s.at[doc, k], grad_sem.at[doc * outer + k]))
+        loads = [
+            begin(grads[doc].at[int(sent), k], grad_s.at[doc, k], grad_sem.at[doc * outer + k])
+            for doc in range(doc_count)
+        ]
         if not sent:
             loads.append(begin(recv.at[k], recv_s.at[k], recv_sem.at[k]))
         grad_loads.append(loads)
     for load in attn_loads:
         load.wait()
     stores = []
-    if not sent:
-        passed_load.wait()
-        stores.append(begin(passed_s, passed_out, passed_sem))
     for k in range(outer):
         term = 0.0
         for doc in range(doc_count):
@@ -446,13 +434,13 @@
         store.wait()
 
 
-def weight_terms(at, step_at, attn, grads, swapped, outer, picked, recv=None, passed=None, after=()):
+def weight_terms(at, attn, grads, recv=None, after=()):
     half, rows = attn[0].shape
     feats = half * INNER
-    doc_count = len(attn) // INNER
-    width = picked * grads[0].shape[1] // (outer * INNER)
+    doc_count = len(grads)
+    _, outer, _, width = grads[0].shape
     sent = recv is None
-    operands = [*attn, *grads, *swapped] + ([] if sent else [recv, passed])
+    operands = [*attn, *grads] + ([] if sent else [recv])
     scratch = [
         pltpu.VMEM((doc_count, feats, rows), jnp.bfloat16),
         pltpu.VMEM((doc_count, outer, rows, width), jnp.bfloat16),
@@ -462,17 +450,13 @@
         pltpu.SemaphoreType.DMA((outer,)),
     ]
     if not sent:
-        scratch = [
-            pltpu.VMEM((outer, feats, width), jnp.bfloat16),
-            pltpu.VMEM(passed.shape, jnp.bfloat16),
-            pltpu.SemaphoreType.DMA((outer,)),
-            pltpu.SemaphoreType.DMA,
-        ] + scratch
+        added = [pltpu.VMEM((outer, feats, width), jnp.bfloat16), pltpu.SemaphoreType.DMA((outer,))]
+        scratch = added + scratch
     return call(
-        functools.partial(weight_kernel, len(grads), doc_count, sent, step_at),
-        bf16(outer, feats, width) if sent else [bf16(feats, width)] * outer + [bf16(*passed.shape)],
+        functools.partial(weight_kernel, doc_count, sent),
+        bf16(outer, feats, width) if sent else [bf16(feats, width)] * outer,
         [SMEM] + [ANY] * len(operands),
-        ANY if sent else [ANY] * (outer + 1),
+        ANY if sent else [ANY] * outer,
         scratch,
         4,
         "weight_sent" if sent else "weight_kept",
@@ -480,51 +464,96 @@
     )(at, *operands)
 
 
-def collect_kernel(at_ref, dq_mine, dq_recv, terms, *refs):
-    outs, (dq_s, terms_s, out_s, dq_sem, sem, out_sem) = refs[:3], refs[3:]
-    count, rows, both = terms.shape
+def add_kernel(count, dq_theirs, *refs):
+    terms, (mine, theirs) = refs[:count], refs[count : count + 2]
+    terms_s, mine_s, theirs_s, dq_s, term_sem, out_sem, dq_sem = refs[count + 2 :]
+    both = mine.shape[1]
+    dq_load = begin(dq_theirs, dq_s, dq_sem)
+    loads = {
+        (side, c): begin(terms[c].at[side], terms_s.at[c, side], term_sem.at[c * INNER + side])
+        for side in (1, 0)
+        for c in range(count)
+    }
+    stores = []
+    for side, (held_s, out) in ((1, (theirs_s, theirs)), (0, (mine_s, mine))):
+        summed = 0.0
+        for c in range(count):
+            loads[side, c].wait()
+            summed = summed + terms_s[c, side].astype(jnp.float32)
+        held_s[:, :both] = summed.astype(jnp.bfloat16)
+        if side:
+            dq_load.wait()
+            held_s[:, both:] = dq_s[...]
+        stores.append(begin(held_s, out, out_sem.at[side]))
+    for store in stores:
+        store.wait()
+
+
+def add_terms(dq_theirs, terms, after):
+    _, rows, both = terms[0].shape
     half = both // 2
-    loads = [begin(terms.at[c], terms_s.at[c], sem.at[c]) for c in range(count)]
-    held = [begin(dq, dq_s.at[i], dq_sem.at[i]) for i, dq in enumerate((dq_mine, dq_recv))]
-    for side, at in enumerate((at_ref[0], 1 - at_ref[0])):
-        held[side].wait()
-        out_s[0, :, pl.ds(pl.multiple_of(at * half, half), half)] = dq_s[side]
-    stores = [begin(out_s.at[0], outs[0], out_sem.at[0])]
+    count = len(terms)
+    return call(
+        functools.partial(add_kernel, count),
+        [bf16(rows, both), bf16(rows, both + half)],
+        [ANY] * (1 + count),
+        [ANY] * 2,
+        [
+            pltpu.VMEM((count, INNER, rows, both), jnp.bfloat16),
+            pltpu.VMEM((rows, both), jnp.bfloat16),
+            pltpu.VMEM((rows, both + half), jnp.bfloat16),
+            pltpu.VMEM((rows, half), jnp.bfloat16),
+            pltpu.SemaphoreType.DMA((count * INNER,)),
+            pltpu.SemaphoreType.DMA((INNER,)),
+            pltpu.SemaphoreType.DMA,
+        ],
+        2,
+        "add_terms",
+        after,
+    )(dq_theirs, *terms)
+
+
+def join_kernel(at_ref, dq_mine, mine, recv, *refs):
+    outs, (dq_s, mine_s, recv_s, out_s, sem, out_sem) = refs[:3], refs[3:]
+    half = dq_mine.shape[1]
+    loads = [
+        begin(dq_mine, dq_s, sem.at[0]),
+        begin(mine, mine_s, sem.at[1]),
+        begin(recv, recv_s, sem.at[2]),
+    ]
+    here = pl.ds(pl.multiple_of(at_ref[0] * half, half), half)
+    there = pl.ds(pl.multiple_of((1 - at_ref[0]) * half, half), half)
     for load in loads:
         load.wait()
-    for side in range(INNER):
-        summed = terms_s[side].astype(jnp.float32)
-        for c in range(side + INNER, count, INNER):
-            summed = summed + terms_s[c].astype(jnp.float32)
-        summed = summed.astype(jnp.bfloat16)
-        for kind in range(2):
-            cols = slice(side * half, (side + 1) * half)
-            out_s[1 + kind, :, cols] = summed[:, kind * half : (kind + 1) * half]
-    for index in (1, 2):
-        stores.append(begin(out_s.at[index], outs[index], out_sem.at[index]))
+    out_s[0, :, here] = dq_s[...]
+    out_s[0, :, there] = recv_s[:, 2 * half :]
+    for kind in range(2):
+        cols = slice(kind * half, (kind + 1) * half)
+        out_s[1 + kind, :, here] = mine_s[:, cols]
+        out_s[1 + kind, :, there] = recv_s[:, cols]
+    stores = [begin(out_s.at[index], out, out_sem.at[index]) for index, out in enumerate(outs)]
     for store in stores:
         store.wait()
 
 
-def collect(at, dq_mine, dq_recv, terms):
-    count, rows, both = terms.shape
-    half = both // 2
+def join_heads(at, dq_mine, mine, recv):
+    rows, half = dq_mine.shape
     return call(
-        collect_kernel,
+        join_kernel,
         [bf16(rows, INNER * half)] * 3,
         [SMEM] + [ANY] * 3,
         [ANY] * 3,
         [
-            pltpu.VMEM((INNER, rows, half), jnp.bfloat16),
-            pltpu.VMEM((count, rows, both), jnp.bfloat16),
+            pltpu.VMEM(dq_mine.shape, jnp.bfloat16),
+            pltpu.VMEM(mine.shape, jnp.bfloat16),
+            pltpu.VMEM(recv.shape, jnp.bfloat16),
             pltpu.VMEM((3, rows, INNER * half), jnp.bfloat16),
-            pltpu.SemaphoreType.DMA((INNER,)),
-            pltpu.SemaphoreType.DMA((count,)),
             pltpu.SemaphoreType.DMA((3,)),
-        ],
-        3,
-        "collect",
-    )(at, dq_mine, dq_recv, terms)
+            pltpu.SemaphoreType.DMA((3,)),
+        ],
+        2,
+        "join_heads",
+    )(at, dq_mine, mine, recv)
 
 
 def per_device(
@@ -559,11 +588,11 @@
     scalars = [inner_at, outer_at, tp_at] + sources
     columns_at = len(scalars)
     scalars = scalars + [(tp_at + step) % tp_count for step in range(1, tp_count)]
-    send_at = len(scalars)
-    for step in range(1, dp_count):
+    groups_at = []
+    for step in range(dp_count):
+        groups_at.append(len(scalars))
         scalars = scalars + dp_steps((dp_at + step) % dp_count)
-    keep_at = len(scalars)
-    at = jnp.stack(scalars + dp_steps(dp_at))
+    at = jnp.stack(scalars)
 
     grad_own = grad_output[0]
     grads = [grad_own] + [
@@ -578,23 +607,22 @@
         for step, side in routes
     ]
     first, key_mask, row_mask = prelude(
-        at, block_pattern, global_offsets, grad_own, out_weight, (kv_recv, *kv_blocks[INNER::INNER])
+        at, block_pattern, global_offsets, grad_own, out_weight, (kv_recv, kv_blocks[INNER], kv_blocks[-INNER])
     )
     g_mine, theirs = grad_heads(at, columns_at, first, queries[0], out_weight, grads)
     recv = lax.ppermute(theirs, "ctx", ctx_pairs(0, 1))
-    grad_sends = [
-        pick_columns(at, send_at + step * picked, grads, picked, (g_mine,))
-        for step in range(dp_count - 1)
-    ]
-    swapped = [
-        lax.ppermute(send, "dp", shift_pairs(dp_count, step + 1))
-        for step, send in enumerate(grad_sends)
+    kept, *sends = pick_columns(at, tuple(groups_at), grads, outer, picked, (g_mine,))
+    grad_blocks = [kept] + [
+        lax.ppermute(send, "dp", shift_pairs(dp_count, step + 1)) for step, send in enumerate(sends)
     ]
 
     attn_mine, attn_theirs, dq_mine, dq_theirs, parts = attention(
         at, queries[0], recv, g_mine, key_mask, row_mask, kv_blocks
     )
-    terms = lax.all_to_all(parts, "ctx", split_axis=0, concat_axis=0, tiled=True)
+    terms = [
+        lax.ppermute(part, "ctx", ctx_pairs(-step, 0)) if step else part
+        for step, part in enumerate(parts)
+    ]
 
     attn = []
     for step in range(dp_count):
@@ -603,17 +631,15 @@
             axes = ("dp", "ctx") if step else "ctx"
             attn.append(lax.ppermute(held, axes, pairs) if step or side else held)
 
-    send = weight_terms(at, keep_at, attn, grads, swapped, outer, picked)
+    send = weight_terms(at, attn, grad_blocks)
     weight_recv = lax.ppermute(send, "ctx", ctx_pairs(0, 1))
-    *weight_sums, dq_theirs = weight_terms(
-        at, keep_at, attn, grads, swapped, outer, picked, weight_recv, dq_theirs
-    )
+    weight_sums = weight_terms(at, attn, grad_blocks, weight_recv)
     weight_parts = [
         lax.ppermute(weight_sums[step], "ctx", ctx_pairs(step, 0)) for step in range(1, outer)
     ]
-    dq_recv = lax.ppermute(dq_theirs, "ctx", ctx_pairs(0, 1))
-    grad_q, grad_k, grad_v = collect(at, dq_mine, dq_recv, terms)
-    weight_parts, grad_k = lax.optimization_barrier((weight_parts, grad_k))
+    terms_mine, terms_theirs = add_terms(dq_theirs, terms, (weight_sums[0],))
+    terms_recv = lax.ppermute(terms_theirs, "ctx", ctx_pairs(0, 1))
+    grad_q, grad_k, grad_v = join_heads(at, dq_mine, terms_mine, terms_recv)
     grad_weight = weight_sums[0].astype(jnp.float32)
     for part in weight_parts:
         grad_weight = grad_weight + part.astype(jnp.float32)

time: 109 us -> 101 us (0.927)
  waiting for transfers between devices: 37.2 us -> 28.9 us
  Pallas kernels: 33.1 us -> 35.4 us
  starting transfers between devices: 32.6 us -> 31.3 us
  local copies, waits for them, and re-layouts: 3.19 us -> 1.96 us
    ppermute x1 -> x4, waiting for transfers between devices: 0.01 us -> 13.8 us  [the longest x3 10.5 us: per_device(): lax.ppermute(part, 'ctx', ctx_pairs(-step, 0))]
    all_to_all x1 -> x0, starting transfers between devices: 8.39 us -> none  [per_device(): lax.all_to_all(parts, 'ctx', split_axis=0, concat_axis=0, tiled=True)]
    ppermute x3, waiting for transfers between devices: 11 us -> 4 us  [per_device(): attn.append(lax.ppermute(held, axes, pairs) if step or side else held)]
    ppermute x6, waiting for transfers between devices: 6.81 us -> 1.41 us  [per_device(): lax.ppermute(kv_recv if side else kv_mine, 'ctx', ctx_pairs(step, 0))]
    ppermute x3, waiting for transfers between devices: 5.02 us -> 0.01 us  [per_device(): lax.ppermute(weight_sums[step], 'ctx', ctx_pairs(step, 0))]
    ppermute x1, waiting for transfers between devices: 12.6 us -> 8.17 us  [per_device(): weight_recv = lax.ppermute(send, 'ctx', ctx_pairs(0, 1))]
    ppermute x1 -> x4, starting transfers between devices: 2.55 us -> 5.7 us  [the longest x3 4.81 us: per_device(): lax.ppermute(part, 'ctx', ctx_pairs(-step, 0))]
    pallas_call x8 -> x9, Pallas kernels: 33.1 us -> 35.4 us  [placed(): return run(*args)]
  transfers between devices with their start and end apart: 19 -> 21, of which waited for: 7 -> 7; matrix products, arithmetic and copies ran while one was open for 2% -> 4% of each run, Pallas kernels for 30% -> 29%
where the time goes in v13:
time: 101 us; the launch traced here: 100 us
  Pallas kernels  35.4 us (35%)
  starting transfers between devices  31.3 us (31%)
  waiting for transfers between devices  28.9 us (29%)
  local copies, waits for them, and re-layouts  1.96 us (2%)
  other arithmetic  1.82 us (2%)
    pallas_call x9, Pallas kernels, placed(): return run(*args)  35.4 us
    ppermute x3, waiting for transfers between devices, per_device(): lax.ppermute(part, 'ctx', ctx_pairs(-step, 0))  10.5 us
    ppermute x6, starting transfers between devices, per_device(): lax.ppermute(kv_recv if side else kv_mine, 'ctx', ctx_pairs(step, 0))  10.4 us
    ppermute x1, waiting for transfers between devices, per_device(): weight_recv = lax.ppermute(send, 'ctx', ctx_pairs(0, 1))  8.17 us
    ppermute x3, starting transfers between devices, per_device(): lax.ppermute(weight_sums[step], 'ctx', ctx_pairs(step, 0))  5.59 us
    ppermute x3, starting transfers between devices, per_device(): lax.ppermute(part, 'ctx', ctx_pairs(-step, 0))  4.81 us
    ppermute x3, waiting for transfers between devices, per_device(): attn.append(lax.ppermute(held, axes, pairs) if step or side else held)  4 us
    ppermute x1, waiting for transfers between devices, per_device(): terms_recv = lax.ppermute(terms_theirs, 'ctx', ctx_pairs(0, 1))  3.33 us
  transfers between devices with their start and end apart: 21, of which 7 were waited for; matrix products, arithmetic and copies ran while one was open for 4% of the time, Pallas kernels for 29%

profile of v13, /device:TPU:0, one launch (start us, length us, event | category | flops | bytes accessed | tf_op | source)
XLA Modules:
  0.0 100.2 jit_solution(7706968704350328702)
XLA Ops:
  0.6 3.0 %collective-permute-start.3 = (bf16[256,2048]{1,0:T(8,128)(2,1)}, bf16[256,2048]{1,0:T(8,128)(2,1)}, u32[]{:S(2)}, u32[]{:S(2)}) collective-permute-start(bf16[256,2048]{1,0:T(8,128)(2,1)} %bitcast.21), channel_id=1, source_target_pairs={{0,1},{1,0},{2,3},{3,2},{4,5},{5,4},{6,7},{7,6},{8,9},{9,8},{10,11... | collective-permute-start | bytes 3145736 | tf_op jit(solution)/shard_map/ppermute | solution.py:599
  3.7 0.6 stack.59.refs_0_.refs_3_.refs_1_
  4.3 2.3 %part_heads.1 = (bf16[256,256]{1,0:T(8,128)(2,1)}, bf16[256,256]{1,0:T(8,128)(2,1)}) custom-call(s32[14]{0:T(128)} %stack.59.refs_0_.refs_3_.refs_1_, bf16[256,256]{1,0:T(8,128)(2,1)} %bitcast.24, bf16[256,256]{1,0:T(8,128)(2,1)} %bitcast.25), custom_call_target="tpu_custom_call" | custom-call | flops 2000000000 | bytes 6000000 | tf_op jit(solution)/shard_map/part_heads/pallas_call | solution.py:56
  6.6 1.6 %collective-permute-start = (bf16[256,256]{1,0:T(8,128)(2,1)}, bf16[256,256]{1,0:T(8,128)(2,1)}, u32[]{:S(2)}, u32[]{:S(2)}) collective-permute-start(bf16[256,256]{1,0:T(8,128)(2,1)} %get-tuple-element.30), channel_id=1, source_target_pairs={{0,2},{2,0},{4,6},{6,4},{8,10},{10,8},{12,14},{14,12},{1,3},{3,1},... | collective-permute-start | bytes 393224 | tf_op jit(solution)/shard_map/ppermute | solution.py:602
  8.2 3.6 %collective-permute-start.2 = (bf16[256,256]{1,0:T(8,128)(2,1)}, bf16[256,256]{1,0:T(8,128)(2,1)}, u32[]{:S(2)}, u32[]{:S(2)}) collective-permute-start(bf16[256,256]{1,0:T(8,128)(2,1)} %get-tuple-element.31.refs_6_), channel_id=1, source_target_pairs={{0,12},{2,14},{4,0},{6,2},{8,4},{10,6},{12,8},{14,10},{1,13},{3,15... | collective-permute-start | bytes 393224 | tf_op jit(solution)/shard_map/ppermute | solution.py:604
  11.8 0.0 collective-permute-start.1
  11.8 1.0 %collective-permute-start.6 = (bf16[256,256]{1,0:T(8,128)(2,1)}, bf16[256,256]{1,0:T(8,128)(2,1)}, u32[]{:S(2)}, u32[]{:S(2)}) collective-permute-start(bf16[256,256]{1,0:T(8,128)(2,1)} %get-tuple-element.31.refs_6_), channel_id=1, source_target_pairs={{0,8},{2,10},{4,12},{6,14},{8,0},{10,2},{12,4},{14,6},{1,9},{3,11}... | collective-permute-start | bytes 393224 | tf_op jit(solution)/shard_map/ppermute | solution.py:604
  12.8 1.3 %copy.11.refs_4_ = s32[8,3]{1,0:T(8,128)} copy(s32[8,3]{0,1:T(4,128)} %param.12) | data formatting | bytes 192 | tf_op args[5]
  14.1 0.0 collective-permute-done.refs_0_.refs_7_
  14.1 2.8 %collective-permute-start.8 = (bf16[256,256]{1,0:T(8,128)(2,1)}, bf16[256,256]{1,0:T(8,128)(2,1)}, u32[]{:S(2)}, u32[]{:S(2)}) collective-permute-start(bf16[256,256]{1,0:T(8,128)(2,1)} %collective-permute-done.refs_0_.refs_7_), channel_id=1, source_target_pairs={{0,12},{2,14},{4,0},{6,2},{8,4},{10,6},{12,8},{14,10},{1,13},{3,15... | collective-permute-start | bytes 393224 | tf_op jit(solution)/shard_map/ppermute | solution.py:604
  17.0 0.0 collective-permute-done.2.refs_2_.refs_12_
  17.0 2.0 %collective-permute-start.7 = (bf16[256,256]{1,0:T(8,128)(2,1)}, bf16[256,256]{1,0:T(8,128)(2,1)}, u32[]{:S(2)}, u32[]{:S(2)}) collective-permute-start(bf16[256,256]{1,0:T(8,128)(2,1)} %collective-permute-done.refs_0_.refs_7_), channel_id=1, source_target_pairs={{0,8},{2,10},{4,12},{6,14},{8,0},{10,2},{12,4},{14,6},{1,9},{3,11}... | collective-permute-start | bytes 393224 | tf_op jit(solution)/shard_map/ppermute | solution.py:604
  19.0 1.4 %collective-permute-done.1.refs_1_.refs_8_ = bf16[256,256]{1,0:T(8,128)(2,1)} collective-permute-done((bf16[256,256]{1,0:T(8,128)(2,1)}, bf16[256,256]{1,0:T(8,128)(2,1)}, u32[]{:S(2)}, u32[]{:S(2)}) %collective-permute-start.1) | collective-permute-done | bytes 131104 | tf_op jit(solution)/shard_map/ppermute | solution.py:604
  20.4 1.0 collective-permute-start.5
  21.3 4.3 %prelude.1 = (f32[256,256]{1,0:T(8,128)}, bf16[2048,128]{1,0:T(8,128)(2,1)}, f32[8,512]{1,0:T(8,128)}) custom-call(bf16[256,256]{1,0:T(8,128)(2,1)} %collective-permute-done.refs_0_.refs_7_, bf16[256,256]{1,0:T(8,128)(2,1)} %collective-permute-done.1.refs_1_.refs_8_, bf16[256,256]{1,0:T(8,128)(2,1)} %collective-permute-done.2.refs_2_.refs_12_, ...), custom_call_target="tpu_custom_call" | custom-call | flops 4000000000 | bytes 12000000 | tf_op jit(solution)/shard_map/prelude/pallas_call | solution.py:56
  25.7 1.5 %collective-permute-done.3.refs_4_.refs_3_ = bf16[256,2048]{1,0:T(8,128)(2,1)} collective-permute-done((bf16[256,2048]{1,0:T(8,128)(2,1)}, bf16[256,2048]{1,0:T(8,128)(2,1)}, u32[]{:S(2)}, u32[]{:S(2)}) %collective-permute-start.3) | collective-permute-done | bytes 1048608 | tf_op jit(solution)/shard_map/ppermute | solution.py:599
  27.1 3.5 %grad_heads.1 = (bf16[128,256]{1,0:T(8,128)(2,1)}, bf16[2,128,256]{2,1,0:T(8,128)(2,1)}) custom-call(s32[14]{0:T(128)} %stack.59.refs_0_.refs_3_.refs_1_, f32[256,256]{1,0:T(8,128)} %get-tuple-element.32.refs_1_, bf16[256,256]{1,0:T(8,128)(2,1)} %bitcast.26, bf16[256,4096]{1,0:T(8,128)(2,1)} %refs_3_.1, bf16[256,2048]{1,0:T(8,128)(2,1)} %collective-permute-done.3.refs_4_.refs_3_), custom_call_target="tpu_custom_call" | custom-call | flops 3000000000 | bytes 9000000 | tf_op jit(solution)/shard_map/grad_heads/pallas_call | solution.py:56
  30.7 1.8 %collective-permute-start.4 = (bf16[2,128,256]{2,1,0:T(8,128)(2,1)}, bf16[2,128,256]{2,1,0:T(8,128)(2,1)}, u32[]{:S(2)}, u32[]{:S(2)}) collective-permute-start(bf16[2,128,256]{2,1,0:T(8,128)(2,1)} %get-tuple-element.33), channel_id=1, source_target_pairs={{0,2},{2,0},{4,6},{6,4},{8,10},{10,8},{12,14},{14,12},{1,3},{3,1},... | collective-permute-start | bytes 393224 | tf_op jit(solution)/shard_map/ppermute | solution.py:613
  32.4 3.7 %pick_columns.1 = (bf16[2,4,256,256]{3,2,1,0:T(8,128)(2,1)}, bf16[2,4,256,256]{3,2,1,0:T(8,128)(2,1)}) custom-call(bf16[128,256]{1,0:T(8,128)(2,1)} %get-tuple-element.34.refs_3_.refs_0_, s32[14]{0:T(128)} %stack.59.refs_0_.refs_3_.refs_1_, bf16[256,2048]{1,0:T(8,128)(2,1)} %bitcast.23, bf16[256,2048]{1,0:T(8,128)(2,1)} %collective-permute-done.3.refs_4_.refs_3_), custom_call_target="tpu_custom_call" | custom-call | flops 3000000000 | bytes 9000000 | tf_op jit(solution)/shard_map/pick_columns/pallas_call | solution.py:56
  36.1 0.0 collective-permute-done.6.refs_10_
  36.1 0.1 collective-permute-start.12
  36.2 0.0 collective-permute-done.8.refs_13_
  36.2 0.0 collective-permute-done.7.refs_11_
  36.2 0.0 collective-permute-done.5.refs_9_
  36.2 0.0 collective-permute-done.4.refs_2_
  36.2 8.9 %attention.1 = (bf16[128,256]{1,0:T(8,128)(2,1)}, bf16[128,256]{1,0:T(8,128)(2,1)}, bf16[256,128]{1,0:T(8,128)(2,1)}, bf16[256,128]{1,0:T(8,128)(2,1)}, bf16[2,2...) custom-call(s32[14]{0:T(128)} %stack.59.refs_0_.refs_3_.refs_1_, ...), custom_call_target="tpu_custom_call" | custom-call | flops 20000000000 | bytes 60000000 | tf_op jit(solution)/shard_map/attention/pallas_call | solution.py:56
  45.1 0.5 collective-permute-start.11
  45.6 1.7 %collective-permute-start.9 = (bf16[128,256]{1,0:T(8,128)(2,1)}, bf16[128,256]{1,0:T(8,128)(2,1)}, u32[]{:S(2)}, u32[]{:S(2)}) collective-permute-start(bf16[128,256]{1,0:T(8,128)(2,1)} %get-tuple-element.39), channel_id=1, source_target_pairs={{0,2},{2,0},{4,6},{6,4},{8,10},{10,8},{12,14},{14,12},{1,3},{3,1},... | collective-permute-start | bytes 196616 | tf_op jit(solution)/shard_map/ppermute | solution.py:632
  47.3 0.0 collective-permute-start.10
  47.3 2.0 %collective-permute-done.11.refs_4_ = bf16[128,256]{1,0:T(8,128)(2,1)} collective-permute-done((bf16[128,256]{1,0:T(8,128)(2,1)}, bf16[128,256]{1,0:T(8,128)(2,1)}, u32[]{:S(2)}, u32[]{:S(2)}) %collective-permute-start.11) | collective-permute-done | bytes 65568 | tf_op jit(solution)/shard_map/ppermute | solution.py:632
  49.3 2.0 %collective-permute-done.9.refs_2_ = bf16[128,256]{1,0:T(8,128)(2,1)} collective-permute-done((bf16[128,256]{1,0:T(8,128)(2,1)}, bf16[128,256]{1,0:T(8,128)(2,1)}, u32[]{:S(2)}, u32[]{:S(2)}) %collective-permute-start.9) | collective-permute-done | bytes 65568 | tf_op jit(solution)/shard_map/ppermute | solution.py:632
  51.3 0.0 collective-permute-done.10.refs_3_
  51.3 0.0 collective-permute-done.12.refs_6_
  51.3 3.9 %weight_sent.1 = bf16[4,256,256]{2,1,0:T(8,128)(2,1)} custom-call(s32[14]{0:T(128)} %stack.59.refs_0_.refs_3_.refs_1_, bf16[128,256]{1,0:T(8,128)(2,1)} %get-tuple-element.38.refs_1_, bf16[128,256]{1,0:T(8,128)(2,1)} %collective-permute-done.9.refs_2_, bf16[128,256]{1,0:T(8,128)(2,1)} %collective-permute-done.10.refs_3_, ...), custom_call_target="tpu_custom_call" | custom-call | flops 4000000000 | bytes 12000000 | tf_op jit(solution)/shard_map/weight_sent/pallas_call | solution.py:56
  55.3 1.0 %collective-permute-start.13 = (bf16[4,256,256]{2,1,0:T(8,128)(2,1)}, bf16[4,256,256]{2,1,0:T(8,128)(2,1)}, u32[]{:S(2)}, u32[]{:S(2)}) collective-permute-start(bf16[4,256,256]{2,1,0:T(8,128)(2,1)} %weight_sent.1), channel_id=1, source_target_pairs={{0,2},{2,0},{4,6},{6,4},{8,10},{10,8},{12,14},{14,12},{1,3},{3,1},... | collective-permute-start | bytes 1572872 | tf_op jit(solution)/shard_map/ppermute | solution.py:635
  56.3 3.8 %collective-permute-start.14 = (bf16[2,256,256]{2,1,0:T(8,128)(2,1)}, bf16[2,256,256]{2,1,0:T(8,128)(2,1)}, u32[]{:S(2)}, u32[]{:S(2)}) collective-permute-start(bf16[2,256,256]{2,1,0:T(8,128)(2,1)} %get-tuple-element.45), channel_id=1, source_target_pairs={{0,12},{2,14},{4,0},{6,2},{8,4},{10,6},{12,8},{14,10},{1,13},{3,15... | collective-permute-start | bytes 786440 | tf_op jit(solution)/shard_map/ppermute | solution.py:623
  60.1 0.0 collective-permute-start.15
  60.1 1.0 collective-permute-start.16
  61.1 8.2 %collective-permute-done.13.refs_7_ = bf16[4,256,256]{2,1,0:T(8,128)(2,1)} collective-permute-done((bf16[4,256,256]{2,1,0:T(8,128)(2,1)}, bf16[4,256,256]{2,1,0:T(8,128)(2,1)}, u32[]{:S(2)}, u32[]{:S(2)}) %collective-permute-start.13) | collective-permute-done | bytes 524320 | tf_op jit(solution)/shard_map/ppermute | solution.py:635
  69.3 4.2 %weight_kept.1 = (bf16[256,256]{1,0:T(8,128)(2,1)}, bf16[256,256]{1,0:T(8,128)(2,1)}, bf16[256,256]{1,0:T(8,128)(2,1)}, bf16[256,256]{1,0:T(8,128)(2,1)}) custom-call(s32[14]{0:T(128)} %stack.59.refs_0_.refs_3_.refs_1_, bf16[128,256]{1,0:T(8,128)(2,1)} %get-tuple-element.38.refs_1_, bf16[128,256]{1,0:T(8,128)(2,1)} %collective-permute-done.9.refs_2_, ...), custom_call_target="tpu_custom_call" | custom-call | flops 4000000000 | bytes 12000000 | tf_op jit(solution)/shard_map/weight_kept/pallas_call | solution.py:56
  73.5 1.6 %collective-permute-start.18 = (bf16[256,256]{1,0:T(8,128)(2,1)}, bf16[256,256]{1,0:T(8,128)(2,1)}, u32[]{:S(2)}, u32[]{:S(2)}) collective-permute-start(bf16[256,256]{1,0:T(8,128)(2,1)} %get-tuple-element.53), channel_id=1, source_target_pairs={{0,4},{2,6},{4,8},{6,10},{8,12},{10,14},{12,0},{14,2},{1,5},{3,7},... | collective-permute-start | bytes 393224 | tf_op jit(solution)/shard_map/ppermute | solution.py:638
  75.1 2.6 %collective-permute-start.19 = (bf16[256,256]{1,0:T(8,128)(2,1)}, bf16[256,256]{1,0:T(8,128)(2,1)}, u32[]{:S(2)}, u32[]{:S(2)}) collective-permute-start(bf16[256,256]{1,0:T(8,128)(2,1)} %get-tuple-element.54), channel_id=1, source_target_pairs={{0,8},{2,10},{4,12},{6,14},{8,0},{10,2},{12,4},{14,6},{1,9},{3,11}... | collective-permute-start | bytes 393224 | tf_op jit(solution)/shard_map/ppermute | solution.py:638
  77.7 0.0 collective-permute-done.14.refs_3_
  77.7 1.3 %collective-permute-start.20 = (bf16[256,256]{1,0:T(8,128)(2,1)}, bf16[256,256]{1,0:T(8,128)(2,1)}, u32[]{:S(2)}, u32[]{:S(2)}) collective-permute-start(bf16[256,256]{1,0:T(8,128)(2,1)} %get-tuple-element.55), channel_id=1, source_target_pairs={{0,12},{2,14},{4,0},{6,2},{8,4},{10,6},{12,8},{14,10},{1,13},{3,15... | collective-permute-start | bytes 393224 | tf_op jit(solution)/shard_map/ppermute | solution.py:638
  79.0 10.5 %collective-permute-done.15.refs_4_ = bf16[2,256,256]{2,1,0:T(8,128)(2,1)} collective-permute-done((bf16[2,256,256]{2,1,0:T(8,128)(2,1)}, bf16[2,256,256]{2,1,0:T(8,128)(2,1)}, u32[]{:S(2)}, u32[]{:S(2)}) %collective-permute-start.15) | collective-permute-done | bytes 262176 | tf_op jit(solution)/shard_map/ppermute | solution.py:623
  89.6 0.0 collective-permute-done.16.refs_5_
  89.6 2.1 %add_terms.1 = (bf16[256,256]{1,0:T(8,128)(2,1)}, bf16[256,384]{1,0:T(8,128)(2,1)}) custom-call(bf16[256,256]{1,0:T(8,128)(2,1)} %get-tuple-element.42.refs_0_, bf16[256,128]{1,0:T(8,128)(2,1)} %get-tuple-element.43.refs_1_, bf16[2,256,256]{2,1,0:T(8,128)(2,1)} %get-tuple-element.44.refs_2_, bf16[2,256,256]{2,1,0:T(8,128)(2,1)} %collective-permute-done.14.refs_3_, ...), custom_call_target="tpu_custom_call" | custom-call | flops 2000000000 | bytes 6000000 | tf_op jit(solution)/shard_map/add_terms/pallas_call | solution.py:56
  91.6 0.9 collective-permute-start.17
  92.5 0.0 collective-permute-done.18
  92.5 0.0 collective-permute-done.19
  92.5 0.0 collective-permute-done.20
  92.5 1.8 %add_convert_fusion = bf16[256,256]{1,0:T(8,128)(2,1)} fusion(bf16[256,256]{1,0:T(8,128)(2,1)} %collective-permute-done.20, bf16[256,256]{1,0:T(8,128)(2,1)} %collective-permute-done.19, bf16[256,256]{1,0:T(8,128)(2,1)} %collective-permute-done.18, bf16[256,256]{1,0:T(8,128)(2,1)} %get-tuple-element.42.refs_0_), kind=kLoop, calls=%fused_computation | loop fusion | flops 524288 | bytes 655360 | tf_op jit(solution)/shard_map/convert_element_type | solution.py:647
  94.4 3.3 %collective-permute-done.17.refs_3_ = bf16[256,384]{1,0:T(8,128)(2,1)} collective-permute-done((bf16[256,384]{1,0:T(8,128)(2,1)}, bf16[256,384]{1,0:T(8,128)(2,1)}, u32[]{:S(2)}, u32[]{:S(2)}) %collective-permute-start.17) | collective-permute-done | bytes 196640 | tf_op jit(solution)/shard_map/ppermute | solution.py:641
  97.7 2.5 %join_heads.1 = (bf16[256,256]{1,0:T(8,128)(2,1)}, bf16[256,256]{1,0:T(8,128)(2,1)}, bf16[256,256]{1,0:T(8,128)(2,1)}) custom-call(s32[14]{0:T(128)} %stack.59.refs_0_.refs_3_.refs_1_, bf16[256,128]{1,0:T(8,128)(2,1)} %get-tuple-element.37.refs_1_, bf16[256,256]{1,0:T(8,128)(2,1)} %get-tuple-element.48.refs_2_, bf16[256,384]{1,0:T(8,128)(2,1)} %collective-permute-done.17.refs_3_), custom_call_target="tpu_custom_call" | custom-call | flops 2000000000 | bytes 6000000 | tf_op jit(solution)/shard_map/join_heads/pallas_call | solution.py:56
Async XLA Ops:
  0.6 26.5 %collective-permute-start.3 = (bf16[256,2048]{1,0:T(8,128)(2,1)}, bf16[256,2048]{1,0:T(8,128)(2,1)}, u32[]{:S(2)}, u32[]{:S(2)}) collective-permute-start(bf16[256,2048]{1,0:T(8,128)(2,1)} %bitcast.21), channel_id=1, source_target_pairs={{0,1},{1,0},{2,3},{3,2},{4,5},{5,4},{6,7},{7,6},{8,9},{9,8},{10,11... | collective-permute-start | bytes 3145736 | tf_op jit(solution)/shard_map/ppermute | solution.py:599
  6.6 7.5 %collective-permute-start = (bf16[256,256]{1,0:T(8,128)(2,1)}, bf16[256,256]{1,0:T(8,128)(2,1)}, u32[]{:S(2)}, u32[]{:S(2)}) collective-permute-start(bf16[256,256]{1,0:T(8,128)(2,1)} %get-tuple-element.30), channel_id=1, source_target_pairs={{0,2},{2,0},{4,6},{6,4},{8,10},{10,8},{12,14},{14,12},{1,3},{3,1},... | collective-permute-start | bytes 393224 | tf_op jit(solution)/shard_map/ppermute | solution.py:602
  8.2 8.8 %collective-permute-start.2 = (bf16[256,256]{1,0:T(8,128)(2,1)}, bf16[256,256]{1,0:T(8,128)(2,1)}, u32[]{:S(2)}, u32[]{:S(2)}) collective-permute-start(bf16[256,256]{1,0:T(8,128)(2,1)} %get-tuple-element.31.refs_6_), channel_id=1, source_target_pairs={{0,12},{2,14},{4,0},{6,2},{8,4},{10,6},{12,8},{14,10},{1,13},{3,15... | collective-permute-start | bytes 393224 | tf_op jit(solution)/shard_map/ppermute | solution.py:604
  11.8 8.6 %collective-permute-start.1 = (bf16[256,256]{1,0:T(8,128)(2,1)}, bf16[256,256]{1,0:T(8,128)(2,1)}, u32[]{:S(2)}, u32[]{:S(2)}) collective-permute-start(bf16[256,256]{1,0:T(8,128)(2,1)} %get-tuple-element.31.refs_6_), channel_id=1, source_target_pairs={{0,4},{2,6},{4,8},{6,10},{8,12},{10,14},{12,0},{14,2},{1,5},{3,7},... | collective-permute-start | bytes 393224 | tf_op jit(solution)/shard_map/ppermute | solution.py:604
  11.8 24.3 %collective-permute-start.6 = (bf16[256,256]{1,0:T(8,128)(2,1)}, bf16[256,256]{1,0:T(8,128)(2,1)}, u32[]{:S(2)}, u32[]{:S(2)}) collective-permute-start(bf16[256,256]{1,0:T(8,128)(2,1)} %get-tuple-element.31.refs_6_), channel_id=1, source_target_pairs={{0,8},{2,10},{4,12},{6,14},{8,0},{10,2},{12,4},{14,6},{1,9},{3,11}... | collective-permute-start | bytes 393224 | tf_op jit(solution)/shard_map/ppermute | solution.py:604
  14.1 22.1 %collective-permute-start.8 = (bf16[256,256]{1,0:T(8,128)(2,1)}, bf16[256,256]{1,0:T(8,128)(2,1)}, u32[]{:S(2)}, u32[]{:S(2)}) collective-permute-start(bf16[256,256]{1,0:T(8,128)(2,1)} %collective-permute-done.refs_0_.refs_7_), channel_id=1, source_target_pairs={{0,12},{2,14},{4,0},{6,2},{8,4},{10,6},{12,8},{14,10},{1,13},{3,15... | collective-permute-start | bytes 393224 | tf_op jit(solution)/shard_map/ppermute | solution.py:604
  17.0 19.3 %collective-permute-start.7 = (bf16[256,256]{1,0:T(8,128)(2,1)}, bf16[256,256]{1,0:T(8,128)(2,1)}, u32[]{:S(2)}, u32[]{:S(2)}) collective-permute-start(bf16[256,256]{1,0:T(8,128)(2,1)} %collective-permute-done.refs_0_.refs_7_), channel_id=1, source_target_pairs={{0,8},{2,10},{4,12},{6,14},{8,0},{10,2},{12,4},{14,6},{1,9},{3,11}... | collective-permute-start | bytes 393224 | tf_op jit(solution)/shard_map/ppermute | solution.py:604
  20.4 15.8 %collective-permute-start.5 = (bf16[256,256]{1,0:T(8,128)(2,1)}, bf16[256,256]{1,0:T(8,128)(2,1)}, u32[]{:S(2)}, u32[]{:S(2)}) collective-permute-start(bf16[256,256]{1,0:T(8,128)(2,1)} %collective-permute-done.refs_0_.refs_7_), channel_id=1, source_target_pairs={{0,4},{2,6},{4,8},{6,10},{8,12},{10,14},{12,0},{14,2},{1,5},{3,7},... | collective-permute-start | bytes 393224 | tf_op jit(solution)/shard_map/ppermute | solution.py:604
  30.7 5.6 %collective-permute-start.4 = (bf16[2,128,256]{2,1,0:T(8,128)(2,1)}, bf16[2,128,256]{2,1,0:T(8,128)(2,1)}, u32[]{:S(2)}, u32[]{:S(2)}) collective-permute-start(bf16[2,128,256]{2,1,0:T(8,128)(2,1)} %get-tuple-element.33), channel_id=1, source_target_pairs={{0,2},{2,0},{4,6},{6,4},{8,10},{10,8},{12,14},{14,12},{1,3},{3,1},... | collective-permute-start | bytes 393224 | tf_op jit(solution)/shard_map/ppermute | solution.py:613
  36.1 15.2 %collective-permute-start.12 = (bf16[2,4,256,256]{3,2,1,0:T(8,128)(2,1)}, bf16[2,4,256,256]{3,2,1,0:T(8,128)(2,1)}, u32[]{:S(2)}, u32[]{:S(2)}) collective-permute-start(bf16[2,4,256,256]{3,2,1,0:T(8,128)(2,1)} %get-tuple-element.41), channel_id=1, source_target_pairs={{0,16},{16,0},{1,17},{17,1},{2,18},{18,2},{3,19},{19,3},{4,20},{20... | collective-permute-start | bytes 3145736 | tf_op jit(solution)/shard_map/ppermute | solution.py:616
  45.1 4.2 %collective-permute-start.11 = (bf16[128,256]{1,0:T(8,128)(2,1)}, bf16[128,256]{1,0:T(8,128)(2,1)}, u32[]{:S(2)}, u32[]{:S(2)}) collective-permute-start(bf16[128,256]{1,0:T(8,128)(2,1)} %get-tuple-element.39), channel_id=1, source_target_pairs={{0,18},{2,16},{4,22},{6,20},{8,26},{10,24},{12,30},{14,28},{16,2},... | collective-permute-start | bytes 196616 | tf_op jit(solution)/shard_map/ppermute | solution.py:632
  45.6 5.7 %collective-permute-start.9 = (bf16[128,256]{1,0:T(8,128)(2,1)}, bf16[128,256]{1,0:T(8,128)(2,1)}, u32[]{:S(2)}, u32[]{:S(2)}) collective-permute-start(bf16[128,256]{1,0:T(8,128)(2,1)} %get-tuple-element.39), channel_id=1, source_target_pairs={{0,2},{2,0},{4,6},{6,4},{8,10},{10,8},{12,14},{14,12},{1,3},{3,1},... | collective-permute-start | bytes 196616 | tf_op jit(solution)/shard_map/ppermute | solution.py:632
  47.3 4.0 %collective-permute-start.10 = (bf16[128,256]{1,0:T(8,128)(2,1)}, bf16[128,256]{1,0:T(8,128)(2,1)}, u32[]{:S(2)}, u32[]{:S(2)}) collective-permute-start(bf16[128,256]{1,0:T(8,128)(2,1)} %get-tuple-element.38.refs_1_), channel_id=1, source_target_pairs={{0,16},{2,18},{4,20},{6,22},{8,24},{10,26},{12,28},{14,30},{16,0},... | collective-permute-start | bytes 196616 | tf_op jit(solution)/shard_map/ppermute | solution.py:632
  55.3 14.0 %collective-permute-start.13 = (bf16[4,256,256]{2,1,0:T(8,128)(2,1)}, bf16[4,256,256]{2,1,0:T(8,128)(2,1)}, u32[]{:S(2)}, u32[]{:S(2)}) collective-permute-start(bf16[4,256,256]{2,1,0:T(8,128)(2,1)} %weight_sent.1), channel_id=1, source_target_pairs={{0,2},{2,0},{4,6},{6,4},{8,10},{10,8},{12,14},{14,12},{1,3},{3,1},... | collective-permute-start | bytes 1572872 | tf_op jit(solution)/shard_map/ppermute | solution.py:635
  56.3 21.4 %collective-permute-start.14 = (bf16[2,256,256]{2,1,0:T(8,128)(2,1)}, bf16[2,256,256]{2,1,0:T(8,128)(2,1)}, u32[]{:S(2)}, u32[]{:S(2)}) collective-permute-start(bf16[2,256,256]{2,1,0:T(8,128)(2,1)} %get-tuple-element.45), channel_id=1, source_target_pairs={{0,12},{2,14},{4,0},{6,2},{8,4},{10,6},{12,8},{14,10},{1,13},{3,15... | collective-permute-start | bytes 786440 | tf_op jit(solution)/shard_map/ppermute | solution.py:623
  60.1 29.5 %collective-permute-start.15 = (bf16[2,256,256]{2,1,0:T(8,128)(2,1)}, bf16[2,256,256]{2,1,0:T(8,128)(2,1)}, u32[]{:S(2)}, u32[]{:S(2)}) collective-permute-start(bf16[2,256,256]{2,1,0:T(8,128)(2,1)} %get-tuple-element.46), channel_id=1, source_target_pairs={{0,8},{2,10},{4,12},{6,14},{8,0},{10,2},{12,4},{14,6},{1,9},{3,11}... | collective-permute-start | bytes 786440 | tf_op jit(solution)/shard_map/ppermute | solution.py:623
  60.1 29.5 %collective-permute-start.16 = (bf16[2,256,256]{2,1,0:T(8,128)(2,1)}, bf16[2,256,256]{2,1,0:T(8,128)(2,1)}, u32[]{:S(2)}, u32[]{:S(2)}) collective-permute-start(bf16[2,256,256]{2,1,0:T(8,128)(2,1)} %get-tuple-element.47), channel_id=1, source_target_pairs={{0,4},{2,6},{4,8},{6,10},{8,12},{10,14},{12,0},{14,2},{1,5},{3,7},... | collective-permute-start | bytes 786440 | tf_op jit(solution)/shard_map/ppermute | solution.py:623
  73.5 19.1 %collective-permute-start.18 = (bf16[256,256]{1,0:T(8,128)(2,1)}, bf16[256,256]{1,0:T(8,128)(2,1)}, u32[]{:S(2)}, u32[]{:S(2)}) collective-permute-start(bf16[256,256]{1,0:T(8,128)(2,1)} %get-tuple-element.53), channel_id=1, source_target_pairs={{0,4},{2,6},{4,8},{6,10},{8,12},{10,14},{12,0},{14,2},{1,5},{3,7},... | collective-permute-start | bytes 393224 | tf_op jit(solution)/shard_map/ppermute | solution.py:638
  75.1 17.5 %collective-permute-start.19 = (bf16[256,256]{1,0:T(8,128)(2,1)}, bf16[256,256]{1,0:T(8,128)(2,1)}, u32[]{:S(2)}, u32[]{:S(2)}) collective-permute-start(bf16[256,256]{1,0:T(8,128)(2,1)} %get-tuple-element.54), channel_id=1, source_target_pairs={{0,8},{2,10},{4,12},{6,14},{8,0},{10,2},{12,4},{14,6},{1,9},{3,11}... | collective-permute-start | bytes 393224 | tf_op jit(solution)/shard_map/ppermute | solution.py:638
  77.7 14.8 %collective-permute-start.20 = (bf16[256,256]{1,0:T(8,128)(2,1)}, bf16[256,256]{1,0:T(8,128)(2,1)}, u32[]{:S(2)}, u32[]{:S(2)}) collective-permute-start(bf16[256,256]{1,0:T(8,128)(2,1)} %get-tuple-element.55), channel_id=1, source_target_pairs={{0,12},{2,14},{4,0},{6,2},{8,4},{10,6},{12,8},{14,10},{1,13},{3,15... | collective-permute-start | bytes 393224 | tf_op jit(solution)/shard_map/ppermute | solution.py:638
  91.6 6.1 %collective-permute-start.17 = (bf16[256,384]{1,0:T(8,128)(2,1)}, bf16[256,384]{1,0:T(8,128)(2,1)}, u32[]{:S(2)}, u32[]{:S(2)}) collective-permute-start(bf16[256,384]{1,0:T(8,128)(2,1)} %get-tuple-element.49), channel_id=1, source_target_pairs={{0,2},{2,0},{4,6},{6,4},{8,10},{10,8},{12,14},{14,12},{1,3},{3,1},... | collective-permute-start | bytes 589832 | tf_op jit(solution)/shard_map/ppermute | solution.py:641

commit v14 on v13

--- a/solution.py
+++ b/solution.py
@@ -176,9 +176,8 @@
 
 def attention_kernel(block_count, head_count, at_ref, q_ref, recv_ref, g_mine, key_mask, row_mask, *refs):
     kv_refs, refs = refs[:block_count], refs[block_count:]
-    outer = block_count // INNER
-    attn_mine, attn_theirs, dq_mine, dq_theirs = refs[:4]
-    part_outs, refs = refs[4 : 4 + outer], refs[4 + outer :]
+    attn_mine, attn_theirs, dq_mine, dq_theirs, part_out = refs[:5]
+    refs = refs[5:]
     q_s, recv_s, g_s, mask_s, row_s, kv_s, e_s, s_ref, attn_s, dq_s, part_s = refs[:11]
     sem, kv_sem, out_sem, part_sem = refs[11:]
     rows = q_ref.shape[0]
@@ -243,7 +242,7 @@
             part_s[j, :, cols] = (score_scale * product(dscore, query)).astype(jnp.bfloat16)
             part_s[j, :, vcols] = product(low, grad).astype(jnp.bfloat16)
             if head == head_count - 1:
-                target = part_outs[j // INNER].at[j % INNER]
+                target = part_out.at[at_ref[SOURCES + j] // INNER, j % INNER]
                 stores.append(begin(part_s.at[j], target, part_sem.at[j]))
         dquery = (score_scale * jnp.transpose(dq_t)).astype(jnp.bfloat16)
         dq_s[0, :, cols] = dquery[:rows]
@@ -259,12 +258,12 @@
     feats, rows = g_mine.shape
     heads = feats // HD
     keys = block_count * rows
-    outer = block_count // INNER
-    out = call(
+    parts = bf16(block_count // INNER, INNER, rows, 2 * feats)
+    return call(
         functools.partial(attention_kernel, block_count, heads),
-        [bf16(feats, rows)] * 2 + [bf16(rows, feats)] * 2 + [bf16(INNER, rows, 2 * feats)] * outer,
+        [bf16(feats, rows)] * 2 + [bf16(rows, feats)] * 2 + [parts],
         [SMEM] + [ANY] * (5 + block_count),
-        [ANY] * (4 + outer),
+        [ANY] * 5,
         [
             pltpu.VMEM((rows, feats), jnp.bfloat16),
             pltpu.VMEM((2, feats, rows), jnp.bfloat16),
@@ -285,7 +284,6 @@
         20,
         "attention",
     )(at, queries, recv, g_mine, key_mask, row_mask, *kv_blocks)
-    return *out[:4], out[4:]
 
 
 def grad_heads_kernel(part_count, place, at_ref, first_ref, q_ref, weight_ref, *refs):
@@ -464,13 +462,12 @@
     )(at, *operands)
 
 
-def add_kernel(count, dq_theirs, *refs):
-    terms, (mine, theirs) = refs[:count], refs[count : count + 2]
-    terms_s, mine_s, theirs_s, dq_s, term_sem, out_sem, dq_sem = refs[count + 2 :]
-    both = mine.shape[1]
+def add_kernel(dq_theirs, terms, mine, theirs, *scratch):
+    terms_s, mine_s, theirs_s, dq_s, term_sem, out_sem, dq_sem = scratch
+    count, _, _, both = terms.shape
     dq_load = begin(dq_theirs, dq_s, dq_sem)
     loads = {
-        (side, c): begin(terms[c].at[side], terms_s.at[c, side], term_sem.at[c * INNER + side])
+        (side, c): begin(terms.at[c, side], terms_s.at[c, side], term_sem.at[c * INNER + side])
         for side in (1, 0)
         for c in range(count)
     }
@@ -490,13 +487,12 @@
 
 
 def add_terms(dq_theirs, terms, after):
-    _, rows, both = terms[0].shape
+    count, _, rows, both = terms.shape
     half = both // 2
-    count = len(terms)
-    return call(
-        functools.partial(add_kernel, count),
+    return call(
+        add_kernel,
         [bf16(rows, both), bf16(rows, both + half)],
-        [ANY] * (1 + count),
+        [ANY] * 2,
         [ANY] * 2,
         [
             pltpu.VMEM((count, INNER, rows, both), jnp.bfloat16),
@@ -510,7 +506,7 @@
         2,
         "add_terms",
         after,
-    )(dq_theirs, *terms)
+    )(dq_theirs, terms)
 
 
 def join_kernel(at_ref, dq_mine, mine, recv, *refs):
@@ -619,10 +615,10 @@
     attn_mine, attn_theirs, dq_mine, dq_theirs, parts = attention(
         at, queries[0], recv, g_mine, key_mask, row_mask, kv_blocks
     )
-    terms = [
-        lax.ppermute(part, "ctx", ctx_pairs(-step, 0)) if step else part
-        for step, part in enumerate(parts)
-    ]
+    columns = [[o * INNER + i for o in range(outer)] for i in range(INNER)]
+    terms = lax.all_to_all(
+        parts, "ctx", split_axis=0, concat_axis=0, axis_index_groups=columns, tiled=True
+    )
 
     attn = []
     for step in range(dp_count):

time: 101 us -> 97.4 us (0.964)
  waiting for transfers between devices: 28.9 us -> 24 us
    ppermute x3 -> x0, waiting for transfers between devices: 10.5 us -> none  [per_device(): lax.ppermute(part, 'ctx', ctx_pairs(-step, 0))]
    all_to_all x0 -> x1, starting transfers between devices: none -> 5.03 us  [per_device(): lax.all_to_all(parts, 'ctx', split_axis=0, concat_axis=0, axis_index_grou...]
    ppermute x1, waiting for transfers between devices: 8.17 us -> 13.2 us  [per_device(): weight_recv = lax.ppermute(send, 'ctx', ctx_pairs(0, 1))]
    ppermute x3 -> x0, starting transfers between devices: 4.81 us -> none  [per_device(): lax.ppermute(part, 'ctx', ctx_pairs(-step, 0))]
    ppermute x3, waiting for transfers between devices: 0.01 us -> 4.04 us  [per_device(): lax.ppermute(weight_sums[step], 'ctx', ctx_pairs(step, 0))]
    ppermute x1, waiting for transfers between devices: 3.33 us -> 0.01 us  [per_device(): terms_recv = lax.ppermute(terms_theirs, 'ctx', ctx_pairs(0, 1))]
  transfers between devices with their start and end apart: 21 -> 19, of which waited for: 7 -> 6; matrix products, arithmetic and copies ran while one was open for 4% -> 4% of each run, Pallas kernels for 29% -> 34%
where the time goes in v14:
time: 97.4 us; the launch traced here: 96.4 us
  Pallas kernels  35.5 us (36%)
  starting transfers between devices  31.7 us (33%)
  waiting for transfers between devices  24 us (25%)
  local copies, waits for them, and re-layouts  2.67 us (3%)
  other arithmetic  1.82 us (2%)
    pallas_call x9, Pallas kernels, placed(): return run(*args)  35.5 us
    ppermute x1, waiting for transfers between devices, per_device(): weight_recv = lax.ppermute(send, 'ctx', ctx_pairs(0, 1))  13.2 us
    ppermute x6, starting transfers between devices, per_device(): lax.ppermute(kv_recv if side else kv_mine, 'ctx', ctx_pairs(step, 0))  10.4 us
    ppermute x3, starting transfers between devices, per_device(): lax.ppermute(weight_sums[step], 'ctx', ctx_pairs(step, 0))  6.12 us
    all_to_all x1, starting transfers between devices, per_device(): lax.all_to_all(parts, 'ctx', split_axis=0, concat_axis=0, axis_index_grou...  5.03 us
    ppermute x3, waiting for transfers between devices, per_device(): lax.ppermute(weight_sums[step], 'ctx', ctx_pairs(step, 0))  4.04 us
    ppermute x3, waiting for transfers between devices, per_device(): attn.append(lax.ppermute(held, axes, pairs) if step or side else held)  3.93 us
    ppermute x1, starting transfers between devices, per_device(): lax.ppermute(grad_own, 'tp', shift_pairs(tp_count, -step))  3.03 us
  transfers between devices with their start and end apart: 19, of which 6 were waited for; matrix products, arithmetic and copies ran while one was open for 4% of the time, Pallas kernels for 34%

profile of v14, /device:TPU:0, one launch (start us, length us, event | category | flops | bytes accessed | tf_op | source)
XLA Modules:
  0.0 96.4 jit_solution(12841630315113460174)
XLA Ops:
  0.6 3.0 %collective-permute-start.3 = (bf16[256,2048]{1,0:T(8,128)(2,1)}, bf16[256,2048]{1,0:T(8,128)(2,1)}, u32[]{:S(2)}, u32[]{:S(2)}) collective-permute-start(bf16[256,2048]{1,0:T(8,128)(2,1)} %bitcast.21), channel_id=1, source_target_pairs={{0,1},{1,0},{2,3},{3,2},{4,5},{5,4},{6,7},{7,6},{8,9},{9,8},{10,11... | collective-permute-start | bytes 3145736 | tf_op jit(solution)/shard_map/ppermute | solution.py:595
  3.7 0.7 stack.59.refs_0_.refs_3_.refs_1_
  4.3 2.3 %part_heads.1 = (bf16[256,256]{1,0:T(8,128)(2,1)}, bf16[256,256]{1,0:T(8,128)(2,1)}) custom-call(s32[14]{0:T(128)} %stack.59.refs_0_.refs_3_.refs_1_, bf16[256,256]{1,0:T(8,128)(2,1)} %bitcast.24, bf16[256,256]{1,0:T(8,128)(2,1)} %bitcast.25), custom_call_target="tpu_custom_call" | custom-call | flops 2000000000 | bytes 6000000 | tf_op jit(solution)/shard_map/part_heads/pallas_call | solution.py:56
  6.7 1.6 %collective-permute-start = (bf16[256,256]{1,0:T(8,128)(2,1)}, bf16[256,256]{1,0:T(8,128)(2,1)}, u32[]{:S(2)}, u32[]{:S(2)}) collective-permute-start(bf16[256,256]{1,0:T(8,128)(2,1)} %get-tuple-element.27), channel_id=1, source_target_pairs={{0,2},{2,0},{4,6},{6,4},{8,10},{10,8},{12,14},{14,12},{1,3},{3,1},... | collective-permute-start | bytes 393224 | tf_op jit(solution)/shard_map/ppermute | solution.py:598
  8.2 3.6 %collective-permute-start.2 = (bf16[256,256]{1,0:T(8,128)(2,1)}, bf16[256,256]{1,0:T(8,128)(2,1)}, u32[]{:S(2)}, u32[]{:S(2)}) collective-permute-start(bf16[256,256]{1,0:T(8,128)(2,1)} %get-tuple-element.28.refs_6_), channel_id=1, source_target_pairs={{0,12},{2,14},{4,0},{6,2},{8,4},{10,6},{12,8},{14,10},{1,13},{3,15... | collective-permute-start | bytes 393224 | tf_op jit(solution)/shard_map/ppermute | solution.py:600
  11.8 0.0 collective-permute-start.1
  11.8 1.0 %collective-permute-start.6 = (bf16[256,256]{1,0:T(8,128)(2,1)}, bf16[256,256]{1,0:T(8,128)(2,1)}, u32[]{:S(2)}, u32[]{:S(2)}) collective-permute-start(bf16[256,256]{1,0:T(8,128)(2,1)} %get-tuple-element.28.refs_6_), channel_id=1, source_target_pairs={{0,8},{2,10},{4,12},{6,14},{8,0},{10,2},{12,4},{14,6},{1,9},{3,11}... | collective-permute-start | bytes 393224 | tf_op jit(solution)/shard_map/ppermute | solution.py:600
  12.8 1.3 %copy.11.refs_4_ = s32[8,3]{1,0:T(8,128)} copy(s32[8,3]{0,1:T(4,128)} %param.12) | data formatting | bytes 192 | tf_op args[5]
  14.2 0.0 collective-permute-done.refs_0_.refs_7_
  14.2 2.8 %collective-permute-start.8 = (bf16[256,256]{1,0:T(8,128)(2,1)}, bf16[256,256]{1,0:T(8,128)(2,1)}, u32[]{:S(2)}, u32[]{:S(2)}) collective-permute-start(bf16[256,256]{1,0:T(8,128)(2,1)} %collective-permute-done.refs_0_.refs_7_), channel_id=1, source_target_pairs={{0,12},{2,14},{4,0},{6,2},{8,4},{10,6},{12,8},{14,10},{1,13},{3,15... | collective-permute-start | bytes 393224 | tf_op jit(solution)/shard_map/ppermute | solution.py:600
  17.0 0.0 collective-permute-done.2.refs_2_.refs_12_
  17.0 2.0 %collective-permute-start.7 = (bf16[256,256]{1,0:T(8,128)(2,1)}, bf16[256,256]{1,0:T(8,128)(2,1)}, u32[]{:S(2)}, u32[]{:S(2)}) collective-permute-start(bf16[256,256]{1,0:T(8,128)(2,1)} %collective-permute-done.refs_0_.refs_7_), channel_id=1, source_target_pairs={{0,8},{2,10},{4,12},{6,14},{8,0},{10,2},{12,4},{14,6},{1,9},{3,11}... | collective-permute-start | bytes 393224 | tf_op jit(solution)/shard_map/ppermute | solution.py:600
  19.0 1.4 %collective-permute-done.1.refs_1_.refs_8_ = bf16[256,256]{1,0:T(8,128)(2,1)} collective-permute-done((bf16[256,256]{1,0:T(8,128)(2,1)}, bf16[256,256]{1,0:T(8,128)(2,1)}, u32[]{:S(2)}, u32[]{:S(2)}) %collective-permute-start.1) | collective-permute-done | bytes 131104 | tf_op jit(solution)/shard_map/ppermute | solution.py:600
  20.4 1.0 collective-permute-start.5
  21.4 4.3 %prelude.1 = (f32[256,256]{1,0:T(8,128)}, bf16[2048,128]{1,0:T(8,128)(2,1)}, f32[8,512]{1,0:T(8,128)}) custom-call(bf16[256,256]{1,0:T(8,128)(2,1)} %collective-permute-done.refs_0_.refs_7_, bf16[256,256]{1,0:T(8,128)(2,1)} %collective-permute-done.1.refs_1_.refs_8_, bf16[256,256]{1,0:T(8,128)(2,1)} %collective-permute-done.2.refs_2_.refs_12_, ...), custom_call_target="tpu_custom_call" | custom-call | flops 4000000000 | bytes 12000000 | tf_op jit(solution)/shard_map/prelude/pallas_call | solution.py:56
  25.7 1.4 %collective-permute-done.3.refs_4_.refs_3_ = bf16[256,2048]{1,0:T(8,128)(2,1)} collective-permute-done((bf16[256,2048]{1,0:T(8,128)(2,1)}, bf16[256,2048]{1,0:T(8,128)(2,1)}, u32[]{:S(2)}, u32[]{:S(2)}) %collective-permute-start.3) | collective-permute-done | bytes 1048608 | tf_op jit(solution)/shard_map/ppermute | solution.py:595
  27.1 3.5 %grad_heads.1 = (bf16[128,256]{1,0:T(8,128)(2,1)}, bf16[2,128,256]{2,1,0:T(8,128)(2,1)}) custom-call(s32[14]{0:T(128)} %stack.59.refs_0_.refs_3_.refs_1_, f32[256,256]{1,0:T(8,128)} %get-tuple-element.29.refs_1_, bf16[256,256]{1,0:T(8,128)(2,1)} %bitcast.26, bf16[256,4096]{1,0:T(8,128)(2,1)} %refs_3_.1, bf16[256,2048]{1,0:T(8,128)(2,1)} %collective-permute-done.3.refs_4_.refs_3_), custom_call_target="tpu_custom_call" | custom-call | flops 3000000000 | bytes 9000000 | tf_op jit(solution)/shard_map/grad_heads/pallas_call | solution.py:56
  30.7 1.8 %collective-permute-start.4 = (bf16[2,128,256]{2,1,0:T(8,128)(2,1)}, bf16[2,128,256]{2,1,0:T(8,128)(2,1)}, u32[]{:S(2)}, u32[]{:S(2)}) collective-permute-start(bf16[2,128,256]{2,1,0:T(8,128)(2,1)} %get-tuple-element.30), channel_id=1, source_target_pairs={{0,2},{2,0},{4,6},{6,4},{8,10},{10,8},{12,14},{14,12},{1,3},{3,1},... | collective-permute-start | bytes 393224 | tf_op jit(solution)/shard_map/ppermute | solution.py:609
  32.4 3.7 %pick_columns.1 = (bf16[2,4,256,256]{3,2,1,0:T(8,128)(2,1)}, bf16[2,4,256,256]{3,2,1,0:T(8,128)(2,1)}) custom-call(bf16[128,256]{1,0:T(8,128)(2,1)} %get-tuple-element.31.refs_3_.refs_0_, s32[14]{0:T(128)} %stack.59.refs_0_.refs_3_.refs_1_, bf16[256,2048]{1,0:T(8,128)(2,1)} %bitcast.23, bf16[256,2048]{1,0:T(8,128)(2,1)} %collective-permute-done.3.refs_4_.refs_3_), custom_call_target="tpu_custom_call" | custom-call | flops 3000000000 | bytes 9000000 | tf_op jit(solution)/shard_map/pick_columns/pallas_call | solution.py:56
  36.2 0.0 collective-permute-done.6.refs_10_
  36.2 0.1 collective-permute-start.12
  36.3 0.0 collective-permute-done.8.refs_13_
  36.3 0.0 collective-permute-done.7.refs_11_
  36.3 0.0 collective-permute-done.5.refs_9_
  36.3 0.0 collective-permute-done.4.refs_2_
  36.3 8.8 %attention.1 = (bf16[128,256]{1,0:T(8,128)(2,1)}, bf16[128,256]{1,0:T(8,128)(2,1)}, bf16[256,128]{1,0:T(8,128)(2,1)}, bf16[256,128]{1,0:T(8,128)(2,1)}, bf16[4,2,256,256]{3,2,1,0:T(8,128)(2,1)}) custom-call(s32[14]{0:T(128)} %stack.59.refs_0_.refs_3_.refs_1_, bf16[256,256]{1,0:T(8,128)(2,1)} %bitcast.27, ...), custom_call_target="tpu_custom_call" | custom-call | flops 20000000000 | bytes 60000000 | tf_op jit(solution)/shard_map/attention/pallas_call | solution.py:56
  45.2 0.0 copy-start.2
  45.2 0.0 copy-start
  45.2 5.0 %all-to-all-start = ((bf16[4,2,256,256]{3,2,1,0:T(8,128)(2,1)}), bf16[4,2,256,256]{3,2,1,0:T(8,128)(2,1)}, u32[]{:S(2)}, u32[]{:S(2)}) async-start(bf16[4,2,256,256]{3,2,1,0:T(8,128)(2,1)} %get-tuple-element.41), calls=%async_computation | async-start | bytes 2097152 | tf_op jit(solution)/shard_map/all_to_all | solution.py:619
  50.2 0.0 copy-done.2
  50.2 0.3 collective-permute-start.11
  50.5 1.5 %collective-permute-start.9 = (bf16[128,256]{1,0:T(8,128)(2,1)S(1)}, bf16[128,256]{1,0:T(8,128)(2,1)S(1)}, u32[]{:S(2)}, u32[]{:S(2)}) collective-permute-start(bf16[128,256]{1,0:T(8,128)(2,1)S(1)} %copy-done.2), channel_id=1, source_target_pairs={{0,2},{2,0},{4,6},{6,4},{8,10},{10,8},{12,14},{14,12},{1,3},{3,1},... | collective-permute-start | bytes 196616 | tf_op jit(solution)/shard_map/ppermute | solution.py:628
  52.0 0.0 copy-done
  52.0 0.0 collective-permute-start.10
  52.1 2.2 %collective-permute-done.11.refs_4_ = bf16[128,256]{1,0:T(8,128)(2,1)S(1)} collective-permute-done((bf16[128,256]{1,0:T(8,128)(2,1)S(1)}, bf16[128,256]{1,0:T(8,128)(2,1)S(1)}, u32[]{:S(2)}, u32[]{:S(2)}) %collective-permute-start.11) | collective-permute-done | bytes 65568 | tf_op jit(solution)/shard_map/ppermute | solution.py:628
  54.3 0.0 copy-start.1
  54.3 1.7 %collective-permute-done.9.refs_2_ = bf16[128,256]{1,0:T(8,128)(2,1)S(1)} collective-permute-done((bf16[128,256]{1,0:T(8,128)(2,1)S(1)}, bf16[128,256]{1,0:T(8,128)(2,1)S(1)}, u32[]{:S(2)}, u32[]{:S(2)}) %collective-permute-start.9) | collective-permute-done | bytes 65568 | tf_op jit(solution)/shard_map/ppermute | solution.py:628
  56.0 0.0 copy-start.3
  56.0 0.0 collective-permute-done.10.refs_3_
  56.0 0.0 copy-done.1
  56.0 0.0 copy-start.4
  56.0 0.0 collective-permute-done.12.refs_6_
  56.0 0.6 copy-done.3
  56.6 0.0 copy-done.4
  56.7 3.9 %weight_sent.1 = bf16[4,256,256]{2,1,0:T(8,128)(2,1)} custom-call(s32[14]{0:T(128)} %stack.59.refs_0_.refs_3_.refs_1_, bf16[128,256]{1,0:T(8,128)(2,1)} %get-tuple-element.35.refs_1_, bf16[128,256]{1,0:T(8,128)(2,1)} %copy-done.3, bf16[128,256]{1,0:T(8,128)(2,1)} %copy-done.4, bf16[128,256]{1,0:T(8,128)(2,1)} %copy-done.1, ...), custom_call_target="tpu_custom_call" | custom-call | flops 4000000000 | bytes 12000000 | tf_op jit(solution)/shard_map/weight_sent/pallas_call | solution.py:56
  60.6 1.0 collective-permute-start.13
  61.6 13.2 %collective-permute-done.13.refs_7_ = bf16[4,256,256]{2,1,0:T(8,128)(2,1)} collective-permute-done((bf16[4,256,256]{2,1,0:T(8,128)(2,1)}, bf16[4,256,256]{2,1,0:T(8,128)(2,1)}, u32[]{:S(2)}, u32[]{:S(2)}) %collective-permute-start.13) | collective-permute-done | bytes 524320 | tf_op jit(solution)/shard_map/ppermute | solution.py:631
  74.7 4.2 %weight_kept.1 = (bf16[256,256]{1,0:T(8,128)(2,1)}, bf16[256,256]{1,0:T(8,128)(2,1)}, bf16[256,256]{1,0:T(8,128)(2,1)}, bf16[256,256]{1,0:T(8,128)(2,1)}) custom-call(s32[14]{0:T(128)} %stack.59.refs_0_.refs_3_.refs_1_, bf16[128,256]{1,0:T(8,128)(2,1)} %get-tuple-element.35.refs_1_, bf16[128,256]{1,0:T(8,128)(2,1)} %copy-done.3, bf16[128,256]{1,0:T(8,128)(2,1)} %copy-done.4, ...), custom_call_target="tpu_custom_call" | custom-call | flops 4000000000 | bytes 12000000 | tf_op jit(solution)/shard_map/weight_kept/pallas_call | solution.py:56
  78.9 2.3 %collective-permute-start.15 = (bf16[256,256]{1,0:T(8,128)(2,1)}, bf16[256,256]{1,0:T(8,128)(2,1)}, u32[]{:S(2)}, u32[]{:S(2)}) collective-permute-start(bf16[256,256]{1,0:T(8,128)(2,1)} %get-tuple-element.47), channel_id=1, source_target_pairs={{0,4},{2,6},{4,8},{6,10},{8,12},{10,14},{12,0},{14,2},{1,5},{3,7},... | collective-permute-start | bytes 393224 | tf_op jit(solution)/shard_map/ppermute | solution.py:634
  81.2 2.4 %collective-permute-start.16 = (bf16[256,256]{1,0:T(8,128)(2,1)}, bf16[256,256]{1,0:T(8,128)(2,1)}, u32[]{:S(2)}, u32[]{:S(2)}) collective-permute-start(bf16[256,256]{1,0:T(8,128)(2,1)} %get-tuple-element.48), channel_id=1, source_target_pairs={{0,8},{2,10},{4,12},{6,14},{8,0},{10,2},{12,4},{14,6},{1,9},{3,11}... | collective-permute-start | bytes 393224 | tf_op jit(solution)/shard_map/ppermute | solution.py:634
  83.6 1.5 %collective-permute-start.17 = (bf16[256,256]{1,0:T(8,128)(2,1)}, bf16[256,256]{1,0:T(8,128)(2,1)}, u32[]{:S(2)}, u32[]{:S(2)}) collective-permute-start(bf16[256,256]{1,0:T(8,128)(2,1)} %get-tuple-element.49), channel_id=1, source_target_pairs={{0,12},{2,14},{4,0},{6,2},{8,4},{10,6},{12,8},{14,10},{1,13},{3,15... | collective-permute-start | bytes 393224 | tf_op jit(solution)/shard_map/ppermute | solution.py:634
  85.0 0.0 all-to-all-done.refs_2_
  85.0 2.1 %add_terms.1 = (bf16[256,256]{1,0:T(8,128)(2,1)}, bf16[256,384]{1,0:T(8,128)(2,1)}) custom-call(bf16[256,256]{1,0:T(8,128)(2,1)} %get-tuple-element.39.refs_0_, bf16[256,128]{1,0:T(8,128)(2,1)} %get-tuple-element.40.refs_1_, bf16[4,2,256,256]{3,2,1,0:T(8,128)(2,1)} %all-to-all-done.refs_2_), custom_call_target="tpu_custom_call" | custom-call | flops 2000000000 | bytes 6000000 | tf_op jit(solution)/shard_map/add_terms/pallas_call | solution.py:56
  87.1 0.9 collective-permute-start.14
  88.0 0.0 collective-permute-done.15
  88.0 4.0 %collective-permute-done.16 = bf16[256,256]{1,0:T(8,128)(2,1)} collective-permute-done((bf16[256,256]{1,0:T(8,128)(2,1)}, bf16[256,256]{1,0:T(8,128)(2,1)}, u32[]{:S(2)}, u32[]{:S(2)}) %collective-permute-start.16) | collective-permute-done | bytes 131104 | tf_op jit(solution)/shard_map/ppermute | solution.py:634
  92.0 0.0 collective-permute-done.17
  92.0 1.8 %add_convert_fusion = bf16[256,256]{1,0:T(8,128)(2,1)} fusion(bf16[256,256]{1,0:T(8,128)(2,1)} %collective-permute-done.17, bf16[256,256]{1,0:T(8,128)(2,1)} %collective-permute-done.16, bf16[256,256]{1,0:T(8,128)(2,1)} %collective-permute-done.15, bf16[256,256]{1,0:T(8,128)(2,1)} %get-tuple-element.39.refs_0_), kind=kLoop, calls=%fused_computation | loop fusion | flops 524288 | bytes 655360 | tf_op jit(solution)/shard_map/convert_element_type | solution.py:643
  93.8 0.0 collective-permute-done.14.refs_3_
  93.8 2.5 %join_heads.1 = (bf16[256,256]{1,0:T(8,128)(2,1)}, bf16[256,256]{1,0:T(8,128)(2,1)}, bf16[256,256]{1,0:T(8,128)(2,1)}) custom-call(s32[14]{0:T(128)} %stack.59.refs_0_.refs_3_.refs_1_, bf16[256,128]{1,0:T(8,128)(2,1)} %get-tuple-element.34.refs_1_, bf16[256,256]{1,0:T(8,128)(2,1)} %get-tuple-element.42.refs_2_, bf16[256,384]{1,0:T(8,128)(2,1)} %collective-permute-done.14.refs_3_), custom_call_target="tpu_custom_call" | custom-call | flops 2000000000 | bytes 6000000 | tf_op jit(solution)/shard_map/join_heads/pallas_call | solution.py:56
Async XLA Ops:
  0.6 26.5 %collective-permute-start.3 = (bf16[256,2048]{1,0:T(8,128)(2,1)}, bf16[256,2048]{1,0:T(8,128)(2,1)}, u32[]{:S(2)}, u32[]{:S(2)}) collective-permute-start(bf16[256,2048]{1,0:T(8,128)(2,1)} %bitcast.21), channel_id=1, source_target_pairs={{0,1},{1,0},{2,3},{3,2},{4,5},{5,4},{6,7},{7,6},{8,9},{9,8},{10,11... | collective-permute-start | bytes 3145736 | tf_op jit(solution)/shard_map/ppermute | solution.py:595
  6.7 7.5 %collective-permute-start = (bf16[256,256]{1,0:T(8,128)(2,1)}, bf16[256,256]{1,0:T(8,128)(2,1)}, u32[]{:S(2)}, u32[]{:S(2)}) collective-permute-start(bf16[256,256]{1,0:T(8,128)(2,1)} %get-tuple-element.27), channel_id=1, source_target_pairs={{0,2},{2,0},{4,6},{6,4},{8,10},{10,8},{12,14},{14,12},{1,3},{3,1},... | collective-permute-start | bytes 393224 | tf_op jit(solution)/shard_map/ppermute | solution.py:598
  8.2 8.8 %collective-permute-start.2 = (bf16[256,256]{1,0:T(8,128)(2,1)}, bf16[256,256]{1,0:T(8,128)(2,1)}, u32[]{:S(2)}, u32[]{:S(2)}) collective-permute-start(bf16[256,256]{1,0:T(8,128)(2,1)} %get-tuple-element.28.refs_6_), channel_id=1, source_target_pairs={{0,12},{2,14},{4,0},{6,2},{8,4},{10,6},{12,8},{14,10},{1,13},{3,15... | collective-permute-start | bytes 393224 | tf_op jit(solution)/shard_map/ppermute | solution.py:600
  11.8 8.6 %collective-permute-start.1 = (bf16[256,256]{1,0:T(8,128)(2,1)}, bf16[256,256]{1,0:T(8,128)(2,1)}, u32[]{:S(2)}, u32[]{:S(2)}) collective-permute-start(bf16[256,256]{1,0:T(8,128)(2,1)} %get-tuple-element.28.refs_6_), channel_id=1, source_target_pairs={{0,4},{2,6},{4,8},{6,10},{8,12},{10,14},{12,0},{14,2},{1,5},{3,7},... | collective-permute-start | bytes 393224 | tf_op jit(solution)/shard_map/ppermute | solution.py:600
  11.8 24.3 %collective-permute-start.6 = (bf16[256,256]{1,0:T(8,128)(2,1)}, bf16[256,256]{1,0:T(8,128)(2,1)}, u32[]{:S(2)}, u32[]{:S(2)}) collective-permute-start(bf16[256,256]{1,0:T(8,128)(2,1)} %get-tuple-element.28.refs_6_), channel_id=1, source_target_pairs={{0,8},{2,10},{4,12},{6,14},{8,0},{10,2},{12,4},{14,6},{1,9},{3,11}... | collective-permute-start | bytes 393224 | tf_op jit(solution)/shard_map/ppermute | solution.py:600
  14.2 22.1 %collective-permute-start.8 = (bf16[256,256]{1,0:T(8,128)(2,1)}, bf16[256,256]{1,0:T(8,128)(2,1)}, u32[]{:S(2)}, u32[]{:S(2)}) collective-permute-start(bf16[256,256]{1,0:T(8,128)(2,1)} %collective-permute-done.refs_0_.refs_7_), channel_id=1, source_target_pairs={{0,12},{2,14},{4,0},{6,2},{8,4},{10,6},{12,8},{14,10},{1,13},{3,15... | collective-permute-start | bytes 393224 | tf_op jit(solution)/shard_map/ppermute | solution.py:600
  17.0 19.3 %collective-permute-start.7 = (bf16[256,256]{1,0:T(8,128)(2,1)}, bf16[256,256]{1,0:T(8,128)(2,1)}, u32[]{:S(2)}, u32[]{:S(2)}) collective-permute-start(bf16[256,256]{1,0:T(8,128)(2,1)} %collective-permute-done.refs_0_.refs_7_), channel_id=1, source_target_pairs={{0,8},{2,10},{4,12},{6,14},{8,0},{10,2},{12,4},{14,6},{1,9},{3,11}... | collective-permute-start | bytes 393224 | tf_op jit(solution)/shard_map/ppermute | solution.py:600
  20.4 15.8 %collective-permute-start.5 = (bf16[256,256]{1,0:T(8,128)(2,1)}, bf16[256,256]{1,0:T(8,128)(2,1)}, u32[]{:S(2)}, u32[]{:S(2)}) collective-permute-start(bf16[256,256]{1,0:T(8,128)(2,1)} %collective-permute-done.refs_0_.refs_7_), channel_id=1, source_target_pairs={{0,4},{2,6},{4,8},{6,10},{8,12},{10,14},{12,0},{14,2},{1,5},{3,7},... | collective-permute-start | bytes 393224 | tf_op jit(solution)/shard_map/ppermute | solution.py:600
  30.7 5.6 %collective-permute-start.4 = (bf16[2,128,256]{2,1,0:T(8,128)(2,1)}, bf16[2,128,256]{2,1,0:T(8,128)(2,1)}, u32[]{:S(2)}, u32[]{:S(2)}) collective-permute-start(bf16[2,128,256]{2,1,0:T(8,128)(2,1)} %get-tuple-element.30), channel_id=1, source_target_pairs={{0,2},{2,0},{4,6},{6,4},{8,10},{10,8},{12,14},{14,12},{1,3},{3,1},... | collective-permute-start | bytes 393224 | tf_op jit(solution)/shard_map/ppermute | solution.py:609
  36.2 19.9 %collective-permute-start.12 = (bf16[2,4,256,256]{3,2,1,0:T(8,128)(2,1)}, bf16[2,4,256,256]{3,2,1,0:T(8,128)(2,1)}, u32[]{:S(2)}, u32[]{:S(2)}) collective-permute-start(bf16[2,4,256,256]{3,2,1,0:T(8,128)(2,1)} %get-tuple-element.38), channel_id=1, source_target_pairs={{0,16},{16,0},{1,17},{17,1},{2,18},{18,2},{3,19},{19,3},{4,20},{20... | collective-permute-start | bytes 3145736 | tf_op jit(solution)/shard_map/ppermute | solution.py:612
  45.2 5.1 %copy-start.2 = (bf16[128,256]{1,0:T(8,128)(2,1)S(1)}, bf16[128,256]{1,0:T(8,128)(2,1)}, u32[]{:S(2)}) copy-start(bf16[128,256]{1,0:T(8,128)(2,1)} %get-tuple-element.36) | copy-start | bytes 196612
  45.2 6.9 %copy-start = (bf16[128,256]{1,0:T(8,128)(2,1)S(1)}, bf16[128,256]{1,0:T(8,128)(2,1)}, u32[]{:S(2)}) copy-start(bf16[128,256]{1,0:T(8,128)(2,1)} %get-tuple-element.35.refs_1_) | copy-start | bytes 196612
  45.2 39.8 %all-to-all-start = ((bf16[4,2,256,256]{3,2,1,0:T(8,128)(2,1)}), bf16[4,2,256,256]{3,2,1,0:T(8,128)(2,1)}, u32[]{:S(2)}, u32[]{:S(2)}) async-start(bf16[4,2,256,256]{3,2,1,0:T(8,128)(2,1)} %get-tuple-element.41), calls=%async_computation | async-start | bytes 2097152 | tf_op jit(solution)/shard_map/all_to_all | solution.py:619
  50.2 4.1 %collective-permute-start.11 = (bf16[128,256]{1,0:T(8,128)(2,1)S(1)}, bf16[128,256]{1,0:T(8,128)(2,1)S(1)}, u32[]{:S(2)}, u32[]{:S(2)}) collective-permute-start(bf16[128,256]{1,0:T(8,128)(2,1)S(1)} %copy-done.2), channel_id=1, source_target_pairs={{0,18},{2,16},{4,22},{6,20},{8,26},{10,24},{12,30},{14,28},{16,2},... | collective-permute-start | bytes 196616 | tf_op jit(solution)/shard_map/ppermute | solution.py:628
  50.5 5.5 %collective-permute-start.9 = (bf16[128,256]{1,0:T(8,128)(2,1)S(1)}, bf16[128,256]{1,0:T(8,128)(2,1)S(1)}, u32[]{:S(2)}, u32[]{:S(2)}) collective-permute-start(bf16[128,256]{1,0:T(8,128)(2,1)S(1)} %copy-done.2), channel_id=1, source_target_pairs={{0,2},{2,0},{4,6},{6,4},{8,10},{10,8},{12,14},{14,12},{1,3},{3,1},... | collective-permute-start | bytes 196616 | tf_op jit(solution)/shard_map/ppermute | solution.py:628
  52.0 4.0 %collective-permute-start.10 = (bf16[128,256]{1,0:T(8,128)(2,1)S(1)}, bf16[128,256]{1,0:T(8,128)(2,1)S(1)}, u32[]{:S(2)}, u32[]{:S(2)}) collective-permute-start(bf16[128,256]{1,0:T(8,128)(2,1)S(1)} %copy-done), channel_id=1, source_target_pairs={{0,16},{2,18},{4,20},{6,22},{8,24},{10,26},{12,28},{14,30},{16,0},... | collective-permute-start | bytes 196616 | tf_op jit(solution)/shard_map/ppermute | solution.py:628
  54.3 1.7 %copy-start.1 = (bf16[128,256]{1,0:T(8,128)(2,1)}, bf16[128,256]{1,0:T(8,128)(2,1)S(1)}, u32[]{:S(2)}) copy-start(bf16[128,256]{1,0:T(8,128)(2,1)S(1)} %collective-permute-done.11.refs_4_) | copy-start | bytes 196612
  56.0 0.6 copy-start.3
  56.0 0.6 copy-start.4
  60.6 14.1 %collective-permute-start.13 = (bf16[4,256,256]{2,1,0:T(8,128)(2,1)}, bf16[4,256,256]{2,1,0:T(8,128)(2,1)}, u32[]{:S(2)}, u32[]{:S(2)}) collective-permute-start(bf16[4,256,256]{2,1,0:T(8,128)(2,1)} %weight_sent.1), channel_id=1, source_target_pairs={{0,2},{2,0},{4,6},{6,4},{8,10},{10,8},{12,14},{14,12},{1,3},{3,1},... | collective-permute-start | bytes 1572872 | tf_op jit(solution)/shard_map/ppermute | solution.py:631
  78.9 9.1 %collective-permute-start.15 = (bf16[256,256]{1,0:T(8,128)(2,1)}, bf16[256,256]{1,0:T(8,128)(2,1)}, u32[]{:S(2)}, u32[]{:S(2)}) collective-permute-start(bf16[256,256]{1,0:T(8,128)(2,1)} %get-tuple-element.47), channel_id=1, source_target_pairs={{0,4},{2,6},{4,8},{6,10},{8,12},{10,14},{12,0},{14,2},{1,5},{3,7},... | collective-permute-start | bytes 393224 | tf_op jit(solution)/shard_map/ppermute | solution.py:634
  81.2 10.8 %collective-permute-start.16 = (bf16[256,256]{1,0:T(8,128)(2,1)}, bf16[256,256]{1,0:T(8,128)(2,1)}, u32[]{:S(2)}, u32[]{:S(2)}) collective-permute-start(bf16[256,256]{1,0:T(8,128)(2,1)} %get-tuple-element.48), channel_id=1, source_target_pairs={{0,8},{2,10},{4,12},{6,14},{8,0},{10,2},{12,4},{14,6},{1,9},{3,11}... | collective-permute-start | bytes 393224 | tf_op jit(solution)/shard_map/ppermute | solution.py:634
  83.6 8.5 %collective-permute-start.17 = (bf16[256,256]{1,0:T(8,128)(2,1)}, bf16[256,256]{1,0:T(8,128)(2,1)}, u32[]{:S(2)}, u32[]{:S(2)}) collective-permute-start(bf16[256,256]{1,0:T(8,128)(2,1)} %get-tuple-element.49), channel_id=1, source_target_pairs={{0,12},{2,14},{4,0},{6,2},{8,4},{10,6},{12,8},{14,10},{1,13},{3,15... | collective-permute-start | bytes 393224 | tf_op jit(solution)/shard_map/ppermute | solution.py:634
  87.1 6.7 %collective-permute-start.14 = (bf16[256,384]{1,0:T(8,128)(2,1)}, bf16[256,384]{1,0:T(8,128)(2,1)}, u32[]{:S(2)}, u32[]{:S(2)}) collective-permute-start(bf16[256,384]{1,0:T(8,128)(2,1)} %get-tuple-element.43), channel_id=1, source_target_pairs={{0,2},{2,0},{4,6},{6,4},{8,10},{10,8},{12,14},{14,12},{1,3},{3,1},... | collective-permute-start | bytes 589832 | tf_op jit(solution)/shard_map/ppermute | solution.py:637

commit v15 on v14

--- a/solution.py
+++ b/solution.py
@@ -387,79 +387,95 @@
     )(at, *grads)
 
 
-def weight_kernel(doc_count, sent, at_ref, *refs):
+def weight_kernel(doc_count, side, steps, at_ref, *refs):
     attn, refs = refs[: INNER * doc_count], refs[INNER * doc_count :]
     grads, refs = refs[:doc_count], refs[doc_count:]
-    if sent:
-        out, refs = refs[0], refs[1:]
-        outs = [out.at[k] for k in range(out.shape[0])]
-    else:
-        recv, refs = refs[0], refs[1:]
-        outs, refs = refs[: recv.shape[0]], refs[recv.shape[0] :]
-        recv_s, recv_sem, refs = refs[0], refs[1], refs[2:]
-    attn_s, grad_s, out_s, attn_sem, grad_sem, out_sem = refs
-    outer, feats, _ = out_s.shape
-    half = feats // INNER
+    out, attn_s, grad_s, out_s, attn_sem, grad_sem, out_sem = refs
+    half = out.shape[1] // INNER
     attn_loads, grad_loads = [], []
     for doc in range(doc_count):
-        for side in range(INNER):
-            at = (1 - at_ref[0]) if side else at_ref[0]
-            index = doc * INNER + side
+        for group in range(INNER):
+            at = (1 - at_ref[0]) if group else at_ref[0]
+            index = doc * INNER + group
             target = attn_s.at[doc, pl.ds(pl.multiple_of(at * half, half), half)]
             attn_loads.append(begin(attn[index], target, attn_sem.at[index]))
-    for k in range(outer):
-        loads = [
-            begin(grads[doc].at[int(sent), k], grad_s.at[doc, k], grad_sem.at[doc * outer + k])
-            for doc in range(doc_count)
-        ]
-        if not sent:
-            loads.append(begin(recv.at[k], recv_s.at[k], recv_sem.at[k]))
-        grad_loads.append(loads)
+    for index, step in enumerate(steps):
+        for doc in range(doc_count):
+            sem = grad_sem.at[doc * len(steps) + index]
+            grad_loads.append(begin(grads[doc].at[side, step], grad_s.at[doc, index], sem))
     for load in attn_loads:
         load.wait()
     stores = []
-    for k in range(outer):
+    for index in range(len(steps)):
         term = 0.0
         for doc in range(doc_count):
-            grad_loads[k][doc].wait()
-            term = term + product(attn_s[doc], grad_s[doc, k])
-        if not sent:
-            grad_loads[k][doc_count].wait()
-            term = term + recv_s[k].astype(jnp.float32)
-        out_s[k] = term.astype(out_s.dtype)
-        stores.append(begin(out_s.at[k], outs[k], out_sem.at[k]))
+            grad_loads[index * doc_count + doc].wait()
+            term = term + product(attn_s[doc], grad_s[doc, index])
+        out_s[index] = term.astype(out_s.dtype)
+        stores.append(begin(out_s.at[index], out.at[index], out_sem.at[index]))
     for store in stores:
         store.wait()
 
 
-def weight_terms(at, attn, grads, recv=None, after=()):
+def weight_terms(at, attn, grads, side, steps, name, after=()):
     half, rows = attn[0].shape
     feats = half * INNER
-    doc_count = len(grads)
-    _, outer, _, width = grads[0].shape
-    sent = recv is None
-    operands = [*attn, *grads] + ([] if sent else [recv])
-    scratch = [
-        pltpu.VMEM((doc_count, feats, rows), jnp.bfloat16),
-        pltpu.VMEM((doc_count, outer, rows, width), jnp.bfloat16),
-        pltpu.VMEM((outer, feats, width), jnp.bfloat16),
-        pltpu.SemaphoreType.DMA((len(attn),)),
-        pltpu.SemaphoreType.DMA((doc_count * outer,)),
-        pltpu.SemaphoreType.DMA((outer,)),
-    ]
-    if not sent:
-        added = [pltpu.VMEM((outer, feats, width), jnp.bfloat16), pltpu.SemaphoreType.DMA((outer,))]
-        scratch = added + scratch
-    return call(
-        functools.partial(weight_kernel, doc_count, sent),
-        bf16(outer, feats, width) if sent else [bf16(feats, width)] * outer,
-        [SMEM] + [ANY] * len(operands),
-        ANY if sent else [ANY] * outer,
-        scratch,
+    doc_count, count = len(grads), len(steps)
+    width = grads[0].shape[3]
+    return call(
+        functools.partial(weight_kernel, doc_count, side, steps),
+        bf16(count, feats, width),
+        [SMEM] + [ANY] * (len(attn) + doc_count),
+        ANY,
+        [
+            pltpu.VMEM((doc_count, feats, rows), jnp.bfloat16),
+            pltpu.VMEM((doc_count, count, rows, width), jnp.bfloat16),
+            pltpu.VMEM((count, feats, width), jnp.bfloat16),
+            pltpu.SemaphoreType.DMA((len(attn),)),
+            pltpu.SemaphoreType.DMA((doc_count * count,)),
+            pltpu.SemaphoreType.DMA((count,)),
+        ],
         4,
-        "weight_sent" if sent else "weight_kept",
+        name,
         after,
-    )(at, *operands)
+    )(at, *attn, *grads)
+
+
+def weight_add_kernel(first, keep, recv, *refs):
+    count = recv.shape[0]
+    outs, (held_s, out_s, sem, out_sem) = refs[:count], refs[count:]
+    loads = []
+    for index in range(count):
+        loads.append(begin(keep.at[first + index], held_s.at[0, index], sem.at[2 * index]))
+        loads.append(begin(recv.at[index], held_s.at[1, index], sem.at[2 * index + 1]))
+    stores = []
+    for index in range(count):
+        loads[2 * index].wait()
+        loads[2 * index + 1].wait()
+        summed = held_s[0, index].astype(jnp.float32) + held_s[1, index].astype(jnp.float32)
+        out_s[index] = summed.astype(jnp.bfloat16)
+        stores.append(begin(out_s.at[index], outs[index], out_sem.at[index]))
+    for store in stores:
+        store.wait()
+
+
+def weight_add(first, keep, recv, after):
+    count, feats, width = recv.shape
+    return call(
+        functools.partial(weight_add_kernel, first),
+        [bf16(feats, width)] * count,
+        [ANY] * 2,
+        [ANY] * count,
+        [
+            pltpu.VMEM((2, count, feats, width), jnp.bfloat16),
+            pltpu.VMEM((count, feats, width), jnp.bfloat16),
+            pltpu.SemaphoreType.DMA((2 * count,)),
+            pltpu.SemaphoreType.DMA((count,)),
+        ],
+        2,
+        "weight_add",
+        after,
+    )(keep, recv)
 
 
 def add_kernel(dq_theirs, terms, mine, theirs, *scratch):
@@ -627,16 +643,24 @@
             axes = ("dp", "ctx") if step else "ctx"
             attn.append(lax.ppermute(held, axes, pairs) if step or side else held)
 
-    send = weight_terms(at, attn, grad_blocks)
-    weight_recv = lax.ppermute(send, "ctx", ctx_pairs(0, 1))
-    weight_sums = weight_terms(at, attn, grad_blocks, weight_recv)
+    order = list(range(1, outer)) + [0]
+    halves = [order[: outer // 2], order[outer // 2 :]]
+    recvs, previous = [], ()
+    for steps in halves:
+        send = weight_terms(at, attn, grad_blocks, 1, steps, "weight_sent", previous)
+        recvs.append(lax.ppermute(send, "ctx", ctx_pairs(0, 1)))
+        previous = (send,)
+    keep = weight_terms(at, attn, grad_blocks, 0, order, "weight_kept", previous)
+    weight_sums = []
+    for recv in recvs:
+        weight_sums = [*weight_sums, *weight_add(len(weight_sums), keep, recv, weight_sums[-1:])]
     weight_parts = [
-        lax.ppermute(weight_sums[step], "ctx", ctx_pairs(step, 0)) for step in range(1, outer)
-    ]
-    terms_mine, terms_theirs = add_terms(dq_theirs, terms, (weight_sums[0],))
+        lax.ppermute(held, "ctx", ctx_pairs(step, 0)) for step, held in zip(order[:-1], weight_sums)
+    ]
+    terms_mine, terms_theirs = add_terms(dq_theirs, terms, (weight_sums[-1],))
     terms_recv = lax.ppermute(terms_theirs, "ctx", ctx_pairs(0, 1))
     grad_q, grad_k, grad_v = join_heads(at, dq_mine, terms_mine, terms_recv)
-    grad_weight = weight_sums[0].astype(jnp.float32)
+    grad_weight = weight_sums[-1].astype(jnp.float32)
     for part in weight_parts:
         grad_weight = grad_weight + part.astype(jnp.float32)
 

time: 97.4 us -> 92.6 us (0.951)
  waiting for transfers between devices: 24 us -> 11.8 us
  Pallas kernels: 35.5 us -> 41.2 us
  starting transfers between devices: 31.7 us -> 33.6 us
    ppermute x4 -> x5, waiting for transfers between devices: 17.2 us -> 4.56 us  [the longest x3 4.2 us: per_device(): lax.ppermute(held, 'ctx', ctx_pairs(step, 0))]
    pallas_call x9 -> x12, Pallas kernels: 35.5 us -> 41.2 us  [placed(): return run(*args)]
    ppermute x4 -> x5, starting transfers between devices: 7.07 us -> 8.96 us  [the longest x3 6.8 us: per_device(): lax.ppermute(held, 'ctx', ctx_pairs(step, 0))]
  transfers between devices with their start and end apart: 19 -> 20, of which waited for: 6 -> 7; matrix products, arithmetic and copies ran while one was open for 4% -> 4% of each run, Pallas kernels for 34% -> 42%
where the time goes in v15:
time: 92.6 us; the launch traced here: 91.9 us
  Pallas kernels  41.2 us (44%)
  starting transfers between devices  33.6 us (36%)
  waiting for transfers between devices  11.8 us (13%)
  local copies, waits for them, and re-layouts  2.66 us (3%)
  other arithmetic  1.82 us (2%)
    pallas_call x12, Pallas kernels, placed(): return run(*args)  41.2 us
    ppermute x6, starting transfers between devices, per_device(): lax.ppermute(kv_recv if side else kv_mine, 'ctx', ctx_pairs(step, 0))  10.4 us
    ppermute x3, starting transfers between devices, per_device(): lax.ppermute(held, 'ctx', ctx_pairs(step, 0))  6.8 us
    all_to_all x1, starting transfers between devices, per_device(): lax.all_to_all(parts, 'ctx', split_axis=0, concat_axis=0, axis_index_grou...  5 us
    ppermute x3, waiting for transfers between devices, per_device(): lax.ppermute(held, 'ctx', ctx_pairs(step, 0))  4.2 us
    ppermute x3, waiting for transfers between devices, per_device(): attn.append(lax.ppermute(held, axes, pairs) if step or side else held)  3.93 us
    ppermute x1, starting transfers between devices, per_device(): lax.ppermute(grad_own, 'tp', shift_pairs(tp_count, -step))  3.03 us
    ppermute x2, starting transfers between devices, per_device(): recvs.append(lax.ppermute(send, 'ctx', ctx_pairs(0, 1)))  2.16 us
  transfers between devices with their start and end apart: 20, of which 7 were waited for; matrix products, arithmetic and copies ran while one was open for 4% of the time, Pallas kernels for 42%

profile of v15, /device:TPU:0, one launch (start us, length us, event | category | flops | bytes accessed | tf_op | source)
XLA Modules:
  0.0 91.9 jit_solution(13208761748270921340)
XLA Ops:
  0.6 3.0 %collective-permute-start.3 = (bf16[256,2048]{1,0:T(8,128)(2,1)}, bf16[256,2048]{1,0:T(8,128)(2,1)}, u32[]{:S(2)}, u32[]{:S(2)}) collective-permute-start(bf16[256,2048]{1,0:T(8,128)(2,1)} %bitcast.21), channel_id=1, source_target_pairs={{0,1},{1,0},{2,3},{3,2},{4,5},{5,4},{6,7},{7,6},{8,9},{9,8},{10,11... | collective-permute-start | bytes 3145736 | tf_op jit(solution)/shard_map/ppermute | solution.py:611
  3.7 0.7 stack.59.refs_0_.refs_3_.refs_1_
  4.3 2.3 %part_heads.1 = (bf16[256,256]{1,0:T(8,128)(2,1)}, bf16[256,256]{1,0:T(8,128)(2,1)}) custom-call(s32[14]{0:T(128)} %stack.59.refs_0_.refs_3_.refs_1_, bf16[256,256]{1,0:T(8,128)(2,1)} %bitcast.24, bf16[256,256]{1,0:T(8,128)(2,1)} %bitcast.25), custom_call_target="tpu_custom_call" | custom-call | flops 2000000000 | bytes 6000000 | tf_op jit(solution)/shard_map/part_heads/pallas_call | solution.py:56
  6.7 1.6 %collective-permute-start = (bf16[256,256]{1,0:T(8,128)(2,1)}, bf16[256,256]{1,0:T(8,128)(2,1)}, u32[]{:S(2)}, u32[]{:S(2)}) collective-permute-start(bf16[256,256]{1,0:T(8,128)(2,1)} %get-tuple-element.27), channel_id=1, source_target_pairs={{0,2},{2,0},{4,6},{6,4},{8,10},{10,8},{12,14},{14,12},{1,3},{3,1},... | collective-permute-start | bytes 393224 | tf_op jit(solution)/shard_map/ppermute | solution.py:614
  8.2 3.6 %collective-permute-start.2 = (bf16[256,256]{1,0:T(8,128)(2,1)}, bf16[256,256]{1,0:T(8,128)(2,1)}, u32[]{:S(2)}, u32[]{:S(2)}) collective-permute-start(bf16[256,256]{1,0:T(8,128)(2,1)} %get-tuple-element.28.refs_6_), channel_id=1, source_target_pairs={{0,12},{2,14},{4,0},{6,2},{8,4},{10,6},{12,8},{14,10},{1,13},{3,15... | collective-permute-start | bytes 393224 | tf_op jit(solution)/shard_map/ppermute | solution.py:616
  11.8 0.0 collective-permute-start.1
  11.8 1.0 %collective-permute-start.6 = (bf16[256,256]{1,0:T(8,128)(2,1)}, bf16[256,256]{1,0:T(8,128)(2,1)}, u32[]{:S(2)}, u32[]{:S(2)}) collective-permute-start(bf16[256,256]{1,0:T(8,128)(2,1)} %get-tuple-element.28.refs_6_), channel_id=1, source_target_pairs={{0,8},{2,10},{4,12},{6,14},{8,0},{10,2},{12,4},{14,6},{1,9},{3,11}... | collective-permute-start | bytes 393224 | tf_op jit(solution)/shard_map/ppermute | solution.py:616
  12.9 1.3 %copy.11.refs_4_ = s32[8,3]{1,0:T(8,128)} copy(s32[8,3]{0,1:T(4,128)} %param.12) | data formatting | bytes 192 | tf_op args[5]
  14.2 0.0 collective-permute-done.refs_0_.refs_7_
  14.2 2.8 %collective-permute-start.8 = (bf16[256,256]{1,0:T(8,128)(2,1)}, bf16[256,256]{1,0:T(8,128)(2,1)}, u32[]{:S(2)}, u32[]{:S(2)}) collective-permute-start(bf16[256,256]{1,0:T(8,128)(2,1)} %collective-permute-done.refs_0_.refs_7_), channel_id=1, source_target_pairs={{0,12},{2,14},{4,0},{6,2},{8,4},{10,6},{12,8},{14,10},{1,13},{3,15... | collective-permute-start | bytes 393224 | tf_op jit(solution)/shard_map/ppermute | solution.py:616
  17.0 0.0 collective-permute-done.2.refs_2_.refs_12_
  17.0 2.0 %collective-permute-start.7 = (bf16[256,256]{1,0:T(8,128)(2,1)}, bf16[256,256]{1,0:T(8,128)(2,1)}, u32[]{:S(2)}, u32[]{:S(2)}) collective-permute-start(bf16[256,256]{1,0:T(8,128)(2,1)} %collective-permute-done.refs_0_.refs_7_), channel_id=1, source_target_pairs={{0,8},{2,10},{4,12},{6,14},{8,0},{10,2},{12,4},{14,6},{1,9},{3,11}... | collective-permute-start | bytes 393224 | tf_op jit(solution)/shard_map/ppermute | solution.py:616
  19.0 1.4 %collective-permute-done.1.refs_1_.refs_8_ = bf16[256,256]{1,0:T(8,128)(2,1)} collective-permute-done((bf16[256,256]{1,0:T(8,128)(2,1)}, bf16[256,256]{1,0:T(8,128)(2,1)}, u32[]{:S(2)}, u32[]{:S(2)}) %collective-permute-start.1) | collective-permute-done | bytes 131104 | tf_op jit(solution)/shard_map/ppermute | solution.py:616
  20.4 1.0 %collective-permute-start.5 = (bf16[256,256]{1,0:T(8,128)(2,1)}, bf16[256,256]{1,0:T(8,128)(2,1)}, u32[]{:S(2)}, u32[]{:S(2)}) collective-permute-start(bf16[256,256]{1,0:T(8,128)(2,1)} %collective-permute-done.refs_0_.refs_7_), channel_id=1, source_target_pairs={{0,4},{2,6},{4,8},{6,10},{8,12},{10,14},{12,0},{14,2},{1,5},{3,7},... | collective-permute-start | bytes 393224 | tf_op jit(solution)/shard_map/ppermute | solution.py:616
  21.4 4.3 %prelude.1 = (f32[256,256]{1,0:T(8,128)}, bf16[2048,128]{1,0:T(8,128)(2,1)}, f32[8,512]{1,0:T(8,128)}) custom-call(bf16[256,256]{1,0:T(8,128)(2,1)} %collective-permute-done.refs_0_.refs_7_, bf16[256,256]{1,0:T(8,128)(2,1)} %collective-permute-done.1.refs_1_.refs_8_, bf16[256,256]{1,0:T(8,128)(2,1)} %collective-permute-done.2.refs_2_.refs_12_, ...), custom_call_target="tpu_custom_call" | custom-call | flops 4000000000 | bytes 12000000 | tf_op jit(solution)/shard_map/prelude/pallas_call | solution.py:56
  25.7 1.4 %collective-permute-done.3.refs_4_.refs_3_ = bf16[256,2048]{1,0:T(8,128)(2,1)} collective-permute-done((bf16[256,2048]{1,0:T(8,128)(2,1)}, bf16[256,2048]{1,0:T(8,128)(2,1)}, u32[]{:S(2)}, u32[]{:S(2)}) %collective-permute-start.3) | collective-permute-done | bytes 1048608 | tf_op jit(solution)/shard_map/ppermute | solution.py:611
  27.1 3.5 %grad_heads.1 = (bf16[128,256]{1,0:T(8,128)(2,1)}, bf16[2,128,256]{2,1,0:T(8,128)(2,1)}) custom-call(s32[14]{0:T(128)} %stack.59.refs_0_.refs_3_.refs_1_, f32[256,256]{1,0:T(8,128)} %get-tuple-element.29.refs_1_, bf16[256,256]{1,0:T(8,128)(2,1)} %bitcast.26, bf16[256,4096]{1,0:T(8,128)(2,1)} %refs_3_.1, bf16[256,2048]{1,0:T(8,128)(2,1)} %collective-permute-done.3.refs_4_.refs_3_), custom_call_target="tpu_custom_call" | custom-call | flops 3000000000 | bytes 9000000 | tf_op jit(solution)/shard_map/grad_heads/pallas_call | solution.py:56
  30.7 1.8 %collective-permute-start.4 = (bf16[2,128,256]{2,1,0:T(8,128)(2,1)}, bf16[2,128,256]{2,1,0:T(8,128)(2,1)}, u32[]{:S(2)}, u32[]{:S(2)}) collective-permute-start(bf16[2,128,256]{2,1,0:T(8,128)(2,1)} %get-tuple-element.30), channel_id=1, source_target_pairs={{0,2},{2,0},{4,6},{6,4},{8,10},{10,8},{12,14},{14,12},{1,3},{3,1},... | collective-permute-start | bytes 393224 | tf_op jit(solution)/shard_map/ppermute | solution.py:625
  32.4 3.7 %pick_columns.1 = (bf16[2,4,256,256]{3,2,1,0:T(8,128)(2,1)}, bf16[2,4,256,256]{3,2,1,0:T(8,128)(2,1)}) custom-call(bf16[128,256]{1,0:T(8,128)(2,1)} %get-tuple-element.31.refs_3_.refs_0_, s32[14]{0:T(128)} %stack.59.refs_0_.refs_3_.refs_1_, bf16[256,2048]{1,0:T(8,128)(2,1)} %bitcast.23, bf16[256,2048]{1,0:T(8,128)(2,1)} %collective-permute-done.3.refs_4_.refs_3_), custom_call_target="tpu_custom_call" | custom-call | flops 3000000000 | bytes 9000000 | tf_op jit(solution)/shard_map/pick_columns/pallas_call | solution.py:56
  36.2 0.0 collective-permute-done.6.refs_10_
  36.2 0.1 collective-permute-start.12
  36.3 0.0 collective-permute-done.8.refs_13_
  36.3 0.0 collective-permute-done.7.refs_11_
  36.3 0.0 collective-permute-done.5.refs_9_
  36.3 0.0 collective-permute-done.4.refs_2_
  36.3 8.9 %attention.1 = (bf16[128,256]{1,0:T(8,128)(2,1)}, bf16[128,256]{1,0:T(8,128)(2,1)}, bf16[256,128]{1,0:T(8,128)(2,1)}, bf16[256,128]{1,0:T(8,128)(2,1)}, bf16[4,2,256,256]{3,2,1,0:T(8,128)(2,1)}) custom-call(s32[14]{0:T(128)} %stack.59.refs_0_.refs_3_.refs_1_, bf16[256,256]{1,0:T(8,128)(2,1)} %bitcast.27, ...), custom_call_target="tpu_custom_call" | custom-call | flops 20000000000 | bytes 60000000 | tf_op jit(solution)/shard_map/attention/pallas_call | solution.py:56
  45.2 0.0 copy-start.1
  45.2 0.0 copy-start
  45.2 5.0 %all-to-all-start = ((bf16[4,2,256,256]{3,2,1,0:T(8,128)(2,1)}), bf16[4,2,256,256]{3,2,1,0:T(8,128)(2,1)}, u32[]{:S(2)}, u32[]{:S(2)}) async-start(bf16[4,2,256,256]{3,2,1,0:T(8,128)(2,1)} %get-tuple-element.42), calls=%async_computation | async-start | bytes 2097152 | tf_op jit(solution)/shard_map/all_to_all | solution.py:635
  50.2 0.0 copy-done.1
  50.2 0.3 collective-permute-start.11
  50.6 1.5 %collective-permute-start.9 = (bf16[128,256]{1,0:T(8,128)(2,1)S(1)}, bf16[128,256]{1,0:T(8,128)(2,1)S(1)}, u32[]{:S(2)}, u32[]{:S(2)}) collective-permute-start(bf16[128,256]{1,0:T(8,128)(2,1)S(1)} %copy-done.1), channel_id=1, source_target_pairs={{0,2},{2,0},{4,6},{6,4},{8,10},{10,8},{12,14},{14,12},{1,3},{3,1},... | collective-permute-start | bytes 196616 | tf_op jit(solution)/shard_map/ppermute | solution.py:644
  52.1 0.0 copy-done
  52.1 0.0 collective-permute-start.10
  52.1 2.2 %collective-permute-done.11.refs_4_.refs_5_ = bf16[128,256]{1,0:T(8,128)(2,1)S(1)} collective-permute-done((bf16[128,256]{1,0:T(8,128)(2,1)S(1)}, bf16[128,256]{1,0:T(8,128)(2,1)S(1)}, u32[]{:S(2)}, u32[]{:S(2)}) %collective-permute-start.11) | collective-permute-done | bytes 65568 | tf_op jit(solution)/shard_map/ppermute | solution.py:644
  54.3 0.0 copy-start.2
  54.3 1.7 %collective-permute-done.9.refs_2_.refs_3_ = bf16[128,256]{1,0:T(8,128)(2,1)S(1)} collective-permute-done((bf16[128,256]{1,0:T(8,128)(2,1)S(1)}, bf16[128,256]{1,0:T(8,128)(2,1)S(1)}, u32[]{:S(2)}, u32[]{:S(2)}) %collective-permute-start.9) | collective-permute-done | bytes 65568 | tf_op jit(solution)/shard_map/ppermute | solution.py:644
  56.0 0.0 collective-permute-done.10.refs_3_.refs_4_
  56.0 0.0 copy-done.2
  56.0 0.0 copy-start.4
  56.1 0.0 collective-permute-done.12.refs_6_.refs_7_
  56.1 0.6 copy-done.3
  56.7 0.0 copy-done.4
  56.7 3.1 %weight_sent.2.refs_0_ = bf16[2,256,256]{2,1,0:T(8,128)(2,1)} custom-call(s32[14]{0:T(128)} %stack.59.refs_0_.refs_3_.refs_1_, bf16[128,256]{1,0:T(8,128)(2,1)} %get-tuple-element.35.refs_1_.refs_2_, bf16[128,256]{1,0:T(8,128)(2,1)} %copy-done.3, bf16[128,256]{1,0:T(8,128)(2,1)} %copy-done.4, bf16[128,256]{1,0:T(8,128)(2,1)} %copy-done.2, ...), custom_call_target="tpu_custom_call" | custom-call | flops 4000000000 | bytes 12000000 | tf_op jit(solution)/shard_map/weight_sent/pallas_call | solution.py:56
  59.8 1.0 %collective-permute-start.13 = (bf16[2,256,256]{2,1,0:T(8,128)(2,1)}, bf16[2,256,256]{2,1,0:T(8,128)(2,1)}, u32[]{:S(2)}, u32[]{:S(2)}) collective-permute-start(bf16[2,256,256]{2,1,0:T(8,128)(2,1)} %weight_sent.2.refs_0_), channel_id=1, source_target_pairs={{0,2},{2,0},{4,6},{6,4},{8,10},{10,8},{12,14},{14,12},{1,3},{3,1},... | collective-permute-start | bytes 786440 | tf_op jit(solution)/shard_map/ppermute | solution.py:651
  60.8 3.1 %weight_sent.3.refs_0_ = bf16[2,256,256]{2,1,0:T(8,128)(2,1)} custom-call(bf16[2,256,256]{2,1,0:T(8,128)(2,1)} %weight_sent.2.refs_0_, s32[14]{0:T(128)} %stack.59.refs_0_.refs_3_.refs_1_, bf16[128,256]{1,0:T(8,128)(2,1)} %get-tuple-element.35.refs_1_.refs_2_, bf16[128,256]{1,0:T(8,128)(2,1)} %copy-done.3, bf16[128,256]{1,0:T(8,128)(2,1)} %copy-done.4, ...), custom_call_target="tpu_custom_call" | custom-call | flops 4000000000 | bytes 12000000 | tf_op jit(solution)/shard_map/weight_sent/pallas_call | solution.py:56
  63.9 1.2 %collective-permute-start.14 = (bf16[2,256,256]{2,1,0:T(8,128)(2,1)}, bf16[2,256,256]{2,1,0:T(8,128)(2,1)}, u32[]{:S(2)}, u32[]{:S(2)}) collective-permute-start(bf16[2,256,256]{2,1,0:T(8,128)(2,1)} %weight_sent.3.refs_0_), channel_id=1, source_target_pairs={{0,2},{2,0},{4,6},{6,4},{8,10},{10,8},{12,14},{14,12},{1,3},{3,1},... | collective-permute-start | bytes 786440 | tf_op jit(solution)/shard_map/ppermute | solution.py:651
  65.1 3.9 %weight_kept.1.refs_0_.refs_1_ = bf16[4,256,256]{2,1,0:T(8,128)(2,1)} custom-call(bf16[2,256,256]{2,1,0:T(8,128)(2,1)} %weight_sent.3.refs_0_, s32[14]{0:T(128)} %stack.59.refs_0_.refs_3_.refs_1_, bf16[128,256]{1,0:T(8,128)(2,1)} %get-tuple-element.35.refs_1_.refs_2_, bf16[128,256]{1,0:T(8,128)(2,1)} %copy-done.3, bf16[128,256]{1,0:T(8,128)(2,1)} %copy-done.4, ...), custom_call_target="tpu_custom_call" | custom-call | flops 4000000000 | bytes 12000000 | tf_op jit(solution)/shard_map/weight_kept/pallas_call | solution.py:56
  69.0 0.4 collective-permute-done.13.refs_1_
  69.4 1.8 %weight_add.2 = (bf16[256,256]{1,0:T(8,128)(2,1)}, bf16[256,256]{1,0:T(8,128)(2,1)}) custom-call(bf16[4,256,256]{2,1,0:T(8,128)(2,1)} %weight_kept.1.refs_0_.refs_1_, bf16[2,256,256]{2,1,0:T(8,128)(2,1)} %collective-permute-done.13.refs_1_), custom_call_target="tpu_custom_call" | custom-call | flops 2000000000 | bytes 6000000 | tf_op jit(solution)/shard_map/weight_add/pallas_call | solution.py:56
  71.2 3.0 %collective-permute-start.17 = (bf16[256,256]{1,0:T(8,128)(2,1)}, bf16[256,256]{1,0:T(8,128)(2,1)}, u32[]{:S(2)}, u32[]{:S(2)}) collective-permute-start(bf16[256,256]{1,0:T(8,128)(2,1)} %get-tuple-element.39.refs_0_), channel_id=1, source_target_pairs={{0,8},{2,10},{4,12},{6,14},{8,0},{10,2},{12,4},{14,6},{1,9},{3,11}... | collective-permute-start | bytes 393224 | tf_op jit(solution)/shard_map/ppermute | solution.py:658
  74.2 0.0 collective-permute-done.14.refs_2_
  74.2 1.8 %weight_add.3 = (bf16[256,256]{1,0:T(8,128)(2,1)}, bf16[256,256]{1,0:T(8,128)(2,1)}) custom-call(bf16[256,256]{1,0:T(8,128)(2,1)} %get-tuple-element.39.refs_0_, bf16[4,256,256]{2,1,0:T(8,128)(2,1)} %weight_kept.1.refs_0_.refs_1_, bf16[2,256,256]{2,1,0:T(8,128)(2,1)} %collective-permute-done.14.refs_2_), custom_call_target="tpu_custom_call" | custom-call | flops 2000000000 | bytes 6000000 | tf_op jit(solution)/shard_map/weight_add/pallas_call | solution.py:56
  76.0 3.8 %collective-permute-start.18 = (bf16[256,256]{1,0:T(8,128)(2,1)}, bf16[256,256]{1,0:T(8,128)(2,1)}, u32[]{:S(2)}, u32[]{:S(2)}) collective-permute-start(bf16[256,256]{1,0:T(8,128)(2,1)} %get-tuple-element.49), channel_id=1, source_target_pairs={{0,12},{2,14},{4,0},{6,2},{8,4},{10,6},{12,8},{14,10},{1,13},{3,15... | collective-permute-start | bytes 393224 | tf_op jit(solution)/shard_map/ppermute | solution.py:658
  79.9 0.0 collective-permute-start.16
  79.9 0.5 all-to-all-done.refs_2_
  80.3 2.1 %add_terms.1 = (bf16[256,256]{1,0:T(8,128)(2,1)}, bf16[256,384]{1,0:T(8,128)(2,1)}) custom-call(bf16[256,256]{1,0:T(8,128)(2,1)} %get-tuple-element.40.refs_0_, bf16[256,128]{1,0:T(8,128)(2,1)} %get-tuple-element.41.refs_1_, bf16[4,2,256,256]{3,2,1,0:T(8,128)(2,1)} %all-to-all-done.refs_2_), custom_call_target="tpu_custom_call" | custom-call | flops 2000000000 | bytes 6000000 | tf_op jit(solution)/shard_map/add_terms/pallas_call | solution.py:56
  82.4 0.9 %collective-permute-start.15 = (bf16[256,384]{1,0:T(8,128)(2,1)}, bf16[256,384]{1,0:T(8,128)(2,1)}, u32[]{:S(2)}, u32[]{:S(2)}) collective-permute-start(bf16[256,384]{1,0:T(8,128)(2,1)} %get-tuple-element.44), channel_id=1, source_target_pairs={{0,2},{2,0},{4,6},{6,4},{8,10},{10,8},{12,14},{14,12},{1,3},{3,1},... | collective-permute-start | bytes 589832 | tf_op jit(solution)/shard_map/ppermute | solution.py:661
  83.4 4.2 %collective-permute-done.18 = bf16[256,256]{1,0:T(8,128)(2,1)} collective-permute-done((bf16[256,256]{1,0:T(8,128)(2,1)}, bf16[256,256]{1,0:T(8,128)(2,1)}, u32[]{:S(2)}, u32[]{:S(2)}) %collective-permute-start.18) | collective-permute-done | bytes 131104 | tf_op jit(solution)/shard_map/ppermute | solution.py:658
  87.6 0.0 collective-permute-done.16
  87.6 0.0 collective-permute-done.17
  87.6 1.8 %add_convert_fusion = bf16[256,256]{1,0:T(8,128)(2,1)} fusion(bf16[256,256]{1,0:T(8,128)(2,1)} %collective-permute-done.18, bf16[256,256]{1,0:T(8,128)(2,1)} %collective-permute-done.17, bf16[256,256]{1,0:T(8,128)(2,1)} %collective-permute-done.16, bf16[256,256]{1,0:T(8,128)(2,1)} %get-tuple-element.40.refs_0_), kind=kLoop, calls=%fused_computation | loop fusion | flops 524288 | bytes 655360 | tf_op jit(solution)/shard_map/convert_element_type | solution.py:667
  89.4 0.0 collective-permute-done.15.refs_3_
  89.4 2.5 %join_heads.1 = (bf16[256,256]{1,0:T(8,128)(2,1)}, bf16[256,256]{1,0:T(8,128)(2,1)}, bf16[256,256]{1,0:T(8,128)(2,1)}) custom-call(s32[14]{0:T(128)} %stack.59.refs_0_.refs_3_.refs_1_, bf16[256,128]{1,0:T(8,128)(2,1)} %get-tuple-element.34.refs_1_, bf16[256,256]{1,0:T(8,128)(2,1)} %get-tuple-element.43.refs_2_, bf16[256,384]{1,0:T(8,128)(2,1)} %collective-permute-done.15.refs_3_), custom_call_target="tpu_custom_call" | custom-call | flops 2000000000 | bytes 6000000 | tf_op jit(solution)/shard_map/join_heads/pallas_call | solution.py:56
  (1 shorter events, 0.0 us)
Async XLA Ops:
  0.6 26.5 %collective-permute-start.3 = (bf16[256,2048]{1,0:T(8,128)(2,1)}, bf16[256,2048]{1,0:T(8,128)(2,1)}, u32[]{:S(2)}, u32[]{:S(2)}) collective-permute-start(bf16[256,2048]{1,0:T(8,128)(2,1)} %bitcast.21), channel_id=1, source_target_pairs={{0,1},{1,0},{2,3},{3,2},{4,5},{5,4},{6,7},{7,6},{8,9},{9,8},{10,11... | collective-permute-start | bytes 3145736 | tf_op jit(solution)/shard_map/ppermute | solution.py:611
  6.7 7.5 %collective-permute-start = (bf16[256,256]{1,0:T(8,128)(2,1)}, bf16[256,256]{1,0:T(8,128)(2,1)}, u32[]{:S(2)}, u32[]{:S(2)}) collective-permute-start(bf16[256,256]{1,0:T(8,128)(2,1)} %get-tuple-element.27), channel_id=1, source_target_pairs={{0,2},{2,0},{4,6},{6,4},{8,10},{10,8},{12,14},{14,12},{1,3},{3,1},... | collective-permute-start | bytes 393224 | tf_op jit(solution)/shard_map/ppermute | solution.py:614
  8.2 8.8 %collective-permute-start.2 = (bf16[256,256]{1,0:T(8,128)(2,1)}, bf16[256,256]{1,0:T(8,128)(2,1)}, u32[]{:S(2)}, u32[]{:S(2)}) collective-permute-start(bf16[256,256]{1,0:T(8,128)(2,1)} %get-tuple-element.28.refs_6_), channel_id=1, source_target_pairs={{0,12},{2,14},{4,0},{6,2},{8,4},{10,6},{12,8},{14,10},{1,13},{3,15... | collective-permute-start | bytes 393224 | tf_op jit(solution)/shard_map/ppermute | solution.py:616
  11.8 8.6 %collective-permute-start.1 = (bf16[256,256]{1,0:T(8,128)(2,1)}, bf16[256,256]{1,0:T(8,128)(2,1)}, u32[]{:S(2)}, u32[]{:S(2)}) collective-permute-start(bf16[256,256]{1,0:T(8,128)(2,1)} %get-tuple-element.28.refs_6_), channel_id=1, source_target_pairs={{0,4},{2,6},{4,8},{6,10},{8,12},{10,14},{12,0},{14,2},{1,5},{3,7},... | collective-permute-start | bytes 393224 | tf_op jit(solution)/shard_map/ppermute | solution.py:616
  11.8 24.4 %collective-permute-start.6 = (bf16[256,256]{1,0:T(8,128)(2,1)}, bf16[256,256]{1,0:T(8,128)(2,1)}, u32[]{:S(2)}, u32[]{:S(2)}) collective-permute-start(bf16[256,256]{1,0:T(8,128)(2,1)} %get-tuple-element.28.refs_6_), channel_id=1, source_target_pairs={{0,8},{2,10},{4,12},{6,14},{8,0},{10,2},{12,4},{14,6},{1,9},{3,11}... | collective-permute-start | bytes 393224 | tf_op jit(solution)/shard_map/ppermute | solution.py:616
  14.2 22.1 %collective-permute-start.8 = (bf16[256,256]{1,0:T(8,128)(2,1)}, bf16[256,256]{1,0:T(8,128)(2,1)}, u32[]{:S(2)}, u32[]{:S(2)}) collective-permute-start(bf16[256,256]{1,0:T(8,128)(2,1)} %collective-permute-done.refs_0_.refs_7_), channel_id=1, source_target_pairs={{0,12},{2,14},{4,0},{6,2},{8,4},{10,6},{12,8},{14,10},{1,13},{3,15... | collective-permute-start | bytes 393224 | tf_op jit(solution)/shard_map/ppermute | solution.py:616
  17.0 19.3 %collective-permute-start.7 = (bf16[256,256]{1,0:T(8,128)(2,1)}, bf16[256,256]{1,0:T(8,128)(2,1)}, u32[]{:S(2)}, u32[]{:S(2)}) collective-permute-start(bf16[256,256]{1,0:T(8,128)(2,1)} %collective-permute-done.refs_0_.refs_7_), channel_id=1, source_target_pairs={{0,8},{2,10},{4,12},{6,14},{8,0},{10,2},{12,4},{14,6},{1,9},{3,11}... | collective-permute-start | bytes 393224 | tf_op jit(solution)/shard_map/ppermute | solution.py:616
  20.4 15.9 %collective-permute-start.5 = (bf16[256,256]{1,0:T(8,128)(2,1)}, bf16[256,256]{1,0:T(8,128)(2,1)}, u32[]{:S(2)}, u32[]{:S(2)}) collective-permute-start(bf16[256,256]{1,0:T(8,128)(2,1)} %collective-permute-done.refs_0_.refs_7_), channel_id=1, source_target_pairs={{0,4},{2,6},{4,8},{6,10},{8,12},{10,14},{12,0},{14,2},{1,5},{3,7},... | collective-permute-start | bytes 393224 | tf_op jit(solution)/shard_map/ppermute | solution.py:616
  30.7 5.7 %collective-permute-start.4 = (bf16[2,128,256]{2,1,0:T(8,128)(2,1)}, bf16[2,128,256]{2,1,0:T(8,128)(2,1)}, u32[]{:S(2)}, u32[]{:S(2)}) collective-permute-start(bf16[2,128,256]{2,1,0:T(8,128)(2,1)} %get-tuple-element.30), channel_id=1, source_target_pairs={{0,2},{2,0},{4,6},{6,4},{8,10},{10,8},{12,14},{14,12},{1,3},{3,1},... | collective-permute-start | bytes 393224 | tf_op jit(solution)/shard_map/ppermute | solution.py:625
  36.2 19.8 %collective-permute-start.12 = (bf16[2,4,256,256]{3,2,1,0:T(8,128)(2,1)}, bf16[2,4,256,256]{3,2,1,0:T(8,128)(2,1)}, u32[]{:S(2)}, u32[]{:S(2)}) collective-permute-start(bf16[2,4,256,256]{3,2,1,0:T(8,128)(2,1)} %get-tuple-element.38), channel_id=1, source_target_pairs={{0,16},{16,0},{1,17},{17,1},{2,18},{18,2},{3,19},{19,3},{4,20},{20... | collective-permute-start | bytes 3145736 | tf_op jit(solution)/shard_map/ppermute | solution.py:628
  45.2 5.0 %copy-start.1 = (bf16[128,256]{1,0:T(8,128)(2,1)S(1)}, bf16[128,256]{1,0:T(8,128)(2,1)}, u32[]{:S(2)}) copy-start(bf16[128,256]{1,0:T(8,128)(2,1)} %get-tuple-element.36) | copy-start | bytes 196612
  45.2 6.8 %copy-start = (bf16[128,256]{1,0:T(8,128)(2,1)S(1)}, bf16[128,256]{1,0:T(8,128)(2,1)}, u32[]{:S(2)}) copy-start(bf16[128,256]{1,0:T(8,128)(2,1)} %get-tuple-element.35.refs_1_.refs_2_) | copy-start | bytes 196612
  45.2 35.1 %all-to-all-start = ((bf16[4,2,256,256]{3,2,1,0:T(8,128)(2,1)}), bf16[4,2,256,256]{3,2,1,0:T(8,128)(2,1)}, u32[]{:S(2)}, u32[]{:S(2)}) async-start(bf16[4,2,256,256]{3,2,1,0:T(8,128)(2,1)} %get-tuple-element.42), calls=%async_computation | async-start | bytes 2097152 | tf_op jit(solution)/shard_map/all_to_all | solution.py:635
  50.2 4.1 %collective-permute-start.11 = (bf16[128,256]{1,0:T(8,128)(2,1)S(1)}, bf16[128,256]{1,0:T(8,128)(2,1)S(1)}, u32[]{:S(2)}, u32[]{:S(2)}) collective-permute-start(bf16[128,256]{1,0:T(8,128)(2,1)S(1)} %copy-done.1), channel_id=1, source_target_pairs={{0,18},{2,16},{4,22},{6,20},{8,26},{10,24},{12,30},{14,28},{16,2},... | collective-permute-start | bytes 196616 | tf_op jit(solution)/shard_map/ppermute | solution.py:644
  50.6 5.5 %collective-permute-start.9 = (bf16[128,256]{1,0:T(8,128)(2,1)S(1)}, bf16[128,256]{1,0:T(8,128)(2,1)S(1)}, u32[]{:S(2)}, u32[]{:S(2)}) collective-permute-start(bf16[128,256]{1,0:T(8,128)(2,1)S(1)} %copy-done.1), channel_id=1, source_target_pairs={{0,2},{2,0},{4,6},{6,4},{8,10},{10,8},{12,14},{14,12},{1,3},{3,1},... | collective-permute-start | bytes 196616 | tf_op jit(solution)/shard_map/ppermute | solution.py:644
  52.1 4.0 %collective-permute-start.10 = (bf16[128,256]{1,0:T(8,128)(2,1)S(1)}, bf16[128,256]{1,0:T(8,128)(2,1)S(1)}, u32[]{:S(2)}, u32[]{:S(2)}) collective-permute-start(bf16[128,256]{1,0:T(8,128)(2,1)S(1)} %copy-done), channel_id=1, source_target_pairs={{0,16},{2,18},{4,20},{6,22},{8,24},{10,26},{12,28},{14,30},{16,0},... | collective-permute-start | bytes 196616 | tf_op jit(solution)/shard_map/ppermute | solution.py:644
  54.3 1.7 %copy-start.2 = (bf16[128,256]{1,0:T(8,128)(2,1)}, bf16[128,256]{1,0:T(8,128)(2,1)S(1)}, u32[]{:S(2)}) copy-start(bf16[128,256]{1,0:T(8,128)(2,1)S(1)} %collective-permute-done.11.refs_4_.refs_5_) | copy-start | bytes 196612
  56.0 0.6 copy-start.3
  56.0 0.6 copy-start.4
  59.8 9.6 %collective-permute-start.13 = (bf16[2,256,256]{2,1,0:T(8,128)(2,1)}, bf16[2,256,256]{2,1,0:T(8,128)(2,1)}, u32[]{:S(2)}, u32[]{:S(2)}) collective-permute-start(bf16[2,256,256]{2,1,0:T(8,128)(2,1)} %weight_sent.2.refs_0_), channel_id=1, source_target_pairs={{0,2},{2,0},{4,6},{6,4},{8,10},{10,8},{12,14},{14,12},{1,3},{3,1},... | collective-permute-start | bytes 786440 | tf_op jit(solution)/shard_map/ppermute | solution.py:651
  63.9 10.3 %collective-permute-start.14 = (bf16[2,256,256]{2,1,0:T(8,128)(2,1)}, bf16[2,256,256]{2,1,0:T(8,128)(2,1)}, u32[]{:S(2)}, u32[]{:S(2)}) collective-permute-start(bf16[2,256,256]{2,1,0:T(8,128)(2,1)} %weight_sent.3.refs_0_), channel_id=1, source_target_pairs={{0,2},{2,0},{4,6},{6,4},{8,10},{10,8},{12,14},{14,12},{1,3},{3,1},... | collective-permute-start | bytes 786440 | tf_op jit(solution)/shard_map/ppermute | solution.py:651
  71.2 16.3 %collective-permute-start.17 = (bf16[256,256]{1,0:T(8,128)(2,1)}, bf16[256,256]{1,0:T(8,128)(2,1)}, u32[]{:S(2)}, u32[]{:S(2)}) collective-permute-start(bf16[256,256]{1,0:T(8,128)(2,1)} %get-tuple-element.39.refs_0_), channel_id=1, source_target_pairs={{0,8},{2,10},{4,12},{6,14},{8,0},{10,2},{12,4},{14,6},{1,9},{3,11}... | collective-permute-start | bytes 393224 | tf_op jit(solution)/shard_map/ppermute | solution.py:658
  76.0 11.5 %collective-permute-start.18 = (bf16[256,256]{1,0:T(8,128)(2,1)}, bf16[256,256]{1,0:T(8,128)(2,1)}, u32[]{:S(2)}, u32[]{:S(2)}) collective-permute-start(bf16[256,256]{1,0:T(8,128)(2,1)} %get-tuple-element.49), channel_id=1, source_target_pairs={{0,12},{2,14},{4,0},{6,2},{8,4},{10,6},{12,8},{14,10},{1,13},{3,15... | collective-permute-start | bytes 393224 | tf_op jit(solution)/shard_map/ppermute | solution.py:658
  79.9 7.7 %collective-permute-start.16 = (bf16[256,256]{1,0:T(8,128)(2,1)}, bf16[256,256]{1,0:T(8,128)(2,1)}, u32[]{:S(2)}, u32[]{:S(2)}) collective-permute-start(bf16[256,256]{1,0:T(8,128)(2,1)} %get-tuple-element.48), channel_id=1, source_target_pairs={{0,4},{2,6},{4,8},{6,10},{8,12},{10,14},{12,0},{14,2},{1,5},{3,7},... | collective-permute-start | bytes 393224 | tf_op jit(solution)/shard_map/ppermute | solution.py:658
  82.4 6.9 %collective-permute-start.15 = (bf16[256,384]{1,0:T(8,128)(2,1)}, bf16[256,384]{1,0:T(8,128)(2,1)}, u32[]{:S(2)}, u32[]{:S(2)}) collective-permute-start(bf16[256,384]{1,0:T(8,128)(2,1)} %get-tuple-element.44), channel_id=1, source_target_pairs={{0,2},{2,0},{4,6},{6,4},{8,10},{10,8},{12,14},{14,12},{1,3},{3,1},... | collective-permute-start | bytes 589832 | tf_op jit(solution)/shard_map/ppermute | solution.py:661

commit v16 on v15

--- a/solution.py
+++ b/solution.py
@@ -176,8 +176,9 @@
 
 def attention_kernel(block_count, head_count, at_ref, q_ref, recv_ref, g_mine, key_mask, row_mask, *refs):
     kv_refs, refs = refs[:block_count], refs[block_count:]
-    attn_mine, attn_theirs, dq_mine, dq_theirs, part_out = refs[:5]
-    refs = refs[5:]
+    outer = block_count // INNER
+    attn_mine, attn_theirs, dq_mine, dq_theirs = refs[:4]
+    part_outs, refs = refs[4 : 4 + outer], refs[4 + outer :]
     q_s, recv_s, g_s, mask_s, row_s, kv_s, e_s, s_ref, attn_s, dq_s, part_s = refs[:11]
     sem, kv_sem, out_sem, part_sem = refs[11:]
     rows = q_ref.shape[0]
@@ -242,7 +243,7 @@
             part_s[j, :, cols] = (score_scale * product(dscore, query)).astype(jnp.bfloat16)
             part_s[j, :, vcols] = product(low, grad).astype(jnp.bfloat16)
             if head == head_count - 1:
-                target = part_out.at[at_ref[SOURCES + j] // INNER, j % INNER]
+                target = part_outs[j // INNER].at[j % INNER]
                 stores.append(begin(part_s.at[j], target, part_sem.at[j]))
         dquery = (score_scale * jnp.transpose(dq_t)).astype(jnp.bfloat16)
         dq_s[0, :, cols] = dquery[:rows]
@@ -258,12 +259,12 @@
     feats, rows = g_mine.shape
     heads = feats // HD
     keys = block_count * rows
-    parts = bf16(block_count // INNER, INNER, rows, 2 * feats)
-    return call(
+    outer = block_count // INNER
+    out = call(
         functools.partial(attention_kernel, block_count, heads),
-        [bf16(feats, rows)] * 2 + [bf16(rows, feats)] * 2 + [parts],
+        [bf16(feats, rows)] * 2 + [bf16(rows, feats)] * 2 + [bf16(INNER, rows, 2 * feats)] * outer,
         [SMEM] + [ANY] * (5 + block_count),
-        [ANY] * 5,
+        [ANY] * (4 + outer),
         [
             pltpu.VMEM((rows, feats), jnp.bfloat16),
             pltpu.VMEM((2, feats, rows), jnp.bfloat16),
@@ -284,6 +285,7 @@
         20,
         "attention",
     )(at, queries, recv, g_mine, key_mask, row_mask, *kv_blocks)
+    return *out[:4], out[4:]
 
 
 def grad_heads_kernel(part_count, place, at_ref, first_ref, q_ref, weight_ref, *refs):
@@ -478,12 +480,13 @@
     )(keep, recv)
 
 
-def add_kernel(dq_theirs, terms, mine, theirs, *scratch):
+def add_kernel(count, dq_theirs, *refs):
+    terms, mine, theirs, scratch = refs[:count], refs[count], refs[count + 1], refs[count + 2 :]
     terms_s, mine_s, theirs_s, dq_s, term_sem, out_sem, dq_sem = scratch
-    count, _, _, both = terms.shape
+    both = mine.shape[1]
     dq_load = begin(dq_theirs, dq_s, dq_sem)
     loads = {
-        (side, c): begin(terms.at[c, side], terms_s.at[c, side], term_sem.at[c * INNER + side])
+        (side, c): begin(terms[c].at[side], terms_s.at[c, side], term_sem.at[c * INNER + side])
         for side in (1, 0)
         for c in range(count)
     }
@@ -503,12 +506,13 @@
 
 
 def add_terms(dq_theirs, terms, after):
-    count, _, rows, both = terms.shape
+    _, rows, both = terms[0].shape
     half = both // 2
-    return call(
-        add_kernel,
+    count = len(terms)
+    return call(
+        functools.partial(add_kernel, count),
         [bf16(rows, both), bf16(rows, both + half)],
-        [ANY] * 2,
+        [ANY] * (1 + count),
         [ANY] * 2,
         [
             pltpu.VMEM((count, INNER, rows, both), jnp.bfloat16),
@@ -522,7 +526,7 @@
         2,
         "add_terms",
         after,
-    )(dq_theirs, terms)
+    )(dq_theirs, *terms)
 
 
 def join_kernel(at_ref, dq_mine, mine, recv, *refs):
@@ -631,11 +635,6 @@
     attn_mine, attn_theirs, dq_mine, dq_theirs, parts = attention(
         at, queries[0], recv, g_mine, key_mask, row_mask, kv_blocks
     )
-    columns = [[o * INNER + i for o in range(outer)] for i in range(INNER)]
-    terms = lax.all_to_all(
-        parts, "ctx", split_axis=0, concat_axis=0, axis_index_groups=columns, tiled=True
-    )
-
     attn = []
     for step in range(dp_count):
         for held, side in ((attn_mine, 0), (attn_theirs, 1)):
@@ -643,27 +642,29 @@
             axes = ("dp", "ctx") if step else "ctx"
             attn.append(lax.ppermute(held, axes, pairs) if step or side else held)
 
+    parts, _ = lax.optimization_barrier((parts, attn[1:]))
+    terms = [
+        lax.ppermute(part, "ctx", ctx_pairs(-step, 0)) if step else part
+        for step, part in enumerate(parts)
+    ]
+
     order = list(range(1, outer)) + [0]
-    halves = [order[: outer // 2], order[outer // 2 :]]
-    recvs, previous = [], ()
-    for steps in halves:
-        send = weight_terms(at, attn, grad_blocks, 1, steps, "weight_sent", previous)
-        recvs.append(lax.ppermute(send, "ctx", ctx_pairs(0, 1)))
-        previous = (send,)
-    keep = weight_terms(at, attn, grad_blocks, 0, order, "weight_kept", previous)
-    weight_sums = []
-    for recv in recvs:
-        weight_sums = [*weight_sums, *weight_add(len(weight_sums), keep, recv, weight_sums[-1:])]
+    send = weight_terms(at, attn, grad_blocks, 1, order[:-1], "weight_sent")
+    weight_recv = lax.ppermute(send, "ctx", ctx_pairs(0, 1))
+    own_send = weight_terms(at, attn, grad_blocks, 1, order[-1:], "weight_own", (send,))
+    own_recv = lax.ppermute(own_send, "ctx", ctx_pairs(0, 1))
+    keep = weight_terms(at, attn, grad_blocks, 0, order, "weight_kept", (own_send,))
+    weight_sums = weight_add(0, keep, weight_recv, ())
     weight_parts = [
-        lax.ppermute(held, "ctx", ctx_pairs(step, 0)) for step, held in zip(order[:-1], weight_sums)
-    ]
-    terms_mine, terms_theirs = add_terms(dq_theirs, terms, (weight_sums[-1],))
+        lax.ppermute(held, "ctx", ctx_pairs(step, 0)) for step, held in zip(order, weight_sums)
+    ]
+    terms_mine, terms_theirs = add_terms(dq_theirs, terms, weight_sums[-1:])
     terms_recv = lax.ppermute(terms_theirs, "ctx", ctx_pairs(0, 1))
     grad_q, grad_k, grad_v = join_heads(at, dq_mine, terms_mine, terms_recv)
-    grad_weight = weight_sums[-1].astype(jnp.float32)
+    grad_weight = keep[-1].astype(jnp.float32) + own_recv[0].astype(jnp.float32)
     for part in weight_parts:
         grad_weight = grad_weight + part.astype(jnp.float32)
-
+    grad_weight = grad_weight.astype(jnp.bfloat16)
     return grad_q[None], grad_k[None], grad_v[None], grad_weight.astype(jnp.bfloat16)
 
 

time: 92.6 us -> 95.6 us (1.032)
  waiting for transfers between devices: 11.8 us -> 20.3 us
  starting transfers between devices: 33.6 us -> 30.7 us
  Pallas kernels: 41.2 us -> 39.3 us
    ppermute x2 -> x5, waiting for transfers between devices: 0.36 us -> 10.5 us  [the longest x3 7.42 us: per_device(): lax.ppermute(part, 'ctx', ctx_pairs(-step, 0))]
    all_to_all x1 -> x0, starting transfers between devices: 5 us -> none  [per_device(): lax.all_to_all(parts, 'ctx', split_axis=0, concat_axis=0, axis_index_grou...]
    ppermute x2 -> x5, starting transfers between devices: 2.16 us -> 6.78 us  [the longest x3 4.61 us: per_device(): lax.ppermute(part, 'ctx', ctx_pairs(-step, 0))]
    ppermute x3, starting transfers between devices: 6.8 us -> 3.72 us  [per_device(): lax.ppermute(held, 'ctx', ctx_pairs(step, 0))]
    ppermute x3, waiting for transfers between devices: 4.2 us -> 1.94 us  [per_device(): lax.ppermute(held, 'ctx', ctx_pairs(step, 0))]
    pallas_call x12 -> x11, Pallas kernels: 41.2 us -> 39.3 us  [placed(): return run(*args)]
    ppermute x1, waiting for transfers between devices: 0.01 us -> 0.96 us  [per_device(): terms_recv = lax.ppermute(terms_theirs, 'ctx', ctx_pairs(0, 1))]
    unnamed x11 -> x1, local copies, waits for them, and re-layouts: 1.99 us -> 1.35 us
  transfers between devices with their start and end apart: 20 -> 22, of which waited for: 7 -> 8; matrix products, arithmetic and copies ran while one was open for 4% -> 4% of each run, Pallas kernels for 42% -> 39%
where the time goes in v16:
time: 95.6 us; the launch traced here: 95 us
  Pallas kernels  39.3 us (41%)
  starting transfers between devices  30.7 us (32%)
  waiting for transfers between devices  20.3 us (21%)
  local copies, waits for them, and re-layouts  1.98 us (2%)
  other arithmetic  1.9 us (2%)
    pallas_call x11, Pallas kernels, placed(): return run(*args)  39.3 us
    ppermute x6, starting transfers between devices, per_device(): lax.ppermute(kv_recv if side else kv_mine, 'ctx', ctx_pairs(step, 0))  10.4 us
    ppermute x3, waiting for transfers between devices, per_device(): lax.ppermute(part, 'ctx', ctx_pairs(-step, 0))  7.42 us
    ppermute x3, starting transfers between devices, per_device(): lax.ppermute(part, 'ctx', ctx_pairs(-step, 0))  4.61 us
    ppermute x3, waiting for transfers between devices, per_device(): attn.append(lax.ppermute(held, axes, pairs) if step or side else held)  4 us
    ppermute x3, starting transfers between devices, per_device(): lax.ppermute(held, 'ctx', ctx_pairs(step, 0))  3.72 us
    ppermute x1, waiting for transfers between devices, per_device(): weight_recv = lax.ppermute(send, 'ctx', ctx_pairs(0, 1))  3.03 us
    ppermute x1, starting transfers between devices, per_device(): lax.ppermute(grad_own, 'tp', shift_pairs(tp_count, -step))  3.03 us
  transfers between devices with their start and end apart: 22, of which 8 were waited for; matrix products, arithmetic and copies ran while one was open for 4% of the time, Pallas kernels for 39%

profile of v16, /device:TPU:0, one launch (start us, length us, event | category | flops | bytes accessed | tf_op | source)
XLA Modules:
  0.0 95.0 jit_solution(15574857179903306562)
XLA Ops:
  0.6 3.0 %collective-permute-start.3 = (bf16[256,2048]{1,0:T(8,128)(2,1)}, bf16[256,2048]{1,0:T(8,128)(2,1)}, u32[]{:S(2)}, u32[]{:S(2)}) collective-permute-start(bf16[256,2048]{1,0:T(8,128)(2,1)} %bitcast.29), channel_id=1, source_target_pairs={{0,1},{1,0},{2,3},{3,2},{4,5},{5,4},{6,7},{7,6},{8,9},{9,8},{10,11... | collective-permute-start | bytes 3145736 | tf_op jit(solution)/shard_map/ppermute | solution.py:615
  3.7 0.6 stack.59.refs_0_.refs_3_.refs_1_
  4.3 2.3 %part_heads.1 = (bf16[256,256]{1,0:T(8,128)(2,1)}, bf16[256,256]{1,0:T(8,128)(2,1)}) custom-call(s32[14]{0:T(128)} %stack.59.refs_0_.refs_3_.refs_1_, bf16[256,256]{1,0:T(8,128)(2,1)} %bitcast.32, bf16[256,256]{1,0:T(8,128)(2,1)} %bitcast.33), custom_call_target="tpu_custom_call" | custom-call | flops 2000000000 | bytes 6000000 | tf_op jit(solution)/shard_map/part_heads/pallas_call | solution.py:56
  6.6 1.6 %collective-permute-start = (bf16[256,256]{1,0:T(8,128)(2,1)}, bf16[256,256]{1,0:T(8,128)(2,1)}, u32[]{:S(2)}, u32[]{:S(2)}) collective-permute-start(bf16[256,256]{1,0:T(8,128)(2,1)} %get-tuple-element.33), channel_id=1, source_target_pairs={{0,2},{2,0},{4,6},{6,4},{8,10},{10,8},{12,14},{14,12},{1,3},{3,1},... | collective-permute-start | bytes 393224 | tf_op jit(solution)/shard_map/ppermute | solution.py:618
  8.2 3.6 %collective-permute-start.2 = (bf16[256,256]{1,0:T(8,128)(2,1)}, bf16[256,256]{1,0:T(8,128)(2,1)}, u32[]{:S(2)}, u32[]{:S(2)}) collective-permute-start(bf16[256,256]{1,0:T(8,128)(2,1)} %get-tuple-element.34.refs_6_), channel_id=1, source_target_pairs={{0,12},{2,14},{4,0},{6,2},{8,4},{10,6},{12,8},{14,10},{1,13},{3,15... | collective-permute-start | bytes 393224 | tf_op jit(solution)/shard_map/ppermute | solution.py:620
  11.8 0.0 collective-permute-start.1
  11.8 1.0 %collective-permute-start.6 = (bf16[256,256]{1,0:T(8,128)(2,1)}, bf16[256,256]{1,0:T(8,128)(2,1)}, u32[]{:S(2)}, u32[]{:S(2)}) collective-permute-start(bf16[256,256]{1,0:T(8,128)(2,1)} %get-tuple-element.34.refs_6_), channel_id=1, source_target_pairs={{0,8},{2,10},{4,12},{6,14},{8,0},{10,2},{12,4},{14,6},{1,9},{3,11}... | collective-permute-start | bytes 393224 | tf_op jit(solution)/shard_map/ppermute | solution.py:620
  12.8 1.3 %copy.11.refs_4_ = s32[8,3]{1,0:T(8,128)} copy(s32[8,3]{0,1:T(4,128)} %param.12) | data formatting | bytes 192 | tf_op args[5]
  14.2 0.0 collective-permute-done.refs_0_.refs_7_
  14.2 2.8 %collective-permute-start.8 = (bf16[256,256]{1,0:T(8,128)(2,1)}, bf16[256,256]{1,0:T(8,128)(2,1)}, u32[]{:S(2)}, u32[]{:S(2)}) collective-permute-start(bf16[256,256]{1,0:T(8,128)(2,1)} %collective-permute-done.refs_0_.refs_7_), channel_id=1, source_target_pairs={{0,12},{2,14},{4,0},{6,2},{8,4},{10,6},{12,8},{14,10},{1,13},{3,15... | collective-permute-start | bytes 393224 | tf_op jit(solution)/shard_map/ppermute | solution.py:620
  17.0 0.0 collective-permute-done.2.refs_2_.refs_12_
  17.0 2.0 %collective-permute-start.7 = (bf16[256,256]{1,0:T(8,128)(2,1)}, bf16[256,256]{1,0:T(8,128)(2,1)}, u32[]{:S(2)}, u32[]{:S(2)}) collective-permute-start(bf16[256,256]{1,0:T(8,128)(2,1)} %collective-permute-done.refs_0_.refs_7_), channel_id=1, source_target_pairs={{0,8},{2,10},{4,12},{6,14},{8,0},{10,2},{12,4},{14,6},{1,9},{3,11}... | collective-permute-start | bytes 393224 | tf_op jit(solution)/shard_map/ppermute | solution.py:620
  19.0 1.4 %collective-permute-done.1.refs_1_.refs_8_ = bf16[256,256]{1,0:T(8,128)(2,1)} collective-permute-done((bf16[256,256]{1,0:T(8,128)(2,1)}, bf16[256,256]{1,0:T(8,128)(2,1)}, u32[]{:S(2)}, u32[]{:S(2)}) %collective-permute-start.1) | collective-permute-done | bytes 131104 | tf_op jit(solution)/shard_map/ppermute | solution.py:620
  20.4 1.0 %collective-permute-start.5 = (bf16[256,256]{1,0:T(8,128)(2,1)}, bf16[256,256]{1,0:T(8,128)(2,1)}, u32[]{:S(2)}, u32[]{:S(2)}) collective-permute-start(bf16[256,256]{1,0:T(8,128)(2,1)} %collective-permute-done.refs_0_.refs_7_), channel_id=1, source_target_pairs={{0,4},{2,6},{4,8},{6,10},{8,12},{10,14},{12,0},{14,2},{1,5},{3,7},... | collective-permute-start | bytes 393224 | tf_op jit(solution)/shard_map/ppermute | solution.py:620
  21.4 4.3 %prelude.1 = (f32[256,256]{1,0:T(8,128)}, bf16[2048,128]{1,0:T(8,128)(2,1)}, f32[8,512]{1,0:T(8,128)}) custom-call(bf16[256,256]{1,0:T(8,128)(2,1)} %collective-permute-done.refs_0_.refs_7_, bf16[256,256]{1,0:T(8,128)(2,1)} %collective-permute-done.1.refs_1_.refs_8_, bf16[256,256]{1,0:T(8,128)(2,1)} %collective-permute-done.2.refs_2_.refs_12_, ...), custom_call_target="tpu_custom_call" | custom-call | flops 4000000000 | bytes 12000000 | tf_op jit(solution)/shard_map/prelude/pallas_call | solution.py:56
  25.7 1.5 %collective-permute-done.3.refs_4_.refs_3_ = bf16[256,2048]{1,0:T(8,128)(2,1)} collective-permute-done((bf16[256,2048]{1,0:T(8,128)(2,1)}, bf16[256,2048]{1,0:T(8,128)(2,1)}, u32[]{:S(2)}, u32[]{:S(2)}) %collective-permute-start.3) | collective-permute-done | bytes 1048608 | tf_op jit(solution)/shard_map/ppermute | solution.py:615
  27.1 3.5 %grad_heads.1 = (bf16[128,256]{1,0:T(8,128)(2,1)}, bf16[2,128,256]{2,1,0:T(8,128)(2,1)}) custom-call(s32[14]{0:T(128)} %stack.59.refs_0_.refs_3_.refs_1_, f32[256,256]{1,0:T(8,128)} %get-tuple-element.35.refs_1_, bf16[256,256]{1,0:T(8,128)(2,1)} %bitcast.34, bf16[256,4096]{1,0:T(8,128)(2,1)} %refs_3_.1, bf16[256,2048]{1,0:T(8,128)(2,1)} %collective-permute-done.3.refs_4_.refs_3_), custom_call_target="tpu_custom_call" | custom-call | flops 3000000000 | bytes 9000000 | tf_op jit(solution)/shard_map/grad_heads/pallas_call | solution.py:56
  30.7 1.8 %collective-permute-start.4 = (bf16[2,128,256]{2,1,0:T(8,128)(2,1)}, bf16[2,128,256]{2,1,0:T(8,128)(2,1)}, u32[]{:S(2)}, u32[]{:S(2)}) collective-permute-start(bf16[2,128,256]{2,1,0:T(8,128)(2,1)} %get-tuple-element.36), channel_id=1, source_target_pairs={{0,2},{2,0},{4,6},{6,4},{8,10},{10,8},{12,14},{14,12},{1,3},{3,1},... | collective-permute-start | bytes 393224 | tf_op jit(solution)/shard_map/ppermute | solution.py:629
  32.4 3.7 %pick_columns.1 = (bf16[2,4,256,256]{3,2,1,0:T(8,128)(2,1)}, bf16[2,4,256,256]{3,2,1,0:T(8,128)(2,1)}) custom-call(bf16[128,256]{1,0:T(8,128)(2,1)} %get-tuple-element.37.refs_3_.refs_0_, s32[14]{0:T(128)} %stack.59.refs_0_.refs_3_.refs_1_, bf16[256,2048]{1,0:T(8,128)(2,1)} %bitcast.31, bf16[256,2048]{1,0:T(8,128)(2,1)} %collective-permute-done.3.refs_4_.refs_3_), custom_call_target="tpu_custom_call" | custom-call | flops 3000000000 | bytes 9000000 | tf_op jit(solution)/shard_map/pick_columns/pallas_call | solution.py:56
  36.1 0.0 collective-permute-done.6.refs_10_
  36.1 0.1 collective-permute-start.12
  36.2 0.0 collective-permute-done.8.refs_13_
  36.2 0.0 collective-permute-done.7.refs_11_
  36.2 0.0 collective-permute-done.5.refs_9_
  36.2 0.0 collective-permute-done.4.refs_2_
  36.2 8.9 %attention.1 = (bf16[128,256]{1,0:T(8,128)(2,1)}, bf16[128,256]{1,0:T(8,128)(2,1)}, bf16[256,128]{1,0:T(8,128)(2,1)}, bf16[256,128]{1,0:T(8,128)(2,1)}, bf16[2,2...) custom-call(s32[14]{0:T(128)} %stack.59.refs_0_.refs_3_.refs_1_, ...), custom_call_target="tpu_custom_call" | custom-call | flops 20000000000 | bytes 60000000 | tf_op jit(solution)/shard_map/attention/pallas_call | solution.py:56
  45.1 0.5 collective-permute-start.11
  45.6 1.7 %collective-permute-start.9 = (bf16[128,256]{1,0:T(8,128)(2,1)}, bf16[128,256]{1,0:T(8,128)(2,1)}, u32[]{:S(2)}, u32[]{:S(2)}) collective-permute-start(bf16[128,256]{1,0:T(8,128)(2,1)} %get-tuple-element.42), channel_id=1, source_target_pairs={{0,2},{2,0},{4,6},{6,4},{8,10},{10,8},{12,14},{14,12},{1,3},{3,1},... | collective-permute-start | bytes 196616 | tf_op jit(solution)/shard_map/ppermute | solution.py:643
  47.3 0.0 collective-permute-start.10
  47.3 2.0 %collective-permute-done.11.refs_4_.refs_5_ = bf16[128,256]{1,0:T(8,128)(2,1)} collective-permute-done((bf16[128,256]{1,0:T(8,128)(2,1)}, bf16[128,256]{1,0:T(8,128)(2,1)}, u32[]{:S(2)}, u32[]{:S(2)}) %collective-permute-start.11) | collective-permute-done | bytes 65568 | tf_op jit(solution)/shard_map/ppermute | solution.py:643
  49.3 2.0 %collective-permute-done.9.refs_2_.refs_3_ = bf16[128,256]{1,0:T(8,128)(2,1)} collective-permute-done((bf16[128,256]{1,0:T(8,128)(2,1)}, bf16[128,256]{1,0:T(8,128)(2,1)}, u32[]{:S(2)}, u32[]{:S(2)}) %collective-permute-start.9) | collective-permute-done | bytes 65568 | tf_op jit(solution)/shard_map/ppermute | solution.py:643
  51.3 0.0 collective-permute-done.10.refs_3_.refs_4_
  51.3 3.6 %collective-permute-start.14 = (bf16[2,256,256]{2,1,0:T(8,128)(2,1)}, bf16[2,256,256]{2,1,0:T(8,128)(2,1)}, u32[]{:S(2)}, u32[]{:S(2)}) collective-permute-start(bf16[2,256,256]{2,1,0:T(8,128)(2,1)} %get-tuple-element.52), channel_id=1, source_target_pairs={{0,12},{2,14},{4,0},{6,2},{8,4},{10,6},{12,8},{14,10},{1,13},{3,15... | collective-permute-start | bytes 786440 | tf_op jit(solution)/shard_map/ppermute | solution.py:647
  54.9 0.0 collective-permute-start.15
  54.9 1.0 %collective-permute-start.16 = (bf16[2,256,256]{2,1,0:T(8,128)(2,1)}, bf16[2,256,256]{2,1,0:T(8,128)(2,1)}, u32[]{:S(2)}, u32[]{:S(2)}) collective-permute-start(bf16[2,256,256]{2,1,0:T(8,128)(2,1)} %get-tuple-element.54), channel_id=1, source_target_pairs={{0,4},{2,6},{4,8},{6,10},{8,12},{10,14},{12,0},{14,2},{1,5},{3,7},... | collective-permute-start | bytes 786440 | tf_op jit(solution)/shard_map/ppermute | solution.py:647
  55.9 0.0 collective-permute-done.12.refs_6_.refs_7_
  55.9 3.5 %weight_sent.1.refs_0_ = bf16[3,256,256]{2,1,0:T(8,128)(2,1)} custom-call(s32[14]{0:T(128)} %stack.59.refs_0_.refs_3_.refs_1_, bf16[128,256]{1,0:T(8,128)(2,1)} %get-tuple-element.41.refs_1_.refs_2_, bf16[128,256]{1,0:T(8,128)(2,1)} %collective-permute-done.9.refs_2_.refs_3_, bf16[128,256]{1,0:T(8,128)(2,1)} %collective-permute-done.10.refs_3_.refs_4_, ...), custom_call_target="tpu_custom_call" | custom-call | flops 4000000000 | bytes 12000000 | tf_op jit(solution)/shard_map/weight_sent/pallas_call | solution.py:56
  59.4 1.3 %collective-permute-start.13 = (bf16[3,256,256]{2,1,0:T(8,128)(2,1)}, bf16[3,256,256]{2,1,0:T(8,128)(2,1)}, u32[]{:S(2)}, u32[]{:S(2)}) collective-permute-start(bf16[3,256,256]{2,1,0:T(8,128)(2,1)} %weight_sent.1.refs_0_), channel_id=1, source_target_pairs={{0,2},{2,0},{4,6},{6,4},{8,10},{10,8},{12,14},{14,12},{1,3},{3,1},... | collective-permute-start | bytes 1179656 | tf_op jit(solution)/shard_map/ppermute | solution.py:653
  60.7 2.7 %weight_own.1.refs_0_ = bf16[1,256,256]{2,1,0:T(8,128)(2,1)} custom-call(bf16[3,256,256]{2,1,0:T(8,128)(2,1)} %weight_sent.1.refs_0_, s32[14]{0:T(128)} %stack.59.refs_0_.refs_3_.refs_1_, bf16[128,256]{1,0:T(8,128)(2,1)} %get-tuple-element.41.refs_1_.refs_2_, bf16[128,256]{1,0:T(8,128)(2,1)} %collective-permute-done.9.refs_2_.refs_3_, ...), custom_call_target="tpu_custom_call" | custom-call | flops 4000000000 | bytes 12000000 | tf_op jit(solution)/shard_map/weight_own/pallas_call | solution.py:56
  63.3 0.9 collective-permute-start.18
  64.2 3.9 %weight_kept.1.refs_0_ = bf16[4,256,256]{2,1,0:T(8,128)(2,1)} custom-call(bf16[1,256,256]{2,1,0:T(8,128)(2,1)} %weight_own.1.refs_0_, s32[14]{0:T(128)} %stack.59.refs_0_.refs_3_.refs_1_, bf16[128,256]{1,0:T(8,128)(2,1)} %get-tuple-element.41.refs_1_.refs_2_, bf16[128,256]{1,0:T(8,128)(2,1)} %collective-permute-done.9.refs_2_.refs_3_, ...), custom_call_target="tpu_custom_call" | custom-call | flops 4000000000 | bytes 12000000 | tf_op jit(solution)/shard_map/weight_kept/pallas_call | solution.py:56
  68.2 3.0 %collective-permute-done.13.refs_1_ = bf16[3,256,256]{2,1,0:T(8,128)(2,1)} collective-permute-done((bf16[3,256,256]{2,1,0:T(8,128)(2,1)}, bf16[3,256,256]{2,1,0:T(8,128)(2,1)}, u32[]{:S(2)}, u32[]{:S(2)}) %collective-permute-start.13) | collective-permute-done | bytes 393248 | tf_op jit(solution)/shard_map/ppermute | solution.py:653
  71.2 2.0 %weight_add.1 = (bf16[256,256]{1,0:T(8,128)(2,1)}, bf16[256,256]{1,0:T(8,128)(2,1)}, bf16[256,256]{1,0:T(8,128)(2,1)}) custom-call(bf16[4,256,256]{2,1,0:T(8,128)(2,1)} %weight_kept.1.refs_0_, bf16[3,256,256]{2,1,0:T(8,128)(2,1)} %collective-permute-done.13.refs_1_), custom_call_target="tpu_custom_call" | custom-call | flops 2000000000 | bytes 6000000 | tf_op jit(solution)/shard_map/weight_add/pallas_call | solution.py:56
  73.2 2.5 %collective-permute-start.19 = (bf16[256,256]{1,0:T(8,128)(2,1)}, bf16[256,256]{1,0:T(8,128)(2,1)}, u32[]{:S(2)}, u32[]{:S(2)}) collective-permute-start(bf16[256,256]{1,0:T(8,128)(2,1)} %get-tuple-element.60), channel_id=1, source_target_pairs={{0,4},{2,6},{4,8},{6,10},{8,12},{10,14},{12,0},{14,2},{1,5},{3,7},... | collective-permute-start | bytes 393224 | tf_op jit(solution)/shard_map/ppermute | solution.py:659
  75.7 0.0 collective-permute-done.14.refs_3_
  75.7 1.2 %collective-permute-start.20 = (bf16[256,256]{1,0:T(8,128)(2,1)}, bf16[256,256]{1,0:T(8,128)(2,1)}, u32[]{:S(2)}, u32[]{:S(2)}) collective-permute-start(bf16[256,256]{1,0:T(8,128)(2,1)} %get-tuple-element.61), channel_id=1, source_target_pairs={{0,8},{2,10},{4,12},{6,14},{8,0},{10,2},{12,4},{14,6},{1,9},{3,11}... | collective-permute-start | bytes 393224 | tf_op jit(solution)/shard_map/ppermute | solution.py:659
  76.9 7.4 %collective-permute-done.15.refs_4_ = bf16[2,256,256]{2,1,0:T(8,128)(2,1)} collective-permute-done((bf16[2,256,256]{2,1,0:T(8,128)(2,1)}, bf16[2,256,256]{2,1,0:T(8,128)(2,1)}, u32[]{:S(2)}, u32[]{:S(2)}) %collective-permute-start.15) | collective-permute-done | bytes 262176 | tf_op jit(solution)/shard_map/ppermute | solution.py:647
  84.3 0.0 collective-permute-start.21
  84.3 0.0 collective-permute-done.16.refs_5_
  84.3 2.1 %add_terms.1 = (bf16[256,256]{1,0:T(8,128)(2,1)}, bf16[256,384]{1,0:T(8,128)(2,1)}) custom-call(bf16[256,256]{1,0:T(8,128)(2,1)} %get-tuple-element.45.refs_0_, bf16[256,128]{1,0:T(8,128)(2,1)} %get-tuple-element.46.refs_1_, bf16[2,256,256]{2,1,0:T(8,128)(2,1)} %get-tuple-element.51.refs_2_, bf16[2,256,256]{2,1,0:T(8,128)(2,1)} %collective-permute-done.14.refs_3_, ...), custom_call_target="tpu_custom_call" | custom-call | flops 2000000000 | bytes 6000000 | tf_op jit(solution)/shard_map/add_terms/pallas_call | solution.py:56
  86.4 1.2 %collective-permute-start.17 = (bf16[256,384]{1,0:T(8,128)(2,1)}, bf16[256,384]{1,0:T(8,128)(2,1)}, u32[]{:S(2)}, u32[]{:S(2)}) collective-permute-start(bf16[256,384]{1,0:T(8,128)(2,1)} %get-tuple-element.56), channel_id=1, source_target_pairs={{0,2},{2,0},{4,6},{6,4},{8,10},{10,8},{12,14},{14,12},{1,3},{3,1},... | collective-permute-start | bytes 589832 | tf_op jit(solution)/shard_map/ppermute | solution.py:662
  87.6 0.0 collective-permute-done.18
  87.6 0.0 collective-permute-done.19
  87.7 0.0 collective-permute-done.20
  87.7 1.9 %collective-permute-done.21 = bf16[256,256]{1,0:T(8,128)(2,1)} collective-permute-done((bf16[256,256]{1,0:T(8,128)(2,1)}, bf16[256,256]{1,0:T(8,128)(2,1)}, u32[]{:S(2)}, u32[]{:S(2)}) %collective-permute-start.21) | collective-permute-done | bytes 131104 | tf_op jit(solution)/shard_map/ppermute | solution.py:659
  89.6 1.9 %fusion.2 = bf16[256,256]{1,0:T(8,128)(2,1)} fusion(bf16[256,256]{1,0:T(8,128)(2,1)} %collective-permute-done.21, bf16[256,256]{1,0:T(8,128)(2,1)} %collective-permute-done.20, bf16[256,256]{1,0:T(8,128)(2,1)} %collective-permute-done.19, bf16[1,256,256]{2,1,0:T(8,128)(2,1)} %collective-permute-done.18, bf16[4,256,256]{2,1,0:T(8,128)(2,1)} %weight_kept.1.refs_0_), kind=kLoop, calls=%fused_computation.3 | loop fusion | flops 655360 | bytes 786432 | tf_op jit(solution)/shard_map/convert_element_type | solution.py:667
  91.5 1.0 %collective-permute-done.17.refs_3_ = bf16[256,384]{1,0:T(8,128)(2,1)} collective-permute-done((bf16[256,384]{1,0:T(8,128)(2,1)}, bf16[256,384]{1,0:T(8,128)(2,1)}, u32[]{:S(2)}, u32[]{:S(2)}) %collective-permute-start.17) | collective-permute-done | bytes 196640 | tf_op jit(solution)/shard_map/ppermute | solution.py:662
  92.5 2.5 %join_heads.1 = (bf16[256,256]{1,0:T(8,128)(2,1)}, bf16[256,256]{1,0:T(8,128)(2,1)}, bf16[256,256]{1,0:T(8,128)(2,1)}) custom-call(s32[14]{0:T(128)} %stack.59.refs_0_.refs_3_.refs_1_, bf16[256,128]{1,0:T(8,128)(2,1)} %get-tuple-element.40.refs_1_, bf16[256,256]{1,0:T(8,128)(2,1)} %get-tuple-element.55.refs_2_, bf16[256,384]{1,0:T(8,128)(2,1)} %collective-permute-done.17.refs_3_), custom_call_target="tpu_custom_call" | custom-call | flops 2000000000 | bytes 6000000 | tf_op jit(solution)/shard_map/join_heads/pallas_call | solution.py:56
Async XLA Ops:
  0.6 26.5 %collective-permute-start.3 = (bf16[256,2048]{1,0:T(8,128)(2,1)}, bf16[256,2048]{1,0:T(8,128)(2,1)}, u32[]{:S(2)}, u32[]{:S(2)}) collective-permute-start(bf16[256,2048]{1,0:T(8,128)(2,1)} %bitcast.29), channel_id=1, source_target_pairs={{0,1},{1,0},{2,3},{3,2},{4,5},{5,4},{6,7},{7,6},{8,9},{9,8},{10,11... | collective-permute-start | bytes 3145736 | tf_op jit(solution)/shard_map/ppermute | solution.py:615
  6.6 7.5 %collective-permute-start = (bf16[256,256]{1,0:T(8,128)(2,1)}, bf16[256,256]{1,0:T(8,128)(2,1)}, u32[]{:S(2)}, u32[]{:S(2)}) collective-permute-start(bf16[256,256]{1,0:T(8,128)(2,1)} %get-tuple-element.33), channel_id=1, source_target_pairs={{0,2},{2,0},{4,6},{6,4},{8,10},{10,8},{12,14},{14,12},{1,3},{3,1},... | collective-permute-start | bytes 393224 | tf_op jit(solution)/shard_map/ppermute | solution.py:618
  8.2 8.8 %collective-permute-start.2 = (bf16[256,256]{1,0:T(8,128)(2,1)}, bf16[256,256]{1,0:T(8,128)(2,1)}, u32[]{:S(2)}, u32[]{:S(2)}) collective-permute-start(bf16[256,256]{1,0:T(8,128)(2,1)} %get-tuple-element.34.refs_6_), channel_id=1, source_target_pairs={{0,12},{2,14},{4,0},{6,2},{8,4},{10,6},{12,8},{14,10},{1,13},{3,15... | collective-permute-start | bytes 393224 | tf_op jit(solution)/shard_map/ppermute | solution.py:620
  11.8 8.6 %collective-permute-start.1 = (bf16[256,256]{1,0:T(8,128)(2,1)}, bf16[256,256]{1,0:T(8,128)(2,1)}, u32[]{:S(2)}, u32[]{:S(2)}) collective-permute-start(bf16[256,256]{1,0:T(8,128)(2,1)} %get-tuple-element.34.refs_6_), channel_id=1, source_target_pairs={{0,4},{2,6},{4,8},{6,10},{8,12},{10,14},{12,0},{14,2},{1,5},{3,7},... | collective-permute-start | bytes 393224 | tf_op jit(solution)/shard_map/ppermute | solution.py:620
  11.8 24.3 %collective-permute-start.6 = (bf16[256,256]{1,0:T(8,128)(2,1)}, bf16[256,256]{1,0:T(8,128)(2,1)}, u32[]{:S(2)}, u32[]{:S(2)}) collective-permute-start(bf16[256,256]{1,0:T(8,128)(2,1)} %get-tuple-element.34.refs_6_), channel_id=1, source_target_pairs={{0,8},{2,10},{4,12},{6,14},{8,0},{10,2},{12,4},{14,6},{1,9},{3,11}... | collective-permute-start | bytes 393224 | tf_op jit(solution)/shard_map/ppermute | solution.py:620
  14.2 22.0 %collective-permute-start.8 = (bf16[256,256]{1,0:T(8,128)(2,1)}, bf16[256,256]{1,0:T(8,128)(2,1)}, u32[]{:S(2)}, u32[]{:S(2)}) collective-permute-start(bf16[256,256]{1,0:T(8,128)(2,1)} %collective-permute-done.refs_0_.refs_7_), channel_id=1, source_target_pairs={{0,12},{2,14},{4,0},{6,2},{8,4},{10,6},{12,8},{14,10},{1,13},{3,15... | collective-permute-start | bytes 393224 | tf_op jit(solution)/shard_map/ppermute | solution.py:620
  17.0 19.2 %collective-permute-start.7 = (bf16[256,256]{1,0:T(8,128)(2,1)}, bf16[256,256]{1,0:T(8,128)(2,1)}, u32[]{:S(2)}, u32[]{:S(2)}) collective-permute-start(bf16[256,256]{1,0:T(8,128)(2,1)} %collective-permute-done.refs_0_.refs_7_), channel_id=1, source_target_pairs={{0,8},{2,10},{4,12},{6,14},{8,0},{10,2},{12,4},{14,6},{1,9},{3,11}... | collective-permute-start | bytes 393224 | tf_op jit(solution)/shard_map/ppermute | solution.py:620
  20.4 15.8 %collective-permute-start.5 = (bf16[256,256]{1,0:T(8,128)(2,1)}, bf16[256,256]{1,0:T(8,128)(2,1)}, u32[]{:S(2)}, u32[]{:S(2)}) collective-permute-start(bf16[256,256]{1,0:T(8,128)(2,1)} %collective-permute-done.refs_0_.refs_7_), channel_id=1, source_target_pairs={{0,4},{2,6},{4,8},{6,10},{8,12},{10,14},{12,0},{14,2},{1,5},{3,7},... | collective-permute-start | bytes 393224 | tf_op jit(solution)/shard_map/ppermute | solution.py:620
  30.7 5.6 %collective-permute-start.4 = (bf16[2,128,256]{2,1,0:T(8,128)(2,1)}, bf16[2,128,256]{2,1,0:T(8,128)(2,1)}, u32[]{:S(2)}, u32[]{:S(2)}) collective-permute-start(bf16[2,128,256]{2,1,0:T(8,128)(2,1)} %get-tuple-element.36), channel_id=1, source_target_pairs={{0,2},{2,0},{4,6},{6,4},{8,10},{10,8},{12,14},{14,12},{1,3},{3,1},... | collective-permute-start | bytes 393224 | tf_op jit(solution)/shard_map/ppermute | solution.py:629
  36.1 19.8 %collective-permute-start.12 = (bf16[2,4,256,256]{3,2,1,0:T(8,128)(2,1)}, bf16[2,4,256,256]{3,2,1,0:T(8,128)(2,1)}, u32[]{:S(2)}, u32[]{:S(2)}) collective-permute-start(bf16[2,4,256,256]{3,2,1,0:T(8,128)(2,1)} %get-tuple-element.44), channel_id=1, source_target_pairs={{0,16},{16,0},{1,17},{17,1},{2,18},{18,2},{3,19},{19,3},{4,20},{20... | collective-permute-start | bytes 3145736 | tf_op jit(solution)/shard_map/ppermute | solution.py:632
  45.1 4.2 %collective-permute-start.11 = (bf16[128,256]{1,0:T(8,128)(2,1)}, bf16[128,256]{1,0:T(8,128)(2,1)}, u32[]{:S(2)}, u32[]{:S(2)}) collective-permute-start(bf16[128,256]{1,0:T(8,128)(2,1)} %get-tuple-element.42), channel_id=1, source_target_pairs={{0,18},{2,16},{4,22},{6,20},{8,26},{10,24},{12,30},{14,28},{16,2},... | collective-permute-start | bytes 196616 | tf_op jit(solution)/shard_map/ppermute | solution.py:643
  45.6 5.7 %collective-permute-start.9 = (bf16[128,256]{1,0:T(8,128)(2,1)}, bf16[128,256]{1,0:T(8,128)(2,1)}, u32[]{:S(2)}, u32[]{:S(2)}) collective-permute-start(bf16[128,256]{1,0:T(8,128)(2,1)} %get-tuple-element.42), channel_id=1, source_target_pairs={{0,2},{2,0},{4,6},{6,4},{8,10},{10,8},{12,14},{14,12},{1,3},{3,1},... | collective-permute-start | bytes 196616 | tf_op jit(solution)/shard_map/ppermute | solution.py:643
  47.3 4.0 %collective-permute-start.10 = (bf16[128,256]{1,0:T(8,128)(2,1)}, bf16[128,256]{1,0:T(8,128)(2,1)}, u32[]{:S(2)}, u32[]{:S(2)}) collective-permute-start(bf16[128,256]{1,0:T(8,128)(2,1)} %get-tuple-element.41.refs_1_.refs_2_), channel_id=1, source_target_pairs={{0,16},{2,18},{4,20},{6,22},{8,24},{10,26},{12,28},{14,30},{16,0},... | collective-permute-start | bytes 196616 | tf_op jit(solution)/shard_map/ppermute | solution.py:643
  51.3 24.4 %collective-permute-start.14 = (bf16[2,256,256]{2,1,0:T(8,128)(2,1)}, bf16[2,256,256]{2,1,0:T(8,128)(2,1)}, u32[]{:S(2)}, u32[]{:S(2)}) collective-permute-start(bf16[2,256,256]{2,1,0:T(8,128)(2,1)} %get-tuple-element.52), channel_id=1, source_target_pairs={{0,12},{2,14},{4,0},{6,2},{8,4},{10,6},{12,8},{14,10},{1,13},{3,15... | collective-permute-start | bytes 786440 | tf_op jit(solution)/shard_map/ppermute | solution.py:647
  54.9 29.4 %collective-permute-start.15 = (bf16[2,256,256]{2,1,0:T(8,128)(2,1)}, bf16[2,256,256]{2,1,0:T(8,128)(2,1)}, u32[]{:S(2)}, u32[]{:S(2)}) collective-permute-start(bf16[2,256,256]{2,1,0:T(8,128)(2,1)} %get-tuple-element.53), channel_id=1, source_target_pairs={{0,8},{2,10},{4,12},{6,14},{8,0},{10,2},{12,4},{14,6},{1,9},{3,11}... | collective-permute-start | bytes 786440 | tf_op jit(solution)/shard_map/ppermute | solution.py:647
  54.9 29.4 %collective-permute-start.16 = (bf16[2,256,256]{2,1,0:T(8,128)(2,1)}, bf16[2,256,256]{2,1,0:T(8,128)(2,1)}, u32[]{:S(2)}, u32[]{:S(2)}) collective-permute-start(bf16[2,256,256]{2,1,0:T(8,128)(2,1)} %get-tuple-element.54), channel_id=1, source_target_pairs={{0,4},{2,6},{4,8},{6,10},{8,12},{10,14},{12,0},{14,2},{1,5},{3,7},... | collective-permute-start | bytes 786440 | tf_op jit(solution)/shard_map/ppermute | solution.py:647
  59.4 11.8 %collective-permute-start.13 = (bf16[3,256,256]{2,1,0:T(8,128)(2,1)}, bf16[3,256,256]{2,1,0:T(8,128)(2,1)}, u32[]{:S(2)}, u32[]{:S(2)}) collective-permute-start(bf16[3,256,256]{2,1,0:T(8,128)(2,1)} %weight_sent.1.refs_0_), channel_id=1, source_target_pairs={{0,2},{2,0},{4,6},{6,4},{8,10},{10,8},{12,14},{14,12},{1,3},{3,1},... | collective-permute-start | bytes 1179656 | tf_op jit(solution)/shard_map/ppermute | solution.py:653
  63.3 24.3 %collective-permute-start.18 = (bf16[1,256,256]{2,1,0:T(8,128)(2,1)}, bf16[1,256,256]{2,1,0:T(8,128)(2,1)}, u32[]{:S(2)}, u32[]{:S(2)}) collective-permute-start(bf16[1,256,256]{2,1,0:T(8,128)(2,1)} %weight_own.1.refs_0_), channel_id=1, source_target_pairs={{0,2},{2,0},{4,6},{6,4},{8,10},{10,8},{12,14},{14,12},{1,3},{3,1},... | collective-permute-start | bytes 393224 | tf_op jit(solution)/shard_map/ppermute | solution.py:655
  73.2 14.5 %collective-permute-start.19 = (bf16[256,256]{1,0:T(8,128)(2,1)}, bf16[256,256]{1,0:T(8,128)(2,1)}, u32[]{:S(2)}, u32[]{:S(2)}) collective-permute-start(bf16[256,256]{1,0:T(8,128)(2,1)} %get-tuple-element.60), channel_id=1, source_target_pairs={{0,4},{2,6},{4,8},{6,10},{8,12},{10,14},{12,0},{14,2},{1,5},{3,7},... | collective-permute-start | bytes 393224 | tf_op jit(solution)/shard_map/ppermute | solution.py:659
  75.7 11.9 %collective-permute-start.20 = (bf16[256,256]{1,0:T(8,128)(2,1)}, bf16[256,256]{1,0:T(8,128)(2,1)}, u32[]{:S(2)}, u32[]{:S(2)}) collective-permute-start(bf16[256,256]{1,0:T(8,128)(2,1)} %get-tuple-element.61), channel_id=1, source_target_pairs={{0,8},{2,10},{4,12},{6,14},{8,0},{10,2},{12,4},{14,6},{1,9},{3,11}... | collective-permute-start | bytes 393224 | tf_op jit(solution)/shard_map/ppermute | solution.py:659
  84.3 5.3 %collective-permute-start.21 = (bf16[256,256]{1,0:T(8,128)(2,1)}, bf16[256,256]{1,0:T(8,128)(2,1)}, u32[]{:S(2)}, u32[]{:S(2)}) collective-permute-start(bf16[256,256]{1,0:T(8,128)(2,1)} %get-tuple-element.45.refs_0_), channel_id=1, source_target_pairs={{0,12},{2,14},{4,0},{6,2},{8,4},{10,6},{12,8},{14,10},{1,13},{3,15... | collective-permute-start | bytes 393224 | tf_op jit(solution)/shard_map/ppermute | solution.py:659
  86.4 6.1 %collective-permute-start.17 = (bf16[256,384]{1,0:T(8,128)(2,1)}, bf16[256,384]{1,0:T(8,128)(2,1)}, u32[]{:S(2)}, u32[]{:S(2)}) collective-permute-start(bf16[256,384]{1,0:T(8,128)(2,1)} %get-tuple-element.56), channel_id=1, source_target_pairs={{0,2},{2,0},{4,6},{6,4},{8,10},{10,8},{12,14},{14,12},{1,3},{3,1},... | collective-permute-start | bytes 589832 | tf_op jit(solution)/shard_map/ppermute | solution.py:662

commit v17 on v16

--- a/solution.py
+++ b/solution.py
@@ -635,6 +635,9 @@
     attn_mine, attn_theirs, dq_mine, dq_theirs, parts = attention(
         at, queries[0], recv, g_mine, key_mask, row_mask, kv_blocks
     )
+    attn_mine, attn_theirs, grad_blocks = lax.optimization_barrier(
+        (attn_mine, attn_theirs, grad_blocks)
+    )
     attn = []
     for step in range(dp_count):
         for held, side in ((attn_mine, 0), (attn_theirs, 1)):
@@ -642,7 +645,6 @@
             axes = ("dp", "ctx") if step else "ctx"
             attn.append(lax.ppermute(held, axes, pairs) if step or side else held)
 
-    parts, _ = lax.optimization_barrier((parts, attn[1:]))
     terms = [
         lax.ppermute(part, "ctx", ctx_pairs(-step, 0)) if step else part
         for step, part in enumerate(parts)

time: 95.6 us -> 92 us (0.962)
  waiting for transfers between devices: 20.3 us -> 16.7 us
    ppermute x3, waiting for transfers between devices: 4 us -> 0.01 us  [per_device(): attn.append(lax.ppermute(held, axes, pairs) if step or side else held)]
  transfers between devices with their start and end apart: 22 -> 22, of which waited for: 8 -> 6; matrix products, arithmetic and copies ran while one was open for 4% -> 4% of each run, Pallas kernels for 39% -> 40%
where the time goes in v17:
time: 92 us; the launch traced here: 91.4 us
  Pallas kernels  39.3 us (43%)
  starting transfers between devices  30.7 us (33%)
  waiting for transfers between devices  16.7 us (18%)
  local copies, waits for them, and re-layouts  1.98 us (2%)
  other arithmetic  1.9 us (2%)
    pallas_call x11, Pallas kernels, placed(): return run(*args)  39.3 us
    ppermute x6, starting transfers between devices, per_device(): lax.ppermute(kv_recv if side else kv_mine, 'ctx', ctx_pairs(step, 0))  10.4 us
    ppermute x3, waiting for transfers between devices, per_device(): lax.ppermute(part, 'ctx', ctx_pairs(-step, 0))  6.86 us
    ppermute x3, starting transfers between devices, per_device(): lax.ppermute(part, 'ctx', ctx_pairs(-step, 0))  4.61 us
    ppermute x1, waiting for transfers between devices, per_device(): weight_recv = lax.ppermute(send, 'ctx', ctx_pairs(0, 1))  3.63 us
    ppermute x3, starting transfers between devices, per_device(): lax.ppermute(held, 'ctx', ctx_pairs(step, 0))  3.58 us
    ppermute x1, starting transfers between devices, per_device(): lax.ppermute(grad_own, 'tp', shift_pairs(tp_count, -step))  3.03 us
    ppermute x3, starting transfers between devices, per_device(): attn.append(lax.ppermute(held, axes, pairs) if step or side else held)  2.17 us
  transfers between devices with their start and end apart: 22, of which 6 were waited for; matrix products, arithmetic and copies ran while one was open for 4% of the time, Pallas kernels for 40%

profile of v17, /device:TPU:0, one launch (start us, length us, event | category | flops | bytes accessed | tf_op | source)
XLA Modules:
  0.0 91.4 jit_solution(1155556726454812658)
XLA Ops:
  0.6 3.0 %collective-permute-start.3 = (bf16[256,2048]{1,0:T(8,128)(2,1)}, bf16[256,2048]{1,0:T(8,128)(2,1)}, u32[]{:S(2)}, u32[]{:S(2)}) collective-permute-start(bf16[256,2048]{1,0:T(8,128)(2,1)} %bitcast.29), channel_id=1, source_target_pairs={{0,1},{1,0},{2,3},{3,2},{4,5},{5,4},{6,7},{7,6},{8,9},{9,8},{10,11... | collective-permute-start | bytes 3145736 | tf_op jit(solution)/shard_map/ppermute | solution.py:615
  3.7 0.6 stack.59.refs_0_.refs_3_.refs_1_
  4.3 2.3 %part_heads.1 = (bf16[256,256]{1,0:T(8,128)(2,1)}, bf16[256,256]{1,0:T(8,128)(2,1)}) custom-call(s32[14]{0:T(128)} %stack.59.refs_0_.refs_3_.refs_1_, bf16[256,256]{1,0:T(8,128)(2,1)} %bitcast.32, bf16[256,256]{1,0:T(8,128)(2,1)} %bitcast.33), custom_call_target="tpu_custom_call" | custom-call | flops 2000000000 | bytes 6000000 | tf_op jit(solution)/shard_map/part_heads/pallas_call | solution.py:56
  6.6 1.6 %collective-permute-start = (bf16[256,256]{1,0:T(8,128)(2,1)}, bf16[256,256]{1,0:T(8,128)(2,1)}, u32[]{:S(2)}, u32[]{:S(2)}) collective-permute-start(bf16[256,256]{1,0:T(8,128)(2,1)} %get-tuple-element.33), channel_id=1, source_target_pairs={{0,2},{2,0},{4,6},{6,4},{8,10},{10,8},{12,14},{14,12},{1,3},{3,1},... | collective-permute-start | bytes 393224 | tf_op jit(solution)/shard_map/ppermute | solution.py:618
  8.2 3.6 %collective-permute-start.2 = (bf16[256,256]{1,0:T(8,128)(2,1)}, bf16[256,256]{1,0:T(8,128)(2,1)}, u32[]{:S(2)}, u32[]{:S(2)}) collective-permute-start(bf16[256,256]{1,0:T(8,128)(2,1)} %get-tuple-element.34.refs_6_), channel_id=1, source_target_pairs={{0,12},{2,14},{4,0},{6,2},{8,4},{10,6},{12,8},{14,10},{1,13},{3,15... | collective-permute-start | bytes 393224 | tf_op jit(solution)/shard_map/ppermute | solution.py:620
  11.8 0.0 collective-permute-start.1
  11.8 1.0 %collective-permute-start.6 = (bf16[256,256]{1,0:T(8,128)(2,1)}, bf16[256,256]{1,0:T(8,128)(2,1)}, u32[]{:S(2)}, u32[]{:S(2)}) collective-permute-start(bf16[256,256]{1,0:T(8,128)(2,1)} %get-tuple-element.34.refs_6_), channel_id=1, source_target_pairs={{0,8},{2,10},{4,12},{6,14},{8,0},{10,2},{12,4},{14,6},{1,9},{3,11}... | collective-permute-start | bytes 393224 | tf_op jit(solution)/shard_map/ppermute | solution.py:620
  12.8 1.3 %copy.11.refs_4_ = s32[8,3]{1,0:T(8,128)} copy(s32[8,3]{0,1:T(4,128)} %param.12) | data formatting | bytes 192 | tf_op args[5]
  14.2 0.0 collective-permute-done.refs_0_.refs_7_
  14.2 2.8 %collective-permute-start.8 = (bf16[256,256]{1,0:T(8,128)(2,1)}, bf16[256,256]{1,0:T(8,128)(2,1)}, u32[]{:S(2)}, u32[]{:S(2)}) collective-permute-start(bf16[256,256]{1,0:T(8,128)(2,1)} %collective-permute-done.refs_0_.refs_7_), channel_id=1, source_target_pairs={{0,12},{2,14},{4,0},{6,2},{8,4},{10,6},{12,8},{14,10},{1,13},{3,15... | collective-permute-start | bytes 393224 | tf_op jit(solution)/shard_map/ppermute | solution.py:620
  17.0 0.0 collective-permute-done.2.refs_2_.refs_12_
  17.0 2.0 %collective-permute-start.7 = (bf16[256,256]{1,0:T(8,128)(2,1)}, bf16[256,256]{1,0:T(8,128)(2,1)}, u32[]{:S(2)}, u32[]{:S(2)}) collective-permute-start(bf16[256,256]{1,0:T(8,128)(2,1)} %collective-permute-done.refs_0_.refs_7_), channel_id=1, source_target_pairs={{0,8},{2,10},{4,12},{6,14},{8,0},{10,2},{12,4},{14,6},{1,9},{3,11}... | collective-permute-start | bytes 393224 | tf_op jit(solution)/shard_map/ppermute | solution.py:620
  19.0 1.4 %collective-permute-done.1.refs_1_.refs_8_ = bf16[256,256]{1,0:T(8,128)(2,1)} collective-permute-done((bf16[256,256]{1,0:T(8,128)(2,1)}, bf16[256,256]{1,0:T(8,128)(2,1)}, u32[]{:S(2)}, u32[]{:S(2)}) %collective-permute-start.1) | collective-permute-done | bytes 131104 | tf_op jit(solution)/shard_map/ppermute | solution.py:620
  20.4 1.0 %collective-permute-start.5 = (bf16[256,256]{1,0:T(8,128)(2,1)}, bf16[256,256]{1,0:T(8,128)(2,1)}, u32[]{:S(2)}, u32[]{:S(2)}) collective-permute-start(bf16[256,256]{1,0:T(8,128)(2,1)} %collective-permute-done.refs_0_.refs_7_), channel_id=1, source_target_pairs={{0,4},{2,6},{4,8},{6,10},{8,12},{10,14},{12,0},{14,2},{1,5},{3,7},... | collective-permute-start | bytes 393224 | tf_op jit(solution)/shard_map/ppermute | solution.py:620
  21.4 4.3 %prelude.1 = (f32[256,256]{1,0:T(8,128)}, bf16[2048,128]{1,0:T(8,128)(2,1)}, f32[8,512]{1,0:T(8,128)}) custom-call(bf16[256,256]{1,0:T(8,128)(2,1)} %collective-permute-done.refs_0_.refs_7_, bf16[256,256]{1,0:T(8,128)(2,1)} %collective-permute-done.1.refs_1_.refs_8_, bf16[256,256]{1,0:T(8,128)(2,1)} %collective-permute-done.2.refs_2_.refs_12_, ...), custom_call_target="tpu_custom_call" | custom-call | flops 4000000000 | bytes 12000000 | tf_op jit(solution)/shard_map/prelude/pallas_call | solution.py:56
  25.7 1.5 %collective-permute-done.3.refs_4_.refs_3_ = bf16[256,2048]{1,0:T(8,128)(2,1)} collective-permute-done((bf16[256,2048]{1,0:T(8,128)(2,1)}, bf16[256,2048]{1,0:T(8,128)(2,1)}, u32[]{:S(2)}, u32[]{:S(2)}) %collective-permute-start.3) | collective-permute-done | bytes 1048608 | tf_op jit(solution)/shard_map/ppermute | solution.py:615
  27.1 3.5 %grad_heads.1 = (bf16[128,256]{1,0:T(8,128)(2,1)}, bf16[2,128,256]{2,1,0:T(8,128)(2,1)}) custom-call(s32[14]{0:T(128)} %stack.59.refs_0_.refs_3_.refs_1_, f32[256,256]{1,0:T(8,128)} %get-tuple-element.35.refs_1_, bf16[256,256]{1,0:T(8,128)(2,1)} %bitcast.34, bf16[256,4096]{1,0:T(8,128)(2,1)} %refs_3_.1, bf16[256,2048]{1,0:T(8,128)(2,1)} %collective-permute-done.3.refs_4_.refs_3_), custom_call_target="tpu_custom_call" | custom-call | flops 3000000000 | bytes 9000000 | tf_op jit(solution)/shard_map/grad_heads/pallas_call | solution.py:56
  30.7 1.8 %collective-permute-start.4 = (bf16[2,128,256]{2,1,0:T(8,128)(2,1)}, bf16[2,128,256]{2,1,0:T(8,128)(2,1)}, u32[]{:S(2)}, u32[]{:S(2)}) collective-permute-start(bf16[2,128,256]{2,1,0:T(8,128)(2,1)} %get-tuple-element.36), channel_id=1, source_target_pairs={{0,2},{2,0},{4,6},{6,4},{8,10},{10,8},{12,14},{14,12},{1,3},{3,1},... | collective-permute-start | bytes 393224 | tf_op jit(solution)/shard_map/ppermute | solution.py:629
  32.4 3.7 %pick_columns.1 = (bf16[2,4,256,256]{3,2,1,0:T(8,128)(2,1)}, bf16[2,4,256,256]{3,2,1,0:T(8,128)(2,1)}) custom-call(bf16[128,256]{1,0:T(8,128)(2,1)} %get-tuple-element.37.refs_3_.refs_0_, s32[14]{0:T(128)} %stack.59.refs_0_.refs_3_.refs_1_, bf16[256,2048]{1,0:T(8,128)(2,1)} %bitcast.31, bf16[256,2048]{1,0:T(8,128)(2,1)} %collective-permute-done.3.refs_4_.refs_3_), custom_call_target="tpu_custom_call" | custom-call | flops 3000000000 | bytes 9000000 | tf_op jit(solution)/shard_map/pick_columns/pallas_call | solution.py:56
  36.1 0.0 collective-permute-done.6.refs_10_
  36.1 0.1 collective-permute-start.9
  36.2 0.0 collective-permute-done.8.refs_13_
  36.2 0.0 collective-permute-done.7.refs_11_
  36.2 0.0 collective-permute-done.5.refs_9_
  36.2 0.0 collective-permute-done.4.refs_2_
  36.2 8.9 %attention.1 = (bf16[128,256]{1,0:T(8,128)(2,1)}, bf16[128,256]{1,0:T(8,128)(2,1)}, bf16[256,128]{1,0:T(8,128)(2,1)}, bf16[256,128]{1,0:T(8,128)(2,1)}, bf16[2,2...) custom-call(s32[14]{0:T(128)} %stack.59.refs_0_.refs_3_.refs_1_, ...), custom_call_target="tpu_custom_call" | custom-call | flops 20000000000 | bytes 60000000 | tf_op jit(solution)/shard_map/attention/pallas_call | solution.py:56
  45.1 0.0 collective-permute-done.9.refs_6_.refs_7_
  45.1 0.5 collective-permute-start.12
  45.6 1.7 %collective-permute-start.10 = (bf16[128,256]{1,0:T(8,128)(2,1)}, bf16[128,256]{1,0:T(8,128)(2,1)}, u32[]{:S(2)}, u32[]{:S(2)}) collective-permute-start(bf16[128,256]{1,0:T(8,128)(2,1)} %get-tuple-element.46), channel_id=1, source_target_pairs={{0,2},{2,0},{4,6},{6,4},{8,10},{10,8},{12,14},{14,12},{1,3},{3,1},... | collective-permute-start | bytes 196616 | tf_op jit(solution)/shard_map/ppermute | solution.py:646
  47.3 0.0 collective-permute-start.11
  47.3 3.6 %collective-permute-start.14 = (bf16[2,256,256]{2,1,0:T(8,128)(2,1)}, bf16[2,256,256]{2,1,0:T(8,128)(2,1)}, u32[]{:S(2)}, u32[]{:S(2)}) collective-permute-start(bf16[2,256,256]{2,1,0:T(8,128)(2,1)} %get-tuple-element.52), channel_id=1, source_target_pairs={{0,12},{2,14},{4,0},{6,2},{8,4},{10,6},{12,8},{14,10},{1,13},{3,15... | collective-permute-start | bytes 786440 | tf_op jit(solution)/shard_map/ppermute | solution.py:649
  50.9 0.0 collective-permute-start.15
  50.9 0.0 collective-permute-done.12.refs_4_.refs_5_
  50.9 1.0 %collective-permute-start.16 = (bf16[2,256,256]{2,1,0:T(8,128)(2,1)}, bf16[2,256,256]{2,1,0:T(8,128)(2,1)}, u32[]{:S(2)}, u32[]{:S(2)}) collective-permute-start(bf16[2,256,256]{2,1,0:T(8,128)(2,1)} %get-tuple-element.54), channel_id=1, source_target_pairs={{0,4},{2,6},{4,8},{6,10},{8,12},{10,14},{12,0},{14,2},{1,5},{3,7},... | collective-permute-start | bytes 786440 | tf_op jit(solution)/shard_map/ppermute | solution.py:649
  51.9 0.0 collective-permute-done.10.refs_2_.refs_3_
  51.9 0.0 collective-permute-done.11.refs_3_.refs_4_
  51.9 3.5 %weight_sent.1.refs_0_ = bf16[3,256,256]{2,1,0:T(8,128)(2,1)} custom-call(s32[14]{0:T(128)} %stack.59.refs_0_.refs_3_.refs_1_, bf16[128,256]{1,0:T(8,128)(2,1)} %get-tuple-element.45.refs_1_.refs_2_, bf16[128,256]{1,0:T(8,128)(2,1)} %collective-permute-done.10.refs_2_.refs_3_, bf16[128,256]{1,0:T(8,128)(2,1)} %collective-permute-done.11.refs_3_.refs_4_, ...), custom_call_target="tpu_custom_call" | custom-call | flops 4000000000 | bytes 12000000 | tf_op jit(solution)/shard_map/weight_sent/pallas_call | solution.py:56
  55.4 1.3 %collective-permute-start.13 = (bf16[3,256,256]{2,1,0:T(8,128)(2,1)}, bf16[3,256,256]{2,1,0:T(8,128)(2,1)}, u32[]{:S(2)}, u32[]{:S(2)}) collective-permute-start(bf16[3,256,256]{2,1,0:T(8,128)(2,1)} %weight_sent.1.refs_0_), channel_id=1, source_target_pairs={{0,2},{2,0},{4,6},{6,4},{8,10},{10,8},{12,14},{14,12},{1,3},{3,1},... | collective-permute-start | bytes 1179656 | tf_op jit(solution)/shard_map/ppermute | solution.py:655
  56.7 2.7 %weight_own.1.refs_0_ = bf16[1,256,256]{2,1,0:T(8,128)(2,1)} custom-call(bf16[3,256,256]{2,1,0:T(8,128)(2,1)} %weight_sent.1.refs_0_, s32[14]{0:T(128)} %stack.59.refs_0_.refs_3_.refs_1_, bf16[128,256]{1,0:T(8,128)(2,1)} %get-tuple-element.45.refs_1_.refs_2_, bf16[128,256]{1,0:T(8,128)(2,1)} %collective-permute-done.10.refs_2_.refs_3_, ...), custom_call_target="tpu_custom_call" | custom-call | flops 4000000000 | bytes 12000000 | tf_op jit(solution)/shard_map/weight_own/pallas_call | solution.py:56
  59.4 0.9 collective-permute-start.18
  60.3 3.9 %weight_kept.1.refs_0_ = bf16[4,256,256]{2,1,0:T(8,128)(2,1)} custom-call(bf16[1,256,256]{2,1,0:T(8,128)(2,1)} %weight_own.1.refs_0_, s32[14]{0:T(128)} %stack.59.refs_0_.refs_3_.refs_1_, bf16[128,256]{1,0:T(8,128)(2,1)} %get-tuple-element.45.refs_1_.refs_2_, bf16[128,256]{1,0:T(8,128)(2,1)} %collective-permute-done.10.refs_2_.refs_3_, ...), custom_call_target="tpu_custom_call" | custom-call | flops 4000000000 | bytes 12000000 | tf_op jit(solution)/shard_map/weight_kept/pallas_call | solution.py:56
  64.2 3.6 %collective-permute-done.13.refs_1_ = bf16[3,256,256]{2,1,0:T(8,128)(2,1)} collective-permute-done((bf16[3,256,256]{2,1,0:T(8,128)(2,1)}, bf16[3,256,256]{2,1,0:T(8,128)(2,1)}, u32[]{:S(2)}, u32[]{:S(2)}) %collective-permute-start.13) | collective-permute-done | bytes 393248 | tf_op jit(solution)/shard_map/ppermute | solution.py:655
  67.8 2.0 %weight_add.1 = (bf16[256,256]{1,0:T(8,128)(2,1)}, bf16[256,256]{1,0:T(8,128)(2,1)}, bf16[256,256]{1,0:T(8,128)(2,1)}) custom-call(bf16[4,256,256]{2,1,0:T(8,128)(2,1)} %weight_kept.1.refs_0_, bf16[3,256,256]{2,1,0:T(8,128)(2,1)} %collective-permute-done.13.refs_1_), custom_call_target="tpu_custom_call" | custom-call | flops 2000000000 | bytes 6000000 | tf_op jit(solution)/shard_map/weight_add/pallas_call | solution.py:56
  69.8 2.5 %collective-permute-start.19 = (bf16[256,256]{1,0:T(8,128)(2,1)}, bf16[256,256]{1,0:T(8,128)(2,1)}, u32[]{:S(2)}, u32[]{:S(2)}) collective-permute-start(bf16[256,256]{1,0:T(8,128)(2,1)} %get-tuple-element.60), channel_id=1, source_target_pairs={{0,4},{2,6},{4,8},{6,10},{8,12},{10,14},{12,0},{14,2},{1,5},{3,7},... | collective-permute-start | bytes 393224 | tf_op jit(solution)/shard_map/ppermute | solution.py:661
  72.3 0.0 collective-permute-done.14.refs_3_
  72.3 1.0 %collective-permute-start.20 = (bf16[256,256]{1,0:T(8,128)(2,1)}, bf16[256,256]{1,0:T(8,128)(2,1)}, u32[]{:S(2)}, u32[]{:S(2)}) collective-permute-start(bf16[256,256]{1,0:T(8,128)(2,1)} %get-tuple-element.61), channel_id=1, source_target_pairs={{0,8},{2,10},{4,12},{6,14},{8,0},{10,2},{12,4},{14,6},{1,9},{3,11}... | collective-permute-start | bytes 393224 | tf_op jit(solution)/shard_map/ppermute | solution.py:661
  73.4 6.9 %collective-permute-done.15.refs_4_ = bf16[2,256,256]{2,1,0:T(8,128)(2,1)} collective-permute-done((bf16[2,256,256]{2,1,0:T(8,128)(2,1)}, bf16[2,256,256]{2,1,0:T(8,128)(2,1)}, u32[]{:S(2)}, u32[]{:S(2)}) %collective-permute-start.15) | collective-permute-done | bytes 262176 | tf_op jit(solution)/shard_map/ppermute | solution.py:649
  80.2 0.0 collective-permute-start.21
  80.2 0.0 collective-permute-done.16.refs_5_
  80.2 2.1 %add_terms.1 = (bf16[256,256]{1,0:T(8,128)(2,1)}, bf16[256,384]{1,0:T(8,128)(2,1)}) custom-call(bf16[256,256]{1,0:T(8,128)(2,1)} %get-tuple-element.49.refs_0_, bf16[256,128]{1,0:T(8,128)(2,1)} %get-tuple-element.50.refs_1_, bf16[2,256,256]{2,1,0:T(8,128)(2,1)} %get-tuple-element.51.refs_2_, bf16[2,256,256]{2,1,0:T(8,128)(2,1)} %collective-permute-done.14.refs_3_, ...), custom_call_target="tpu_custom_call" | custom-call | flops 2000000000 | bytes 6000000 | tf_op jit(solution)/shard_map/add_terms/pallas_call | solution.py:56
  82.3 1.4 %collective-permute-start.17 = (bf16[256,384]{1,0:T(8,128)(2,1)}, bf16[256,384]{1,0:T(8,128)(2,1)}, u32[]{:S(2)}, u32[]{:S(2)}) collective-permute-start(bf16[256,384]{1,0:T(8,128)(2,1)} %get-tuple-element.56), channel_id=1, source_target_pairs={{0,2},{2,0},{4,6},{6,4},{8,10},{10,8},{12,14},{14,12},{1,3},{3,1},... | collective-permute-start | bytes 589832 | tf_op jit(solution)/shard_map/ppermute | solution.py:664
  83.7 0.0 collective-permute-done.18
  83.7 0.0 collective-permute-done.19
  83.7 0.0 collective-permute-done.20
  83.7 1.9 %collective-permute-done.21 = bf16[256,256]{1,0:T(8,128)(2,1)} collective-permute-done((bf16[256,256]{1,0:T(8,128)(2,1)}, bf16[256,256]{1,0:T(8,128)(2,1)}, u32[]{:S(2)}, u32[]{:S(2)}) %collective-permute-start.21) | collective-permute-done | bytes 131104 | tf_op jit(solution)/shard_map/ppermute | solution.py:661
  85.6 1.9 %fusion.2 = bf16[256,256]{1,0:T(8,128)(2,1)} fusion(bf16[256,256]{1,0:T(8,128)(2,1)} %collective-permute-done.21, bf16[256,256]{1,0:T(8,128)(2,1)} %collective-permute-done.20, bf16[256,256]{1,0:T(8,128)(2,1)} %collective-permute-done.19, bf16[1,256,256]{2,1,0:T(8,128)(2,1)} %collective-permute-done.18, bf16[4,256,256]{2,1,0:T(8,128)(2,1)} %weight_kept.1.refs_0_), kind=kLoop, calls=%fused_computation.3 | loop fusion | flops 655360 | bytes 786432 | tf_op jit(solution)/shard_map/convert_element_type | solution.py:669
  87.5 1.4 %collective-permute-done.17.refs_3_ = bf16[256,384]{1,0:T(8,128)(2,1)} collective-permute-done((bf16[256,384]{1,0:T(8,128)(2,1)}, bf16[256,384]{1,0:T(8,128)(2,1)}, u32[]{:S(2)}, u32[]{:S(2)}) %collective-permute-start.17) | collective-permute-done | bytes 196640 | tf_op jit(solution)/shard_map/ppermute | solution.py:664
  88.9 2.5 %join_heads.1 = (bf16[256,256]{1,0:T(8,128)(2,1)}, bf16[256,256]{1,0:T(8,128)(2,1)}, bf16[256,256]{1,0:T(8,128)(2,1)}) custom-call(s32[14]{0:T(128)} %stack.59.refs_0_.refs_3_.refs_1_, bf16[256,128]{1,0:T(8,128)(2,1)} %get-tuple-element.40.refs_1_, bf16[256,256]{1,0:T(8,128)(2,1)} %get-tuple-element.55.refs_2_, bf16[256,384]{1,0:T(8,128)(2,1)} %collective-permute-done.17.refs_3_), custom_call_target="tpu_custom_call" | custom-call | flops 2000000000 | bytes 6000000 | tf_op jit(solution)/shard_map/join_heads/pallas_call | solution.py:56
Async XLA Ops:
  0.6 26.5 %collective-permute-start.3 = (bf16[256,2048]{1,0:T(8,128)(2,1)}, bf16[256,2048]{1,0:T(8,128)(2,1)}, u32[]{:S(2)}, u32[]{:S(2)}) collective-permute-start(bf16[256,2048]{1,0:T(8,128)(2,1)} %bitcast.29), channel_id=1, source_target_pairs={{0,1},{1,0},{2,3},{3,2},{4,5},{5,4},{6,7},{7,6},{8,9},{9,8},{10,11... | collective-permute-start | bytes 3145736 | tf_op jit(solution)/shard_map/ppermute | solution.py:615
  6.6 7.5 %collective-permute-start = (bf16[256,256]{1,0:T(8,128)(2,1)}, bf16[256,256]{1,0:T(8,128)(2,1)}, u32[]{:S(2)}, u32[]{:S(2)}) collective-permute-start(bf16[256,256]{1,0:T(8,128)(2,1)} %get-tuple-element.33), channel_id=1, source_target_pairs={{0,2},{2,0},{4,6},{6,4},{8,10},{10,8},{12,14},{14,12},{1,3},{3,1},... | collective-permute-start | bytes 393224 | tf_op jit(solution)/shard_map/ppermute | solution.py:618
  8.2 8.8 %collective-permute-start.2 = (bf16[256,256]{1,0:T(8,128)(2,1)}, bf16[256,256]{1,0:T(8,128)(2,1)}, u32[]{:S(2)}, u32[]{:S(2)}) collective-permute-start(bf16[256,256]{1,0:T(8,128)(2,1)} %get-tuple-element.34.refs_6_), channel_id=1, source_target_pairs={{0,12},{2,14},{4,0},{6,2},{8,4},{10,6},{12,8},{14,10},{1,13},{3,15... | collective-permute-start | bytes 393224 | tf_op jit(solution)/shard_map/ppermute | solution.py:620
  11.8 8.6 %collective-permute-start.1 = (bf16[256,256]{1,0:T(8,128)(2,1)}, bf16[256,256]{1,0:T(8,128)(2,1)}, u32[]{:S(2)}, u32[]{:S(2)}) collective-permute-start(bf16[256,256]{1,0:T(8,128)(2,1)} %get-tuple-element.34.refs_6_), channel_id=1, source_target_pairs={{0,4},{2,6},{4,8},{6,10},{8,12},{10,14},{12,0},{14,2},{1,5},{3,7},... | collective-permute-start | bytes 393224 | tf_op jit(solution)/shard_map/ppermute | solution.py:620
  11.8 24.3 %collective-permute-start.6 = (bf16[256,256]{1,0:T(8,128)(2,1)}, bf16[256,256]{1,0:T(8,128)(2,1)}, u32[]{:S(2)}, u32[]{:S(2)}) collective-permute-start(bf16[256,256]{1,0:T(8,128)(2,1)} %get-tuple-element.34.refs_6_), channel_id=1, source_target_pairs={{0,8},{2,10},{4,12},{6,14},{8,0},{10,2},{12,4},{14,6},{1,9},{3,11}... | collective-permute-start | bytes 393224 | tf_op jit(solution)/shard_map/ppermute | solution.py:620
  14.2 22.0 %collective-permute-start.8 = (bf16[256,256]{1,0:T(8,128)(2,1)}, bf16[256,256]{1,0:T(8,128)(2,1)}, u32[]{:S(2)}, u32[]{:S(2)}) collective-permute-start(bf16[256,256]{1,0:T(8,128)(2,1)} %collective-permute-done.refs_0_.refs_7_), channel_id=1, source_target_pairs={{0,12},{2,14},{4,0},{6,2},{8,4},{10,6},{12,8},{14,10},{1,13},{3,15... | collective-permute-start | bytes 393224 | tf_op jit(solution)/shard_map/ppermute | solution.py:620
  17.0 19.2 %collective-permute-start.7 = (bf16[256,256]{1,0:T(8,128)(2,1)}, bf16[256,256]{1,0:T(8,128)(2,1)}, u32[]{:S(2)}, u32[]{:S(2)}) collective-permute-start(bf16[256,256]{1,0:T(8,128)(2,1)} %collective-permute-done.refs_0_.refs_7_), channel_id=1, source_target_pairs={{0,8},{2,10},{4,12},{6,14},{8,0},{10,2},{12,4},{14,6},{1,9},{3,11}... | collective-permute-start | bytes 393224 | tf_op jit(solution)/shard_map/ppermute | solution.py:620
  20.4 15.8 %collective-permute-start.5 = (bf16[256,256]{1,0:T(8,128)(2,1)}, bf16[256,256]{1,0:T(8,128)(2,1)}, u32[]{:S(2)}, u32[]{:S(2)}) collective-permute-start(bf16[256,256]{1,0:T(8,128)(2,1)} %collective-permute-done.refs_0_.refs_7_), channel_id=1, source_target_pairs={{0,4},{2,6},{4,8},{6,10},{8,12},{10,14},{12,0},{14,2},{1,5},{3,7},... | collective-permute-start | bytes 393224 | tf_op jit(solution)/shard_map/ppermute | solution.py:620
  30.7 5.6 %collective-permute-start.4 = (bf16[2,128,256]{2,1,0:T(8,128)(2,1)}, bf16[2,128,256]{2,1,0:T(8,128)(2,1)}, u32[]{:S(2)}, u32[]{:S(2)}) collective-permute-start(bf16[2,128,256]{2,1,0:T(8,128)(2,1)} %get-tuple-element.36), channel_id=1, source_target_pairs={{0,2},{2,0},{4,6},{6,4},{8,10},{10,8},{12,14},{14,12},{1,3},{3,1},... | collective-permute-start | bytes 393224 | tf_op jit(solution)/shard_map/ppermute | solution.py:629
  36.1 9.0 %collective-permute-start.9 = (bf16[2,4,256,256]{3,2,1,0:T(8,128)(2,1)}, bf16[2,4,256,256]{3,2,1,0:T(8,128)(2,1)}, u32[]{:S(2)}, u32[]{:S(2)}) collective-permute-start(bf16[2,4,256,256]{3,2,1,0:T(8,128)(2,1)} %get-tuple-element.44), channel_id=1, source_target_pairs={{0,16},{16,0},{1,17},{17,1},{2,18},{18,2},{3,19},{19,3},{4,20},{20... | collective-permute-start | bytes 3145736 | tf_op jit(solution)/shard_map/ppermute | solution.py:632
  45.1 5.8 %collective-permute-start.12 = (bf16[128,256]{1,0:T(8,128)(2,1)}, bf16[128,256]{1,0:T(8,128)(2,1)}, u32[]{:S(2)}, u32[]{:S(2)}) collective-permute-start(bf16[128,256]{1,0:T(8,128)(2,1)} %get-tuple-element.46), channel_id=1, source_target_pairs={{0,18},{2,16},{4,22},{6,20},{8,26},{10,24},{12,30},{14,28},{16,2},... | collective-permute-start | bytes 196616 | tf_op jit(solution)/shard_map/ppermute | solution.py:646
  45.6 6.3 %collective-permute-start.10 = (bf16[128,256]{1,0:T(8,128)(2,1)}, bf16[128,256]{1,0:T(8,128)(2,1)}, u32[]{:S(2)}, u32[]{:S(2)}) collective-permute-start(bf16[128,256]{1,0:T(8,128)(2,1)} %get-tuple-element.46), channel_id=1, source_target_pairs={{0,2},{2,0},{4,6},{6,4},{8,10},{10,8},{12,14},{14,12},{1,3},{3,1},... | collective-permute-start | bytes 196616 | tf_op jit(solution)/shard_map/ppermute | solution.py:646
  47.3 4.6 %collective-permute-start.11 = (bf16[128,256]{1,0:T(8,128)(2,1)}, bf16[128,256]{1,0:T(8,128)(2,1)}, u32[]{:S(2)}, u32[]{:S(2)}) collective-permute-start(bf16[128,256]{1,0:T(8,128)(2,1)} %get-tuple-element.45.refs_1_.refs_2_), channel_id=1, source_target_pairs={{0,16},{2,18},{4,20},{6,22},{8,24},{10,26},{12,28},{14,30},{16,0},... | collective-permute-start | bytes 196616 | tf_op jit(solution)/shard_map/ppermute | solution.py:646
  47.3 25.0 %collective-permute-start.14 = (bf16[2,256,256]{2,1,0:T(8,128)(2,1)}, bf16[2,256,256]{2,1,0:T(8,128)(2,1)}, u32[]{:S(2)}, u32[]{:S(2)}) collective-permute-start(bf16[2,256,256]{2,1,0:T(8,128)(2,1)} %get-tuple-element.52), channel_id=1, source_target_pairs={{0,12},{2,14},{4,0},{6,2},{8,4},{10,6},{12,8},{14,10},{1,13},{3,15... | collective-permute-start | bytes 786440 | tf_op jit(solution)/shard_map/ppermute | solution.py:649
  50.9 29.3 %collective-permute-start.15 = (bf16[2,256,256]{2,1,0:T(8,128)(2,1)}, bf16[2,256,256]{2,1,0:T(8,128)(2,1)}, u32[]{:S(2)}, u32[]{:S(2)}) collective-permute-start(bf16[2,256,256]{2,1,0:T(8,128)(2,1)} %get-tuple-element.53), channel_id=1, source_target_pairs={{0,8},{2,10},{4,12},{6,14},{8,0},{10,2},{12,4},{14,6},{1,9},{3,11}... | collective-permute-start | bytes 786440 | tf_op jit(solution)/shard_map/ppermute | solution.py:649
  50.9 29.3 %collective-permute-start.16 = (bf16[2,256,256]{2,1,0:T(8,128)(2,1)}, bf16[2,256,256]{2,1,0:T(8,128)(2,1)}, u32[]{:S(2)}, u32[]{:S(2)}) collective-permute-start(bf16[2,256,256]{2,1,0:T(8,128)(2,1)} %get-tuple-element.54), channel_id=1, source_target_pairs={{0,4},{2,6},{4,8},{6,10},{8,12},{10,14},{12,0},{14,2},{1,5},{3,7},... | collective-permute-start | bytes 786440 | tf_op jit(solution)/shard_map/ppermute | solution.py:649
  55.4 12.4 %collective-permute-start.13 = (bf16[3,256,256]{2,1,0:T(8,128)(2,1)}, bf16[3,256,256]{2,1,0:T(8,128)(2,1)}, u32[]{:S(2)}, u32[]{:S(2)}) collective-permute-start(bf16[3,256,256]{2,1,0:T(8,128)(2,1)} %weight_sent.1.refs_0_), channel_id=1, source_target_pairs={{0,2},{2,0},{4,6},{6,4},{8,10},{10,8},{12,14},{14,12},{1,3},{3,1},... | collective-permute-start | bytes 1179656 | tf_op jit(solution)/shard_map/ppermute | solution.py:655
  59.4 24.3 %collective-permute-start.18 = (bf16[1,256,256]{2,1,0:T(8,128)(2,1)}, bf16[1,256,256]{2,1,0:T(8,128)(2,1)}, u32[]{:S(2)}, u32[]{:S(2)}) collective-permute-start(bf16[1,256,256]{2,1,0:T(8,128)(2,1)} %weight_own.1.refs_0_), channel_id=1, source_target_pairs={{0,2},{2,0},{4,6},{6,4},{8,10},{10,8},{12,14},{14,12},{1,3},{3,1},... | collective-permute-start | bytes 393224 | tf_op jit(solution)/shard_map/ppermute | solution.py:657
  69.8 13.9 %collective-permute-start.19 = (bf16[256,256]{1,0:T(8,128)(2,1)}, bf16[256,256]{1,0:T(8,128)(2,1)}, u32[]{:S(2)}, u32[]{:S(2)}) collective-permute-start(bf16[256,256]{1,0:T(8,128)(2,1)} %get-tuple-element.60), channel_id=1, source_target_pairs={{0,4},{2,6},{4,8},{6,10},{8,12},{10,14},{12,0},{14,2},{1,5},{3,7},... | collective-permute-start | bytes 393224 | tf_op jit(solution)/shard_map/ppermute | solution.py:661
  72.3 11.4 %collective-permute-start.20 = (bf16[256,256]{1,0:T(8,128)(2,1)}, bf16[256,256]{1,0:T(8,128)(2,1)}, u32[]{:S(2)}, u32[]{:S(2)}) collective-permute-start(bf16[256,256]{1,0:T(8,128)(2,1)} %get-tuple-element.61), channel_id=1, source_target_pairs={{0,8},{2,10},{4,12},{6,14},{8,0},{10,2},{12,4},{14,6},{1,9},{3,11}... | collective-permute-start | bytes 393224 | tf_op jit(solution)/shard_map/ppermute | solution.py:661
  80.2 5.3 %collective-permute-start.21 = (bf16[256,256]{1,0:T(8,128)(2,1)}, bf16[256,256]{1,0:T(8,128)(2,1)}, u32[]{:S(2)}, u32[]{:S(2)}) collective-permute-start(bf16[256,256]{1,0:T(8,128)(2,1)} %get-tuple-element.49.refs_0_), channel_id=1, source_target_pairs={{0,12},{2,14},{4,0},{6,2},{8,4},{10,6},{12,8},{14,10},{1,13},{3,15... | collective-permute-start | bytes 393224 | tf_op jit(solution)/shard_map/ppermute | solution.py:661
  82.3 6.5 %collective-permute-start.17 = (bf16[256,384]{1,0:T(8,128)(2,1)}, bf16[256,384]{1,0:T(8,128)(2,1)}, u32[]{:S(2)}, u32[]{:S(2)}) collective-permute-start(bf16[256,384]{1,0:T(8,128)(2,1)} %get-tuple-element.56), channel_id=1, source_target_pairs={{0,2},{2,0},{4,6},{6,4},{8,10},{10,8},{12,14},{14,12},{1,3},{3,1},... | collective-permute-start | bytes 589832 | tf_op jit(solution)/shard_map/ppermute | solution.py:664

commit v18 on v17

--- a/solution.py
+++ b/solution.py
@@ -645,10 +645,9 @@
             axes = ("dp", "ctx") if step else "ctx"
             attn.append(lax.ppermute(held, axes, pairs) if step or side else held)
 
-    terms = [
-        lax.ppermute(part, "ctx", ctx_pairs(-step, 0)) if step else part
-        for step, part in enumerate(parts)
-    ]
+    far_first = sorted(range(1, outer), key=lambda step: -min(step, outer - step))
+    terms = [lax.ppermute(parts[step], "ctx", ctx_pairs(-step, 0)) for step in far_first]
+    terms = [parts[0], *terms]
 
     order = list(range(1, outer)) + [0]
     send = weight_terms(at, attn, grad_blocks, 1, order[:-1], "weight_sent")

time: 92 us -> 90.8 us (0.987)
  waiting for transfers between devices: 16.7 us -> 13.7 us
  starting transfers between devices: 30.7 us -> 32.2 us
    ppermute x3, waiting for transfers between devices: 6.86 us -> 0.01 us  [per_device(): lax.ppermute(parts[step], 'ctx', ctx_pairs(-step, 0))]
    ppermute x3, waiting for transfers between devices: 1.88 us -> 7.12 us  [per_device(): lax.ppermute(held, 'ctx', ctx_pairs(step, 0))]
    ppermute x1, waiting for transfers between devices: 1.38 us -> 0.01 us  [per_device(): terms_recv = lax.ppermute(terms_theirs, 'ctx', ctx_pairs(0, 1))]
    ppermute x3, starting transfers between devices: 3.58 us -> 4.9 us  [per_device(): lax.ppermute(held, 'ctx', ctx_pairs(step, 0))]
  transfers between devices with their start and end apart: 22 -> 22, of which waited for: 6 -> 5; matrix products, arithmetic and copies ran while one was open for 4% -> 4% of each run, Pallas kernels for 40% -> 41%
where the time goes in v18:
time: 90.8 us; the launch traced here: 89.8 us
  Pallas kernels  39.3 us (43%)
  starting transfers between devices  32.2 us (35%)
  waiting for transfers between devices  13.7 us (15%)
  local copies, waits for them, and re-layouts  1.98 us (2%)
  other arithmetic  1.9 us (2%)
    pallas_call x11, Pallas kernels, placed(): return run(*args)  39.3 us
    ppermute x6, starting transfers between devices, per_device(): lax.ppermute(kv_recv if side else kv_mine, 'ctx', ctx_pairs(step, 0))  10.4 us
    ppermute x3, waiting for transfers between devices, per_device(): lax.ppermute(held, 'ctx', ctx_pairs(step, 0))  7.12 us
    ppermute x3, starting transfers between devices, per_device(): lax.ppermute(held, 'ctx', ctx_pairs(step, 0))  4.9 us
    ppermute x3, starting transfers between devices, per_device(): lax.ppermute(parts[step], 'ctx', ctx_pairs(-step, 0))  4.61 us
    ppermute x1, waiting for transfers between devices, per_device(): weight_recv = lax.ppermute(send, 'ctx', ctx_pairs(0, 1))  3.63 us
    ppermute x1, starting transfers between devices, per_device(): lax.ppermute(grad_own, 'tp', shift_pairs(tp_count, -step))  3.03 us
    ppermute x3, starting transfers between devices, per_device(): attn.append(lax.ppermute(held, axes, pairs) if step or side else held)  2.17 us
  transfers between devices with their start and end apart: 22, of which 5 were waited for; matrix products, arithmetic and copies ran while one was open for 4% of the time, Pallas kernels for 41%

profile of v18, /device:TPU:0, one launch (start us, length us, event | category | flops | bytes accessed | tf_op | source)
XLA Modules:
  0.0 89.8 jit_solution(11056825880865216556)
XLA Ops:
  0.6 3.0 %collective-permute-start.3 = (bf16[256,2048]{1,0:T(8,128)(2,1)}, bf16[256,2048]{1,0:T(8,128)(2,1)}, u32[]{:S(2)}, u32[]{:S(2)}) collective-permute-start(bf16[256,2048]{1,0:T(8,128)(2,1)} %bitcast.29), channel_id=1, source_target_pairs={{0,1},{1,0},{2,3},{3,2},{4,5},{5,4},{6,7},{7,6},{8,9},{9,8},{10,11... | collective-permute-start | bytes 3145736 | tf_op jit(solution)/shard_map/ppermute | solution.py:615
  3.7 0.6 stack.59.refs_0_.refs_3_.refs_1_
  4.3 2.3 %part_heads.1 = (bf16[256,256]{1,0:T(8,128)(2,1)}, bf16[256,256]{1,0:T(8,128)(2,1)}) custom-call(s32[14]{0:T(128)} %stack.59.refs_0_.refs_3_.refs_1_, bf16[256,256]{1,0:T(8,128)(2,1)} %bitcast.32, bf16[256,256]{1,0:T(8,128)(2,1)} %bitcast.33), custom_call_target="tpu_custom_call" | custom-call | flops 2000000000 | bytes 6000000 | tf_op jit(solution)/shard_map/part_heads/pallas_call | solution.py:56
  6.6 1.6 %collective-permute-start = (bf16[256,256]{1,0:T(8,128)(2,1)}, bf16[256,256]{1,0:T(8,128)(2,1)}, u32[]{:S(2)}, u32[]{:S(2)}) collective-permute-start(bf16[256,256]{1,0:T(8,128)(2,1)} %get-tuple-element.33), channel_id=1, source_target_pairs={{0,2},{2,0},{4,6},{6,4},{8,10},{10,8},{12,14},{14,12},{1,3},{3,1},... | collective-permute-start | bytes 393224 | tf_op jit(solution)/shard_map/ppermute | solution.py:618
  8.2 3.6 %collective-permute-start.2 = (bf16[256,256]{1,0:T(8,128)(2,1)}, bf16[256,256]{1,0:T(8,128)(2,1)}, u32[]{:S(2)}, u32[]{:S(2)}) collective-permute-start(bf16[256,256]{1,0:T(8,128)(2,1)} %get-tuple-element.34.refs_6_), channel_id=1, source_target_pairs={{0,12},{2,14},{4,0},{6,2},{8,4},{10,6},{12,8},{14,10},{1,13},{3,15... | collective-permute-start | bytes 393224 | tf_op jit(solution)/shard_map/ppermute | solution.py:620
  11.8 0.0 collective-permute-start.1
  11.8 1.0 %collective-permute-start.6 = (bf16[256,256]{1,0:T(8,128)(2,1)}, bf16[256,256]{1,0:T(8,128)(2,1)}, u32[]{:S(2)}, u32[]{:S(2)}) collective-permute-start(bf16[256,256]{1,0:T(8,128)(2,1)} %get-tuple-element.34.refs_6_), channel_id=1, source_target_pairs={{0,8},{2,10},{4,12},{6,14},{8,0},{10,2},{12,4},{14,6},{1,9},{3,11}... | collective-permute-start | bytes 393224 | tf_op jit(solution)/shard_map/ppermute | solution.py:620
  12.8 1.3 %copy.11.refs_4_ = s32[8,3]{1,0:T(8,128)} copy(s32[8,3]{0,1:T(4,128)} %param.12) | data formatting | bytes 192 | tf_op args[5]
  14.2 0.0 collective-permute-done.refs_0_.refs_7_
  14.2 2.8 %collective-permute-start.8 = (bf16[256,256]{1,0:T(8,128)(2,1)}, bf16[256,256]{1,0:T(8,128)(2,1)}, u32[]{:S(2)}, u32[]{:S(2)}) collective-permute-start(bf16[256,256]{1,0:T(8,128)(2,1)} %collective-permute-done.refs_0_.refs_7_), channel_id=1, source_target_pairs={{0,12},{2,14},{4,0},{6,2},{8,4},{10,6},{12,8},{14,10},{1,13},{3,15... | collective-permute-start | bytes 393224 | tf_op jit(solution)/shard_map/ppermute | solution.py:620
  17.0 0.0 collective-permute-done.2.refs_2_.refs_12_
  17.0 2.0 %collective-permute-start.7 = (bf16[256,256]{1,0:T(8,128)(2,1)}, bf16[256,256]{1,0:T(8,128)(2,1)}, u32[]{:S(2)}, u32[]{:S(2)}) collective-permute-start(bf16[256,256]{1,0:T(8,128)(2,1)} %collective-permute-done.refs_0_.refs_7_), channel_id=1, source_target_pairs={{0,8},{2,10},{4,12},{6,14},{8,0},{10,2},{12,4},{14,6},{1,9},{3,11}... | collective-permute-start | bytes 393224 | tf_op jit(solution)/shard_map/ppermute | solution.py:620
  19.0 1.4 %collective-permute-done.1.refs_1_.refs_8_ = bf16[256,256]{1,0:T(8,128)(2,1)} collective-permute-done((bf16[256,256]{1,0:T(8,128)(2,1)}, bf16[256,256]{1,0:T(8,128)(2,1)}, u32[]{:S(2)}, u32[]{:S(2)}) %collective-permute-start.1) | collective-permute-done | bytes 131104 | tf_op jit(solution)/shard_map/ppermute | solution.py:620
  20.4 1.0 %collective-permute-start.5 = (bf16[256,256]{1,0:T(8,128)(2,1)}, bf16[256,256]{1,0:T(8,128)(2,1)}, u32[]{:S(2)}, u32[]{:S(2)}) collective-permute-start(bf16[256,256]{1,0:T(8,128)(2,1)} %collective-permute-done.refs_0_.refs_7_), channel_id=1, source_target_pairs={{0,4},{2,6},{4,8},{6,10},{8,12},{10,14},{12,0},{14,2},{1,5},{3,7},... | collective-permute-start | bytes 393224 | tf_op jit(solution)/shard_map/ppermute | solution.py:620
  21.4 4.3 %prelude.1 = (f32[256,256]{1,0:T(8,128)}, bf16[2048,128]{1,0:T(8,128)(2,1)}, f32[8,512]{1,0:T(8,128)}) custom-call(bf16[256,256]{1,0:T(8,128)(2,1)} %collective-permute-done.refs_0_.refs_7_, bf16[256,256]{1,0:T(8,128)(2,1)} %collective-permute-done.1.refs_1_.refs_8_, bf16[256,256]{1,0:T(8,128)(2,1)} %collective-permute-done.2.refs_2_.refs_12_, ...), custom_call_target="tpu_custom_call" | custom-call | flops 4000000000 | bytes 12000000 | tf_op jit(solution)/shard_map/prelude/pallas_call | solution.py:56
  25.7 1.5 %collective-permute-done.3.refs_4_.refs_3_ = bf16[256,2048]{1,0:T(8,128)(2,1)} collective-permute-done((bf16[256,2048]{1,0:T(8,128)(2,1)}, bf16[256,2048]{1,0:T(8,128)(2,1)}, u32[]{:S(2)}, u32[]{:S(2)}) %collective-permute-start.3) | collective-permute-done | bytes 1048608 | tf_op jit(solution)/shard_map/ppermute | solution.py:615
  27.1 3.5 %grad_heads.1 = (bf16[128,256]{1,0:T(8,128)(2,1)}, bf16[2,128,256]{2,1,0:T(8,128)(2,1)}) custom-call(s32[14]{0:T(128)} %stack.59.refs_0_.refs_3_.refs_1_, f32[256,256]{1,0:T(8,128)} %get-tuple-element.35.refs_1_, bf16[256,256]{1,0:T(8,128)(2,1)} %bitcast.34, bf16[256,4096]{1,0:T(8,128)(2,1)} %refs_3_.1, bf16[256,2048]{1,0:T(8,128)(2,1)} %collective-permute-done.3.refs_4_.refs_3_), custom_call_target="tpu_custom_call" | custom-call | flops 3000000000 | bytes 9000000 | tf_op jit(solution)/shard_map/grad_heads/pallas_call | solution.py:56
  30.7 1.8 %collective-permute-start.4 = (bf16[2,128,256]{2,1,0:T(8,128)(2,1)}, bf16[2,128,256]{2,1,0:T(8,128)(2,1)}, u32[]{:S(2)}, u32[]{:S(2)}) collective-permute-start(bf16[2,128,256]{2,1,0:T(8,128)(2,1)} %get-tuple-element.36), channel_id=1, source_target_pairs={{0,2},{2,0},{4,6},{6,4},{8,10},{10,8},{12,14},{14,12},{1,3},{3,1},... | collective-permute-start | bytes 393224 | tf_op jit(solution)/shard_map/ppermute | solution.py:629
  32.4 3.7 %pick_columns.1 = (bf16[2,4,256,256]{3,2,1,0:T(8,128)(2,1)}, bf16[2,4,256,256]{3,2,1,0:T(8,128)(2,1)}) custom-call(bf16[128,256]{1,0:T(8,128)(2,1)} %get-tuple-element.37.refs_3_.refs_0_, s32[14]{0:T(128)} %stack.59.refs_0_.refs_3_.refs_1_, bf16[256,2048]{1,0:T(8,128)(2,1)} %bitcast.31, bf16[256,2048]{1,0:T(8,128)(2,1)} %collective-permute-done.3.refs_4_.refs_3_), custom_call_target="tpu_custom_call" | custom-call | flops 3000000000 | bytes 9000000 | tf_op jit(solution)/shard_map/pick_columns/pallas_call | solution.py:56
  36.1 0.0 collective-permute-done.6.refs_10_
  36.1 0.1 collective-permute-start.9
  36.2 0.0 collective-permute-done.8.refs_13_
  36.2 0.0 collective-permute-done.7.refs_11_
  36.2 0.0 collective-permute-done.5.refs_9_
  36.2 0.0 collective-permute-done.4.refs_2_
  36.2 8.9 %attention.1 = (bf16[128,256]{1,0:T(8,128)(2,1)}, bf16[128,256]{1,0:T(8,128)(2,1)}, bf16[256,128]{1,0:T(8,128)(2,1)}, bf16[256,128]{1,0:T(8,128)(2,1)}, bf16[2,2...) custom-call(s32[14]{0:T(128)} %stack.59.refs_0_.refs_3_.refs_1_, ...), custom_call_target="tpu_custom_call" | custom-call | flops 20000000000 | bytes 60000000 | tf_op jit(solution)/shard_map/attention/pallas_call | solution.py:56
  45.1 0.0 collective-permute-done.9.refs_6_.refs_7_
  45.1 0.5 collective-permute-start.12
  45.6 1.7 %collective-permute-start.10 = (bf16[128,256]{1,0:T(8,128)(2,1)}, bf16[128,256]{1,0:T(8,128)(2,1)}, u32[]{:S(2)}, u32[]{:S(2)}) collective-permute-start(bf16[128,256]{1,0:T(8,128)(2,1)} %get-tuple-element.46), channel_id=1, source_target_pairs={{0,2},{2,0},{4,6},{6,4},{8,10},{10,8},{12,14},{14,12},{1,3},{3,1},... | collective-permute-start | bytes 196616 | tf_op jit(solution)/shard_map/ppermute | solution.py:646
  47.3 0.0 collective-permute-start.11
  47.3 2.6 %collective-permute-start.14 = (bf16[2,256,256]{2,1,0:T(8,128)(2,1)}, bf16[2,256,256]{2,1,0:T(8,128)(2,1)}, u32[]{:S(2)}, u32[]{:S(2)}) collective-permute-start(bf16[2,256,256]{2,1,0:T(8,128)(2,1)} %get-tuple-element.52), channel_id=1, source_target_pairs={{0,8},{2,10},{4,12},{6,14},{8,0},{10,2},{12,4},{14,6},{1,9},{3,11}... | collective-permute-start | bytes 786440 | tf_op jit(solution)/shard_map/ppermute | solution.py:649
  49.9 1.4 %collective-permute-start.15 = (bf16[2,256,256]{2,1,0:T(8,128)(2,1)}, bf16[2,256,256]{2,1,0:T(8,128)(2,1)}, u32[]{:S(2)}, u32[]{:S(2)}) collective-permute-start(bf16[2,256,256]{2,1,0:T(8,128)(2,1)} %get-tuple-element.53), channel_id=1, source_target_pairs={{0,12},{2,14},{4,0},{6,2},{8,4},{10,6},{12,8},{14,10},{1,13},{3,15... | collective-permute-start | bytes 786440 | tf_op jit(solution)/shard_map/ppermute | solution.py:649
  51.3 0.0 collective-permute-done.12.refs_4_.refs_5_
  51.3 0.7 collective-permute-start.16
  51.9 0.0 collective-permute-done.10.refs_2_.refs_3_
  51.9 0.0 collective-permute-done.11.refs_3_.refs_4_
  51.9 3.5 %weight_sent.1.refs_0_ = bf16[3,256,256]{2,1,0:T(8,128)(2,1)} custom-call(s32[14]{0:T(128)} %stack.59.refs_0_.refs_3_.refs_1_, bf16[128,256]{1,0:T(8,128)(2,1)} %get-tuple-element.45.refs_1_.refs_2_, bf16[128,256]{1,0:T(8,128)(2,1)} %collective-permute-done.10.refs_2_.refs_3_, bf16[128,256]{1,0:T(8,128)(2,1)} %collective-permute-done.11.refs_3_.refs_4_, ...), custom_call_target="tpu_custom_call" | custom-call | flops 4000000000 | bytes 12000000 | tf_op jit(solution)/shard_map/weight_sent/pallas_call | solution.py:56
  55.4 1.3 %collective-permute-start.13 = (bf16[3,256,256]{2,1,0:T(8,128)(2,1)}, bf16[3,256,256]{2,1,0:T(8,128)(2,1)}, u32[]{:S(2)}, u32[]{:S(2)}) collective-permute-start(bf16[3,256,256]{2,1,0:T(8,128)(2,1)} %weight_sent.1.refs_0_), channel_id=1, source_target_pairs={{0,2},{2,0},{4,6},{6,4},{8,10},{10,8},{12,14},{14,12},{1,3},{3,1},... | collective-permute-start | bytes 1179656 | tf_op jit(solution)/shard_map/ppermute | solution.py:654
  56.7 2.7 %weight_own.1.refs_0_ = bf16[1,256,256]{2,1,0:T(8,128)(2,1)} custom-call(bf16[3,256,256]{2,1,0:T(8,128)(2,1)} %weight_sent.1.refs_0_, s32[14]{0:T(128)} %stack.59.refs_0_.refs_3_.refs_1_, bf16[128,256]{1,0:T(8,128)(2,1)} %get-tuple-element.45.refs_1_.refs_2_, bf16[128,256]{1,0:T(8,128)(2,1)} %collective-permute-done.10.refs_2_.refs_3_, ...), custom_call_target="tpu_custom_call" | custom-call | flops 4000000000 | bytes 12000000 | tf_op jit(solution)/shard_map/weight_own/pallas_call | solution.py:56
  59.4 0.9 collective-permute-start.18
  60.3 3.9 %weight_kept.1.refs_0_ = bf16[4,256,256]{2,1,0:T(8,128)(2,1)} custom-call(bf16[1,256,256]{2,1,0:T(8,128)(2,1)} %weight_own.1.refs_0_, s32[14]{0:T(128)} %stack.59.refs_0_.refs_3_.refs_1_, bf16[128,256]{1,0:T(8,128)(2,1)} %get-tuple-element.45.refs_1_.refs_2_, bf16[128,256]{1,0:T(8,128)(2,1)} %collective-permute-done.10.refs_2_.refs_3_, ...), custom_call_target="tpu_custom_call" | custom-call | flops 4000000000 | bytes 12000000 | tf_op jit(solution)/shard_map/weight_kept/pallas_call | solution.py:56
  64.2 3.6 %collective-permute-done.13.refs_1_ = bf16[3,256,256]{2,1,0:T(8,128)(2,1)} collective-permute-done((bf16[3,256,256]{2,1,0:T(8,128)(2,1)}, bf16[3,256,256]{2,1,0:T(8,128)(2,1)}, u32[]{:S(2)}, u32[]{:S(2)}) %collective-permute-start.13) | collective-permute-done | bytes 393248 | tf_op jit(solution)/shard_map/ppermute | solution.py:654
  67.8 2.0 %weight_add.1 = (bf16[256,256]{1,0:T(8,128)(2,1)}, bf16[256,256]{1,0:T(8,128)(2,1)}, bf16[256,256]{1,0:T(8,128)(2,1)}) custom-call(bf16[4,256,256]{2,1,0:T(8,128)(2,1)} %weight_kept.1.refs_0_, bf16[3,256,256]{2,1,0:T(8,128)(2,1)} %collective-permute-done.13.refs_1_), custom_call_target="tpu_custom_call" | custom-call | flops 2000000000 | bytes 6000000 | tf_op jit(solution)/shard_map/weight_add/pallas_call | solution.py:56
  69.8 1.6 %collective-permute-start.19 = (bf16[256,256]{1,0:T(8,128)(2,1)}, bf16[256,256]{1,0:T(8,128)(2,1)}, u32[]{:S(2)}, u32[]{:S(2)}) collective-permute-start(bf16[256,256]{1,0:T(8,128)(2,1)} %get-tuple-element.60), channel_id=1, source_target_pairs={{0,4},{2,6},{4,8},{6,10},{8,12},{10,14},{12,0},{14,2},{1,5},{3,7},... | collective-permute-start | bytes 393224 | tf_op jit(solution)/shard_map/ppermute | solution.py:660
  71.4 0.0 collective-permute-done.14.refs_3_
  71.4 2.1 %collective-permute-start.20 = (bf16[256,256]{1,0:T(8,128)(2,1)}, bf16[256,256]{1,0:T(8,128)(2,1)}, u32[]{:S(2)}, u32[]{:S(2)}) collective-permute-start(bf16[256,256]{1,0:T(8,128)(2,1)} %get-tuple-element.61), channel_id=1, source_target_pairs={{0,8},{2,10},{4,12},{6,14},{8,0},{10,2},{12,4},{14,6},{1,9},{3,11}... | collective-permute-start | bytes 393224 | tf_op jit(solution)/shard_map/ppermute | solution.py:660
  73.6 0.0 collective-permute-done.15.refs_4_
  73.6 1.1 %collective-permute-start.21 = (bf16[256,256]{1,0:T(8,128)(2,1)}, bf16[256,256]{1,0:T(8,128)(2,1)}, u32[]{:S(2)}, u32[]{:S(2)}) collective-permute-start(bf16[256,256]{1,0:T(8,128)(2,1)} %get-tuple-element.49.refs_0_), channel_id=1, source_target_pairs={{0,12},{2,14},{4,0},{6,2},{8,4},{10,6},{12,8},{14,10},{1,13},{3,15... | collective-permute-start | bytes 393224 | tf_op jit(solution)/shard_map/ppermute | solution.py:660
  74.7 0.0 collective-permute-done.16.refs_5_
  74.7 2.1 %add_terms.1 = (bf16[256,256]{1,0:T(8,128)(2,1)}, bf16[256,384]{1,0:T(8,128)(2,1)}) custom-call(bf16[256,256]{1,0:T(8,128)(2,1)} %get-tuple-element.49.refs_0_, bf16[256,128]{1,0:T(8,128)(2,1)} %get-tuple-element.50.refs_1_, bf16[2,256,256]{2,1,0:T(8,128)(2,1)} %get-tuple-element.51.refs_2_, bf16[2,256,256]{2,1,0:T(8,128)(2,1)} %collective-permute-done.14.refs_3_, ...), custom_call_target="tpu_custom_call" | custom-call | flops 2000000000 | bytes 6000000 | tf_op jit(solution)/shard_map/add_terms/pallas_call | solution.py:56
  76.8 1.5 %collective-permute-start.17 = (bf16[256,384]{1,0:T(8,128)(2,1)}, bf16[256,384]{1,0:T(8,128)(2,1)}, u32[]{:S(2)}, u32[]{:S(2)}) collective-permute-start(bf16[256,384]{1,0:T(8,128)(2,1)} %get-tuple-element.56), channel_id=1, source_target_pairs={{0,2},{2,0},{4,6},{6,4},{8,10},{10,8},{12,14},{14,12},{1,3},{3,1},... | collective-permute-start | bytes 589832 | tf_op jit(solution)/shard_map/ppermute | solution.py:663
  78.3 0.0 collective-permute-done.18
  78.3 0.0 collective-permute-done.19
  78.3 4.4 %collective-permute-done.20 = bf16[256,256]{1,0:T(8,128)(2,1)} collective-permute-done((bf16[256,256]{1,0:T(8,128)(2,1)}, bf16[256,256]{1,0:T(8,128)(2,1)}, u32[]{:S(2)}, u32[]{:S(2)}) %collective-permute-start.20) | collective-permute-done | bytes 131104 | tf_op jit(solution)/shard_map/ppermute | solution.py:660
  82.7 2.7 %collective-permute-done.21 = bf16[256,256]{1,0:T(8,128)(2,1)} collective-permute-done((bf16[256,256]{1,0:T(8,128)(2,1)}, bf16[256,256]{1,0:T(8,128)(2,1)}, u32[]{:S(2)}, u32[]{:S(2)}) %collective-permute-start.21) | collective-permute-done | bytes 131104 | tf_op jit(solution)/shard_map/ppermute | solution.py:660
  85.4 1.9 %fusion.2 = bf16[256,256]{1,0:T(8,128)(2,1)} fusion(bf16[256,256]{1,0:T(8,128)(2,1)} %collective-permute-done.21, bf16[256,256]{1,0:T(8,128)(2,1)} %collective-permute-done.20, bf16[256,256]{1,0:T(8,128)(2,1)} %collective-permute-done.19, bf16[1,256,256]{2,1,0:T(8,128)(2,1)} %collective-permute-done.18, bf16[4,256,256]{2,1,0:T(8,128)(2,1)} %weight_kept.1.refs_0_), kind=kLoop, calls=%fused_computation.3 | loop fusion | flops 655360 | bytes 786432 | tf_op jit(solution)/shard_map/convert_element_type | solution.py:668
  87.3 0.0 collective-permute-done.17.refs_3_
  87.3 2.5 %join_heads.1 = (bf16[256,256]{1,0:T(8,128)(2,1)}, bf16[256,256]{1,0:T(8,128)(2,1)}, bf16[256,256]{1,0:T(8,128)(2,1)}) custom-call(s32[14]{0:T(128)} %stack.59.refs_0_.refs_3_.refs_1_, bf16[256,128]{1,0:T(8,128)(2,1)} %get-tuple-element.40.refs_1_, bf16[256,256]{1,0:T(8,128)(2,1)} %get-tuple-element.55.refs_2_, bf16[256,384]{1,0:T(8,128)(2,1)} %collective-permute-done.17.refs_3_), custom_call_target="tpu_custom_call" | custom-call | flops 2000000000 | bytes 6000000 | tf_op jit(solution)/shard_map/join_heads/pallas_call | solution.py:56
Async XLA Ops:
  0.6 26.5 %collective-permute-start.3 = (bf16[256,2048]{1,0:T(8,128)(2,1)}, bf16[256,2048]{1,0:T(8,128)(2,1)}, u32[]{:S(2)}, u32[]{:S(2)}) collective-permute-start(bf16[256,2048]{1,0:T(8,128)(2,1)} %bitcast.29), channel_id=1, source_target_pairs={{0,1},{1,0},{2,3},{3,2},{4,5},{5,4},{6,7},{7,6},{8,9},{9,8},{10,11... | collective-permute-start | bytes 3145736 | tf_op jit(solution)/shard_map/ppermute | solution.py:615
  6.6 7.5 %collective-permute-start = (bf16[256,256]{1,0:T(8,128)(2,1)}, bf16[256,256]{1,0:T(8,128)(2,1)}, u32[]{:S(2)}, u32[]{:S(2)}) collective-permute-start(bf16[256,256]{1,0:T(8,128)(2,1)} %get-tuple-element.33), channel_id=1, source_target_pairs={{0,2},{2,0},{4,6},{6,4},{8,10},{10,8},{12,14},{14,12},{1,3},{3,1},... | collective-permute-start | bytes 393224 | tf_op jit(solution)/shard_map/ppermute | solution.py:618
  8.2 8.8 %collective-permute-start.2 = (bf16[256,256]{1,0:T(8,128)(2,1)}, bf16[256,256]{1,0:T(8,128)(2,1)}, u32[]{:S(2)}, u32[]{:S(2)}) collective-permute-start(bf16[256,256]{1,0:T(8,128)(2,1)} %get-tuple-element.34.refs_6_), channel_id=1, source_target_pairs={{0,12},{2,14},{4,0},{6,2},{8,4},{10,6},{12,8},{14,10},{1,13},{3,15... | collective-permute-start | bytes 393224 | tf_op jit(solution)/shard_map/ppermute | solution.py:620
  11.8 8.6 %collective-permute-start.1 = (bf16[256,256]{1,0:T(8,128)(2,1)}, bf16[256,256]{1,0:T(8,128)(2,1)}, u32[]{:S(2)}, u32[]{:S(2)}) collective-permute-start(bf16[256,256]{1,0:T(8,128)(2,1)} %get-tuple-element.34.refs_6_), channel_id=1, source_target_pairs={{0,4},{2,6},{4,8},{6,10},{8,12},{10,14},{12,0},{14,2},{1,5},{3,7},... | collective-permute-start | bytes 393224 | tf_op jit(solution)/shard_map/ppermute | solution.py:620
  11.8 24.3 %collective-permute-start.6 = (bf16[256,256]{1,0:T(8,128)(2,1)}, bf16[256,256]{1,0:T(8,128)(2,1)}, u32[]{:S(2)}, u32[]{:S(2)}) collective-permute-start(bf16[256,256]{1,0:T(8,128)(2,1)} %get-tuple-element.34.refs_6_), channel_id=1, source_target_pairs={{0,8},{2,10},{4,12},{6,14},{8,0},{10,2},{12,4},{14,6},{1,9},{3,11}... | collective-permute-start | bytes 393224 | tf_op jit(solution)/shard_map/ppermute | solution.py:620
  14.2 22.0 %collective-permute-start.8 = (bf16[256,256]{1,0:T(8,128)(2,1)}, bf16[256,256]{1,0:T(8,128)(2,1)}, u32[]{:S(2)}, u32[]{:S(2)}) collective-permute-start(bf16[256,256]{1,0:T(8,128)(2,1)} %collective-permute-done.refs_0_.refs_7_), channel_id=1, source_target_pairs={{0,12},{2,14},{4,0},{6,2},{8,4},{10,6},{12,8},{14,10},{1,13},{3,15... | collective-permute-start | bytes 393224 | tf_op jit(solution)/shard_map/ppermute | solution.py:620
  17.0 19.2 %collective-permute-start.7 = (bf16[256,256]{1,0:T(8,128)(2,1)}, bf16[256,256]{1,0:T(8,128)(2,1)}, u32[]{:S(2)}, u32[]{:S(2)}) collective-permute-start(bf16[256,256]{1,0:T(8,128)(2,1)} %collective-permute-done.refs_0_.refs_7_), channel_id=1, source_target_pairs={{0,8},{2,10},{4,12},{6,14},{8,0},{10,2},{12,4},{14,6},{1,9},{3,11}... | collective-permute-start | bytes 393224 | tf_op jit(solution)/shard_map/ppermute | solution.py:620
  20.4 15.8 %collective-permute-start.5 = (bf16[256,256]{1,0:T(8,128)(2,1)}, bf16[256,256]{1,0:T(8,128)(2,1)}, u32[]{:S(2)}, u32[]{:S(2)}) collective-permute-start(bf16[256,256]{1,0:T(8,128)(2,1)} %collective-permute-done.refs_0_.refs_7_), channel_id=1, source_target_pairs={{0,4},{2,6},{4,8},{6,10},{8,12},{10,14},{12,0},{14,2},{1,5},{3,7},... | collective-permute-start | bytes 393224 | tf_op jit(solution)/shard_map/ppermute | solution.py:620
  30.7 5.6 %collective-permute-start.4 = (bf16[2,128,256]{2,1,0:T(8,128)(2,1)}, bf16[2,128,256]{2,1,0:T(8,128)(2,1)}, u32[]{:S(2)}, u32[]{:S(2)}) collective-permute-start(bf16[2,128,256]{2,1,0:T(8,128)(2,1)} %get-tuple-element.36), channel_id=1, source_target_pairs={{0,2},{2,0},{4,6},{6,4},{8,10},{10,8},{12,14},{14,12},{1,3},{3,1},... | collective-permute-start | bytes 393224 | tf_op jit(solution)/shard_map/ppermute | solution.py:629
  36.1 9.0 %collective-permute-start.9 = (bf16[2,4,256,256]{3,2,1,0:T(8,128)(2,1)}, bf16[2,4,256,256]{3,2,1,0:T(8,128)(2,1)}, u32[]{:S(2)}, u32[]{:S(2)}) collective-permute-start(bf16[2,4,256,256]{3,2,1,0:T(8,128)(2,1)} %get-tuple-element.44), channel_id=1, source_target_pairs={{0,16},{16,0},{1,17},{17,1},{2,18},{18,2},{3,19},{19,3},{4,20},{20... | collective-permute-start | bytes 3145736 | tf_op jit(solution)/shard_map/ppermute | solution.py:632
  45.1 6.1 %collective-permute-start.12 = (bf16[128,256]{1,0:T(8,128)(2,1)}, bf16[128,256]{1,0:T(8,128)(2,1)}, u32[]{:S(2)}, u32[]{:S(2)}) collective-permute-start(bf16[128,256]{1,0:T(8,128)(2,1)} %get-tuple-element.46), channel_id=1, source_target_pairs={{0,18},{2,16},{4,22},{6,20},{8,26},{10,24},{12,30},{14,28},{16,2},... | collective-permute-start | bytes 196616 | tf_op jit(solution)/shard_map/ppermute | solution.py:646
  45.6 6.3 %collective-permute-start.10 = (bf16[128,256]{1,0:T(8,128)(2,1)}, bf16[128,256]{1,0:T(8,128)(2,1)}, u32[]{:S(2)}, u32[]{:S(2)}) collective-permute-start(bf16[128,256]{1,0:T(8,128)(2,1)} %get-tuple-element.46), channel_id=1, source_target_pairs={{0,2},{2,0},{4,6},{6,4},{8,10},{10,8},{12,14},{14,12},{1,3},{3,1},... | collective-permute-start | bytes 196616 | tf_op jit(solution)/shard_map/ppermute | solution.py:646
  47.3 4.6 %collective-permute-start.11 = (bf16[128,256]{1,0:T(8,128)(2,1)}, bf16[128,256]{1,0:T(8,128)(2,1)}, u32[]{:S(2)}, u32[]{:S(2)}) collective-permute-start(bf16[128,256]{1,0:T(8,128)(2,1)} %get-tuple-element.45.refs_1_.refs_2_), channel_id=1, source_target_pairs={{0,16},{2,18},{4,20},{6,22},{8,24},{10,26},{12,28},{14,30},{16,0},... | collective-permute-start | bytes 196616 | tf_op jit(solution)/shard_map/ppermute | solution.py:646
  47.3 24.1 %collective-permute-start.14 = (bf16[2,256,256]{2,1,0:T(8,128)(2,1)}, bf16[2,256,256]{2,1,0:T(8,128)(2,1)}, u32[]{:S(2)}, u32[]{:S(2)}) collective-permute-start(bf16[2,256,256]{2,1,0:T(8,128)(2,1)} %get-tuple-element.52), channel_id=1, source_target_pairs={{0,8},{2,10},{4,12},{6,14},{8,0},{10,2},{12,4},{14,6},{1,9},{3,11}... | collective-permute-start | bytes 786440 | tf_op jit(solution)/shard_map/ppermute | solution.py:649
  49.9 23.7 %collective-permute-start.15 = (bf16[2,256,256]{2,1,0:T(8,128)(2,1)}, bf16[2,256,256]{2,1,0:T(8,128)(2,1)}, u32[]{:S(2)}, u32[]{:S(2)}) collective-permute-start(bf16[2,256,256]{2,1,0:T(8,128)(2,1)} %get-tuple-element.53), channel_id=1, source_target_pairs={{0,12},{2,14},{4,0},{6,2},{8,4},{10,6},{12,8},{14,10},{1,13},{3,15... | collective-permute-start | bytes 786440 | tf_op jit(solution)/shard_map/ppermute | solution.py:649
  51.3 23.4 %collective-permute-start.16 = (bf16[2,256,256]{2,1,0:T(8,128)(2,1)}, bf16[2,256,256]{2,1,0:T(8,128)(2,1)}, u32[]{:S(2)}, u32[]{:S(2)}) collective-permute-start(bf16[2,256,256]{2,1,0:T(8,128)(2,1)} %get-tuple-element.54), channel_id=1, source_target_pairs={{0,4},{2,6},{4,8},{6,10},{8,12},{10,14},{12,0},{14,2},{1,5},{3,7},... | collective-permute-start | bytes 786440 | tf_op jit(solution)/shard_map/ppermute | solution.py:649
  55.4 12.4 %collective-permute-start.13 = (bf16[3,256,256]{2,1,0:T(8,128)(2,1)}, bf16[3,256,256]{2,1,0:T(8,128)(2,1)}, u32[]{:S(2)}, u32[]{:S(2)}) collective-permute-start(bf16[3,256,256]{2,1,0:T(8,128)(2,1)} %weight_sent.1.refs_0_), channel_id=1, source_target_pairs={{0,2},{2,0},{4,6},{6,4},{8,10},{10,8},{12,14},{14,12},{1,3},{3,1},... | collective-permute-start | bytes 1179656 | tf_op jit(solution)/shard_map/ppermute | solution.py:654
  59.4 18.9 %collective-permute-start.18 = (bf16[1,256,256]{2,1,0:T(8,128)(2,1)}, bf16[1,256,256]{2,1,0:T(8,128)(2,1)}, u32[]{:S(2)}, u32[]{:S(2)}) collective-permute-start(bf16[1,256,256]{2,1,0:T(8,128)(2,1)} %weight_own.1.refs_0_), channel_id=1, source_target_pairs={{0,2},{2,0},{4,6},{6,4},{8,10},{10,8},{12,14},{14,12},{1,3},{3,1},... | collective-permute-start | bytes 393224 | tf_op jit(solution)/shard_map/ppermute | solution.py:656
  69.8 8.5 %collective-permute-start.19 = (bf16[256,256]{1,0:T(8,128)(2,1)}, bf16[256,256]{1,0:T(8,128)(2,1)}, u32[]{:S(2)}, u32[]{:S(2)}) collective-permute-start(bf16[256,256]{1,0:T(8,128)(2,1)} %get-tuple-element.60), channel_id=1, source_target_pairs={{0,4},{2,6},{4,8},{6,10},{8,12},{10,14},{12,0},{14,2},{1,5},{3,7},... | collective-permute-start | bytes 393224 | tf_op jit(solution)/shard_map/ppermute | solution.py:660
  71.4 11.3 %collective-permute-start.20 = (bf16[256,256]{1,0:T(8,128)(2,1)}, bf16[256,256]{1,0:T(8,128)(2,1)}, u32[]{:S(2)}, u32[]{:S(2)}) collective-permute-start(bf16[256,256]{1,0:T(8,128)(2,1)} %get-tuple-element.61), channel_id=1, source_target_pairs={{0,8},{2,10},{4,12},{6,14},{8,0},{10,2},{12,4},{14,6},{1,9},{3,11}... | collective-permute-start | bytes 393224 | tf_op jit(solution)/shard_map/ppermute | solution.py:660
  73.6 11.8 %collective-permute-start.21 = (bf16[256,256]{1,0:T(8,128)(2,1)}, bf16[256,256]{1,0:T(8,128)(2,1)}, u32[]{:S(2)}, u32[]{:S(2)}) collective-permute-start(bf16[256,256]{1,0:T(8,128)(2,1)} %get-tuple-element.49.refs_0_), channel_id=1, source_target_pairs={{0,12},{2,14},{4,0},{6,2},{8,4},{10,6},{12,8},{14,10},{1,13},{3,15... | collective-permute-start | bytes 393224 | tf_op jit(solution)/shard_map/ppermute | solution.py:660
  76.8 10.5 %collective-permute-start.17 = (bf16[256,384]{1,0:T(8,128)(2,1)}, bf16[256,384]{1,0:T(8,128)(2,1)}, u32[]{:S(2)}, u32[]{:S(2)}) collective-permute-start(bf16[256,384]{1,0:T(8,128)(2,1)} %get-tuple-element.56), channel_id=1, source_target_pairs={{0,2},{2,0},{4,6},{6,4},{8,10},{10,8},{12,14},{14,12},{1,3},{3,1},... | collective-permute-start | bytes 589832 | tf_op jit(solution)/shard_map/ppermute | solution.py:663

commit v19 on v18

--- a/solution.py
+++ b/solution.py
@@ -649,7 +649,7 @@
     terms = [lax.ppermute(parts[step], "ctx", ctx_pairs(-step, 0)) for step in far_first]
     terms = [parts[0], *terms]
 
-    order = list(range(1, outer)) + [0]
+    order = [*far_first, 0]
     send = weight_terms(at, attn, grad_blocks, 1, order[:-1], "weight_sent")
     weight_recv = lax.ppermute(send, "ctx", ctx_pairs(0, 1))
     own_send = weight_terms(at, attn, grad_blocks, 1, order[-1:], "weight_own", (send,))

time: 90.8 us -> 90.4 us (level)
    ppermute x3, waiting for transfers between devices: 7.12 us -> 6.21 us  [per_device(): lax.ppermute(held, 'ctx', ctx_pairs(step, 0))]
    ppermute x3, starting transfers between devices: 4.9 us -> 5.81 us  [per_device(): lax.ppermute(held, 'ctx', ctx_pairs(step, 0))]
where the time goes in v19:
time: 90.4 us; the launch traced here: 89.8 us
  Pallas kernels  39.3 us (43%)
  starting transfers between devices  33.1 us (37%)
  waiting for transfers between devices  12.8 us (14%)
  local copies, waits for them, and re-layouts  1.98 us (2%)
  other arithmetic  1.9 us (2%)
    pallas_call x11, Pallas kernels, placed(): return run(*args)  39.3 us
    ppermute x6, starting transfers between devices, per_device(): lax.ppermute(kv_recv if side else kv_mine, 'ctx', ctx_pairs(step, 0))  10.4 us
    ppermute x3, waiting for transfers between devices, per_device(): lax.ppermute(held, 'ctx', ctx_pairs(step, 0))  6.21 us
    ppermute x3, starting transfers between devices, per_device(): lax.ppermute(held, 'ctx', ctx_pairs(step, 0))  5.81 us
    ppermute x3, starting transfers between devices, per_device(): lax.ppermute(parts[step], 'ctx', ctx_pairs(-step, 0))  4.61 us
    ppermute x1, waiting for transfers between devices, per_device(): weight_recv = lax.ppermute(send, 'ctx', ctx_pairs(0, 1))  3.63 us
    ppermute x1, starting transfers between devices, per_device(): lax.ppermute(grad_own, 'tp', shift_pairs(tp_count, -step))  3.03 us
    ppermute x3, starting transfers between devices, per_device(): attn.append(lax.ppermute(held, axes, pairs) if step or side else held)  2.17 us
  transfers between devices with their start and end apart: 22, of which 5 were waited for; matrix products, arithmetic and copies ran while one was open for 4% of the time, Pallas kernels for 41%

profile of v19, /device:TPU:0, one launch (start us, length us, event | category | flops | bytes accessed | tf_op | source)
XLA Modules:
  0.0 89.8 jit_solution(5773776929937106348)
XLA Ops:
  0.6 3.0 %collective-permute-start.3 = (bf16[256,2048]{1,0:T(8,128)(2,1)}, bf16[256,2048]{1,0:T(8,128)(2,1)}, u32[]{:S(2)}, u32[]{:S(2)}) collective-permute-start(bf16[256,2048]{1,0:T(8,128)(2,1)} %bitcast.29), channel_id=1, source_target_pairs={{0,1},{1,0},{2,3},{3,2},{4,5},{5,4},{6,7},{7,6},{8,9},{9,8},{10,11... | collective-permute-start | bytes 3145736 | tf_op jit(solution)/shard_map/ppermute | solution.py:615
  3.7 0.6 stack.59.refs_0_.refs_3_.refs_1_
  4.3 2.3 %part_heads.1 = (bf16[256,256]{1,0:T(8,128)(2,1)}, bf16[256,256]{1,0:T(8,128)(2,1)}) custom-call(s32[14]{0:T(128)} %stack.59.refs_0_.refs_3_.refs_1_, bf16[256,256]{1,0:T(8,128)(2,1)} %bitcast.32, bf16[256,256]{1,0:T(8,128)(2,1)} %bitcast.33), custom_call_target="tpu_custom_call" | custom-call | flops 2000000000 | bytes 6000000 | tf_op jit(solution)/shard_map/part_heads/pallas_call | solution.py:56
  6.6 1.6 %collective-permute-start = (bf16[256,256]{1,0:T(8,128)(2,1)}, bf16[256,256]{1,0:T(8,128)(2,1)}, u32[]{:S(2)}, u32[]{:S(2)}) collective-permute-start(bf16[256,256]{1,0:T(8,128)(2,1)} %get-tuple-element.33), channel_id=1, source_target_pairs={{0,2},{2,0},{4,6},{6,4},{8,10},{10,8},{12,14},{14,12},{1,3},{3,1},... | collective-permute-start | bytes 393224 | tf_op jit(solution)/shard_map/ppermute | solution.py:618
  8.2 3.6 %collective-permute-start.2 = (bf16[256,256]{1,0:T(8,128)(2,1)}, bf16[256,256]{1,0:T(8,128)(2,1)}, u32[]{:S(2)}, u32[]{:S(2)}) collective-permute-start(bf16[256,256]{1,0:T(8,128)(2,1)} %get-tuple-element.34.refs_6_), channel_id=1, source_target_pairs={{0,12},{2,14},{4,0},{6,2},{8,4},{10,6},{12,8},{14,10},{1,13},{3,15... | collective-permute-start | bytes 393224 | tf_op jit(solution)/shard_map/ppermute | solution.py:620
  11.8 0.0 collective-permute-start.1
  11.8 1.0 %collective-permute-start.6 = (bf16[256,256]{1,0:T(8,128)(2,1)}, bf16[256,256]{1,0:T(8,128)(2,1)}, u32[]{:S(2)}, u32[]{:S(2)}) collective-permute-start(bf16[256,256]{1,0:T(8,128)(2,1)} %get-tuple-element.34.refs_6_), channel_id=1, source_target_pairs={{0,8},{2,10},{4,12},{6,14},{8,0},{10,2},{12,4},{14,6},{1,9},{3,11}... | collective-permute-start | bytes 393224 | tf_op jit(solution)/shard_map/ppermute | solution.py:620
  12.8 1.3 %copy.11.refs_4_ = s32[8,3]{1,0:T(8,128)} copy(s32[8,3]{0,1:T(4,128)} %param.12) | data formatting | bytes 192 | tf_op args[5]
  14.2 0.0 collective-permute-done.refs_0_.refs_7_
  14.2 2.8 %collective-permute-start.8 = (bf16[256,256]{1,0:T(8,128)(2,1)}, bf16[256,256]{1,0:T(8,128)(2,1)}, u32[]{:S(2)}, u32[]{:S(2)}) collective-permute-start(bf16[256,256]{1,0:T(8,128)(2,1)} %collective-permute-done.refs_0_.refs_7_), channel_id=1, source_target_pairs={{0,12},{2,14},{4,0},{6,2},{8,4},{10,6},{12,8},{14,10},{1,13},{3,15... | collective-permute-start | bytes 393224 | tf_op jit(solution)/shard_map/ppermute | solution.py:620
  17.0 0.0 collective-permute-done.2.refs_2_.refs_12_
  17.0 2.0 %collective-permute-start.7 = (bf16[256,256]{1,0:T(8,128)(2,1)}, bf16[256,256]{1,0:T(8,128)(2,1)}, u32[]{:S(2)}, u32[]{:S(2)}) collective-permute-start(bf16[256,256]{1,0:T(8,128)(2,1)} %collective-permute-done.refs_0_.refs_7_), channel_id=1, source_target_pairs={{0,8},{2,10},{4,12},{6,14},{8,0},{10,2},{12,4},{14,6},{1,9},{3,11}... | collective-permute-start | bytes 393224 | tf_op jit(solution)/shard_map/ppermute | solution.py:620
  19.0 1.4 %collective-permute-done.1.refs_1_.refs_8_ = bf16[256,256]{1,0:T(8,128)(2,1)} collective-permute-done((bf16[256,256]{1,0:T(8,128)(2,1)}, bf16[256,256]{1,0:T(8,128)(2,1)}, u32[]{:S(2)}, u32[]{:S(2)}) %collective-permute-start.1) | collective-permute-done | bytes 131104 | tf_op jit(solution)/shard_map/ppermute | solution.py:620
  20.4 1.0 %collective-permute-start.5 = (bf16[256,256]{1,0:T(8,128)(2,1)}, bf16[256,256]{1,0:T(8,128)(2,1)}, u32[]{:S(2)}, u32[]{:S(2)}) collective-permute-start(bf16[256,256]{1,0:T(8,128)(2,1)} %collective-permute-done.refs_0_.refs_7_), channel_id=1, source_target_pairs={{0,4},{2,6},{4,8},{6,10},{8,12},{10,14},{12,0},{14,2},{1,5},{3,7},... | collective-permute-start | bytes 393224 | tf_op jit(solution)/shard_map/ppermute | solution.py:620
  21.4 4.3 %prelude.1 = (f32[256,256]{1,0:T(8,128)}, bf16[2048,128]{1,0:T(8,128)(2,1)}, f32[8,512]{1,0:T(8,128)}) custom-call(bf16[256,256]{1,0:T(8,128)(2,1)} %collective-permute-done.refs_0_.refs_7_, bf16[256,256]{1,0:T(8,128)(2,1)} %collective-permute-done.1.refs_1_.refs_8_, bf16[256,256]{1,0:T(8,128)(2,1)} %collective-permute-done.2.refs_2_.refs_12_, ...), custom_call_target="tpu_custom_call" | custom-call | flops 4000000000 | bytes 12000000 | tf_op jit(solution)/shard_map/prelude/pallas_call | solution.py:56
  25.7 1.5 %collective-permute-done.3.refs_4_.refs_3_ = bf16[256,2048]{1,0:T(8,128)(2,1)} collective-permute-done((bf16[256,2048]{1,0:T(8,128)(2,1)}, bf16[256,2048]{1,0:T(8,128)(2,1)}, u32[]{:S(2)}, u32[]{:S(2)}) %collective-permute-start.3) | collective-permute-done | bytes 1048608 | tf_op jit(solution)/shard_map/ppermute | solution.py:615
  27.1 3.5 %grad_heads.1 = (bf16[128,256]{1,0:T(8,128)(2,1)}, bf16[2,128,256]{2,1,0:T(8,128)(2,1)}) custom-call(s32[14]{0:T(128)} %stack.59.refs_0_.refs_3_.refs_1_, f32[256,256]{1,0:T(8,128)} %get-tuple-element.35.refs_1_, bf16[256,256]{1,0:T(8,128)(2,1)} %bitcast.34, bf16[256,4096]{1,0:T(8,128)(2,1)} %refs_3_.1, bf16[256,2048]{1,0:T(8,128)(2,1)} %collective-permute-done.3.refs_4_.refs_3_), custom_call_target="tpu_custom_call" | custom-call | flops 3000000000 | bytes 9000000 | tf_op jit(solution)/shard_map/grad_heads/pallas_call | solution.py:56
  30.7 1.8 %collective-permute-start.4 = (bf16[2,128,256]{2,1,0:T(8,128)(2,1)}, bf16[2,128,256]{2,1,0:T(8,128)(2,1)}, u32[]{:S(2)}, u32[]{:S(2)}) collective-permute-start(bf16[2,128,256]{2,1,0:T(8,128)(2,1)} %get-tuple-element.36), channel_id=1, source_target_pairs={{0,2},{2,0},{4,6},{6,4},{8,10},{10,8},{12,14},{14,12},{1,3},{3,1},... | collective-permute-start | bytes 393224 | tf_op jit(solution)/shard_map/ppermute | solution.py:629
  32.4 3.7 %pick_columns.1 = (bf16[2,4,256,256]{3,2,1,0:T(8,128)(2,1)}, bf16[2,4,256,256]{3,2,1,0:T(8,128)(2,1)}) custom-call(bf16[128,256]{1,0:T(8,128)(2,1)} %get-tuple-element.37.refs_3_.refs_0_, s32[14]{0:T(128)} %stack.59.refs_0_.refs_3_.refs_1_, bf16[256,2048]{1,0:T(8,128)(2,1)} %bitcast.31, bf16[256,2048]{1,0:T(8,128)(2,1)} %collective-permute-done.3.refs_4_.refs_3_), custom_call_target="tpu_custom_call" | custom-call | flops 3000000000 | bytes 9000000 | tf_op jit(solution)/shard_map/pick_columns/pallas_call | solution.py:56
  36.1 0.0 collective-permute-done.6.refs_10_
  36.1 0.1 collective-permute-start.9
  36.2 0.0 collective-permute-done.8.refs_13_
  36.2 0.0 collective-permute-done.7.refs_11_
  36.2 0.0 collective-permute-done.5.refs_9_
  36.2 0.0 collective-permute-done.4.refs_2_
  36.2 8.9 %attention.1 = (bf16[128,256]{1,0:T(8,128)(2,1)}, bf16[128,256]{1,0:T(8,128)(2,1)}, bf16[256,128]{1,0:T(8,128)(2,1)}, bf16[256,128]{1,0:T(8,128)(2,1)}, bf16[2,2...) custom-call(s32[14]{0:T(128)} %stack.59.refs_0_.refs_3_.refs_1_, ...), custom_call_target="tpu_custom_call" | custom-call | flops 20000000000 | bytes 60000000 | tf_op jit(solution)/shard_map/attention/pallas_call | solution.py:56
  45.1 0.0 collective-permute-done.9.refs_6_.refs_7_
  45.1 0.5 collective-permute-start.12
  45.6 1.7 %collective-permute-start.10 = (bf16[128,256]{1,0:T(8,128)(2,1)}, bf16[128,256]{1,0:T(8,128)(2,1)}, u32[]{:S(2)}, u32[]{:S(2)}) collective-permute-start(bf16[128,256]{1,0:T(8,128)(2,1)} %get-tuple-element.46), channel_id=1, source_target_pairs={{0,2},{2,0},{4,6},{6,4},{8,10},{10,8},{12,14},{14,12},{1,3},{3,1},... | collective-permute-start | bytes 196616 | tf_op jit(solution)/shard_map/ppermute | solution.py:646
  47.3 0.0 collective-permute-start.11
  47.3 2.6 %collective-permute-start.14 = (bf16[2,256,256]{2,1,0:T(8,128)(2,1)}, bf16[2,256,256]{2,1,0:T(8,128)(2,1)}, u32[]{:S(2)}, u32[]{:S(2)}) collective-permute-start(bf16[2,256,256]{2,1,0:T(8,128)(2,1)} %get-tuple-element.52), channel_id=1, source_target_pairs={{0,8},{2,10},{4,12},{6,14},{8,0},{10,2},{12,4},{14,6},{1,9},{3,11}... | collective-permute-start | bytes 786440 | tf_op jit(solution)/shard_map/ppermute | solution.py:649
  49.9 1.4 %collective-permute-start.15 = (bf16[2,256,256]{2,1,0:T(8,128)(2,1)}, bf16[2,256,256]{2,1,0:T(8,128)(2,1)}, u32[]{:S(2)}, u32[]{:S(2)}) collective-permute-start(bf16[2,256,256]{2,1,0:T(8,128)(2,1)} %get-tuple-element.53), channel_id=1, source_target_pairs={{0,12},{2,14},{4,0},{6,2},{8,4},{10,6},{12,8},{14,10},{1,13},{3,15... | collective-permute-start | bytes 786440 | tf_op jit(solution)/shard_map/ppermute | solution.py:649
  51.3 0.0 collective-permute-done.12.refs_4_.refs_5_
  51.3 0.7 collective-permute-start.16
  51.9 0.0 collective-permute-done.10.refs_2_.refs_3_
  51.9 0.0 collective-permute-done.11.refs_3_.refs_4_
  51.9 3.5 %weight_sent.1.refs_0_ = bf16[3,256,256]{2,1,0:T(8,128)(2,1)} custom-call(s32[14]{0:T(128)} %stack.59.refs_0_.refs_3_.refs_1_, bf16[128,256]{1,0:T(8,128)(2,1)} %get-tuple-element.45.refs_1_.refs_2_, bf16[128,256]{1,0:T(8,128)(2,1)} %collective-permute-done.10.refs_2_.refs_3_, bf16[128,256]{1,0:T(8,128)(2,1)} %collective-permute-done.11.refs_3_.refs_4_, ...), custom_call_target="tpu_custom_call" | custom-call | flops 4000000000 | bytes 12000000 | tf_op jit(solution)/shard_map/weight_sent/pallas_call | solution.py:56
  55.4 1.3 %collective-permute-start.13 = (bf16[3,256,256]{2,1,0:T(8,128)(2,1)}, bf16[3,256,256]{2,1,0:T(8,128)(2,1)}, u32[]{:S(2)}, u32[]{:S(2)}) collective-permute-start(bf16[3,256,256]{2,1,0:T(8,128)(2,1)} %weight_sent.1.refs_0_), channel_id=1, source_target_pairs={{0,2},{2,0},{4,6},{6,4},{8,10},{10,8},{12,14},{14,12},{1,3},{3,1},... | collective-permute-start | bytes 1179656 | tf_op jit(solution)/shard_map/ppermute | solution.py:654
  56.7 2.7 %weight_own.1.refs_0_ = bf16[1,256,256]{2,1,0:T(8,128)(2,1)} custom-call(bf16[3,256,256]{2,1,0:T(8,128)(2,1)} %weight_sent.1.refs_0_, s32[14]{0:T(128)} %stack.59.refs_0_.refs_3_.refs_1_, bf16[128,256]{1,0:T(8,128)(2,1)} %get-tuple-element.45.refs_1_.refs_2_, bf16[128,256]{1,0:T(8,128)(2,1)} %collective-permute-done.10.refs_2_.refs_3_, ...), custom_call_target="tpu_custom_call" | custom-call | flops 4000000000 | bytes 12000000 | tf_op jit(solution)/shard_map/weight_own/pallas_call | solution.py:56
  59.4 0.9 collective-permute-start.18
  60.3 3.9 %weight_kept.1.refs_0_ = bf16[4,256,256]{2,1,0:T(8,128)(2,1)} custom-call(bf16[1,256,256]{2,1,0:T(8,128)(2,1)} %weight_own.1.refs_0_, s32[14]{0:T(128)} %stack.59.refs_0_.refs_3_.refs_1_, bf16[128,256]{1,0:T(8,128)(2,1)} %get-tuple-element.45.refs_1_.refs_2_, bf16[128,256]{1,0:T(8,128)(2,1)} %collective-permute-done.10.refs_2_.refs_3_, ...), custom_call_target="tpu_custom_call" | custom-call | flops 4000000000 | bytes 12000000 | tf_op jit(solution)/shard_map/weight_kept/pallas_call | solution.py:56
  64.2 3.6 %collective-permute-done.13.refs_1_ = bf16[3,256,256]{2,1,0:T(8,128)(2,1)} collective-permute-done((bf16[3,256,256]{2,1,0:T(8,128)(2,1)}, bf16[3,256,256]{2,1,0:T(8,128)(2,1)}, u32[]{:S(2)}, u32[]{:S(2)}) %collective-permute-start.13) | collective-permute-done | bytes 393248 | tf_op jit(solution)/shard_map/ppermute | solution.py:654
  67.8 2.0 %weight_add.1 = (bf16[256,256]{1,0:T(8,128)(2,1)}, bf16[256,256]{1,0:T(8,128)(2,1)}, bf16[256,256]{1,0:T(8,128)(2,1)}) custom-call(bf16[4,256,256]{2,1,0:T(8,128)(2,1)} %weight_kept.1.refs_0_, bf16[3,256,256]{2,1,0:T(8,128)(2,1)} %collective-permute-done.13.refs_1_), custom_call_target="tpu_custom_call" | custom-call | flops 2000000000 | bytes 6000000 | tf_op jit(solution)/shard_map/weight_add/pallas_call | solution.py:56
  69.8 2.0 %collective-permute-start.19 = (bf16[256,256]{1,0:T(8,128)(2,1)}, bf16[256,256]{1,0:T(8,128)(2,1)}, u32[]{:S(2)}, u32[]{:S(2)}) collective-permute-start(bf16[256,256]{1,0:T(8,128)(2,1)} %get-tuple-element.60), channel_id=1, source_target_pairs={{0,8},{2,10},{4,12},{6,14},{8,0},{10,2},{12,4},{14,6},{1,9},{3,11}... | collective-permute-start | bytes 393224 | tf_op jit(solution)/shard_map/ppermute | solution.py:660
  71.8 0.0 collective-permute-done.14.refs_3_
  71.8 1.8 %collective-permute-start.20 = (bf16[256,256]{1,0:T(8,128)(2,1)}, bf16[256,256]{1,0:T(8,128)(2,1)}, u32[]{:S(2)}, u32[]{:S(2)}) collective-permute-start(bf16[256,256]{1,0:T(8,128)(2,1)} %get-tuple-element.61), channel_id=1, source_target_pairs={{0,4},{2,6},{4,8},{6,10},{8,12},{10,14},{12,0},{14,2},{1,5},{3,7},... | collective-permute-start | bytes 393224 | tf_op jit(solution)/shard_map/ppermute | solution.py:660
  73.6 0.0 collective-permute-done.15.refs_4_
  73.6 2.0 %collective-permute-start.21 = (bf16[256,256]{1,0:T(8,128)(2,1)}, bf16[256,256]{1,0:T(8,128)(2,1)}, u32[]{:S(2)}, u32[]{:S(2)}) collective-permute-start(bf16[256,256]{1,0:T(8,128)(2,1)} %get-tuple-element.49.refs_0_), channel_id=1, source_target_pairs={{0,12},{2,14},{4,0},{6,2},{8,4},{10,6},{12,8},{14,10},{1,13},{3,15... | collective-permute-start | bytes 393224 | tf_op jit(solution)/shard_map/ppermute | solution.py:660
  75.6 0.0 collective-permute-done.16.refs_5_
  75.6 2.1 %add_terms.1 = (bf16[256,256]{1,0:T(8,128)(2,1)}, bf16[256,384]{1,0:T(8,128)(2,1)}) custom-call(bf16[256,256]{1,0:T(8,128)(2,1)} %get-tuple-element.49.refs_0_, bf16[256,128]{1,0:T(8,128)(2,1)} %get-tuple-element.50.refs_1_, bf16[2,256,256]{2,1,0:T(8,128)(2,1)} %get-tuple-element.51.refs_2_, bf16[2,256,256]{2,1,0:T(8,128)(2,1)} %collective-permute-done.14.refs_3_, ...), custom_call_target="tpu_custom_call" | custom-call | flops 2000000000 | bytes 6000000 | tf_op jit(solution)/shard_map/add_terms/pallas_call | solution.py:56
  77.7 1.5 %collective-permute-start.17 = (bf16[256,384]{1,0:T(8,128)(2,1)}, bf16[256,384]{1,0:T(8,128)(2,1)}, u32[]{:S(2)}, u32[]{:S(2)}) collective-permute-start(bf16[256,384]{1,0:T(8,128)(2,1)} %get-tuple-element.56), channel_id=1, source_target_pairs={{0,2},{2,0},{4,6},{6,4},{8,10},{10,8},{12,14},{14,12},{1,3},{3,1},... | collective-permute-start | bytes 589832 | tf_op jit(solution)/shard_map/ppermute | solution.py:663
  79.2 0.0 collective-permute-done.18
  79.2 3.5 %collective-permute-done.19 = bf16[256,256]{1,0:T(8,128)(2,1)} collective-permute-done((bf16[256,256]{1,0:T(8,128)(2,1)}, bf16[256,256]{1,0:T(8,128)(2,1)}, u32[]{:S(2)}, u32[]{:S(2)}) %collective-permute-start.19) | collective-permute-done | bytes 131104 | tf_op jit(solution)/shard_map/ppermute | solution.py:660
  82.7 0.0 collective-permute-done.20
  82.7 2.7 %collective-permute-done.21 = bf16[256,256]{1,0:T(8,128)(2,1)} collective-permute-done((bf16[256,256]{1,0:T(8,128)(2,1)}, bf16[256,256]{1,0:T(8,128)(2,1)}, u32[]{:S(2)}, u32[]{:S(2)}) %collective-permute-start.21) | collective-permute-done | bytes 131104 | tf_op jit(solution)/shard_map/ppermute | solution.py:660
  85.4 1.9 %fusion.2 = bf16[256,256]{1,0:T(8,128)(2,1)} fusion(bf16[256,256]{1,0:T(8,128)(2,1)} %collective-permute-done.21, bf16[256,256]{1,0:T(8,128)(2,1)} %collective-permute-done.20, bf16[256,256]{1,0:T(8,128)(2,1)} %collective-permute-done.19, bf16[1,256,256]{2,1,0:T(8,128)(2,1)} %collective-permute-done.18, bf16[4,256,256]{2,1,0:T(8,128)(2,1)} %weight_kept.1.refs_0_), kind=kLoop, calls=%fused_computation.3 | loop fusion | flops 655360 | bytes 786432 | tf_op jit(solution)/shard_map/convert_element_type | solution.py:668
  87.3 0.0 collective-permute-done.17.refs_3_
  87.3 2.5 %join_heads.1 = (bf16[256,256]{1,0:T(8,128)(2,1)}, bf16[256,256]{1,0:T(8,128)(2,1)}, bf16[256,256]{1,0:T(8,128)(2,1)}) custom-call(s32[14]{0:T(128)} %stack.59.refs_0_.refs_3_.refs_1_, bf16[256,128]{1,0:T(8,128)(2,1)} %get-tuple-element.40.refs_1_, bf16[256,256]{1,0:T(8,128)(2,1)} %get-tuple-element.55.refs_2_, bf16[256,384]{1,0:T(8,128)(2,1)} %collective-permute-done.17.refs_3_), custom_call_target="tpu_custom_call" | custom-call | flops 2000000000 | bytes 6000000 | tf_op jit(solution)/shard_map/join_heads/pallas_call | solution.py:56
Async XLA Ops:
  0.6 26.5 %collective-permute-start.3 = (bf16[256,2048]{1,0:T(8,128)(2,1)}, bf16[256,2048]{1,0:T(8,128)(2,1)}, u32[]{:S(2)}, u32[]{:S(2)}) collective-permute-start(bf16[256,2048]{1,0:T(8,128)(2,1)} %bitcast.29), channel_id=1, source_target_pairs={{0,1},{1,0},{2,3},{3,2},{4,5},{5,4},{6,7},{7,6},{8,9},{9,8},{10,11... | collective-permute-start | bytes 3145736 | tf_op jit(solution)/shard_map/ppermute | solution.py:615
  6.6 7.5 %collective-permute-start = (bf16[256,256]{1,0:T(8,128)(2,1)}, bf16[256,256]{1,0:T(8,128)(2,1)}, u32[]{:S(2)}, u32[]{:S(2)}) collective-permute-start(bf16[256,256]{1,0:T(8,128)(2,1)} %get-tuple-element.33), channel_id=1, source_target_pairs={{0,2},{2,0},{4,6},{6,4},{8,10},{10,8},{12,14},{14,12},{1,3},{3,1},... | collective-permute-start | bytes 393224 | tf_op jit(solution)/shard_map/ppermute | solution.py:618
  8.2 8.8 %collective-permute-start.2 = (bf16[256,256]{1,0:T(8,128)(2,1)}, bf16[256,256]{1,0:T(8,128)(2,1)}, u32[]{:S(2)}, u32[]{:S(2)}) collective-permute-start(bf16[256,256]{1,0:T(8,128)(2,1)} %get-tuple-element.34.refs_6_), channel_id=1, source_target_pairs={{0,12},{2,14},{4,0},{6,2},{8,4},{10,6},{12,8},{14,10},{1,13},{3,15... | collective-permute-start | bytes 393224 | tf_op jit(solution)/shard_map/ppermute | solution.py:620
  11.8 8.6 %collective-permute-start.1 = (bf16[256,256]{1,0:T(8,128)(2,1)}, bf16[256,256]{1,0:T(8,128)(2,1)}, u32[]{:S(2)}, u32[]{:S(2)}) collective-permute-start(bf16[256,256]{1,0:T(8,128)(2,1)} %get-tuple-element.34.refs_6_), channel_id=1, source_target_pairs={{0,4},{2,6},{4,8},{6,10},{8,12},{10,14},{12,0},{14,2},{1,5},{3,7},... | collective-permute-start | bytes 393224 | tf_op jit(solution)/shard_map/ppermute | solution.py:620
  11.8 24.3 %collective-permute-start.6 = (bf16[256,256]{1,0:T(8,128)(2,1)}, bf16[256,256]{1,0:T(8,128)(2,1)}, u32[]{:S(2)}, u32[]{:S(2)}) collective-permute-start(bf16[256,256]{1,0:T(8,128)(2,1)} %get-tuple-element.34.refs_6_), channel_id=1, source_target_pairs={{0,8},{2,10},{4,12},{6,14},{8,0},{10,2},{12,4},{14,6},{1,9},{3,11}... | collective-permute-start | bytes 393224 | tf_op jit(solution)/shard_map/ppermute | solution.py:620
  14.2 22.0 %collective-permute-start.8 = (bf16[256,256]{1,0:T(8,128)(2,1)}, bf16[256,256]{1,0:T(8,128)(2,1)}, u32[]{:S(2)}, u32[]{:S(2)}) collective-permute-start(bf16[256,256]{1,0:T(8,128)(2,1)} %collective-permute-done.refs_0_.refs_7_), channel_id=1, source_target_pairs={{0,12},{2,14},{4,0},{6,2},{8,4},{10,6},{12,8},{14,10},{1,13},{3,15... | collective-permute-start | bytes 393224 | tf_op jit(solution)/shard_map/ppermute | solution.py:620
  17.0 19.2 %collective-permute-start.7 = (bf16[256,256]{1,0:T(8,128)(2,1)}, bf16[256,256]{1,0:T(8,128)(2,1)}, u32[]{:S(2)}, u32[]{:S(2)}) collective-permute-start(bf16[256,256]{1,0:T(8,128)(2,1)} %collective-permute-done.refs_0_.refs_7_), channel_id=1, source_target_pairs={{0,8},{2,10},{4,12},{6,14},{8,0},{10,2},{12,4},{14,6},{1,9},{3,11}... | collective-permute-start | bytes 393224 | tf_op jit(solution)/shard_map/ppermute | solution.py:620
  20.4 15.8 %collective-permute-start.5 = (bf16[256,256]{1,0:T(8,128)(2,1)}, bf16[256,256]{1,0:T(8,128)(2,1)}, u32[]{:S(2)}, u32[]{:S(2)}) collective-permute-start(bf16[256,256]{1,0:T(8,128)(2,1)} %collective-permute-done.refs_0_.refs_7_), channel_id=1, source_target_pairs={{0,4},{2,6},{4,8},{6,10},{8,12},{10,14},{12,0},{14,2},{1,5},{3,7},... | collective-permute-start | bytes 393224 | tf_op jit(solution)/shard_map/ppermute | solution.py:620
  30.7 5.6 %collective-permute-start.4 = (bf16[2,128,256]{2,1,0:T(8,128)(2,1)}, bf16[2,128,256]{2,1,0:T(8,128)(2,1)}, u32[]{:S(2)}, u32[]{:S(2)}) collective-permute-start(bf16[2,128,256]{2,1,0:T(8,128)(2,1)} %get-tuple-element.36), channel_id=1, source_target_pairs={{0,2},{2,0},{4,6},{6,4},{8,10},{10,8},{12,14},{14,12},{1,3},{3,1},... | collective-permute-start | bytes 393224 | tf_op jit(solution)/shard_map/ppermute | solution.py:629
  36.1 9.0 %collective-permute-start.9 = (bf16[2,4,256,256]{3,2,1,0:T(8,128)(2,1)}, bf16[2,4,256,256]{3,2,1,0:T(8,128)(2,1)}, u32[]{:S(2)}, u32[]{:S(2)}) collective-permute-start(bf16[2,4,256,256]{3,2,1,0:T(8,128)(2,1)} %get-tuple-element.44), channel_id=1, source_target_pairs={{0,16},{16,0},{1,17},{17,1},{2,18},{18,2},{3,19},{19,3},{4,20},{20... | collective-permute-start | bytes 3145736 | tf_op jit(solution)/shard_map/ppermute | solution.py:632
  45.1 6.1 %collective-permute-start.12 = (bf16[128,256]{1,0:T(8,128)(2,1)}, bf16[128,256]{1,0:T(8,128)(2,1)}, u32[]{:S(2)}, u32[]{:S(2)}) collective-permute-start(bf16[128,256]{1,0:T(8,128)(2,1)} %get-tuple-element.46), channel_id=1, source_target_pairs={{0,18},{2,16},{4,22},{6,20},{8,26},{10,24},{12,30},{14,28},{16,2},... | collective-permute-start | bytes 196616 | tf_op jit(solution)/shard_map/ppermute | solution.py:646
  45.6 6.3 %collective-permute-start.10 = (bf16[128,256]{1,0:T(8,128)(2,1)}, bf16[128,256]{1,0:T(8,128)(2,1)}, u32[]{:S(2)}, u32[]{:S(2)}) collective-permute-start(bf16[128,256]{1,0:T(8,128)(2,1)} %get-tuple-element.46), channel_id=1, source_target_pairs={{0,2},{2,0},{4,6},{6,4},{8,10},{10,8},{12,14},{14,12},{1,3},{3,1},... | collective-permute-start | bytes 196616 | tf_op jit(solution)/shard_map/ppermute | solution.py:646
  47.3 4.6 %collective-permute-start.11 = (bf16[128,256]{1,0:T(8,128)(2,1)}, bf16[128,256]{1,0:T(8,128)(2,1)}, u32[]{:S(2)}, u32[]{:S(2)}) collective-permute-start(bf16[128,256]{1,0:T(8,128)(2,1)} %get-tuple-element.45.refs_1_.refs_2_), channel_id=1, source_target_pairs={{0,16},{2,18},{4,20},{6,22},{8,24},{10,26},{12,28},{14,30},{16,0},... | collective-permute-start | bytes 196616 | tf_op jit(solution)/shard_map/ppermute | solution.py:646
  47.3 24.5 %collective-permute-start.14 = (bf16[2,256,256]{2,1,0:T(8,128)(2,1)}, bf16[2,256,256]{2,1,0:T(8,128)(2,1)}, u32[]{:S(2)}, u32[]{:S(2)}) collective-permute-start(bf16[2,256,256]{2,1,0:T(8,128)(2,1)} %get-tuple-element.52), channel_id=1, source_target_pairs={{0,8},{2,10},{4,12},{6,14},{8,0},{10,2},{12,4},{14,6},{1,9},{3,11}... | collective-permute-start | bytes 786440 | tf_op jit(solution)/shard_map/ppermute | solution.py:649
  49.9 23.7 %collective-permute-start.15 = (bf16[2,256,256]{2,1,0:T(8,128)(2,1)}, bf16[2,256,256]{2,1,0:T(8,128)(2,1)}, u32[]{:S(2)}, u32[]{:S(2)}) collective-permute-start(bf16[2,256,256]{2,1,0:T(8,128)(2,1)} %get-tuple-element.53), channel_id=1, source_target_pairs={{0,12},{2,14},{4,0},{6,2},{8,4},{10,6},{12,8},{14,10},{1,13},{3,15... | collective-permute-start | bytes 786440 | tf_op jit(solution)/shard_map/ppermute | solution.py:649
  51.3 24.3 %collective-permute-start.16 = (bf16[2,256,256]{2,1,0:T(8,128)(2,1)}, bf16[2,256,256]{2,1,0:T(8,128)(2,1)}, u32[]{:S(2)}, u32[]{:S(2)}) collective-permute-start(bf16[2,256,256]{2,1,0:T(8,128)(2,1)} %get-tuple-element.54), channel_id=1, source_target_pairs={{0,4},{2,6},{4,8},{6,10},{8,12},{10,14},{12,0},{14,2},{1,5},{3,7},... | collective-permute-start | bytes 786440 | tf_op jit(solution)/shard_map/ppermute | solution.py:649
  55.4 12.4 %collective-permute-start.13 = (bf16[3,256,256]{2,1,0:T(8,128)(2,1)}, bf16[3,256,256]{2,1,0:T(8,128)(2,1)}, u32[]{:S(2)}, u32[]{:S(2)}) collective-permute-start(bf16[3,256,256]{2,1,0:T(8,128)(2,1)} %weight_sent.1.refs_0_), channel_id=1, source_target_pairs={{0,2},{2,0},{4,6},{6,4},{8,10},{10,8},{12,14},{14,12},{1,3},{3,1},... | collective-permute-start | bytes 1179656 | tf_op jit(solution)/shard_map/ppermute | solution.py:654
  59.4 19.8 %collective-permute-start.18 = (bf16[1,256,256]{2,1,0:T(8,128)(2,1)}, bf16[1,256,256]{2,1,0:T(8,128)(2,1)}, u32[]{:S(2)}, u32[]{:S(2)}) collective-permute-start(bf16[1,256,256]{2,1,0:T(8,128)(2,1)} %weight_own.1.refs_0_), channel_id=1, source_target_pairs={{0,2},{2,0},{4,6},{6,4},{8,10},{10,8},{12,14},{14,12},{1,3},{3,1},... | collective-permute-start | bytes 393224 | tf_op jit(solution)/shard_map/ppermute | solution.py:656
  69.8 12.9 %collective-permute-start.19 = (bf16[256,256]{1,0:T(8,128)(2,1)}, bf16[256,256]{1,0:T(8,128)(2,1)}, u32[]{:S(2)}, u32[]{:S(2)}) collective-permute-start(bf16[256,256]{1,0:T(8,128)(2,1)} %get-tuple-element.60), channel_id=1, source_target_pairs={{0,8},{2,10},{4,12},{6,14},{8,0},{10,2},{12,4},{14,6},{1,9},{3,11}... | collective-permute-start | bytes 393224 | tf_op jit(solution)/shard_map/ppermute | solution.py:660
  71.8 10.9 %collective-permute-start.20 = (bf16[256,256]{1,0:T(8,128)(2,1)}, bf16[256,256]{1,0:T(8,128)(2,1)}, u32[]{:S(2)}, u32[]{:S(2)}) collective-permute-start(bf16[256,256]{1,0:T(8,128)(2,1)} %get-tuple-element.61), channel_id=1, source_target_pairs={{0,4},{2,6},{4,8},{6,10},{8,12},{10,14},{12,0},{14,2},{1,5},{3,7},... | collective-permute-start | bytes 393224 | tf_op jit(solution)/shard_map/ppermute | solution.py:660
  73.6 11.8 %collective-permute-start.21 = (bf16[256,256]{1,0:T(8,128)(2,1)}, bf16[256,256]{1,0:T(8,128)(2,1)}, u32[]{:S(2)}, u32[]{:S(2)}) collective-permute-start(bf16[256,256]{1,0:T(8,128)(2,1)} %get-tuple-element.49.refs_0_), channel_id=1, source_target_pairs={{0,12},{2,14},{4,0},{6,2},{8,4},{10,6},{12,8},{14,10},{1,13},{3,15... | collective-permute-start | bytes 393224 | tf_op jit(solution)/shard_map/ppermute | solution.py:660
  77.7 9.6 %collective-permute-start.17 = (bf16[256,384]{1,0:T(8,128)(2,1)}, bf16[256,384]{1,0:T(8,128)(2,1)}, u32[]{:S(2)}, u32[]{:S(2)}) collective-permute-start(bf16[256,384]{1,0:T(8,128)(2,1)} %get-tuple-element.56), channel_id=1, source_target_pairs={{0,2},{2,0},{4,6},{6,4},{8,10},{10,8},{12,14},{14,12},{1,3},{3,1},... | collective-permute-start | bytes 589832 | tf_op jit(solution)/shard_map/ppermute | solution.py:663
